TPU v7x, 32 devices: a whole 2x2x4 slice. The times are simulated.
32 devices in a mesh: section: 4 (over y, x), dp: 8 (over z, core).
Axes of the slice: x: 2, y: 2, z: 4, core: 2. Of those that a mesh axis runs over, the one named last changes fastest.
Arguments:
- acts: bfloat16 [4, 128, 196, 1024], P('section', 'dp'), may hold values from -8 to 8, as said below
- patches: bfloat16 [128, 196, 768], P('dp', None, 'section'), may hold values from -6 to 6
- labels: int32 [128], P('dp'), may hold values from 0 to 11263
- w_first: bfloat16 [4, 1024, 256], P('section'), may hold values from -0.1875 to 0.1875
- w_second: bfloat16 [4, 256, 1024], P('section'), may hold values from -0.375 to 0.375
- w_decode: bfloat16 [4, 1024, 768], P('section'), may hold values from -0.1875 to 0.1875
- w_aux: bfloat16 [4, 1024, 512], P('section'), may hold values from -0.1875 to 0.1875
- w_class: bfloat16 [4, 11264, 512], P('section', 'dp'), may hold values from -1.5 to 1.5
Outputs:
- grad_first: float32 [4, 1024, 256], P('section', 'dp')
- grad_second: float32 [4, 256, 1024], P('section', 'dp')
- grad_decode: float32 [4, 1024, 768], P('section', 'dp')
- grad_aux: float32 [4, 1024, 512], P('section', 'dp')
- grad_class: float32 [4, 11264, 512], P('section', 'dp')
Inputs may be any that keep to these rules, and one draw needn't show every extreme that they name: `acts`: feature maps with a per-image, per-channel offset.
All inputs are finite; a program needn't handle non-finite values.
Results may differ from a plain program's by a relative error of at most 0.03.
The roundings to bfloat16 on the way count: a program that leaves them out, or rounds other values in their place, can miss the bound.
Values may be sent and summed in bfloat16 or wider, within the bound.
No kernel may reach another device: no remote copies, remote signals or barrier semaphores. Data moves between devices by JAX's collectives and lax.ppermute only.
A program may use at most 192 MiB of HBM per device.

v0:
```python
import jax
import jax.numpy as jnp
from jax import lax
from jax.sharding import PartitionSpec as P

C = 1024
PIX = 196
PATCH = 768
CLASSES = 11264


def local(acts, patches, labels, w_first, w_second, w_decode, w_aux, w_class):
    local_acts = acts[0]
    images_here = local_acts.shape[0]
    rows_here = images_here * PIX
    flat = local_acts.reshape(rows_here, C)
    groups = lax.axis_size("dp")
    total_rows = groups * rows_here
    total_images = groups * images_here
    first = w_first[0]
    second = w_second[0]
    decode = w_decode[0]
    aux = w_aux[0]
    class_shard = w_class[0]
    target = lax.all_gather(patches, "section", axis=2, tiled=True).reshape(rows_here, PATCH)
    pre_act = jnp.dot(flat, first, preferred_element_type=jnp.float32)
    hidden = jax.nn.relu(pre_act).astype(jnp.bfloat16)
    feature = (
        flat.astype(jnp.float32) + jnp.dot(hidden, second, preferred_element_type=jnp.float32)
    ).astype(jnp.bfloat16)
    recon = jnp.dot(feature, decode, preferred_element_type=jnp.float32)
    recon_grad = ((recon - target.astype(jnp.float32)) / total_rows**0.5).astype(jnp.bfloat16)
    pooled = jnp.mean(feature.reshape(images_here, PIX, C).astype(jnp.float32), axis=1).astype(
        jnp.bfloat16
    )
    aux_pre = jnp.dot(pooled, aux, preferred_element_type=jnp.float32)
    aux_out = jax.nn.relu(aux_pre).astype(jnp.bfloat16)
    all_rows = lax.all_gather(class_shard, "dp", axis=0, tiled=True)
    logits = jnp.dot(aux_out, all_rows.T, preferred_element_type=jnp.float32)
    top = jnp.max(logits, axis=1, keepdims=True)
    expo = jnp.exp(logits - top)
    prob = expo / jnp.sum(expo, axis=1, keepdims=True)
    onehot = (labels[:, None] == jnp.arange(CLASSES, dtype=jnp.int32)[None, :]).astype(jnp.float32)
    logit_grad = ((prob - onehot) / total_images**0.5).astype(jnp.bfloat16)
    grad_class = lax.psum_scatter(
        jnp.dot(logit_grad.T, aux_out, preferred_element_type=jnp.float32).astype(jnp.bfloat16),
        "dp",
        scatter_dimension=0,
        tiled=True,
    ).astype(jnp.float32)
    back = jnp.dot(logit_grad, all_rows, preferred_element_type=jnp.float32)
    aux_grad = jnp.where(aux_pre > 0, back, 0.0).astype(jnp.bfloat16)
    pooled_grad = jnp.dot(aux_grad, aux.T, preferred_element_type=jnp.float32)
    dec_back = jnp.dot(recon_grad, decode.T, preferred_element_type=jnp.float32)
    feature_grad = (
        (dec_back.reshape(images_here, PIX, C) + pooled_grad[:, None, :] / PIX)
        .reshape(rows_here, C)
        .astype(jnp.bfloat16)
    )
    hid_back = jnp.dot(feature_grad, second.T, preferred_element_type=jnp.float32)
    hidden_grad = jnp.where(pre_act > 0, hid_back, 0.0).astype(jnp.bfloat16)
    part_first = jnp.dot(flat.T, hidden_grad, preferred_element_type=jnp.float32)
    part_second = jnp.dot(hidden.T, feature_grad, preferred_element_type=jnp.float32)
    part_decode = jnp.dot(feature.T, recon_grad, preferred_element_type=jnp.float32)
    part_aux = jnp.dot(pooled.T, aux_grad, preferred_element_type=jnp.float32)
    grad_first, grad_second, grad_decode, grad_aux = (
        lax.psum_scatter(
            part_first.astype(jnp.bfloat16), "dp", scatter_dimension=0, tiled=True
        ).astype(jnp.float32),
        lax.psum_scatter(
            part_second.astype(jnp.bfloat16), "dp", scatter_dimension=0, tiled=True
        ).astype(jnp.float32),
        lax.psum_scatter(
            part_decode.astype(jnp.bfloat16), "dp", scatter_dimension=0, tiled=True
        ).astype(jnp.float32),
        lax.psum_scatter(
            part_aux.astype(jnp.bfloat16), "dp", scatter_dimension=0, tiled=True
        ).astype(jnp.float32),
    )
    return (
        grad_first[None],
        grad_second[None],
        grad_decode[None],
        grad_aux[None],
        grad_class[None],
    )


def solution(mesh):
    in_specs = (
        P("section", "dp", None, None),
        P("dp", None, "section"),
        P("dp"),
        P("section", None, None),
        P("section", None, None),
        P("section", None, None),
        P("section", None, None),
        P("section", "dp", None),
    )
    out_specs = (
        P("section", "dp", None),
        P("section", "dp", None),
        P("section", "dp", None),
        P("section", "dp", None),
        P("section", "dp", None),
    )
    return jax.shard_map(local, mesh=mesh, in_specs=in_specs, out_specs=out_specs, check_vma=False)
```

profile of v0, /device:TPU:0, one launch (start us, length us, event | category | flops | bytes accessed | tf_op | source)
XLA Modules:
  0.0 456.5 jit_solution(5844214032111943192)
XLA Ops:
  7.2 0.0 all-gather.4.cloned.1.call-start
  7.2 3.5 copy.27
  10.8 0.0 all-gather.4.cloned.1.call-update
  10.8 0.0 all-gather.6.cloned.1.call-start
  10.8 0.7 all-gather.6.cloned.1.call-update
  11.5 0.0 reduce-scatter.10.cloned.1.call-start
  11.6 9.1 %copy.26 = bf16[1,16,196,1024]{3,2,1,0:T(8,128)(2,1)} copy(bf16[1,16,196,1024]{3,1,2,0:T(8,128)(2,1)} %param.8) | data formatting | bytes 12845056 | tf_op args[0]
  20.7 8.6 %reshape_squeeze.3 = bf16[3136,1024]{1,0:T(8,128)(2,1)} reshape(bf16[1,16,196,1024]{3,2,1,0:T(8,128)(2,1)} %copy.26) | data formatting | bytes 12845056 | tf_op jit(solution)/shard_map/reshape;squeeze | solution.py:16
  29.3 4.8 %fusion.21 = f32[3136,256]{1,0:T(8,128)S(1)} fusion(bf16[3136,1024]{1,0:T(8,128)(2,1)} %reshape_squeeze.3, bf16[1,1024,256]{2,1,0:T(8,128)(2,1)S(1)} %copy-done.8), kind=kOutput, calls=%fused_computation.31 | convolution fusion | flops 1644167168 | bytes 10158080 | tf_op jit(solution)/shard_map/dot_general | solution.py:26
  34.1 1.7 copy-done.3
  35.8 4.6 %add_convert_fusion.1 = bf16[3136,1024]{1,0:T(8,128)(2,1)} fusion(bf16[3136,1024]{1,0:T(8,128)(2,1)S(1)} %copy-done.2, f32[3136,256]{1,0:T(8,128)S(1)} %fusion.21, bf16[1,256,1024]{2,1,0:T(8,128)(2,1)S(1)} %copy-done.5), kind=kOutput, calls=%fused_computation.2 | convolution fusion | flops 1655406592 | bytes 16580608 | tf_op jit(solution)/shard_map/dot_general | solution.py:29
  40.4 9.2 %reshape.27 = f32[16,196,1024]{2,1,0:T(8,128)} reshape(bf16[3136,1024]{1,0:T(8,128)(2,1)} %add_convert_fusion.1) | data formatting | bytes 19267584 | tf_op jit(solution)/shard_map/convert_element_type | solution.py:33
  49.6 6.5 %reduce_sum.18 = f32[16,1024]{1,0:T(8,128)S(1)} reduce(f32[16,196,1024]{2,1,0:T(8,128)} %reshape.27, f32[]{:T(128)} %constant.6.clone.1), dimensions={1}, to_apply=%region_0.1 | reduce | flops 3194880 | bytes 12910596 | tf_op jit(solution)/shard_map/reduce_sum | solution.py:33
  56.1 0.2 fusion.15
  56.3 27.5 %all-gather.4.cloned.1.call-done = bf16[16,196,768]{1,0,2:T(8,128)(2,1)} async-done(((bf16[16,196,192]{1,0,2:T(8,128)(2,1)}), bf16[16,196,768]{1,0,2:T(8,128)(2,1)}) %all-gather.4.cloned.1.call-update) | async-done | bytes 4816912 | tf_op jit(solution)/shard_map/all_gather | solution.py:25
  83.8 9.6 %copy.28 = bf16[16,196,768]{2,0,1:T(8,128)(2,1)} copy(bf16[16,196,768]{1,0,2:T(8,128)(2,1)} %all-gather.4.cloned.1.call-done) | data formatting | bytes 9633792 | tf_op jit(solution)/shard_map/all_gather | solution.py:25
  93.4 8.4 %copy.29 = f32[16,196,768]{2,1,0:T(8,128)} copy(bf16[16,196,768]{2,0,1:T(8,128)(2,1)} %copy.28) | data formatting | bytes 14450688 | tf_op jit(solution)/shard_map/convert_element_type | solution.py:32
  101.7 10.0 %reshape.26 = f32[3136,768]{1,0:T(8,128)} reshape(f32[16,196,768]{2,1,0:T(8,128)} %copy.29) | data formatting | bytes 19267584 | tf_op jit(solution)/shard_map/convert_element_type | solution.py:32
  111.7 11.3 %multiply_convert_fusion = bf16[3136,768]{1,0:T(8,128)(2,1)} fusion(f32[3136,768]{1,0:T(8,128)} %reshape.26, bf16[3136,1024]{1,0:T(8,128)(2,1)} %add_convert_fusion.1, bf16[1,1024,768]{2,1,0:T(8,128)(2,1)S(1)} %copy-done), kind=kOutput, calls=%fused_computation.7 | convolution fusion | flops 4939726848 | bytes 22446080 | tf_op jit(solution)/shard_map/dot_general | solution.py:31
  123.0 7.2 %dot_general.47 = bf16[16,196,768]{2,1,0:T(8,128)(2,1)} reshape(bf16[3136,768]{1,0:T(8,128)(2,1)} %multiply_convert_fusion) | data formatting | bytes 9633792 | tf_op jit(solution)/shard_map/dot_general | solution.py:54
  130.2 10.1 %convolution_convert_fusion.1 = bf16[1024,768]{1,0:T(8,128)(2,1)} fusion(bf16[3136,1024]{1,0:T(8,128)(2,1)} %add_convert_fusion.1, bf16[3136,768]{1,0:T(8,128)(2,1)} %multiply_convert_fusion), kind=kOutput, calls=%fused_computation.11 | convolution fusion | flops 4933287936 | bytes 12812288 | tf_op jit(solution)/shard_map/dot_general | solution.py:64
  140.3 0.0 reduce-scatter.16.cloned.1.call-start
  140.4 53.2 %all-gather.6.cloned.1.call-done = bf16[1,11264,512]{2,1,0:T(8,128)(2,1)} async-done(((bf16[1,1408,512]{2,1,0:T(8,128)(2,1)}), bf16[1,11264,512]{2,1,0:T(8,128)(2,1)}) %all-gather.6.cloned.1.call-update) | async-done | bytes 11534352 | tf_op jit(solution)/shard_map/all_gather | solution.py:38
  193.5 7.6 %fusion.30 = (f32[16]{0:T(128)S(1)}, f32[16,11264]{1,0:T(8,128)S(1)}) fusion(bf16[1,11264,512]{2,1,0:T(8,128)(2,1)} %all-gather.6.cloned.1.call-done, f32[16,512]{1,0:T(8,128)S(1)} %fusion.15), kind=kOutput, calls=%fused_computation.46 | convolution fusion | flops 184745968 | bytes 12288064 | tf_op jit(solution)/shard_map/dot_general | solution.py:39
  201.2 0.3 fusion.17
  201.6 1.6 fusion.11
  203.2 0.4 convolution_multiply_fusion
  203.6 7.6 %add_convert_fusion = bf16[16,196,1024]{2,1,0:T(8,128)(2,1)} fusion(bf16[16,196,768]{2,1,0:T(8,128)(2,1)S(1)} %bitcast.60, f32[16,1024]{1,0:T(8,128)S(1)} %convolution_multiply_fusion, bf16[1,1024,768]{2,1,0:T(8,128)(2,1)S(1)} %copy-done), kind=kOutput, calls=%fused_computation.1 | convolution fusion | flops 4938924032 | bytes 12877824 | tf_op jit(solution)/shard_map/dot_general | solution.py:54
  211.3 8.4 %convert_element_type.86 = bf16[3136,1024]{1,0:T(8,128)(2,1)} reshape(bf16[16,196,1024]{2,1,0:T(8,128)(2,1)} %add_convert_fusion) | data formatting | bytes 12845056 | tf_op jit(solution)/shard_map/convert_element_type | solution.py:58
  219.7 12.1 %fusion.7 = bf16[1024,256]{0,1:T(8,128)(2,1)S(1)} fusion(bf16[3136,1024]{1,0:T(8,128)(2,1)} %reshape_squeeze.3, bf16[3136,1024]{1,0:T(8,128)(2,1)} %convert_element_type.86, f32[3136,256]{1,0:T(8,128)} %copy-done.3, bf16[1,256,1024]{2,1,0:T(8,128)(2,1)S(1)} %copy-done.6), kind=kOutput, calls=%fused_computation.18 | convolution fusion | flops 3291004928 | bytes 17104896 | tf_op jit(solution)/shard_map/dot_general | solution.py:62
  231.8 1.0 copy.31
  232.9 0.0 reduce-scatter.8.cloned.1.call-start
  232.9 6.6 %convolution_convert_fusion.3 = bf16[256,1024]{1,0:T(8,128)(2,1)} fusion(bf16[3136,1024]{1,0:T(8,128)(2,1)} %convert_element_type.86, f32[3136,256]{1,0:T(8,128)} %copy-done.3), kind=kOutput, calls=%fused_computation.16 | convolution fusion | flops 1646034944 | bytes 10158080 | tf_op jit(solution)/shard_map/dot_general | solution.py:63
  239.5 0.0 reduce-scatter.12.cloned.1.call-start
  239.5 1.4 convolution_convert_fusion.2
  241.0 0.0 reduce-scatter.14.cloned.1.call-start
  241.0 6.2 %convolution_convert_fusion = bf16[11264,512]{1,0:T(8,128)(2,1)} fusion(f32[16,512]{1,0:T(8,128)S(1)} %fusion.15, f32[16,11264]{1,0:T(8,128)S(1)} %get-tuple-element.31, s32[16]{0:T(128)S(1)} %copy-done.7, f32[16]{0:T(128)S(1)} %fusion.17, f32[16]{0:T(128)S(1)} %get-tuple-element.30), kind=kOutput, calls=%fused_computation | convolution fusion | flops 191594496 | bytes 12288192 | tf_op jit(solution)/shard_map/dot_general | solution.py:46
  247.3 0.0 reduce-scatter.10.cloned.1.call-done
  247.3 1.7 bitcast_convert_fusion.1
  249.0 13.4 %reduce-scatter.16.cloned.1.call-done = bf16[128,256]{1,0:T(8,128)(2,1)} async-done(((bf16[1024,256]{1,0:T(8,128)(2,1)}), bf16[128,256]{1,0:T(8,128)(2,1)}) %reduce-scatter.16.cloned.1.call-update) | async-done | bytes 65552
  262.4 0.9 copy.32
  263.4 0.8 copy.30
  264.1 29.6 %reduce-scatter.8.cloned.1.call-done = bf16[32,1024]{1,0:T(8,128)(2,1)} async-done(((bf16[256,1024]{1,0:T(8,128)(2,1)}), bf16[32,1024]{1,0:T(8,128)(2,1)}) %reduce-scatter.8.cloned.1.call-update) | async-done | bytes 65552 | tf_op jit(solution)/shard_map/reduce_scatter | solution.py:70
  293.7 1.5 bitcast_convert_fusion.3
  295.2 31.2 %reduce-scatter.12.cloned.1.call-done = bf16[128,512]{1,0:T(8,128)(2,1)} async-done(((bf16[1024,512]{1,0:T(8,128)(2,1)}), bf16[128,512]{1,0:T(8,128)(2,1)}) %reduce-scatter.12.cloned.1.call-update) | async-done | bytes 131088 | tf_op jit(solution)/shard_map/reduce_scatter | solution.py:76
  326.4 1.6 bitcast_convert_fusion.2
  328.0 118.3 %reduce-scatter.14.cloned.1.call-done = bf16[1408,512]{1,0:T(8,128)(2,1)} async-done(((bf16[11264,512]{1,0:T(8,128)(2,1)}), bf16[1408,512]{1,0:T(8,128)(2,1)}) %reduce-scatter.14.cloned.1.call-update) | async-done | bytes 1441808 | tf_op jit(solution)/shard_map/reduce_scatter | solution.py:45
  446.4 3.3 bitcast_convert_fusion
  (28 shorter events, 0.1 us)
Async XLA Ops:
  7.2 104.5 %copy-start = (bf16[1,1024,768]{2,1,0:T(8,128)(2,1)S(1)}, bf16[1,1024,768]{2,1,0:T(8,128)(2,1)}, u32[]{:S(2)}) copy-start(bf16[1,1024,768]{2,1,0:T(8,128)(2,1)} %param.13) | copy-start | bytes 4718596
  7.2 76.6 %all-gather.4.cloned.1.call-start = ((), (), s32[]{:S(2)}) async-start(), calls=%async_computation.5 | async-start | bytes 7864320 | tf_op jit(solution)/shard_map/all_gather | solution.py:25
  10.8 182.8 %all-gather.6.cloned.1.call-start = ((), (), s32[]{:S(2)}) async-start(), calls=%async_computation.10 | async-start | bytes 12976128 | tf_op jit(solution)/shard_map/all_gather | solution.py:38
  11.5 235.8 %reduce-scatter.10.cloned.1.call-start = ((), (), s32[]{:S(2)}) async-start(), calls=%async_computation.7 | async-start | bytes 1769472 | tf_op jit(solution)/shard_map/reduce_scatter | solution.py:73
  20.7 8.6 %copy-start.8 = (bf16[1,1024,256]{2,1,0:T(8,128)(2,1)S(1)}, bf16[1,1024,256]{2,1,0:T(8,128)(2,1)}, u32[]{:S(2)}) copy-start(bf16[1,1024,256]{2,1,0:T(8,128)(2,1)} %param.11) | copy-start | bytes 1572868
  29.3 6.5 %copy-start.2 = (bf16[3136,1024]{1,0:T(8,128)(2,1)S(1)}, bf16[3136,1024]{1,0:T(8,128)(2,1)}, u32[]{:S(2)}) copy-start(bf16[3136,1024]{1,0:T(8,128)(2,1)} %reshape_squeeze.3) | copy-start | bytes 19267588
  29.3 6.5 %copy-start.5 = (bf16[1,256,1024]{2,1,0:T(8,128)(2,1)S(1)}, bf16[1,256,1024]{2,1,0:T(8,128)(2,1)}, u32[]{:S(2)}) copy-start(bf16[1,256,1024]{2,1,0:T(8,128)(2,1)} %param.12) | copy-start | bytes 1572868
  34.1 1.7 copy-start.3
  49.6 6.5 %copy-start.4 = (bf16[1,1024,512]{2,1,0:T(8,128)(2,1)S(1)}, bf16[1,1024,512]{2,1,0:T(8,128)(2,1)}, u32[]{:S(2)}) copy-start(bf16[1,1024,512]{2,1,0:T(8,128)(2,1)} %param.14) | copy-start | bytes 3145732
  140.3 61.2 %copy-start.7 = (s32[16]{0:T(128)S(1)}, s32[16]{0:T(128)}, u32[]{:S(2)}) copy-start(s32[16]{0:T(128)} %param.10) | copy-start | bytes 196
  140.3 122.1 %reduce-scatter.16.cloned.1.call-start = ((), (), s32[]{:S(2)}) async-start(), calls=%async_computation.11 | async-start | bytes 589824
  193.5 8.0 %copy-start.1 = (bf16[1,11264,512]{2,1,0:T(8,128)(2,1)S(1)}, bf16[1,11264,512]{2,1,0:T(8,128)(2,1)}, u32[]{:S(2)}) copy-start(bf16[1,11264,512]{2,1,0:T(8,128)(2,1)} %all-gather.6.cloned.1.call-done) | copy-start | bytes 34603012
  201.2 2.4 slice-start
  201.5 2.0 slice-start.1
  211.3 8.5 %copy-start.6 = (bf16[1,256,1024]{2,1,0:T(8,128)(2,1)S(1)}, bf16[1,256,1024]{2,1,0:T(8,128)(2,1)}, u32[]{:S(2)}) copy-start(bf16[1,256,1024]{2,1,0:T(8,128)(2,1)} %param.12) | copy-start | bytes 1572868
  232.9 60.9 %reduce-scatter.8.cloned.1.call-start = ((), (), s32[]{:S(2)}) async-start(), calls=%async_computation.6 | async-start | bytes 589824 | tf_op jit(solution)/shard_map/reduce_scatter | solution.py:70
  239.5 86.9 %reduce-scatter.12.cloned.1.call-start = ((), (), s32[]{:S(2)}) async-start(), calls=%async_computation.8 | async-start | bytes 1179648 | tf_op jit(solution)/shard_map/reduce_scatter | solution.py:76
  241.0 205.4 %reduce-scatter.14.cloned.1.call-start = ((), (), s32[]{:S(2)}) async-start(), calls=%async_computation.9 | async-start | bytes 12976128 | tf_op jit(solution)/shard_map/reduce_scatter | solution.py:45
Sparse Core Ops, SparseCore 0:
  10.9 72.8 all-gather.3
  85.4 108.0 all-gather.5
  196.4 32.3 reduce-scatter.9
  233.0 29.3 reduce-scatter.15
  264.6 29.1 reduce-scatter.7
  295.9 30.4 reduce-scatter.11
  328.7 117.6 reduce-scatter.13
where the time goes:
time: 458 us; the launch traced here: 457 us
  waiting for transfers between devices  274 us (60%)
  local copies, waits for them, and re-layouts  78.4 us (17%)
  matrix products  74.6 us (16%)
  other arithmetic  15 us (3%)
  between operations  14.3 us (3%)
    reduce_scatter x1, waiting for transfers between devices, local(): lax.psum_scatter(jnp.dot(logit_grad.T, aux_out, preferred_element_type=jn...  118 us
    all_gather x1, waiting for transfers between devices, local(): all_rows = lax.all_gather(class_shard, 'dp', axis=0, tiled=True)  53.2 us
    reduce_scatter x1, waiting for transfers between devices, local(): lax.psum_scatter(part_aux.astype(jnp.bfloat16), 'dp', scatter_dimension=0...  31.2 us
    reduce_scatter x1, waiting for transfers between devices, local(): lax.psum_scatter(part_second.astype(jnp.bfloat16), 'dp', scatter_dimensio...  29.6 us
    all_gather x1, waiting for transfers between devices, local(): lax.all_gather(patches, 'section', axis=2, tiled=True)  27.5 us
    convert_element_type x2, local copies, waits for them, and re-layouts, local(): target.astype(jnp.float32)  18.3 us
    unnamed x27, local copies, waits for them, and re-layouts  17.1 us
    unnamed x8, waiting for transfers between devices  14.2 us
  transfers between devices with their start and end apart: 7, of which 6 were waited for; matrix products, arithmetic and copies ran while one was open for 35% of the time, Pallas kernels for 0%

commit v1 on v0

v1 whole, which is shorter than its diff:
```python
import jax
import jax.numpy as jnp
from jax import lax
from jax.sharding import PartitionSpec as P

F32 = jnp.float32
BF16 = jnp.bfloat16


def swap(value, axis, bits):
    count = lax.axis_size(axis)
    return lax.ppermute(value, axis, [(i, i ^ bits) for i in range(count)])


def gather_blocks(block, axis):
    count = lax.axis_size(axis)
    blocks = [block] + [None] * (count - 1)
    for k in range(1, count):
        if k & (k - 1) == 0:
            blocks[k] = swap(block, axis, k)
    half = block.shape[0] // 2
    for k in range(1, count):
        if blocks[k] is None:
            low, high = k & -k, 1 << (k.bit_length() - 1)
            first = swap(blocks[k ^ low][:half], axis, low)
            last = swap(blocks[k ^ high][half:], axis, high)
            blocks[k] = jnp.concatenate([first, last], axis=0)
    return blocks


def spread(block, axis):
    return [block] + [swap(block, axis, k) for k in range(1, lax.axis_size(axis))]


def reduce_rows(part):
    count = lax.axis_size("dp")
    me = lax.axis_index("dp")
    rows = part.shape[0] // count
    cut = part.reshape(count // 2, 2, rows, part.shape[1])
    core = lax.rem(me, 2)
    chip = lax.div(me, 2)
    other = swap(lax.dynamic_index_in_dim(cut, 1 - core, 1, keepdims=False), "dp", 1)
    mine = lax.dynamic_index_in_dim(cut, core, 1, keepdims=False)
    both = mine.astype(F32) + other.astype(F32)
    total = lax.dynamic_index_in_dim(both, chip, 0, keepdims=False)
    rounded = both.astype(BF16)
    for k in range(1, count // 2):
        piece = lax.dynamic_index_in_dim(rounded, chip ^ k, 0, keepdims=False)
        total = total + swap(piece, "dp", 2 * k).astype(F32)
    return total


def local(acts, patches, labels, w_first, w_second, w_decode, w_aux, w_class):
    local_acts = acts[0]
    images_here, pix, width = local_acts.shape
    rows_here = images_here * pix
    groups = lax.axis_size("dp")
    me = lax.axis_index("dp")
    section = lax.axis_index("section")
    total_rows = groups * rows_here
    total_images = groups * images_here
    first, second, decode, aux, klass = w_first[0], w_second[0], w_decode[0], w_aux[0], w_class[0]
    classes_here = klass.shape[0]

    target = gather_blocks(patches, "section")
    flat = local_acts.reshape(rows_here, width)
    pre_act = jnp.dot(flat, first, preferred_element_type=F32)
    hidden = jax.nn.relu(pre_act).astype(BF16)
    feature = (flat.astype(F32) + jnp.dot(hidden, second, preferred_element_type=F32)).astype(BF16)
    pooled = jnp.mean(feature.reshape(images_here, pix, width).astype(F32), axis=1).astype(BF16)
    aux_pre = jnp.dot(pooled, aux, preferred_element_type=F32)
    aux_out = jax.nn.relu(aux_pre).astype(BF16)

    sent = jnp.concatenate([aux_out, pooled], axis=1)
    blocks = jnp.stack(spread(sent, "dp"))
    head = aux_out.shape[1]
    all_out = blocks[:, :, :head].reshape(total_images, head)
    all_labels = jnp.stack(spread(labels, "dp")).reshape(total_images)
    logits = jnp.dot(all_out, klass.T, preferred_element_type=F32)
    top = jnp.max(logits, axis=1)
    denom = jnp.sum(jnp.exp(logits - top[:, None]), axis=1)
    stats = jnp.stack(spread(jnp.stack([top, denom]).reshape(2, groups, images_here), "dp"))
    order = jnp.array([[j ^ k for j in range(groups)] for k in range(groups)], jnp.int32)
    stats = jnp.stack([stats[k][:, order[k]] for k in range(groups)]).reshape(groups, 2, total_images)
    all_top = jnp.max(stats[:, 0], axis=0)
    all_denom = jnp.sum(stats[:, 1] * jnp.exp(stats[:, 0] - all_top[None]), axis=0)
    prob = jnp.exp(logits - all_top[:, None]) / all_denom[:, None]
    ids = me * classes_here + jnp.arange(classes_here, dtype=jnp.int32)
    onehot = (all_labels[:, None] == ids[None, :]).astype(F32)
    logit_grad = ((prob - onehot) / total_images**0.5).astype(BF16)
    grad_class = jnp.dot(logit_grad.T, all_out, preferred_element_type=F32)
    back_part = jnp.dot(logit_grad, klass, preferred_element_type=F32).reshape(groups, images_here, head)
    back = back_part[0]
    for k in range(1, groups):
        back = back + swap(back_part[k], "dp", k)
    aux_grad = jnp.where(aux_pre > 0, back, 0.0).astype(BF16)
    pooled_grad = jnp.dot(aux_grad, aux.T, preferred_element_type=F32)

    all_aux_grad = jnp.stack(spread(aux_grad, "dp"))
    rows_aux = width // groups
    all_pooled = lax.dynamic_slice_in_dim(blocks, head + me * rows_aux, rows_aux, 2)
    grad_aux = jnp.sum(
        lax.optimization_barrier(
            jnp.einsum("kia,kib->kab", all_pooled, all_aux_grad, preferred_element_type=F32).astype(BF16)
        ).astype(F32),
        axis=0,
    )

    span = patches.shape[2]
    dec_back = 0.0
    parts = []
    for k in range(len(target)):
        columns = lax.dynamic_slice_in_dim(decode, (section ^ k) * span, span, 1)
        recon = jnp.dot(feature, columns, preferred_element_type=F32)
        recon_grad = ((recon - target[k].reshape(rows_here, span).astype(F32)) / total_rows**0.5).astype(BF16)
        dec_back = dec_back + jnp.dot(recon_grad, columns.T, preferred_element_type=F32)
        parts.append(jnp.dot(feature.T, recon_grad, preferred_element_type=F32).astype(BF16))
    summed = reduce_rows(jnp.concatenate(parts, axis=1)).reshape(width // groups, len(target), span)
    grad_decode = jnp.concatenate(
        [lax.dynamic_index_in_dim(summed, section ^ k, 1, keepdims=False) for k in range(len(target))], axis=1
    )
    feature_grad = (
        (dec_back.reshape(images_here, pix, width) + pooled_grad[:, None, :] / pix)
        .reshape(rows_here, width)
        .astype(BF16)
    )
    hid_back = jnp.dot(feature_grad, second.T, preferred_element_type=F32)
    hidden_grad = jnp.where(pre_act > 0, hid_back, 0.0).astype(BF16)
    grad_first = reduce_rows(jnp.dot(flat.T, hidden_grad, preferred_element_type=F32).astype(BF16))
    grad_second = reduce_rows(jnp.dot(hidden.T, feature_grad, preferred_element_type=F32).astype(BF16))
    return grad_first[None], grad_second[None], grad_decode[None], grad_aux[None], grad_class[None]


def solution(mesh):
    in_specs = (
        P("section", "dp", None, None),
        P("dp", None, "section"),
        P("dp"),
        P("section", None, None),
        P("section", None, None),
        P("section", None, None),
        P("section", None, None),
        P("section", "dp", None),
    )
    out_specs = (P("section", "dp", None),) * 5
    return jax.shard_map(local, mesh=mesh, in_specs=in_specs, out_specs=out_specs, check_vma=False)
```

time: 458 us -> 370 us (0.81)
  waiting for transfers between devices: 274 us -> 28.4 us
  starting transfers between devices: 0.29 us -> 61.5 us
  local copies, waits for them, and re-layouts: 78.4 us -> 130 us
  matrix products: 74.6 us -> 117 us
  between operations: 14.3 us -> 1.39 us
  other arithmetic: 15 us -> 26.9 us
    reduce_scatter x4 -> x0, waiting for transfers between devices: 179 us -> none  [the longest x1 118 us: local(): lax.psum_scatter(jnp.dot(logit_grad.T, aux_out, preferred_element_type=jn...]
    all_gather x2 -> x0, waiting for transfers between devices: 80.6 us -> none  [the longest x1 53.2 us: local(): all_rows = lax.all_gather(class_shard, 'dp', axis=0, tiled=True)]
    ppermute x0 -> x51, starting transfers between devices: none -> 61.5 us  [swap(): return lax.ppermute(value, axis, [(i, i ^ bits) for i in range(count)])]
    dot_general x13 -> x22, matrix products: 74.6 us -> 117 us  [the longest x4 38 us: local(): jnp.dot(recon_grad, columns.T, preferred_element_type=F32)]
    ppermute x0 -> x51, waiting for transfers between devices: none -> 28.4 us  [swap(): return lax.ppermute(value, axis, [(i, i ^ bits) for i in range(count)])]
    add x0 -> x3, local copies, waits for them, and re-layouts: none -> 18.3 us  [the longest x2 18.1 us: local(): dec_back.reshape(images_here, pix, width) + pooled_grad[:, None, :] / pix]
    unnamed x8 -> x0, waiting for transfers between devices: 14.2 us -> none
    unnamed x27 -> x75, local copies, waits for them, and re-layouts: 17.1 us -> 28.6 us
  transfers between devices with their start and end apart: 7 -> 51, of which waited for: 6 -> 14; matrix products, arithmetic and copies ran while one was open for 35% -> 43% of each run, Pallas kernels for 0% -> 0%
where the time goes in v1:
time: 370 us; the launch traced here: 365 us
  local copies, waits for them, and re-layouts  130 us (35%)
  matrix products  117 us (32%)
  starting transfers between devices  61.5 us (17%)
  waiting for transfers between devices  28.4 us (8%)
  other arithmetic  26.9 us (7%)
    ppermute x51, starting transfers between devices, swap(): return lax.ppermute(value, axis, [(i, i ^ bits) for i in range(count)])  61.5 us
    dot_general x4, matrix products, local(): jnp.dot(recon_grad, columns.T, preferred_element_type=F32)  38 us
    convert_element_type x8, local copies, waits for them, and re-layouts, local(): target[k].reshape(rows_here, span).astype(F32)  34.8 us
    unnamed x75, local copies, waits for them, and re-layouts  28.6 us
    ppermute x51, waiting for transfers between devices, swap(): return lax.ppermute(value, axis, [(i, i ^ bits) for i in range(count)])  28.4 us
    dot_general x4, matrix products, local(): recon = jnp.dot(feature, columns, preferred_element_type=F32)  24.9 us
    dot_general x4, matrix products, local(): jnp.dot(feature.T, recon_grad, preferred_element_type=F32).astype(BF16)  19.7 us
    add x2, local copies, waits for them, and re-layouts, local(): dec_back.reshape(images_here, pix, width) + pooled_grad[:, None, :] / pix  18.1 us
  transfers between devices with their start and end apart: 51, of which 14 were waited for; matrix products, arithmetic and copies ran while one was open for 43% of the time, Pallas kernels for 0%

profile of v1, /device:TPU:0, one launch (start us, length us, event | category | flops | bytes accessed | tf_op | source)
XLA Modules:
  0.0 364.9 jit_solution(7173796854817596228)
XLA Ops:
  0.6 9.2 %copy.37 = bf16[1,16,196,1024]{3,2,1,0:T(8,128)(2,1)} copy(bf16[1,16,196,1024]{3,1,2,0:T(8,128)(2,1)} %param.9) | data formatting | bytes 12845056 | tf_op args[0]
  9.9 8.5 %reshape_squeeze.3 = bf16[3136,1024]{1,0:T(8,128)(2,1)} reshape(bf16[1,16,196,1024]{3,2,1,0:T(8,128)(2,1)} %copy.37) | data formatting | bytes 12845056 | tf_op jit(solution)/shard_map/reshape;squeeze | solution.py:66
  18.4 4.8 %fusion.28 = f32[3136,256]{1,0:T(8,128)S(1)} fusion(bf16[3136,1024]{1,0:T(8,128)(2,1)} %reshape_squeeze.3, bf16[1,1024,256]{2,1,0:T(8,128)(2,1)S(1)} %copy-done.24), kind=kOutput, calls=%fused_computation.60 | convolution fusion | flops 1644167168 | bytes 10158080 | tf_op jit(solution)/shard_map/dot_general | solution.py:67
  24.9 4.6 %add_convert_fusion.1 = bf16[3136,1024]{1,0:T(8,128)(2,1)} fusion(bf16[3136,1024]{1,0:T(8,128)(2,1)S(1)} %copy-done.1, f32[3136,256]{1,0:T(8,128)S(1)} %fusion.28, bf16[1,256,1024]{2,1,0:T(8,128)(2,1)S(1)} %copy-done.8), kind=kOutput, calls=%fused_computation.9 | convolution fusion | flops 1655406592 | bytes 16580608 | tf_op jit(solution)/shard_map/dot_general | solution.py:69
  29.5 9.0 %reshape.336 = f32[16,196,1024]{2,1,0:T(8,128)} reshape(bf16[3136,1024]{1,0:T(8,128)(2,1)} %add_convert_fusion.1) | data formatting | bytes 19267584 | tf_op jit(solution)/shard_map/convert_element_type | solution.py:70
  38.5 6.5 %reduce_sum.36 = f32[16,1024]{1,0:T(8,128)S(1)} reduce(f32[16,196,1024]{2,1,0:T(8,128)} %reshape.336, f32[]{:T(128)} %constant.113.clone.1), dimensions={1}, to_apply=%region_0.1 | reduce | flops 3194880 | bytes 12910596 | tf_op jit(solution)/shard_map/reduce_sum | solution.py:70
  45.8 2.6 collective-permute-start.5
  50.6 3.9 %copy.38 = f32[16,196,192]{1,0,2:T(8,128)} copy(bf16[16,196,192]{1,2,0:T(8,128)(2,1)} %param.10) | data formatting | bytes 3612672 | tf_op jit(solution)/shard_map/convert_element_type | solution.py:115
  54.5 4.9 %reshape.332 = f32[3136,192]{0,1:T(8,128)} reshape(f32[16,196,192]{1,0,2:T(8,128)} %copy.38) | data formatting | bytes 4816896 | tf_op jit(solution)/shard_map/convert_element_type | solution.py:115
  59.4 5.7 %fusion.2 = bf16[3136,192]{0,1:T(8,128)(2,1)S(1)} fusion(f32[3136,192]{0,1:T(8,128)} %reshape.332, bf16[3136,1024]{1,0:T(8,128)(2,1)} %add_convert_fusion.1, bf16[1,1024,768]{2,1,0:T(8,128)(2,1)S(1)} %copy-done, s32[]{:T(128)S(6)} %select_n.155), kind=kOutput, calls=%fused_computation.14 | convolution fusion | flops 1234931712 | bytes 10559492 | tf_op jit(solution)/shard_map/dot_general | solution.py:114
  65.1 5.2 %convolution_convert_fusion.6 = bf16[1024,192]{0,1:T(8,128)(2,1)} fusion(bf16[3136,192]{0,1:T(8,128)(2,1)S(1)} %fusion.2, bf16[3136,1024]{1,0:T(8,128)(2,1)} %add_convert_fusion.1), kind=kOutput, calls=%fused_computation.34 | convolution fusion | flops 1233321984 | bytes 8019968 | tf_op jit(solution)/shard_map/dot_general | solution.py:117
  70.3 6.8 %fusion.22 = f32[3136,1024]{1,0:T(8,128)} fusion(bf16[3136,192]{0,1:T(8,128)(2,1)S(1)} %fusion.2, bf16[1,1024,768]{2,1,0:T(8,128)(2,1)S(1)} %copy-done, s32[]{:T(128)S(6)} %select_n.155), kind=kOutput, calls=%fused_computation.55 | convolution fusion | flops 1233125376 | bytes 14598148 | tf_op jit(solution)/shard_map/dot_general | solution.py:116
  80.2 6.4 %fusion.12 = f32[3136,192]{0,1:T(8,128)} fusion(bf16[3136,1024]{1,0:T(8,128)(2,1)} %add_convert_fusion.1, bf16[1,1024,768]{2,1,0:T(8,128)(2,1)S(1)} %copy-done, s32[]{:T(128)S(6)} %select_n.158), kind=kOutput, calls=%fused_computation.45 | convolution fusion | flops 1233125376 | bytes 9355268 | tf_op jit(solution)/shard_map/dot_general | solution.py:114
  86.6 6.4 %fusion.16 = f32[3136,192]{0,1:T(8,128)} fusion(bf16[3136,1024]{1,0:T(8,128)(2,1)} %add_convert_fusion.1, bf16[1,1024,768]{2,1,0:T(8,128)(2,1)S(1)} %copy-done, s32[]{:T(128)S(6)} %select_n.157), kind=kOutput, calls=%fused_computation.49 | convolution fusion | flops 1233125376 | bytes 9355268 | tf_op jit(solution)/shard_map/dot_general | solution.py:114
  93.7 2.7 collective-permute-start.21
  98.7 2.9 collective-permute-start.23
  147.6 6.4 %fusion.20 = f32[3136,192]{0,1:T(8,128)} fusion(bf16[3136,1024]{1,0:T(8,128)(2,1)} %add_convert_fusion.1, bf16[1,1024,768]{2,1,0:T(8,128)(2,1)S(1)} %copy-done, s32[]{:T(128)S(6)} %select_n.156), kind=kOutput, calls=%fused_computation.53 | convolution fusion | flops 1233125376 | bytes 9355268 | tf_op jit(solution)/shard_map/dot_general | solution.py:114
  155.6 2.8 collective-permute-start.29
  161.6 2.8 convolution_bitcast_fusion
  170.6 6.4 %add.265 = f32[16,196,1024]{2,1,0:T(8,128)} broadcast(f32[16,1024]{1,0:T(8,128)S(1)} %convolution_multiply_fusion), dimensions={0,2} | broadcast | bytes 12910592 | tf_op jit(solution)/shard_map/add | solution.py:123
  177.0 11.7 %add.266 = f32[3136,1024]{1,0:T(8,128)} reshape(f32[16,196,1024]{2,1,0:T(8,128)} %add.265) | data formatting | bytes 25690112 | tf_op jit(solution)/shard_map/add | solution.py:123
  188.9 2.6 collective-permute-start.48
  205.4 4.0 %copy.40 = f32[16,196,192]{1,0,2:T(8,128)} copy(bf16[16,196,192]{1,2,0:T(8,128)(2,1)} %collective-permute-done.1) | data formatting | bytes 3612672 | tf_op jit(solution)/shard_map/convert_element_type | solution.py:115
  209.4 4.9 %reshape.334 = f32[3136,192]{0,1:T(8,128)} reshape(f32[16,196,192]{1,0,2:T(8,128)} %copy.40) | data formatting | bytes 4816896 | tf_op jit(solution)/shard_map/convert_element_type | solution.py:115
  214.2 2.7 multiply_convert_fusion.1
  216.9 4.3 %convolution_convert_fusion.4 = bf16[1024,192]{0,1:T(8,128)(2,1)S(1)} fusion(bf16[3136,192]{0,1:T(8,128)(2,1)S(1)} %multiply_convert_fusion.1, bf16[3136,1024]{1,0:T(8,128)(2,1)} %add_convert_fusion.1), kind=kOutput, calls=%fused_computation.32 | convolution fusion | flops 1233321984 | bytes 8019968 | tf_op jit(solution)/shard_map/dot_general | solution.py:117
  221.3 6.9 %fusion.14 = f32[3136,1024]{1,0:T(8,128)} fusion(bf16[3136,192]{0,1:T(8,128)(2,1)S(1)} %multiply_convert_fusion.1, bf16[1,1024,768]{2,1,0:T(8,128)(2,1)S(1)} %copy-done, s32[]{:T(128)S(6)} %select_n.157), kind=kOutput, calls=%fused_computation.47 | convolution fusion | flops 1233125376 | bytes 14598148 | tf_op jit(solution)/shard_map/dot_general | solution.py:116
  231.8 4.0 %copy.39 = f32[16,196,192]{1,0,2:T(8,128)} copy(bf16[16,196,192]{1,2,0:T(8,128)(2,1)} %collective-permute-done) | data formatting | bytes 3612672 | tf_op jit(solution)/shard_map/convert_element_type | solution.py:115
  235.7 4.7 %reshape.333 = f32[3136,192]{0,1:T(8,128)} reshape(f32[16,196,192]{1,0,2:T(8,128)} %copy.39) | data formatting | bytes 4816896 | tf_op jit(solution)/shard_map/convert_element_type | solution.py:115
  240.5 2.7 multiply_convert_fusion.2
  243.2 5.0 %convolution_convert_fusion.5 = bf16[1024,192]{0,1:T(8,128)(2,1)} fusion(bf16[3136,192]{0,1:T(8,128)(2,1)S(1)} %multiply_convert_fusion.2, bf16[3136,1024]{1,0:T(8,128)(2,1)} %add_convert_fusion.1), kind=kOutput, calls=%fused_computation.33 | convolution fusion | flops 1233321984 | bytes 8019968 | tf_op jit(solution)/shard_map/dot_general | solution.py:117
  248.2 6.8 %fusion.18 = f32[3136,1024]{1,0:T(8,128)} fusion(bf16[3136,192]{0,1:T(8,128)(2,1)S(1)} %multiply_convert_fusion.2, bf16[1,1024,768]{2,1,0:T(8,128)(2,1)S(1)} %copy-done, s32[]{:T(128)S(6)} %select_n.156), kind=kOutput, calls=%fused_computation.51 | convolution fusion | flops 1233125376 | bytes 14598148 | tf_op jit(solution)/shard_map/dot_general | solution.py:116
  255.4 3.5 copy.41
  258.9 4.9 %reshape.335 = f32[3136,192]{0,1:T(8,128)} reshape(f32[16,196,192]{1,0,2:T(8,128)} %copy.41) | data formatting | bytes 4816896 | tf_op jit(solution)/shard_map/convert_element_type | solution.py:115
  263.8 2.7 multiply_convert_fusion
  266.5 5.1 %convolution_convert_fusion.3 = bf16[1024,192]{0,1:T(8,128)(2,1)} fusion(bf16[3136,192]{0,1:T(8,128)(2,1)S(1)} %multiply_convert_fusion, bf16[3136,1024]{1,0:T(8,128)(2,1)} %add_convert_fusion.1), kind=kOutput, calls=%fused_computation.31 | convolution fusion | flops 1233321984 | bytes 8019968 | tf_op jit(solution)/shard_map/dot_general | solution.py:117
  271.7 17.4 %add_convert_fusion = bf16[3136,1024]{1,0:T(8,128)(2,1)S(1)} fusion(f32[3136,1024]{1,0:T(8,128)} %add.266, f32[3136,1024]{1,0:T(8,128)} %fusion.14, f32[3136,1024]{1,0:T(8,128)} %fusion.22, f32[3136,1024]{1,0:T(8,128)} %fusion.18, bf16[3136,192]{0,1:T(8,128)(2,1)S(1)} %multiply_convert_fusion, bf16[1,1024,768]{2,1,0:T(8,128)(2,1)S(1)} %copy-done, ...), kind=kOutput, calls=%fused_computation.8 | convolution fusion | flops 1249181696 | bytes 59555844 | tf_op jit(solution)/shard_map/dot_general | solution.py:116
  289.1 2.7 copy-done.4
  291.8 2.7 convolution_convert_fusion.1
  294.5 12.8 %fusion.7 = bf16[1024,256]{0,1:T(8,128)(2,1)} fusion(bf16[3136,1024]{1,0:T(8,128)(2,1)} %reshape_squeeze.3, bf16[3136,1024]{1,0:T(8,128)(2,1)} %copy-done.4, f32[3136,256]{1,0:T(8,128)} %copy-done.2, bf16[1,256,1024]{2,1,0:T(8,128)(2,1)S(1)} %copy-done.9), kind=kOutput, calls=%fused_computation.35 | convolution fusion | flops 3291004928 | bytes 17104896 | tf_op jit(solution)/shard_map/dot_general | solution.py:129
  309.7 3.1 reshape.330
  314.5 4.9 %constant_dynamic-slice_fusion.1 = (bf16[4,1,128,768]{2,1,0,3:T(2,128)(2,1)}, bf16[4,1,128,768]{2,1,0,3:T(2,128)(2,1)}) fusion(bf16[4,2,128,768]{2,1,0,3:T(2,128)(2,1)S(1)} %reshape.330, s32[]{:T(128)S(6)} %select_n.169, s32[]{:T(128)S(6)} %select_n.170), kind=kLoop, calls=%fused_computation.140 | loop fusion | bytes 3145736 | tf_op jit(solution)/shard_map/jit(dynamic_index_in_dim)/dynamic_slice | solution.py:43
  319.3 4.8 %copy.63 = bf16[4,1,128,768]{3,2,0,1:T(8,128)(2,1)} copy(bf16[4,1,128,768]{2,1,0,3:T(2,128)(2,1)} %get-tuple-element.17) | data formatting | bytes 1572864
  324.7 2.9 copy.62
  334.4 2.8 collective-permute-start.39
  343.9 3.9 %collective-permute-start.41 = (bf16[128,768]{1,0:T(8,128)(2,1)S(1)}, bf16[128,768]{1,0:T(8,128)(2,1)S(1)}, u32[]{:S(2)}, u32[]{:S(2)}) collective-permute-start(bf16[128,768]{1,0:T(8,128)(2,1)S(1)} %get-tuple-element.18), channel_id=1, source_target_pairs={{0,2},{1,3},{2,0},{3,1},{4,6},{5,7},{6,4},{7,5},{8,10},{9,11},{10,... | collective-permute-start | bytes 589832 | tf_op jit(solution)/shard_map/ppermute | solution.py:12
  351.0 3.4 collective-permute-done.41
  354.3 9.0 %collective-permute-done.42 = bf16[128,768]{1,0:T(8,128)(2,1)S(1)} collective-permute-done((bf16[128,768]{1,0:T(8,128)(2,1)S(1)}, bf16[128,768]{1,0:T(8,128)(2,1)S(1)}, u32[]{:S(2)}, u32[]{:S(2)}) %collective-permute-start.42) | collective-permute-done | bytes 196640 | tf_op jit(solution)/shard_map/ppermute | solution.py:12
  (241 shorter events, 107.8 us)
Async XLA Ops:
  45.3 61.7 %collective-permute-start.4 = (bf16[16,1536]{1,0:T(8,128)(2,1)S(1)}, bf16[16,1536]{1,0:T(8,128)(2,1)S(1)}, u32[]{:S(2)}, u32[]{:S(2)}) collective-permute-start(bf16[16,1536]{1,0:T(8,128)(2,1)S(1)} %pad_maximum_fusion.1), channel_id=1, source_target_pairs={{0,1},{1,0},{2,3},{3,2},{4,5},{5,4},{6,7},{7,6},{8,9},{9,8},{10,11... | collective-permute-start | bytes 147464 | tf_op jit(solution)/shard_map/ppermute | solution.py:12
  45.8 62.7 %collective-permute-start.5 = (bf16[16,1536]{1,0:T(8,128)(2,1)S(1)}, bf16[16,1536]{1,0:T(8,128)(2,1)S(1)}, u32[]{:S(2)}, u32[]{:S(2)}) collective-permute-start(bf16[16,1536]{1,0:T(8,128)(2,1)S(1)} %pad_maximum_fusion.1), channel_id=1, source_target_pairs={{0,2},{1,3},{2,0},{3,1},{4,6},{5,7},{6,4},{7,5},{8,10},{9,11},{10,... | collective-permute-start | bytes 147464 | tf_op jit(solution)/shard_map/ppermute | solution.py:12
  48.4 62.5 %collective-permute-start.6 = (bf16[16,1536]{1,0:T(8,128)(2,1)S(1)}, bf16[16,1536]{1,0:T(8,128)(2,1)S(1)}, u32[]{:S(2)}, u32[]{:S(2)}) collective-permute-start(bf16[16,1536]{1,0:T(8,128)(2,1)S(1)} %pad_maximum_fusion.1), channel_id=1, source_target_pairs={{0,3},{1,2},{2,1},{3,0},{4,7},{5,6},{6,5},{7,4},{8,11},{9,10},{10,... | collective-permute-start | bytes 147464 | tf_op jit(solution)/shard_map/ppermute | solution.py:12
  48.5 45.2 %collective-permute-start.18 = (s32[16]{0:T(128)S(1)}, s32[16]{0:T(128)S(1)}, u32[]{:S(2)}, u32[]{:S(2)}) collective-permute-start(s32[16]{0:T(128)S(1)} %copy-done.16), channel_id=1, source_target_pairs={{0,1},{1,0},{2,3},{3,2},{4,5},{5,4},{6,7},{7,6},{8,9},{9,8},{10,11... | collective-permute-start | bytes 200 | tf_op jit(solution)/shard_map/ppermute | solution.py:12
  48.6 45.1 %collective-permute-start.19 = (s32[16]{0:T(128)S(1)}, s32[16]{0:T(128)S(1)}, u32[]{:S(2)}, u32[]{:S(2)}) collective-permute-start(s32[16]{0:T(128)S(1)} %copy-done.16), channel_id=1, source_target_pairs={{0,2},{1,3},{2,0},{3,1},{4,6},{5,7},{6,4},{7,5},{8,10},{9,11},{10,... | collective-permute-start | bytes 200 | tf_op jit(solution)/shard_map/ppermute | solution.py:12
  93.7 5.0 %collective-permute-start.21 = (s32[16]{0:T(128)S(1)}, s32[16]{0:T(128)S(1)}, u32[]{:S(2)}, u32[]{:S(2)}) collective-permute-start(s32[16]{0:T(128)S(1)} %copy-done.16), channel_id=1, source_target_pairs={{0,4},{1,5},{2,6},{3,7},{4,0},{5,1},{6,2},{7,3},{8,12},{9,13},{10,... | collective-permute-start | bytes 200 | tf_op jit(solution)/shard_map/ppermute | solution.py:12
  96.6 5.0 %collective-permute-start.22 = (s32[16]{0:T(128)S(1)}, s32[16]{0:T(128)S(1)}, u32[]{:S(2)}, u32[]{:S(2)}) collective-permute-start(s32[16]{0:T(128)S(1)} %copy-done.16), channel_id=1, source_target_pairs={{0,5},{1,4},{2,7},{3,6},{4,1},{5,0},{6,3},{7,2},{8,13},{9,12},{10,... | collective-permute-start | bytes 200 | tf_op jit(solution)/shard_map/ppermute | solution.py:12
  98.7 5.3 %collective-permute-start.23 = (s32[16]{0:T(128)S(1)}, s32[16]{0:T(128)S(1)}, u32[]{:S(2)}, u32[]{:S(2)}) collective-permute-start(s32[16]{0:T(128)S(1)} %copy-done.16), channel_id=1, source_target_pairs={{0,6},{1,7},{2,4},{3,5},{4,2},{5,3},{6,0},{7,1},{8,14},{9,15},{10,... | collective-permute-start | bytes 200 | tf_op jit(solution)/shard_map/ppermute | solution.py:12
  104.1 6.9 %collective-permute-start.7 = (bf16[16,1536]{1,0:T(8,128)(2,1)S(1)}, bf16[16,1536]{1,0:T(8,128)(2,1)S(1)}, u32[]{:S(2)}, u32[]{:S(2)}) collective-permute-start(bf16[16,1536]{1,0:T(8,128)(2,1)S(1)} %pad_maximum_fusion.1), channel_id=1, source_target_pairs={{0,4},{1,5},{2,6},{3,7},{4,0},{5,1},{6,2},{7,3},{8,12},{9,13},{10,... | collective-permute-start | bytes 147464 | tf_op jit(solution)/shard_map/ppermute | solution.py:12
  106.4 5.4 %collective-permute-start.8 = (bf16[16,1536]{1,0:T(8,128)(2,1)S(1)}, bf16[16,1536]{1,0:T(8,128)(2,1)S(1)}, u32[]{:S(2)}, u32[]{:S(2)}) collective-permute-start(bf16[16,1536]{1,0:T(8,128)(2,1)S(1)} %pad_maximum_fusion.1), channel_id=1, source_target_pairs={{0,5},{1,4},{2,7},{3,6},{4,1},{5,0},{6,3},{7,2},{8,13},{9,12},{10,... | collective-permute-start | bytes 147464 | tf_op jit(solution)/shard_map/ppermute | solution.py:12
  107.0 6.2 %collective-permute-start.9 = (bf16[16,1536]{1,0:T(8,128)(2,1)S(1)}, bf16[16,1536]{1,0:T(8,128)(2,1)S(1)}, u32[]{:S(2)}, u32[]{:S(2)}) collective-permute-start(bf16[16,1536]{1,0:T(8,128)(2,1)S(1)} %pad_maximum_fusion.1), channel_id=1, source_target_pairs={{0,6},{1,7},{2,4},{3,5},{4,2},{5,3},{6,0},{7,1},{8,14},{9,15},{10,... | collective-permute-start | bytes 147464 | tf_op jit(solution)/shard_map/ppermute | solution.py:12
  108.5 5.4 %collective-permute-start.10 = (bf16[16,1536]{1,0:T(8,128)(2,1)S(1)}, bf16[16,1536]{1,0:T(8,128)(2,1)S(1)}, u32[]{:S(2)}, u32[]{:S(2)}) collective-permute-start(bf16[16,1536]{1,0:T(8,128)(2,1)S(1)} %pad_maximum_fusion.1), channel_id=1, source_target_pairs={{0,7},{1,6},{2,5},{3,4},{4,3},{5,2},{6,1},{7,0},{8,15},{9,14},{10,... | collective-permute-start | bytes 147464 | tf_op jit(solution)/shard_map/ppermute | solution.py:12
  117.2 7.0 %collective-permute-start.11 = (f32[2,8,16]{2,0,1:T(2,128)S(1)}, f32[2,8,16]{2,0,1:T(2,128)}, u32[]{:S(2)}, u32[]{:S(2)}) collective-permute-start(f32[2,8,16]{2,0,1:T(2,128)S(1)} %pad_maximum_fusion.2), channel_id=1, source_target_pairs={{0,1},{1,0},{2,3},{3,2},{4,5},{5,4},{6,7},{7,6},{8,9},{9,8},{10,11... | collective-permute-start | bytes 3080 | tf_op jit(solution)/shard_map/ppermute | solution.py:12
  119.1 7.6 %collective-permute-start.12 = (f32[2,8,16]{2,0,1:T(2,128)S(1)}, f32[2,8,16]{2,0,1:T(2,128)}, u32[]{:S(2)}, u32[]{:S(2)}) collective-permute-start(f32[2,8,16]{2,0,1:T(2,128)S(1)} %pad_maximum_fusion.2), channel_id=1, source_target_pairs={{0,2},{1,3},{2,0},{3,1},{4,6},{5,7},{6,4},{7,5},{8,10},{9,11},{10,... | collective-permute-start | bytes 3080 | tf_op jit(solution)/shard_map/ppermute | solution.py:12
  119.3 11.7 %collective-permute-start.13 = (f32[2,8,16]{2,0,1:T(2,128)S(1)}, f32[2,8,16]{2,0,1:T(2,128)}, u32[]{:S(2)}, u32[]{:S(2)}) collective-permute-start(f32[2,8,16]{2,0,1:T(2,128)S(1)} %pad_maximum_fusion.2), channel_id=1, source_target_pairs={{0,3},{1,2},{2,1},{3,0},{4,7},{5,6},{6,5},{7,4},{8,11},{9,10},{10,... | collective-permute-start | bytes 3080 | tf_op jit(solution)/shard_map/ppermute | solution.py:12
  120.5 12.6 %collective-permute-start.14 = (f32[2,8,16]{2,0,1:T(2,128)S(1)}, f32[2,8,16]{2,0,1:T(2,128)}, u32[]{:S(2)}, u32[]{:S(2)}) collective-permute-start(f32[2,8,16]{2,0,1:T(2,128)S(1)} %pad_maximum_fusion.2), channel_id=1, source_target_pairs={{0,4},{1,5},{2,6},{3,7},{4,0},{5,1},{6,2},{7,3},{8,12},{9,13},{10,... | collective-permute-start | bytes 3080 | tf_op jit(solution)/shard_map/ppermute | solution.py:12
  122.2 12.9 %collective-permute-start.15 = (f32[2,8,16]{2,0,1:T(2,128)S(1)}, f32[2,8,16]{2,0,1:T(2,128)}, u32[]{:S(2)}, u32[]{:S(2)}) collective-permute-start(f32[2,8,16]{2,0,1:T(2,128)S(1)} %pad_maximum_fusion.2), channel_id=1, source_target_pairs={{0,5},{1,4},{2,7},{3,6},{4,1},{5,0},{6,3},{7,2},{8,13},{9,12},{10,... | collective-permute-start | bytes 3080 | tf_op jit(solution)/shard_map/ppermute | solution.py:12
  124.1 13.0 %collective-permute-start.16 = (f32[2,8,16]{2,0,1:T(2,128)S(1)}, f32[2,8,16]{2,0,1:T(2,128)}, u32[]{:S(2)}, u32[]{:S(2)}) collective-permute-start(f32[2,8,16]{2,0,1:T(2,128)S(1)} %pad_maximum_fusion.2), channel_id=1, source_target_pairs={{0,6},{1,7},{2,4},{3,5},{4,2},{5,3},{6,0},{7,1},{8,14},{9,15},{10,... | collective-permute-start | bytes 3080 | tf_op jit(solution)/shard_map/ppermute | solution.py:12
  126.7 11.9 %collective-permute-start.17 = (f32[2,8,16]{2,0,1:T(2,128)S(1)}, f32[2,8,16]{2,0,1:T(2,128)}, u32[]{:S(2)}, u32[]{:S(2)}) collective-permute-start(f32[2,8,16]{2,0,1:T(2,128)S(1)} %pad_maximum_fusion.2), channel_id=1, source_target_pairs={{0,7},{1,6},{2,5},{3,4},{4,3},{5,2},{6,1},{7,0},{8,15},{9,14},{10,... | collective-permute-start | bytes 3080 | tf_op jit(solution)/shard_map/ppermute | solution.py:12
  146.9 11.5 %collective-permute-start.25 = (f32[16,512]{1,0:T(8,128)}, f32[16,512]{1,0:T(8,128)}, u32[]{:S(2)}, u32[]{:S(2)}) collective-permute-start(f32[16,512]{1,0:T(8,128)} %get-tuple-element.35), channel_id=1, source_target_pairs={{0,1},{1,0},{2,3},{3,2},{4,5},{5,4},{6,7},{7,6},{8,9},{9,8},{10,11... | collective-permute-start | bytes 98312 | tf_op jit(solution)/shard_map/ppermute | solution.py:12
  147.6 11.8 %collective-permute-start.26 = (f32[16,512]{1,0:T(8,128)}, f32[16,512]{1,0:T(8,128)}, u32[]{:S(2)}, u32[]{:S(2)}) collective-permute-start(f32[16,512]{1,0:T(8,128)} %get-tuple-element.41), channel_id=1, source_target_pairs={{0,2},{1,3},{2,0},{3,1},{4,6},{5,7},{6,4},{7,5},{8,10},{9,11},{10,... | collective-permute-start | bytes 98312 | tf_op jit(solution)/shard_map/ppermute | solution.py:12
  154.0 10.4 %collective-permute-start.27 = (f32[16,512]{1,0:T(8,128)}, f32[16,512]{1,0:T(8,128)S(1)}, u32[]{:S(2)}, u32[]{:S(2)}) collective-permute-start(f32[16,512]{1,0:T(8,128)} %get-tuple-element.40), channel_id=1, source_target_pairs={{0,3},{1,2},{2,1},{3,0},{4,7},{5,6},{6,5},{7,4},{8,11},{9,10},{10,... | collective-permute-start | bytes 98312 | tf_op jit(solution)/shard_map/ppermute | solution.py:12
  155.4 10.6 %collective-permute-start.28 = (f32[16,512]{1,0:T(8,128)}, f32[16,512]{1,0:T(8,128)S(1)}, u32[]{:S(2)}, u32[]{:S(2)}) collective-permute-start(f32[16,512]{1,0:T(8,128)} %get-tuple-element.39), channel_id=1, source_target_pairs={{0,4},{1,5},{2,6},{3,7},{4,0},{5,1},{6,2},{7,3},{8,12},{9,13},{10,... | collective-permute-start | bytes 98312 | tf_op jit(solution)/shard_map/ppermute | solution.py:12
  155.6 11.9 %collective-permute-start.29 = (f32[16,512]{1,0:T(8,128)}, f32[16,512]{1,0:T(8,128)S(1)}, u32[]{:S(2)}, u32[]{:S(2)}) collective-permute-start(f32[16,512]{1,0:T(8,128)} %get-tuple-element.38), channel_id=1, source_target_pairs={{0,5},{1,4},{2,7},{3,6},{4,1},{5,0},{6,3},{7,2},{8,13},{9,12},{10,... | collective-permute-start | bytes 98312 | tf_op jit(solution)/shard_map/ppermute | solution.py:12
  158.4 9.1 %collective-permute-start.30 = (f32[16,512]{1,0:T(8,128)}, f32[16,512]{1,0:T(8,128)S(1)}, u32[]{:S(2)}, u32[]{:S(2)}) collective-permute-start(f32[16,512]{1,0:T(8,128)} %get-tuple-element.37), channel_id=1, source_target_pairs={{0,6},{1,7},{2,4},{3,5},{4,2},{5,3},{6,0},{7,1},{8,14},{9,15},{10,... | collective-permute-start | bytes 98312 | tf_op jit(solution)/shard_map/ppermute | solution.py:12
  159.4 8.1 %collective-permute-start.31 = (f32[16,512]{1,0:T(8,128)S(1)}, f32[16,512]{1,0:T(8,128)S(1)}, u32[]{:S(2)}, u32[]{:S(2)}) collective-permute-start(f32[16,512]{1,0:T(8,128)S(1)} %get-tuple-element.36), channel_id=1, source_target_pairs={{0,7},{1,6},{2,5},{3,4},{4,3},{5,2},{6,1},{7,0},{8,15},{9,14},{10,... | collective-permute-start | bytes 98312 | tf_op jit(solution)/shard_map/ppermute | solution.py:12
  164.5 37.4 %collective-permute-start.1 = (bf16[16,196,192]{1,2,0:T(8,128)(2,1)}, bf16[16,196,192]{1,2,0:T(8,128)(2,1)}, u32[]{:S(2)}, u32[]{:S(2)}) collective-permute-start(bf16[16,196,192]{1,2,0:T(8,128)(2,1)} %param.10), channel_id=1, source_target_pairs={{0,16},{8,24},{16,0},{24,8},{1,17},{9,25},{17,1},{25,9},{2,18},{10... | collective-permute-start | bytes 3612680 | tf_op jit(solution)/shard_map/ppermute | solution.py:12
  166.0 62.1 %collective-permute-start = (bf16[16,196,192]{1,2,0:T(8,128)(2,1)}, bf16[16,196,192]{1,2,0:T(8,128)(2,1)}, u32[]{:S(2)}, u32[]{:S(2)}) collective-permute-start(bf16[16,196,192]{1,2,0:T(8,128)(2,1)} %param.10), channel_id=1, source_target_pairs={{0,8},{8,0},{16,24},{24,16},{1,9},{9,1},{17,25},{25,17},{2,10},{10... | collective-permute-start | bytes 3612680 | tf_op jit(solution)/shard_map/ppermute | solution.py:12
  168.3 20.4 %collective-permute-start.44 = (bf16[16,512]{1,0:T(8,128)(2,1)S(1)}, bf16[16,512]{1,0:T(8,128)(2,1)S(1)}, u32[]{:S(2)}, u32[]{:S(2)}) collective-permute-start(bf16[16,512]{1,0:T(8,128)(2,1)S(1)} %get-tuple-element.11), channel_id=1, source_target_pairs={{0,1},{1,0},{2,3},{3,2},{4,5},{5,4},{6,7},{7,6},{8,9},{9,8},{10,11... | collective-permute-start | bytes 49160 | tf_op jit(solution)/shard_map/ppermute | solution.py:12
  168.6 20.3 %collective-permute-start.45 = (bf16[16,512]{1,0:T(8,128)(2,1)S(1)}, bf16[16,512]{1,0:T(8,128)(2,1)S(1)}, u32[]{:S(2)}, u32[]{:S(2)}) collective-permute-start(bf16[16,512]{1,0:T(8,128)(2,1)S(1)} %get-tuple-element.11), channel_id=1, source_target_pairs={{0,2},{1,3},{2,0},{3,1},{4,6},{5,7},{6,4},{7,5},{8,10},{9,11},{10,... | collective-permute-start | bytes 49160 | tf_op jit(solution)/shard_map/ppermute | solution.py:12
  168.6 22.9 %collective-permute-start.46 = (bf16[16,512]{1,0:T(8,128)(2,1)S(1)}, bf16[16,512]{1,0:T(8,128)(2,1)S(1)}, u32[]{:S(2)}, u32[]{:S(2)}) collective-permute-start(bf16[16,512]{1,0:T(8,128)(2,1)S(1)} %get-tuple-element.11), channel_id=1, source_target_pairs={{0,3},{1,2},{2,1},{3,0},{4,7},{5,6},{6,5},{7,4},{8,11},{9,10},{10,... | collective-permute-start | bytes 49160 | tf_op jit(solution)/shard_map/ppermute | solution.py:12
  188.9 6.1 %collective-permute-start.48 = (bf16[16,512]{1,0:T(8,128)(2,1)S(1)}, bf16[16,512]{1,0:T(8,128)(2,1)S(1)}, u32[]{:S(2)}, u32[]{:S(2)}) collective-permute-start(bf16[16,512]{1,0:T(8,128)(2,1)S(1)} %get-tuple-element.11), channel_id=1, source_target_pairs={{0,5},{1,4},{2,7},{3,6},{4,1},{5,0},{6,3},{7,2},{8,13},{9,12},{10,... | collective-permute-start | bytes 49160 | tf_op jit(solution)/shard_map/ppermute | solution.py:12
  191.5 5.5 %collective-permute-start.49 = (bf16[16,512]{1,0:T(8,128)(2,1)S(1)}, bf16[16,512]{1,0:T(8,128)(2,1)S(1)}, u32[]{:S(2)}, u32[]{:S(2)}) collective-permute-start(bf16[16,512]{1,0:T(8,128)(2,1)S(1)} %get-tuple-element.11), channel_id=1, source_target_pairs={{0,6},{1,7},{2,4},{3,5},{4,2},{5,3},{6,0},{7,1},{8,14},{9,15},{10,... | collective-permute-start | bytes 49160 | tf_op jit(solution)/shard_map/ppermute | solution.py:12
  193.4 5.0 %collective-permute-start.50 = (bf16[16,512]{1,0:T(8,128)(2,1)S(1)}, bf16[16,512]{1,0:T(8,128)(2,1)S(1)}, u32[]{:S(2)}, u32[]{:S(2)}) collective-permute-start(bf16[16,512]{1,0:T(8,128)(2,1)S(1)} %get-tuple-element.11), channel_id=1, source_target_pairs={{0,7},{1,6},{2,5},{3,4},{4,3},{5,2},{6,1},{7,0},{8,15},{9,14},{10,... | collective-permute-start | bytes 49160 | tf_op jit(solution)/shard_map/ppermute | solution.py:12
  203.9 51.2 %collective-permute-start.2 = (bf16[8,196,192]{1,2,0:T(8,128)(2,1)}, bf16[8,196,192]{1,2,0:T(8,128)(2,1)S(1)}, u32[]{:S(2)}, u32[]{:S(2)}) collective-permute-start(bf16[8,196,192]{1,2,0:T(8,128)(2,1)} %slice.109), channel_id=1, source_target_pairs={{0,8},{8,0},{16,24},{24,16},{1,9},{9,1},{17,25},{25,17},{2,10},{10... | collective-permute-start | bytes 1806344 | tf_op jit(solution)/shard_map/ppermute | solution.py:12
  230.2 24.8 %collective-permute-start.3 = (bf16[8,196,192]{1,2,0:T(8,128)(2,1)}, bf16[8,196,192]{1,2,0:T(8,128)(2,1)S(1)}, u32[]{:S(2)}, u32[]{:S(2)}) collective-permute-start(bf16[8,196,192]{1,2,0:T(8,128)(2,1)} %slice.110), channel_id=1, source_target_pairs={{0,16},{8,24},{16,0},{24,8},{1,17},{9,25},{17,1},{25,9},{2,18},{10... | collective-permute-start | bytes 1806344 | tf_op jit(solution)/shard_map/ppermute | solution.py:12
  314.5 17.2 %collective-permute-start.36 = (bf16[4,32,1024]{2,1,0:T(8,128)(2,1)}, bf16[4,32,1024]{2,1,0:T(8,128)(2,1)}, u32[]{:S(2)}, u32[]{:S(2)}) collective-permute-start(bf16[4,32,1024]{2,1,0:T(8,128)(2,1)} %dynamic-slice_bitcast_fusion), channel_id=1, source_target_pairs={{0,1},{1,0},{2,3},{3,2},{4,5},{5,4},{6,7},{7,6},{8,9},{9,8},{10,11... | collective-permute-start | bytes 786440 | tf_op jit(solution)/shard_map/ppermute | solution.py:12
  324.1 18.4 %collective-permute-start.40 = (bf16[4,128,768]{2,1,0:T(8,128)(2,1)}, bf16[4,128,768]{2,1,0:T(8,128)(2,1)}, u32[]{:S(2)}, u32[]{:S(2)}) collective-permute-start(bf16[4,128,768]{2,1,0:T(8,128)(2,1)} %bitcast.217), channel_id=1, source_target_pairs={{0,1},{1,0},{2,3},{3,2},{4,5},{5,4},{6,7},{7,6},{8,9},{9,8},{10,11... | collective-permute-start | bytes 2359304 | tf_op jit(solution)/shard_map/ppermute | solution.py:12
  331.2 6.1 %collective-permute-start.32 = (bf16[4,128,256]{2,1,0:T(8,128)(2,1)}, bf16[4,128,256]{2,1,0:T(8,128)(2,1)S(1)}, u32[]{:S(2)}, u32[]{:S(2)}) collective-permute-start(bf16[4,128,256]{2,1,0:T(8,128)(2,1)} %bitcast.221), channel_id=1, source_target_pairs={{0,1},{1,0},{2,3},{3,2},{4,5},{5,4},{6,7},{7,6},{8,9},{9,8},{10,11... | collective-permute-start | bytes 786440 | tf_op jit(solution)/shard_map/ppermute | solution.py:12
  332.8 5.7 %collective-permute-start.37 = (bf16[32,1024]{1,0:T(8,128)(2,1)S(1)}, bf16[32,1024]{1,0:T(8,128)(2,1)S(1)}, u32[]{:S(2)}, u32[]{:S(2)}) collective-permute-start(bf16[32,1024]{1,0:T(8,128)(2,1)S(1)} %get-tuple-element.29), channel_id=1, source_target_pairs={{0,2},{1,3},{2,0},{3,1},{4,6},{5,7},{6,4},{7,5},{8,10},{9,11},{10,... | collective-permute-start | bytes 196616 | tf_op jit(solution)/shard_map/ppermute | solution.py:12
  332.9 8.7 %collective-permute-start.38 = (bf16[32,1024]{1,0:T(8,128)(2,1)S(1)}, bf16[32,1024]{1,0:T(8,128)(2,1)S(1)}, u32[]{:S(2)}, u32[]{:S(2)}) collective-permute-start(bf16[32,1024]{1,0:T(8,128)(2,1)S(1)} %get-tuple-element.31), channel_id=1, source_target_pairs={{0,4},{1,5},{2,6},{3,7},{4,0},{5,1},{6,2},{7,3},{8,12},{9,13},{10,... | collective-permute-start | bytes 196616 | tf_op jit(solution)/shard_map/ppermute | solution.py:12
  334.4 7.4 %collective-permute-start.39 = (bf16[32,1024]{1,0:T(8,128)(2,1)S(1)}, bf16[32,1024]{1,0:T(8,128)(2,1)S(1)}, u32[]{:S(2)}, u32[]{:S(2)}) collective-permute-start(bf16[32,1024]{1,0:T(8,128)(2,1)S(1)} %get-tuple-element.30), channel_id=1, source_target_pairs={{0,6},{1,7},{2,4},{3,5},{4,2},{5,3},{6,0},{7,1},{8,14},{9,15},{10,... | collective-permute-start | bytes 196616 | tf_op jit(solution)/shard_map/ppermute | solution.py:12
  337.4 10.7 %collective-permute-start.33 = (bf16[128,256]{1,0:T(8,128)(2,1)S(1)}, bf16[128,256]{1,0:T(8,128)(2,1)S(1)}, u32[]{:S(2)}, u32[]{:S(2)}) collective-permute-start(bf16[128,256]{1,0:T(8,128)(2,1)S(1)} %get-tuple-element.32), channel_id=1, source_target_pairs={{0,2},{1,3},{2,0},{3,1},{4,6},{5,7},{6,4},{7,5},{8,10},{9,11},{10,... | collective-permute-start | bytes 196616 | tf_op jit(solution)/shard_map/ppermute | solution.py:12
  338.5 11.8 %collective-permute-start.34 = (bf16[128,256]{1,0:T(8,128)(2,1)S(1)}, bf16[128,256]{1,0:T(8,128)(2,1)S(1)}, u32[]{:S(2)}, u32[]{:S(2)}) collective-permute-start(bf16[128,256]{1,0:T(8,128)(2,1)S(1)} %get-tuple-element.34), channel_id=1, source_target_pairs={{0,4},{1,5},{2,6},{3,7},{4,0},{5,1},{6,2},{7,3},{8,12},{9,13},{10,... | collective-permute-start | bytes 196616 | tf_op jit(solution)/shard_map/ppermute | solution.py:12
  341.5 8.7 %collective-permute-start.35 = (bf16[128,256]{1,0:T(8,128)(2,1)S(1)}, bf16[128,256]{1,0:T(8,128)(2,1)S(1)}, u32[]{:S(2)}, u32[]{:S(2)}) collective-permute-start(bf16[128,256]{1,0:T(8,128)(2,1)S(1)} %get-tuple-element.33), channel_id=1, source_target_pairs={{0,6},{1,7},{2,4},{3,5},{4,2},{5,3},{6,0},{7,1},{8,14},{9,15},{10,... | collective-permute-start | bytes 196616 | tf_op jit(solution)/shard_map/ppermute | solution.py:12
  343.9 10.4 %collective-permute-start.41 = (bf16[128,768]{1,0:T(8,128)(2,1)S(1)}, bf16[128,768]{1,0:T(8,128)(2,1)S(1)}, u32[]{:S(2)}, u32[]{:S(2)}) collective-permute-start(bf16[128,768]{1,0:T(8,128)(2,1)S(1)} %get-tuple-element.18), channel_id=1, source_target_pairs={{0,2},{1,3},{2,0},{3,1},{4,6},{5,7},{6,4},{7,5},{8,10},{9,11},{10,... | collective-permute-start | bytes 589832 | tf_op jit(solution)/shard_map/ppermute | solution.py:12
  347.8 15.5 %collective-permute-start.42 = (bf16[128,768]{1,0:T(8,128)(2,1)S(1)}, bf16[128,768]{1,0:T(8,128)(2,1)S(1)}, u32[]{:S(2)}, u32[]{:S(2)}) collective-permute-start(bf16[128,768]{1,0:T(8,128)(2,1)S(1)} %get-tuple-element.20), channel_id=1, source_target_pairs={{0,4},{1,5},{2,6},{3,7},{4,0},{5,1},{6,2},{7,3},{8,12},{9,13},{10,... | collective-permute-start | bytes 589832 | tf_op jit(solution)/shard_map/ppermute | solution.py:12
  348.1 15.3 %collective-permute-start.43 = (bf16[128,768]{1,0:T(8,128)(2,1)S(1)}, bf16[128,768]{1,0:T(8,128)(2,1)S(1)}, u32[]{:S(2)}, u32[]{:S(2)}) collective-permute-start(bf16[128,768]{1,0:T(8,128)(2,1)S(1)} %get-tuple-element.19), channel_id=1, source_target_pairs={{0,6},{1,7},{2,4},{3,5},{4,2},{5,3},{6,0},{7,1},{8,14},{9,15},{10,... | collective-permute-start | bytes 589832 | tf_op jit(solution)/shard_map/ppermute | solution.py:12
  (28 other events, 251.5 us)

commit v2 on v1

v2 whole, which is shorter than its diff:
```python
import functools

import jax
import jax.numpy as jnp
from jax import lax
from jax.experimental import pallas as pl
from jax.experimental.pallas import tpu as pltpu
from jax.sharding import PartitionSpec as P

F32 = jnp.float32
BF16 = jnp.bfloat16
STEP = 4
LANES = 128
VMEM_LIMIT = 56 * 1024 * 1024
ROWS_0 = (((0,), (0,)), ((), ()))
COLS_1 = (((1,), (1,)), ((), ()))


def dot(left, right, dims=(((1,), (0,)), ((), ()))):
    return lax.dot_general(left, right, dims, preferred_element_type=F32)


def call(kernel, out_shape, *, flops=0, moved=0, **kwargs):
    return pl.pallas_call(
        kernel,
        out_shape=out_shape,
        compiler_params=pltpu.CompilerParams(vmem_limit_bytes=VMEM_LIMIT),
        cost_estimate=pl.CostEstimate(flops=int(flops), bytes_accessed=int(moved), transcendentals=0),
        **kwargs,
    )


def shape(dims, kind):
    return jax.ShapeDtypeStruct(dims, kind)


def swap(value, axis, bits):
    count = lax.axis_size(axis)
    return lax.ppermute(value, axis, [(i, i ^ bits) for i in range(count)])


def exchange(value, groups=None):
    return lax.all_to_all(value, "dp", 0, 0, axis_index_groups=groups, tiled=True)


def split_width(span):
    full = span // LANES * LANES
    return full, span - full


def pack_kernel(full, rem, patches_ref, *halves):
    for h, half in enumerate(halves):
        count = patches_ref.shape[0] // 2
        base = h * count
        if rem == 64 and full:
            half[:count] = patches_ref[base : base + count, :, :full]
            for j in range(count // 2):
                half[count + j] = jnp.concatenate(
                    [patches_ref[base + j, :, full:], patches_ref[base + count // 2 + j, :, full:]], axis=1
                )
        else:
            half[...] = patches_ref[base : base + count]


def pack(patches):
    images, pix, span = patches.shape
    full, rem = split_width(span)
    half = images // 2
    dims = (half + half // 2, pix, full) if rem == 64 and full else (half, pix, span)
    return call(
        functools.partial(pack_kernel, full, rem),
        [shape(dims, BF16)] * 2,
        moved=2 * patches.size * 2,
        name="pack_patches",
    )(patches)


def gather_patches(halves):
    count = lax.axis_size("section")
    blocks = [list(halves)] + [None] * (count - 1)
    for k in range(1, count):
        if k & (k - 1) == 0:
            blocks[k] = [swap(half, "section", k) for half in halves]
    for k in range(1, count):
        if blocks[k] is None:
            low, high = k & -k, 1 << (k.bit_length() - 1)
            blocks[k] = [swap(blocks[k ^ low][0], "section", low), swap(blocks[k ^ high][1], "section", high)]
    return blocks


def block_columns(count, span):
    full, rem = split_width(span)
    early = []
    if full:
        early += [(k, 0, full) for k in range(count - 1)]
    if rem:
        early += [(k, full, span) for k in range(count - 1)]
    return early, [(count - 1, 0, span)]


def order_kernel(count, span, where_ref, decode_ref, early_ref, last_ref):
    early, last = block_columns(count, span)
    for s in range(count):

        @pl.when(where_ref[0] == s)
        def _():
            for pieces, out in ((early, early_ref), (last, last_ref)):
                out[...] = jnp.concatenate(
                    [decode_ref[:, (s ^ k) * span + a : (s ^ k) * span + b] for k, a, b in pieces], axis=1
                )


def order_decode(where, decode, count, span):
    width = decode.shape[0]
    return call(
        functools.partial(order_kernel, count, span),
        [shape((width, (count - 1) * span), BF16), shape((width, span), BF16)],
        in_specs=[pl.BlockSpec(memory_space=pltpu.SMEM), pl.BlockSpec(memory_space=pltpu.VMEM)],
        moved=4 * decode.size,
        name="order_decode",
    )(where, decode)


def forward_kernel(
    pix, groups, acts_ref, first_ref, second_ref, aux_ref, labels_ref,
    wide_ref, hidden_ref, feature_ref, aux_pre_ref, sent_ref, pooled,
):
    step = pl.program_id(0)
    count, rows, width = wide_ref.shape
    for i in range(count):
        wide_ref[i, :pix, :] = acts_ref[i]
        wide_ref[i, pix:, :] = jnp.zeros((rows - pix, width), BF16)
    flat = wide_ref[...].reshape(count * rows, width)
    pre_act = dot(flat, first_ref[...])
    hidden = jnp.maximum(pre_act, 0.0).astype(BF16)
    hidden_ref[...] = hidden.reshape(hidden_ref.shape)
    feature = (flat.astype(F32) + dot(hidden, second_ref[...])).astype(BF16)
    feature_ref[...] = feature.reshape(feature_ref.shape)
    sums = jnp.sum(feature.reshape(count, rows, width).astype(F32), axis=1)
    pooled[step] = sums / pix

    @pl.when(step == pl.num_programs(0) - 1)
    def _():
        mean = pooled[...].reshape(-1, width).astype(BF16)
        aux_pre = dot(mean, aux_ref[...])
        aux_pre_ref[...] = aux_pre
        head = aux_pre.shape[1]
        part = width // groups
        out = jnp.maximum(aux_pre, 0.0).astype(BF16)
        label = labels_ref[...]
        lane = lax.broadcasted_iota(jnp.int32, (label.shape[0], LANES), 1)
        digits = jnp.where(lane == 0, label // LANES, jnp.where(lane == 1, label % LANES, 0))
        digits = digits.astype(F32).astype(BF16)
        for d in range(groups):
            sent_ref[d, :, :head] = out
            sent_ref[d, :, head : head + part] = mean[:, d * part : (d + 1) * part]
            sent_ref[d, :, head + LANES :] = digits


def forward(acts, first, second, aux, labels, groups, rows):
    images, pix, width = acts.shape
    inner, head = first.shape[1], aux.shape[1]
    steps = images // STEP
    whole = lambda g: (0, 0)
    block = lambda n: pl.BlockSpec((STEP, rows, n), lambda g: (g, 0, 0))
    return call(
        functools.partial(forward_kernel, pix, groups),
        [
            shape((images, rows, width), BF16),
            shape((images, rows, inner), BF16),
            shape((images, rows, width), BF16),
            shape((images, head), F32),
            shape((groups, images, head + 2 * LANES), BF16),
        ],
        grid=(steps,),
        in_specs=[
            pl.BlockSpec((STEP, pix, width), lambda g: (g, 0, 0)),
            pl.BlockSpec(first.shape, whole),
            pl.BlockSpec(second.shape, whole),
            pl.BlockSpec(aux.shape, whole),
            pl.BlockSpec((images, 1), whole),
        ],
        out_specs=[
            block(width),
            block(inner),
            block(width),
            pl.BlockSpec((images, head), whole),
            pl.BlockSpec((groups, images, head + 2 * LANES), lambda g: (0, 0, 0)),
        ],
        scratch_shapes=[pltpu.VMEM((steps, STEP, width), F32)],
        flops=4 * images * rows * width * inner,
        moved=2 * images * rows * (3 * width + inner),
        name="forward",
    )(acts, first, second, aux, labels)


def recon_kernel(feature_ref, early_ref, last_ref, recon_early_ref, recon_last_ref):
    count, rows, width = feature_ref.shape
    feature = feature_ref[...].reshape(count * rows, width)
    recon_early_ref[...] = dot(feature, early_ref[...]).reshape(recon_early_ref.shape)
    recon_last_ref[...] = dot(feature, last_ref[...]).reshape(recon_last_ref.shape)


def reconstruct(feature, early, last):
    images, rows, width = feature.shape
    block = lambda n: pl.BlockSpec((STEP, rows, n), lambda g: (g, 0, 0))
    whole = lambda g: (0, 0)
    n_early, n_last = early.shape[1], last.shape[1]
    return call(
        recon_kernel,
        [shape((images, rows, n_early), F32), shape((images, rows, n_last), F32)],
        grid=(images // STEP,),
        in_specs=[block(width), pl.BlockSpec(early.shape, whole), pl.BlockSpec(last.shape, whole)],
        out_specs=[block(n_early), block(n_last)],
        flops=2 * images * rows * width * (n_early + n_last),
        moved=images * rows * (2 * width + 4 * (n_early + n_last)),
        name="reconstruct",
    )(feature, early, last)


def patch_specs(halves, images):
    per_half = images // 2 // STEP
    specs = []
    for h, half in enumerate(halves):
        dims = (STEP,) + half.shape[1:]
        index = lambda g, h=h: (jnp.clip(g - h * per_half, 0, per_half - 1), 0, 0)
        specs.append(pl.BlockSpec(dims, index))
        if half.shape[0] != images // 2:
            specs.append(pl.BlockSpec(dims, lambda g: (per_half, 0, 0)))
        else:
            specs.append(pl.BlockSpec(memory_space=pl.ANY))
    return specs


def residual(step, steps, pieces, scale, packed, patch_refs, recon_ref, grad_ref):
    count, rows, _ = recon_ref.shape
    pix = patch_refs[0][0].shape[1]
    per_half = steps // 2
    first_block = pieces[0][0]
    for g in range(steps):

        @pl.when(step == g)
        def _():
            h = g // per_half
            at = 0
            for k, a, b in pieces:
                refs = patch_refs[k - first_block]
                spans = [(refs[2 * h], a, b)]
                if packed:
                    side = 64 * (g % per_half)
                    cut = refs[0].shape[2]
                    spans = []
                    if a < cut:
                        spans.append((refs[2 * h], a, min(b, cut)))
                    if b > cut:
                        spans.append((refs[2 * h + 1], side, side + 64))
                for ref, lo, hi in spans:
                    size = hi - lo
                    for i in range(count):
                        value = recon_ref[i, :pix, at : at + size] - ref[i, :, lo:hi].astype(F32)
                        grad_ref[i, :pix, at : at + size] = (value * scale).astype(BF16)
                    at += size

    @pl.when(step == 0)
    def _():
        grad_ref[:, pix:, :] = jnp.zeros((count, rows - pix, grad_ref.shape[2]), BF16)


def deal(where_ref, sums, part, keep_ref, send_ref):
    core = where_ref[1]
    at = 0
    for value in sums:
        height = value.shape[0]
        for z in range(keep_ref.shape[0]):
            even = value[:, 2 * z * part : (2 * z + 1) * part]
            odd = value[:, (2 * z + 1) * part : (2 * z + 2) * part]
            mine = jnp.where(core == 0, even, odd)
            other = jnp.where(core == 0, odd, even)
            keep_ref[z, at : at + height, :] = mine.astype(BF16)
            send_ref[z, at : at + height, :] = other.astype(BF16)
        at += height


def early_kernel(
    pieces, scale, packed, groups, where_ref, feature_ref, recon_ref, decode_ref, *refs
):
    n_refs = len(refs) - 5
    patch = [refs[4 * j : 4 * j + 4] for j in range(n_refs // 4)]
    back_ref, keep_ref, send_ref, grad, total = refs[n_refs:]
    step = pl.program_id(0)
    count, rows, width = feature_ref.shape
    residual(step, pl.num_programs(0), pieces, scale, packed, patch, recon_ref, grad)
    flat = grad[...].reshape(count * rows, -1)
    feature = feature_ref[...].reshape(count * rows, width)
    back_ref[...] = dot(flat, decode_ref[...], COLS_1).reshape(back_ref.shape)
    now = dot(flat, feature, ROWS_0)

    @pl.when(step == 0)
    def _():
        total[...] = now

    @pl.when(step > 0)
    def _():
        total[...] += now

    @pl.when(step == pl.num_programs(0) - 1)
    def _():
        deal(where_ref, [total], width // groups, keep_ref, send_ref)


def early_blocks(where, feature, recon, decode, blocks, pieces, scale, groups):
    images, rows, width = feature.shape
    n = decode.shape[1]
    block = lambda m: pl.BlockSpec((STEP, rows, m), lambda g: (g, 0, 0))
    packed = blocks[0][0].shape[0] != images // 2
    parts = (groups // 2, n, width // groups)
    dealt = pl.BlockSpec(parts, lambda g: (0, 0, 0))
    patch_args, specs = [], []
    for halves in blocks:
        specs += patch_specs(halves, images)
        patch_args += [halves[0], halves[0], halves[1], halves[1]]
    return call(
        functools.partial(early_kernel, pieces, scale, packed, groups),
        [shape((images, rows, width), F32), shape(parts, BF16), shape(parts, BF16)],
        grid=(images // STEP,),
        in_specs=[
            pl.BlockSpec(memory_space=pltpu.SMEM),
            block(width),
            block(n),
            pl.BlockSpec(decode.shape, lambda g: (0, 0)),
            *specs,
        ],
        out_specs=[block(width), dealt, dealt],
        scratch_shapes=[pltpu.VMEM((STEP, rows, n), BF16), pltpu.VMEM((n, width), F32)],
        flops=4 * images * rows * width * n,
        moved=images * rows * (6 * width + 6 * n),
        name="early_blocks",
    )(where, feature, recon, decode, *patch_args)


def last_kernel(
    pieces, scale, packed, groups, where_ref, feature_ref, recon_ref, decode_ref, *refs
):
    patch = [refs[:4]]
    (back_ref, pooled_ref, hidden_ref, wide_ref, second_ref, keep_ref, send_ref,
     grad, total_decode, total_second, total_first) = refs[4:]
    step = pl.program_id(0)
    count, rows, width = feature_ref.shape
    residual(step, pl.num_programs(0), pieces, scale, packed, patch, recon_ref, grad)
    flat = grad[...].reshape(count * rows, -1)
    feature = feature_ref[...].reshape(count * rows, width)
    decode_back = dot(flat, decode_ref[...], COLS_1).reshape(count, rows, width)
    pooled = pooled_ref[step]
    feature_grad = (back_ref[...] + decode_back + pooled[:, None, :]).astype(BF16).reshape(count * rows, width)
    hidden = hidden_ref[...].reshape(count * rows, -1)
    hidden_back = dot(feature_grad, second_ref[...], COLS_1)
    hidden_grad = jnp.where(hidden.astype(F32) > 0, hidden_back, 0.0).astype(BF16)
    wide = wide_ref[...].reshape(count * rows, width)
    sums = (
        (total_decode, dot(flat, feature, ROWS_0)),
        (total_second, dot(hidden, feature_grad, ROWS_0)),
        (total_first, dot(hidden_grad, wide, ROWS_0)),
    )

    @pl.when(step == 0)
    def _():
        for total, now in sums:
            total[...] = now

    @pl.when(step > 0)
    def _():
        for total, now in sums:
            total[...] += now

    @pl.when(step == pl.num_programs(0) - 1)
    def _():
        part = width // groups
        tall = total_second.shape[0] // groups
        second = jnp.concatenate(
            [
                jnp.concatenate(
                    [total_second[d * tall : (d + 1) * tall, q * part : (q + 1) * part] for q in range(groups)], axis=0
                )
                for d in range(groups)
            ],
            axis=1,
        )
        deal(where_ref, [total_decode, second, total_first], part, keep_ref, send_ref)


def last_block(where, feature, recon, decode, halves, pieces, scale, groups, back, pooled, hidden, wide, second):
    images, rows, width = feature.shape
    n, inner = decode.shape[1], second.shape[0]
    block = lambda m: pl.BlockSpec((STEP, rows, m), lambda g: (g, 0, 0))
    whole = lambda g: (0, 0)
    packed = halves[0].shape[0] != images // 2
    parts = (groups // 2, n + 2 * inner, width // groups)
    dealt = pl.BlockSpec(parts, lambda g: (0, 0, 0))
    return call(
        functools.partial(last_kernel, pieces, scale, packed, groups),
        [shape(parts, BF16), shape(parts, BF16)],
        grid=(images // STEP,),
        in_specs=[
            pl.BlockSpec(memory_space=pltpu.SMEM),
            block(width),
            block(n),
            pl.BlockSpec(decode.shape, whole),
            *patch_specs(halves, images),
            block(width),
            pl.BlockSpec(pooled.shape, lambda g: (0, 0, 0)),
            block(inner),
            block(width),
            pl.BlockSpec(second.shape, whole),
        ],
        out_specs=[dealt, dealt],
        scratch_shapes=[
            pltpu.VMEM((STEP, rows, n), BF16),
            pltpu.VMEM((n, width), F32),
            pltpu.VMEM((inner, width), F32),
            pltpu.VMEM((inner, width), F32),
        ],
        flops=images * rows * width * (4 * n + 6 * inner),
        moved=images * rows * (8 * width + 6 * n + 2 * inner),
        name="last_block",
    )(where, feature, recon, decode, halves[0], halves[0], halves[1], halves[1], back, pooled, hidden, wide, second)


def labels_of(got, head):
    digits = got[:, head + LANES : head + LANES + 2].astype(F32)
    return (digits[:, 0:1] * LANES + digits[:, 1:2]).astype(jnp.int32)


def logits_kernel(where_ref, got_ref, klass_ref, logits_ref, sent_ref):
    groups, images, _ = got_ref.shape
    classes, head = klass_ref.shape
    got = got_ref[...].reshape(groups * images, -1)
    logits = dot(got[:, :head], klass_ref[...], COLS_1)
    logits_ref[...] = logits
    ids = lax.broadcasted_iota(jnp.int32, logits.shape, 1) + where_ref[2] * classes
    hit = labels_of(got, head) == ids
    top = jnp.max(logits, axis=1, keepdims=True)
    expo = jnp.exp(logits - top)
    denom = jnp.sum(expo, axis=1, keepdims=True)
    own = jnp.sum(jnp.where(hit, expo, 0.0), axis=1, keepdims=True)
    rest = jnp.where(hit, 0.0, expo).astype(BF16)
    onehot = jnp.where(hit, 1.0, 0.0).astype(BF16)
    sent_ref[:, :, :head] = dot(rest, klass_ref[...]).reshape(groups, images, head)
    sent_ref[:, :, head : 2 * head] = dot(onehot, klass_ref[...]).reshape(groups, images, head)
    lane = lax.broadcasted_iota(jnp.int32, (groups * images, LANES), 1)
    stats = jnp.where(lane == 0, top, jnp.where(lane == 1, denom, jnp.where(lane == 2, own, 0.0)))
    sent_ref[:, :, 2 * head :] = stats.reshape(groups, images, LANES)


def class_logits(where, got, klass):
    groups, images, _ = got.shape
    classes, head = klass.shape
    smem, vmem = pl.BlockSpec(memory_space=pltpu.SMEM), pl.BlockSpec(memory_space=pltpu.VMEM)
    return call(
        logits_kernel,
        [shape((groups * images, classes), F32), shape((groups, images, 2 * head + LANES), F32)],
        in_specs=[smem, vmem, vmem],
        flops=6 * groups * images * classes * head,
        moved=2 * klass.size + 4 * groups * images * classes,
        name="class_logits",
    )(where, got, klass)


def aux_kernel(pix, norm, got_ref, aux_pre_ref, aux_ref, pooled_ref, sent_ref):
    groups, images, _ = got_ref.shape
    head = aux_pre_ref.shape[1]
    stats = [got_ref[d, :, 2 * head : 2 * head + 3] for d in range(groups)]
    top = functools.reduce(jnp.maximum, [s[:, 0:1] for s in stats])
    scales = [jnp.exp(s[:, 0:1] - top) for s in stats]
    denom = sum(s[:, 1:2] * f for s, f in zip(stats, scales))
    own = sum(s[:, 2:3] * f for s, f in zip(stats, scales)) / denom
    rest = sum(got_ref[d, :, :head] * scales[d] for d in range(groups)) / (denom * norm)
    row = sum(got_ref[d, :, head : 2 * head] for d in range(groups))
    back = rest + row * ((own - 1.0) / norm).astype(BF16).astype(F32)
    aux_grad = jnp.where(aux_pre_ref[...] > 0, back, 0.0).astype(BF16)
    pooled_ref[...] = (dot(aux_grad, aux_ref[...], COLS_1) / pix).reshape(pooled_ref.shape)
    lane = lax.broadcasted_iota(jnp.int32, (images, LANES), 1)
    tail = jnp.where(lane == 0, top, jnp.where(lane == 1, denom, 0.0))
    for d in range(groups):
        sent_ref[d, :, :head] = aux_grad.astype(F32)
        sent_ref[d, :, head:] = tail


def aux_backward(got, aux_pre, aux, pix, norm):
    groups, images, _ = got.shape
    width, head = aux.shape
    return call(
        functools.partial(aux_kernel, pix, norm),
        [shape((images // STEP, STEP, width), F32), shape((groups, images, head + LANES), F32)],
        flops=2 * images * width * head,
        moved=2 * aux.size + 4 * got.size,
        name="aux_backward",
    )(got, aux_pre, aux)


def class_kernel(norm, where_ref, logits_ref, got_ref, grads_ref, class_ref, aux_ref):
    groups, images, _ = got_ref.shape
    classes, head = class_ref.shape
    part = aux_ref.shape[0]
    got = got_ref[...].reshape(groups * images, -1)
    grads = grads_ref[...].reshape(groups * images, -1)
    top, denom = grads[:, head : head + 1], grads[:, head + 1 : head + 2]
    logits = logits_ref[...]
    ids = lax.broadcasted_iota(jnp.int32, logits.shape, 1) + where_ref[2] * classes
    onehot = jnp.where(labels_of(got, head) == ids, 1.0, 0.0)
    logit_grad = ((jnp.exp(logits - top) / denom - onehot) / norm).astype(BF16)
    class_ref[...] = dot(logit_grad, got[:, :head], ROWS_0)
    total = jnp.zeros(aux_ref.shape, F32)
    for d in range(groups):
        pooled = got_ref[d, :, head : head + part]
        total += dot(pooled, grads_ref[d, :, :head].astype(BF16), ROWS_0).astype(BF16).astype(F32)
    aux_ref[...] = total


def class_backward(where, logits, got, grads, classes, part, norm):
    groups, images, wide = grads.shape
    head = wide - LANES
    smem, vmem = pl.BlockSpec(memory_space=pltpu.SMEM), pl.BlockSpec(memory_space=pltpu.VMEM)
    return call(
        functools.partial(class_kernel, norm),
        [shape((classes, head), F32), shape((part, head), F32)],
        in_specs=[smem, vmem, vmem, vmem],
        flops=2 * groups * images * classes * head,
        moved=4 * classes * head + 4 * logits.size,
        name="class_backward",
    )(where, logits, got, grads)


def chip_kernel(keep_ref, got_ref, out_ref):
    out_ref[...] = (keep_ref[...].astype(F32) + got_ref[...].astype(F32)).astype(BF16)


def reduce_parts(keep, send, name):
    count = lax.axis_size("dp")
    got = swap(send, "dp", 1)
    chip = call(
        chip_kernel,
        shape(keep.shape, BF16),
        flops=keep.size,
        moved=6 * keep.size,
        name=name,
    )(keep, got)
    return exchange(chip, [[z + core for z in range(0, count, 2)] for core in range(2)])


def finish_kernel(count, span, inner, where_ref, early_ref, last_ref, first_ref, second_ref, decode_ref):
    chips, _, part = early_ref.shape
    early = sum(early_ref[z].astype(F32) for z in range(chips))
    last = sum(last_ref[z].astype(F32) for z in range(chips))
    first_ref[...] = last[span + inner :].T
    tall, groups = second_ref.shape[0], inner // second_ref.shape[0]
    for q in range(groups):
        second_ref[:, q * part : (q + 1) * part] = last[span + q * tall : span + (q + 1) * tall]
    pieces, tail = block_columns(count, span)
    columns = {}
    at = 0
    for k, a, b in pieces:
        columns[k, a] = early[at : at + b - a].T
        at += b - a
    for k, a, b in tail:
        columns[k, a] = last[:span].T
    for s in range(count):

        @pl.when(where_ref[0] == s)
        def _():
            for (k, a), value in columns.items():
                start = (s ^ k) * span + a
                decode_ref[:, start : start + value.shape[1]] = value


def finish(where, early, last, count, span, inner, groups):
    part = early.shape[2]
    smem, vmem = pl.BlockSpec(memory_space=pltpu.SMEM), pl.BlockSpec(memory_space=pltpu.VMEM)
    return call(
        functools.partial(finish_kernel, count, span, inner),
        [shape((part, inner), F32), shape((inner // groups, part * groups), F32), shape((part, count * span), F32)],
        in_specs=[smem, vmem, vmem],
        moved=2 * early.size + 2 * last.size,
        name="finish",
    )(where, early, last)


def local(acts, patches, labels, w_first, w_second, w_decode, w_aux, w_class):
    acts = acts[0]
    images, pix, width = acts.shape
    groups, count = lax.axis_size("dp"), lax.axis_size("section")
    me, section = lax.axis_index("dp"), lax.axis_index("section")
    where = jnp.stack([section, lax.rem(me, 2), me]).astype(jnp.int32)
    rows = -(-pix // 16) * 16
    scale = (groups * images * pix) ** -0.5
    norm = (groups * images) ** 0.5
    first, second, decode, aux, klass = w_first[0], w_second[0], w_decode[0], w_aux[0], w_class[0]
    span = patches.shape[2]
    inner = first.shape[1]
    pieces, tail = block_columns(count, span)

    blocks = gather_patches(pack(patches))
    early, last = order_decode(where, decode, count, span)
    wide, hidden, feature, aux_pre, sent = forward(acts, first, second, aux, labels[:, None], groups, rows)
    got = exchange(sent)
    recon_early, recon_last = reconstruct(feature, early, last)
    logits, partial = class_logits(where, got, klass)
    pooled_grad, sent = aux_backward(exchange(partial), aux_pre, aux, pix, norm)
    grads = exchange(sent)
    back, keep, send = early_blocks(where, feature, recon_early, early, blocks[:-1], pieces, scale, groups)
    sum_early = reduce_parts(keep, send, "chip_sum_early")
    grad_class, grad_aux = class_backward(where, logits, got, grads, klass.shape[0], width // groups, norm)
    keep, send = last_block(
        where, feature, recon_last, last, blocks[-1], tail, scale, groups, back, pooled_grad, hidden, wide, second
    )
    sum_last = reduce_parts(keep, send, "chip_sum_last")
    grad_first, grad_second, grad_decode = finish(where, sum_early, sum_last, count, span, inner, groups)
    return grad_first[None], grad_second[None], grad_decode[None], grad_aux[None], grad_class[None]


def solution(mesh):
    in_specs = (
        P("section", "dp", None, None),
        P("dp", None, "section"),
        P("dp"),
        P("section", None, None),
        P("section", None, None),
        P("section", None, None),
        P("section", None, None),
        P("section", "dp", None),
    )
    out_specs = (P("section", "dp", None),) * 5
    return jax.shard_map(local, mesh=mesh, in_specs=in_specs, out_specs=out_specs, check_vma=False)
```

time: 370 us -> 164 us (0.44); the launches traced: 365 us -> 164 us
  matrix products: 117 us -> 0 us
  local copies, waits for them, and re-layouts: 130 us -> 18.3 us
  Pallas kernels: 0 us -> 85.4 us
  starting transfers between devices: 61.5 us -> 32.6 us
  other arithmetic: 26.9 us -> 0.65 us
    dot_general x22 -> x0, matrix products: 117 us -> none  [the longest x4 38 us: local(): jnp.dot(recon_grad, columns.T, preferred_element_type=F32)]
    pallas_call x0 -> x12, Pallas kernels: none -> 85.4 us  [the longest x1 19.8 us: early_blocks(): call(functools.partial(early_kernel, pieces, scale, packed, groups), [sha...]
    ppermute x51 -> x8, starting transfers between devices: 61.5 us -> 7.45 us  [swap(): return lax.ppermute(value, axis, [(i, i ^ bits) for i in range(count)])]
    convert_element_type x9 -> x0, local copies, waits for them, and re-layouts: 43.8 us -> none  [the longest x8 34.8 us: local(): target[k].reshape(rows_here, span).astype(F32)]
    ppermute x51 -> x8, waiting for transfers between devices: 28.4 us -> 2.41 us  [swap(): return lax.ppermute(value, axis, [(i, i ^ bits) for i in range(count)])]
    all_to_all x0 -> x5, starting transfers between devices: none -> 25.1 us  [exchange(): lax.all_to_all(value, 'dp', 0, 0, axis_index_groups=groups, tiled=True)]
    all_to_all x0 -> x5, waiting for transfers between devices: none -> 23.4 us  [exchange(): lax.all_to_all(value, 'dp', 0, 0, axis_index_groups=groups, tiled=True)]
    add x3 -> x0, local copies, waits for them, and re-layouts: 18.3 us -> none  [the longest x2 18.1 us: local(): dec_back.reshape(images_here, pix, width) + pooled_grad[:, None, :] / pix]
  transfers between devices with their start and end apart: 51 -> 13, of which waited for: 14 -> 3; matrix products, arithmetic and copies ran while one was open for 43% -> 2% of each run, Pallas kernels for 0% -> 43%
where the time goes in v2:
time: 164 us
  Pallas kernels  85.4 us (52%)
  starting transfers between devices  32.6 us (20%)
  waiting for transfers between devices  25.8 us (16%)
  local copies, waits for them, and re-layouts  18.3 us (11%)
    all_to_all x5, starting transfers between devices, exchange(): lax.all_to_all(value, 'dp', 0, 0, axis_index_groups=groups, tiled=True)  25.1 us
    all_to_all x5, waiting for transfers between devices, exchange(): lax.all_to_all(value, 'dp', 0, 0, axis_index_groups=groups, tiled=True)  23.4 us
    pallas_call x1, Pallas kernels, early_blocks(): call(functools.partial(early_kernel, pieces, scale, packed, groups), [sha...  19.8 us
    pallas_call x1, Pallas kernels, last_block(): call(functools.partial(last_kernel, pieces, scale, packed, groups), [shap...  18 us
    unnamed x28, local copies, waits for them, and re-layouts  17.6 us
    pallas_call x1, Pallas kernels, forward(): call(functools.partial(forward_kernel, pix, groups), [shape((images, rows...  12.6 us
    pallas_call x1, Pallas kernels, reconstruct(): call(recon_kernel, [shape((images, rows, n_early), F32), shape((images, r...  12 us
    ppermute x8, starting transfers between devices, swap(): return lax.ppermute(value, axis, [(i, i ^ bits) for i in range(count)])  7.45 us
  transfers between devices with their start and end apart: 13, of which 3 were waited for; matrix products, arithmetic and copies ran while one was open for 2% of the time, Pallas kernels for 43%

profile of v2, /device:TPU:0, one launch (start us, length us, event | category | flops | bytes accessed | tf_op | source)
XLA Modules:
  0.0 163.5 jit_solution(17081366634923348579)
XLA Ops:
  0.6 9.2 %copy.17 = bf16[1,16,196,1024]{3,2,1,0:T(8,128)(2,1)} copy(bf16[1,16,196,1024]{3,1,2,0:T(8,128)(2,1)} %param.8) | data formatting | bytes 12845056 | tf_op args[0]
  9.8 0.7 copy.14.labels_ref
  10.5 12.6 %forward.1 = (bf16[16,208,1024]{2,1,0:T(8,128)(2,1)}, bf16[16,208,256]{2,1,0:T(8,128)(2,1)}, bf16[16,208,1024]{2,1,0:T(8,128)(2,1)}, f32[16,512]{1,0:T(8,128)}, bf16[8,16,768]{2,1,0:T(8,128)(2,1)}) custom-call(bf16[16,196,1024]{2,1,0:T(8,128)(2,1)} %bitcast.17, bf16[1024,256]{1,0:T(8,128)(2,1)} %bitcast.26, bf16[256,1024]{1,0:T(8,128)(2,1)} %bitcast.21, ...), custom_call_target="tpu_custom_call" | custom-call | flops 3489660928 | bytes 22151168 | tf_op jit(solution)/shard_map/forward/pallas_call | solution.py:166
  23.2 6.3 %all-to-all-start.1 = ((bf16[8,16,768]{2,1,0:T(8,128)(2,1)}), bf16[8,16,768]{2,1,0:T(8,128)(2,1)S(1)}, u32[]{:S(2)}, u32[]{:S(2)}) async-start(bf16[8,16,768]{2,1,0:T(8,128)(2,1)} %get-tuple-element.40), calls=%async_computation.1 | async-start | bytes 393216 | tf_op jit(solution)/shard_map/all_to_all | solution.py:43
  29.5 2.5 %copy.15.patches_ref = bf16[16,196,192]{2,1,0:T(8,128)(2,1)} copy(bf16[16,196,192]{1,2,0:T(8,128)(2,1)S(1)} %copy-done.5) | data formatting | bytes 2408448 | tf_op args[1]
  32.0 2.7 %pack_patches.1 = (bf16[12,196,128]{2,1,0:T(8,128)(2,1)}, bf16[12,196,128]{2,1,0:T(8,128)(2,1)}) custom-call(bf16[16,196,192]{2,1,0:T(8,128)(2,1)} %copy.15.patches_ref), custom_call_target="tpu_custom_call" | custom-call | bytes 2408448 | tf_op jit(solution)/shard_map/pack_patches/pallas_call | solution.py:70
  34.7 1.5 collective-permute-start
  36.1 1.5 collective-permute-start.2
  37.7 0.5 collective-permute-start.1
  38.2 0.5 collective-permute-start.3
  38.7 0.7 pad_add_fusion.where_ref
  39.4 3.1 %order_decode.1 = (bf16[1024,576]{1,0:T(8,128)(2,1)}, bf16[1024,192]{1,0:T(8,128)(2,1)}) custom-call(s32[3]{0:T(128)} %pad_add_fusion.where_ref, bf16[1024,768]{1,0:T(8,128)(2,1)} %bitcast.18), custom_call_target="tpu_custom_call" | custom-call | bytes 3145728 | tf_op jit(solution)/shard_map/order_decode/pallas_call | solution.py:115
  42.5 0.0 all-to-all-done.1.got_ref
  42.5 0.7 copy-done.7
  43.2 3.7 %class_logits.1 = (f32[128,1408]{1,0:T(8,128)}, f32[8,16,1152]{2,1,0:T(8,128)}) custom-call(s32[3]{0:T(128)} %pad_add_fusion.where_ref, bf16[8,16,768]{2,1,0:T(8,128)(2,1)} %copy-done.7, bf16[1408,512]{1,0:T(8,128)(2,1)} %bitcast.25), custom_call_target="tpu_custom_call" | custom-call | flops 553648128 | bytes 2162688 | tf_op jit(solution)/shard_map/class_logits/pallas_call | solution.py:458
  46.8 5.1 %all-to-all-start.2 = ((f32[8,16,1152]{2,1,0:T(8,128)}), f32[8,16,1152]{2,1,0:T(8,128)S(1)}, u32[]{:S(2)}, u32[]{:S(2)}) async-start(f32[8,16,1152]{2,1,0:T(8,128)} %get-tuple-element.41), calls=%async_computation.2 | async-start | bytes 1179648 | tf_op jit(solution)/shard_map/all_to_all | solution.py:43
  51.9 12.0 %reconstruct.1 = (f32[16,208,576]{2,1,0:T(8,128)}, f32[16,208,192]{2,1,0:T(8,128)}) custom-call(bf16[16,208,1024]{2,1,0:T(8,128)(2,1)} %get-tuple-element.30.feature_ref, bf16[1024,576]{1,0:T(8,128)(2,1)} %get-tuple-element.31.early_ref.decode_ref, bf16[1024,192]{1,0:T(8,128)(2,1)} %get-tuple-element.32.last_ref.decode_ref), custom_call_target="tpu_custom_call" | custom-call | flops 5234491392 | bytes 17039360 | tf_op jit(solution)/shard_map/reconstruct/pallas_call | solution.py:209
  63.9 0.0 collective-permute-done.2.refs_8_.refs_9_
  63.9 1.7 %collective-permute-start.5 = (bf16[12,196,128]{2,1,0:T(8,128)(2,1)S(1)}, bf16[12,196,128]{2,1,0:T(8,128)(2,1)S(1)}, u32[]{:S(2)}, u32[]{:S(2)}) collective-permute-start(bf16[12,196,128]{2,1,0:T(8,128)(2,1)S(1)} %collective-permute-done.2.refs_8_.refs_9_), channel_id=1, source_target_pairs={{0,8},{8,0},{16,24},{24,16},{1,9},{9,1},{17,25},{25,17},{2,10},{10... | collective-permute-start | bytes 1806344 | tf_op jit(solution)/shard_map/ppermute | solution.py:39
  65.7 0.0 collective-permute-done.1.refs_6_.refs_7_
  65.7 1.5 collective-permute-start.6
  67.2 0.0 collective-permute-done.refs_4_.refs_5_
  67.2 0.0 collective-permute-done.3.refs_10_.refs_11_
  67.2 0.8 copy-done.12
  68.0 19.8 %early_blocks.1 = (f32[16,208,1024]{2,1,0:T(8,128)}, bf16[4,576,128]{2,1,0:T(8,128)(2,1)}, bf16[4,576,128]{2,1,0:T(8,128)(2,1)}) custom-call(s32[3]{0:T(128)} %pad_add_fusion.where_ref, bf16[16,208,1024]{2,1,0:T(8,128)(2,1)} %get-tuple-element.30.feature_ref, f32[16,208,576]{2,1,0:T(8,128)} %get-tuple-element.33.recon_ref, ...), custom_call_target="tpu_custom_call" | custom-call | flops 7851737088 | bytes 31948800 | tf_op jit(solution)/shard_map/early_blocks/pallas_call | solution.py:322
  87.9 0.1 collective-permute-start.4
  87.9 0.0 all-to-all-done.2.got_ref
  88.0 0.8 copy-done.3
  88.8 2.6 %aux_backward.1 = (f32[4,4,1024]{2,1,0:T(4,128)}, f32[8,16,640]{2,1,0:T(8,128)}) custom-call(f32[8,16,1152]{2,1,0:T(8,128)} %copy-done.3, f32[16,512]{1,0:T(8,128)} %get-tuple-element.42.aux_pre_ref, bf16[1024,512]{1,0:T(8,128)(2,1)} %bitcast.20), custom_call_target="tpu_custom_call" | custom-call | flops 16777216 | bytes 1638400 | tf_op jit(solution)/shard_map/aux_backward/pallas_call | solution.py:491
  91.4 5.2 %all-to-all-start.4 = ((f32[8,16,640]{2,1,0:T(8,128)}), f32[8,16,640]{2,1,0:T(8,128)S(1)}, u32[]{:S(2)}, u32[]{:S(2)}) async-start(f32[8,16,640]{2,1,0:T(8,128)} %get-tuple-element.52), calls=%async_computation.4 | async-start | bytes 655360 | tf_op jit(solution)/shard_map/all_to_all | solution.py:43
  96.6 0.0 collective-permute-done.4.got_ref
  96.6 0.8 copy-done.9
  97.5 2.2 %chip_sum_early.1 = bf16[4,576,128]{2,1,0:T(8,128)(2,1)} custom-call(bf16[4,576,128]{2,1,0:T(8,128)(2,1)} %get-tuple-element.36.keep_ref, bf16[4,576,128]{2,1,0:T(8,128)(2,1)} %copy-done.9), custom_call_target="tpu_custom_call" | custom-call | flops 294912 | bytes 1769472 | tf_op jit(solution)/shard_map/chip_sum_early/pallas_call | solution.py:540
  99.7 8.1 %all-to-all-done.4.grads_ref = f32[8,16,640]{2,1,0:T(8,128)S(1)} async-done(((f32[8,16,640]{2,1,0:T(8,128)}), f32[8,16,640]{2,1,0:T(8,128)S(1)}, u32[]{:S(2)}, u32[]{:S(2)}) %all-to-all-start.4) | async-done | bytes 327712 | tf_op jit(solution)/shard_map/all_to_all | solution.py:43
  107.8 3.5 %all-to-all-start = ((bf16[4,576,128]{2,1,0:T(8,128)(2,1)}), bf16[4,576,128]{2,1,0:T(8,128)(2,1)S(1)}, u32[]{:S(2)}, u32[]{:S(2)}) async-start(bf16[4,576,128]{2,1,0:T(8,128)(2,1)} %chip_sum_early.1), calls=%async_computation | async-start | bytes 1179648 | tf_op jit(solution)/shard_map/all_to_all | solution.py:43
  111.3 0.8 copy-done.1
  112.1 0.2 copy-done.2
  112.4 18.0 %last_block.1 = (bf16[4,704,128]{2,1,0:T(8,128)(2,1)}, bf16[4,704,128]{2,1,0:T(8,128)(2,1)}) custom-call(s32[3]{0:T(128)} %pad_add_fusion.where_ref, bf16[16,208,1024]{2,1,0:T(8,128)(2,1)} %get-tuple-element.30.feature_ref, f32[16,208,192]{2,1,0:T(8,128)} %get-tuple-element.38.recon_ref, bf16[1024,192]{1,0:T(8,128)(2,1)} %get-tuple-element.32.last_ref.decode_ref, ...), custom_call_target="tpu_custom_call" | custom-call | flops 7851737088 | bytes 32800768 | tf_op jit(solution)/shard_map/last_block/pallas_call | solution.py:399
  130.4 0.1 collective-permute-start.7
  130.5 2.4 %collective-permute-done.7.got_ref = bf16[4,704,128]{2,1,0:T(8,128)(2,1)S(1)} collective-permute-done((bf16[4,704,128]{2,1,0:T(8,128)(2,1)}, bf16[4,704,128]{2,1,0:T(8,128)(2,1)S(1)}, u32[]{:S(2)}, u32[]{:S(2)}) %collective-permute-start.7) | collective-permute-done | bytes 720928 | tf_op jit(solution)/shard_map/ppermute | solution.py:39
  132.9 0.9 copy-done.8
  133.7 2.4 %chip_sum_last.1 = bf16[4,704,128]{2,1,0:T(8,128)(2,1)} custom-call(bf16[4,704,128]{2,1,0:T(8,128)(2,1)} %get-tuple-element.46.keep_ref, bf16[4,704,128]{2,1,0:T(8,128)(2,1)} %copy-done.8), custom_call_target="tpu_custom_call" | custom-call | flops 360448 | bytes 2162688 | tf_op jit(solution)/shard_map/chip_sum_last/pallas_call | solution.py:540
  136.1 0.0 all-to-all-done.early_ref
  136.1 5.0 %all-to-all-start.3 = ((bf16[4,704,128]{2,1,0:T(8,128)(2,1)}), bf16[4,704,128]{2,1,0:T(8,128)(2,1)S(1)}, u32[]{:S(2)}, u32[]{:S(2)}) async-start(bf16[4,704,128]{2,1,0:T(8,128)(2,1)} %chip_sum_last.1), calls=%async_computation.3 | async-start | bytes 1441792 | tf_op jit(solution)/shard_map/all_to_all | solution.py:43
  141.1 3.7 %class_backward.1 = (f32[1408,512]{1,0:T(8,128)}, f32[128,512]{1,0:T(8,128)}) custom-call(s32[3]{0:T(128)} %pad_add_fusion.where_ref, f32[128,1408]{1,0:T(8,128)} %get-tuple-element.51.logits_ref, bf16[8,16,768]{2,1,0:T(8,128)(2,1)} %copy-done.7, f32[8,16,640]{2,1,0:T(8,128)} %copy-done.6), custom_call_target="tpu_custom_call" | custom-call | flops 184549376 | bytes 3604480 | tf_op jit(solution)/shard_map/class_backward/pallas_call | solution.py:523
  144.8 15.3 %all-to-all-done.3.last_ref = bf16[4,704,128]{2,1,0:T(8,128)(2,1)S(1)} async-done(((bf16[4,704,128]{2,1,0:T(8,128)(2,1)}), bf16[4,704,128]{2,1,0:T(8,128)(2,1)S(1)}, u32[]{:S(2)}, u32[]{:S(2)}) %all-to-all-start.3) | async-done | bytes 720928 | tf_op jit(solution)/shard_map/all_to_all | solution.py:43
  160.1 0.9 copy-done
  161.0 2.5 %finish.1 = (f32[128,256]{1,0:T(8,128)}, f32[32,1024]{1,0:T(8,128)}, f32[128,768]{1,0:T(8,128)}) custom-call(s32[3]{0:T(128)} %pad_add_fusion.where_ref, bf16[4,576,128]{2,1,0:T(8,128)(2,1)} %copy-done.4, bf16[4,704,128]{2,1,0:T(8,128)(2,1)} %copy-done), custom_call_target="tpu_custom_call" | custom-call | bytes 1310720 | tf_op jit(solution)/shard_map/finish/pallas_call | solution.py:578
  (20 shorter events, 0.0 us)
Async XLA Ops:
  0.6 9.2 %copy-start.10 = (s32[16]{0:T(128)S(1)}, s32[16]{0:T(128)}, u32[]{:S(2)}) copy-start(s32[16]{0:T(128)} %param.10) | copy-start | bytes 196
  10.5 19.0 %copy-start.5 = (bf16[16,196,192]{1,2,0:T(8,128)(2,1)S(1)}, bf16[16,196,192]{1,2,0:T(8,128)(2,1)}, u32[]{:S(2)}) copy-start(bf16[16,196,192]{1,2,0:T(8,128)(2,1)} %param.9) | copy-start | bytes 3612676
  23.2 19.3 %all-to-all-start.1 = ((bf16[8,16,768]{2,1,0:T(8,128)(2,1)}), bf16[8,16,768]{2,1,0:T(8,128)(2,1)S(1)}, u32[]{:S(2)}, u32[]{:S(2)}) async-start(bf16[8,16,768]{2,1,0:T(8,128)(2,1)} %get-tuple-element.40), calls=%async_computation.1 | async-start | bytes 393216 | tf_op jit(solution)/shard_map/all_to_all | solution.py:43
  34.7 32.5 %collective-permute-start = (bf16[12,196,128]{2,1,0:T(8,128)(2,1)}, bf16[12,196,128]{2,1,0:T(8,128)(2,1)S(1)}, u32[]{:S(2)}, u32[]{:S(2)}) collective-permute-start(bf16[12,196,128]{2,1,0:T(8,128)(2,1)} %get-tuple-element.34.refs_0_.refs_1_), channel_id=1, source_target_pairs={{0,8},{8,0},{16,24},{24,16},{1,9},{9,1},{17,25},{25,17},{2,10},{10... | collective-permute-start | bytes 1806344 | tf_op jit(solution)/shard_map/ppermute | solution.py:39
  36.1 27.8 %collective-permute-start.2 = (bf16[12,196,128]{2,1,0:T(8,128)(2,1)}, bf16[12,196,128]{2,1,0:T(8,128)(2,1)S(1)}, u32[]{:S(2)}, u32[]{:S(2)}) collective-permute-start(bf16[12,196,128]{2,1,0:T(8,128)(2,1)} %get-tuple-element.34.refs_0_.refs_1_), channel_id=1, source_target_pairs={{0,16},{8,24},{16,0},{24,8},{1,17},{9,25},{17,1},{25,9},{2,18},{10... | collective-permute-start | bytes 1806344 | tf_op jit(solution)/shard_map/ppermute | solution.py:39
  37.7 28.0 %collective-permute-start.1 = (bf16[12,196,128]{2,1,0:T(8,128)(2,1)}, bf16[12,196,128]{2,1,0:T(8,128)(2,1)}, u32[]{:S(2)}, u32[]{:S(2)}) collective-permute-start(bf16[12,196,128]{2,1,0:T(8,128)(2,1)} %get-tuple-element.35.refs_2_.refs_3_), channel_id=1, source_target_pairs={{0,8},{8,0},{16,24},{24,16},{1,9},{9,1},{17,25},{25,17},{2,10},{10... | collective-permute-start | bytes 1806344 | tf_op jit(solution)/shard_map/ppermute | solution.py:39
  38.2 29.0 %collective-permute-start.3 = (bf16[12,196,128]{2,1,0:T(8,128)(2,1)}, bf16[12,196,128]{2,1,0:T(8,128)(2,1)}, u32[]{:S(2)}, u32[]{:S(2)}) collective-permute-start(bf16[12,196,128]{2,1,0:T(8,128)(2,1)} %get-tuple-element.35.refs_2_.refs_3_), channel_id=1, source_target_pairs={{0,16},{8,24},{16,0},{24,8},{1,17},{9,25},{17,1},{25,9},{2,18},{10... | collective-permute-start | bytes 1806344 | tf_op jit(solution)/shard_map/ppermute | solution.py:39
  42.5 0.7 copy-start.7
  46.8 41.1 %all-to-all-start.2 = ((f32[8,16,1152]{2,1,0:T(8,128)}), f32[8,16,1152]{2,1,0:T(8,128)S(1)}, u32[]{:S(2)}, u32[]{:S(2)}) async-start(f32[8,16,1152]{2,1,0:T(8,128)} %get-tuple-element.41), calls=%async_computation.2 | async-start | bytes 1179648 | tf_op jit(solution)/shard_map/all_to_all | solution.py:43
  63.9 3.3 %copy-start.11 = (bf16[12,196,128]{2,1,0:T(8,128)(2,1)}, bf16[12,196,128]{2,1,0:T(8,128)(2,1)S(1)}, u32[]{:S(2)}) copy-start(bf16[12,196,128]{2,1,0:T(8,128)(2,1)S(1)} %collective-permute-done.2.refs_8_.refs_9_) | copy-start | bytes 1806340
  63.9 47.3 %collective-permute-start.5 = (bf16[12,196,128]{2,1,0:T(8,128)(2,1)S(1)}, bf16[12,196,128]{2,1,0:T(8,128)(2,1)S(1)}, u32[]{:S(2)}, u32[]{:S(2)}) collective-permute-start(bf16[12,196,128]{2,1,0:T(8,128)(2,1)S(1)} %collective-permute-done.2.refs_8_.refs_9_), channel_id=1, source_target_pairs={{0,8},{8,0},{16,24},{24,16},{1,9},{9,1},{17,25},{25,17},{2,10},{10... | collective-permute-start | bytes 1806344 | tf_op jit(solution)/shard_map/ppermute | solution.py:39
  65.7 45.6 %collective-permute-start.6 = (bf16[12,196,128]{2,1,0:T(8,128)(2,1)}, bf16[12,196,128]{2,1,0:T(8,128)(2,1)S(1)}, u32[]{:S(2)}, u32[]{:S(2)}) collective-permute-start(bf16[12,196,128]{2,1,0:T(8,128)(2,1)} %collective-permute-done.1.refs_6_.refs_7_), channel_id=1, source_target_pairs={{0,16},{8,24},{16,0},{24,8},{1,17},{9,25},{17,1},{25,9},{2,18},{10... | collective-permute-start | bytes 1806344 | tf_op jit(solution)/shard_map/ppermute | solution.py:39
  67.2 0.8 copy-start.12
  87.9 8.8 %collective-permute-start.4 = (bf16[4,576,128]{2,1,0:T(8,128)(2,1)}, bf16[4,576,128]{2,1,0:T(8,128)(2,1)S(1)}, u32[]{:S(2)}, u32[]{:S(2)}) collective-permute-start(bf16[4,576,128]{2,1,0:T(8,128)(2,1)} %get-tuple-element.37), channel_id=1, source_target_pairs={{0,1},{1,0},{2,3},{3,2},{4,5},{5,4},{6,7},{7,6},{8,9},{9,8},{10,11... | collective-permute-start | bytes 1769480 | tf_op jit(solution)/shard_map/ppermute | solution.py:39
  88.0 0.8 copy-start.3
  91.4 16.3 %all-to-all-start.4 = ((f32[8,16,640]{2,1,0:T(8,128)}), f32[8,16,640]{2,1,0:T(8,128)S(1)}, u32[]{:S(2)}, u32[]{:S(2)}) async-start(f32[8,16,640]{2,1,0:T(8,128)} %get-tuple-element.52), calls=%async_computation.4 | async-start | bytes 655360 | tf_op jit(solution)/shard_map/all_to_all | solution.py:43
  96.6 0.8 copy-start.9
  107.8 22.6 %copy-start.6 = (f32[8,16,640]{2,1,0:T(8,128)}, f32[8,16,640]{2,1,0:T(8,128)S(1)}, u32[]{:S(2)}) copy-start(f32[8,16,640]{2,1,0:T(8,128)S(1)} %all-to-all-done.4.grads_ref) | copy-start | bytes 983044
  107.8 28.3 %all-to-all-start = ((bf16[4,576,128]{2,1,0:T(8,128)(2,1)}), bf16[4,576,128]{2,1,0:T(8,128)(2,1)S(1)}, u32[]{:S(2)}, u32[]{:S(2)}) async-start(bf16[4,576,128]{2,1,0:T(8,128)(2,1)} %chip_sum_early.1), calls=%async_computation | async-start | bytes 1179648 | tf_op jit(solution)/shard_map/all_to_all | solution.py:43
  111.3 0.8 copy-start.1
  111.3 1.1 copy-start.2
  130.4 2.5 %collective-permute-start.7 = (bf16[4,704,128]{2,1,0:T(8,128)(2,1)}, bf16[4,704,128]{2,1,0:T(8,128)(2,1)S(1)}, u32[]{:S(2)}, u32[]{:S(2)}) collective-permute-start(bf16[4,704,128]{2,1,0:T(8,128)(2,1)} %get-tuple-element.47), channel_id=1, source_target_pairs={{0,1},{1,0},{2,3},{3,2},{4,5},{5,4},{6,7},{7,6},{8,9},{9,8},{10,11... | collective-permute-start | bytes 2162696 | tf_op jit(solution)/shard_map/ppermute | solution.py:39
  132.9 0.9 copy-start.8
  136.1 24.1 %copy-start.4 = (bf16[4,576,128]{2,1,0:T(8,128)(2,1)}, bf16[4,576,128]{2,1,0:T(8,128)(2,1)S(1)}, u32[]{:S(2)}) copy-start(bf16[4,576,128]{2,1,0:T(8,128)(2,1)S(1)} %all-to-all-done.early_ref) | copy-start | bytes 1769476
  136.1 24.1 %all-to-all-start.3 = ((bf16[4,704,128]{2,1,0:T(8,128)(2,1)}), bf16[4,704,128]{2,1,0:T(8,128)(2,1)S(1)}, u32[]{:S(2)}, u32[]{:S(2)}) async-start(bf16[4,704,128]{2,1,0:T(8,128)(2,1)} %chip_sum_last.1), calls=%async_computation.3 | async-start | bytes 1441792 | tf_op jit(solution)/shard_map/all_to_all | solution.py:43
  160.1 0.9 copy-start

commit v3 on v0

v3 whole, which is shorter than its diff:
```python
import functools

import jax
import jax.numpy as jnp
from jax import lax
from jax.experimental import pallas as pl
from jax.experimental.pallas import tpu as pltpu
from jax.sharding import PartitionSpec as P

F32 = jnp.float32
BF16 = jnp.bfloat16
STEPS = 4
LANES = 128
EARLY = 4
MIB = 1024 * 1024
ROWS_0 = (((0,), (0,)), ((), ()))
COLS_1 = (((1,), (1,)), ((), ()))
PARITY, CORE, ME, TILES = 0, 1, 2, 3


def dot(left, right, dims=(((1,), (0,)), ((), ()))):
    return lax.dot_general(left, right, dims, preferred_element_type=F32)


def call(kernel, out_shape, *, limit, flops=0, moved=0, **kwargs):
    return pl.pallas_call(
        kernel,
        out_shape=out_shape,
        compiler_params=pltpu.CompilerParams(vmem_limit_bytes=limit * MIB),
        cost_estimate=pl.CostEstimate(flops=int(flops), bytes_accessed=int(moved), transcendentals=0),
        **kwargs,
    )


def shape(dims, kind):
    return jax.ShapeDtypeStruct(dims, kind)


SMEM = pl.BlockSpec(memory_space=pltpu.SMEM)
VMEM = pl.BlockSpec(memory_space=pltpu.VMEM)
ANY = pl.BlockSpec(memory_space=pl.ANY)
HBM = pl.BlockSpec(memory_space=pltpu.HBM)


def swap(value, axis, bits):
    count = lax.axis_size(axis)
    return lax.ppermute(value, axis, [(i, i ^ bits) for i in range(count)])


def exchange(value, groups=None):
    return lax.all_to_all(value, "dp", 0, 0, axis_index_groups=groups, tiled=True)


def pack_kernel(where_ref, patches_ref, *refs):
    out_ref, turned, own, shared = refs
    images, span, pix = patches_ref.shape
    padded = turned.shape[1]
    parity = where_ref[PARITY]
    at_own = pl.multiple_of(64 * parity, 64)
    at_shared = pl.multiple_of(128 * (1 - parity), 64)
    unit = lambda n: (
        lax.broadcasted_iota(jnp.int32, (n, n), 0) == lax.broadcasted_iota(jnp.int32, (n, n), 1)
    ).astype(F32).astype(BF16)
    eye = unit(pix)
    for i in range(images):
        turned[i, :pix, :LANES] = dot(eye, patches_ref[i, pl.ds(at_own, LANES), :], COLS_1).astype(BF16)
        turned[i, :pix, LANES:] = dot(eye, patches_ref[i, pl.ds(at_shared, 64), :], COLS_1).astype(BF16)
        turned[i, pix:, :] = jnp.zeros((padded - pix, span), BF16)
    size = 16 * images
    row = lax.broadcasted_iota(jnp.int32, (size, size), 0)
    column = lax.broadcasted_iota(jnp.int32, (size, size), 1)
    order = (row // images == column % 16) & (row % images == column // 16)
    order = order.astype(F32).astype(BF16)
    for b in range(padded // 16):
        rows = turned[:, 16 * b : 16 * b + 16, :].reshape(size, span)
        out = dot(order, rows).astype(BF16)
        own[16 * b : 16 * b + 16] = out[:, :LANES].reshape(16, images, LANES)
        shared[16 * b : 16 * b + 16] = out[:, LANES:].reshape(16, images, 64)
    count = pix // 2
    quarter = count // 2
    for h in range(2):
        base = h * count
        half = out_ref.at[h]
        half[:count] = own[base : base + count]
        half[count:] = jnp.concatenate(
            [shared[base : base + quarter], shared[base + quarter : base + count]], axis=2
        )


def pack(where, patches):
    images, span, pix = patches.shape
    padded = -(-pix // 16) * 16
    half = pix // 2
    return call(
        pack_kernel,
        shape((2, half + half // 2, images, LANES), BF16),
        limit=20,
        in_specs=[SMEM, VMEM],
        scratch_shapes=[
            pltpu.VMEM((images, padded, span), BF16),
            pltpu.VMEM((padded, images, LANES), BF16),
            pltpu.VMEM((padded, images, 64), BF16),
        ],
        name="pack_patches",
    )(where, patches)


def forward_kernel(
    groups, pix, acts_ref, first_ref, second_ref, aux_ref, labels_ref, *refs
):
    hidden_ref, feature_ref, aux_pre_ref, sent_ref, pooled = refs[-5:]
    step = pl.program_id(0)
    block, images, width = acts_ref.shape
    flat = acts_ref[...].reshape(block * images, width)
    hidden = jnp.maximum(dot(flat, first_ref[...]), 0.0).astype(BF16)
    hidden_ref[...] = hidden
    feature = (flat.astype(F32) + dot(hidden, second_ref[...])).astype(BF16)
    feature_ref[...] = feature
    sums = jnp.sum(feature.reshape(block, images, width).astype(F32), axis=0)

    @pl.when(step == 0)
    def _():
        pooled[...] = sums

    @pl.when(step > 0)
    def _():
        pooled[...] += sums

    @pl.when(step == pl.num_programs(0) - 1)
    def _():
        mean = (pooled[...] / pix).astype(BF16)
        aux_pre = dot(mean, aux_ref[...])
        aux_pre_ref[...] = aux_pre
        head = aux_pre.shape[1]
        part = width // groups
        out = jnp.maximum(aux_pre, 0.0).astype(BF16)
        label = labels_ref[...]
        lane = lax.broadcasted_iota(jnp.int32, (label.shape[0], LANES), 1)
        digits = jnp.where(lane == 0, label // LANES, jnp.where(lane == 1, label % LANES, 0))
        digits = digits.astype(F32).astype(BF16)
        for d in range(groups):
            sent_ref[d, :, :head] = out
            sent_ref[d, :, head : head + part] = mean[:, d * part : (d + 1) * part]
            sent_ref[d, :, head + LANES :] = digits


def forward(acts, first, second, aux, labels, groups, before):
    pix, images, width = acts.shape
    inner, head = first.shape[1], aux.shape[1]
    block = pix // STEPS
    whole = lambda g: (0, 0)
    rows = lambda n: pl.BlockSpec((block * images, n), lambda g: (g, 0))
    return call(
        functools.partial(forward_kernel, groups, pix),
        [
            shape((pix * images, inner), BF16),
            shape((pix * images, width), BF16),
            shape((images, head), F32),
            shape((groups, images, head + 2 * LANES), BF16),
        ],
        limit=58,
        grid=(STEPS,),
        in_specs=[
            pl.BlockSpec((block, images, width), lambda g: (g, 0, 0)),
            pl.BlockSpec(first.shape, whole),
            pl.BlockSpec(second.shape, whole),
            pl.BlockSpec(aux.shape, whole),
            pl.BlockSpec((images, 1), whole),
            *[ANY] * len(before),
        ],
        out_specs=[
            rows(inner),
            rows(width),
            pl.BlockSpec((images, head), whole),
            pl.BlockSpec((groups, images, head + 2 * LANES), lambda g: (0, 0, 0)),
        ],
        scratch_shapes=[pltpu.VMEM((images, width), F32)],
        name="forward",
    )(acts, first, second, aux, labels, *before)


def patch_operands(own_blocks, shared_blocks):
    per_half = STEPS // 2
    own = lambda g, where: (g // per_half, g % per_half, 0, 0)
    shared = lambda g, where: (g // per_half, per_half, 0, 0)
    args = [*own_blocks, *shared_blocks]
    dims = (1, args[0].shape[1] // (per_half + 1)) + args[0].shape[2:]
    specs = [pl.BlockSpec(dims, own)] * len(own_blocks) + [pl.BlockSpec(dims, shared)] * len(shared_blocks)
    return args, specs


def lay_target(step, where_ref, refs, target):
    if len(refs) == 1:
        target[...] = refs[0][...]
        return
    own, shared = refs[:-2], refs[-2:]
    for j, ref in enumerate(own):
        target[:, :, j * LANES : (j + 1) * LANES] = ref[0]
    first, second = shared[0][0].astype(F32), shared[1][0].astype(F32)
    even_first = where_ref[PARITY] == 0
    even = jnp.where(even_first, first, second)
    odd = jnp.where(even_first, second, first)
    turn = lambda v: jnp.concatenate([v[:, :, 64:], v[:, :, :64]], axis=2)
    upper = step % (STEPS // 2) == 1
    low = jnp.where(upper, turn(even), even)
    high = jnp.where(upper, odd, turn(odd))
    lane = lax.broadcasted_iota(jnp.int32, even.shape, 2)
    target[:, :, len(own) * LANES :] = jnp.where(lane < 64, low, high).astype(BF16)


def deal(where_ref, sums, part, keep_ref, send_ref):
    core = where_ref[CORE]
    at = 0
    for value in sums:
        height = value.shape[0]
        for z in range(keep_ref.shape[0]):
            even = value[:, 2 * z * part : (2 * z + 1) * part]
            odd = value[:, (2 * z + 1) * part : (2 * z + 2) * part]
            mine = jnp.where(core == 0, even, odd)
            other = jnp.where(core == 0, odd, even)
            keep_ref[z, at : at + height, :] = mine.astype(BF16)
            send_ref[z, at : at + height, :] = other.astype(BF16)
        at += height


def fetch(source, held, sems, step):
    size = held.shape[0] // STEPS
    copies = [
        pltpu.make_async_copy(source.at[pl.ds(g * size, size)], held.at[pl.ds(g * size, size)], sems.at[g])
        for g in range(STEPS)
    ]

    @pl.when(step == 0)
    def _():
        for copy in copies:
            copy.start()

    for g in range(STEPS):

        @pl.when(step == g)
        def _():
            copies[g].wait()


def early_kernel(groups, scale, n_tiles, n_patch, where_ref, feature_ref, *refs):
    decode_refs, refs = refs[:n_tiles], refs[n_tiles:]
    patch_refs, refs = refs[:n_patch], refs[n_patch:]
    aux_ref, back_ref, keep_ref, send_ref, target, feature, grads, sems = refs
    step = pl.program_id(0)
    size = back_ref.shape[0]
    fetch(feature_ref, feature, sems, step)
    lay_target(step, where_ref, patch_refs, target)
    rows = pl.ds(pl.multiple_of(step * size, size), size)
    decode = jnp.concatenate([ref[...] for ref in decode_refs], axis=1)
    recon = dot(feature[rows], decode)
    grad = ((recon - target[...].reshape(recon.shape).astype(F32)) * scale).astype(BF16)
    grads[rows] = grad
    back_ref[...] = dot(grad, decode, COLS_1)

    @pl.when(step == STEPS - 1)
    def _():
        width = feature.shape[1]
        part = width // groups
        total = dot(grads[...], feature[...], ROWS_0)
        n = total.shape[0]
        deal(where_ref, [total], part, keep_ref, send_ref)
        aux = aux_ref[...].astype(F32)
        images, head = aux.shape
        for c in range(2):
            value = jnp.where(where_ref[CORE] == c, aux, 0.0).astype(BF16)
            for q in range(head // part):
                at = n + (c * (head // part) + q) * images
                for z in range(keep_ref.shape[0]):
                    keep_ref[z, at : at + images, :] = value[:, q * part : (q + 1) * part]
                    send_ref[z, at : at + images, :] = value[:, q * part : (q + 1) * part]


def early_blocks(where, feature, decode, patch_args, patch_specs, aux_grad, images, scale, groups):
    rows, width = feature.shape
    n = EARLY * LANES
    size = rows // STEPS
    part = width // groups
    parts = (groups // 2, n + 2 * aux_grad.size // part, part)
    dealt = pl.BlockSpec(parts, lambda g, where: (0, 0, 0))
    tile = lambda j: pl.BlockSpec((width, LANES), lambda g, where: (0, where[TILES + j]))
    return call(
        functools.partial(early_kernel, groups, scale, EARLY, len(patch_args)),
        [shape((rows, width), F32), shape(parts, BF16), shape(parts, BF16)],
        limit=58,
        flops=6 * rows * width * n,
        moved=rows * (6 * width),
        grid_spec=pltpu.PrefetchScalarGridSpec(
            num_scalar_prefetch=1,
            grid=(STEPS,),
            in_specs=[
                HBM,
                *[tile(j) for j in range(EARLY)],
                *patch_specs,
                pl.BlockSpec(aux_grad.shape, lambda g, where: (0, 0)),
            ],
            out_specs=[pl.BlockSpec((size, width), lambda g, where: (g, 0)), dealt, dealt],
            scratch_shapes=[
                pltpu.VMEM((size // images, images, n), BF16),
                pltpu.VMEM((rows, width), BF16),
                pltpu.VMEM((rows, n), BF16),
                pltpu.SemaphoreType.DMA((STEPS,)),
            ],
        ),
        name="early_blocks",
    )(where, feature, *[decode] * EARLY, *patch_args, aux_grad)


def last_kernel(groups, scale, n_tiles, n_patch, where_ref, feature_ref, hidden_ref, acts_ref, *refs):
    decode_refs, refs = refs[:n_tiles], refs[n_tiles:]
    patch_refs, refs = refs[:n_patch], refs[n_patch:]
    (back_ref, pooled_ref, second_ref, _, keep_ref, send_ref,
     target, feature, hidden, acts, grads, feature_grads, hidden_grads, sems) = refs
    step = pl.program_id(0)
    size, width = back_ref.shape
    fetch(feature_ref, feature, sems.at[0], step)
    fetch(hidden_ref, hidden, sems.at[1], step)
    fetch(acts_ref, acts, sems.at[2], step)
    lay_target(step, where_ref, patch_refs, target)
    rows = pl.ds(pl.multiple_of(step * size, size), size)
    decode = jnp.concatenate([ref[...] for ref in decode_refs], axis=1)
    recon = dot(feature[rows], decode)
    grad = ((recon - target[...].reshape(recon.shape).astype(F32)) * scale).astype(BF16)
    grads[rows] = grad
    images = pooled_ref.shape[0]
    decode_back = back_ref[...] + dot(grad, decode, COLS_1)
    feature_grad = (decode_back.reshape(size // images, images, width) + pooled_ref[...][None]).astype(BF16)
    feature_grad = feature_grad.reshape(size, width)
    feature_grads[rows] = feature_grad
    hidden_back = dot(feature_grad, second_ref[...], COLS_1)
    hidden_grads[rows] = jnp.where(hidden[rows].astype(F32) > 0, hidden_back, 0.0).astype(BF16)

    @pl.when(step == STEPS - 1)
    def _():
        part = width // groups
        total_decode = dot(grads[...], feature[...], ROWS_0)
        total_second = dot(hidden[...], feature_grads[...], ROWS_0)
        total_first = dot(hidden_grads[...], acts[...].reshape(feature.shape), ROWS_0)
        tall = total_second.shape[0] // groups
        second = jnp.concatenate(
            [
                jnp.concatenate(
                    [total_second[d * tall : (d + 1) * tall, q * part : (q + 1) * part] for q in range(groups)], axis=0
                )
                for d in range(groups)
            ],
            axis=1,
        )
        deal(where_ref, [total_decode, second, total_first], part, keep_ref, send_ref)


def last_blocks(
    where, feature, hidden, acts, decode, patch_args, patch_specs, back, pooled, second, before, scale, groups
):
    rows, width = feature.shape
    inner = hidden.shape[1]
    n_tiles = decode.shape[1] // LANES - EARLY
    n = n_tiles * LANES
    size = rows // STEPS
    images = pooled.shape[0]
    parts = (groups // 2, n + 2 * inner, width // groups)
    dealt = pl.BlockSpec(parts, lambda g, where: (0, 0, 0))
    tile = lambda j: pl.BlockSpec((width, LANES), lambda g, where: (0, where[TILES + EARLY + j]))
    whole = lambda g, where: (0, 0)
    return call(
        functools.partial(last_kernel, groups, scale, n_tiles, len(patch_args)),
        [shape(parts, BF16), shape(parts, BF16)],
        limit=58,
        flops=6 * rows * width * (n + inner),
        moved=rows * (8 * width),
        grid_spec=pltpu.PrefetchScalarGridSpec(
            num_scalar_prefetch=1,
            grid=(STEPS,),
            in_specs=[
                HBM,
                HBM,
                HBM,
                *[tile(j) for j in range(n_tiles)],
                *patch_specs,
                pl.BlockSpec((size, width), lambda g, where: (g, 0)),
                pl.BlockSpec(pooled.shape, whole),
                pl.BlockSpec(second.shape, whole),
                ANY,
            ],
            out_specs=[dealt, dealt],
            scratch_shapes=[
                pltpu.VMEM((size // images, images, n), BF16),
                pltpu.VMEM((rows, width), BF16),
                pltpu.VMEM((rows, inner), BF16),
                pltpu.VMEM(acts.shape, BF16),
                pltpu.VMEM((rows, n), BF16),
                pltpu.VMEM((rows, width), BF16),
                pltpu.VMEM((rows, inner), BF16),
                pltpu.SemaphoreType.DMA((3, STEPS)),
            ],
        ),
        name="last_blocks",
    )(where, feature, hidden, acts, *[decode] * n_tiles, *patch_args, back, pooled, second, before)


TOPS, DENOMS = 16, 64


def labels_of(got, head):
    digits = got[:, head + LANES : head + LANES + 2].astype(F32)
    return (digits[:, 0:1] * LANES + digits[:, 1:2]).astype(jnp.int32)


def logits_kernel(where_ref, got_ref, klass_ref, logits_ref, sent_ref):
    groups, images, _ = got_ref.shape
    classes, head = klass_ref.shape
    got = got_ref[...].reshape(groups * images, -1)
    logits = dot(got[:, :head], klass_ref[...], COLS_1)
    logits_ref[...] = logits
    ids = lax.broadcasted_iota(jnp.int32, logits.shape, 1) + where_ref[ME] * classes
    hit = labels_of(got, head) == ids
    top = jnp.max(logits, axis=1, keepdims=True)
    expo = jnp.exp(logits - top)
    denom = jnp.sum(expo, axis=1, keepdims=True)
    own = jnp.sum(jnp.where(hit, expo, 0.0), axis=1, keepdims=True)
    rest = jnp.where(hit, 0.0, expo).astype(BF16)
    onehot = jnp.where(hit, 1.0, 0.0).astype(BF16)
    sent_ref[:, :, :head] = dot(rest, klass_ref[...]).reshape(groups, images, head)
    sent_ref[:, :, head : 2 * head] = dot(onehot, klass_ref[...]).reshape(groups, images, head)
    lane = lax.broadcasted_iota(jnp.int32, (images, LANES), 1)
    cut = lambda value, d: value[d * images : (d + 1) * images]
    common = jnp.zeros((images, LANES), F32)
    for d in range(groups):
        common = jnp.where(lane == TOPS + d, cut(top, d), common)
        common = jnp.where(lane == DENOMS + d, cut(denom, d), common)
    for d in range(groups):
        stats = jnp.where(lane == 1, cut(denom, d), jnp.where(lane == 2, cut(own, d), common))
        sent_ref[d, :, 2 * head :] = jnp.where(lane == 0, cut(top, d), stats)


def class_logits(where, got, klass):
    groups, images, _ = got.shape
    classes, head = klass.shape
    return call(
        logits_kernel,
        [shape((groups * images, classes), F32), shape((groups, images, 2 * head + LANES), F32)],
        limit=16,
        in_specs=[SMEM, VMEM, VMEM],
        name="class_logits",
    )(where, got, klass)


def aux_kernel(pix, norm, got_ref, aux_pre_ref, aux_ref, pooled_ref, grad_ref):
    groups = got_ref.shape[0]
    head = aux_pre_ref.shape[1]
    stats = [got_ref[d, :, 2 * head : 2 * head + 3] for d in range(groups)]
    top = functools.reduce(jnp.maximum, [s[:, 0:1] for s in stats])
    scales = [jnp.exp(s[:, 0:1] - top) for s in stats]
    denom = sum(s[:, 1:2] * f for s, f in zip(stats, scales))
    own = sum(s[:, 2:3] * f for s, f in zip(stats, scales)) / denom
    rest = sum(got_ref[d, :, :head] * scales[d] for d in range(groups)) / (denom * norm)
    row = sum(got_ref[d, :, head : 2 * head] for d in range(groups))
    back = rest + row * ((own - 1.0) / norm).astype(BF16).astype(F32)
    aux_grad = jnp.where(aux_pre_ref[...] > 0, back, 0.0).astype(BF16)
    pooled_ref[...] = dot(aux_grad, aux_ref[...], COLS_1) / pix
    grad_ref[...] = aux_grad


def aux_backward(got, aux_pre, aux, pix, norm):
    images = got.shape[1]
    width, head = aux.shape
    return call(
        functools.partial(aux_kernel, pix, norm),
        [shape((images, width), F32), shape((images, head), BF16)],
        limit=16,
        name="aux_backward",
    )(got, aux_pre, aux)


def class_kernel(norm, n, where_ref, logits_ref, got_ref, stats_ref, grads_ref, class_ref, aux_ref):
    groups, images, _ = got_ref.shape
    head = class_ref.shape[1]
    classes, part = class_ref.shape[0], aux_ref.shape[0]
    got = got_ref[...].reshape(groups * images, -1)
    tops, denoms = [], []
    for d in range(groups):
        top = functools.reduce(jnp.maximum, [stats_ref[e, :, TOPS + d : TOPS + d + 1] for e in range(groups)])
        tops.append(top)
        denoms.append(
            sum(
                stats_ref[e, :, DENOMS + d : DENOMS + d + 1] * jnp.exp(stats_ref[e, :, TOPS + d : TOPS + d + 1] - top)
                for e in range(groups)
            )
        )
    top, denom = jnp.concatenate(tops, axis=0), jnp.concatenate(denoms, axis=0)
    logits = logits_ref[...]
    ids = lax.broadcasted_iota(jnp.int32, logits.shape, 1) + where_ref[ME] * classes
    onehot = jnp.where(labels_of(got, head) == ids, 1.0, 0.0)
    logit_grad = ((jnp.exp(logits - top) / denom - onehot) / norm).astype(BF16)
    class_ref[...] = dot(logit_grad, got[:, :head], ROWS_0)
    total = jnp.zeros(aux_ref.shape, F32)
    for d in range(groups):
        at = n + d % 2 * (head // part) * images
        grad = jnp.concatenate(
            [grads_ref[d // 2, at + q * images : at + (q + 1) * images, :] for q in range(head // part)], axis=1
        )
        pooled = got_ref[d, :, head : head + part]
        total += dot(pooled, grad, ROWS_0).astype(BF16).astype(F32)
    aux_ref[...] = total


def class_backward(where, logits, got, partial, grads, classes, head, norm):
    groups, images, wide = partial.shape
    whole = lambda *dims: pl.BlockSpec(dims, lambda i: (0,) * len(dims))
    part = grads.shape[2]
    return call(
        functools.partial(class_kernel, norm, EARLY * LANES),
        [shape((classes, head), F32), shape((part, head), F32)],
        limit=20,
        flops=2 * groups * images * classes * head,
        moved=4 * classes * head,
        grid=(1,),
        in_specs=[
            SMEM,
            whole(*logits.shape),
            whole(*got.shape),
            pl.BlockSpec((groups, images, LANES), lambda i: (0, 0, wide // LANES - 1)),
            whole(*grads.shape),
        ],
        out_specs=[whole(classes, head), whole(part, head)],
        name="class_backward",
    )(where, logits, got, partial, grads)


def add_cores(keep, send):
    return (keep.astype(F32) + swap(send, "dp", 1).astype(F32)).astype(BF16)


def exchange_chips(parts):
    count = lax.axis_size("dp")
    return exchange(parts, [[z + core for z in range(0, count, 2)] for core in range(2)])


def finish_kernel(inner, n_tiles, where_ref, early_ref, last_ref, first_ref, second_ref, decode_ref):
    chips, _, part = early_ref.shape
    n_last = (n_tiles - EARLY) * LANES
    last = sum(last_ref[z].astype(F32) for z in range(chips))
    first_ref[...] = last[n_last + inner :].T
    tall = second_ref.shape[0]
    for q in range(inner // tall):
        at = n_last + q * tall
        second_ref[:, q * part : (q + 1) * part] = last[at : at + tall]
    early = sum(early_ref[z, : EARLY * LANES].astype(F32) for z in range(chips))
    for j in range(n_tiles):
        value = early[j * LANES : (j + 1) * LANES] if j < EARLY else last[(j - EARLY) * LANES : (j - EARLY + 1) * LANES]
        decode_ref[:, pl.ds(pl.multiple_of(where_ref[TILES + j] * LANES, LANES), LANES)] = value.T


def finish(where, early, last, inner, groups, n_tiles):
    part = early.shape[2]
    return call(
        functools.partial(finish_kernel, inner, n_tiles),
        [shape((part, inner), F32), shape((inner // groups, part * groups), F32), shape((part, n_tiles * LANES), F32)],
        limit=16,
        in_specs=[SMEM, VMEM, VMEM],
        name="finish",
    )(where, early, last)


def local(acts, patches, labels, w_first, w_second, w_decode, w_aux, w_class):
    acts = acts[0].transpose(1, 0, 2)
    pix, images, width = acts.shape
    groups, count = lax.axis_size("dp"), lax.axis_size("section")
    me, section = lax.axis_index("dp"), lax.axis_index("section")
    scale = (groups * images * pix) ** -0.5
    norm = (groups * images) ** 0.5
    first, second, decode, aux, klass = w_first[0], w_second[0], w_decode[0], w_aux[0], w_class[0]
    inner, head = first.shape[1], aux.shape[1]
    n_tiles = decode.shape[1] // LANES
    span = patches.shape[2]
    paired = count == 4 and span == 192

    if paired:
        own_tile = lambda s: 3 * (s >> 1) + 2 * (s & 1)
        shared_tile = lambda s: 3 * (s >> 1) + 1
        tiles = [own_tile(section), own_tile(section ^ 1), own_tile(section ^ 2), shared_tile(section)]
        tiles += [own_tile(section ^ 3), shared_tile(section ^ 2)]
    else:
        tiles = [jnp.int32(j) for j in range(n_tiles)]
    where = jnp.stack([section & 1, me & 1, me, *tiles]).astype(jnp.int32)

    before = []
    if paired:
        packed = pack(where, patches.transpose(0, 2, 1))
        before = [packed]
        near = [swap(packed, "section", 1), swap(packed, "section", 2)]
    hidden, feature, aux_pre, sent = forward(acts, first, second, aux, labels[:, None], groups, before)
    got = exchange(sent)
    if paired:
        packed, got = lax.optimization_barrier((packed, got))
        diagonal = swap(packed, "section", 3)
        early_patches = patch_operands([packed, *near], [packed, near[0]])
        last_patches = patch_operands([diagonal], [near[1], diagonal])
    else:
        target = lax.all_gather(patches, "section", axis=2, tiled=True).transpose(1, 0, 2)
        n_early = EARLY * LANES
        block = lambda n: pl.BlockSpec((pix // STEPS, images, n), lambda g, where: (g, 0, 0))
        early_patches = [target[:, :, :n_early]], [block(n_early)]
        last_patches = [target[:, :, n_early:]], [block(n_tiles * LANES - n_early)]
    logits, partial = class_logits(where, got, klass)
    partial = exchange(partial)
    pooled_grad, aux_grad = aux_backward(partial, aux_pre, aux, pix, norm)
    back, keep, send = early_blocks(where, feature, decode, *early_patches, aux_grad, images, scale, groups)
    chip_early = add_cores(keep, send)
    sum_early = exchange_chips(chip_early)
    keep, send = last_blocks(
        where, feature, hidden, acts, decode, *last_patches, back, pooled_grad, second, chip_early, scale, groups
    )
    sum_last = exchange_chips(add_cores(keep, send))
    grad_class, grad_aux = class_backward(where, logits, got, partial, sum_early, klass.shape[0], head, norm)
    grad_first, grad_second, grad_decode = finish(where, sum_early, sum_last, inner, groups, n_tiles)
    return grad_first[None], grad_second[None], grad_decode[None], grad_aux[None], grad_class[None]


def solution(mesh):
    in_specs = (
        P("section", "dp", None, None),
        P("dp", None, "section"),
        P("dp"),
        P("section", None, None),
        P("section", None, None),
        P("section", None, None),
        P("section", None, None),
        P("section", "dp", None),
    )
    out_specs = (P("section", "dp", None),) * 5
    return jax.shard_map(local, mesh=mesh, in_specs=in_specs, out_specs=out_specs, check_vma=False)
```

time: 458 us -> 173 us (0.38)
  waiting for transfers between devices: 274 us -> 73 us
  matrix products: 74.6 us -> 0 us
  local copies, waits for them, and re-layouts: 78.4 us -> 9.23 us
  Pallas kernels: 0 us -> 60.7 us
  starting transfers between devices: 0.29 us -> 24.4 us
  between operations: 14.3 us -> 0.79 us
  other arithmetic: 15 us -> 4.41 us
    reduce_scatter x4 -> x0, waiting for transfers between devices: 179 us -> none  [the longest x1 118 us: local(): lax.psum_scatter(jnp.dot(logit_grad.T, aux_out, preferred_element_type=jn...]
    all_gather x2 -> x0, waiting for transfers between devices: 80.6 us -> none  [the longest x1 53.2 us: local(): all_rows = lax.all_gather(class_shard, 'dp', axis=0, tiled=True)]
    dot_general x13 -> x0, matrix products: 74.6 us -> none  [the longest x1 12.1 us: local(): jnp.dot(flat.T, hidden_grad, preferred_element_type=jnp.float32)]
    pallas_call x0 -> x8, Pallas kernels: none -> 60.7 us  [the longest x1 21.7 us: last_blocks(): call(functools.partial(last_kernel, groups, scale, n_tiles, len(patch_arg...]
    all_to_all x0 -> x4, waiting for transfers between devices: none -> 50.2 us  [exchange(): lax.all_to_all(value, 'dp', 0, 0, axis_index_groups=groups, tiled=True)]
    convert_element_type x4 -> x0, local copies, waits for them, and re-layouts: 36 us -> none  [the longest x2 18.3 us: local(): target.astype(jnp.float32)]
    ppermute x0 -> x5, waiting for transfers between devices: none -> 22.8 us  [swap(): return lax.ppermute(value, axis, [(i, i ^ bits) for i in range(count)])]
    all_to_all x0 -> x4, starting transfers between devices: none -> 18.5 us  [exchange(): lax.all_to_all(value, 'dp', 0, 0, axis_index_groups=groups, tiled=True)]
  transfers between devices with their start and end apart: 7 -> 9, of which waited for: 6 -> 6; matrix products, arithmetic and copies ran while one was open for 35% -> 3% of each run, Pallas kernels for 0% -> 14%
where the time goes in v3:
time: 173 us
  waiting for transfers between devices  73 us (42%)
  Pallas kernels  60.7 us (35%)
  starting transfers between devices  24.4 us (14%)
  local copies, waits for them, and re-layouts  9.23 us (5%)
  other arithmetic  4.41 us (3%)
    all_to_all x4, waiting for transfers between devices, exchange(): lax.all_to_all(value, 'dp', 0, 0, axis_index_groups=groups, tiled=True)  50.2 us
    ppermute x5, waiting for transfers between devices, swap(): return lax.ppermute(value, axis, [(i, i ^ bits) for i in range(count)])  22.8 us
    pallas_call x1, Pallas kernels, last_blocks(): call(functools.partial(last_kernel, groups, scale, n_tiles, len(patch_arg...  21.7 us
    all_to_all x4, starting transfers between devices, exchange(): lax.all_to_all(value, 'dp', 0, 0, axis_index_groups=groups, tiled=True)  18.5 us
    pallas_call x1, Pallas kernels, early_blocks(): call(functools.partial(early_kernel, groups, scale, EARLY, len(patch_args...  18.2 us
    pallas_call x1, Pallas kernels, forward(): call(functools.partial(forward_kernel, groups, pix), [shape((pix * images...  11.3 us
    unnamed x34, local copies, waits for them, and re-layouts  7.82 us
    ppermute x5, starting transfers between devices, swap(): return lax.ppermute(value, axis, [(i, i ^ bits) for i in range(count)])  5.87 us
  transfers between devices with their start and end apart: 9, of which 6 were waited for; matrix products, arithmetic and copies ran while one was open for 3% of the time, Pallas kernels for 14%

profile of v3, /device:TPU:0, one launch (start us, length us, event | category | flops | bytes accessed | tf_op | source)
XLA Modules:
  0.0 172.5 jit_solution(12066199824932784588)
XLA Ops:
  0.7 1.3 copy.13.labels_ref
  2.0 0.1 stack.39.where_ref
  2.1 1.4 copy-done.5
  3.5 2.4 %pack_patches.1.refs_0_.refs_4_.refs_7_ = bf16[2,147,16,128]{3,2,1,0:T(8,128)(2,1)S(1)} custom-call(s32[9]{0:T(128)S(1)} %stack.39.where_ref, bf16[16,192,196]{2,1,0:T(8,128)(2,1)S(1)} %bitcast.26), custom_call_target="tpu_custom_call" | custom-call | tf_op jit(solution)/shard_map/pack_patches/pallas_call | solution.py:94
  5.9 1.1 copy-done
  6.9 11.3 %forward.1 = (bf16[3136,256]{1,0:T(8,128)(2,1)}, bf16[3136,1024]{1,0:T(8,128)(2,1)}, f32[16,512]{1,0:T(8,128)}, bf16[8,16,768]{2,1,0:T(8,128)(2,1)}) custom-call(bf16[196,16,1024]{2,1,0:T(8,128)(2,1)} %bitcast.28, bf16[1024,256]{1,0:T(8,128)(2,1)} %bitcast.30, bf16[256,1024]{1,0:T(8,128)(2,1)} %bitcast.31, bf16[1024,512]{1,0:T(8,128)(2,1)} %bitcast.24, ...), custom_call_target="tpu_custom_call" | custom-call | tf_op jit(solution)/shard_map/forward/pallas_call | solution.py:153
  18.2 0.0 copy-start.2
  18.2 6.5 %all-to-all-start = ((bf16[8,16,768]{2,1,0:T(8,128)(2,1)}), bf16[8,16,768]{2,1,0:T(8,128)(2,1)S(1)}, u32[]{:S(2)}, u32[]{:S(2)}) async-start(bf16[8,16,768]{2,1,0:T(8,128)(2,1)} %get-tuple-element.26), calls=%async_computation | async-start | bytes 393216 | tf_op jit(solution)/shard_map/all_to_all | solution.py:51
  24.7 0.0 copy-done.1
  24.7 1.6 collective-permute-start
  26.2 1.5 collective-permute-start.1
  27.7 5.3 %all-to-all-done.got_ref = bf16[8,16,768]{2,1,0:T(8,128)(2,1)S(1)} async-done(((bf16[8,16,768]{2,1,0:T(8,128)(2,1)}), bf16[8,16,768]{2,1,0:T(8,128)(2,1)S(1)}, u32[]{:S(2)}, u32[]{:S(2)}) %all-to-all-start) | async-done | bytes 196640 | tf_op jit(solution)/shard_map/all_to_all | solution.py:51
  33.0 0.0 copy-done.11
  33.0 1.4 copy-done.6
  34.4 1.9 %class_logits.1 = (f32[128,1408]{1,0:T(8,128)S(1)}, f32[8,16,1152]{2,1,0:T(8,128)S(1)}) custom-call(s32[9]{0:T(128)S(1)} %stack.39.where_ref, bf16[8,16,768]{2,1,0:T(8,128)(2,1)S(1)} %all-to-all-done.got_ref, bf16[1408,512]{1,0:T(8,128)(2,1)S(1)} %bitcast.27), custom_call_target="tpu_custom_call" | custom-call | tf_op jit(solution)/shard_map/class_logits/pallas_call | solution.py:443
  36.4 0.0 copy-start.7
  36.4 0.9 copy-done.7
  37.3 0.8 copy-done.9
  38.1 3.7 %all-to-all-start.1 = ((f32[8,16,1152]{2,1,0:T(8,128)}), f32[8,16,1152]{2,1,0:T(8,128)S(1)}, u32[]{:S(2)}, u32[]{:S(2)}) async-start(f32[8,16,1152]{2,1,0:T(8,128)} %copy-done.9), calls=%async_computation.1 | async-start | bytes 1179648 | tf_op jit(solution)/shard_map/all_to_all | solution.py:51
  41.9 2.5 %collective-permute-start.3 = (bf16[2,147,16,128]{3,2,1,0:T(8,128)(2,1)S(1)}, bf16[2,147,16,128]{3,2,1,0:T(8,128)(2,1)}, u32[]{:S(2)}, u32[]{:S(2)}) collective-permute-start(bf16[2,147,16,128]{3,2,1,0:T(8,128)(2,1)S(1)} %copy-done.1), channel_id=1, source_target_pairs={{0,24},{8,16},{16,8},{24,0},{1,25},{9,17},{17,9},{25,1},{2,26},{10... | collective-permute-start | bytes 3612680 | tf_op jit(solution)/shard_map/ppermute | solution.py:47
  44.4 14.0 %all-to-all-done.1.got_ref.stats_ref = f32[8,16,1152]{2,1,0:T(8,128)S(1)} async-done(((f32[8,16,1152]{2,1,0:T(8,128)}), f32[8,16,1152]{2,1,0:T(8,128)S(1)}, u32[]{:S(2)}, u32[]{:S(2)}) %all-to-all-start.1) | async-done | bytes 589856 | tf_op jit(solution)/shard_map/all_to_all | solution.py:51
  58.4 0.0 copy-done.2
  58.4 0.0 copy-done.10
  58.4 0.6 aux_backward.1
  58.9 0.0 copy-done.3
  58.9 0.6 copy-done.13
  59.6 0.6 copy-done.14
  60.2 0.0 collective-permute-done.refs_5_.refs_8_
  60.2 20.5 %collective-permute-done.1.refs_6_.refs_3_ = bf16[2,147,16,128]{3,2,1,0:T(8,128)(2,1)} collective-permute-done((bf16[2,147,16,128]{3,2,1,0:T(8,128)(2,1)S(1)}, bf16[2,147,16,128]{3,2,1,0:T(8,128)(2,1)}, u32[]{:S(2)}, u32[]{:S(2)}) %collective-permute-start.1) | collective-permute-done | bytes 1204256 | tf_op jit(solution)/shard_map/ppermute | solution.py:47
  80.7 18.2 %early_blocks.1 = (f32[3136,1024]{1,0:T(8,128)}, bf16[4,640,128]{2,1,0:T(8,128)(2,1)}, bf16[4,640,128]{2,1,0:T(8,128)(2,1)}) custom-call(s32[9]{0:T(128)} %copy-done.11, bf16[3136,1024]{1,0:T(8,128)(2,1)} %get-tuple-element.25.feature_ref, bf16[1024,768]{1,0:T(8,128)(2,1)} %bitcast.35, bf16[1024,768]{1,0:T(8,128)(2,1)} %bitcast.36, ...), custom_call_target="tpu_custom_call" | custom-call | flops 9865003008 | bytes 19267584 | tf_op jit(solution)/shard_map/early_blocks/pallas_call | solution.py:286
  98.9 0.1 collective-permute-start.2
  99.0 2.3 %collective-permute-done.2 = bf16[4,640,128]{2,1,0:T(8,128)(2,1)S(1)} collective-permute-done((bf16[4,640,128]{2,1,0:T(8,128)(2,1)}, bf16[4,640,128]{2,1,0:T(8,128)(2,1)S(1)}, u32[]{:S(2)}, u32[]{:S(2)}) %collective-permute-start.2) | collective-permute-done | bytes 655392 | tf_op jit(solution)/shard_map/ppermute | solution.py:47
  101.3 2.1 %add_convert_fusion.1.refs_8_ = bf16[4,640,128]{2,1,0:T(8,128)(2,1)} fusion(bf16[4,640,128]{2,1,0:T(8,128)(2,1)S(1)} %collective-permute-done.2, bf16[4,640,128]{2,1,0:T(8,128)(2,1)} %get-tuple-element.32), kind=kLoop, calls=%fused_computation.1 | loop fusion | flops 1310720 | bytes 1966080 | tf_op jit(solution)/shard_map/convert_element_type | solution.py:535
  103.4 0.0 collective-permute-done.3.refs_2_.refs_4_
  103.4 21.7 %last_blocks.1 = (bf16[4,768,128]{2,1,0:T(8,128)(2,1)}, bf16[4,768,128]{2,1,0:T(8,128)(2,1)}) custom-call(s32[9]{0:T(128)} %copy-done.11, bf16[3136,1024]{1,0:T(8,128)(2,1)} %get-tuple-element.25.feature_ref, bf16[3136,256]{1,0:T(8,128)(2,1)} %get-tuple-element.34.hidden_ref, bf16[196,16,1024]{2,1,0:T(8,128)(2,1)} %bitcast.29, bf16[1024,768]{1,0:T(8,128)(2,1)} %bitcast.39, ...), custom_call_target="tpu_custom_call" | custom-call | flops 9865003008 | bytes 25690112 | tf_op jit(solution)/shard_map/last_blocks/pallas_call | solution.py:369
  125.1 0.0 copy-start.15
  125.1 0.2 collective-permute-start.4
  125.3 4.9 %all-to-all-start.2 = ((bf16[4,640,128]{2,1,0:T(8,128)(2,1)}), bf16[4,640,128]{2,1,0:T(8,128)(2,1)S(1)}, u32[]{:S(2)}, u32[]{:S(2)}) async-start(bf16[4,640,128]{2,1,0:T(8,128)(2,1)} %add_convert_fusion.1.refs_8_), calls=%async_computation.2 | async-start | bytes 1310720 | tf_op jit(solution)/shard_map/all_to_all | solution.py:51
  130.2 0.0 collective-permute-done.4
  130.2 0.9 copy-done.16
  131.1 0.0 copy-done.15
  131.1 2.3 %add_convert_fusion = bf16[4,768,128]{2,1,0:T(8,128)(2,1)} fusion(bf16[4,768,128]{2,1,0:T(8,128)(2,1)} %copy-done.16, bf16[4,768,128]{2,1,0:T(8,128)(2,1)S(1)} %copy-done.15), kind=kLoop, calls=%fused_computation | loop fusion | flops 1572864 | bytes 2359296 | tf_op jit(solution)/shard_map/convert_element_type | solution.py:535
  133.4 14.5 %all-to-all-done.2.early_ref.grads_ref = bf16[4,640,128]{2,1,0:T(8,128)(2,1)S(1)} async-done(((bf16[4,640,128]{2,1,0:T(8,128)(2,1)}), bf16[4,640,128]{2,1,0:T(8,128)(2,1)S(1)}, u32[]{:S(2)}, u32[]{:S(2)}) %all-to-all-start.2) | async-done | bytes 655392 | tf_op jit(solution)/shard_map/all_to_all | solution.py:51
  147.9 3.5 %all-to-all-start.3 = ((bf16[4,768,128]{2,1,0:T(8,128)(2,1)}), bf16[4,768,128]{2,1,0:T(8,128)(2,1)S(1)}, u32[]{:S(2)}, u32[]{:S(2)}) async-start(bf16[4,768,128]{2,1,0:T(8,128)(2,1)} %add_convert_fusion), calls=%async_computation.3 | async-start | bytes 1572864 | tf_op jit(solution)/shard_map/all_to_all | solution.py:51
  151.4 0.0 copy-done.4
  151.4 3.2 %class_backward.1 = (f32[1408,512]{1,0:T(8,128)}, f32[128,512]{1,0:T(8,128)}) custom-call(s32[9]{0:T(128)S(1)} %copy-done.12, f32[128,1408]{1,0:T(8,128)S(1)} %copy-done.8, bf16[8,16,768]{2,1,0:T(8,128)(2,1)S(1)} %copy-done.4, f32[8,16,1152]{2,1,0:T(8,128)S(1)} %all-to-all-done.1.got_ref.stats_ref, bf16[4,640,128]{2,1,0:T(8,128)(2,1)S(1)} %all-to-all-done.2.early_ref.grads_ref), custom_call_target="tpu_custom_call" | custom-call | flops 184549376 | bytes 2883584 | tf_op jit(solution)/shard_map/class_backward/pallas_call | solution.py:515
  154.6 16.4 %all-to-all-done.3.last_ref = bf16[4,768,128]{2,1,0:T(8,128)(2,1)S(1)} async-done(((bf16[4,768,128]{2,1,0:T(8,128)(2,1)}), bf16[4,768,128]{2,1,0:T(8,128)(2,1)S(1)}, u32[]{:S(2)}, u32[]{:S(2)}) %all-to-all-start.3) | async-done | bytes 786464 | tf_op jit(solution)/shard_map/all_to_all | solution.py:51
  171.0 1.5 finish.1
  (16 shorter events, 0.0 us)
Async XLA Ops:
  2.1 30.9 %copy-start.11 = (s32[9]{0:T(128)}, s32[9]{0:T(128)S(1)}, u32[]{:S(2)}) copy-start(s32[9]{0:T(128)S(1)} %stack.39.where_ref) | copy-start | bytes 112
  2.1 1.4 copy-start.5
  5.9 1.1 copy-start
  6.9 17.7 %copy-start.1 = (bf16[2,147,16,128]{3,2,1,0:T(8,128)(2,1)S(1)}, bf16[2,147,16,128]{3,2,1,0:T(8,128)(2,1)}, u32[]{:S(2)}) copy-start(bf16[2,147,16,128]{3,2,1,0:T(8,128)(2,1)} %copy-done) | copy-start | bytes 3612676
  18.2 40.2 %copy-start.2 = (bf16[1,1024,512]{2,1,0:T(8,128)(2,1)S(1)}, bf16[1,1024,512]{2,1,0:T(8,128)(2,1)}, u32[]{:S(2)}) copy-start(bf16[1,1024,512]{2,1,0:T(8,128)(2,1)} %param.14) | copy-start | bytes 3145732
  18.2 14.8 %all-to-all-start = ((bf16[8,16,768]{2,1,0:T(8,128)(2,1)}), bf16[8,16,768]{2,1,0:T(8,128)(2,1)S(1)}, u32[]{:S(2)}, u32[]{:S(2)}) async-start(bf16[8,16,768]{2,1,0:T(8,128)(2,1)} %get-tuple-element.26), calls=%async_computation | async-start | bytes 393216 | tf_op jit(solution)/shard_map/all_to_all | solution.py:51
  24.7 35.5 %collective-permute-start = (bf16[2,147,16,128]{3,2,1,0:T(8,128)(2,1)S(1)}, bf16[2,147,16,128]{3,2,1,0:T(8,128)(2,1)}, u32[]{:S(2)}, u32[]{:S(2)}) collective-permute-start(bf16[2,147,16,128]{3,2,1,0:T(8,128)(2,1)S(1)} %copy-done.1), channel_id=1, source_target_pairs={{0,8},{8,0},{16,24},{24,16},{1,9},{9,1},{17,25},{25,17},{2,10},{10... | collective-permute-start | bytes 3612680 | tf_op jit(solution)/shard_map/ppermute | solution.py:47
  26.2 54.5 %collective-permute-start.1 = (bf16[2,147,16,128]{3,2,1,0:T(8,128)(2,1)S(1)}, bf16[2,147,16,128]{3,2,1,0:T(8,128)(2,1)}, u32[]{:S(2)}, u32[]{:S(2)}) collective-permute-start(bf16[2,147,16,128]{3,2,1,0:T(8,128)(2,1)S(1)} %copy-done.1), channel_id=1, source_target_pairs={{0,16},{8,24},{16,0},{24,8},{1,17},{9,25},{17,1},{25,9},{2,18},{10... | collective-permute-start | bytes 3612680 | tf_op jit(solution)/shard_map/ppermute | solution.py:47
  33.0 25.9 %copy-start.3 = (bf16[8,16,768]{2,1,0:T(8,128)(2,1)}, bf16[8,16,768]{2,1,0:T(8,128)(2,1)S(1)}, u32[]{:S(2)}) copy-start(bf16[8,16,768]{2,1,0:T(8,128)(2,1)S(1)} %all-to-all-done.got_ref) | copy-start | bytes 589828
  33.0 1.4 copy-start.6
  34.4 23.9 %copy-start.10 = (f32[16,512]{1,0:T(8,128)S(1)}, f32[16,512]{1,0:T(8,128)}, u32[]{:S(2)}) copy-start(f32[16,512]{1,0:T(8,128)} %get-tuple-element.30.aux_pre_ref) | copy-start | bytes 98308
  36.4 0.9 copy-start.7
  37.3 0.8 copy-start.9
  38.1 20.2 %all-to-all-start.1 = ((f32[8,16,1152]{2,1,0:T(8,128)}), f32[8,16,1152]{2,1,0:T(8,128)S(1)}, u32[]{:S(2)}, u32[]{:S(2)}) async-start(f32[8,16,1152]{2,1,0:T(8,128)} %copy-done.9), calls=%async_computation.1 | async-start | bytes 1179648 | tf_op jit(solution)/shard_map/all_to_all | solution.py:51
  41.9 61.5 %collective-permute-start.3 = (bf16[2,147,16,128]{3,2,1,0:T(8,128)(2,1)S(1)}, bf16[2,147,16,128]{3,2,1,0:T(8,128)(2,1)}, u32[]{:S(2)}, u32[]{:S(2)}) collective-permute-start(bf16[2,147,16,128]{3,2,1,0:T(8,128)(2,1)S(1)} %copy-done.1), channel_id=1, source_target_pairs={{0,24},{8,16},{16,8},{24,0},{1,25},{9,17},{17,9},{25,1},{2,26},{10... | collective-permute-start | bytes 3612680 | tf_op jit(solution)/shard_map/ppermute | solution.py:47
  58.9 0.6 copy-start.13
  59.6 0.6 copy-start.14
  98.9 2.4 %collective-permute-start.2 = (bf16[4,640,128]{2,1,0:T(8,128)(2,1)}, bf16[4,640,128]{2,1,0:T(8,128)(2,1)S(1)}, u32[]{:S(2)}, u32[]{:S(2)}) collective-permute-start(bf16[4,640,128]{2,1,0:T(8,128)(2,1)} %get-tuple-element.33), channel_id=1, source_target_pairs={{0,1},{1,0},{2,3},{3,2},{4,5},{5,4},{6,7},{7,6},{8,9},{9,8},{10,11... | collective-permute-start | bytes 1966088 | tf_op jit(solution)/shard_map/ppermute | solution.py:47
  125.1 6.0 %copy-start.15 = (bf16[4,768,128]{2,1,0:T(8,128)(2,1)S(1)}, bf16[4,768,128]{2,1,0:T(8,128)(2,1)}, u32[]{:S(2)}) copy-start(bf16[4,768,128]{2,1,0:T(8,128)(2,1)} %get-tuple-element.37) | copy-start | bytes 2359300
  125.1 5.1 %collective-permute-start.4 = (bf16[4,768,128]{2,1,0:T(8,128)(2,1)}, bf16[4,768,128]{2,1,0:T(8,128)(2,1)S(1)}, u32[]{:S(2)}, u32[]{:S(2)}) collective-permute-start(bf16[4,768,128]{2,1,0:T(8,128)(2,1)} %get-tuple-element.38), channel_id=1, source_target_pairs={{0,1},{1,0},{2,3},{3,2},{4,5},{5,4},{6,7},{7,6},{8,9},{9,8},{10,11... | collective-permute-start | bytes 2359304 | tf_op jit(solution)/shard_map/ppermute | solution.py:47
  125.3 22.6 %all-to-all-start.2 = ((bf16[4,640,128]{2,1,0:T(8,128)(2,1)}), bf16[4,640,128]{2,1,0:T(8,128)(2,1)S(1)}, u32[]{:S(2)}, u32[]{:S(2)}) async-start(bf16[4,640,128]{2,1,0:T(8,128)(2,1)} %add_convert_fusion.1.refs_8_), calls=%async_computation.2 | async-start | bytes 1310720 | tf_op jit(solution)/shard_map/all_to_all | solution.py:51
  130.2 0.9 copy-start.16
  131.1 20.3 %copy-start.4 = (bf16[8,16,768]{2,1,0:T(8,128)(2,1)S(1)}, bf16[8,16,768]{2,1,0:T(8,128)(2,1)}, u32[]{:S(2)}) copy-start(bf16[8,16,768]{2,1,0:T(8,128)(2,1)} %copy-done.3) | copy-start | bytes 589828
  131.1 20.3 %copy-start.8 = (f32[128,1408]{1,0:T(8,128)S(1)}, f32[128,1408]{1,0:T(8,128)}, u32[]{:S(2)}) copy-start(f32[128,1408]{1,0:T(8,128)} %copy-done.7) | copy-start | bytes 2162692
  131.1 20.3 %copy-start.12 = (s32[9]{0:T(128)S(1)}, s32[9]{0:T(128)}, u32[]{:S(2)}) copy-start(s32[9]{0:T(128)} %copy-done.11) | copy-start | bytes 112
  147.9 23.1 %all-to-all-start.3 = ((bf16[4,768,128]{2,1,0:T(8,128)(2,1)}), bf16[4,768,128]{2,1,0:T(8,128)(2,1)S(1)}, u32[]{:S(2)}, u32[]{:S(2)}) async-start(bf16[4,768,128]{2,1,0:T(8,128)(2,1)} %add_convert_fusion), calls=%async_computation.3 | async-start | bytes 1572864 | tf_op jit(solution)/shard_map/all_to_all | solution.py:51

commit v4 on v3

--- a/solution.py
+++ b/solution.py
@@ -52,7 +52,7 @@
 
 
 def pack_kernel(where_ref, patches_ref, *refs):
-    out_ref, turned, own, shared = refs
+    halves, (turned, own, shared) = refs[:-3], refs[-3:]
     images, span, pix = patches_ref.shape
     padded = turned.shape[1]
     parity = where_ref[PARITY]
@@ -78,9 +78,8 @@
         shared[16 * b : 16 * b + 16] = out[:, LANES:].reshape(16, images, 64)
     count = pix // 2
     quarter = count // 2
-    for h in range(2):
+    for h, half in enumerate(halves):
         base = h * count
-        half = out_ref.at[h]
         half[:count] = own[base : base + count]
         half[count:] = jnp.concatenate(
             [shared[base : base + quarter], shared[base + quarter : base + count]], axis=2
@@ -93,7 +92,7 @@
     half = pix // 2
     return call(
         pack_kernel,
-        shape((2, half + half // 2, images, LANES), BF16),
+        [shape((half + half // 2, images, LANES), BF16)] * 2,
         limit=20,
         in_specs=[SMEM, VMEM],
         scratch_shapes=[
@@ -105,10 +104,13 @@
     )(where, patches)
 
 
-def forward_kernel(
-    groups, pix, acts_ref, first_ref, second_ref, aux_ref, labels_ref, *refs
-):
-    hidden_ref, feature_ref, aux_pre_ref, sent_ref, pooled = refs[-5:]
+def gather_patches(halves):
+    x = [swap(half, "section", 1) for half in halves]
+    y = [swap(half, "section", 2) for half in halves]
+    return [halves, x, y, [swap(y[0], "section", 1), swap(x[1], "section", 2)]]
+
+
+def forward_kernel(acts_ref, first_ref, second_ref, hidden_ref, feature_ref, pooled_ref):
     step = pl.program_id(0)
     block, images, width = acts_ref.shape
     flat = acts_ref[...].reshape(block * images, width)
@@ -120,72 +122,90 @@
 
     @pl.when(step == 0)
     def _():
-        pooled[...] = sums
+        pooled_ref[...] = sums
 
     @pl.when(step > 0)
     def _():
-        pooled[...] += sums
-
-    @pl.when(step == pl.num_programs(0) - 1)
-    def _():
-        mean = (pooled[...] / pix).astype(BF16)
-        aux_pre = dot(mean, aux_ref[...])
-        aux_pre_ref[...] = aux_pre
-        head = aux_pre.shape[1]
-        part = width // groups
-        out = jnp.maximum(aux_pre, 0.0).astype(BF16)
-        label = labels_ref[...]
-        lane = lax.broadcasted_iota(jnp.int32, (label.shape[0], LANES), 1)
-        digits = jnp.where(lane == 0, label // LANES, jnp.where(lane == 1, label % LANES, 0))
-        digits = digits.astype(F32).astype(BF16)
-        for d in range(groups):
-            sent_ref[d, :, :head] = out
-            sent_ref[d, :, head : head + part] = mean[:, d * part : (d + 1) * part]
-            sent_ref[d, :, head + LANES :] = digits
-
-
-def forward(acts, first, second, aux, labels, groups, before):
+        pooled_ref[...] += sums
+
+
+def forward(acts, first, second):
     pix, images, width = acts.shape
-    inner, head = first.shape[1], aux.shape[1]
-    block = pix // STEPS
+    inner = first.shape[1]
+    steps = 7 if pix % 7 == 0 else STEPS
+    block = pix // steps
     whole = lambda g: (0, 0)
     rows = lambda n: pl.BlockSpec((block * images, n), lambda g: (g, 0))
     return call(
-        functools.partial(forward_kernel, groups, pix),
+        forward_kernel,
         [
             shape((pix * images, inner), BF16),
             shape((pix * images, width), BF16),
-            shape((images, head), F32),
-            shape((groups, images, head + 2 * LANES), BF16),
+            shape((images, width), F32),
         ],
         limit=58,
-        grid=(STEPS,),
+        grid=(steps,),
         in_specs=[
             pl.BlockSpec((block, images, width), lambda g: (g, 0, 0)),
             pl.BlockSpec(first.shape, whole),
             pl.BlockSpec(second.shape, whole),
-            pl.BlockSpec(aux.shape, whole),
-            pl.BlockSpec((images, 1), whole),
-            *[ANY] * len(before),
         ],
-        out_specs=[
-            rows(inner),
-            rows(width),
-            pl.BlockSpec((images, head), whole),
-            pl.BlockSpec((groups, images, head + 2 * LANES), lambda g: (0, 0, 0)),
-        ],
-        scratch_shapes=[pltpu.VMEM((images, width), F32)],
+        out_specs=[rows(inner), rows(width), pl.BlockSpec((images, width), whole)],
         name="forward",
-    )(acts, first, second, aux, labels, *before)
-
-
-def patch_operands(own_blocks, shared_blocks):
+    )(acts, first, second)
+
+
+def head_kernel(pix, pooled_ref, aux_ref, labels_ref, *refs):
+    aux_pre_ref, sent_ref = refs[-2:]
+    groups, images, _ = sent_ref.shape
+    width, head = aux_ref.shape
+    part = width // groups
+    mean = (pooled_ref[...] / pix).astype(BF16)
+    aux_pre = dot(mean, aux_ref[...])
+    aux_pre_ref[...] = aux_pre
+    out = jnp.maximum(aux_pre, 0.0).astype(BF16)
+    row = lax.broadcasted_iota(jnp.int32, (images, LANES), 0)
+    lane = lax.broadcasted_iota(jnp.int32, (images, LANES), 1)
+    digits = jnp.zeros((images, LANES), jnp.int32)
+    for i in range(images):
+        label = labels_ref[i]
+        digits = jnp.where((row == i) & (lane == 0), label // LANES, digits)
+        digits = jnp.where((row == i) & (lane == 1), label % LANES, digits)
+    digits = digits.astype(F32).astype(BF16)
+    for d in range(groups):
+        sent_ref[d, :, :head] = out
+        sent_ref[d, :, head : head + part] = mean[:, d * part : (d + 1) * part]
+        sent_ref[d, :, head + LANES :] = digits
+
+
+def aux_head(pooled, aux, labels, pix, groups, before):
+    images, head = pooled.shape[0], aux.shape[1]
+    return call(
+        functools.partial(head_kernel, pix),
+        [shape((images, head), F32), shape((groups, images, head + 2 * LANES), BF16)],
+        limit=16,
+        in_specs=[VMEM, VMEM, SMEM, *[ANY] * len(before)],
+        name="aux_head",
+    )(pooled, aux, labels, *before)
+
+
+def own_index(h):
     per_half = STEPS // 2
-    own = lambda g, where: (g // per_half, g % per_half, 0, 0)
-    shared = lambda g, where: (g // per_half, per_half, 0, 0)
-    args = [*own_blocks, *shared_blocks]
-    dims = (1, args[0].shape[1] // (per_half + 1)) + args[0].shape[2:]
-    specs = [pl.BlockSpec(dims, own)] * len(own_blocks) + [pl.BlockSpec(dims, shared)] * len(shared_blocks)
+    return lambda g, where: (jnp.clip(g - h * per_half, 0, per_half - 1), 0, 0)
+
+
+def patch_operands(blocks, own_blocks, shared_blocks):
+    args, specs = [], []
+    for k in own_blocks:
+        for h, half in enumerate(blocks[k]):
+            dims = (half.shape[0] // 3,) + half.shape[1:]
+            args.append(half)
+            specs.append(pl.BlockSpec(dims, own_index(h)))
+    for k in shared_blocks:
+        for half in blocks[k]:
+            dims = (half.shape[0] // 3,) + half.shape[1:]
+            args.append(half)
+            specs.append(pl.BlockSpec(dims, lambda g, where: (2, 0, 0)))
     return args, specs
 
 
@@ -193,19 +213,30 @@
     if len(refs) == 1:
         target[...] = refs[0][...]
         return
-    own, shared = refs[:-2], refs[-2:]
-    for j, ref in enumerate(own):
-        target[:, :, j * LANES : (j + 1) * LANES] = ref[0]
-    first, second = shared[0][0].astype(F32), shared[1][0].astype(F32)
+    pairs = [refs[j : j + 2] for j in range(0, len(refs), 2)]
+    own, shared = pairs[:-2], pairs[-2:]
+    per_half = STEPS // 2
     even_first = where_ref[PARITY] == 0
-    even = jnp.where(even_first, first, second)
-    odd = jnp.where(even_first, second, first)
-    turn = lambda v: jnp.concatenate([v[:, :, 64:], v[:, :, :64]], axis=2)
-    upper = step % (STEPS // 2) == 1
-    low = jnp.where(upper, turn(even), even)
-    high = jnp.where(upper, odd, turn(odd))
-    lane = lax.broadcasted_iota(jnp.int32, even.shape, 2)
-    target[:, :, len(own) * LANES :] = jnp.where(lane < 64, low, high).astype(BF16)
+    for h in range(2):
+
+        @pl.when(step // per_half == h)
+        def _():
+            for j, pair in enumerate(own):
+                target[:, :, j * LANES : (j + 1) * LANES] = pair[h][...]
+
+    for g in range(STEPS):
+
+        @pl.when(step == g)
+        def _():
+            h, side = g // per_half, g % per_half
+            mine, other = shared[0][h][...].astype(F32), shared[1][h][...].astype(F32)
+            even = jnp.where(even_first, mine, other)
+            odd = jnp.where(even_first, other, mine)
+            turn = lambda v: jnp.concatenate([v[:, :, 64:], v[:, :, :64]], axis=2)
+            lane = lax.broadcasted_iota(jnp.int32, even.shape, 2)
+            low = turn(even) if side else even
+            high = odd if side else turn(odd)
+            target[:, :, len(own) * LANES :] = jnp.where(lane < 64, low, high).astype(BF16)
 
 
 def deal(where_ref, sums, part, keep_ref, send_ref):
@@ -245,7 +276,7 @@
 def early_kernel(groups, scale, n_tiles, n_patch, where_ref, feature_ref, *refs):
     decode_refs, refs = refs[:n_tiles], refs[n_tiles:]
     patch_refs, refs = refs[:n_patch], refs[n_patch:]
-    aux_ref, back_ref, keep_ref, send_ref, target, feature, grads, sems = refs
+    _, back_ref, keep_ref, send_ref, target, feature, grads, sems = refs
     step = pl.program_id(0)
     size = back_ref.shape[0]
     fetch(feature_ref, feature, sems, step)
@@ -261,26 +292,15 @@
     def _():
         width = feature.shape[1]
         part = width // groups
-        total = dot(grads[...], feature[...], ROWS_0)
-        n = total.shape[0]
-        deal(where_ref, [total], part, keep_ref, send_ref)
-        aux = aux_ref[...].astype(F32)
-        images, head = aux.shape
-        for c in range(2):
-            value = jnp.where(where_ref[CORE] == c, aux, 0.0).astype(BF16)
-            for q in range(head // part):
-                at = n + (c * (head // part) + q) * images
-                for z in range(keep_ref.shape[0]):
-                    keep_ref[z, at : at + images, :] = value[:, q * part : (q + 1) * part]
-                    send_ref[z, at : at + images, :] = value[:, q * part : (q + 1) * part]
-
-
-def early_blocks(where, feature, decode, patch_args, patch_specs, aux_grad, images, scale, groups):
+        deal(where_ref, [dot(grads[...], feature[...], ROWS_0)], part, keep_ref, send_ref)
+
+
+def early_blocks(where, feature, decode, patch_args, patch_specs, before, images, scale, groups):
     rows, width = feature.shape
     n = EARLY * LANES
     size = rows // STEPS
     part = width // groups
-    parts = (groups // 2, n + 2 * aux_grad.size // part, part)
+    parts = (groups // 2, n, part)
     dealt = pl.BlockSpec(parts, lambda g, where: (0, 0, 0))
     tile = lambda j: pl.BlockSpec((width, LANES), lambda g, where: (0, where[TILES + j]))
     return call(
@@ -296,7 +316,7 @@
                 HBM,
                 *[tile(j) for j in range(EARLY)],
                 *patch_specs,
-                pl.BlockSpec(aux_grad.shape, lambda g, where: (0, 0)),
+                ANY,
             ],
             out_specs=[pl.BlockSpec((size, width), lambda g, where: (g, 0)), dealt, dealt],
             scratch_shapes=[
@@ -307,19 +327,18 @@
             ],
         ),
         name="early_blocks",
-    )(where, feature, *[decode] * EARLY, *patch_args, aux_grad)
-
-
-def last_kernel(groups, scale, n_tiles, n_patch, where_ref, feature_ref, hidden_ref, acts_ref, *refs):
+    )(where, feature, *[decode] * EARLY, *patch_args, before)
+
+
+def last_kernel(groups, scale, n_tiles, n_patch, where_ref, feature_ref, hidden_ref, *refs):
     decode_refs, refs = refs[:n_tiles], refs[n_tiles:]
     patch_refs, refs = refs[:n_patch], refs[n_patch:]
-    (back_ref, pooled_ref, second_ref, _, keep_ref, send_ref,
-     target, feature, hidden, acts, grads, feature_grads, hidden_grads, sems) = refs
+    (back_ref, pooled_ref, second_ref, _, hidden_grad_ref, keep_ref, send_ref,
+     target, feature, hidden, grads, feature_grads, sems) = refs
     step = pl.program_id(0)
     size, width = back_ref.shape
     fetch(feature_ref, feature, sems.at[0], step)
     fetch(hidden_ref, hidden, sems.at[1], step)
-    fetch(acts_ref, acts, sems.at[2], step)
     lay_target(step, where_ref, patch_refs, target)
     rows = pl.ds(pl.multiple_of(step * size, size), size)
     decode = jnp.concatenate([ref[...] for ref in decode_refs], axis=1)
@@ -332,14 +351,13 @@
     feature_grad = feature_grad.reshape(size, width)
     feature_grads[rows] = feature_grad
     hidden_back = dot(feature_grad, second_ref[...], COLS_1)
-    hidden_grads[rows] = jnp.where(hidden[rows].astype(F32) > 0, hidden_back, 0.0).astype(BF16)
+    hidden_grad_ref[...] = jnp.where(hidden[rows].astype(F32) > 0, hidden_back, 0.0).astype(BF16)
 
     @pl.when(step == STEPS - 1)
     def _():
         part = width // groups
         total_decode = dot(grads[...], feature[...], ROWS_0)
         total_second = dot(hidden[...], feature_grads[...], ROWS_0)
-        total_first = dot(hidden_grads[...], acts[...].reshape(feature.shape), ROWS_0)
         tall = total_second.shape[0] // groups
         second = jnp.concatenate(
             [
@@ -350,59 +368,119 @@
             ],
             axis=1,
         )
-        deal(where_ref, [total_decode, second, total_first], part, keep_ref, send_ref)
-
-
-def last_blocks(
-    where, feature, hidden, acts, decode, patch_args, patch_specs, back, pooled, second, before, scale, groups
-):
+        deal(where_ref, [total_decode, second], part, keep_ref, send_ref)
+
+
+def last_blocks(where, feature, hidden, decode, patch_args, patch_specs, back, pooled, second, before, scale, groups):
     rows, width = feature.shape
     inner = hidden.shape[1]
     n_tiles = decode.shape[1] // LANES - EARLY
     n = n_tiles * LANES
     size = rows // STEPS
     images = pooled.shape[0]
-    parts = (groups // 2, n + 2 * inner, width // groups)
+    parts = (groups // 2, n + inner, width // groups)
     dealt = pl.BlockSpec(parts, lambda g, where: (0, 0, 0))
     tile = lambda j: pl.BlockSpec((width, LANES), lambda g, where: (0, where[TILES + EARLY + j]))
     whole = lambda g, where: (0, 0)
+    block = lambda m: pl.BlockSpec((size, m), lambda g, where: (g, 0))
     return call(
         functools.partial(last_kernel, groups, scale, n_tiles, len(patch_args)),
-        [shape(parts, BF16), shape(parts, BF16)],
+        [shape((rows, inner), BF16), shape(parts, BF16), shape(parts, BF16)],
         limit=58,
-        flops=6 * rows * width * (n + inner),
-        moved=rows * (8 * width),
         grid_spec=pltpu.PrefetchScalarGridSpec(
             num_scalar_prefetch=1,
             grid=(STEPS,),
             in_specs=[
                 HBM,
                 HBM,
-                HBM,
                 *[tile(j) for j in range(n_tiles)],
                 *patch_specs,
-                pl.BlockSpec((size, width), lambda g, where: (g, 0)),
+                block(width),
                 pl.BlockSpec(pooled.shape, whole),
                 pl.BlockSpec(second.shape, whole),
                 ANY,
             ],
-            out_specs=[dealt, dealt],
+            out_specs=[block(inner), dealt, dealt],
             scratch_shapes=[
                 pltpu.VMEM((size // images, images, n), BF16),
                 pltpu.VMEM((rows, width), BF16),
                 pltpu.VMEM((rows, inner), BF16),
-                pltpu.VMEM(acts.shape, BF16),
                 pltpu.VMEM((rows, n), BF16),
                 pltpu.VMEM((rows, width), BF16),
-                pltpu.VMEM((rows, inner), BF16),
-                pltpu.SemaphoreType.DMA((3, STEPS)),
+                pltpu.SemaphoreType.DMA((2, STEPS)),
             ],
         ),
         name="last_blocks",
-    )(where, feature, hidden, acts, *[decode] * n_tiles, *patch_args, back, pooled, second, before)
-
-
-TOPS, DENOMS = 16, 64
+    )(where, feature, hidden, *[decode] * n_tiles, *patch_args, back, pooled, second, before)
+
+
+def first_kernel(groups, cuts, where_ref, grads_ref, acts_ref, kept_ref, sent_ref, _, keep_ref, send_ref, grads, acts, sems):
+    images = acts.shape[1]
+    copies = []
+    for c, (a, b) in enumerate(cuts):
+        copies.append(
+            [
+                pltpu.make_async_copy(
+                    grads_ref.at[pl.ds(a * images, (b - a) * images)], grads.at[pl.ds(a * images, (b - a) * images)], sems.at[0, c]
+                ),
+                pltpu.make_async_copy(acts_ref.at[pl.ds(a, b - a)], acts.at[pl.ds(a, b - a)], sems.at[1, c]),
+            ]
+        )
+    for pair in copies:
+        for copy in pair:
+            copy.start()
+    width = acts.shape[2]
+    done = kept_ref.shape[1]
+    keep_ref[:, :done, :] = kept_ref[...]
+    send_ref[:, :done, :] = sent_ref[...]
+    total = None
+    for pair, (a, b) in zip(copies, cuts):
+        for copy in pair:
+            copy.wait()
+        now = dot(grads[a * images : b * images], acts[a:b].reshape((b - a) * images, width), ROWS_0)
+        total = now if total is None else total + now
+    deal(where_ref, [total], width // groups, keep_ref.at[:, done:], send_ref.at[:, done:])
+
+
+def first_grad(where, hidden_grad, acts, keep, send, before, groups):
+    pix, images, width = acts.shape
+    inner = hidden_grad.shape[1]
+    unit = max(256 // images, 1) * 3
+    cuts = [(a, min(a + unit, pix)) for a in range(0, pix, unit)]
+    if len(cuts) > 1 and 2 * (cuts[-1][1] - cuts[-1][0]) < unit:
+        cuts[-2:] = [(cuts[-2][0], pix)]
+    parts = (keep.shape[0], keep.shape[1] + inner, keep.shape[2])
+    return call(
+        functools.partial(first_kernel, groups, cuts),
+        [shape(parts, BF16), shape(parts, BF16)],
+        limit=58,
+        in_specs=[SMEM, HBM, HBM, VMEM, VMEM, ANY],
+        scratch_shapes=[
+            pltpu.VMEM(hidden_grad.shape, BF16),
+            pltpu.VMEM(acts.shape, BF16),
+            pltpu.SemaphoreType.DMA((2, len(cuts))),
+        ],
+        name="first_grad",
+    )(where, hidden_grad, acts, keep, send, before)
+
+
+TOPS, DENOMS = 3, 19
+DIGIT = 40
+
+
+def to_digits(value):
+    rest, lanes = value, []
+    for _ in range(3):
+        digit = rest.astype(BF16).astype(F32)
+        lanes.append(digit[:, :DIGIT])
+        rest = rest - digit
+    lanes.append(jnp.zeros((value.shape[0], LANES - 3 * DIGIT), F32))
+    return jnp.concatenate(lanes, axis=1).astype(BF16)
+
+
+def from_digits(value):
+    value = value.astype(F32)
+    return sum(value[:, j * DIGIT : (j + 1) * DIGIT] for j in (2, 1, 0))
 
 
 def labels_of(got, head):
@@ -424,8 +502,8 @@
     own = jnp.sum(jnp.where(hit, expo, 0.0), axis=1, keepdims=True)
     rest = jnp.where(hit, 0.0, expo).astype(BF16)
     onehot = jnp.where(hit, 1.0, 0.0).astype(BF16)
-    sent_ref[:, :, :head] = dot(rest, klass_ref[...]).reshape(groups, images, head)
-    sent_ref[:, :, head : 2 * head] = dot(onehot, klass_ref[...]).reshape(groups, images, head)
+    sent_ref[:, :, :head] = dot(rest, klass_ref[...]).astype(BF16).reshape(groups, images, head)
+    sent_ref[:, :, head : 2 * head] = dot(onehot, klass_ref[...]).astype(BF16).reshape(groups, images, head)
     lane = lax.broadcasted_iota(jnp.int32, (images, LANES), 1)
     cut = lambda value, d: value[d * images : (d + 1) * images]
     common = jnp.zeros((images, LANES), F32)
@@ -434,7 +512,7 @@
         common = jnp.where(lane == DENOMS + d, cut(denom, d), common)
     for d in range(groups):
         stats = jnp.where(lane == 1, cut(denom, d), jnp.where(lane == 2, cut(own, d), common))
-        sent_ref[d, :, 2 * head :] = jnp.where(lane == 0, cut(top, d), stats)
+        sent_ref[d, :, 2 * head :] = to_digits(jnp.where(lane == 0, cut(top, d), stats))
 
 
 def class_logits(where, got, klass):
@@ -442,38 +520,43 @@
     classes, head = klass.shape
     return call(
         logits_kernel,
-        [shape((groups * images, classes), F32), shape((groups, images, 2 * head + LANES), F32)],
+        [shape((groups * images, classes), F32), shape((groups, images, 2 * head + LANES), BF16)],
         limit=16,
         in_specs=[SMEM, VMEM, VMEM],
         name="class_logits",
     )(where, got, klass)
 
 
-def aux_kernel(pix, norm, got_ref, aux_pre_ref, aux_ref, pooled_ref, grad_ref):
+def aux_kernel(pix, norm, got_ref, aux_pre_ref, aux_ref, *refs):
+    pooled_ref, grad_ref = refs[-2:]
     groups = got_ref.shape[0]
     head = aux_pre_ref.shape[1]
-    stats = [got_ref[d, :, 2 * head : 2 * head + 3] for d in range(groups)]
+    stats = [from_digits(got_ref[d, :, 2 * head :]) for d in range(groups)]
     top = functools.reduce(jnp.maximum, [s[:, 0:1] for s in stats])
     scales = [jnp.exp(s[:, 0:1] - top) for s in stats]
     denom = sum(s[:, 1:2] * f for s, f in zip(stats, scales))
     own = sum(s[:, 2:3] * f for s, f in zip(stats, scales)) / denom
-    rest = sum(got_ref[d, :, :head] * scales[d] for d in range(groups)) / (denom * norm)
-    row = sum(got_ref[d, :, head : 2 * head] for d in range(groups))
+    rest = sum(got_ref[d, :, :head].astype(F32) * scales[d] for d in range(groups)) / (denom * norm)
+    row = sum(got_ref[d, :, head : 2 * head].astype(F32) for d in range(groups))
     back = rest + row * ((own - 1.0) / norm).astype(BF16).astype(F32)
     aux_grad = jnp.where(aux_pre_ref[...] > 0, back, 0.0).astype(BF16)
     pooled_ref[...] = dot(aux_grad, aux_ref[...], COLS_1) / pix
-    grad_ref[...] = aux_grad
-
-
-def aux_backward(got, aux_pre, aux, pix, norm):
-    images = got.shape[1]
+    images, part = aux_grad.shape[0], grad_ref.shape[1]
+    for q in range(head // part):
+        grad_ref[q * images : (q + 1) * images, :] = aux_grad[:, q * part : (q + 1) * part]
+
+
+def aux_backward(got, aux_pre, aux, before, pix, norm):
+    groups, images, _ = got.shape
     width, head = aux.shape
+    part = width // groups
     return call(
         functools.partial(aux_kernel, pix, norm),
-        [shape((images, width), F32), shape((images, head), BF16)],
+        [shape((images, width), F32), shape((images * head // part, part), BF16)],
         limit=16,
+        in_specs=[VMEM, VMEM, VMEM, *[ANY] * len(before)],
         name="aux_backward",
-    )(got, aux_pre, aux)
+    )(got, aux_pre, aux, *before)
 
 
 def class_kernel(norm, n, where_ref, logits_ref, got_ref, stats_ref, grads_ref, class_ref, aux_ref):
@@ -481,16 +564,12 @@
     head = class_ref.shape[1]
     classes, part = class_ref.shape[0], aux_ref.shape[0]
     got = got_ref[...].reshape(groups * images, -1)
+    stats = [from_digits(stats_ref[e]) for e in range(groups)]
     tops, denoms = [], []
     for d in range(groups):
-        top = functools.reduce(jnp.maximum, [stats_ref[e, :, TOPS + d : TOPS + d + 1] for e in range(groups)])
+        top = functools.reduce(jnp.maximum, [s[:, TOPS + d : TOPS + d + 1] for s in stats])
         tops.append(top)
-        denoms.append(
-            sum(
-                stats_ref[e, :, DENOMS + d : DENOMS + d + 1] * jnp.exp(stats_ref[e, :, TOPS + d : TOPS + d + 1] - top)
-                for e in range(groups)
-            )
-        )
+        denoms.append(sum(s[:, DENOMS + d : DENOMS + d + 1] * jnp.exp(s[:, TOPS + d : TOPS + d + 1] - top) for s in stats))
     top, denom = jnp.concatenate(tops, axis=0), jnp.concatenate(denoms, axis=0)
     logits = logits_ref[...]
     ids = lax.broadcasted_iota(jnp.int32, logits.shape, 1) + where_ref[ME] * classes
@@ -531,8 +610,31 @@
     )(where, logits, got, partial, grads)
 
 
-def add_cores(keep, send):
-    return (keep.astype(F32) + swap(send, "dp", 1).astype(F32)).astype(BF16)
+def chip_kernel(where_ref, keep_ref, got_ref, *refs):
+    out_ref = refs[-1]
+    n = keep_ref.shape[1]
+    out_ref[:, :n, :] = (keep_ref[...].astype(F32) + got_ref[...].astype(F32)).astype(BF16)
+    if len(refs) > 1:
+        mine, other = refs[0][...].astype(F32), refs[1][...].astype(F32)
+        even = where_ref[CORE] == 0
+        pair = [jnp.where(even, mine, other).astype(BF16), jnp.where(even, other, mine).astype(BF16)]
+        size = mine.shape[0]
+        for z in range(out_ref.shape[0]):
+            for c in range(2):
+                out_ref[z, n + c * size : n + (c + 1) * size, :] = pair[c]
+
+
+def add_cores(where, keep, send, *extra):
+    chips, n, part = keep.shape
+    extra = [e for own in extra for e in (own, swap(own, "dp", 1))]
+    rows = n + sum(e.shape[0] for e in extra)
+    return call(
+        chip_kernel,
+        shape((chips, rows, part), BF16),
+        limit=16,
+        in_specs=[SMEM, VMEM, VMEM, *[VMEM] * len(extra)],
+        name="add_cores",
+    )(where, keep, swap(send, "dp", 1), *extra)
 
 
 def exchange_chips(parts):
@@ -588,34 +690,32 @@
         tiles = [jnp.int32(j) for j in range(n_tiles)]
     where = jnp.stack([section & 1, me & 1, me, *tiles]).astype(jnp.int32)
 
-    before = []
+    hidden, feature, pooled = forward(acts, first, second)
     if paired:
-        packed = pack(where, patches.transpose(0, 2, 1))
-        before = [packed]
-        near = [swap(packed, "section", 1), swap(packed, "section", 2)]
-    hidden, feature, aux_pre, sent = forward(acts, first, second, aux, labels[:, None], groups, before)
-    got = exchange(sent)
-    if paired:
-        packed, got = lax.optimization_barrier((packed, got))
-        diagonal = swap(packed, "section", 3)
-        early_patches = patch_operands([packed, *near], [packed, near[0]])
-        last_patches = patch_operands([diagonal], [near[1], diagonal])
+        blocks = gather_patches(pack(where, patches.transpose(0, 2, 1)))
+        before = [blocks[1][0], blocks[2][0]]
+        early_patches = patch_operands(blocks, [0, 1, 2], [0, 1])
+        last_patches = patch_operands(blocks, [3], [2, 3])
     else:
         target = lax.all_gather(patches, "section", axis=2, tiled=True).transpose(1, 0, 2)
+        before = []
         n_early = EARLY * LANES
         block = lambda n: pl.BlockSpec((pix // STEPS, images, n), lambda g, where: (g, 0, 0))
         early_patches = [target[:, :, :n_early]], [block(n_early)]
         last_patches = [target[:, :, n_early:]], [block(n_tiles * LANES - n_early)]
-    logits, partial = class_logits(where, got, klass)
-    partial = exchange(partial)
-    pooled_grad, aux_grad = aux_backward(partial, aux_pre, aux, pix, norm)
-    back, keep, send = early_blocks(where, feature, decode, *early_patches, aux_grad, images, scale, groups)
-    chip_early = add_cores(keep, send)
+    aux_pre, sent = aux_head(pooled, aux, labels, pix, groups, before)
+    got = exchange(sent)
+    logits, sent = class_logits(where, got, klass)
+    partial = exchange(sent)
+    back, keep, send = early_blocks(where, feature, decode, *early_patches, sent, images, scale, groups)
+    pooled_grad, aux_grad = aux_backward(partial, aux_pre, aux, last_patches[0][:2], pix, norm)
+    chip_early = add_cores(where, keep, send, aux_grad)
     sum_early = exchange_chips(chip_early)
-    keep, send = last_blocks(
-        where, feature, hidden, acts, decode, *last_patches, back, pooled_grad, second, chip_early, scale, groups
+    hidden_grad, keep, send = last_blocks(
+        where, feature, hidden, decode, *last_patches, back, pooled_grad, second, chip_early, scale, groups
     )
-    sum_last = exchange_chips(add_cores(keep, send))
+    keep, send = first_grad(where, hidden_grad, acts, keep, send, sum_early, groups)
+    sum_last = exchange_chips(add_cores(where, keep, send))
     grad_class, grad_aux = class_backward(where, logits, got, partial, sum_early, klass.shape[0], head, norm)
     grad_first, grad_second, grad_decode = finish(where, sum_early, sum_last, inner, groups, n_tiles)
     return grad_first[None], grad_second[None], grad_decode[None], grad_aux[None], grad_class[None]

time: 173 us -> 137 us (0.79)
  waiting for transfers between devices: 73 us -> 30 us
  Pallas kernels: 60.7 us -> 71.8 us
  other arithmetic: 4.41 us -> 0 us
    all_to_all x4, waiting for transfers between devices: 50.2 us -> 20.2 us  [exchange(): lax.all_to_all(value, 'dp', 0, 0, axis_index_groups=groups, tiled=True)]
    pallas_call x2 -> x6, Pallas kernels: 13.6 us -> 27 us  [the longest x1 11.9 us: forward(): call(forward_kernel, [shape((pix * images, inner), BF16), shape((pix * im...]
    ppermute x5 -> x9, waiting for transfers between devices: 22.8 us -> 9.83 us  [swap(): return lax.ppermute(value, axis, [(i, i ^ bits) for i in range(count)])]
    convert_element_type x2 -> x0, other arithmetic: 4.41 us -> none  [add_cores(): return (keep.astype(F32) + swap(send, 'dp', 1).astype(F32)).astype(BF16)]
    pallas_call x1, Pallas kernels: 21.7 us -> 18.9 us  [last_blocks(): call(functools.partial(last_kernel, groups, scale, n_tiles, len(patch_arg...]
    ppermute x5 -> x9, starting transfers between devices: 5.87 us -> 7.28 us  [swap(): return lax.ppermute(value, axis, [(i, i ^ bits) for i in range(count)])]
    unnamed x34 -> x42, local copies, waits for them, and re-layouts: 7.82 us -> 7.91 us
  transfers between devices with their start and end apart: 9 -> 13, of which waited for: 6 -> 8; matrix products, arithmetic and copies ran while one was open for 3% -> 0% of each run, Pallas kernels for 14% -> 42%
where the time goes in v4:
time: 137 us; the launch traced here: 136 us
  Pallas kernels  71.8 us (52%)
  waiting for transfers between devices  30 us (22%)
  starting transfers between devices  25.4 us (19%)
  local copies, waits for them, and re-layouts  8 us (6%)
    all_to_all x4, waiting for transfers between devices, exchange(): lax.all_to_all(value, 'dp', 0, 0, axis_index_groups=groups, tiled=True)  20.2 us
    pallas_call x1, Pallas kernels, last_blocks(): call(functools.partial(last_kernel, groups, scale, n_tiles, len(patch_arg...  18.9 us
    pallas_call x1, Pallas kernels, early_blocks(): call(functools.partial(early_kernel, groups, scale, EARLY, len(patch_args...  18.6 us
    all_to_all x4, starting transfers between devices, exchange(): lax.all_to_all(value, 'dp', 0, 0, axis_index_groups=groups, tiled=True)  18.2 us
    pallas_call x1, Pallas kernels, forward(): call(forward_kernel, [shape((pix * images, inner), BF16), shape((pix * im...  11.9 us
    ppermute x9, waiting for transfers between devices, swap(): return lax.ppermute(value, axis, [(i, i ^ bits) for i in range(count)])  9.83 us
    unnamed x42, local copies, waits for them, and re-layouts  7.91 us
    ppermute x9, starting transfers between devices, swap(): return lax.ppermute(value, axis, [(i, i ^ bits) for i in range(count)])  7.28 us
  transfers between devices with their start and end apart: 13, of which 8 were waited for; matrix products, arithmetic and copies ran while one was open for 0% of the time, Pallas kernels for 42%

profile of v4, /device:TPU:0, one launch (start us, length us, event | category | flops | bytes accessed | tf_op | source)
XLA Modules:
  0.0 136.1 jit_solution(7503159306898934564)
XLA Ops:
  0.7 0.1 stack.39.where_ref
  0.7 1.4 %copy-done.6 = bf16[16,196,192]{1,2,0:T(8,128)(2,1)S(1)} copy-done((bf16[16,196,192]{1,2,0:T(8,128)(2,1)S(1)}, bf16[16,196,192]{1,2,0:T(8,128)(2,1)}, u32[]{:S(2)}) %copy-start.6) | copy-done | bytes 1204248
  2.2 3.2 %pack_patches.1 = (bf16[147,16,128]{2,1,0:T(8,128)(2,1)S(1)}, bf16[147,16,128]{2,1,0:T(8,128)(2,1)}) custom-call(s32[9]{0:T(128)S(1)} %stack.39.where_ref, bf16[16,192,196]{2,1,0:T(8,128)(2,1)S(1)} %bitcast.25), custom_call_target="tpu_custom_call" | custom-call | tf_op jit(solution)/shard_map/pack_patches/pallas_call | solution.py:93
  5.4 3.0 %collective-permute-start.2 = (bf16[147,16,128]{2,1,0:T(8,128)(2,1)S(1)}, bf16[147,16,128]{2,1,0:T(8,128)(2,1)S(1)}, u32[]{:S(2)}, u32[]{:S(2)}) collective-permute-start(bf16[147,16,128]{2,1,0:T(8,128)(2,1)S(1)} %get-tuple-element.30.refs_4_.refs_10_), channel_id=1, source_target_pairs={{0,16},{8,24},{16,0},{24,8},{1,17},{9,25},{17,1},{25,9},{2,18},{10... | collective-permute-start | bytes 1806344 | tf_op jit(solution)/shard_map/ppermute | solution.py:47
  8.3 1.5 %collective-permute-start = (bf16[147,16,128]{2,1,0:T(8,128)(2,1)S(1)}, bf16[147,16,128]{2,1,0:T(8,128)(2,1)S(1)}, u32[]{:S(2)}, u32[]{:S(2)}) collective-permute-start(bf16[147,16,128]{2,1,0:T(8,128)(2,1)S(1)} %get-tuple-element.30.refs_4_.refs_10_), channel_id=1, source_target_pairs={{0,8},{8,0},{16,24},{24,16},{1,9},{9,1},{17,25},{25,17},{2,10},{10... | collective-permute-start | bytes 1806344 | tf_op jit(solution)/shard_map/ppermute | solution.py:47
  9.8 0.5 collective-permute-start.1
  10.4 0.0 collective-permute-start.3
  10.4 11.9 %forward.1 = (bf16[3136,256]{1,0:T(8,128)(2,1)}, bf16[3136,1024]{1,0:T(8,128)(2,1)}, f32[16,1024]{1,0:T(8,128)}) custom-call(bf16[196,16,1024]{2,1,0:T(8,128)(2,1)} %bitcast.27, bf16[1024,256]{1,0:T(8,128)(2,1)} %bitcast.37, bf16[256,1024]{1,0:T(8,128)(2,1)} %bitcast.35), custom_call_target="tpu_custom_call" | custom-call | tf_op jit(solution)/shard_map/forward/pallas_call | solution.py:139
  22.3 0.4 collective-permute-done.2.refs_1_.refs_8_.refs_4_
  22.7 2.1 %collective-permute-done.refs_0_.refs_6_.refs_12_ = bf16[147,16,128]{2,1,0:T(8,128)(2,1)S(1)} collective-permute-done((bf16[147,16,128]{2,1,0:T(8,128)(2,1)S(1)}, bf16[147,16,128]{2,1,0:T(8,128)(2,1)S(1)}, u32[]{:S(2)}, u32[]{:S(2)}) %collective-permute-start) | collective-permute-done | bytes 602144 | tf_op jit(solution)/shard_map/ppermute | solution.py:47
  24.9 0.9 copy-done.15
  25.7 1.5 %aux_head.1 = (f32[16,512]{1,0:T(8,128)S(1)}, bf16[8,16,768]{2,1,0:T(8,128)(2,1)}) custom-call(f32[16,1024]{1,0:T(8,128)S(1)} %copy-done.15, bf16[1024,512]{1,0:T(8,128)(2,1)S(1)} %bitcast.23, s32[16]{0:T(128)S(1)} %copy-done.19, bf16[147,16,128]{2,1,0:T(8,128)(2,1)S(1)} %collective-permute-done.refs_0_.refs_6_.refs_12_, ...), custom_call_target="tpu_custom_call" | custom-call | tf_op jit(solution)/shard_map/aux_head/pallas_call | solution.py:183
  27.2 4.9 %all-to-all-start = ((bf16[8,16,768]{2,1,0:T(8,128)(2,1)}), bf16[8,16,768]{2,1,0:T(8,128)(2,1)S(1)}, u32[]{:S(2)}, u32[]{:S(2)}) async-start(bf16[8,16,768]{2,1,0:T(8,128)(2,1)} %get-tuple-element.33), calls=%async_computation | async-start | bytes 393216 | tf_op jit(solution)/shard_map/all_to_all | solution.py:51
  32.1 1.5 %collective-permute-start.5 = (bf16[147,16,128]{2,1,0:T(8,128)(2,1)S(1)}, bf16[147,16,128]{2,1,0:T(8,128)(2,1)S(1)}, u32[]{:S(2)}, u32[]{:S(2)}) collective-permute-start(bf16[147,16,128]{2,1,0:T(8,128)(2,1)S(1)} %collective-permute-done.2.refs_1_.refs_8_.refs_4_), channel_id=1, source_target_pairs={{0,8},{8,0},{16,24},{24,16},{1,9},{9,1},{17,25},{25,17},{2,10},{10... | collective-permute-start | bytes 1806344 | tf_op jit(solution)/shard_map/ppermute | solution.py:47
  33.6 3.8 %collective-permute-done.1.refs_7_.refs_13_ = bf16[147,16,128]{2,1,0:T(8,128)(2,1)} collective-permute-done((bf16[147,16,128]{2,1,0:T(8,128)(2,1)}, bf16[147,16,128]{2,1,0:T(8,128)(2,1)}, u32[]{:S(2)}, u32[]{:S(2)}) %collective-permute-start.1) | collective-permute-done | bytes 602144 | tf_op jit(solution)/shard_map/ppermute | solution.py:47
  37.4 0.1 collective-permute-start.6
  37.5 3.0 %all-to-all-done.got_ref = bf16[8,16,768]{2,1,0:T(8,128)(2,1)S(1)} async-done(((bf16[8,16,768]{2,1,0:T(8,128)(2,1)}), bf16[8,16,768]{2,1,0:T(8,128)(2,1)S(1)}, u32[]{:S(2)}, u32[]{:S(2)}) %all-to-all-start) | async-done | bytes 196640 | tf_op jit(solution)/shard_map/all_to_all | solution.py:51
  40.4 1.4 %copy-done.7 = bf16[1,1408,512]{2,1,0:T(8,128)(2,1)S(1)} copy-done((bf16[1,1408,512]{2,1,0:T(8,128)(2,1)S(1)}, bf16[1,1408,512]{2,1,0:T(8,128)(2,1)}, u32[]{:S(2)}) %copy-start.7) | copy-done | bytes 1441816
  41.8 1.9 %class_logits.1 = (f32[128,1408]{1,0:T(8,128)S(1)}, bf16[8,16,1152]{2,1,0:T(8,128)(2,1)S(1)}) custom-call(s32[9]{0:T(128)S(1)} %stack.39.where_ref, bf16[8,16,768]{2,1,0:T(8,128)(2,1)S(1)} %all-to-all-done.got_ref, bf16[1408,512]{1,0:T(8,128)(2,1)S(1)} %bitcast.26), custom_call_target="tpu_custom_call" | custom-call | tf_op jit(solution)/shard_map/class_logits/pallas_call | solution.py:521
  43.8 0.9 copy-done.9
  44.7 0.7 copy-done.13
  45.4 3.4 %all-to-all-start.1 = ((bf16[8,16,1152]{2,1,0:T(8,128)(2,1)}), bf16[8,16,1152]{2,1,0:T(8,128)(2,1)S(1)}, u32[]{:S(2)}, u32[]{:S(2)}) async-start(bf16[8,16,1152]{2,1,0:T(8,128)(2,1)} %copy-done.13), calls=%async_computation.1 | async-start | bytes 589824 | tf_op jit(solution)/shard_map/all_to_all | solution.py:51
  48.8 0.0 collective-permute-done.3.refs_9_.refs_5_
  48.8 18.6 %early_blocks.1 = (f32[3136,1024]{1,0:T(8,128)}, bf16[4,512,128]{2,1,0:T(8,128)(2,1)}, bf16[4,512,128]{2,1,0:T(8,128)(2,1)}) custom-call(s32[9]{0:T(128)} %copy-done.16, bf16[3136,1024]{1,0:T(8,128)(2,1)} %get-tuple-element.29.feature_ref, bf16[1024,768]{1,0:T(8,128)(2,1)} %bitcast.29, bf16[1024,768]{1,0:T(8,128)(2,1)} %bitcast.30, ...), custom_call_target="tpu_custom_call" | custom-call | flops 9865003008 | bytes 19267584 | tf_op jit(solution)/shard_map/early_blocks/pallas_call | solution.py:306
  67.4 0.0 copy-start.17
  67.4 0.4 collective-permute-start.4
  67.9 0.0 collective-permute-done.5.refs_0_.refs_2_.refs_6_
  67.9 0.0 collective-permute-done.6.refs_1_.refs_3_.refs_7_
  67.9 0.0 all-to-all-done.1.got_ref.stats_ref
  67.9 0.6 aux_backward.1
  68.6 0.6 copy-done.14
  69.2 0.1 collective-permute-start.7
  69.3 0.4 collective-permute-done.4.got_ref
  69.8 0.6 collective-permute-done.7.refs_1_
  70.4 2.0 %add_cores.2.refs_11_ = bf16[4,640,128]{2,1,0:T(8,128)(2,1)} custom-call(s32[9]{0:T(128)S(1)} %copy-done.17, bf16[4,512,128]{2,1,0:T(8,128)(2,1)S(1)} %copy-done.12, bf16[4,512,128]{2,1,0:T(8,128)(2,1)} %collective-permute-done.4.got_ref, bf16[64,128]{1,0:T(8,128)(2,1)S(1)} %get-tuple-element.38.refs_0_, bf16[64,128]{1,0:T(8,128)(2,1)S(1)} %collective-permute-done.7.refs_1_), custom_call_target="tpu_custom_call" | custom-call | tf_op jit(solution)/shard_map/add_cores/pallas_call | solution.py:631
  72.4 4.8 %all-to-all-start.2 = ((bf16[4,640,128]{2,1,0:T(8,128)(2,1)}), bf16[4,640,128]{2,1,0:T(8,128)(2,1)S(1)}, u32[]{:S(2)}, u32[]{:S(2)}) async-start(bf16[4,640,128]{2,1,0:T(8,128)(2,1)} %add_cores.2.refs_11_), calls=%async_computation.2 | async-start | bytes 1310720 | tf_op jit(solution)/shard_map/all_to_all | solution.py:51
  77.2 18.9 %last_blocks.1 = (bf16[3136,256]{1,0:T(8,128)(2,1)}, bf16[4,512,128]{2,1,0:T(8,128)(2,1)}, bf16[4,512,128]{2,1,0:T(8,128)(2,1)}) custom-call(s32[9]{0:T(128)} %copy-done.16, bf16[3136,1024]{1,0:T(8,128)(2,1)} %get-tuple-element.29.feature_ref, bf16[3136,256]{1,0:T(8,128)(2,1)} %get-tuple-element.39.hidden_ref, bf16[1024,768]{1,0:T(8,128)(2,1)} %bitcast.33, ...), custom_call_target="tpu_custom_call" | custom-call | tf_op jit(solution)/shard_map/last_blocks/pallas_call | solution.py:386
  96.2 0.0 all-to-all-done.2._.early_ref.grads_ref
  96.2 0.8 copy-done
  97.0 6.7 %first_grad.1 = (bf16[4,768,128]{2,1,0:T(8,128)(2,1)}, bf16[4,768,128]{2,1,0:T(8,128)(2,1)}) custom-call(s32[9]{0:T(128)} %copy-done.16, bf16[3136,256]{1,0:T(8,128)(2,1)} %get-tuple-element.42.grads_ref, bf16[196,16,1024]{2,1,0:T(8,128)(2,1)} %bitcast.28, bf16[4,512,128]{2,1,0:T(8,128)(2,1)} %get-tuple-element.43.kept_ref, ...), custom_call_target="tpu_custom_call" | custom-call | tf_op jit(solution)/shard_map/first_grad/pallas_call | solution.py:453
  103.7 0.1 collective-permute-start.8
  103.9 2.4 %collective-permute-done.8.got_ref = bf16[4,768,128]{2,1,0:T(8,128)(2,1)S(1)} collective-permute-done((bf16[4,768,128]{2,1,0:T(8,128)(2,1)}, bf16[4,768,128]{2,1,0:T(8,128)(2,1)S(1)}, u32[]{:S(2)}, u32[]{:S(2)}) %collective-permute-start.8) | collective-permute-done | bytes 786464 | tf_op jit(solution)/shard_map/ppermute | solution.py:47
  106.3 1.1 copy-done.8
  107.4 1.6 %add_cores.3 = bf16[4,768,128]{2,1,0:T(8,128)(2,1)} custom-call(s32[9]{0:T(128)S(1)} %copy-done.18, bf16[4,768,128]{2,1,0:T(8,128)(2,1)S(1)} %copy-done.8, bf16[4,768,128]{2,1,0:T(8,128)(2,1)S(1)} %collective-permute-done.8.got_ref), custom_call_target="tpu_custom_call" | custom-call | tf_op jit(solution)/shard_map/add_cores/pallas_call | solution.py:631
  109.1 5.1 %all-to-all-start.3 = ((bf16[4,768,128]{2,1,0:T(8,128)(2,1)}), bf16[4,768,128]{2,1,0:T(8,128)(2,1)S(1)}, u32[]{:S(2)}, u32[]{:S(2)}) async-start(bf16[4,768,128]{2,1,0:T(8,128)(2,1)} %add_cores.3), calls=%async_computation.3 | async-start | bytes 1572864 | tf_op jit(solution)/shard_map/all_to_all | solution.py:51
  114.1 3.2 %class_backward.1 = (f32[1408,512]{1,0:T(8,128)}, f32[128,512]{1,0:T(8,128)}) custom-call(s32[9]{0:T(128)S(1)} %copy-done.18, f32[128,1408]{1,0:T(8,128)S(1)} %copy-done.10, bf16[8,16,768]{2,1,0:T(8,128)(2,1)S(1)} %all-to-all-done.got_ref, bf16[8,16,1152]{2,1,0:T(8,128)(2,1)S(1)} %all-to-all-done.1.got_ref.stats_ref, bf16[4,640,128]{2,1,0:T(8,128)(2,1)S(1)} %copy-done.1), custom_call_target="tpu_custom_call" | custom-call | flops 184549376 | bytes 2883584 | tf_op jit(solution)/shard_map/class_backward/pallas_call | solution.py:594
  117.4 17.2 %all-to-all-done.3.last_ref = bf16[4,768,128]{2,1,0:T(8,128)(2,1)S(1)} async-done(((bf16[4,768,128]{2,1,0:T(8,128)(2,1)}), bf16[4,768,128]{2,1,0:T(8,128)(2,1)S(1)}, u32[]{:S(2)}, u32[]{:S(2)}) %all-to-all-start.3) | async-done | bytes 786464 | tf_op jit(solution)/shard_map/all_to_all | solution.py:51
  134.6 1.5 %finish.1 = (f32[128,256]{1,0:T(8,128)}, f32[32,1024]{1,0:T(8,128)}, f32[128,768]{1,0:T(8,128)}) custom-call(s32[9]{0:T(128)S(1)} %copy-done.18, bf16[4,640,128]{2,1,0:T(8,128)(2,1)S(1)} %copy-done.1, bf16[4,768,128]{2,1,0:T(8,128)(2,1)S(1)} %all-to-all-done.3.last_ref), custom_call_target="tpu_custom_call" | custom-call | tf_op jit(solution)/shard_map/finish/pallas_call | solution.py:662
  (33 shorter events, 0.1 us)
Async XLA Ops:
  0.7 39.7 %copy-start.16 = (s32[9]{0:T(128)}, s32[9]{0:T(128)S(1)}, u32[]{:S(2)}) copy-start(s32[9]{0:T(128)S(1)} %stack.39.where_ref) | copy-start | bytes 112
  0.7 1.4 %copy-start.6 = (bf16[16,196,192]{1,2,0:T(8,128)(2,1)S(1)}, bf16[16,196,192]{1,2,0:T(8,128)(2,1)}, u32[]{:S(2)}) copy-start(bf16[16,196,192]{1,2,0:T(8,128)(2,1)} %param.9) | copy-start | bytes 3612676
  5.4 16.9 %copy-start.20 = (bf16[147,16,128]{2,1,0:T(8,128)(2,1)}, bf16[147,16,128]{2,1,0:T(8,128)(2,1)S(1)}, u32[]{:S(2)}) copy-start(bf16[147,16,128]{2,1,0:T(8,128)(2,1)S(1)} %get-tuple-element.30.refs_4_.refs_10_) | copy-start | bytes 1806340
  5.4 17.4 %collective-permute-start.2 = (bf16[147,16,128]{2,1,0:T(8,128)(2,1)S(1)}, bf16[147,16,128]{2,1,0:T(8,128)(2,1)S(1)}, u32[]{:S(2)}, u32[]{:S(2)}) collective-permute-start(bf16[147,16,128]{2,1,0:T(8,128)(2,1)S(1)} %get-tuple-element.30.refs_4_.refs_10_), channel_id=1, source_target_pairs={{0,16},{8,24},{16,0},{24,8},{1,17},{9,25},{17,1},{25,9},{2,18},{10... | collective-permute-start | bytes 1806344 | tf_op jit(solution)/shard_map/ppermute | solution.py:47
  8.3 16.5 %collective-permute-start = (bf16[147,16,128]{2,1,0:T(8,128)(2,1)S(1)}, bf16[147,16,128]{2,1,0:T(8,128)(2,1)S(1)}, u32[]{:S(2)}, u32[]{:S(2)}) collective-permute-start(bf16[147,16,128]{2,1,0:T(8,128)(2,1)S(1)} %get-tuple-element.30.refs_4_.refs_10_), channel_id=1, source_target_pairs={{0,8},{8,0},{16,24},{24,16},{1,9},{9,1},{17,25},{25,17},{2,10},{10... | collective-permute-start | bytes 1806344 | tf_op jit(solution)/shard_map/ppermute | solution.py:47
  9.8 27.6 %collective-permute-start.1 = (bf16[147,16,128]{2,1,0:T(8,128)(2,1)}, bf16[147,16,128]{2,1,0:T(8,128)(2,1)}, u32[]{:S(2)}, u32[]{:S(2)}) collective-permute-start(bf16[147,16,128]{2,1,0:T(8,128)(2,1)} %get-tuple-element.31.refs_5_.refs_11_), channel_id=1, source_target_pairs={{0,8},{8,0},{16,24},{24,16},{1,9},{9,1},{17,25},{25,17},{2,10},{10... | collective-permute-start | bytes 1806344 | tf_op jit(solution)/shard_map/ppermute | solution.py:47
  10.4 38.4 %collective-permute-start.3 = (bf16[147,16,128]{2,1,0:T(8,128)(2,1)}, bf16[147,16,128]{2,1,0:T(8,128)(2,1)}, u32[]{:S(2)}, u32[]{:S(2)}) collective-permute-start(bf16[147,16,128]{2,1,0:T(8,128)(2,1)} %get-tuple-element.31.refs_5_.refs_11_), channel_id=1, source_target_pairs={{0,16},{8,24},{16,0},{24,8},{1,17},{9,25},{17,1},{25,9},{2,18},{10... | collective-permute-start | bytes 1806344 | tf_op jit(solution)/shard_map/ppermute | solution.py:47
  10.4 14.5 %copy-start.4 = (bf16[1,1024,512]{2,1,0:T(8,128)(2,1)S(1)}, bf16[1,1024,512]{2,1,0:T(8,128)(2,1)}, u32[]{:S(2)}) copy-start(bf16[1,1024,512]{2,1,0:T(8,128)(2,1)} %param.14) | copy-start | bytes 3145732
  10.4 14.5 %copy-start.19 = (s32[16]{0:T(128)S(1)}, s32[16]{0:T(128)}, u32[]{:S(2)}) copy-start(s32[16]{0:T(128)} %labels_ref.1) | copy-start | bytes 196
  22.7 21.0 %copy-start.5 = (bf16[147,16,128]{2,1,0:T(8,128)(2,1)}, bf16[147,16,128]{2,1,0:T(8,128)(2,1)S(1)}, u32[]{:S(2)}) copy-start(bf16[147,16,128]{2,1,0:T(8,128)(2,1)S(1)} %collective-permute-done.2.refs_1_.refs_8_.refs_4_) | copy-start | bytes 1806340
  24.8 2.4 %copy-start.11 = (bf16[147,16,128]{2,1,0:T(8,128)(2,1)}, bf16[147,16,128]{2,1,0:T(8,128)(2,1)S(1)}, u32[]{:S(2)}) copy-start(bf16[147,16,128]{2,1,0:T(8,128)(2,1)S(1)} %collective-permute-done.refs_0_.refs_6_.refs_12_) | copy-start | bytes 1806340
  24.9 0.9 copy-start.15
  27.2 13.2 %all-to-all-start = ((bf16[8,16,768]{2,1,0:T(8,128)(2,1)}), bf16[8,16,768]{2,1,0:T(8,128)(2,1)S(1)}, u32[]{:S(2)}, u32[]{:S(2)}) async-start(bf16[8,16,768]{2,1,0:T(8,128)(2,1)} %get-tuple-element.33), calls=%async_computation | async-start | bytes 393216 | tf_op jit(solution)/shard_map/all_to_all | solution.py:51
  32.1 35.8 %collective-permute-start.5 = (bf16[147,16,128]{2,1,0:T(8,128)(2,1)S(1)}, bf16[147,16,128]{2,1,0:T(8,128)(2,1)S(1)}, u32[]{:S(2)}, u32[]{:S(2)}) collective-permute-start(bf16[147,16,128]{2,1,0:T(8,128)(2,1)S(1)} %collective-permute-done.2.refs_1_.refs_8_.refs_4_), channel_id=1, source_target_pairs={{0,8},{8,0},{16,24},{24,16},{1,9},{9,1},{17,25},{25,17},{2,10},{10... | collective-permute-start | bytes 1806344 | tf_op jit(solution)/shard_map/ppermute | solution.py:47
  37.4 30.5 %collective-permute-start.6 = (bf16[147,16,128]{2,1,0:T(8,128)(2,1)}, bf16[147,16,128]{2,1,0:T(8,128)(2,1)S(1)}, u32[]{:S(2)}, u32[]{:S(2)}) collective-permute-start(bf16[147,16,128]{2,1,0:T(8,128)(2,1)} %collective-permute-done.1.refs_7_.refs_13_), channel_id=1, source_target_pairs={{0,16},{8,24},{16,0},{24,8},{1,17},{9,25},{17,1},{25,9},{2,18},{10... | collective-permute-start | bytes 1806344 | tf_op jit(solution)/shard_map/ppermute | solution.py:47
  40.4 1.4 %copy-start.7 = (bf16[1,1408,512]{2,1,0:T(8,128)(2,1)S(1)}, bf16[1,1408,512]{2,1,0:T(8,128)(2,1)}, u32[]{:S(2)}) copy-start(bf16[1,1408,512]{2,1,0:T(8,128)(2,1)} %param.15) | copy-start | bytes 4325380
  43.8 0.9 copy-start.9
  44.7 0.7 copy-start.13
  45.4 22.5 %all-to-all-start.1 = ((bf16[8,16,1152]{2,1,0:T(8,128)(2,1)}), bf16[8,16,1152]{2,1,0:T(8,128)(2,1)S(1)}, u32[]{:S(2)}, u32[]{:S(2)}) async-start(bf16[8,16,1152]{2,1,0:T(8,128)(2,1)} %copy-done.13), calls=%async_computation.1 | async-start | bytes 589824 | tf_op jit(solution)/shard_map/all_to_all | solution.py:51
  67.4 3.0 %copy-start.17 = (s32[9]{0:T(128)S(1)}, s32[9]{0:T(128)}, u32[]{:S(2)}) copy-start(s32[9]{0:T(128)} %copy-done.16) | copy-start | bytes 112
  67.4 2.3 %collective-permute-start.4 = (bf16[4,512,128]{2,1,0:T(8,128)(2,1)}, bf16[4,512,128]{2,1,0:T(8,128)(2,1)}, u32[]{:S(2)}, u32[]{:S(2)}) collective-permute-start(bf16[4,512,128]{2,1,0:T(8,128)(2,1)} %get-tuple-element.36), channel_id=1, source_target_pairs={{0,1},{1,0},{2,3},{3,2},{4,5},{5,4},{6,7},{7,6},{8,9},{9,8},{10,11... | collective-permute-start | bytes 1572872 | tf_op jit(solution)/shard_map/ppermute | solution.py:47
  67.9 4.5 %copy-start.2 = (bf16[147,16,128]{2,1,0:T(8,128)(2,1)}, bf16[147,16,128]{2,1,0:T(8,128)(2,1)S(1)}, u32[]{:S(2)}) copy-start(bf16[147,16,128]{2,1,0:T(8,128)(2,1)S(1)} %collective-permute-done.5.refs_0_.refs_2_.refs_6_) | copy-start | bytes 1806340
  67.9 2.5 %copy-start.12 = (bf16[4,512,128]{2,1,0:T(8,128)(2,1)S(1)}, bf16[4,512,128]{2,1,0:T(8,128)(2,1)}, u32[]{:S(2)}) copy-start(bf16[4,512,128]{2,1,0:T(8,128)(2,1)} %get-tuple-element.35.keep_ref) | copy-start | bytes 1572868
  67.9 4.5 %copy-start.3 = (bf16[147,16,128]{2,1,0:T(8,128)(2,1)}, bf16[147,16,128]{2,1,0:T(8,128)(2,1)S(1)}, u32[]{:S(2)}) copy-start(bf16[147,16,128]{2,1,0:T(8,128)(2,1)S(1)} %collective-permute-done.6.refs_1_.refs_3_.refs_7_) | copy-start | bytes 1806340
  68.6 0.6 copy-start.14
  69.2 1.2 collective-permute-start.7
  72.4 23.7 %all-to-all-start.2 = ((bf16[4,640,128]{2,1,0:T(8,128)(2,1)}), bf16[4,640,128]{2,1,0:T(8,128)(2,1)S(1)}, u32[]{:S(2)}, u32[]{:S(2)}) async-start(bf16[4,640,128]{2,1,0:T(8,128)(2,1)} %add_cores.2.refs_11_), calls=%async_computation.2 | async-start | bytes 1310720 | tf_op jit(solution)/shard_map/all_to_all | solution.py:51
  96.2 0.8 copy-start
  97.0 9.3 %copy-start.18 = (s32[9]{0:T(128)S(1)}, s32[9]{0:T(128)}, u32[]{:S(2)}) copy-start(s32[9]{0:T(128)} %copy-done.16) | copy-start | bytes 112
  103.7 2.6 %collective-permute-start.8 = (bf16[4,768,128]{2,1,0:T(8,128)(2,1)}, bf16[4,768,128]{2,1,0:T(8,128)(2,1)S(1)}, u32[]{:S(2)}, u32[]{:S(2)}) collective-permute-start(bf16[4,768,128]{2,1,0:T(8,128)(2,1)} %get-tuple-element.46), channel_id=1, source_target_pairs={{0,1},{1,0},{2,3},{3,2},{4,5},{5,4},{6,7},{7,6},{8,9},{9,8},{10,11... | collective-permute-start | bytes 2359304 | tf_op jit(solution)/shard_map/ppermute | solution.py:47
  106.3 1.1 copy-start.8
  107.4 6.7 %copy-start.1 = (bf16[4,640,128]{2,1,0:T(8,128)(2,1)S(1)}, bf16[4,640,128]{2,1,0:T(8,128)(2,1)}, u32[]{:S(2)}) copy-start(bf16[4,640,128]{2,1,0:T(8,128)(2,1)} %copy-done) | copy-start | bytes 1966084
  107.4 6.7 %copy-start.10 = (f32[128,1408]{1,0:T(8,128)S(1)}, f32[128,1408]{1,0:T(8,128)}, u32[]{:S(2)}) copy-start(f32[128,1408]{1,0:T(8,128)} %copy-done.9) | copy-start | bytes 2162692
  109.1 25.5 %all-to-all-start.3 = ((bf16[4,768,128]{2,1,0:T(8,128)(2,1)}), bf16[4,768,128]{2,1,0:T(8,128)(2,1)S(1)}, u32[]{:S(2)}, u32[]{:S(2)}) async-start(bf16[4,768,128]{2,1,0:T(8,128)(2,1)} %add_cores.3), calls=%async_computation.3 | async-start | bytes 1572864 | tf_op jit(solution)/shard_map/all_to_all | solution.py:51

commit v5 on v4

v5 whole, which is shorter than its diff:
```python
import functools

import jax
import jax.numpy as jnp
from jax import lax
from jax.experimental import pallas as pl
from jax.experimental.pallas import tpu as pltpu
from jax.sharding import PartitionSpec as P

F32 = jnp.float32
BF16 = jnp.bfloat16
STEPS = 4
LANES = 128
TILE = 256
MIB = 1024 * 1024
TOKEN = (8, LANES)
ROWS_0 = (((0,), (0,)), ((), ()))
COLS_1 = (((1,), (1,)), ((), ()))
PARITY, CORE, ME, TILES = 0, 1, 2, 3


def dot(left, right, dims=(((1,), (0,)), ((), ()))):
    return lax.dot_general(left, right, dims, preferred_element_type=F32)


def call(kernel, out_shape, *, limit, flops=0, moved=0, **kwargs):
    return pl.pallas_call(
        kernel,
        out_shape=out_shape,
        compiler_params=pltpu.CompilerParams(vmem_limit_bytes=limit * MIB),
        cost_estimate=pl.CostEstimate(flops=int(flops), bytes_accessed=int(moved), transcendentals=0),
        **kwargs,
    )


def shape(dims, kind):
    return jax.ShapeDtypeStruct(dims, kind)


SMEM = pl.BlockSpec(memory_space=pltpu.SMEM)
VMEM = pl.BlockSpec(memory_space=pltpu.VMEM)
ANY = pl.BlockSpec(memory_space=pl.ANY)
HBM = pl.BlockSpec(memory_space=pltpu.HBM)


def swap(value, axis, bits):
    count = lax.axis_size(axis)
    return lax.ppermute(value, axis, [(i, i ^ bits) for i in range(count)])


def exchange(value, groups=None):
    return lax.all_to_all(value, "dp", 0, 0, axis_index_groups=groups, tiled=True)


def pack_kernel(first, where_ref, patches_ref, out_ref, token_ref, turned, own, shared):
    images, span, pix = patches_ref.shape
    padded = turned.shape[1]
    count = out_ref.shape[0] // 3 * 2
    parity = where_ref[PARITY]
    at_own = pl.multiple_of(64 * parity, 64)
    at_shared = pl.multiple_of(128 * (1 - parity), 64)
    row = lax.broadcasted_iota(jnp.int32, (padded, pix), 0)
    column = lax.broadcasted_iota(jnp.int32, (padded, pix), 1)
    pick = ((row < count) & (column == row + first)).astype(F32).astype(BF16)
    for i in range(images):
        turned[i, :, :LANES] = dot(pick, patches_ref[i, pl.ds(at_own, LANES), :], COLS_1).astype(BF16)
        turned[i, :, LANES:] = dot(pick, patches_ref[i, pl.ds(at_shared, 64), :], COLS_1).astype(BF16)
    size = 16 * images
    row = lax.broadcasted_iota(jnp.int32, (size, size), 0)
    column = lax.broadcasted_iota(jnp.int32, (size, size), 1)
    order = (row // images == column % 16) & (row % images == column // 16)
    order = order.astype(F32).astype(BF16)
    for b in range(padded // 16):
        rows = turned[:, 16 * b : 16 * b + 16, :].reshape(size, span)
        out = dot(order, rows).astype(BF16)
        own[16 * b : 16 * b + 16] = out[:, :LANES].reshape(16, images, LANES)
        shared[16 * b : 16 * b + 16] = out[:, LANES:].reshape(16, images, 64)
    out_ref[:count] = own[:count]
    out_ref[count:] = jnp.concatenate([shared[: count // 2], shared[count // 2 : count]], axis=2)
    token_ref[...] = jnp.zeros(token_ref.shape, F32)


def pack(where, patches, h):
    images, span, pix = patches.shape
    half = pix // 2
    padded = -(-half // 16) * 16
    return call(
        functools.partial(pack_kernel, h * half),
        [shape((half + half // 2, images, LANES), BF16), shape(TOKEN, F32)],
        limit=20,
        in_specs=[SMEM, VMEM],
        scratch_shapes=[
            pltpu.VMEM((images, padded, span), BF16),
            pltpu.VMEM((padded, images, LANES), BF16),
            pltpu.VMEM((padded, images, 64), BF16),
        ],
        name="pack_patches",
    )(where, patches)


def after(value, other):
    return lax.optimization_barrier((value, other))[0]


def forward_kernel(acts_ref, first_ref, second_ref, *refs):
    hidden_ref, feature_ref, pooled_ref = refs[-3:]
    step = pl.program_id(0)
    block, images, width = acts_ref.shape
    flat = acts_ref[...].reshape(block * images, width)
    hidden = jnp.maximum(dot(flat, first_ref[...]), 0.0).astype(BF16)
    hidden_ref[...] = hidden

    @pl.when(step == 0)
    def _():
        pooled_ref[...] = jnp.zeros(pooled_ref.shape, F32)

    for at in range(0, width, TILE):
        cut = slice(at, at + TILE)
        feature = (flat[:, cut].astype(F32) + dot(hidden, second_ref[:, cut])).astype(BF16)
        feature_ref[:, cut] = feature
        pooled_ref[:, cut] += jnp.sum(feature.reshape(block, images, TILE).astype(F32), axis=0)


def forward(acts, first, second, before):
    pix, images, width = acts.shape
    inner = first.shape[1]
    block = pix // STEPS
    whole = lambda g: (0, 0)
    rows = lambda n: pl.BlockSpec((block * images, n), lambda g: (g, 0))
    return call(
        forward_kernel,
        [
            shape((pix * images, inner), BF16),
            shape((pix * images, width), BF16),
            shape((images, width), F32),
        ],
        limit=58,
        flops=4 * pix * images * width * inner,
        moved=2 * pix * images * (2 * width + inner),
        grid=(STEPS,),
        in_specs=[
            pl.BlockSpec((block, images, width), lambda g: (g, 0, 0)),
            pl.BlockSpec(first.shape, whole),
            pl.BlockSpec(second.shape, whole),
            *[ANY] * len(before),
        ],
        out_specs=[rows(inner), rows(width), pl.BlockSpec((images, width), whole)],
        name="forward",
    )(acts, first, second, *before)


def head_kernel(pix, pooled_ref, aux_ref, labels_ref, *refs):
    aux_pre_ref, sent_ref = refs[-2:]
    groups, images, _ = sent_ref.shape
    width, head = aux_ref.shape
    part = width // groups
    mean = (pooled_ref[...] / pix).astype(BF16)
    aux_pre = dot(mean, aux_ref[...])
    aux_pre_ref[...] = aux_pre
    out = jnp.maximum(aux_pre, 0.0).astype(BF16)
    row = lax.broadcasted_iota(jnp.int32, (images, LANES), 0)
    lane = lax.broadcasted_iota(jnp.int32, (images, LANES), 1)
    digits = jnp.zeros((images, LANES), jnp.int32)
    for i in range(images):
        label = labels_ref[i]
        digits = jnp.where((row == i) & (lane == 0), label // LANES, digits)
        digits = jnp.where((row == i) & (lane == 1), label % LANES, digits)
    digits = digits.astype(F32).astype(BF16)
    for d in range(groups):
        sent_ref[d, :, :head] = out
        sent_ref[d, :, head : head + part] = mean[:, d * part : (d + 1) * part]
        sent_ref[d, :, head + LANES :] = digits


def aux_head(pooled, aux, labels, pix, groups, before):
    images, head = pooled.shape[0], aux.shape[1]
    return call(
        functools.partial(head_kernel, pix),
        [shape((images, head), F32), shape((groups, images, head + 2 * LANES), BF16)],
        limit=16,
        in_specs=[VMEM, VMEM, SMEM, *[ANY] * len(before)],
        name="aux_head",
    )(pooled, aux, labels, *before)


def recon_kernel(feature_ref, decode_ref, _, recon_ref, token_ref):
    token_ref[...] = jnp.zeros(token_ref.shape, F32)
    feature = feature_ref[...]
    for at in range(0, recon_ref.shape[1], TILE):
        cut = slice(at, at + TILE)
        recon_ref[:, cut] = dot(feature, decode_ref[:, cut])


def reconstruct(feature, decode, before):
    rows, width = feature.shape
    n = decode.shape[1]
    block = lambda m: pl.BlockSpec((rows // STEPS, m), lambda g: (g, 0))
    return call(
        recon_kernel,
        [shape((rows, n), F32), shape(TOKEN, F32)],
        limit=58,
        flops=2 * rows * width * n,
        moved=rows * (2 * width + 4 * n),
        grid=(STEPS,),
        in_specs=[block(width), pl.BlockSpec(decode.shape, lambda g: (0, 0)), ANY],
        out_specs=[block(n), pl.BlockSpec(TOKEN, lambda g: (0, 0))],
        name="reconstruct",
    )(feature, decode, before)


def own_index(h):
    per_half = STEPS // 2
    return lambda g, where: (jnp.clip(g - h * per_half, 0, per_half - 1), 0, 0)


def patch_operands(blocks, own_blocks, shared_blocks):
    args, specs = [], []
    for k in own_blocks:
        for h, half in enumerate(blocks[k]):
            dims = (half.shape[0] // 3,) + half.shape[1:]
            args.append(half)
            specs.append(pl.BlockSpec(dims, own_index(h)))
    for k in shared_blocks:
        for half in blocks[k]:
            dims = (half.shape[0] // 3,) + half.shape[1:]
            args.append(half)
            specs.append(pl.BlockSpec(dims, lambda g, where: (2, 0, 0)))
    return args, specs


def lay_target(step, where_ref, refs, target):
    if len(refs) == 1:
        target[...] = refs[0][...]
        return
    pairs = [refs[j : j + 2] for j in range(0, len(refs), 2)]
    own, shared = pairs[: len(pairs) // 2], pairs[len(pairs) // 2 :]
    per_half = STEPS // 2
    even_first = where_ref[PARITY] == 0
    lanes = lambda j: pl.ds(pl.multiple_of(where_ref[TILES + j] * LANES, LANES), LANES)
    for h in range(2):

        @pl.when(step // per_half == h)
        def _():
            for k, pair in enumerate(own):
                target[:, :, lanes(2 * k)] = pair[h][...]

    turn = lambda v: jnp.concatenate([v[:, :, 64:], v[:, :, :64]], axis=2)
    for g in range(STEPS):

        @pl.when(step == g)
        def _():
            h, side = g // per_half, g % per_half
            for k in range(0, len(shared), 2):
                mine, other = shared[k][h][...].astype(F32), shared[k + 1][h][...].astype(F32)
                even = jnp.where(even_first, mine, other)
                odd = jnp.where(even_first, other, mine)
                lane = lax.broadcasted_iota(jnp.int32, even.shape, 2)
                low = turn(even) if side else even
                high = odd if side else turn(odd)
                target[:, :, lanes(2 * k + 1)] = jnp.where(lane < 64, low, high).astype(BF16)


def deal(where_ref, sums, part, keep_ref, send_ref):
    core = where_ref[CORE]
    at = 0
    for value in sums:
        height = value.shape[0]
        for z in range(keep_ref.shape[0]):
            even = value[:, 2 * z * part : (2 * z + 1) * part]
            odd = value[:, (2 * z + 1) * part : (2 * z + 2) * part]
            mine = jnp.where(core == 0, even, odd)
            other = jnp.where(core == 0, odd, even)
            keep_ref[z, at : at + height, :] = mine.astype(BF16)
            send_ref[z, at : at + height, :] = other.astype(BF16)
        at += height


def fetch(source, held, sems, step):
    size = held.shape[0] // STEPS
    copies = [
        pltpu.make_async_copy(source.at[pl.ds(g * size, size)], held.at[pl.ds(g * size, size)], sems.at[g])
        for g in range(STEPS)
    ]

    @pl.when(step == 0)
    def _():
        for copy in copies:
            copy.start()

    for g in range(STEPS):

        @pl.when(step == g)
        def _():
            copies[g].wait()


def fetch(source, held, sems, step):
    size = held.shape[0] // STEPS
    copies = [
        pltpu.make_async_copy(source.at[pl.ds(g * size, size)], held.at[pl.ds(g * size, size)], sems.at[g])
        for g in range(STEPS)
    ]

    @pl.when(step == 0)
    def _():
        for copy in copies:
            copy.start()

    for g in range(STEPS):

        @pl.when(step == g)
        def _():
            copies[g].wait()


def contract(step, rows, pairs):
    unit = rows // STEPS // TILE * TILE
    for g in range(STEPS):

        @pl.when(step == g)
        def _():
            span = slice(g * unit, rows if g == STEPS - 1 else (g + 1) * unit)
            for total, left, right in pairs:
                now = dot(left[span], right[span], ROWS_0)
                total[...] = now if g == 0 else total[...] + now


def residual_kernel(groups, scale, n_patch, where_ref, feature_ref, recon_ref, *refs):
    patch_refs, refs = refs[:n_patch], refs[n_patch:]
    _, grad_ref, keep_ref, send_ref, target, feature, grads, total, sems = refs
    step = pl.program_id(0)
    rows, width = feature.shape
    size = grad_ref.shape[0]
    fetch(feature_ref, feature, sems, step)
    lay_target(step, where_ref, patch_refs, target)
    grad = ((recon_ref[...] - target[...].reshape(recon_ref.shape).astype(F32)) * scale).astype(BF16)
    grad_ref[...] = grad
    grads[pl.ds(pl.multiple_of(step * size, size), size)] = grad
    contract(step, rows, [(total, grads, feature)])

    @pl.when(step == STEPS - 1)
    def _():
        deal(where_ref, [total], width // groups, keep_ref, send_ref)


def residual(where, feature, recon, patch_args, patch_specs, before, images, scale, groups):
    rows, width = feature.shape
    n = recon.shape[1]
    size = rows // STEPS
    parts = (groups // 2, n, width // groups)
    dealt = pl.BlockSpec(parts, lambda g, where: (0, 0, 0))
    block = pl.BlockSpec((size, n), lambda g, where: (g, 0))
    return call(
        functools.partial(residual_kernel, groups, scale, len(patch_args)),
        [shape((rows, n), BF16), shape(parts, BF16), shape(parts, BF16)],
        limit=58,
        flops=2 * rows * width * n,
        moved=rows * (2 * width + 6 * n),
        grid_spec=pltpu.PrefetchScalarGridSpec(
            num_scalar_prefetch=1,
            grid=(STEPS,),
            in_specs=[HBM, block, *patch_specs, ANY],
            out_specs=[block, dealt, dealt],
            scratch_shapes=[
                pltpu.VMEM((size // images, images, n), BF16),
                pltpu.VMEM((rows, width), BF16),
                pltpu.VMEM((rows, n), BF16),
                pltpu.VMEM((n, width), F32),
                pltpu.SemaphoreType.DMA((STEPS,)),
            ],
        ),
        name="residual",
    )(where, feature, recon, *patch_args, before)


def backward_kernel(
    groups, where_ref, grad_ref, hidden_ref, acts_ref, decode_ref, pooled_ref, second_ref, _,
    keep_ref, send_ref, hidden, acts, feature_grads, hidden_grads, total_second, total_first, sems,
):
    step = pl.program_id(0)
    rows, width = feature_grads.shape
    size = grad_ref.shape[0]
    images = pooled_ref.shape[0]
    fetch(hidden_ref, hidden, sems.at[0], step)
    fetch(acts_ref, acts, sems.at[1], step)
    here = pl.ds(pl.multiple_of(step * size, size), size)
    grad = grad_ref[...]
    for at in range(0, width, TILE):
        cut = slice(at, at + TILE)
        back = dot(grad, decode_ref[cut, :], COLS_1).reshape(size // images, images, TILE)
        feature_grads[here, cut] = (back + pooled_ref[:, cut][None]).astype(BF16).reshape(size, TILE)
    hidden_back = dot(feature_grads[here], second_ref[...], COLS_1)
    hidden_grads[here] = jnp.where(hidden[here].astype(F32) > 0, hidden_back, 0.0).astype(BF16)
    contract(step, rows, [(total_second, hidden, feature_grads), (total_first, hidden_grads, acts)])

    @pl.when(step == STEPS - 1)
    def _():
        part = width // groups
        tall = total_second.shape[0] // groups
        second = jnp.concatenate(
            [
                jnp.concatenate(
                    [total_second[d * tall : (d + 1) * tall, q * part : (q + 1) * part] for q in range(groups)], axis=0
                )
                for d in range(groups)
            ],
            axis=1,
        )
        deal(where_ref, [second, total_first], part, keep_ref, send_ref)


def backward(where, grad, hidden, acts, decode, pooled, second, before, groups):
    rows, width = acts.shape
    inner, n = hidden.shape[1], grad.shape[1]
    size = rows // STEPS
    parts = (groups // 2, 2 * inner, width // groups)
    dealt = pl.BlockSpec(parts, lambda g, where: (0, 0, 0))
    whole = lambda array: pl.BlockSpec(array.shape, lambda g, where: (0, 0))
    return call(
        functools.partial(backward_kernel, groups),
        [shape(parts, BF16), shape(parts, BF16)],
        limit=58,
        flops=2 * rows * width * (n + 3 * inner),
        moved=2 * rows * (width + n + inner),
        grid_spec=pltpu.PrefetchScalarGridSpec(
            num_scalar_prefetch=1,
            grid=(STEPS,),
            in_specs=[
                pl.BlockSpec((size, n), lambda g, where: (g, 0)),
                HBM,
                HBM,
                whole(decode),
                whole(pooled),
                whole(second),
                ANY,
            ],
            out_specs=[dealt, dealt],
            scratch_shapes=[
                pltpu.VMEM((rows, inner), BF16),
                pltpu.VMEM((rows, width), BF16),
                pltpu.VMEM((rows, width), BF16),
                pltpu.VMEM((rows, inner), BF16),
                pltpu.VMEM((inner, width), F32),
                pltpu.VMEM((inner, width), F32),
                pltpu.SemaphoreType.DMA((2, STEPS)),
            ],
        ),
        name="backward",
    )(where, grad, hidden, acts, decode, pooled, second, before)


TOPS, DENOMS = 3, 19
DIGIT = 40


def to_digits(value):
    rest, lanes = value, []
    for _ in range(3):
        digit = rest.astype(BF16).astype(F32)
        lanes.append(digit[:, :DIGIT])
        rest = rest - digit
    lanes.append(jnp.zeros((value.shape[0], LANES - 3 * DIGIT), F32))
    return jnp.concatenate(lanes, axis=1).astype(BF16)


def from_digits(value):
    value = value.astype(F32)
    return sum(value[:, j * DIGIT : (j + 1) * DIGIT] for j in (2, 1, 0))


def labels_of(got, head):
    digits = got[:, head + LANES : head + LANES + 2].astype(F32)
    return (digits[:, 0:1] * LANES + digits[:, 1:2]).astype(jnp.int32)


def logits_kernel(where_ref, got_ref, klass_ref, _, logits_ref, sent_ref):
    groups, images, _ = got_ref.shape
    classes, head = klass_ref.shape
    got = got_ref[...].reshape(groups * images, -1)
    logits = dot(got[:, :head], klass_ref[...], COLS_1)
    logits_ref[...] = logits
    ids = lax.broadcasted_iota(jnp.int32, logits.shape, 1) + where_ref[ME] * classes
    hit = labels_of(got, head) == ids
    top = jnp.max(logits, axis=1, keepdims=True)
    expo = jnp.exp(logits - top)
    denom = jnp.sum(expo, axis=1, keepdims=True)
    own = jnp.sum(jnp.where(hit, expo, 0.0), axis=1, keepdims=True)
    rest = jnp.where(hit, 0.0, expo).astype(BF16)
    onehot = jnp.where(hit, 1.0, 0.0).astype(BF16)
    sent_ref[:, :, :head] = dot(rest, klass_ref[...]).astype(BF16).reshape(groups, images, head)
    sent_ref[:, :, head : 2 * head] = dot(onehot, klass_ref[...]).astype(BF16).reshape(groups, images, head)
    lane = lax.broadcasted_iota(jnp.int32, (images, LANES), 1)
    cut = lambda value, d: value[d * images : (d + 1) * images]
    common = jnp.zeros((images, LANES), F32)
    for d in range(groups):
        common = jnp.where(lane == TOPS + d, cut(top, d), common)
        common = jnp.where(lane == DENOMS + d, cut(denom, d), common)
    for d in range(groups):
        stats = jnp.where(lane == 1, cut(denom, d), jnp.where(lane == 2, cut(own, d), common))
        sent_ref[d, :, 2 * head :] = to_digits(jnp.where(lane == 0, cut(top, d), stats))


def class_logits(where, got, klass, before):
    groups, images, _ = got.shape
    classes, head = klass.shape
    return call(
        logits_kernel,
        [shape((groups * images, classes), F32), shape((groups, images, 2 * head + LANES), BF16)],
        limit=16,
        in_specs=[SMEM, VMEM, VMEM, ANY],
        name="class_logits",
    )(where, got, klass, before)


def aux_kernel(pix, norm, got_ref, aux_pre_ref, aux_ref, pooled_ref, grad_ref):
    groups = got_ref.shape[0]
    head = aux_pre_ref.shape[1]
    stats = [from_digits(got_ref[d, :, 2 * head :]) for d in range(groups)]
    top = functools.reduce(jnp.maximum, [s[:, 0:1] for s in stats])
    scales = [jnp.exp(s[:, 0:1] - top) for s in stats]
    denom = sum(s[:, 1:2] * f for s, f in zip(stats, scales))
    own = sum(s[:, 2:3] * f for s, f in zip(stats, scales)) / denom
    rest = sum(got_ref[d, :, :head].astype(F32) * scales[d] for d in range(groups)) / (denom * norm)
    row = sum(got_ref[d, :, head : 2 * head].astype(F32) for d in range(groups))
    back = rest + row * ((own - 1.0) / norm).astype(BF16).astype(F32)
    aux_grad = jnp.where(aux_pre_ref[...] > 0, back, 0.0).astype(BF16)
    pooled_ref[...] = dot(aux_grad, aux_ref[...], COLS_1) / pix
    images, part = aux_grad.shape[0], grad_ref.shape[1]
    for q in range(head // part):
        grad_ref[q * images : (q + 1) * images, :] = aux_grad[:, q * part : (q + 1) * part]


def aux_backward(got, aux_pre, aux, pix, norm):
    groups, images, _ = got.shape
    width, head = aux.shape
    part = width // groups
    return call(
        functools.partial(aux_kernel, pix, norm),
        [shape((images, width), F32), shape((images * head // part, part), BF16)],
        limit=16,
        name="aux_backward",
    )(got, aux_pre, aux)


def class_kernel(norm, n, where_ref, logits_ref, got_ref, stats_ref, grads_ref, class_ref, aux_ref):
    groups, images, _ = got_ref.shape
    head = class_ref.shape[1]
    classes, part = class_ref.shape[0], aux_ref.shape[0]
    got = got_ref[...].reshape(groups * images, -1)
    stats = [from_digits(stats_ref[e]) for e in range(groups)]
    tops, denoms = [], []
    for d in range(groups):
        top = functools.reduce(jnp.maximum, [s[:, TOPS + d : TOPS + d + 1] for s in stats])
        tops.append(top)
        denoms.append(sum(s[:, DENOMS + d : DENOMS + d + 1] * jnp.exp(s[:, TOPS + d : TOPS + d + 1] - top) for s in stats))
    top, denom = jnp.concatenate(tops, axis=0), jnp.concatenate(denoms, axis=0)
    logits = logits_ref[...]
    ids = lax.broadcasted_iota(jnp.int32, logits.shape, 1) + where_ref[ME] * classes
    onehot = jnp.where(labels_of(got, head) == ids, 1.0, 0.0)
    logit_grad = ((jnp.exp(logits - top) / denom - onehot) / norm).astype(BF16)
    class_ref[...] = dot(logit_grad, got[:, :head], ROWS_0)
    total = jnp.zeros(aux_ref.shape, F32)
    for d in range(groups):
        at = n + d % 2 * (head // part) * images
        grad = jnp.concatenate(
            [grads_ref[d // 2, at + q * images : at + (q + 1) * images, :] for q in range(head // part)], axis=1
        )
        pooled = got_ref[d, :, head : head + part]
        total += dot(pooled, grad, ROWS_0).astype(BF16).astype(F32)
    aux_ref[...] = total


def class_backward(where, logits, got, partial, grads, n_decode, classes, head, norm):
    groups, images, wide = partial.shape
    whole = lambda *dims: pl.BlockSpec(dims, lambda i: (0,) * len(dims))
    part = grads.shape[2]
    return call(
        functools.partial(class_kernel, norm, n_decode),
        [shape((classes, head), F32), shape((part, head), F32)],
        limit=20,
        flops=2 * groups * images * classes * head,
        moved=4 * classes * head,
        grid=(1,),
        in_specs=[
            SMEM,
            whole(*logits.shape),
            whole(*got.shape),
            pl.BlockSpec((groups, images, LANES), lambda i: (0, 0, wide // LANES - 1)),
            whole(*grads.shape),
        ],
        out_specs=[whole(classes, head), whole(part, head)],
        name="class_backward",
    )(where, logits, got, partial, grads)


def chip_kernel(has_extra, where_ref, keep_ref, got_ref, *refs):
    out_ref, token_ref = refs[-2:]
    token_ref[...] = jnp.zeros(token_ref.shape, F32)
    n = keep_ref.shape[1]
    out_ref[:, :n, :] = (keep_ref[...].astype(F32) + got_ref[...].astype(F32)).astype(BF16)
    if has_extra:
        mine, other = refs[0][...].astype(F32), refs[1][...].astype(F32)
        even = where_ref[CORE] == 0
        pair = [jnp.where(even, mine, other).astype(BF16), jnp.where(even, other, mine).astype(BF16)]
        size = mine.shape[0]
        for z in range(out_ref.shape[0]):
            for c in range(2):
                out_ref[z, n + c * size : n + (c + 1) * size, :] = pair[c]


def add_cores(where, keep, send, extra=(), before=()):
    chips, n, part = keep.shape
    extra = [e for own in extra for e in (own, swap(own, "dp", 1))]
    rows = n + sum(e.shape[0] for e in extra)
    return call(
        functools.partial(chip_kernel, len(extra) > 0),
        [shape((chips, rows, part), BF16), shape(TOKEN, F32)],
        limit=16,
        in_specs=[SMEM, VMEM, VMEM, *[VMEM] * len(extra), *[ANY] * len(before)],
        name="add_cores",
    )(where, keep, swap(send, "dp", 1), *extra, *before)


def exchange_chips(parts):
    count = lax.axis_size("dp")
    return exchange(parts, [[z + core for z in range(0, count, 2)] for core in range(2)])


def finish_kernel(inner, early_ref, last_ref, first_ref, second_ref, decode_ref):
    chips, _, part = early_ref.shape
    n = decode_ref.shape[1]
    last = sum(last_ref[z].astype(F32) for z in range(chips))
    first_ref[...] = last[inner:].T
    tall = second_ref.shape[0]
    for q in range(inner // tall):
        second_ref[:, q * part : (q + 1) * part] = last[q * tall : (q + 1) * tall]
    decode_ref[...] = sum(early_ref[z, :n].astype(F32) for z in range(chips)).T


def finish(early, last, inner, groups, n):
    part = early.shape[2]
    return call(
        functools.partial(finish_kernel, inner),
        [shape((part, inner), F32), shape((inner // groups, part * groups), F32), shape((part, n), F32)],
        limit=16,
        name="finish",
    )(early, last)


def local(acts, patches, labels, w_first, w_second, w_decode, w_aux, w_class):
    acts = acts[0].transpose(1, 0, 2)
    pix, images, width = acts.shape
    groups, count = lax.axis_size("dp"), lax.axis_size("section")
    me, section = lax.axis_index("dp"), lax.axis_index("section")
    scale = (groups * images * pix) ** -0.5
    norm = (groups * images) ** 0.5
    first, second, decode, aux, klass = w_first[0], w_second[0], w_decode[0], w_aux[0], w_class[0]
    inner, head = first.shape[1], aux.shape[1]
    n_decode = decode.shape[1]
    rows = pix * images

    paired = count == 4 and patches.shape[2] == 192
    if paired:
        near = [section ^ k for k in range(4)]
        tiles = [t for s in near for t in (3 * (s >> 1) + 2 * (s & 1), 3 * (s >> 1) + 1)]
        where = jnp.stack([section & 1, me & 1, me, *tiles]).astype(jnp.int32)
        turned = patches.transpose(0, 2, 1)
        packed = [pack(where, turned, h) for h in range(2)]
        before_forward = [packed[1][1]]
        halves = [half for half, _ in packed]
        x, y = [swap(halves[0], "section", 1)], [swap(halves[0], "section", 2)]
        before_head = [x[0], y[0]]
    else:
        where = jnp.stack([section & 1, me & 1, me]).astype(jnp.int32)
        before_forward = before_head = []
        target = lax.all_gather(patches, "section", axis=2, tiled=True).transpose(1, 0, 2)

    hidden, feature, pooled = forward(acts, first, second, before_forward)
    aux_pre, sent = aux_head(pooled, aux, labels, pix, groups, before_head)
    got = exchange(sent)
    if paired:
        last = after(halves[1], pooled)
        x.append(swap(last, "section", 1))
        y.append(swap(last, "section", 2))
        diagonal = [swap(after(y[0], aux_pre), "section", 1), swap(after(x[1], aux_pre), "section", 2)]
        blocks = [halves, x, y, diagonal]
        target = patch_operands(blocks, [0, 1, 2, 3], [0, 1, 2, 3])
    else:
        target = [target], [pl.BlockSpec((pix // STEPS, images, n_decode), lambda g, where: (g, 0, 0))]
    recon, token = reconstruct(feature, decode, sent)
    logits, sent = class_logits(where, got, klass, token)
    partial = exchange(sent)
    grad, keep, send = residual(where, feature, recon, *target, sent, images, scale, groups)
    pooled_grad, aux_grad = aux_backward(partial, aux_pre, aux, pix, norm)
    chip_decode, token = add_cores(where, keep, send, [aux_grad])
    sum_decode = exchange_chips(chip_decode)
    keep, send = backward(
        where, grad, hidden, acts.reshape(rows, width), decode, pooled_grad, second, token, groups
    )
    sum_last = exchange_chips(add_cores(where, keep, send, before=[sum_decode])[0])
    grad_class, grad_aux = class_backward(
        where, logits, got, partial, sum_decode, n_decode, klass.shape[0], head, norm
    )
    grad_first, grad_second, grad_decode = finish(sum_decode, sum_last, inner, groups, n_decode)
    return grad_first[None], grad_second[None], grad_decode[None], grad_aux[None], grad_class[None]


def solution(mesh):
    in_specs = (
        P("section", "dp", None, None),
        P("dp", None, "section"),
        P("dp"),
        P("section", None, None),
        P("section", None, None),
        P("section", None, None),
        P("section", None, None),
        P("section", "dp", None),
    )
    out_specs = (P("section", "dp", None),) * 5
    return jax.shard_map(local, mesh=mesh, in_specs=in_specs, out_specs=out_specs, check_vma=False)
```

time: 137 us -> 146 us (1.066)
  blocking collectives: 0 us -> 15 us
  starting transfers between devices: 25.4 us -> 20.5 us
  local copies, waits for them, and re-layouts: 8 us -> 10.1 us
  waiting for transfers between devices: 30 us -> 28.2 us
    all_to_all x0 -> x1, blocking collectives: none -> 15 us  [exchange(): lax.all_to_all(value, 'dp', 0, 0, axis_index_groups=groups, tiled=True)]
    all_to_all x4 -> x3, waiting for transfers between devices: 20.2 us -> 13.3 us  [exchange(): lax.all_to_all(value, 'dp', 0, 0, axis_index_groups=groups, tiled=True)]
    all_to_all x4 -> x3, starting transfers between devices: 18.2 us -> 12.1 us  [exchange(): lax.all_to_all(value, 'dp', 0, 0, axis_index_groups=groups, tiled=True)]
    ppermute x9, waiting for transfers between devices: 9.83 us -> 14.8 us  [swap(): return lax.ppermute(value, axis, [(i, i ^ bits) for i in range(count)])]
    unnamed x42 -> x44, local copies, waits for them, and re-layouts: 7.91 us -> 9.98 us
    pallas_call x8 -> x9, Pallas kernels: 55.8 us -> 55.9 us  [the longest x1 18.7 us: backward(): call(functools.partial(backward_kernel, groups), [shape(parts, BF16), sha...]
  transfers between devices with their start and end apart: 13 -> 12, of which waited for: 8 -> 5; matrix products, arithmetic and copies ran while one was open for 0% -> 0% of each run, Pallas kernels for 42% -> 34%
where the time goes in v5:
time: 146 us
  Pallas kernels  71.1 us (49%)
  waiting for transfers between devices  28.2 us (19%)
  starting transfers between devices  20.5 us (14%)
  blocking collectives  15 us (10%)
  local copies, waits for them, and re-layouts  10.1 us (7%)
    pallas_call x1, Pallas kernels, backward(): call(functools.partial(backward_kernel, groups), [shape(parts, BF16), sha...  18.7 us
    pallas_call x1, Pallas kernels, residual(): call(functools.partial(residual_kernel, groups, scale, len(patch_args)),...  16.3 us
    all_to_all x1, blocking collectives, exchange(): lax.all_to_all(value, 'dp', 0, 0, axis_index_groups=groups, tiled=True)  15 us
    ppermute x9, waiting for transfers between devices, swap(): return lax.ppermute(value, axis, [(i, i ^ bits) for i in range(count)])  14.8 us
    all_to_all x3, waiting for transfers between devices, exchange(): lax.all_to_all(value, 'dp', 0, 0, axis_index_groups=groups, tiled=True)  13.3 us
    all_to_all x3, starting transfers between devices, exchange(): lax.all_to_all(value, 'dp', 0, 0, axis_index_groups=groups, tiled=True)  12.1 us
    pallas_call x1, Pallas kernels, forward(): call(forward_kernel, [shape((pix * images, inner), BF16), shape((pix * im...  11.2 us
    pallas_call x1, Pallas kernels, reconstruct(): call(recon_kernel, [shape((rows, n), F32), shape(TOKEN, F32)], limit=58,...  10.1 us
  transfers between devices with their start and end apart: 12, of which 5 were waited for; matrix products, arithmetic and copies ran while one was open for 0% of the time, Pallas kernels for 34%

profile of v5, /device:TPU:0, one launch (start us, length us, event | category | flops | bytes accessed | tf_op | source)
XLA Modules:
  0.0 145.7 jit_solution(10614402353651621684)
XLA Ops:
  0.7 0.1 stack.47.where_ref
  0.7 0.0 copy-start
  0.8 1.4 copy-done
  2.2 1.7 %pack_patches.3 = (bf16[147,16,128]{2,1,0:T(8,128)(2,1)S(1)}, f32[8,128]{1,0:T(8,128)}) custom-call(s32[11]{0:T(128)S(1)} %stack.47.where_ref, bf16[16,192,196]{2,1,0:T(8,128)(2,1)S(1)} %bitcast.27), custom_call_target="tpu_custom_call" | custom-call | tf_op jit(solution)/shard_map/pack_patches/pallas_call | solution.py:87
  3.9 3.0 %collective-permute-start.1 = (bf16[147,16,128]{2,1,0:T(8,128)(2,1)S(1)}, bf16[147,16,128]{2,1,0:T(8,128)(2,1)S(1)}, u32[]{:S(2)}, u32[]{:S(2)}) collective-permute-start(bf16[147,16,128]{2,1,0:T(8,128)(2,1)S(1)} %get-tuple-element.38.refs_0_.refs_8_), channel_id=1, source_target_pairs={{0,16},{8,24},{16,0},{24,8},{1,17},{9,25},{17,1},{25,9},{2,18},{10... | collective-permute-start | bytes 1806344 | tf_op jit(solution)/shard_map/ppermute | solution.py:48
  6.9 1.5 %collective-permute-start = (bf16[147,16,128]{2,1,0:T(8,128)(2,1)S(1)}, bf16[147,16,128]{2,1,0:T(8,128)(2,1)S(1)}, u32[]{:S(2)}, u32[]{:S(2)}) collective-permute-start(bf16[147,16,128]{2,1,0:T(8,128)(2,1)S(1)} %get-tuple-element.38.refs_0_.refs_8_), channel_id=1, source_target_pairs={{0,8},{8,0},{16,24},{24,16},{1,9},{9,1},{17,25},{25,17},{2,10},{10... | collective-permute-start | bytes 1806344 | tf_op jit(solution)/shard_map/ppermute | solution.py:48
  8.4 1.7 %pack_patches.2 = (bf16[147,16,128]{2,1,0:T(8,128)(2,1)S(1)}, f32[8,128]{1,0:T(8,128)S(1)}) custom-call(s32[11]{0:T(128)S(1)} %stack.47.where_ref, bf16[16,192,196]{2,1,0:T(8,128)(2,1)S(1)} %bitcast.28), custom_call_target="tpu_custom_call" | custom-call | tf_op jit(solution)/shard_map/pack_patches/pallas_call | solution.py:87
  10.1 0.0 copy-start.21
  10.1 0.6 copy-done.21
  10.7 11.2 %forward.1 = (bf16[3136,256]{1,0:T(8,128)(2,1)}, bf16[3136,1024]{1,0:T(8,128)(2,1)}, f32[16,1024]{1,0:T(8,128)}) custom-call(bf16[196,16,1024]{2,1,0:T(8,128)(2,1)} %bitcast.32, bf16[1024,256]{1,0:T(8,128)(2,1)} %bitcast.37, bf16[256,1024]{1,0:T(8,128)(2,1)} %bitcast.38, f32[8,128]{1,0:T(8,128)} %copy-done.21), custom_call_target="tpu_custom_call" | custom-call | flops 3288334336 | bytes 14450688 | tf_op jit(solution)/shard_map/forward/pallas_call | solution.py:130
  21.9 0.6 collective-permute-start.2
  22.5 0.1 collective-permute-start.3
  22.7 0.0 copy-start.13
  22.7 0.9 copy-done.13
  23.6 1.5 %aux_head.1 = (f32[16,512]{1,0:T(8,128)S(1)}, bf16[8,16,768]{2,1,0:T(8,128)(2,1)}) custom-call(f32[16,1024]{1,0:T(8,128)S(1)} %copy-done.13, bf16[1024,512]{1,0:T(8,128)(2,1)S(1)} %bitcast.29, s32[16]{0:T(128)S(1)} %copy-done.18, bf16[147,16,128]{2,1,0:T(8,128)(2,1)S(1)} %collective-permute-done.refs_0_.refs_2_.refs_10_, ...), custom_call_target="tpu_custom_call" | custom-call | tf_op jit(solution)/shard_map/aux_head/pallas_call | solution.py:177
  25.0 1.9 %collective-permute-start.4 = (bf16[147,16,128]{2,1,0:T(8,128)(2,1)S(1)}, bf16[147,16,128]{2,1,0:T(8,128)(2,1)}, u32[]{:S(2)}, u32[]{:S(2)}) collective-permute-start(bf16[147,16,128]{2,1,0:T(8,128)(2,1)S(1)} %collective-permute-done.1.refs_1_.refs_4_.refs_12_), channel_id=1, source_target_pairs={{0,8},{8,0},{16,24},{24,16},{1,9},{9,1},{17,25},{25,17},{2,10},{10... | collective-permute-start | bytes 1806344 | tf_op jit(solution)/shard_map/ppermute | solution.py:48
  27.0 11.7 %collective-permute-done.2.refs_3_.refs_11_ = bf16[147,16,128]{2,1,0:T(8,128)(2,1)} collective-permute-done((bf16[147,16,128]{2,1,0:T(8,128)(2,1)S(1)}, bf16[147,16,128]{2,1,0:T(8,128)(2,1)}, u32[]{:S(2)}, u32[]{:S(2)}) %collective-permute-start.2) | collective-permute-done | bytes 602144 | tf_op jit(solution)/shard_map/ppermute | solution.py:48
  38.6 0.5 collective-permute-start.5
  39.1 4.9 %all-to-all-start = ((bf16[8,16,768]{2,1,0:T(8,128)(2,1)}), bf16[8,16,768]{2,1,0:T(8,128)(2,1)S(1)}, u32[]{:S(2)}, u32[]{:S(2)}) async-start(bf16[8,16,768]{2,1,0:T(8,128)(2,1)} %get-tuple-element.39._), calls=%async_computation | async-start | bytes 393216 | tf_op jit(solution)/shard_map/all_to_all | solution.py:52
  44.0 10.1 %reconstruct.1 = (f32[3136,768]{1,0:T(8,128)}, f32[8,128]{1,0:T(8,128)}) custom-call(bf16[3136,1024]{1,0:T(8,128)(2,1)} %get-tuple-element.36.feature_ref, bf16[1024,768]{1,0:T(8,128)(2,1)} %bitcast.35, bf16[8,16,768]{2,1,0:T(8,128)(2,1)} %get-tuple-element.39._), custom_call_target="tpu_custom_call" | custom-call | flops 4932501504 | bytes 16056320 | tf_op jit(solution)/shard_map/reconstruct/pallas_call | solution.py:198
  54.1 0.0 all-to-all-done.got_ref
  54.1 0.0 copy-start.6
  54.1 1.4 copy-done.6
  55.5 0.7 copy-done.17
  56.2 2.0 %class_logits.1 = (f32[128,1408]{1,0:T(8,128)S(1)}, bf16[8,16,1152]{2,1,0:T(8,128)(2,1)S(1)}) custom-call(s32[11]{0:T(128)S(1)} %stack.47.where_ref, bf16[8,16,768]{2,1,0:T(8,128)(2,1)S(1)} %all-to-all-done.got_ref, bf16[1408,512]{1,0:T(8,128)(2,1)S(1)} %bitcast.31, f32[8,128]{1,0:T(8,128)S(1)} %copy-done.17), custom_call_target="tpu_custom_call" | custom-call | tf_op jit(solution)/shard_map/class_logits/pallas_call | solution.py:506
  58.1 0.0 copy-start.7
  58.1 0.7 copy-done.7
  58.8 0.9 copy-done.10
  59.7 16.3 %residual.1 = (bf16[3136,768]{1,0:T(8,128)(2,1)}, bf16[4,768,128]{2,1,0:T(8,128)(2,1)}, bf16[4,768,128]{2,1,0:T(8,128)(2,1)}) custom-call(s32[11]{0:T(128)} %copy-done.14, bf16[3136,1024]{1,0:T(8,128)(2,1)} %get-tuple-element.36.feature_ref, f32[3136,768]{1,0:T(8,128)} %get-tuple-element.40.recon_ref, bf16[147,16,128]{2,1,0:T(8,128)(2,1)} %copy-done.4, ...), custom_call_target="tpu_custom_call" | custom-call | flops 4932501504 | bytes 20873216 | tf_op jit(solution)/shard_map/residual/pallas_call | solution.py:353
  76.1 0.6 collective-permute-start.6
  76.6 15.0 %all_to_all.20.got_ref.stats_ref = bf16[8,16,1152]{2,1,0:T(8,128)(2,1)S(1)} all-to-all(bf16[8,16,1152]{2,1,0:T(8,128)(2,1)S(1)} %copy-done.8), channel_id=1, replica_groups=mesh['section'=4,'dp'=8] {'dp'}, dimensions={0} | all-to-all | bytes 589824 | tf_op jit(solution)/shard_map/all_to_all | solution.py:52
  91.6 0.6 aux_backward.1
  92.2 0.6 copy-done.19
  92.9 1.2 collective-permute-done.7.refs_1_
  94.1 1.1 copy-done.9
  95.2 1.7 %add_cores.2 = (bf16[4,896,128]{2,1,0:T(8,128)(2,1)}, f32[8,128]{1,0:T(8,128)S(1)}) custom-call(s32[11]{0:T(128)S(1)} %copy-done.15, bf16[4,768,128]{2,1,0:T(8,128)(2,1)S(1)} %copy-done.9, bf16[4,768,128]{2,1,0:T(8,128)(2,1)S(1)} %collective-permute-done.6.got_ref, bf16[64,128]{1,0:T(8,128)(2,1)S(1)} %get-tuple-element.50.refs_0_, ...), custom_call_target="tpu_custom_call" | custom-call | tf_op jit(solution)/shard_map/add_cores/pallas_call | solution.py:615
  96.9 0.6 copy-done.20
  97.5 3.7 %all-to-all-start.2 = ((bf16[4,896,128]{2,1,0:T(8,128)(2,1)}), bf16[4,896,128]{2,1,0:T(8,128)(2,1)S(1)}, u32[]{:S(2)}, u32[]{:S(2)}) async-start(bf16[4,896,128]{2,1,0:T(8,128)(2,1)} %get-tuple-element.51), calls=%async_computation.2 | async-start | bytes 1835008 | tf_op jit(solution)/shard_map/all_to_all | solution.py:52
  101.2 18.7 %backward.1 = (bf16[4,512,128]{2,1,0:T(8,128)(2,1)}, bf16[4,512,128]{2,1,0:T(8,128)(2,1)}) custom-call(s32[11]{0:T(128)} %copy-done.14, bf16[3136,768]{1,0:T(8,128)(2,1)} %get-tuple-element.52.grad_ref, bf16[3136,256]{1,0:T(8,128)(2,1)} %get-tuple-element.53.hidden_ref, bf16[3136,1024]{1,0:T(8,128)(2,1)} %bitcast.33, bf16[1024,768]{1,0:T(8,128)(2,1)} %bitcast.36, ...), custom_call_target="tpu_custom_call" | custom-call | flops 9865003008 | bytes 12845056 | tf_op jit(solution)/shard_map/backward/pallas_call | solution.py:419
  120.0 0.2 collective-permute-start.8
  120.2 2.0 %collective-permute-done.8.got_ref = bf16[4,512,128]{2,1,0:T(8,128)(2,1)S(1)} collective-permute-done((bf16[4,512,128]{2,1,0:T(8,128)(2,1)}, bf16[4,512,128]{2,1,0:T(8,128)(2,1)S(1)}, u32[]{:S(2)}, u32[]{:S(2)}) %collective-permute-start.8) | collective-permute-done | bytes 524320 | tf_op jit(solution)/shard_map/ppermute | solution.py:48
  122.1 2.4 %all-to-all-done.2.refs_0_.early_ref.grads_ref = bf16[4,896,128]{2,1,0:T(8,128)(2,1)S(1)} async-done(((bf16[4,896,128]{2,1,0:T(8,128)(2,1)}), bf16[4,896,128]{2,1,0:T(8,128)(2,1)S(1)}, u32[]{:S(2)}, u32[]{:S(2)}) %all-to-all-start.2) | async-done | bytes 917536 | tf_op jit(solution)/shard_map/all_to_all | solution.py:52
  124.5 1.0 copy-done.12
  125.5 1.5 %add_cores.3 = (bf16[4,512,128]{2,1,0:T(8,128)(2,1)}, f32[8,128]{1,0:T(8,128)}) custom-call(s32[11]{0:T(128)S(1)} %copy-done.16, bf16[4,512,128]{2,1,0:T(8,128)(2,1)S(1)} %copy-done.12, bf16[4,512,128]{2,1,0:T(8,128)(2,1)S(1)} %collective-permute-done.8.got_ref, bf16[4,896,128]{2,1,0:T(8,128)(2,1)S(1)} %all-to-all-done.2.refs_0_.early_ref.grads_ref), custom_call_target="tpu_custom_call" | custom-call | tf_op jit(solution)/shard_map/add_cores/pallas_call | solution.py:615
  127.0 3.5 %all-to-all-start.3 = ((bf16[4,512,128]{2,1,0:T(8,128)(2,1)}), bf16[4,512,128]{2,1,0:T(8,128)(2,1)S(1)}, u32[]{:S(2)}, u32[]{:S(2)}) async-start(bf16[4,512,128]{2,1,0:T(8,128)(2,1)} %get-tuple-element.58), calls=%async_computation.3 | async-start | bytes 1048576 | tf_op jit(solution)/shard_map/all_to_all | solution.py:52
  130.5 3.2 %class_backward.1 = (f32[1408,512]{1,0:T(8,128)}, f32[128,512]{1,0:T(8,128)}) custom-call(s32[11]{0:T(128)S(1)} %copy-done.16, f32[128,1408]{1,0:T(8,128)S(1)} %copy-done.11, bf16[8,16,768]{2,1,0:T(8,128)(2,1)S(1)} %all-to-all-done.got_ref, bf16[8,16,1152]{2,1,0:T(8,128)(2,1)S(1)} %all_to_all.20.got_ref.stats_ref, ...), custom_call_target="tpu_custom_call" | custom-call | flops 184549376 | bytes 2883584 | tf_op jit(solution)/shard_map/class_backward/pallas_call | solution.py:577
  133.7 11.0 %all-to-all-done.3.last_ref = bf16[4,512,128]{2,1,0:T(8,128)(2,1)S(1)} async-done(((bf16[4,512,128]{2,1,0:T(8,128)(2,1)}), bf16[4,512,128]{2,1,0:T(8,128)(2,1)S(1)}, u32[]{:S(2)}, u32[]{:S(2)}) %all-to-all-start.3) | async-done | bytes 524320 | tf_op jit(solution)/shard_map/all_to_all | solution.py:52
  144.7 1.0 finish.1
  (35 shorter events, 0.1 us)
Async XLA Ops:
  0.7 53.4 %copy-start.14 = (s32[11]{0:T(128)}, s32[11]{0:T(128)S(1)}, u32[]{:S(2)}) copy-start(s32[11]{0:T(128)S(1)} %stack.47.where_ref) | copy-start | bytes 136
  0.7 1.4 copy-start
  3.9 18.1 %copy-start.4 = (bf16[147,16,128]{2,1,0:T(8,128)(2,1)}, bf16[147,16,128]{2,1,0:T(8,128)(2,1)S(1)}, u32[]{:S(2)}) copy-start(bf16[147,16,128]{2,1,0:T(8,128)(2,1)S(1)} %get-tuple-element.38.refs_0_.refs_8_) | copy-start | bytes 1806340
  3.9 18.7 %collective-permute-start.1 = (bf16[147,16,128]{2,1,0:T(8,128)(2,1)S(1)}, bf16[147,16,128]{2,1,0:T(8,128)(2,1)S(1)}, u32[]{:S(2)}, u32[]{:S(2)}) collective-permute-start(bf16[147,16,128]{2,1,0:T(8,128)(2,1)S(1)} %get-tuple-element.38.refs_0_.refs_8_), channel_id=1, source_target_pairs={{0,16},{8,24},{16,0},{24,8},{1,17},{9,25},{17,1},{25,9},{2,18},{10... | collective-permute-start | bytes 1806344 | tf_op jit(solution)/shard_map/ppermute | solution.py:48
  6.9 15.7 %collective-permute-start = (bf16[147,16,128]{2,1,0:T(8,128)(2,1)S(1)}, bf16[147,16,128]{2,1,0:T(8,128)(2,1)S(1)}, u32[]{:S(2)}, u32[]{:S(2)}) collective-permute-start(bf16[147,16,128]{2,1,0:T(8,128)(2,1)S(1)} %get-tuple-element.38.refs_0_.refs_8_), channel_id=1, source_target_pairs={{0,8},{8,0},{16,24},{24,16},{1,9},{9,1},{17,25},{25,17},{2,10},{10... | collective-permute-start | bytes 1806344 | tf_op jit(solution)/shard_map/ppermute | solution.py:48
  10.1 0.6 copy-start.21
  10.7 11.8 %copy-start.5 = (bf16[147,16,128]{2,1,0:T(8,128)(2,1)}, bf16[147,16,128]{2,1,0:T(8,128)(2,1)S(1)}, u32[]{:S(2)}) copy-start(bf16[147,16,128]{2,1,0:T(8,128)(2,1)S(1)} %get-tuple-element.42.refs_1_.refs_9_) | copy-start | bytes 1806340
  10.7 11.9 %copy-start.3 = (bf16[1,1024,512]{2,1,0:T(8,128)(2,1)S(1)}, bf16[1,1024,512]{2,1,0:T(8,128)(2,1)}, u32[]{:S(2)}) copy-start(bf16[1,1024,512]{2,1,0:T(8,128)(2,1)} %param.14) | copy-start | bytes 3145732
  10.7 11.9 %copy-start.18 = (s32[16]{0:T(128)S(1)}, s32[16]{0:T(128)}, u32[]{:S(2)}) copy-start(s32[16]{0:T(128)} %labels_ref.1) | copy-start | bytes 196
  21.9 16.7 %collective-permute-start.2 = (bf16[147,16,128]{2,1,0:T(8,128)(2,1)S(1)}, bf16[147,16,128]{2,1,0:T(8,128)(2,1)}, u32[]{:S(2)}, u32[]{:S(2)}) collective-permute-start(bf16[147,16,128]{2,1,0:T(8,128)(2,1)S(1)} %get-tuple-element.42.refs_1_.refs_9_), channel_id=1, source_target_pairs={{0,8},{8,0},{16,24},{24,16},{1,9},{9,1},{17,25},{25,17},{2,10},{10... | collective-permute-start | bytes 1806344 | tf_op jit(solution)/shard_map/ppermute | solution.py:48
  22.5 37.2 %collective-permute-start.3 = (bf16[147,16,128]{2,1,0:T(8,128)(2,1)S(1)}, bf16[147,16,128]{2,1,0:T(8,128)(2,1)}, u32[]{:S(2)}, u32[]{:S(2)}) collective-permute-start(bf16[147,16,128]{2,1,0:T(8,128)(2,1)S(1)} %get-tuple-element.42.refs_1_.refs_9_), channel_id=1, source_target_pairs={{0,16},{8,24},{16,0},{24,8},{1,17},{9,25},{17,1},{25,9},{2,18},{10... | collective-permute-start | bytes 1806344 | tf_op jit(solution)/shard_map/ppermute | solution.py:48
  22.6 31.5 %copy-start.1 = (bf16[147,16,128]{2,1,0:T(8,128)(2,1)}, bf16[147,16,128]{2,1,0:T(8,128)(2,1)S(1)}, u32[]{:S(2)}) copy-start(bf16[147,16,128]{2,1,0:T(8,128)(2,1)S(1)} %collective-permute-done.1.refs_1_.refs_4_.refs_12_) | copy-start | bytes 1806340
  22.6 31.5 %copy-start.2 = (bf16[147,16,128]{2,1,0:T(8,128)(2,1)}, bf16[147,16,128]{2,1,0:T(8,128)(2,1)S(1)}, u32[]{:S(2)}) copy-start(bf16[147,16,128]{2,1,0:T(8,128)(2,1)S(1)} %collective-permute-done.refs_0_.refs_2_.refs_10_) | copy-start | bytes 1806340
  22.7 0.9 copy-start.13
  25.0 34.7 %collective-permute-start.4 = (bf16[147,16,128]{2,1,0:T(8,128)(2,1)S(1)}, bf16[147,16,128]{2,1,0:T(8,128)(2,1)}, u32[]{:S(2)}, u32[]{:S(2)}) collective-permute-start(bf16[147,16,128]{2,1,0:T(8,128)(2,1)S(1)} %collective-permute-done.1.refs_1_.refs_4_.refs_12_), channel_id=1, source_target_pairs={{0,8},{8,0},{16,24},{24,16},{1,9},{9,1},{17,25},{25,17},{2,10},{10... | collective-permute-start | bytes 1806344 | tf_op jit(solution)/shard_map/ppermute | solution.py:48
  38.6 21.1 %collective-permute-start.5 = (bf16[147,16,128]{2,1,0:T(8,128)(2,1)}, bf16[147,16,128]{2,1,0:T(8,128)(2,1)}, u32[]{:S(2)}, u32[]{:S(2)}) collective-permute-start(bf16[147,16,128]{2,1,0:T(8,128)(2,1)} %collective-permute-done.2.refs_3_.refs_11_), channel_id=1, source_target_pairs={{0,16},{8,24},{16,0},{24,8},{1,17},{9,25},{17,1},{25,9},{2,18},{10... | collective-permute-start | bytes 1806344 | tf_op jit(solution)/shard_map/ppermute | solution.py:48
  39.1 15.0 %all-to-all-start = ((bf16[8,16,768]{2,1,0:T(8,128)(2,1)}), bf16[8,16,768]{2,1,0:T(8,128)(2,1)S(1)}, u32[]{:S(2)}, u32[]{:S(2)}) async-start(bf16[8,16,768]{2,1,0:T(8,128)(2,1)} %get-tuple-element.39._), calls=%async_computation | async-start | bytes 393216 | tf_op jit(solution)/shard_map/all_to_all | solution.py:52
  54.1 1.4 copy-start.6
  55.5 0.7 copy-start.17
  58.1 0.7 copy-start.7
  58.8 0.9 copy-start.10
  59.7 16.9 %copy-start.8 = (bf16[8,16,1152]{2,1,0:T(8,128)(2,1)S(1)}, bf16[8,16,1152]{2,1,0:T(8,128)(2,1)}, u32[]{:S(2)}) copy-start(bf16[8,16,1152]{2,1,0:T(8,128)(2,1)} %copy-done.7) | copy-start | bytes 884740
  59.7 34.4 %copy-start.15 = (s32[11]{0:T(128)S(1)}, s32[11]{0:T(128)}, u32[]{:S(2)}) copy-start(s32[11]{0:T(128)} %copy-done.14) | copy-start | bytes 136
  76.1 18.0 %collective-permute-start.6 = (bf16[4,768,128]{2,1,0:T(8,128)(2,1)}, bf16[4,768,128]{2,1,0:T(8,128)(2,1)S(1)}, u32[]{:S(2)}, u32[]{:S(2)}) collective-permute-start(bf16[4,768,128]{2,1,0:T(8,128)(2,1)} %get-tuple-element.49), channel_id=1, source_target_pairs={{0,1},{1,0},{2,3},{3,2},{4,5},{5,4},{6,7},{7,6},{8,9},{9,8},{10,11... | collective-permute-start | bytes 2359304 | tf_op jit(solution)/shard_map/ppermute | solution.py:48
  92.2 0.6 copy-start.19
  92.9 1.2 collective-permute-start.7
  94.1 1.1 copy-start.9
  96.9 0.6 copy-start.20
  97.5 27.0 %all-to-all-start.2 = ((bf16[4,896,128]{2,1,0:T(8,128)(2,1)}), bf16[4,896,128]{2,1,0:T(8,128)(2,1)S(1)}, u32[]{:S(2)}, u32[]{:S(2)}) async-start(bf16[4,896,128]{2,1,0:T(8,128)(2,1)} %get-tuple-element.51), calls=%async_computation.2 | async-start | bytes 1835008 | tf_op jit(solution)/shard_map/all_to_all | solution.py:52
  101.2 23.3 %copy-start.16 = (s32[11]{0:T(128)S(1)}, s32[11]{0:T(128)}, u32[]{:S(2)}) copy-start(s32[11]{0:T(128)} %copy-done.14) | copy-start | bytes 136
  119.9 10.5 %copy-start.11 = (f32[128,1408]{1,0:T(8,128)S(1)}, f32[128,1408]{1,0:T(8,128)}, u32[]{:S(2)}) copy-start(f32[128,1408]{1,0:T(8,128)} %copy-done.10) | copy-start | bytes 2162692
  120.0 2.2 %collective-permute-start.8 = (bf16[4,512,128]{2,1,0:T(8,128)(2,1)}, bf16[4,512,128]{2,1,0:T(8,128)(2,1)S(1)}, u32[]{:S(2)}, u32[]{:S(2)}) collective-permute-start(bf16[4,512,128]{2,1,0:T(8,128)(2,1)} %get-tuple-element.57), channel_id=1, source_target_pairs={{0,1},{1,0},{2,3},{3,2},{4,5},{5,4},{6,7},{7,6},{8,9},{9,8},{10,11... | collective-permute-start | bytes 1572872 | tf_op jit(solution)/shard_map/ppermute | solution.py:48
  124.5 1.0 copy-start.12
  127.0 17.7 %all-to-all-start.3 = ((bf16[4,512,128]{2,1,0:T(8,128)(2,1)}), bf16[4,512,128]{2,1,0:T(8,128)(2,1)S(1)}, u32[]{:S(2)}, u32[]{:S(2)}) async-start(bf16[4,512,128]{2,1,0:T(8,128)(2,1)} %get-tuple-element.58), calls=%async_computation.3 | async-start | bytes 1048576 | tf_op jit(solution)/shard_map/all_to_all | solution.py:52

commit v6 on v5

--- a/solution.py
+++ b/solution.py
@@ -13,7 +13,6 @@
 LANES = 128
 TILE = 256
 MIB = 1024 * 1024
-TOKEN = (8, LANES)
 ROWS_0 = (((0,), (0,)), ((), ()))
 COLS_1 = (((1,), (1,)), ((), ()))
 PARITY, CORE, ME, TILES = 0, 1, 2, 3
@@ -39,7 +38,6 @@
 
 SMEM = pl.BlockSpec(memory_space=pltpu.SMEM)
 VMEM = pl.BlockSpec(memory_space=pltpu.VMEM)
-ANY = pl.BlockSpec(memory_space=pl.ANY)
 HBM = pl.BlockSpec(memory_space=pltpu.HBM)
 
 
@@ -52,7 +50,7 @@
     return lax.all_to_all(value, "dp", 0, 0, axis_index_groups=groups, tiled=True)
 
 
-def pack_kernel(first, where_ref, patches_ref, out_ref, token_ref, turned, own, shared):
+def pack_kernel(first, where_ref, patches_ref, out_ref, turned, own, shared):
     images, span, pix = patches_ref.shape
     padded = turned.shape[1]
     count = out_ref.shape[0] // 3 * 2
@@ -76,8 +74,15 @@
         own[16 * b : 16 * b + 16] = out[:, :LANES].reshape(16, images, LANES)
         shared[16 * b : 16 * b + 16] = out[:, LANES:].reshape(16, images, 64)
     out_ref[:count] = own[:count]
-    out_ref[count:] = jnp.concatenate([shared[: count // 2], shared[count // 2 : count]], axis=2)
-    token_ref[...] = jnp.zeros(token_ref.shape, F32)
+    lower, upper = shared[: count // 2], shared[count // 2 : count]
+
+    @pl.when(parity == 0)
+    def _():
+        out_ref[count:] = jnp.concatenate([lower, upper], axis=2)
+
+    @pl.when(parity == 1)
+    def _():
+        out_ref[count:] = jnp.concatenate([upper, lower], axis=2)
 
 
 def pack(where, patches, h):
@@ -86,7 +91,7 @@
     padded = -(-half // 16) * 16
     return call(
         functools.partial(pack_kernel, h * half),
-        [shape((half + half // 2, images, LANES), BF16), shape(TOKEN, F32)],
+        shape((half + half // 2, images, LANES), BF16),
         limit=20,
         in_specs=[SMEM, VMEM],
         scratch_shapes=[
@@ -102,8 +107,7 @@
     return lax.optimization_barrier((value, other))[0]
 
 
-def forward_kernel(acts_ref, first_ref, second_ref, *refs):
-    hidden_ref, feature_ref, pooled_ref = refs[-3:]
+def forward_kernel(acts_ref, first_ref, second_ref, hidden_ref, feature_ref, pooled_ref):
     step = pl.program_id(0)
     block, images, width = acts_ref.shape
     flat = acts_ref[...].reshape(block * images, width)
@@ -121,7 +125,7 @@
         pooled_ref[:, cut] += jnp.sum(feature.reshape(block, images, TILE).astype(F32), axis=0)
 
 
-def forward(acts, first, second, before):
+def forward(acts, first, second):
     pix, images, width = acts.shape
     inner = first.shape[1]
     block = pix // STEPS
@@ -142,15 +146,13 @@
             pl.BlockSpec((block, images, width), lambda g: (g, 0, 0)),
             pl.BlockSpec(first.shape, whole),
             pl.BlockSpec(second.shape, whole),
-            *[ANY] * len(before),
         ],
         out_specs=[rows(inner), rows(width), pl.BlockSpec((images, width), whole)],
         name="forward",
-    )(acts, first, second, *before)
-
-
-def head_kernel(pix, pooled_ref, aux_ref, labels_ref, *refs):
-    aux_pre_ref, sent_ref = refs[-2:]
+    )(acts, first, second)
+
+
+def head_kernel(pix, pooled_ref, aux_ref, labels_ref, aux_pre_ref, sent_ref):
     groups, images, _ = sent_ref.shape
     width, head = aux_ref.shape
     part = width // groups
@@ -172,40 +174,39 @@
         sent_ref[d, :, head + LANES :] = digits
 
 
-def aux_head(pooled, aux, labels, pix, groups, before):
+def aux_head(pooled, aux, labels, pix, groups):
     images, head = pooled.shape[0], aux.shape[1]
     return call(
         functools.partial(head_kernel, pix),
         [shape((images, head), F32), shape((groups, images, head + 2 * LANES), BF16)],
         limit=16,
-        in_specs=[VMEM, VMEM, SMEM, *[ANY] * len(before)],
+        in_specs=[VMEM, VMEM, SMEM],
         name="aux_head",
-    )(pooled, aux, labels, *before)
-
-
-def recon_kernel(feature_ref, decode_ref, _, recon_ref, token_ref):
-    token_ref[...] = jnp.zeros(token_ref.shape, F32)
+    )(pooled, aux, labels)
+
+
+def recon_kernel(feature_ref, decode_ref, recon_ref):
     feature = feature_ref[...]
     for at in range(0, recon_ref.shape[1], TILE):
         cut = slice(at, at + TILE)
         recon_ref[:, cut] = dot(feature, decode_ref[:, cut])
 
 
-def reconstruct(feature, decode, before):
+def reconstruct(feature, decode):
     rows, width = feature.shape
     n = decode.shape[1]
     block = lambda m: pl.BlockSpec((rows // STEPS, m), lambda g: (g, 0))
     return call(
         recon_kernel,
-        [shape((rows, n), F32), shape(TOKEN, F32)],
-        limit=58,
+        shape((rows, n), F32),
+        limit=57,
         flops=2 * rows * width * n,
         moved=rows * (2 * width + 4 * n),
         grid=(STEPS,),
-        in_specs=[block(width), pl.BlockSpec(decode.shape, lambda g: (0, 0)), ANY],
-        out_specs=[block(n), pl.BlockSpec(TOKEN, lambda g: (0, 0))],
+        in_specs=[block(width), pl.BlockSpec(decode.shape, lambda g: (0, 0))],
+        out_specs=block(n),
         name="reconstruct",
-    )(feature, decode, before)
+    )(feature, decode)
 
 
 def own_index(h):
@@ -235,7 +236,6 @@
     pairs = [refs[j : j + 2] for j in range(0, len(refs), 2)]
     own, shared = pairs[: len(pairs) // 2], pairs[len(pairs) // 2 :]
     per_half = STEPS // 2
-    even_first = where_ref[PARITY] == 0
     lanes = lambda j: pl.ds(pl.multiple_of(where_ref[TILES + j] * LANES, LANES), LANES)
     for h in range(2):
 
@@ -244,20 +244,19 @@
             for k, pair in enumerate(own):
                 target[:, :, lanes(2 * k)] = pair[h][...]
 
-    turn = lambda v: jnp.concatenate([v[:, :, 64:], v[:, :, :64]], axis=2)
     for g in range(STEPS):
-
-        @pl.when(step == g)
-        def _():
-            h, side = g // per_half, g % per_half
-            for k in range(0, len(shared), 2):
-                mine, other = shared[k][h][...].astype(F32), shared[k + 1][h][...].astype(F32)
-                even = jnp.where(even_first, mine, other)
-                odd = jnp.where(even_first, other, mine)
-                lane = lax.broadcasted_iota(jnp.int32, even.shape, 2)
-                low = turn(even) if side else even
-                high = odd if side else turn(odd)
-                target[:, :, lanes(2 * k + 1)] = jnp.where(lane < 64, low, high).astype(BF16)
+        for parity in range(2):
+
+            @pl.when((step == g) & (where_ref[PARITY] == parity))
+            def _():
+                h, side = g // per_half, g % per_half
+                for k in range(0, len(shared), 2):
+                    even, odd = shared[k + parity][h][...].astype(F32), shared[k + 1 - parity][h][...].astype(F32)
+                    lane = lax.broadcasted_iota(jnp.int32, even.shape, 2)
+                    value = jnp.where((lane < 64) == (side == 0), even, odd)
+                    if side:
+                        value = jnp.concatenate([value[:, :, 64:], value[:, :, :64]], axis=2)
+                    target[:, :, lanes(2 * k + 1)] = value.astype(BF16)
 
 
 def deal(where_ref, sums, part, keep_ref, send_ref):
@@ -327,7 +326,7 @@
 
 def residual_kernel(groups, scale, n_patch, where_ref, feature_ref, recon_ref, *refs):
     patch_refs, refs = refs[:n_patch], refs[n_patch:]
-    _, grad_ref, keep_ref, send_ref, target, feature, grads, total, sems = refs
+    grad_ref, keep_ref, send_ref, target, feature, grads, total, sems = refs
     step = pl.program_id(0)
     rows, width = feature.shape
     size = grad_ref.shape[0]
@@ -343,7 +342,7 @@
         deal(where_ref, [total], width // groups, keep_ref, send_ref)
 
 
-def residual(where, feature, recon, patch_args, patch_specs, before, images, scale, groups):
+def residual(where, feature, recon, patch_args, patch_specs, images, scale, groups):
     rows, width = feature.shape
     n = recon.shape[1]
     size = rows // STEPS
@@ -353,13 +352,13 @@
     return call(
         functools.partial(residual_kernel, groups, scale, len(patch_args)),
         [shape((rows, n), BF16), shape(parts, BF16), shape(parts, BF16)],
-        limit=58,
+        limit=48,
         flops=2 * rows * width * n,
         moved=rows * (2 * width + 6 * n),
         grid_spec=pltpu.PrefetchScalarGridSpec(
             num_scalar_prefetch=1,
             grid=(STEPS,),
-            in_specs=[HBM, block, *patch_specs, ANY],
+            in_specs=[HBM, block, *patch_specs],
             out_specs=[block, dealt, dealt],
             scratch_shapes=[
                 pltpu.VMEM((size // images, images, n), BF16),
@@ -370,11 +369,11 @@
             ],
         ),
         name="residual",
-    )(where, feature, recon, *patch_args, before)
+    )(where, feature, recon, *patch_args)
 
 
 def backward_kernel(
-    groups, where_ref, grad_ref, hidden_ref, acts_ref, decode_ref, pooled_ref, second_ref, _,
+    groups, where_ref, grad_ref, hidden_ref, acts_ref, decode_ref, pooled_ref, second_ref,
     keep_ref, send_ref, hidden, acts, feature_grads, hidden_grads, total_second, total_first, sems,
 ):
     step = pl.program_id(0)
@@ -409,7 +408,7 @@
         deal(where_ref, [second, total_first], part, keep_ref, send_ref)
 
 
-def backward(where, grad, hidden, acts, decode, pooled, second, before, groups):
+def backward(where, grad, hidden, acts, decode, pooled, second, groups):
     rows, width = acts.shape
     inner, n = hidden.shape[1], grad.shape[1]
     size = rows // STEPS
@@ -419,7 +418,7 @@
     return call(
         functools.partial(backward_kernel, groups),
         [shape(parts, BF16), shape(parts, BF16)],
-        limit=58,
+        limit=44,
         flops=2 * rows * width * (n + 3 * inner),
         moved=2 * rows * (width + n + inner),
         grid_spec=pltpu.PrefetchScalarGridSpec(
@@ -432,7 +431,6 @@
                 whole(decode),
                 whole(pooled),
                 whole(second),
-                ANY,
             ],
             out_specs=[dealt, dealt],
             scratch_shapes=[
@@ -446,7 +444,7 @@
             ],
         ),
         name="backward",
-    )(where, grad, hidden, acts, decode, pooled, second, before)
+    )(where, grad, hidden, acts, decode, pooled, second)
 
 
 TOPS, DENOMS = 3, 19
@@ -473,7 +471,7 @@
     return (digits[:, 0:1] * LANES + digits[:, 1:2]).astype(jnp.int32)
 
 
-def logits_kernel(where_ref, got_ref, klass_ref, _, logits_ref, sent_ref):
+def logits_kernel(where_ref, got_ref, klass_ref, logits_ref, sent_ref):
     groups, images, _ = got_ref.shape
     classes, head = klass_ref.shape
     got = got_ref[...].reshape(groups * images, -1)
@@ -500,16 +498,16 @@
         sent_ref[d, :, 2 * head :] = to_digits(jnp.where(lane == 0, cut(top, d), stats))
 
 
-def class_logits(where, got, klass, before):
+def class_logits(where, got, klass):
     groups, images, _ = got.shape
     classes, head = klass.shape
     return call(
         logits_kernel,
         [shape((groups * images, classes), F32), shape((groups, images, 2 * head + LANES), BF16)],
         limit=16,
-        in_specs=[SMEM, VMEM, VMEM, ANY],
+        in_specs=[SMEM, VMEM, VMEM],
         name="class_logits",
-    )(where, got, klass, before)
+    )(where, got, klass)
 
 
 def aux_kernel(pix, norm, got_ref, aux_pre_ref, aux_ref, pooled_ref, grad_ref):
@@ -538,11 +536,13 @@
         functools.partial(aux_kernel, pix, norm),
         [shape((images, width), F32), shape((images * head // part, part), BF16)],
         limit=16,
+        flops=2e10,
         name="aux_backward",
     )(got, aux_pre, aux)
 
 
-def class_kernel(norm, n, where_ref, logits_ref, got_ref, stats_ref, grads_ref, class_ref, aux_ref):
+def class_kernel(norm, n, where_ref, logits_ref, got_ref, stats_ref, *refs):
+    grads_refs, (class_ref, aux_ref) = refs[:-2], refs[-2:]
     groups, images, _ = got_ref.shape
     head = class_ref.shape[1]
     classes, part = class_ref.shape[0], aux_ref.shape[0]
@@ -561,11 +561,12 @@
     class_ref[...] = dot(logit_grad, got[:, :head], ROWS_0)
     total = jnp.zeros(aux_ref.shape, F32)
     for d in range(groups):
-        at = n + d % 2 * (head // part) * images
+        k, core = d // 2, d % 2
+        at = n + core * (head // part) * images
         grad = jnp.concatenate(
-            [grads_ref[d // 2, at + q * images : at + (q + 1) * images, :] for q in range(head // part)], axis=1
+            [grads_refs[k][at + q * images : at + (q + 1) * images, :] for q in range(head // part)], axis=1
         )
-        pooled = got_ref[d, :, head : head + part]
+        pooled = got_ref[((where_ref[ME] >> 1) ^ k) * 2 + core, :, head : head + part]
         total += dot(pooled, grad, ROWS_0).astype(BF16).astype(F32)
     aux_ref[...] = total
 
@@ -573,7 +574,7 @@
 def class_backward(where, logits, got, partial, grads, n_decode, classes, head, norm):
     groups, images, wide = partial.shape
     whole = lambda *dims: pl.BlockSpec(dims, lambda i: (0,) * len(dims))
-    part = grads.shape[2]
+    part = grads[0].shape[1]
     return call(
         functools.partial(class_kernel, norm, n_decode),
         [shape((classes, head), F32), shape((part, head), F32)],
@@ -586,65 +587,65 @@
             whole(*logits.shape),
             whole(*got.shape),
             pl.BlockSpec((groups, images, LANES), lambda i: (0, 0, wide // LANES - 1)),
-            whole(*grads.shape),
+            *[whole(*g.shape) for g in grads],
         ],
         out_specs=[whole(classes, head), whole(part, head)],
         name="class_backward",
-    )(where, logits, got, partial, grads)
-
-
-def chip_kernel(has_extra, where_ref, keep_ref, got_ref, *refs):
-    out_ref, token_ref = refs[-2:]
-    token_ref[...] = jnp.zeros(token_ref.shape, F32)
+    )(where, logits, got, partial, *grads)
+
+
+def chip_kernel(n_extra, where_ref, keep_ref, got_ref, *refs):
+    extra, outs = refs[:n_extra], refs[n_extra:]
     n = keep_ref.shape[1]
-    out_ref[:, :n, :] = (keep_ref[...].astype(F32) + got_ref[...].astype(F32)).astype(BF16)
-    if has_extra:
-        mine, other = refs[0][...].astype(F32), refs[1][...].astype(F32)
+    chip = where_ref[ME] >> 1
+    for k, out_ref in enumerate(outs):
+        out_ref[:n] = (keep_ref[chip ^ k].astype(F32) + got_ref[chip ^ k].astype(F32)).astype(BF16)
+    if n_extra:
+        mine, other = extra[0][...].astype(F32), extra[1][...].astype(F32)
         even = where_ref[CORE] == 0
         pair = [jnp.where(even, mine, other).astype(BF16), jnp.where(even, other, mine).astype(BF16)]
         size = mine.shape[0]
-        for z in range(out_ref.shape[0]):
+        for out_ref in outs:
             for c in range(2):
-                out_ref[z, n + c * size : n + (c + 1) * size, :] = pair[c]
-
-
-def add_cores(where, keep, send, extra=(), before=()):
+                out_ref[n + c * size : n + (c + 1) * size] = pair[c]
+
+
+def add_cores(where, keep, send, extra=()):
     chips, n, part = keep.shape
     extra = [e for own in extra for e in (own, swap(own, "dp", 1))]
     rows = n + sum(e.shape[0] for e in extra)
     return call(
-        functools.partial(chip_kernel, len(extra) > 0),
-        [shape((chips, rows, part), BF16), shape(TOKEN, F32)],
+        functools.partial(chip_kernel, len(extra)),
+        [shape((rows, part), BF16)] * chips,
         limit=16,
-        in_specs=[SMEM, VMEM, VMEM, *[VMEM] * len(extra), *[ANY] * len(before)],
+        in_specs=[SMEM, VMEM, VMEM, *[VMEM] * len(extra)],
         name="add_cores",
-    )(where, keep, swap(send, "dp", 1), *extra, *before)
+    )(where, keep, swap(send, "dp", 1), *extra)
 
 
 def exchange_chips(parts):
-    count = lax.axis_size("dp")
-    return exchange(parts, [[z + core for z in range(0, count, 2)] for core in range(2)])
-
-
-def finish_kernel(inner, early_ref, last_ref, first_ref, second_ref, decode_ref):
-    chips, _, part = early_ref.shape
+    return [parts[0]] + [swap(part, "dp", 2 * k) for k, part in enumerate(parts) if k]
+
+
+def finish_kernel(inner, chips, *refs):
+    early, last, (first_ref, second_ref, decode_ref) = refs[:chips], refs[chips : 2 * chips], refs[2 * chips :]
     n = decode_ref.shape[1]
-    last = sum(last_ref[z].astype(F32) for z in range(chips))
-    first_ref[...] = last[inner:].T
-    tall = second_ref.shape[0]
+    total = sum(ref[...].astype(F32) for ref in last)
+    first_ref[...] = total[inner:].T
+    tall, part = second_ref.shape[0], total.shape[1]
     for q in range(inner // tall):
-        second_ref[:, q * part : (q + 1) * part] = last[q * tall : (q + 1) * tall]
-    decode_ref[...] = sum(early_ref[z, :n].astype(F32) for z in range(chips)).T
+        second_ref[:, q * part : (q + 1) * part] = total[q * tall : (q + 1) * tall]
+    decode_ref[...] = sum(ref[:n].astype(F32) for ref in early).T
 
 
 def finish(early, last, inner, groups, n):
-    part = early.shape[2]
-    return call(
-        functools.partial(finish_kernel, inner),
+    part = early[0].shape[1]
+    return call(
+        functools.partial(finish_kernel, inner, len(early)),
         [shape((part, inner), F32), shape((inner // groups, part * groups), F32), shape((part, n), F32)],
         limit=16,
         name="finish",
-    )(early, last)
+    )(*early, *last)
 
 
 def local(acts, patches, labels, w_first, w_second, w_decode, w_aux, w_class):
@@ -665,39 +666,37 @@
         tiles = [t for s in near for t in (3 * (s >> 1) + 2 * (s & 1), 3 * (s >> 1) + 1)]
         where = jnp.stack([section & 1, me & 1, me, *tiles]).astype(jnp.int32)
         turned = patches.transpose(0, 2, 1)
-        packed = [pack(where, turned, h) for h in range(2)]
-        before_forward = [packed[1][1]]
-        halves = [half for half, _ in packed]
+        halves = [pack(where, turned, h) for h in range(2)]
         x, y = [swap(halves[0], "section", 1)], [swap(halves[0], "section", 2)]
-        before_head = [x[0], y[0]]
+        first = after(first, halves[1])
+        labels = after(labels, (x[0], y[0]))
     else:
         where = jnp.stack([section & 1, me & 1, me]).astype(jnp.int32)
-        before_forward = before_head = []
         target = lax.all_gather(patches, "section", axis=2, tiled=True).transpose(1, 0, 2)
 
-    hidden, feature, pooled = forward(acts, first, second, before_forward)
-    aux_pre, sent = aux_head(pooled, aux, labels, pix, groups, before_head)
+    hidden, feature, pooled = forward(acts, first, second)
+    aux_pre, sent = aux_head(pooled, aux, labels, pix, groups)
     got = exchange(sent)
+    recon = reconstruct(after(feature, sent), decode)
     if paired:
         last = after(halves[1], pooled)
         x.append(swap(last, "section", 1))
         y.append(swap(last, "section", 2))
-        diagonal = [swap(after(y[0], aux_pre), "section", 1), swap(after(x[1], aux_pre), "section", 2)]
+        diagonal = [swap(after(y[0], aux_pre), "section", 1), swap(after(x[1], recon), "section", 2)]
         blocks = [halves, x, y, diagonal]
         target = patch_operands(blocks, [0, 1, 2, 3], [0, 1, 2, 3])
     else:
         target = [target], [pl.BlockSpec((pix // STEPS, images, n_decode), lambda g, where: (g, 0, 0))]
-    recon, token = reconstruct(feature, decode, sent)
-    logits, sent = class_logits(where, got, klass, token)
+    logits, sent = class_logits(where, after(got, recon), klass)
     partial = exchange(sent)
-    grad, keep, send = residual(where, feature, recon, *target, sent, images, scale, groups)
+    grad, keep, send = residual(after(where, sent), feature, recon, *target, images, scale, groups)
     pooled_grad, aux_grad = aux_backward(partial, aux_pre, aux, pix, norm)
-    chip_decode, token = add_cores(where, keep, send, [aux_grad])
+    chip_decode = add_cores(where, keep, send, [aux_grad])
     sum_decode = exchange_chips(chip_decode)
     keep, send = backward(
-        where, grad, hidden, acts.reshape(rows, width), decode, pooled_grad, second, token, groups
+        where, grad, hidden, acts.reshape(rows, width), decode, after(pooled_grad, chip_decode[0]), second, groups
     )
-    sum_last = exchange_chips(add_cores(where, keep, send, before=[sum_decode])[0])
+    sum_last = exchange_chips(add_cores(where, keep, after(send, sum_decode)))
     grad_class, grad_aux = class_backward(
         where, logits, got, partial, sum_decode, n_decode, klass.shape[0], head, norm
     )

time: 146 us -> 121 us (0.83)
  waiting for transfers between devices: 28.2 us -> 13.4 us
  Pallas kernels: 71.1 us -> 63.7 us
  local copies, waits for them, and re-layouts: 10.1 us -> 6.08 us
  starting transfers between devices: 20.5 us -> 23.3 us
  blocking collectives: 15 us -> 13 us
    all_to_all x3 -> x1, waiting for transfers between devices: 13.3 us -> 0.01 us  [exchange(): lax.all_to_all(value, 'dp', 0, 0, axis_index_groups=groups, tiled=True)]
    ppermute x9 -> x15, starting transfers between devices: 8.42 us -> 19.7 us  [swap(): return lax.ppermute(value, axis, [(i, i ^ bits) for i in range(count)])]
    all_to_all x3 -> x1, starting transfers between devices: 12.1 us -> 3.6 us  [exchange(): lax.all_to_all(value, 'dp', 0, 0, axis_index_groups=groups, tiled=True)]
    unnamed x44 -> x30, local copies, waits for them, and re-layouts: 9.98 us -> 5.99 us
    pallas_call x1, Pallas kernels: 18.7 us -> 15.2 us  [backward(): call(functools.partial(backward_kernel, groups), [shape(parts, BF16), sha...]
    all_to_all x1, blocking collectives: 15 us -> 13 us  [exchange(): lax.all_to_all(value, 'dp', 0, 0, axis_index_groups=groups, tiled=True)]
    pallas_call x1, Pallas kernels: 16.3 us -> 14.7 us  [residual(): call(functools.partial(residual_kernel, groups, scale, len(patch_args)),...]
    ppermute x9 -> x15, waiting for transfers between devices: 14.8 us -> 13.4 us  [swap(): return lax.ppermute(value, axis, [(i, i ^ bits) for i in range(count)])]
  transfers between devices with their start and end apart: 12 -> 16, of which waited for: 5 -> 5; matrix products, arithmetic and copies ran while one was open for 0% -> 0% of each run, Pallas kernels for 34% -> 49%
where the time goes in v6:
time: 121 us; the launch traced here: 120 us
  Pallas kernels  63.7 us (53%)
  starting transfers between devices  23.3 us (19%)
  waiting for transfers between devices  13.4 us (11%)
  blocking collectives  13 us (11%)
  local copies, waits for them, and re-layouts  6.08 us (5%)
    ppermute x15, starting transfers between devices, swap(): return lax.ppermute(value, axis, [(i, i ^ bits) for i in range(count)])  19.7 us
    pallas_call x1, Pallas kernels, backward(): call(functools.partial(backward_kernel, groups), [shape(parts, BF16), sha...  15.2 us
    pallas_call x1, Pallas kernels, residual(): call(functools.partial(residual_kernel, groups, scale, len(patch_args)),...  14.7 us
    ppermute x15, waiting for transfers between devices, swap(): return lax.ppermute(value, axis, [(i, i ^ bits) for i in range(count)])  13.4 us
    all_to_all x1, blocking collectives, exchange(): lax.all_to_all(value, 'dp', 0, 0, axis_index_groups=groups, tiled=True)  13 us
    pallas_call x1, Pallas kernels, forward(): call(forward_kernel, [shape((pix * images, inner), BF16), shape((pix * im...  11.1 us
    pallas_call x1, Pallas kernels, reconstruct(): call(recon_kernel, shape((rows, n), F32), limit=57, flops=2 * rows * widt...  10.2 us
    unnamed x30, local copies, waits for them, and re-layouts  5.99 us
  transfers between devices with their start and end apart: 16, of which 5 were waited for; matrix products, arithmetic and copies ran while one was open for 0% of the time, Pallas kernels for 49%

profile of v6, /device:TPU:0, one launch (start us, length us, event | category | flops | bytes accessed | tf_op | source)
XLA Modules:
  0.0 120.4 jit_solution(2448524424911596530)
XLA Ops:
  0.7 0.1 stack.47.where_ref
  0.7 1.4 %copy-done = bf16[16,196,192]{1,2,0:T(8,128)(2,1)S(1)} copy-done((bf16[16,196,192]{1,2,0:T(8,128)(2,1)S(1)}, bf16[16,196,192]{1,2,0:T(8,128)(2,1)}, u32[]{:S(2)}) %copy-start) | copy-done | bytes 1204248
  2.2 1.8 %pack_patches.3.refs_0_.refs_8_ = bf16[147,16,128]{2,1,0:T(8,128)(2,1)S(1)} custom-call(s32[11]{0:T(128)S(1)} %stack.47.where_ref, bf16[16,192,196]{2,1,0:T(8,128)(2,1)S(1)} %bitcast.27), custom_call_target="tpu_custom_call" | custom-call | tf_op jit(solution)/shard_map/pack_patches/pallas_call | solution.py:92
  4.0 3.0 %collective-permute-start.1 = (bf16[147,16,128]{2,1,0:T(8,128)(2,1)S(1)}, bf16[147,16,128]{2,1,0:T(8,128)(2,1)S(1)}, u32[]{:S(2)}, u32[]{:S(2)}) collective-permute-start(bf16[147,16,128]{2,1,0:T(8,128)(2,1)S(1)} %pack_patches.3.refs_0_.refs_8_), channel_id=1, source_target_pairs={{0,16},{8,24},{16,0},{24,8},{1,17},{9,25},{17,1},{25,9},{2,18},{10... | collective-permute-start | bytes 1806344 | tf_op jit(solution)/shard_map/ppermute | solution.py:46
  7.0 1.5 %collective-permute-start = (bf16[147,16,128]{2,1,0:T(8,128)(2,1)S(1)}, bf16[147,16,128]{2,1,0:T(8,128)(2,1)S(1)}, u32[]{:S(2)}, u32[]{:S(2)}) collective-permute-start(bf16[147,16,128]{2,1,0:T(8,128)(2,1)S(1)} %pack_patches.3.refs_0_.refs_8_), channel_id=1, source_target_pairs={{0,8},{8,0},{16,24},{24,16},{1,9},{9,1},{17,25},{25,17},{2,10},{10... | collective-permute-start | bytes 1806344 | tf_op jit(solution)/shard_map/ppermute | solution.py:46
  8.5 1.8 %pack_patches.2.refs_1_.refs_9_ = bf16[147,16,128]{2,1,0:T(8,128)(2,1)S(1)} custom-call(s32[11]{0:T(128)S(1)} %stack.47.where_ref, bf16[16,192,196]{2,1,0:T(8,128)(2,1)S(1)} %bitcast.28), custom_call_target="tpu_custom_call" | custom-call | tf_op jit(solution)/shard_map/pack_patches/pallas_call | solution.py:92
  10.3 0.0 copy-start.2
  10.3 0.0 copy-start.10
  10.4 11.1 %forward.1 = (bf16[3136,256]{1,0:T(8,128)(2,1)}, bf16[3136,1024]{1,0:T(8,128)(2,1)}, f32[16,1024]{1,0:T(8,128)}) custom-call(bf16[196,16,1024]{2,1,0:T(8,128)(2,1)} %bitcast.36, bf16[1024,256]{1,0:T(8,128)(2,1)} %bitcast.39, bf16[256,1024]{1,0:T(8,128)(2,1)} %bitcast.34), custom_call_target="tpu_custom_call" | custom-call | flops 3288334336 | bytes 14450688 | tf_op jit(solution)/shard_map/forward/pallas_call | solution.py:134
  21.4 0.6 collective-permute-start.2
  22.0 0.1 collective-permute-start.3
  22.1 0.0 copy-start.9
  22.1 0.8 copy-done.9
  22.9 0.8 aux_head.1
  23.7 2.0 %collective-permute-start.4 = (bf16[147,16,128]{2,1,0:T(8,128)(2,1)S(1)}, bf16[147,16,128]{2,1,0:T(8,128)(2,1)}, u32[]{:S(2)}, u32[]{:S(2)}) collective-permute-start(bf16[147,16,128]{2,1,0:T(8,128)(2,1)S(1)} %collective-permute-done.1.refs_4_.refs_12_), channel_id=1, source_target_pairs={{0,8},{8,0},{16,24},{24,16},{1,9},{9,1},{17,25},{25,17},{2,10},{10... | collective-permute-start | bytes 1806344 | tf_op jit(solution)/shard_map/ppermute | solution.py:46
  25.7 10.2 %reconstruct.1.recon_ref = f32[3136,768]{1,0:T(8,128)} custom-call(bf16[3136,1024]{1,0:T(8,128)(2,1)} %get-tuple-element.47.feature_ref, bf16[1024,768]{1,0:T(8,128)(2,1)} %bitcast.32), custom_call_target="tpu_custom_call" | custom-call | flops 4932501504 | bytes 16056320 | tf_op jit(solution)/shard_map/reconstruct/pallas_call | solution.py:199
  35.9 2.1 %collective-permute-done.2.refs_3_.refs_11_ = bf16[147,16,128]{2,1,0:T(8,128)(2,1)S(1)} collective-permute-done((bf16[147,16,128]{2,1,0:T(8,128)(2,1)S(1)}, bf16[147,16,128]{2,1,0:T(8,128)(2,1)S(1)}, u32[]{:S(2)}, u32[]{:S(2)}) %collective-permute-start.2) | collective-permute-done | bytes 602144 | tf_op jit(solution)/shard_map/ppermute | solution.py:46
  38.0 0.5 collective-permute-start.5
  38.5 13.0 %all_to_all.10.got_ref = bf16[8,16,768]{2,1,0:T(8,128)(2,1)S(1)} all-to-all(bf16[8,16,768]{2,1,0:T(8,128)(2,1)S(1)} %get-tuple-element.45), channel_id=1, replica_groups=mesh['section'=4,'dp'=8] {'dp'}, dimensions={0} | all-to-all | bytes 393216 | tf_op jit(solution)/shard_map/all_to_all | solution.py:50
  51.5 2.0 %class_logits.1 = (f32[128,1408]{1,0:T(8,128)S(1)}, bf16[8,16,1152]{2,1,0:T(8,128)(2,1)S(1)}) custom-call(s32[11]{0:T(128)S(1)} %stack.47.where_ref, bf16[8,16,768]{2,1,0:T(8,128)(2,1)S(1)} %all_to_all.10.got_ref, bf16[1408,512]{1,0:T(8,128)(2,1)S(1)} %bitcast.29), custom_call_target="tpu_custom_call" | custom-call | tf_op jit(solution)/shard_map/class_logits/pallas_call | solution.py:504
  53.5 0.9 copy-done.6
  54.4 0.7 copy-done.8
  55.1 3.6 %all-to-all-start.1 = ((bf16[8,16,1152]{2,1,0:T(8,128)(2,1)}), bf16[8,16,1152]{2,1,0:T(8,128)(2,1)S(1)}, u32[]{:S(2)}, u32[]{:S(2)}) async-start(bf16[8,16,1152]{2,1,0:T(8,128)(2,1)} %copy-done.8), calls=%async_computation.1 | async-start | bytes 589824 | tf_op jit(solution)/shard_map/all_to_all | solution.py:50
  58.7 0.0 collective-permute-done.5.refs_7_.refs_15_
  58.7 14.7 %residual.1 = (bf16[3136,768]{1,0:T(8,128)(2,1)}, bf16[4,768,128]{2,1,0:T(8,128)(2,1)S(1)}, bf16[4,768,128]{2,1,0:T(8,128)(2,1)}) custom-call(s32[11]{0:T(128)S(1)} %stack.47.where_ref, bf16[3136,1024]{1,0:T(8,128)(2,1)} %get-tuple-element.47.feature_ref, f32[3136,768]{1,0:T(8,128)} %reconstruct.1.recon_ref, ...), custom_call_target="tpu_custom_call" | custom-call | flops 4932501504 | bytes 20873216 | tf_op jit(solution)/shard_map/residual/pallas_call | solution.py:352
  73.4 0.9 copy-done.4
  74.3 0.2 collective-permute-start.6
  74.5 1.2 %copy-done.3 = bf16[1,1024,512]{2,1,0:T(8,128)(2,1)S(1)} copy-done((bf16[1,1024,512]{2,1,0:T(8,128)(2,1)S(1)}, bf16[1,1024,512]{2,1,0:T(8,128)(2,1)}, u32[]{:S(2)}) %copy-start.3) | copy-done | bytes 1048600
  75.7 0.0 copy-start.14
  75.7 0.6 aux_backward.1
  76.4 0.3 collective-permute-start.7
  76.7 0.9 collective-permute-done.7.refs_1_
  77.6 0.0 collective-permute-done.6.got_ref
  77.6 0.7 add_cores.2
  78.3 1.7 %collective-permute-start.8 = (bf16[896,128]{1,0:T(8,128)(2,1)S(1)}, bf16[896,128]{1,0:T(8,128)(2,1)S(1)}, u32[]{:S(2)}, u32[]{:S(2)}) collective-permute-start(bf16[896,128]{1,0:T(8,128)(2,1)S(1)} %get-tuple-element.59), channel_id=1, source_target_pairs={{0,2},{1,3},{2,0},{3,1},{4,6},{5,7},{6,4},{7,5},{8,10},{9,11},{10,... | collective-permute-start | bytes 688136 | tf_op jit(solution)/shard_map/ppermute | solution.py:46
  80.1 2.4 %collective-permute-start.9 = (bf16[896,128]{1,0:T(8,128)(2,1)S(1)}, bf16[896,128]{1,0:T(8,128)(2,1)S(1)}, u32[]{:S(2)}, u32[]{:S(2)}) collective-permute-start(bf16[896,128]{1,0:T(8,128)(2,1)S(1)} %get-tuple-element.60), channel_id=1, source_target_pairs={{0,4},{1,5},{2,6},{3,7},{4,0},{5,1},{6,2},{7,3},{8,12},{9,13},{10,... | collective-permute-start | bytes 688136 | tf_op jit(solution)/shard_map/ppermute | solution.py:46
  82.5 0.3 collective-permute-start.10
  82.8 15.2 %backward.1 = (bf16[4,512,128]{2,1,0:T(8,128)(2,1)S(1)}, bf16[4,512,128]{2,1,0:T(8,128)(2,1)S(1)}) custom-call(s32[11]{0:T(128)S(1)} %stack.47.where_ref, bf16[3136,768]{1,0:T(8,128)(2,1)S(1)} %copy-done.11, bf16[3136,256]{1,0:T(8,128)(2,1)S(1)} %copy-done.14, bf16[3136,1024]{1,0:T(8,128)(2,1)} %bitcast.37, bf16[1024,768]{1,0:T(8,128)(2,1)S(1)} %bitcast.33, ...), custom_call_target="tpu_custom_call" | custom-call | flops 9865003008 | bytes 12845056 | tf_op jit(solution)/shard_map/backward/pallas_call | solution.py:418
  98.1 1.2 %collective-permute-done.9.refs_2_ = bf16[896,128]{1,0:T(8,128)(2,1)S(1)} collective-permute-done((bf16[896,128]{1,0:T(8,128)(2,1)S(1)}, bf16[896,128]{1,0:T(8,128)(2,1)S(1)}, u32[]{:S(2)}, u32[]{:S(2)}) %collective-permute-start.9) | collective-permute-done | bytes 229408 | tf_op jit(solution)/shard_map/ppermute | solution.py:46
  99.3 0.0 collective-permute-done.10.refs_3_
  99.3 1.9 %collective-permute-done.11.got_ref = bf16[4,512,128]{2,1,0:T(8,128)(2,1)S(1)} collective-permute-done((bf16[4,512,128]{2,1,0:T(8,128)(2,1)S(1)}, bf16[4,512,128]{2,1,0:T(8,128)(2,1)S(1)}, u32[]{:S(2)}, u32[]{:S(2)}) %collective-permute-start.11) | collective-permute-done | bytes 524320 | tf_op jit(solution)/shard_map/ppermute | solution.py:46
  101.2 0.7 add_cores.3
  101.9 4.7 %collective-permute-start.12 = (bf16[512,128]{1,0:T(8,128)(2,1)S(1)}, bf16[512,128]{1,0:T(8,128)(2,1)S(1)}, u32[]{:S(2)}, u32[]{:S(2)}) collective-permute-start(bf16[512,128]{1,0:T(8,128)(2,1)S(1)} %get-tuple-element.70), channel_id=1, source_target_pairs={{0,2},{1,3},{2,0},{3,1},{4,6},{5,7},{6,4},{7,5},{8,10},{9,11},{10,... | collective-permute-start | bytes 393224 | tf_op jit(solution)/shard_map/ppermute | solution.py:46
  106.6 1.0 collective-permute-start.13
  107.5 1.4 %collective-permute-start.14 = (bf16[512,128]{1,0:T(8,128)(2,1)S(1)}, bf16[512,128]{1,0:T(8,128)(2,1)S(1)}, u32[]{:S(2)}, u32[]{:S(2)}) collective-permute-start(bf16[512,128]{1,0:T(8,128)(2,1)S(1)} %get-tuple-element.72), channel_id=1, source_target_pairs={{0,6},{1,7},{2,4},{3,5},{4,2},{5,3},{6,0},{7,1},{8,14},{9,15},{10,... | collective-permute-start | bytes 393224 | tf_op jit(solution)/shard_map/ppermute | solution.py:46
  109.0 3.2 %class_backward.1 = (f32[1408,512]{1,0:T(8,128)}, f32[128,512]{1,0:T(8,128)}) custom-call(s32[11]{0:T(128)S(1)} %stack.47.where_ref, f32[128,1408]{1,0:T(8,128)S(1)} %copy-done.7, bf16[8,16,768]{2,1,0:T(8,128)(2,1)S(1)} %all_to_all.10.got_ref, bf16[8,16,1152]{2,1,0:T(8,128)(2,1)S(1)} %all-to-all-done.1.got_ref.stats_ref, ...), custom_call_target="tpu_custom_call" | custom-call | flops 184549376 | bytes 2883584 | tf_op jit(solution)/shard_map/class_backward/pallas_call | solution.py:578
  112.2 7.2 %collective-permute-done.13.refs_6_ = bf16[512,128]{1,0:T(8,128)(2,1)S(1)} collective-permute-done((bf16[512,128]{1,0:T(8,128)(2,1)S(1)}, bf16[512,128]{1,0:T(8,128)(2,1)S(1)}, u32[]{:S(2)}, u32[]{:S(2)}) %collective-permute-start.13) | collective-permute-done | bytes 131104 | tf_op jit(solution)/shard_map/ppermute | solution.py:46
  119.5 1.0 finish.1
  (29 shorter events, 0.1 us)
Async XLA Ops:
  0.7 1.4 %copy-start = (bf16[16,196,192]{1,2,0:T(8,128)(2,1)S(1)}, bf16[16,196,192]{1,2,0:T(8,128)(2,1)}, u32[]{:S(2)}) copy-start(bf16[16,196,192]{1,2,0:T(8,128)(2,1)} %param.9) | copy-start | bytes 3612676
  4.0 18.1 %collective-permute-start.1 = (bf16[147,16,128]{2,1,0:T(8,128)(2,1)S(1)}, bf16[147,16,128]{2,1,0:T(8,128)(2,1)S(1)}, u32[]{:S(2)}, u32[]{:S(2)}) collective-permute-start(bf16[147,16,128]{2,1,0:T(8,128)(2,1)S(1)} %pack_patches.3.refs_0_.refs_8_), channel_id=1, source_target_pairs={{0,16},{8,24},{16,0},{24,8},{1,17},{9,25},{17,1},{25,9},{2,18},{10... | collective-permute-start | bytes 1806344 | tf_op jit(solution)/shard_map/ppermute | solution.py:46
  7.0 15.1 %collective-permute-start = (bf16[147,16,128]{2,1,0:T(8,128)(2,1)S(1)}, bf16[147,16,128]{2,1,0:T(8,128)(2,1)S(1)}, u32[]{:S(2)}, u32[]{:S(2)}) collective-permute-start(bf16[147,16,128]{2,1,0:T(8,128)(2,1)S(1)} %pack_patches.3.refs_0_.refs_8_), channel_id=1, source_target_pairs={{0,8},{8,0},{16,24},{24,16},{1,9},{9,1},{17,25},{25,17},{2,10},{10... | collective-permute-start | bytes 1806344 | tf_op jit(solution)/shard_map/ppermute | solution.py:46
  10.3 11.7 %copy-start.2 = (bf16[1,1024,512]{2,1,0:T(8,128)(2,1)S(1)}, bf16[1,1024,512]{2,1,0:T(8,128)(2,1)}, u32[]{:S(2)}) copy-start(bf16[1,1024,512]{2,1,0:T(8,128)(2,1)} %param.14) | copy-start | bytes 3145732
  10.3 11.7 %copy-start.10 = (s32[16]{0:T(128)S(1)}, s32[16]{0:T(128)}, u32[]{:S(2)}) copy-start(s32[16]{0:T(128)} %labels_ref) | copy-start | bytes 196
  21.4 16.6 %collective-permute-start.2 = (bf16[147,16,128]{2,1,0:T(8,128)(2,1)S(1)}, bf16[147,16,128]{2,1,0:T(8,128)(2,1)S(1)}, u32[]{:S(2)}, u32[]{:S(2)}) collective-permute-start(bf16[147,16,128]{2,1,0:T(8,128)(2,1)S(1)} %pack_patches.2.refs_1_.refs_9_), channel_id=1, source_target_pairs={{0,8},{8,0},{16,24},{24,16},{1,9},{9,1},{17,25},{25,17},{2,10},{10... | collective-permute-start | bytes 1806344 | tf_op jit(solution)/shard_map/ppermute | solution.py:46
  22.0 36.7 %collective-permute-start.3 = (bf16[147,16,128]{2,1,0:T(8,128)(2,1)S(1)}, bf16[147,16,128]{2,1,0:T(8,128)(2,1)}, u32[]{:S(2)}, u32[]{:S(2)}) collective-permute-start(bf16[147,16,128]{2,1,0:T(8,128)(2,1)S(1)} %pack_patches.2.refs_1_.refs_9_), channel_id=1, source_target_pairs={{0,16},{8,24},{16,0},{24,8},{1,17},{9,25},{17,1},{25,9},{2,18},{10... | collective-permute-start | bytes 1806344 | tf_op jit(solution)/shard_map/ppermute | solution.py:46
  22.1 0.8 copy-start.9
  23.7 35.0 %collective-permute-start.4 = (bf16[147,16,128]{2,1,0:T(8,128)(2,1)S(1)}, bf16[147,16,128]{2,1,0:T(8,128)(2,1)}, u32[]{:S(2)}, u32[]{:S(2)}) collective-permute-start(bf16[147,16,128]{2,1,0:T(8,128)(2,1)S(1)} %collective-permute-done.1.refs_4_.refs_12_), channel_id=1, source_target_pairs={{0,8},{8,0},{16,24},{24,16},{1,9},{9,1},{17,25},{25,17},{2,10},{10... | collective-permute-start | bytes 1806344 | tf_op jit(solution)/shard_map/ppermute | solution.py:46
  25.7 25.8 %copy-start.1 = (bf16[1,1408,512]{2,1,0:T(8,128)(2,1)S(1)}, bf16[1,1408,512]{2,1,0:T(8,128)(2,1)}, u32[]{:S(2)}) copy-start(bf16[1,1408,512]{2,1,0:T(8,128)(2,1)} %param.15) | copy-start | bytes 4325380
  38.0 20.7 %collective-permute-start.5 = (bf16[147,16,128]{2,1,0:T(8,128)(2,1)S(1)}, bf16[147,16,128]{2,1,0:T(8,128)(2,1)}, u32[]{:S(2)}, u32[]{:S(2)}) collective-permute-start(bf16[147,16,128]{2,1,0:T(8,128)(2,1)S(1)} %collective-permute-done.2.refs_3_.refs_11_), channel_id=1, source_target_pairs={{0,16},{8,24},{16,0},{24,8},{1,17},{9,25},{17,1},{25,9},{2,18},{10... | collective-permute-start | bytes 1806344 | tf_op jit(solution)/shard_map/ppermute | solution.py:46
  53.5 0.9 copy-start.6
  54.3 0.7 copy-start.8
  55.1 19.4 %all-to-all-start.1 = ((bf16[8,16,1152]{2,1,0:T(8,128)(2,1)}), bf16[8,16,1152]{2,1,0:T(8,128)(2,1)S(1)}, u32[]{:S(2)}, u32[]{:S(2)}) async-start(bf16[8,16,1152]{2,1,0:T(8,128)(2,1)} %copy-done.8), calls=%async_computation.1 | async-start | bytes 589824 | tf_op jit(solution)/shard_map/all_to_all | solution.py:50
  73.4 0.9 copy-start.4
  74.3 3.3 %collective-permute-start.6 = (bf16[4,768,128]{2,1,0:T(8,128)(2,1)}, bf16[4,768,128]{2,1,0:T(8,128)(2,1)S(1)}, u32[]{:S(2)}, u32[]{:S(2)}) collective-permute-start(bf16[4,768,128]{2,1,0:T(8,128)(2,1)} %get-tuple-element.56), channel_id=1, source_target_pairs={{0,1},{1,0},{2,3},{3,2},{4,5},{5,4},{6,7},{7,6},{8,9},{9,8},{10,11... | collective-permute-start | bytes 2359304 | tf_op jit(solution)/shard_map/ppermute | solution.py:46
  74.5 1.2 %copy-start.3 = (bf16[1,1024,512]{2,1,0:T(8,128)(2,1)S(1)}, bf16[1,1024,512]{2,1,0:T(8,128)(2,1)}, u32[]{:S(2)}) copy-start(bf16[1,1024,512]{2,1,0:T(8,128)(2,1)} %param.14) | copy-start | bytes 3145732
  75.7 1.9 %copy-start.5 = (bf16[4,768,128]{2,1,0:T(8,128)(2,1)S(1)}, bf16[4,768,128]{2,1,0:T(8,128)(2,1)}, u32[]{:S(2)}) copy-start(bf16[4,768,128]{2,1,0:T(8,128)(2,1)} %copy-done.4) | copy-start | bytes 2359300
  75.7 7.1 %copy-start.11 = (bf16[3136,768]{1,0:T(8,128)(2,1)S(1)}, bf16[3136,768]{1,0:T(8,128)(2,1)}, u32[]{:S(2)}) copy-start(bf16[3136,768]{1,0:T(8,128)(2,1)} %get-tuple-element.62.grad_ref) | copy-start | bytes 14450692
  75.7 7.1 %copy-start.12 = (bf16[1,1024,768]{2,1,0:T(8,128)(2,1)S(1)}, bf16[1,1024,768]{2,1,0:T(8,128)(2,1)}, u32[]{:S(2)}) copy-start(bf16[1,1024,768]{2,1,0:T(8,128)(2,1)} %param.13) | copy-start | bytes 4718596
  75.7 7.1 %copy-start.13 = (bf16[1,256,1024]{2,1,0:T(8,128)(2,1)S(1)}, bf16[1,256,1024]{2,1,0:T(8,128)(2,1)}, u32[]{:S(2)}) copy-start(bf16[1,256,1024]{2,1,0:T(8,128)(2,1)} %param.12) | copy-start | bytes 1572868
  75.7 7.1 %copy-start.14 = (bf16[3136,256]{1,0:T(8,128)(2,1)S(1)}, bf16[3136,256]{1,0:T(8,128)(2,1)}, u32[]{:S(2)}) copy-start(bf16[3136,256]{1,0:T(8,128)(2,1)} %get-tuple-element.63.hidden_ref) | copy-start | bytes 4816900
  76.4 1.2 collective-permute-start.7
  78.3 19.7 %collective-permute-start.8 = (bf16[896,128]{1,0:T(8,128)(2,1)S(1)}, bf16[896,128]{1,0:T(8,128)(2,1)S(1)}, u32[]{:S(2)}, u32[]{:S(2)}) collective-permute-start(bf16[896,128]{1,0:T(8,128)(2,1)S(1)} %get-tuple-element.59), channel_id=1, source_target_pairs={{0,2},{1,3},{2,0},{3,1},{4,6},{5,7},{6,4},{7,5},{8,10},{9,11},{10,... | collective-permute-start | bytes 688136 | tf_op jit(solution)/shard_map/ppermute | solution.py:46
  80.1 19.2 %collective-permute-start.9 = (bf16[896,128]{1,0:T(8,128)(2,1)S(1)}, bf16[896,128]{1,0:T(8,128)(2,1)S(1)}, u32[]{:S(2)}, u32[]{:S(2)}) collective-permute-start(bf16[896,128]{1,0:T(8,128)(2,1)S(1)} %get-tuple-element.60), channel_id=1, source_target_pairs={{0,4},{1,5},{2,6},{3,7},{4,0},{5,1},{6,2},{7,3},{8,12},{9,13},{10,... | collective-permute-start | bytes 688136 | tf_op jit(solution)/shard_map/ppermute | solution.py:46
  82.5 16.8 %collective-permute-start.10 = (bf16[896,128]{1,0:T(8,128)(2,1)S(1)}, bf16[896,128]{1,0:T(8,128)(2,1)S(1)}, u32[]{:S(2)}, u32[]{:S(2)}) collective-permute-start(bf16[896,128]{1,0:T(8,128)(2,1)S(1)} %get-tuple-element.61), channel_id=1, source_target_pairs={{0,6},{1,7},{2,4},{3,5},{4,2},{5,3},{6,0},{7,1},{8,14},{9,15},{10,... | collective-permute-start | bytes 688136 | tf_op jit(solution)/shard_map/ppermute | solution.py:46
  82.8 26.2 %copy-start.7 = (f32[128,1408]{1,0:T(8,128)S(1)}, f32[128,1408]{1,0:T(8,128)}, u32[]{:S(2)}) copy-start(f32[128,1408]{1,0:T(8,128)} %copy-done.6) | copy-start | bytes 2162692
  99.3 1.9 %collective-permute-start.11 = (bf16[4,512,128]{2,1,0:T(8,128)(2,1)S(1)}, bf16[4,512,128]{2,1,0:T(8,128)(2,1)S(1)}, u32[]{:S(2)}, u32[]{:S(2)}) collective-permute-start(bf16[4,512,128]{2,1,0:T(8,128)(2,1)S(1)} %get-tuple-element.68), channel_id=1, source_target_pairs={{0,1},{1,0},{2,3},{3,2},{4,5},{5,4},{6,7},{7,6},{8,9},{9,8},{10,11... | collective-permute-start | bytes 1572872 | tf_op jit(solution)/shard_map/ppermute | solution.py:46
  101.9 10.3 %collective-permute-start.12 = (bf16[512,128]{1,0:T(8,128)(2,1)S(1)}, bf16[512,128]{1,0:T(8,128)(2,1)S(1)}, u32[]{:S(2)}, u32[]{:S(2)}) collective-permute-start(bf16[512,128]{1,0:T(8,128)(2,1)S(1)} %get-tuple-element.70), channel_id=1, source_target_pairs={{0,2},{1,3},{2,0},{3,1},{4,6},{5,7},{6,4},{7,5},{8,10},{9,11},{10,... | collective-permute-start | bytes 393224 | tf_op jit(solution)/shard_map/ppermute | solution.py:46
  106.6 12.9 %collective-permute-start.13 = (bf16[512,128]{1,0:T(8,128)(2,1)S(1)}, bf16[512,128]{1,0:T(8,128)(2,1)S(1)}, u32[]{:S(2)}, u32[]{:S(2)}) collective-permute-start(bf16[512,128]{1,0:T(8,128)(2,1)S(1)} %get-tuple-element.71), channel_id=1, source_target_pairs={{0,4},{1,5},{2,6},{3,7},{4,0},{5,1},{6,2},{7,3},{8,12},{9,13},{10,... | collective-permute-start | bytes 393224 | tf_op jit(solution)/shard_map/ppermute | solution.py:46
  107.5 11.9 %collective-permute-start.14 = (bf16[512,128]{1,0:T(8,128)(2,1)S(1)}, bf16[512,128]{1,0:T(8,128)(2,1)S(1)}, u32[]{:S(2)}, u32[]{:S(2)}) collective-permute-start(bf16[512,128]{1,0:T(8,128)(2,1)S(1)} %get-tuple-element.72), channel_id=1, source_target_pairs={{0,6},{1,7},{2,4},{3,5},{4,2},{5,3},{6,0},{7,1},{8,14},{9,15},{10,... | collective-permute-start | bytes 393224 | tf_op jit(solution)/shard_map/ppermute | solution.py:46

commit v7 on v6

--- a/solution.py
+++ b/solution.py
@@ -107,10 +107,13 @@
     return lax.optimization_barrier((value, other))[0]
 
 
-def forward_kernel(acts_ref, first_ref, second_ref, hidden_ref, feature_ref, pooled_ref):
+def forward_kernel(n_tiles, *refs):
+    acts_refs, refs = refs[:n_tiles], refs[n_tiles:]
+    first_ref, second_ref, hidden_ref = refs[:3]
+    feature_refs, pooled_ref = refs[3:-1], refs[-1]
     step = pl.program_id(0)
-    block, images, width = acts_ref.shape
-    flat = acts_ref[...].reshape(block * images, width)
+    block, images, _ = acts_refs[0].shape
+    flat = jnp.concatenate([ref[...].reshape(block * images, TILE) for ref in acts_refs], axis=1)
     hidden = jnp.maximum(dot(flat, first_ref[...]), 0.0).astype(BF16)
     hidden_ref[...] = hidden
 
@@ -118,10 +121,10 @@
     def _():
         pooled_ref[...] = jnp.zeros(pooled_ref.shape, F32)
 
-    for at in range(0, width, TILE):
-        cut = slice(at, at + TILE)
+    for j, feature_ref in enumerate(feature_refs):
+        cut = slice(j * TILE, (j + 1) * TILE)
         feature = (flat[:, cut].astype(F32) + dot(hidden, second_ref[:, cut])).astype(BF16)
-        feature_ref[:, cut] = feature
+        feature_ref[...] = feature
         pooled_ref[:, cut] += jnp.sum(feature.reshape(block, images, TILE).astype(F32), axis=0)
 
 
@@ -131,11 +134,13 @@
     block = pix // STEPS
     whole = lambda g: (0, 0)
     rows = lambda n: pl.BlockSpec((block * images, n), lambda g: (g, 0))
-    return call(
-        forward_kernel,
+    n_tiles = width // TILE
+    column = lambda j: pl.BlockSpec((block, images, TILE), lambda g: (g, 0, j))
+    hidden, *feature, pooled = call(
+        functools.partial(forward_kernel, n_tiles),
         [
             shape((pix * images, inner), BF16),
-            shape((pix * images, width), BF16),
+            *[shape((pix * images, TILE), BF16)] * n_tiles,
             shape((images, width), F32),
         ],
         limit=58,
@@ -143,13 +148,14 @@
         moved=2 * pix * images * (2 * width + inner),
         grid=(STEPS,),
         in_specs=[
-            pl.BlockSpec((block, images, width), lambda g: (g, 0, 0)),
+            *[column(j) for j in range(n_tiles)],
             pl.BlockSpec(first.shape, whole),
             pl.BlockSpec(second.shape, whole),
         ],
-        out_specs=[rows(inner), rows(width), pl.BlockSpec((images, width), whole)],
+        out_specs=[rows(inner), *[rows(TILE)] * n_tiles, pl.BlockSpec((images, width), whole)],
         name="forward",
-    )(acts, first, second)
+    )(*[acts] * n_tiles, first, second)
+    return hidden, feature, pooled
 
 
 def head_kernel(pix, pooled_ref, aux_ref, labels_ref, aux_pre_ref, sent_ref):
@@ -185,28 +191,28 @@
     )(pooled, aux, labels)
 
 
-def recon_kernel(feature_ref, decode_ref, recon_ref):
-    feature = feature_ref[...]
-    for at in range(0, recon_ref.shape[1], TILE):
-        cut = slice(at, at + TILE)
-        recon_ref[:, cut] = dot(feature, decode_ref[:, cut])
+def recon_kernel(n_feature, *refs):
+    feature_refs, decode_ref, recon_refs = refs[:n_feature], refs[n_feature], refs[n_feature + 1 :]
+    feature = jnp.concatenate([ref[...] for ref in feature_refs], axis=1)
+    for j, recon_ref in enumerate(recon_refs):
+        recon_ref[...] = dot(feature, decode_ref[:, j * TILE : (j + 1) * TILE])
 
 
 def reconstruct(feature, decode):
-    rows, width = feature.shape
-    n = decode.shape[1]
-    block = lambda m: pl.BlockSpec((rows // STEPS, m), lambda g: (g, 0))
-    return call(
-        recon_kernel,
-        shape((rows, n), F32),
+    rows = feature[0].shape[0]
+    width, n = decode.shape
+    block = pl.BlockSpec((rows // STEPS, TILE), lambda g: (g, 0))
+    return call(
+        functools.partial(recon_kernel, len(feature)),
+        [shape((rows, TILE), F32)] * (n // TILE),
         limit=57,
         flops=2 * rows * width * n,
         moved=rows * (2 * width + 4 * n),
         grid=(STEPS,),
-        in_specs=[block(width), pl.BlockSpec(decode.shape, lambda g: (0, 0))],
-        out_specs=block(n),
+        in_specs=[*[block] * len(feature), pl.BlockSpec(decode.shape, lambda g: (0, 0))],
+        out_specs=[block] * (n // TILE),
         name="reconstruct",
-    )(feature, decode)
+    )(*feature, decode)
 
 
 def own_index(h):
@@ -274,42 +280,30 @@
         at += height
 
 
-def fetch(source, held, sems, step):
-    size = held.shape[0] // STEPS
+def fetch(sources, held, sems, step):
+    size, wide = held.shape[0] // STEPS, sources[0].shape[1]
     copies = [
-        pltpu.make_async_copy(source.at[pl.ds(g * size, size)], held.at[pl.ds(g * size, size)], sems.at[g])
+        [
+            pltpu.make_async_copy(
+                source.at[pl.ds(g * size, size)], held.at[pl.ds(g * size, size), pl.ds(j * wide, wide)], sems.at[g, j]
+            )
+            for j, source in enumerate(sources)
+        ]
         for g in range(STEPS)
     ]
 
     @pl.when(step == 0)
     def _():
-        for copy in copies:
-            copy.start()
+        for several in copies:
+            for copy in several:
+                copy.start()
 
     for g in range(STEPS):
 
         @pl.when(step == g)
         def _():
-            copies[g].wait()
-
-
-def fetch(source, held, sems, step):
-    size = held.shape[0] // STEPS
-    copies = [
-        pltpu.make_async_copy(source.at[pl.ds(g * size, size)], held.at[pl.ds(g * size, size)], sems.at[g])
-        for g in range(STEPS)
-    ]
-
-    @pl.when(step == 0)
-    def _():
-        for copy in copies:
-            copy.start()
-
-    for g in range(STEPS):
-
-        @pl.when(step == g)
-        def _():
-            copies[g].wait()
+            for copy in copies[g]:
+                copy.wait()
 
 
 def contract(step, rows, pairs):
@@ -324,17 +318,22 @@
                 total[...] = now if g == 0 else total[...] + now
 
 
-def residual_kernel(groups, scale, n_patch, where_ref, feature_ref, recon_ref, *refs):
+def residual_kernel(groups, scale, n_feature, n_recon, n_patch, where_ref, *refs):
+    feature_refs, refs = refs[:n_feature], refs[n_feature:]
+    recon_refs, refs = refs[:n_recon], refs[n_recon:]
     patch_refs, refs = refs[:n_patch], refs[n_patch:]
-    grad_ref, keep_ref, send_ref, target, feature, grads, total, sems = refs
+    grad_refs, refs = refs[:n_recon], refs[n_recon:]
+    keep_ref, send_ref, target, feature, grads, total, sems = refs
     step = pl.program_id(0)
     rows, width = feature.shape
-    size = grad_ref.shape[0]
-    fetch(feature_ref, feature, sems, step)
+    size = recon_refs[0].shape[0]
+    fetch(feature_refs, feature, sems, step)
     lay_target(step, where_ref, patch_refs, target)
-    grad = ((recon_ref[...] - target[...].reshape(recon_ref.shape).astype(F32)) * scale).astype(BF16)
-    grad_ref[...] = grad
-    grads[pl.ds(pl.multiple_of(step * size, size), size)] = grad
+    for j, (recon_ref, grad_ref) in enumerate(zip(recon_refs, grad_refs)):
+        cut = slice(j * TILE, (j + 1) * TILE)
+        grad = ((recon_ref[...] - target[:, :, cut].reshape(size, TILE).astype(F32)) * scale).astype(BF16)
+        grad_ref[...] = grad
+        grads[pl.ds(pl.multiple_of(step * size, size), size), cut] = grad
     contract(step, rows, [(total, grads, feature)])
 
     @pl.when(step == STEPS - 1)
@@ -343,47 +342,48 @@
 
 
 def residual(where, feature, recon, patch_args, patch_specs, images, scale, groups):
-    rows, width = feature.shape
-    n = recon.shape[1]
+    rows = feature[0].shape[0]
+    width, n = len(feature) * TILE, len(recon) * TILE
     size = rows // STEPS
     parts = (groups // 2, n, width // groups)
     dealt = pl.BlockSpec(parts, lambda g, where: (0, 0, 0))
-    block = pl.BlockSpec((size, n), lambda g, where: (g, 0))
-    return call(
-        functools.partial(residual_kernel, groups, scale, len(patch_args)),
-        [shape((rows, n), BF16), shape(parts, BF16), shape(parts, BF16)],
+    block = pl.BlockSpec((size, TILE), lambda g, where: (g, 0))
+    *grad, keep, send = call(
+        functools.partial(residual_kernel, groups, scale, len(feature), len(recon), len(patch_args)),
+        [*[shape((rows, TILE), BF16)] * len(recon), shape(parts, BF16), shape(parts, BF16)],
         limit=48,
         flops=2 * rows * width * n,
         moved=rows * (2 * width + 6 * n),
         grid_spec=pltpu.PrefetchScalarGridSpec(
             num_scalar_prefetch=1,
             grid=(STEPS,),
-            in_specs=[HBM, block, *patch_specs],
-            out_specs=[block, dealt, dealt],
+            in_specs=[*[HBM] * len(feature), *[block] * len(recon), *patch_specs],
+            out_specs=[*[block] * len(recon), dealt, dealt],
             scratch_shapes=[
                 pltpu.VMEM((size // images, images, n), BF16),
                 pltpu.VMEM((rows, width), BF16),
                 pltpu.VMEM((rows, n), BF16),
                 pltpu.VMEM((n, width), F32),
-                pltpu.SemaphoreType.DMA((STEPS,)),
+                pltpu.SemaphoreType.DMA((STEPS, len(feature))),
             ],
         ),
         name="residual",
-    )(where, feature, recon, *patch_args)
-
-
-def backward_kernel(
-    groups, where_ref, grad_ref, hidden_ref, acts_ref, decode_ref, pooled_ref, second_ref,
-    keep_ref, send_ref, hidden, acts, feature_grads, hidden_grads, total_second, total_first, sems,
-):
+    )(where, *feature, *recon, *patch_args)
+    return grad, keep, send
+
+
+def backward_kernel(groups, n_grad, where_ref, *refs):
+    grad_refs, refs = refs[:n_grad], refs[n_grad:]
+    (hidden_ref, acts_ref, decode_ref, pooled_ref, second_ref, keep_ref, send_ref,
+     hidden, acts, feature_grads, hidden_grads, total_second, total_first, sems) = refs
     step = pl.program_id(0)
     rows, width = feature_grads.shape
-    size = grad_ref.shape[0]
+    size = grad_refs[0].shape[0]
     images = pooled_ref.shape[0]
-    fetch(hidden_ref, hidden, sems.at[0], step)
-    fetch(acts_ref, acts, sems.at[1], step)
+    fetch([hidden_ref], hidden, sems.at[0], step)
+    fetch([acts_ref], acts, sems.at[1], step)
     here = pl.ds(pl.multiple_of(step * size, size), size)
-    grad = grad_ref[...]
+    grad = jnp.concatenate([ref[...] for ref in grad_refs], axis=1)
     for at in range(0, width, TILE):
         cut = slice(at, at + TILE)
         back = dot(grad, decode_ref[cut, :], COLS_1).reshape(size // images, images, TILE)
@@ -410,13 +410,13 @@
 
 def backward(where, grad, hidden, acts, decode, pooled, second, groups):
     rows, width = acts.shape
-    inner, n = hidden.shape[1], grad.shape[1]
+    inner, n = hidden.shape[1], len(grad) * TILE
     size = rows // STEPS
     parts = (groups // 2, 2 * inner, width // groups)
     dealt = pl.BlockSpec(parts, lambda g, where: (0, 0, 0))
     whole = lambda array: pl.BlockSpec(array.shape, lambda g, where: (0, 0))
     return call(
-        functools.partial(backward_kernel, groups),
+        functools.partial(backward_kernel, groups, len(grad)),
         [shape(parts, BF16), shape(parts, BF16)],
         limit=44,
         flops=2 * rows * width * (n + 3 * inner),
@@ -425,7 +425,7 @@
             num_scalar_prefetch=1,
             grid=(STEPS,),
             in_specs=[
-                pl.BlockSpec((size, n), lambda g, where: (g, 0)),
+                *[pl.BlockSpec((size, TILE), lambda g, where: (g, 0))] * len(grad),
                 HBM,
                 HBM,
                 whole(decode),
@@ -440,11 +440,11 @@
                 pltpu.VMEM((rows, inner), BF16),
                 pltpu.VMEM((inner, width), F32),
                 pltpu.VMEM((inner, width), F32),
-                pltpu.SemaphoreType.DMA((2, STEPS)),
+                pltpu.SemaphoreType.DMA((2, STEPS, 1)),
             ],
         ),
         name="backward",
-    )(where, grad, hidden, acts, decode, pooled, second)
+    )(where, *grad, hidden, acts, decode, pooled, second)
 
 
 TOPS, DENOMS = 3, 19
@@ -505,6 +505,7 @@
         logits_kernel,
         [shape((groups * images, classes), F32), shape((groups, images, 2 * head + LANES), BF16)],
         limit=16,
+        flops=2e10,
         in_specs=[SMEM, VMEM, VMEM],
         name="class_logits",
     )(where, got, klass)
@@ -677,17 +678,17 @@
     hidden, feature, pooled = forward(acts, first, second)
     aux_pre, sent = aux_head(pooled, aux, labels, pix, groups)
     got = exchange(sent)
-    recon = reconstruct(after(feature, sent), decode)
+    recon = reconstruct([after(feature[0], sent), *feature[1:]], decode)
     if paired:
         last = after(halves[1], pooled)
         x.append(swap(last, "section", 1))
         y.append(swap(last, "section", 2))
-        diagonal = [swap(after(y[0], aux_pre), "section", 1), swap(after(x[1], recon), "section", 2)]
+        diagonal = [swap(after(y[0], aux_pre), "section", 1), swap(after(x[1], recon[0]), "section", 2)]
         blocks = [halves, x, y, diagonal]
         target = patch_operands(blocks, [0, 1, 2, 3], [0, 1, 2, 3])
     else:
         target = [target], [pl.BlockSpec((pix // STEPS, images, n_decode), lambda g, where: (g, 0, 0))]
-    logits, sent = class_logits(where, after(got, recon), klass)
+    logits, sent = class_logits(where, after(got, recon[0]), klass)
     partial = exchange(sent)
     grad, keep, send = residual(after(where, sent), feature, recon, *target, images, scale, groups)
     pooled_grad, aux_grad = aux_backward(partial, aux_pre, aux, pix, norm)

time: 121 us -> 119 us (0.983)
  blocking collectives: 13 us -> 0 us
  starting transfers between devices: 23.3 us -> 30.7 us
  waiting for transfers between devices: 13.4 us -> 15.6 us
  local copies, waits for them, and re-layouts: 6.08 us -> 7.44 us
    all_to_all x1 -> x0, blocking collectives: 13 us -> none  [exchange(): lax.all_to_all(value, 'dp', 0, 0, axis_index_groups=groups, tiled=True)]
    all_to_all x1 -> x2, starting transfers between devices: 3.6 us -> 10.3 us  [exchange(): lax.all_to_all(value, 'dp', 0, 0, axis_index_groups=groups, tiled=True)]
    ppermute x15, waiting for transfers between devices: 13.4 us -> 15.5 us  [swap(): return lax.ppermute(value, axis, [(i, i ^ bits) for i in range(count)])]
    unnamed x30 -> x34, local copies, waits for them, and re-layouts: 5.99 us -> 7.36 us
  transfers between devices with their start and end apart: 16 -> 17, of which waited for: 5 -> 6; matrix products, arithmetic and copies ran while one was open for 0% -> 0% of each run, Pallas kernels for 49% -> 51%
where the time goes in v7:
time: 119 us
  Pallas kernels  64.4 us (54%)
  starting transfers between devices  30.7 us (26%)
  waiting for transfers between devices  15.6 us (13%)
  local copies, waits for them, and re-layouts  7.44 us (6%)
    ppermute x15, starting transfers between devices, swap(): return lax.ppermute(value, axis, [(i, i ^ bits) for i in range(count)])  20.4 us
    ppermute x15, waiting for transfers between devices, swap(): return lax.ppermute(value, axis, [(i, i ^ bits) for i in range(count)])  15.5 us
    pallas_call x1, Pallas kernels, backward(): call(functools.partial(backward_kernel, groups, len(grad)), [shape(parts,...  15.3 us
    pallas_call x1, Pallas kernels, residual(): call(functools.partial(residual_kernel, groups, scale, len(feature), len(...  15.1 us
    pallas_call x1, Pallas kernels, forward(): call(functools.partial(forward_kernel, n_tiles), [shape((pix * images, in...  10.9 us
    all_to_all x2, starting transfers between devices, exchange(): lax.all_to_all(value, 'dp', 0, 0, axis_index_groups=groups, tiled=True)  10.3 us
    pallas_call x1, Pallas kernels, reconstruct(): call(functools.partial(recon_kernel, len(feature)), [shape((rows, TILE),...  9.82 us
    unnamed x34, local copies, waits for them, and re-layouts  7.36 us
  transfers between devices with their start and end apart: 17, of which 6 were waited for; matrix products, arithmetic and copies ran while one was open for 0% of the time, Pallas kernels for 51%

profile of v7, /device:TPU:0, one launch (start us, length us, event | category | flops | bytes accessed | tf_op | source)
XLA Modules:
  0.0 118.9 jit_solution(11032417287507357189)
XLA Ops:
  0.7 0.1 stack.47.where_ref
  0.7 1.4 %copy-done = bf16[16,196,192]{1,2,0:T(8,128)(2,1)S(1)} copy-done((bf16[16,196,192]{1,2,0:T(8,128)(2,1)S(1)}, bf16[16,196,192]{1,2,0:T(8,128)(2,1)}, u32[]{:S(2)}) %copy-start) | copy-done | bytes 1204248
  2.2 1.8 %pack_patches.3.refs_7_.refs_15_ = bf16[147,16,128]{2,1,0:T(8,128)(2,1)S(1)} custom-call(s32[11]{0:T(128)S(1)} %stack.47.where_ref, bf16[16,192,196]{2,1,0:T(8,128)(2,1)S(1)} %bitcast.27), custom_call_target="tpu_custom_call" | custom-call | tf_op jit(solution)/shard_map/pack_patches/pallas_call | solution.py:92
  4.0 3.0 %collective-permute-start.1 = (bf16[147,16,128]{2,1,0:T(8,128)(2,1)S(1)}, bf16[147,16,128]{2,1,0:T(8,128)(2,1)S(1)}, u32[]{:S(2)}, u32[]{:S(2)}) collective-permute-start(bf16[147,16,128]{2,1,0:T(8,128)(2,1)S(1)} %pack_patches.3.refs_7_.refs_15_), channel_id=1, source_target_pairs={{0,16},{8,24},{16,0},{24,8},{1,17},{9,25},{17,1},{25,9},{2,18},{10... | collective-permute-start | bytes 1806344 | tf_op jit(solution)/shard_map/ppermute | solution.py:46
  7.0 1.5 %collective-permute-start = (bf16[147,16,128]{2,1,0:T(8,128)(2,1)S(1)}, bf16[147,16,128]{2,1,0:T(8,128)(2,1)S(1)}, u32[]{:S(2)}, u32[]{:S(2)}) collective-permute-start(bf16[147,16,128]{2,1,0:T(8,128)(2,1)S(1)} %pack_patches.3.refs_7_.refs_15_), channel_id=1, source_target_pairs={{0,8},{8,0},{16,24},{24,16},{1,9},{9,1},{17,25},{25,17},{2,10},{10... | collective-permute-start | bytes 1806344 | tf_op jit(solution)/shard_map/ppermute | solution.py:46
  8.5 1.8 %pack_patches.2.refs_8_.refs_16_ = bf16[147,16,128]{2,1,0:T(8,128)(2,1)S(1)} custom-call(s32[11]{0:T(128)S(1)} %stack.47.where_ref, bf16[16,192,196]{2,1,0:T(8,128)(2,1)S(1)} %bitcast.28), custom_call_target="tpu_custom_call" | custom-call | tf_op jit(solution)/shard_map/pack_patches/pallas_call | solution.py:92
  10.3 0.0 copy-start.1
  10.3 0.0 copy-start.10
  10.4 10.9 %forward.1 = (bf16[3136,256]{1,0:T(8,128)(2,1)}, bf16[3136,256]{1,0:T(8,128)(2,1)}, bf16[3136,256]{1,0:T(8,128)(2,1)}, bf16[3136,256]{1,0:T(8,128)(2,1)}, bf16[3136,256]{1,0:T(8,128)(2,1)}, /*index=5*/f32[16,1024]{1,0:T(8,128)}) custom-call(bf16[196,16,1024]{2,1,0:T(8,128)(2,1)} %bitcast.36, bf16[196,16,1024]{2,1,0:T(8,128)(2,1)} %bitcast.37, ...), custom_call_target="tpu_custom_call" | custom-call | flops 3288334336 | bytes 14450688 | tf_op jit(solution)/shard_map/forward/pallas_call | solution.py:139
  21.3 0.6 collective-permute-start.2
  21.9 0.1 collective-permute-start.3
  22.0 0.1 collective-permute-done.refs_9_.refs_17_
  22.1 0.8 copy-done.9
  22.9 1.5 %aux_head.1 = (f32[16,512]{1,0:T(8,128)S(1)}, bf16[8,16,768]{2,1,0:T(8,128)(2,1)}) custom-call(f32[16,1024]{1,0:T(8,128)S(1)} %copy-done.9, bf16[1024,512]{1,0:T(8,128)(2,1)S(1)} %bitcast.29, s32[16]{0:T(128)S(1)} %copy-done.10), custom_call_target="tpu_custom_call" | custom-call | tf_op jit(solution)/shard_map/aux_head/pallas_call | solution.py:185
  24.4 5.2 %all-to-all-start = ((bf16[8,16,768]{2,1,0:T(8,128)(2,1)}), bf16[8,16,768]{2,1,0:T(8,128)(2,1)S(1)}, u32[]{:S(2)}, u32[]{:S(2)}) async-start(bf16[8,16,768]{2,1,0:T(8,128)(2,1)} %get-tuple-element.53), calls=%async_computation | async-start | bytes 393216 | tf_op jit(solution)/shard_map/all_to_all | solution.py:50
  29.6 1.5 %collective-permute-start.4 = (bf16[147,16,128]{2,1,0:T(8,128)(2,1)S(1)}, bf16[147,16,128]{2,1,0:T(8,128)(2,1)}, u32[]{:S(2)}, u32[]{:S(2)}) collective-permute-start(bf16[147,16,128]{2,1,0:T(8,128)(2,1)S(1)} %collective-permute-done.1.refs_11_.refs_19_), channel_id=1, source_target_pairs={{0,8},{8,0},{16,24},{24,16},{1,9},{9,1},{17,25},{25,17},{2,10},{10... | collective-permute-start | bytes 1806344 | tf_op jit(solution)/shard_map/ppermute | solution.py:46
  31.1 9.8 %reconstruct.1 = (f32[3136,256]{1,0:T(8,128)}, f32[3136,256]{1,0:T(8,128)}, f32[3136,256]{1,0:T(8,128)}) custom-call(bf16[3136,256]{1,0:T(8,128)(2,1)} %get-tuple-element.55.refs_0_, bf16[3136,256]{1,0:T(8,128)(2,1)} %get-tuple-element.56.refs_1_, bf16[3136,256]{1,0:T(8,128)(2,1)} %get-tuple-element.57.refs_2_, bf16[3136,256]{1,0:T(8,128)(2,1)} %get-tuple-element.58.refs_3_, ...), custom_call_target="tpu_custom_call" | custom-call | flops 4932501504 | bytes 16056320 | tf_op jit(solution)/shard_map/reconstruct/pallas_call | solution.py:205
  40.9 1.6 %collective-permute-start.5 = (bf16[147,16,128]{2,1,0:T(8,128)(2,1)S(1)}, bf16[147,16,128]{2,1,0:T(8,128)(2,1)}, u32[]{:S(2)}, u32[]{:S(2)}) collective-permute-start(bf16[147,16,128]{2,1,0:T(8,128)(2,1)S(1)} %collective-permute-done.2.refs_10_.refs_18_), channel_id=1, source_target_pairs={{0,16},{8,24},{16,0},{24,8},{1,17},{9,25},{17,1},{25,9},{2,18},{10... | collective-permute-start | bytes 1806344 | tf_op jit(solution)/shard_map/ppermute | solution.py:46
  42.5 1.4 %copy-done.16 = bf16[1,1408,512]{2,1,0:T(8,128)(2,1)S(1)} copy-done((bf16[1,1408,512]{2,1,0:T(8,128)(2,1)S(1)}, bf16[1,1408,512]{2,1,0:T(8,128)(2,1)}, u32[]{:S(2)}) %copy-start.16) | copy-done | bytes 1441816
  43.9 2.0 %class_logits.1 = (f32[128,1408]{1,0:T(8,128)S(1)}, bf16[8,16,1152]{2,1,0:T(8,128)(2,1)S(1)}) custom-call(s32[11]{0:T(128)S(1)} %stack.47.where_ref, bf16[8,16,768]{2,1,0:T(8,128)(2,1)S(1)} %all-to-all-done.got_ref, bf16[1408,512]{1,0:T(8,128)(2,1)S(1)} %bitcast.35), custom_call_target="tpu_custom_call" | custom-call | flops 20000000000 | tf_op jit(solution)/shard_map/class_logits/pallas_call | solution.py:504
  45.8 0.9 copy-done.5
  46.7 0.7 copy-done.8
  47.4 5.1 %all-to-all-start.1 = ((bf16[8,16,1152]{2,1,0:T(8,128)(2,1)}), bf16[8,16,1152]{2,1,0:T(8,128)(2,1)S(1)}, u32[]{:S(2)}, u32[]{:S(2)}) async-start(bf16[8,16,1152]{2,1,0:T(8,128)(2,1)} %copy-done.8), calls=%async_computation.1 | async-start | bytes 589824 | tf_op jit(solution)/shard_map/all_to_all | solution.py:50
  52.5 0.0 collective-permute-done.3.refs_12_.refs_20_
  52.5 0.0 collective-permute-done.4.refs_13_.refs_21_
  52.5 4.3 %collective-permute-done.5.refs_14_.refs_22_ = bf16[147,16,128]{2,1,0:T(8,128)(2,1)} collective-permute-done((bf16[147,16,128]{2,1,0:T(8,128)(2,1)S(1)}, bf16[147,16,128]{2,1,0:T(8,128)(2,1)}, u32[]{:S(2)}, u32[]{:S(2)}) %collective-permute-start.5) | collective-permute-done | bytes 602144 | tf_op jit(solution)/shard_map/ppermute | solution.py:46
  56.8 15.1 %residual.1 = (bf16[3136,256]{1,0:T(8,128)(2,1)}, bf16[3136,256]{1,0:T(8,128)(2,1)}, bf16[3136,256]{1,0:T(8,128)(2,1)}, bf16[4,768,128]{2,1,0:T(8,128)(2,1)S(1)}, bf16[4,768,128]{2,1,0:T(8,128)(2,1)}) custom-call(s32[11]{0:T(128)S(1)} %stack.47.where_ref, bf16[3136,256]{1,0:T(8,128)(2,1)} %get-tuple-element.55.refs_0_, ...), custom_call_target="tpu_custom_call" | custom-call | flops 4932501504 | bytes 20873216 | tf_op jit(solution)/shard_map/residual/pallas_call | solution.py:351
  71.9 0.9 copy-done.3
  72.8 0.0 collective-permute-start.6
  72.8 1.2 %copy-done.2 = bf16[1,1024,512]{2,1,0:T(8,128)(2,1)S(1)} copy-done((bf16[1,1024,512]{2,1,0:T(8,128)(2,1)S(1)}, bf16[1,1024,512]{2,1,0:T(8,128)(2,1)}, u32[]{:S(2)}) %copy-start.2) | copy-done | bytes 1048600
  74.0 0.0 copy-start.15
  74.0 0.6 aux_backward.1
  74.7 0.5 collective-permute-start.7
  75.2 0.8 collective-permute-done.7.refs_1_
  76.0 0.7 add_cores.2
  76.8 1.7 %collective-permute-start.8 = (bf16[896,128]{1,0:T(8,128)(2,1)S(1)}, bf16[896,128]{1,0:T(8,128)(2,1)S(1)}, u32[]{:S(2)}, u32[]{:S(2)}) collective-permute-start(bf16[896,128]{1,0:T(8,128)(2,1)S(1)} %get-tuple-element.73), channel_id=1, source_target_pairs={{0,2},{1,3},{2,0},{3,1},{4,6},{5,7},{6,4},{7,5},{8,10},{9,11},{10,... | collective-permute-start | bytes 688136 | tf_op jit(solution)/shard_map/ppermute | solution.py:46
  78.5 2.4 %collective-permute-start.9 = (bf16[896,128]{1,0:T(8,128)(2,1)S(1)}, bf16[896,128]{1,0:T(8,128)(2,1)S(1)}, u32[]{:S(2)}, u32[]{:S(2)}) collective-permute-start(bf16[896,128]{1,0:T(8,128)(2,1)S(1)} %get-tuple-element.74), channel_id=1, source_target_pairs={{0,4},{1,5},{2,6},{3,7},{4,0},{5,1},{6,2},{7,3},{8,12},{9,13},{10,... | collective-permute-start | bytes 688136 | tf_op jit(solution)/shard_map/ppermute | solution.py:46
  80.9 0.4 collective-permute-start.10
  81.3 15.3 %backward.1 = (bf16[4,512,128]{2,1,0:T(8,128)(2,1)S(1)}, bf16[4,512,128]{2,1,0:T(8,128)(2,1)S(1)}) custom-call(s32[11]{0:T(128)S(1)} %stack.47.where_ref, bf16[3136,256]{1,0:T(8,128)(2,1)S(1)} %copy-done.12, bf16[3136,256]{1,0:T(8,128)(2,1)S(1)} %copy-done.13, bf16[3136,256]{1,0:T(8,128)(2,1)S(1)} %copy-done.14, bf16[3136,256]{1,0:T(8,128)(2,1)S(1)} %copy-done.11, ...), custom_call_target="tpu_custom_call" | custom-call | flops 9865003008 | bytes 12845056 | tf_op jit(solution)/shard_map/backward/pallas_call | solution.py:418
  96.6 1.2 collective-permute-done.9.refs_2_
  97.8 1.9 %collective-permute-done.11.got_ref = bf16[4,512,128]{2,1,0:T(8,128)(2,1)S(1)} collective-permute-done((bf16[4,512,128]{2,1,0:T(8,128)(2,1)S(1)}, bf16[4,512,128]{2,1,0:T(8,128)(2,1)S(1)}, u32[]{:S(2)}, u32[]{:S(2)}) %collective-permute-start.11) | collective-permute-done | bytes 524320 | tf_op jit(solution)/shard_map/ppermute | solution.py:46
  99.7 0.7 add_cores.3
  100.4 4.7 %collective-permute-start.12 = (bf16[512,128]{1,0:T(8,128)(2,1)S(1)}, bf16[512,128]{1,0:T(8,128)(2,1)S(1)}, u32[]{:S(2)}, u32[]{:S(2)}) collective-permute-start(bf16[512,128]{1,0:T(8,128)(2,1)S(1)} %get-tuple-element.86), channel_id=1, source_target_pairs={{0,2},{1,3},{2,0},{3,1},{4,6},{5,7},{6,4},{7,5},{8,10},{9,11},{10,... | collective-permute-start | bytes 393224 | tf_op jit(solution)/shard_map/ppermute | solution.py:46
  105.0 1.0 collective-permute-start.13
  106.0 1.5 %collective-permute-start.14 = (bf16[512,128]{1,0:T(8,128)(2,1)S(1)}, bf16[512,128]{1,0:T(8,128)(2,1)S(1)}, u32[]{:S(2)}, u32[]{:S(2)}) collective-permute-start(bf16[512,128]{1,0:T(8,128)(2,1)S(1)} %get-tuple-element.88), channel_id=1, source_target_pairs={{0,6},{1,7},{2,4},{3,5},{4,2},{5,3},{6,0},{7,1},{8,14},{9,15},{10,... | collective-permute-start | bytes 393224 | tf_op jit(solution)/shard_map/ppermute | solution.py:46
  107.5 3.2 %class_backward.1 = (f32[1408,512]{1,0:T(8,128)}, f32[128,512]{1,0:T(8,128)}) custom-call(s32[11]{0:T(128)S(1)} %stack.47.where_ref, f32[128,1408]{1,0:T(8,128)S(1)} %copy-done.6, bf16[8,16,768]{2,1,0:T(8,128)(2,1)S(1)} %all-to-all-done.got_ref, bf16[8,16,1152]{2,1,0:T(8,128)(2,1)S(1)} %all-to-all-done.1.got_ref.stats_ref, ...), custom_call_target="tpu_custom_call" | custom-call | flops 184549376 | bytes 2883584 | tf_op jit(solution)/shard_map/class_backward/pallas_call | solution.py:579
  110.7 7.2 %collective-permute-done.13.refs_6_ = bf16[512,128]{1,0:T(8,128)(2,1)S(1)} collective-permute-done((bf16[512,128]{1,0:T(8,128)(2,1)S(1)}, bf16[512,128]{1,0:T(8,128)(2,1)S(1)}, u32[]{:S(2)}, u32[]{:S(2)}) %collective-permute-start.13) | collective-permute-done | bytes 131104 | tf_op jit(solution)/shard_map/ppermute | solution.py:46
  117.9 1.0 finish.1
  (34 shorter events, 0.1 us)
Async XLA Ops:
  0.7 1.4 %copy-start = (bf16[16,196,192]{1,2,0:T(8,128)(2,1)S(1)}, bf16[16,196,192]{1,2,0:T(8,128)(2,1)}, u32[]{:S(2)}) copy-start(bf16[16,196,192]{1,2,0:T(8,128)(2,1)} %param.9) | copy-start | bytes 3612676
  4.0 18.0 %collective-permute-start.1 = (bf16[147,16,128]{2,1,0:T(8,128)(2,1)S(1)}, bf16[147,16,128]{2,1,0:T(8,128)(2,1)S(1)}, u32[]{:S(2)}, u32[]{:S(2)}) collective-permute-start(bf16[147,16,128]{2,1,0:T(8,128)(2,1)S(1)} %pack_patches.3.refs_7_.refs_15_), channel_id=1, source_target_pairs={{0,16},{8,24},{16,0},{24,8},{1,17},{9,25},{17,1},{25,9},{2,18},{10... | collective-permute-start | bytes 1806344 | tf_op jit(solution)/shard_map/ppermute | solution.py:46
  7.0 15.1 %collective-permute-start = (bf16[147,16,128]{2,1,0:T(8,128)(2,1)S(1)}, bf16[147,16,128]{2,1,0:T(8,128)(2,1)S(1)}, u32[]{:S(2)}, u32[]{:S(2)}) collective-permute-start(bf16[147,16,128]{2,1,0:T(8,128)(2,1)S(1)} %pack_patches.3.refs_7_.refs_15_), channel_id=1, source_target_pairs={{0,8},{8,0},{16,24},{24,16},{1,9},{9,1},{17,25},{25,17},{2,10},{10... | collective-permute-start | bytes 1806344 | tf_op jit(solution)/shard_map/ppermute | solution.py:46
  10.3 11.7 %copy-start.1 = (bf16[1,1024,512]{2,1,0:T(8,128)(2,1)S(1)}, bf16[1,1024,512]{2,1,0:T(8,128)(2,1)}, u32[]{:S(2)}) copy-start(bf16[1,1024,512]{2,1,0:T(8,128)(2,1)} %param.14) | copy-start | bytes 3145732
  10.3 11.7 %copy-start.10 = (s32[16]{0:T(128)S(1)}, s32[16]{0:T(128)}, u32[]{:S(2)}) copy-start(s32[16]{0:T(128)} %labels_ref) | copy-start | bytes 196
  21.3 19.6 %collective-permute-start.2 = (bf16[147,16,128]{2,1,0:T(8,128)(2,1)S(1)}, bf16[147,16,128]{2,1,0:T(8,128)(2,1)S(1)}, u32[]{:S(2)}, u32[]{:S(2)}) collective-permute-start(bf16[147,16,128]{2,1,0:T(8,128)(2,1)S(1)} %pack_patches.2.refs_8_.refs_16_), channel_id=1, source_target_pairs={{0,8},{8,0},{16,24},{24,16},{1,9},{9,1},{17,25},{25,17},{2,10},{10... | collective-permute-start | bytes 1806344 | tf_op jit(solution)/shard_map/ppermute | solution.py:46
  21.9 30.6 %collective-permute-start.3 = (bf16[147,16,128]{2,1,0:T(8,128)(2,1)S(1)}, bf16[147,16,128]{2,1,0:T(8,128)(2,1)}, u32[]{:S(2)}, u32[]{:S(2)}) collective-permute-start(bf16[147,16,128]{2,1,0:T(8,128)(2,1)S(1)} %pack_patches.2.refs_8_.refs_16_), channel_id=1, source_target_pairs={{0,16},{8,24},{16,0},{24,8},{1,17},{9,25},{17,1},{25,9},{2,18},{10... | collective-permute-start | bytes 1806344 | tf_op jit(solution)/shard_map/ppermute | solution.py:46
  22.1 0.8 copy-start.9
  24.4 18.1 %all-to-all-start = ((bf16[8,16,768]{2,1,0:T(8,128)(2,1)}), bf16[8,16,768]{2,1,0:T(8,128)(2,1)S(1)}, u32[]{:S(2)}, u32[]{:S(2)}) async-start(bf16[8,16,768]{2,1,0:T(8,128)(2,1)} %get-tuple-element.53), calls=%async_computation | async-start | bytes 393216 | tf_op jit(solution)/shard_map/all_to_all | solution.py:50
  29.6 22.9 %collective-permute-start.4 = (bf16[147,16,128]{2,1,0:T(8,128)(2,1)S(1)}, bf16[147,16,128]{2,1,0:T(8,128)(2,1)}, u32[]{:S(2)}, u32[]{:S(2)}) collective-permute-start(bf16[147,16,128]{2,1,0:T(8,128)(2,1)S(1)} %collective-permute-done.1.refs_11_.refs_19_), channel_id=1, source_target_pairs={{0,8},{8,0},{16,24},{24,16},{1,9},{9,1},{17,25},{25,17},{2,10},{10... | collective-permute-start | bytes 1806344 | tf_op jit(solution)/shard_map/ppermute | solution.py:46
  40.9 15.9 %collective-permute-start.5 = (bf16[147,16,128]{2,1,0:T(8,128)(2,1)S(1)}, bf16[147,16,128]{2,1,0:T(8,128)(2,1)}, u32[]{:S(2)}, u32[]{:S(2)}) collective-permute-start(bf16[147,16,128]{2,1,0:T(8,128)(2,1)S(1)} %collective-permute-done.2.refs_10_.refs_18_), channel_id=1, source_target_pairs={{0,16},{8,24},{16,0},{24,8},{1,17},{9,25},{17,1},{25,9},{2,18},{10... | collective-permute-start | bytes 1806344 | tf_op jit(solution)/shard_map/ppermute | solution.py:46
  42.5 1.4 %copy-start.16 = (bf16[1,1408,512]{2,1,0:T(8,128)(2,1)S(1)}, bf16[1,1408,512]{2,1,0:T(8,128)(2,1)}, u32[]{:S(2)}) copy-start(bf16[1,1408,512]{2,1,0:T(8,128)(2,1)} %param.15) | copy-start | bytes 4325380
  45.8 0.9 copy-start.5
  46.7 0.7 copy-start.8
  47.4 25.4 %all-to-all-start.1 = ((bf16[8,16,1152]{2,1,0:T(8,128)(2,1)}), bf16[8,16,1152]{2,1,0:T(8,128)(2,1)S(1)}, u32[]{:S(2)}, u32[]{:S(2)}) async-start(bf16[8,16,1152]{2,1,0:T(8,128)(2,1)} %copy-done.8), calls=%async_computation.1 | async-start | bytes 589824 | tf_op jit(solution)/shard_map/all_to_all | solution.py:50
  71.9 0.9 copy-start.3
  72.8 3.3 %collective-permute-start.6 = (bf16[4,768,128]{2,1,0:T(8,128)(2,1)}, bf16[4,768,128]{2,1,0:T(8,128)(2,1)S(1)}, u32[]{:S(2)}, u32[]{:S(2)}) collective-permute-start(bf16[4,768,128]{2,1,0:T(8,128)(2,1)} %get-tuple-element.70), channel_id=1, source_target_pairs={{0,1},{1,0},{2,3},{3,2},{4,5},{5,4},{6,7},{7,6},{8,9},{9,8},{10,11... | collective-permute-start | bytes 2359304 | tf_op jit(solution)/shard_map/ppermute | solution.py:46
  72.8 1.2 %copy-start.2 = (bf16[1,1024,512]{2,1,0:T(8,128)(2,1)S(1)}, bf16[1,1024,512]{2,1,0:T(8,128)(2,1)}, u32[]{:S(2)}) copy-start(bf16[1,1024,512]{2,1,0:T(8,128)(2,1)} %param.14) | copy-start | bytes 3145732
  74.0 2.0 %copy-start.4 = (bf16[4,768,128]{2,1,0:T(8,128)(2,1)S(1)}, bf16[4,768,128]{2,1,0:T(8,128)(2,1)}, u32[]{:S(2)}) copy-start(bf16[4,768,128]{2,1,0:T(8,128)(2,1)} %copy-done.3) | copy-start | bytes 2359300
  74.0 7.2 %copy-start.11 = (bf16[3136,256]{1,0:T(8,128)(2,1)S(1)}, bf16[3136,256]{1,0:T(8,128)(2,1)}, u32[]{:S(2)}) copy-start(bf16[3136,256]{1,0:T(8,128)(2,1)} %get-tuple-element.79.refs_3_) | copy-start | bytes 4816900
  74.0 7.2 %copy-start.12 = (bf16[3136,256]{1,0:T(8,128)(2,1)S(1)}, bf16[3136,256]{1,0:T(8,128)(2,1)}, u32[]{:S(2)}) copy-start(bf16[3136,256]{1,0:T(8,128)(2,1)} %get-tuple-element.76.refs_0_) | copy-start | bytes 4816900
  74.0 7.2 %copy-start.13 = (bf16[3136,256]{1,0:T(8,128)(2,1)S(1)}, bf16[3136,256]{1,0:T(8,128)(2,1)}, u32[]{:S(2)}) copy-start(bf16[3136,256]{1,0:T(8,128)(2,1)} %get-tuple-element.77.refs_1_) | copy-start | bytes 4816900
  74.0 7.2 %copy-start.14 = (bf16[3136,256]{1,0:T(8,128)(2,1)S(1)}, bf16[3136,256]{1,0:T(8,128)(2,1)}, u32[]{:S(2)}) copy-start(bf16[3136,256]{1,0:T(8,128)(2,1)} %get-tuple-element.78.refs_2_) | copy-start | bytes 4816900
  74.0 7.2 %copy-start.15 = (bf16[1,1024,768]{2,1,0:T(8,128)(2,1)S(1)}, bf16[1,1024,768]{2,1,0:T(8,128)(2,1)}, u32[]{:S(2)}) copy-start(bf16[1,1024,768]{2,1,0:T(8,128)(2,1)} %param.13) | copy-start | bytes 4718596
  74.7 6.6 %copy-start.7 = (bf16[1,256,1024]{2,1,0:T(8,128)(2,1)S(1)}, bf16[1,256,1024]{2,1,0:T(8,128)(2,1)}, u32[]{:S(2)}) copy-start(bf16[1,256,1024]{2,1,0:T(8,128)(2,1)} %param.12) | copy-start | bytes 1572868
  74.7 1.4 %collective-permute-start.7 = (bf16[64,128]{1,0:T(8,128)(2,1)S(1)}, bf16[64,128]{1,0:T(8,128)(2,1)S(1)}, u32[]{:S(2)}, u32[]{:S(2)}) collective-permute-start(bf16[64,128]{1,0:T(8,128)(2,1)S(1)} %get-tuple-element.71.refs_0_), channel_id=1, source_target_pairs={{0,1},{1,0},{2,3},{3,2},{4,5},{5,4},{6,7},{7,6},{8,9},{9,8},{10,11... | collective-permute-start | bytes 49160 | tf_op jit(solution)/shard_map/ppermute | solution.py:46
  76.8 19.8 %collective-permute-start.8 = (bf16[896,128]{1,0:T(8,128)(2,1)S(1)}, bf16[896,128]{1,0:T(8,128)(2,1)S(1)}, u32[]{:S(2)}, u32[]{:S(2)}) collective-permute-start(bf16[896,128]{1,0:T(8,128)(2,1)S(1)} %get-tuple-element.73), channel_id=1, source_target_pairs={{0,2},{1,3},{2,0},{3,1},{4,6},{5,7},{6,4},{7,5},{8,10},{9,11},{10,... | collective-permute-start | bytes 688136 | tf_op jit(solution)/shard_map/ppermute | solution.py:46
  78.5 19.2 %collective-permute-start.9 = (bf16[896,128]{1,0:T(8,128)(2,1)S(1)}, bf16[896,128]{1,0:T(8,128)(2,1)S(1)}, u32[]{:S(2)}, u32[]{:S(2)}) collective-permute-start(bf16[896,128]{1,0:T(8,128)(2,1)S(1)} %get-tuple-element.74), channel_id=1, source_target_pairs={{0,4},{1,5},{2,6},{3,7},{4,0},{5,1},{6,2},{7,3},{8,12},{9,13},{10,... | collective-permute-start | bytes 688136 | tf_op jit(solution)/shard_map/ppermute | solution.py:46
  80.9 16.9 %collective-permute-start.10 = (bf16[896,128]{1,0:T(8,128)(2,1)S(1)}, bf16[896,128]{1,0:T(8,128)(2,1)S(1)}, u32[]{:S(2)}, u32[]{:S(2)}) collective-permute-start(bf16[896,128]{1,0:T(8,128)(2,1)S(1)} %get-tuple-element.75), channel_id=1, source_target_pairs={{0,6},{1,7},{2,4},{3,5},{4,2},{5,3},{6,0},{7,1},{8,14},{9,15},{10,... | collective-permute-start | bytes 688136 | tf_op jit(solution)/shard_map/ppermute | solution.py:46
  81.3 26.2 %copy-start.6 = (f32[128,1408]{1,0:T(8,128)S(1)}, f32[128,1408]{1,0:T(8,128)}, u32[]{:S(2)}) copy-start(f32[128,1408]{1,0:T(8,128)} %copy-done.5) | copy-start | bytes 2162692
  97.8 1.9 %collective-permute-start.11 = (bf16[4,512,128]{2,1,0:T(8,128)(2,1)S(1)}, bf16[4,512,128]{2,1,0:T(8,128)(2,1)S(1)}, u32[]{:S(2)}, u32[]{:S(2)}) collective-permute-start(bf16[4,512,128]{2,1,0:T(8,128)(2,1)S(1)} %get-tuple-element.84), channel_id=1, source_target_pairs={{0,1},{1,0},{2,3},{3,2},{4,5},{5,4},{6,7},{7,6},{8,9},{9,8},{10,11... | collective-permute-start | bytes 1572872 | tf_op jit(solution)/shard_map/ppermute | solution.py:46
  100.4 10.3 %collective-permute-start.12 = (bf16[512,128]{1,0:T(8,128)(2,1)S(1)}, bf16[512,128]{1,0:T(8,128)(2,1)S(1)}, u32[]{:S(2)}, u32[]{:S(2)}) collective-permute-start(bf16[512,128]{1,0:T(8,128)(2,1)S(1)} %get-tuple-element.86), channel_id=1, source_target_pairs={{0,2},{1,3},{2,0},{3,1},{4,6},{5,7},{6,4},{7,5},{8,10},{9,11},{10,... | collective-permute-start | bytes 393224 | tf_op jit(solution)/shard_map/ppermute | solution.py:46
  105.0 12.9 %collective-permute-start.13 = (bf16[512,128]{1,0:T(8,128)(2,1)S(1)}, bf16[512,128]{1,0:T(8,128)(2,1)S(1)}, u32[]{:S(2)}, u32[]{:S(2)}) collective-permute-start(bf16[512,128]{1,0:T(8,128)(2,1)S(1)} %get-tuple-element.87), channel_id=1, source_target_pairs={{0,4},{1,5},{2,6},{3,7},{4,0},{5,1},{6,2},{7,3},{8,12},{9,13},{10,... | collective-permute-start | bytes 393224 | tf_op jit(solution)/shard_map/ppermute | solution.py:46
  106.0 11.9 %collective-permute-start.14 = (bf16[512,128]{1,0:T(8,128)(2,1)S(1)}, bf16[512,128]{1,0:T(8,128)(2,1)S(1)}, u32[]{:S(2)}, u32[]{:S(2)}) collective-permute-start(bf16[512,128]{1,0:T(8,128)(2,1)S(1)} %get-tuple-element.88), channel_id=1, source_target_pairs={{0,6},{1,7},{2,4},{3,5},{4,2},{5,3},{6,0},{7,1},{8,14},{9,15},{10,... | collective-permute-start | bytes 393224 | tf_op jit(solution)/shard_map/ppermute | solution.py:46

commit v8 on v7

--- a/solution.py
+++ b/solution.py
@@ -107,41 +107,65 @@
     return lax.optimization_barrier((value, other))[0]
 
 
-def forward_kernel(n_tiles, *refs):
+def forward_kernel(n_tiles, pix, *refs):
     acts_refs, refs = refs[:n_tiles], refs[n_tiles:]
-    first_ref, second_ref, hidden_ref = refs[:3]
-    feature_refs, pooled_ref = refs[3:-1], refs[-1]
+    first_ref, second_ref, aux_ref, labels_ref, hidden_ref = refs[:5]
+    feature_refs, (aux_pre_ref, sent_ref, pooled) = refs[5:-3], refs[-3:]
     step = pl.program_id(0)
     block, images, _ = acts_refs[0].shape
-    flat = jnp.concatenate([ref[...].reshape(block * images, TILE) for ref in acts_refs], axis=1)
-    hidden = jnp.maximum(dot(flat, first_ref[...]), 0.0).astype(BF16)
-    hidden_ref[...] = hidden
-
-    @pl.when(step == 0)
+    cut = lambda j: slice(j * TILE, (j + 1) * TILE)
+    start = step == 0
+    halves = []
+    for a, b in ((0, block // 2), (block // 2, block)):
+        flat = jnp.concatenate([ref[a:b].reshape((b - a) * images, TILE) for ref in acts_refs], axis=1)
+        halves.append((a, b, flat, jnp.maximum(dot(flat, first_ref[...]), 0.0).astype(BF16)))
+    for a, b, flat, hidden in halves:
+        rows = slice(a * images, b * images)
+        hidden_ref[rows] = hidden
+        for j, feature_ref in enumerate(feature_refs):
+            feature = (flat[:, cut(j)].astype(F32) + dot(hidden, second_ref[:, cut(j)])).astype(BF16)
+            feature_ref[rows] = feature
+            sums = jnp.sum(feature.reshape(b - a, images, TILE).astype(F32), axis=0)
+            pooled[:, cut(j)] = sums + (pooled[:, cut(j)] if a else jnp.where(start, 0.0, pooled[:, cut(j)]))
+
+    @pl.when(step == pl.num_programs(0) - 1)
     def _():
-        pooled_ref[...] = jnp.zeros(pooled_ref.shape, F32)
-
-    for j, feature_ref in enumerate(feature_refs):
-        cut = slice(j * TILE, (j + 1) * TILE)
-        feature = (flat[:, cut].astype(F32) + dot(hidden, second_ref[:, cut])).astype(BF16)
-        feature_ref[...] = feature
-        pooled_ref[:, cut] += jnp.sum(feature.reshape(block, images, TILE).astype(F32), axis=0)
-
-
-def forward(acts, first, second):
+        groups = sent_ref.shape[0]
+        width, head = aux_ref.shape
+        part = width // groups
+        mean = (pooled[...] / pix).astype(BF16)
+        aux_pre = dot(mean, aux_ref[...])
+        aux_pre_ref[...] = aux_pre
+        out = jnp.maximum(aux_pre, 0.0).astype(BF16)
+        row = lax.broadcasted_iota(jnp.int32, (images, LANES), 0)
+        lane = lax.broadcasted_iota(jnp.int32, (images, LANES), 1)
+        digits = jnp.zeros((images, LANES), jnp.int32)
+        for i in range(images):
+            label = labels_ref[i]
+            digits = jnp.where((row == i) & (lane == 0), label // LANES, digits)
+            digits = jnp.where((row == i) & (lane == 1), label % LANES, digits)
+        digits = digits.astype(F32).astype(BF16)
+        for d in range(groups):
+            sent_ref[d, :, :head] = out
+            sent_ref[d, :, head : head + part] = mean[:, d * part : (d + 1) * part]
+            sent_ref[d, :, head + LANES :] = digits
+
+
+def forward(acts, first, second, aux, labels, groups):
     pix, images, width = acts.shape
-    inner = first.shape[1]
+    inner, head = first.shape[1], aux.shape[1]
     block = pix // STEPS
-    whole = lambda g: (0, 0)
+    n_tiles = width // TILE
+    whole = lambda *dims: pl.BlockSpec(dims, lambda g: (0,) * len(dims))
     rows = lambda n: pl.BlockSpec((block * images, n), lambda g: (g, 0))
-    n_tiles = width // TILE
     column = lambda j: pl.BlockSpec((block, images, TILE), lambda g: (g, 0, j))
-    hidden, *feature, pooled = call(
-        functools.partial(forward_kernel, n_tiles),
+    hidden, *feature, aux_pre, sent = call(
+        functools.partial(forward_kernel, n_tiles, pix),
         [
             shape((pix * images, inner), BF16),
             *[shape((pix * images, TILE), BF16)] * n_tiles,
-            shape((images, width), F32),
+            shape((images, head), F32),
+            shape((groups, images, head + 2 * LANES), BF16),
         ],
         limit=58,
         flops=4 * pix * images * width * inner,
@@ -149,70 +173,21 @@
         grid=(STEPS,),
         in_specs=[
             *[column(j) for j in range(n_tiles)],
-            pl.BlockSpec(first.shape, whole),
-            pl.BlockSpec(second.shape, whole),
+            whole(*first.shape),
+            whole(*second.shape),
+            whole(*aux.shape),
+            SMEM,
         ],
-        out_specs=[rows(inner), *[rows(TILE)] * n_tiles, pl.BlockSpec((images, width), whole)],
+        out_specs=[
+            rows(inner),
+            *[rows(TILE)] * n_tiles,
+            whole(images, head),
+            whole(groups, images, head + 2 * LANES),
+        ],
+        scratch_shapes=[pltpu.VMEM((images, width), F32)],
         name="forward",
-    )(*[acts] * n_tiles, first, second)
-    return hidden, feature, pooled
-
-
-def head_kernel(pix, pooled_ref, aux_ref, labels_ref, aux_pre_ref, sent_ref):
-    groups, images, _ = sent_ref.shape
-    width, head = aux_ref.shape
-    part = width // groups
-    mean = (pooled_ref[...] / pix).astype(BF16)
-    aux_pre = dot(mean, aux_ref[...])
-    aux_pre_ref[...] = aux_pre
-    out = jnp.maximum(aux_pre, 0.0).astype(BF16)
-    row = lax.broadcasted_iota(jnp.int32, (images, LANES), 0)
-    lane = lax.broadcasted_iota(jnp.int32, (images, LANES), 1)
-    digits = jnp.zeros((images, LANES), jnp.int32)
-    for i in range(images):
-        label = labels_ref[i]
-        digits = jnp.where((row == i) & (lane == 0), label // LANES, digits)
-        digits = jnp.where((row == i) & (lane == 1), label % LANES, digits)
-    digits = digits.astype(F32).astype(BF16)
-    for d in range(groups):
-        sent_ref[d, :, :head] = out
-        sent_ref[d, :, head : head + part] = mean[:, d * part : (d + 1) * part]
-        sent_ref[d, :, head + LANES :] = digits
-
-
-def aux_head(pooled, aux, labels, pix, groups):
-    images, head = pooled.shape[0], aux.shape[1]
-    return call(
-        functools.partial(head_kernel, pix),
-        [shape((images, head), F32), shape((groups, images, head + 2 * LANES), BF16)],
-        limit=16,
-        in_specs=[VMEM, VMEM, SMEM],
-        name="aux_head",
-    )(pooled, aux, labels)
-
-
-def recon_kernel(n_feature, *refs):
-    feature_refs, decode_ref, recon_refs = refs[:n_feature], refs[n_feature], refs[n_feature + 1 :]
-    feature = jnp.concatenate([ref[...] for ref in feature_refs], axis=1)
-    for j, recon_ref in enumerate(recon_refs):
-        recon_ref[...] = dot(feature, decode_ref[:, j * TILE : (j + 1) * TILE])
-
-
-def reconstruct(feature, decode):
-    rows = feature[0].shape[0]
-    width, n = decode.shape
-    block = pl.BlockSpec((rows // STEPS, TILE), lambda g: (g, 0))
-    return call(
-        functools.partial(recon_kernel, len(feature)),
-        [shape((rows, TILE), F32)] * (n // TILE),
-        limit=57,
-        flops=2 * rows * width * n,
-        moved=rows * (2 * width + 4 * n),
-        grid=(STEPS,),
-        in_specs=[*[block] * len(feature), pl.BlockSpec(decode.shape, lambda g: (0, 0))],
-        out_specs=[block] * (n // TILE),
-        name="reconstruct",
-    )(*feature, decode)
+    )(*[acts] * n_tiles, first, second, aux, labels)
+    return hidden, feature, aux_pre, sent
 
 
 def own_index(h):
@@ -235,34 +210,24 @@
     return args, specs
 
 
-def lay_target(step, where_ref, refs, target):
+def lay_target(g, where_ref, refs, target):
     if len(refs) == 1:
         target[...] = refs[0][...]
         return
     pairs = [refs[j : j + 2] for j in range(0, len(refs), 2)]
     own, shared = pairs[: len(pairs) // 2], pairs[len(pairs) // 2 :]
     per_half = STEPS // 2
+    h, side = g // per_half, g % per_half
     lanes = lambda j: pl.ds(pl.multiple_of(where_ref[TILES + j] * LANES, LANES), LANES)
-    for h in range(2):
-
-        @pl.when(step // per_half == h)
-        def _():
-            for k, pair in enumerate(own):
-                target[:, :, lanes(2 * k)] = pair[h][...]
-
-    for g in range(STEPS):
-        for parity in range(2):
-
-            @pl.when((step == g) & (where_ref[PARITY] == parity))
-            def _():
-                h, side = g // per_half, g % per_half
-                for k in range(0, len(shared), 2):
-                    even, odd = shared[k + parity][h][...].astype(F32), shared[k + 1 - parity][h][...].astype(F32)
-                    lane = lax.broadcasted_iota(jnp.int32, even.shape, 2)
-                    value = jnp.where((lane < 64) == (side == 0), even, odd)
-                    if side:
-                        value = jnp.concatenate([value[:, :, 64:], value[:, :, :64]], axis=2)
-                    target[:, :, lanes(2 * k + 1)] = value.astype(BF16)
+    for k, pair in enumerate(own):
+        target[:, :, lanes(2 * k)] = pair[h][...]
+    for k in range(0, len(shared), 2):
+        mine, other = shared[k][h][...].astype(F32), shared[k + 1][h][...].astype(F32)
+        lane = lax.broadcasted_iota(jnp.int32, mine.shape, 2)
+        value = jnp.where((lane < 64) == ((where_ref[PARITY] == 0) == (side == 0)), mine, other)
+        if side:
+            value = jnp.concatenate([value[:, :, 64:], value[:, :, :64]], axis=2)
+        target[:, :, lanes(2 * k + 1)] = value.astype(BF16)
 
 
 def deal(where_ref, sums, part, keep_ref, send_ref):
@@ -280,9 +245,9 @@
         at += height
 
 
-def fetch(sources, held, sems, step):
+def copies_of(sources, held, sems):
     size, wide = held.shape[0] // STEPS, sources[0].shape[1]
-    copies = [
+    return [
         [
             pltpu.make_async_copy(
                 source.at[pl.ds(g * size, size)], held.at[pl.ds(g * size, size), pl.ds(j * wide, wide)], sems.at[g, j]
@@ -292,73 +257,78 @@
         for g in range(STEPS)
     ]
 
-    @pl.when(step == 0)
-    def _():
-        for several in copies:
-            for copy in several:
-                copy.start()
-
+
+def by_step(copies, body):
+    step = pl.program_id(0)
     for g in range(STEPS):
 
         @pl.when(step == g)
         def _():
+            if g == 0:
+                for h in range(STEPS):
+                    for copy in copies[h]:
+                        copy.start()
             for copy in copies[g]:
                 copy.wait()
-
-
-def contract(step, rows, pairs):
+            body(g)
+
+
+def contract(g, rows, pairs):
     unit = rows // STEPS // TILE * TILE
-    for g in range(STEPS):
-
-        @pl.when(step == g)
-        def _():
-            span = slice(g * unit, rows if g == STEPS - 1 else (g + 1) * unit)
-            for total, left, right in pairs:
-                now = dot(left[span], right[span], ROWS_0)
-                total[...] = now if g == 0 else total[...] + now
-
-
-def residual_kernel(groups, scale, n_feature, n_recon, n_patch, where_ref, *refs):
+    span = slice(g * unit, rows if g == STEPS - 1 else (g + 1) * unit)
+    for total, left, right in pairs:
+        now = dot(left[span], right[span], ROWS_0)
+        total[...] = now if g == 0 else total[...] + now
+
+
+def residual_kernel(groups, scale, n_feature, n_tiles, n_patch, where_ref, *refs):
     feature_refs, refs = refs[:n_feature], refs[n_feature:]
-    recon_refs, refs = refs[:n_recon], refs[n_recon:]
+    decode_refs, refs = refs[:n_tiles], refs[n_tiles:]
     patch_refs, refs = refs[:n_patch], refs[n_patch:]
-    grad_refs, refs = refs[:n_recon], refs[n_recon:]
+    grad_refs, refs = refs[:n_tiles], refs[n_tiles:]
     keep_ref, send_ref, target, feature, grads, total, sems = refs
-    step = pl.program_id(0)
     rows, width = feature.shape
-    size = recon_refs[0].shape[0]
-    fetch(feature_refs, feature, sems, step)
-    lay_target(step, where_ref, patch_refs, target)
-    for j, (recon_ref, grad_ref) in enumerate(zip(recon_refs, grad_refs)):
-        cut = slice(j * TILE, (j + 1) * TILE)
-        grad = ((recon_ref[...] - target[:, :, cut].reshape(size, TILE).astype(F32)) * scale).astype(BF16)
-        grad_ref[...] = grad
-        grads[pl.ds(pl.multiple_of(step * size, size), size), cut] = grad
-    contract(step, rows, [(total, grads, feature)])
-
-    @pl.when(step == STEPS - 1)
-    def _():
-        deal(where_ref, [total], width // groups, keep_ref, send_ref)
-
-
-def residual(where, feature, recon, patch_args, patch_specs, images, scale, groups):
+    size = grad_refs[0].shape[0]
+
+    def body(g):
+        here = slice(g * size, (g + 1) * size)
+        lay_target(g, where_ref, patch_refs, target)
+        if g:
+            contract(g - 1, rows, [(total, grads, feature)])
+        now = feature[here]
+        for j, grad_ref in enumerate(grad_refs):
+            cut = slice(j * TILE, (j + 1) * TILE)
+            recon = dot(now, decode_refs[j][...])
+            grad = ((recon - target[:, :, cut].reshape(size, TILE).astype(F32)) * scale).astype(BF16)
+            grad_ref[...] = grad
+            grads[here, cut] = grad
+        if g == STEPS - 1:
+            contract(g, rows, [(total, grads, feature)])
+            deal(where_ref, [total], width // groups, keep_ref, send_ref)
+
+    by_step(copies_of(feature_refs, feature, sems), body)
+
+
+def residual(where, feature, decode, patch_args, patch_specs, images, scale, groups):
     rows = feature[0].shape[0]
-    width, n = len(feature) * TILE, len(recon) * TILE
+    width, n = decode.shape
     size = rows // STEPS
+    n_tiles = n // TILE
     parts = (groups // 2, n, width // groups)
     dealt = pl.BlockSpec(parts, lambda g, where: (0, 0, 0))
     block = pl.BlockSpec((size, TILE), lambda g, where: (g, 0))
+    column = lambda j: pl.BlockSpec((width, TILE), lambda g, where: (0, j))
     *grad, keep, send = call(
-        functools.partial(residual_kernel, groups, scale, len(feature), len(recon), len(patch_args)),
-        [*[shape((rows, TILE), BF16)] * len(recon), shape(parts, BF16), shape(parts, BF16)],
-        limit=48,
-        flops=2 * rows * width * n,
+        functools.partial(residual_kernel, groups, scale, len(feature), n_tiles, len(patch_args)),
+        [*[shape((rows, TILE), BF16)] * n_tiles, shape(parts, BF16), shape(parts, BF16)],
+        limit=58,
+        flops=4 * rows * width * n,
         moved=rows * (2 * width + 6 * n),
         grid_spec=pltpu.PrefetchScalarGridSpec(
             num_scalar_prefetch=1,
             grid=(STEPS,),
-            in_specs=[*[HBM] * len(feature), *[block] * len(recon), *patch_specs],
-            out_specs=[*[block] * len(recon), dealt, dealt],
+            in_specs=[*[HBM] * len(feature), *[column(j) for j in range(n_tiles)], *patch_specs],
+            out_specs=[*[block] * n_tiles, dealt, dealt],
             scratch_shapes=[
                 pltpu.VMEM((size // images, images, n), BF16),
                 pltpu.VMEM((rows, width), BF16),
@@ -368,57 +338,63 @@
             ],
         ),
         name="residual",
-    )(where, *feature, *recon, *patch_args)
+    )(where, *feature, *[decode] * n_tiles, *patch_args)
     return grad, keep, send
 
 
-def backward_kernel(groups, n_grad, where_ref, *refs):
+def backward_kernel(groups, n_grad, n_decode, where_ref, *refs):
     grad_refs, refs = refs[:n_grad], refs[n_grad:]
-    (hidden_ref, acts_ref, decode_ref, pooled_ref, second_ref, keep_ref, send_ref,
+    decode_refs, refs = refs[:n_decode], refs[n_decode:]
+    (hidden_ref, acts_ref, pooled_ref, second_ref, keep_ref, send_ref,
      hidden, acts, feature_grads, hidden_grads, total_second, total_first, sems) = refs
-    step = pl.program_id(0)
     rows, width = feature_grads.shape
     size = grad_refs[0].shape[0]
     images = pooled_ref.shape[0]
-    fetch([hidden_ref], hidden, sems.at[0], step)
-    fetch([acts_ref], acts, sems.at[1], step)
-    here = pl.ds(pl.multiple_of(step * size, size), size)
-    grad = jnp.concatenate([ref[...] for ref in grad_refs], axis=1)
-    for at in range(0, width, TILE):
-        cut = slice(at, at + TILE)
-        back = dot(grad, decode_ref[cut, :], COLS_1).reshape(size // images, images, TILE)
-        feature_grads[here, cut] = (back + pooled_ref[:, cut][None]).astype(BF16).reshape(size, TILE)
-    hidden_back = dot(feature_grads[here], second_ref[...], COLS_1)
-    hidden_grads[here] = jnp.where(hidden[here].astype(F32) > 0, hidden_back, 0.0).astype(BF16)
-    contract(step, rows, [(total_second, hidden, feature_grads), (total_first, hidden_grads, acts)])
-
-    @pl.when(step == STEPS - 1)
-    def _():
-        part = width // groups
-        tall = total_second.shape[0] // groups
-        second = jnp.concatenate(
-            [
-                jnp.concatenate(
-                    [total_second[d * tall : (d + 1) * tall, q * part : (q + 1) * part] for q in range(groups)], axis=0
-                )
-                for d in range(groups)
-            ],
-            axis=1,
-        )
-        deal(where_ref, [second, total_first], part, keep_ref, send_ref)
+    pairs = [(total_second, hidden, feature_grads), (total_first, hidden_grads, acts)]
+
+    def body(g):
+        here = slice(g * size, (g + 1) * size)
+        if g:
+            contract(g - 1, rows, pairs)
+        grad = jnp.concatenate([ref[...] for ref in grad_refs], axis=1)
+        for j, decode_ref in enumerate(decode_refs):
+            cut = slice(j * TILE, (j + 1) * TILE)
+            back = dot(grad, decode_ref[...], COLS_1).reshape(size // images, images, TILE)
+            feature_grads[here, cut] = (back + pooled_ref[:, cut][None]).astype(BF16).reshape(size, TILE)
+        hidden_back = dot(feature_grads[here], second_ref[...], COLS_1)
+        hidden_grads[here] = jnp.where(hidden[here].astype(F32) > 0, hidden_back, 0.0).astype(BF16)
+        if g == STEPS - 1:
+            contract(g, rows, pairs)
+            part = width // groups
+            tall = total_second.shape[0] // groups
+            second = jnp.concatenate(
+                [
+                    jnp.concatenate(
+                        [total_second[d * tall : (d + 1) * tall, q * part : (q + 1) * part] for q in range(groups)], axis=0
+                    )
+                    for d in range(groups)
+                ],
+                axis=1,
+            )
+            deal(where_ref, [second, total_first], part, keep_ref, send_ref)
+
+    copies = zip(copies_of([hidden_ref], hidden, sems.at[0]), copies_of([acts_ref], acts, sems.at[1]))
+    by_step([one + other for one, other in copies], body)
 
 
 def backward(where, grad, hidden, acts, decode, pooled, second, groups):
     rows, width = acts.shape
     inner, n = hidden.shape[1], len(grad) * TILE
+    n_decode = width // TILE
+    row_block = lambda j: pl.BlockSpec((TILE, n), lambda g, where: (j, 0))
     size = rows // STEPS
     parts = (groups // 2, 2 * inner, width // groups)
     dealt = pl.BlockSpec(parts, lambda g, where: (0, 0, 0))
     whole = lambda array: pl.BlockSpec(array.shape, lambda g, where: (0, 0))
     return call(
-        functools.partial(backward_kernel, groups, len(grad)),
+        functools.partial(backward_kernel, groups, len(grad), n_decode),
         [shape(parts, BF16), shape(parts, BF16)],
-        limit=44,
+        limit=58,
         flops=2 * rows * width * (n + 3 * inner),
         moved=2 * rows * (width + n + inner),
         grid_spec=pltpu.PrefetchScalarGridSpec(
@@ -426,9 +402,9 @@
             grid=(STEPS,),
             in_specs=[
                 *[pl.BlockSpec((size, TILE), lambda g, where: (g, 0))] * len(grad),
+                *[row_block(j) for j in range(n_decode)],
                 HBM,
                 HBM,
-                whole(decode),
                 whole(pooled),
                 whole(second),
             ],
@@ -444,7 +420,7 @@
             ],
         ),
         name="backward",
-    )(where, *grad, hidden, acts, decode, pooled, second)
+    )(where, *grad, *[decode] * n_decode, hidden, acts, pooled, second)
 
 
 TOPS, DENOMS = 3, 19
@@ -471,12 +447,21 @@
     return (digits[:, 0:1] * LANES + digits[:, 1:2]).astype(jnp.int32)
 
 
-def logits_kernel(where_ref, got_ref, klass_ref, logits_ref, sent_ref):
+def logits_kernel(where_ref, got_ref, klass_hbm, sent_ref, klass_ref, logits_ref, sems):
     groups, images, _ = got_ref.shape
     classes, head = klass_ref.shape
+    size = classes // sems.shape[0]
+    copies = [
+        pltpu.make_async_copy(klass_hbm.at[pl.ds(j * size, size)], klass_ref.at[pl.ds(j * size, size)], sems.at[j])
+        for j in range(sems.shape[0])
+    ]
+    for copy in copies:
+        copy.start()
     got = got_ref[...].reshape(groups * images, -1)
-    logits = dot(got[:, :head], klass_ref[...], COLS_1)
-    logits_ref[...] = logits
+    for copy in copies:
+        copy.wait()
+    logits_ref[...] = dot(got[:, :head], klass_ref[...], COLS_1)
+    logits = logits_ref[...]
     ids = lax.broadcasted_iota(jnp.int32, logits.shape, 1) + where_ref[ME] * classes
     hit = labels_of(got, head) == ids
     top = jnp.max(logits, axis=1, keepdims=True)
@@ -503,15 +488,27 @@
     classes, head = klass.shape
     return call(
         logits_kernel,
-        [shape((groups * images, classes), F32), shape((groups, images, 2 * head + LANES), BF16)],
-        limit=16,
+        shape((groups, images, 2 * head + LANES), BF16),
+        limit=58,
         flops=2e10,
-        in_specs=[SMEM, VMEM, VMEM],
+        in_specs=[SMEM, VMEM, HBM],
+        scratch_shapes=[
+            pltpu.VMEM(klass.shape, BF16),
+            pltpu.VMEM((groups * images, classes), F32),
+            pltpu.SemaphoreType.DMA((4,)),
+        ],
         name="class_logits",
     )(where, got, klass)
 
 
-def aux_kernel(pix, norm, got_ref, aux_pre_ref, aux_ref, pooled_ref, grad_ref):
+def aux_kernel(pix, norm, got_ref, aux_pre_ref, aux_hbm, pooled_ref, grad_ref, aux_ref, sems):
+    size = aux_ref.shape[0] // sems.shape[0]
+    copies = [
+        pltpu.make_async_copy(aux_hbm.at[pl.ds(j * size, size)], aux_ref.at[pl.ds(j * size, size)], sems.at[j])
+        for j in range(sems.shape[0])
+    ]
+    for copy in copies:
+        copy.start()
     groups = got_ref.shape[0]
     head = aux_pre_ref.shape[1]
     stats = [from_digits(got_ref[d, :, 2 * head :]) for d in range(groups)]
@@ -523,6 +520,8 @@
     row = sum(got_ref[d, :, head : 2 * head].astype(F32) for d in range(groups))
     back = rest + row * ((own - 1.0) / norm).astype(BF16).astype(F32)
     aux_grad = jnp.where(aux_pre_ref[...] > 0, back, 0.0).astype(BF16)
+    for copy in copies:
+        copy.wait()
     pooled_ref[...] = dot(aux_grad, aux_ref[...], COLS_1) / pix
     images, part = aux_grad.shape[0], grad_ref.shape[1]
     for q in range(head // part):
@@ -536,13 +535,15 @@
     return call(
         functools.partial(aux_kernel, pix, norm),
         [shape((images, width), F32), shape((images * head // part, part), BF16)],
-        limit=16,
+        limit=58,
         flops=2e10,
+        in_specs=[VMEM, VMEM, HBM],
+        scratch_shapes=[pltpu.VMEM(aux.shape, BF16), pltpu.SemaphoreType.DMA((4,))],
         name="aux_backward",
     )(got, aux_pre, aux)
 
 
-def class_kernel(norm, n, where_ref, logits_ref, got_ref, stats_ref, *refs):
+def class_kernel(norm, n, where_ref, klass_ref, got_ref, stats_ref, *refs):
     grads_refs, (class_ref, aux_ref) = refs[:-2], refs[-2:]
     groups, images, _ = got_ref.shape
     head = class_ref.shape[1]
@@ -555,7 +556,7 @@
         tops.append(top)
         denoms.append(sum(s[:, DENOMS + d : DENOMS + d + 1] * jnp.exp(s[:, TOPS + d : TOPS + d + 1] - top) for s in stats))
     top, denom = jnp.concatenate(tops, axis=0), jnp.concatenate(denoms, axis=0)
-    logits = logits_ref[...]
+    logits = dot(got[:, :head], klass_ref[...], COLS_1)
     ids = lax.broadcasted_iota(jnp.int32, logits.shape, 1) + where_ref[ME] * classes
     onehot = jnp.where(labels_of(got, head) == ids, 1.0, 0.0)
     logit_grad = ((jnp.exp(logits - top) / denom - onehot) / norm).astype(BF16)
@@ -572,8 +573,9 @@
     aux_ref[...] = total
 
 
-def class_backward(where, logits, got, partial, grads, n_decode, classes, head, norm):
+def class_backward(where, klass, got, partial, grads, n_decode, norm):
     groups, images, wide = partial.shape
+    classes, head = klass.shape
     whole = lambda *dims: pl.BlockSpec(dims, lambda i: (0,) * len(dims))
     part = grads[0].shape[1]
     return call(
@@ -585,14 +587,14 @@
         grid=(1,),
         in_specs=[
             SMEM,
-            whole(*logits.shape),
+            whole(*klass.shape),
             whole(*got.shape),
             pl.BlockSpec((groups, images, LANES), lambda i: (0, 0, wide // LANES - 1)),
             *[whole(*g.shape) for g in grads],
         ],
         out_specs=[whole(classes, head), whole(part, head)],
         name="class_backward",
-    )(where, logits, got, partial, *grads)
+    )(where, klass, got, partial, *grads)
 
 
 def chip_kernel(n_extra, where_ref, keep_ref, got_ref, *refs):
@@ -657,7 +659,7 @@
     scale = (groups * images * pix) ** -0.5
     norm = (groups * images) ** 0.5
     first, second, decode, aux, klass = w_first[0], w_second[0], w_decode[0], w_aux[0], w_class[0]
-    inner, head = first.shape[1], aux.shape[1]
+    inner = first.shape[1]
     n_decode = decode.shape[1]
     rows = pix * images
 
@@ -668,29 +670,24 @@
         where = jnp.stack([section & 1, me & 1, me, *tiles]).astype(jnp.int32)
         turned = patches.transpose(0, 2, 1)
         halves = [pack(where, turned, h) for h in range(2)]
-        x, y = [swap(halves[0], "section", 1)], [swap(halves[0], "section", 2)]
+        x = [swap(half, "section", 1) for half in halves]
+        y = [swap(half, "section", 2) for half in halves]
         first = after(first, halves[1])
-        labels = after(labels, (x[0], y[0]))
     else:
         where = jnp.stack([section & 1, me & 1, me]).astype(jnp.int32)
         target = lax.all_gather(patches, "section", axis=2, tiled=True).transpose(1, 0, 2)
 
-    hidden, feature, pooled = forward(acts, first, second)
-    aux_pre, sent = aux_head(pooled, aux, labels, pix, groups)
-    got = exchange(sent)
-    recon = reconstruct([after(feature[0], sent), *feature[1:]], decode)
+    hidden, feature, aux_pre, sent = forward(acts, first, second, aux, labels, groups)
     if paired:
-        last = after(halves[1], pooled)
-        x.append(swap(last, "section", 1))
-        y.append(swap(last, "section", 2))
-        diagonal = [swap(after(y[0], aux_pre), "section", 1), swap(after(x[1], recon[0]), "section", 2)]
-        blocks = [halves, x, y, diagonal]
-        target = patch_operands(blocks, [0, 1, 2, 3], [0, 1, 2, 3])
+        sent = after(sent, (x[0], y[0]))
+        diagonal = [swap(after(y[0], aux_pre), "section", 1), swap(after(x[1], aux_pre), "section", 2)]
+        target = patch_operands([halves, x, y, diagonal], [0, 1, 2, 3], [0, 1, 2, 3])
     else:
         target = [target], [pl.BlockSpec((pix // STEPS, images, n_decode), lambda g, where: (g, 0, 0))]
-    logits, sent = class_logits(where, after(got, recon[0]), klass)
+    got = exchange(sent)
+    sent = class_logits(where, got, klass)
     partial = exchange(sent)
-    grad, keep, send = residual(after(where, sent), feature, recon, *target, images, scale, groups)
+    grad, keep, send = residual(after(where, sent), feature, decode, *target, images, scale, groups)
     pooled_grad, aux_grad = aux_backward(partial, aux_pre, aux, pix, norm)
     chip_decode = add_cores(where, keep, send, [aux_grad])
     sum_decode = exchange_chips(chip_decode)
@@ -698,9 +695,7 @@
         where, grad, hidden, acts.reshape(rows, width), decode, after(pooled_grad, chip_decode[0]), second, groups
     )
     sum_last = exchange_chips(add_cores(where, keep, after(send, sum_decode)))
-    grad_class, grad_aux = class_backward(
-        where, logits, got, partial, sum_decode, n_decode, klass.shape[0], head, norm
-    )
+    grad_class, grad_aux = class_backward(where, klass, got, partial, sum_decode, n_decode, norm)
     grad_first, grad_second, grad_decode = finish(sum_decode, sum_last, inner, groups, n_decode)
     return grad_first[None], grad_second[None], grad_decode[None], grad_aux[None], grad_class[None]
 

time: 119 us -> 126 us (1.059)
  waiting for transfers between devices: 15.6 us -> 29.9 us
  starting transfers between devices: 30.7 us -> 26.7 us
  local copies, waits for them, and re-layouts: 7.44 us -> 4.69 us
  Pallas kernels: 64.4 us -> 62.8 us
    ppermute x15, waiting for transfers between devices: 15.5 us -> 29.6 us  [swap(): return lax.ppermute(value, axis, [(i, i ^ bits) for i in range(count)])]
    pallas_call x6 -> x4, Pallas kernels: 54.5 us -> 50.3 us  [the longest x1 18.8 us: residual(): call(functools.partial(residual_kernel, groups, scale, len(feature), n_ti...]
    ppermute x15, starting transfers between devices: 20.4 us -> 16.8 us  [swap(): return lax.ppermute(value, axis, [(i, i ^ bits) for i in range(count)])]
    unnamed x34 -> x36, local copies, waits for them, and re-layouts: 7.36 us -> 4.6 us
    pallas_call x1, Pallas kernels: 0.64 us -> 3.21 us  [aux_backward(): call(functools.partial(aux_kernel, pix, norm), [shape((images, width), F3...]
  transfers between devices with their start and end apart: 17 -> 17, of which waited for: 6 -> 10; matrix products, arithmetic and copies ran while one was open for 0% -> 0% of each run, Pallas kernels for 51% -> 47%
where the time goes in v8:
time: 126 us; the launch traced here: 125 us
  Pallas kernels  62.8 us (50%)
  waiting for transfers between devices  29.9 us (24%)
  starting transfers between devices  26.7 us (21%)
  local copies, waits for them, and re-layouts  4.69 us (4%)
    ppermute x15, waiting for transfers between devices, swap(): return lax.ppermute(value, axis, [(i, i ^ bits) for i in range(count)])  29.6 us
    pallas_call x1, Pallas kernels, residual(): call(functools.partial(residual_kernel, groups, scale, len(feature), n_ti...  18.8 us
    pallas_call x1, Pallas kernels, backward(): call(functools.partial(backward_kernel, groups, len(grad), n_decode), [sh...  17.4 us
    ppermute x15, starting transfers between devices, swap(): return lax.ppermute(value, axis, [(i, i ^ bits) for i in range(count)])  16.8 us
    all_to_all x2, starting transfers between devices, exchange(): lax.all_to_all(value, 'dp', 0, 0, axis_index_groups=groups, tiled=True)  9.96 us
    pallas_call x1, Pallas kernels, forward(): call(functools.partial(forward_kernel, n_tiles, pix), [shape((pix * image...  9.65 us
    unnamed x36, local copies, waits for them, and re-layouts  4.6 us
    pallas_call x1, Pallas kernels, class_logits(): call(logits_kernel, shape((groups, images, 2 * head + LANES), BF16), limi...  4.4 us
  transfers between devices with their start and end apart: 17, of which 10 were waited for; matrix products, arithmetic and copies ran while one was open for 0% of the time, Pallas kernels for 47%

profile of v8, /device:TPU:0, one launch (start us, length us, event | category | flops | bytes accessed | tf_op | source)
XLA Modules:
  0.0 125.0 jit_solution(10681149294311741416)
XLA Ops:
  0.7 0.1 stack.47.where_ref
  0.7 0.0 copy-start
  0.8 1.4 %copy-done = bf16[16,196,192]{1,2,0:T(8,128)(2,1)S(1)} copy-done((bf16[16,196,192]{1,2,0:T(8,128)(2,1)S(1)}, bf16[16,196,192]{1,2,0:T(8,128)(2,1)}, u32[]{:S(2)}) %copy-start) | copy-done | bytes 1204248
  2.2 1.8 %pack_patches.3.refs_7_.refs_15_ = bf16[147,16,128]{2,1,0:T(8,128)(2,1)S(1)} custom-call(s32[11]{0:T(128)S(1)} %stack.47.where_ref, bf16[16,192,196]{2,1,0:T(8,128)(2,1)S(1)} %bitcast.27), custom_call_target="tpu_custom_call" | custom-call | tf_op jit(solution)/shard_map/pack_patches/pallas_call | solution.py:92
  4.0 3.0 %collective-permute-start.1 = (bf16[147,16,128]{2,1,0:T(8,128)(2,1)S(1)}, bf16[147,16,128]{2,1,0:T(8,128)(2,1)S(1)}, u32[]{:S(2)}, u32[]{:S(2)}) collective-permute-start(bf16[147,16,128]{2,1,0:T(8,128)(2,1)S(1)} %pack_patches.3.refs_7_.refs_15_), channel_id=1, source_target_pairs={{0,16},{8,24},{16,0},{24,8},{1,17},{9,25},{17,1},{25,9},{2,18},{10... | collective-permute-start | bytes 1806344 | tf_op jit(solution)/shard_map/ppermute | solution.py:46
  7.0 1.5 %collective-permute-start = (bf16[147,16,128]{2,1,0:T(8,128)(2,1)S(1)}, bf16[147,16,128]{2,1,0:T(8,128)(2,1)S(1)}, u32[]{:S(2)}, u32[]{:S(2)}) collective-permute-start(bf16[147,16,128]{2,1,0:T(8,128)(2,1)S(1)} %pack_patches.3.refs_7_.refs_15_), channel_id=1, source_target_pairs={{0,8},{8,0},{16,24},{24,16},{1,9},{9,1},{17,25},{25,17},{2,10},{10... | collective-permute-start | bytes 1806344 | tf_op jit(solution)/shard_map/ppermute | solution.py:46
  8.5 1.8 %pack_patches.2.refs_8_.refs_16_ = bf16[147,16,128]{2,1,0:T(8,128)(2,1)S(1)} custom-call(s32[11]{0:T(128)S(1)} %stack.47.where_ref, bf16[16,192,196]{2,1,0:T(8,128)(2,1)S(1)} %bitcast.28), custom_call_target="tpu_custom_call" | custom-call | tf_op jit(solution)/shard_map/pack_patches/pallas_call | solution.py:92
  10.4 0.6 collective-permute-start.2
  11.0 9.7 %forward.1 = (bf16[3136,256]{1,0:T(8,128)(2,1)}, bf16[3136,256]{1,0:T(8,128)(2,1)}, bf16[3136,256]{1,0:T(8,128)(2,1)}, bf16[3136,256]{1,0:T(8,128)(2,1)}, bf16[3...) custom-call(bf16[196,16,1024]{2,1,0:T(8,128)(2,1)} %bitcast.31, ...), custom_call_target="tpu_custom_call" | custom-call | flops 3288334336 | bytes 14450688 | tf_op jit(solution)/shard_map/forward/pallas_call | solution.py:162
  20.6 2.9 %collective-permute-done.refs_9_.refs_17_ = bf16[147,16,128]{2,1,0:T(8,128)(2,1)S(1)} collective-permute-done((bf16[147,16,128]{2,1,0:T(8,128)(2,1)S(1)}, bf16[147,16,128]{2,1,0:T(8,128)(2,1)S(1)}, u32[]{:S(2)}, u32[]{:S(2)}) %collective-permute-start) | collective-permute-done | bytes 602144 | tf_op jit(solution)/shard_map/ppermute | solution.py:46
  23.5 4.9 %all-to-all-start = ((bf16[8,16,768]{2,1,0:T(8,128)(2,1)}), bf16[8,16,768]{2,1,0:T(8,128)(2,1)S(1)}, u32[]{:S(2)}, u32[]{:S(2)}) async-start(bf16[8,16,768]{2,1,0:T(8,128)(2,1)} %get-tuple-element.43), calls=%async_computation | async-start | bytes 393216 | tf_op jit(solution)/shard_map/all_to_all | solution.py:50
  28.4 0.6 collective-permute-start.3
  29.0 1.5 %collective-permute-start.4 = (bf16[147,16,128]{2,1,0:T(8,128)(2,1)S(1)}, bf16[147,16,128]{2,1,0:T(8,128)(2,1)}, u32[]{:S(2)}, u32[]{:S(2)}) collective-permute-start(bf16[147,16,128]{2,1,0:T(8,128)(2,1)S(1)} %collective-permute-done.1.refs_11_.refs_19_), channel_id=1, source_target_pairs={{0,8},{8,0},{16,24},{24,16},{1,9},{9,1},{17,25},{25,17},{2,10},{10... | collective-permute-start | bytes 1806344 | tf_op jit(solution)/shard_map/ppermute | solution.py:46
  30.5 5.9 %collective-permute-done.2.refs_10_.refs_18_ = bf16[147,16,128]{2,1,0:T(8,128)(2,1)S(1)} collective-permute-done((bf16[147,16,128]{2,1,0:T(8,128)(2,1)S(1)}, bf16[147,16,128]{2,1,0:T(8,128)(2,1)S(1)}, u32[]{:S(2)}, u32[]{:S(2)}) %collective-permute-start.2) | collective-permute-done | bytes 602144 | tf_op jit(solution)/shard_map/ppermute | solution.py:46
  36.4 0.0 collective-permute-start.5
  36.5 0.3 all-to-all-done.got_ref
  36.8 0.7 copy-done.4
  37.4 4.4 %class_logits.1 = bf16[8,16,1152]{2,1,0:T(8,128)(2,1)} custom-call(s32[11]{0:T(128)} %copy-done.10, bf16[8,16,768]{2,1,0:T(8,128)(2,1)} %copy-done.4, bf16[1408,512]{1,0:T(8,128)(2,1)} %bitcast.29), custom_call_target="tpu_custom_call" | custom-call | flops 20000000000 | tf_op jit(solution)/shard_map/class_logits/pallas_call | solution.py:489
  41.9 5.1 %all-to-all-start.1 = ((bf16[8,16,1152]{2,1,0:T(8,128)(2,1)}), bf16[8,16,1152]{2,1,0:T(8,128)(2,1)S(1)}, u32[]{:S(2)}, u32[]{:S(2)}) async-start(bf16[8,16,1152]{2,1,0:T(8,128)(2,1)} %class_logits.1), calls=%async_computation.1 | async-start | bytes 589824 | tf_op jit(solution)/shard_map/all_to_all | solution.py:50
  47.0 0.0 collective-permute-done.3.refs_12_.refs_20_
  47.0 1.0 collective-permute-done.4.refs_13_.refs_21_
  48.0 9.4 %collective-permute-done.5.refs_14_.refs_22_ = bf16[147,16,128]{2,1,0:T(8,128)(2,1)} collective-permute-done((bf16[147,16,128]{2,1,0:T(8,128)(2,1)S(1)}, bf16[147,16,128]{2,1,0:T(8,128)(2,1)}, u32[]{:S(2)}, u32[]{:S(2)}) %collective-permute-start.5) | collective-permute-done | bytes 602144 | tf_op jit(solution)/shard_map/ppermute | solution.py:46
  57.4 18.8 %residual.1 = (bf16[3136,256]{1,0:T(8,128)(2,1)}, bf16[3136,256]{1,0:T(8,128)(2,1)}, bf16[3136,256]{1,0:T(8,128)(2,1)}, bf16[4,768,128]{2,1,0:T(8,128)(2,1)}, bf16[4,768,128]{2,1,0:T(8,128)(2,1)}) custom-call(s32[11]{0:T(128)} %copy-done.10, bf16[3136,256]{1,0:T(8,128)(2,1)} %get-tuple-element.45.refs_0_, bf16[3136,256]{1,0:T(8,128)(2,1)} %get-tuple-element.46.refs_1_, ...), custom_call_target="tpu_custom_call" | custom-call | flops 9865003008 | bytes 20873216 | tf_op jit(solution)/shard_map/residual/pallas_call | solution.py:321
  76.3 0.1 collective-permute-start.6
  76.4 0.0 all-to-all-done.1.got_ref.stats_ref
  76.4 0.0 copy-start.2
  76.4 0.7 copy-done.2
  77.1 3.2 %aux_backward.1 = (f32[16,1024]{1,0:T(8,128)}, bf16[64,128]{1,0:T(8,128)(2,1)}) custom-call(bf16[8,16,1152]{2,1,0:T(8,128)(2,1)} %copy-done.2, f32[16,512]{1,0:T(8,128)} %get-tuple-element.49.aux_pre_ref, bf16[1024,512]{1,0:T(8,128)(2,1)} %bitcast.37), custom_call_target="tpu_custom_call" | custom-call | flops 20000000000 | tf_op jit(solution)/shard_map/aux_backward/pallas_call | solution.py:535
  80.3 0.6 collective-permute-start.7
  80.9 1.0 collective-permute-done.7.refs_1_
  81.9 0.0 collective-permute-done.6.got_ref
  81.9 0.7 copy-done.13
  82.6 0.7 add_cores.2
  83.4 3.5 %collective-permute-start.10 = (bf16[896,128]{1,0:T(8,128)(2,1)S(1)}, bf16[896,128]{1,0:T(8,128)(2,1)S(1)}, u32[]{:S(2)}, u32[]{:S(2)}) collective-permute-start(bf16[896,128]{1,0:T(8,128)(2,1)S(1)} %get-tuple-element.58), channel_id=1, source_target_pairs={{0,6},{1,7},{2,4},{3,5},{4,2},{5,3},{6,0},{7,1},{8,14},{9,15},{10,... | collective-permute-start | bytes 688136 | tf_op jit(solution)/shard_map/ppermute | solution.py:46
  86.9 0.0 collective-permute-start.8
  86.9 0.9 collective-permute-start.9
  87.9 17.4 %backward.1 = (bf16[4,512,128]{2,1,0:T(8,128)(2,1)}, bf16[4,512,128]{2,1,0:T(8,128)(2,1)}) custom-call(s32[11]{0:T(128)} %copy-done.10, bf16[3136,256]{1,0:T(8,128)(2,1)} %get-tuple-element.59.refs_0_, bf16[3136,256]{1,0:T(8,128)(2,1)} %get-tuple-element.60.refs_1_, bf16[3136,256]{1,0:T(8,128)(2,1)} %get-tuple-element.61.refs_2_, ...), custom_call_target="tpu_custom_call" | custom-call | flops 9865003008 | bytes 12845056 | tf_op jit(solution)/shard_map/backward/pallas_call | solution.py:394
  105.3 1.8 %collective-permute-done.9.refs_2_ = bf16[896,128]{1,0:T(8,128)(2,1)S(1)} collective-permute-done((bf16[896,128]{1,0:T(8,128)(2,1)S(1)}, bf16[896,128]{1,0:T(8,128)(2,1)S(1)}, u32[]{:S(2)}, u32[]{:S(2)}) %collective-permute-start.9) | collective-permute-done | bytes 229408 | tf_op jit(solution)/shard_map/ppermute | solution.py:46
  107.2 2.1 %collective-permute-done.11.got_ref = bf16[4,512,128]{2,1,0:T(8,128)(2,1)S(1)} collective-permute-done((bf16[4,512,128]{2,1,0:T(8,128)(2,1)}, bf16[4,512,128]{2,1,0:T(8,128)(2,1)S(1)}, u32[]{:S(2)}, u32[]{:S(2)}) %collective-permute-start.11) | collective-permute-done | bytes 524320 | tf_op jit(solution)/shard_map/ppermute | solution.py:46
  109.3 1.0 copy-done.9
  110.3 0.7 add_cores.3
  111.0 0.1 collective-permute-start.12
  111.1 2.9 %collective-permute-start.13 = (bf16[512,128]{1,0:T(8,128)(2,1)S(1)}, bf16[512,128]{1,0:T(8,128)(2,1)S(1)}, u32[]{:S(2)}, u32[]{:S(2)}) collective-permute-start(bf16[512,128]{1,0:T(8,128)(2,1)S(1)} %get-tuple-element.70), channel_id=1, source_target_pairs={{0,4},{1,5},{2,6},{3,7},{4,0},{5,1},{6,2},{7,3},{8,12},{9,13},{10,... | collective-permute-start | bytes 393224 | tf_op jit(solution)/shard_map/ppermute | solution.py:46
  114.0 1.5 %collective-permute-start.14 = (bf16[512,128]{1,0:T(8,128)(2,1)S(1)}, bf16[512,128]{1,0:T(8,128)(2,1)S(1)}, u32[]{:S(2)}, u32[]{:S(2)}) collective-permute-start(bf16[512,128]{1,0:T(8,128)(2,1)S(1)} %get-tuple-element.71), channel_id=1, source_target_pairs={{0,6},{1,7},{2,4},{3,5},{4,2},{5,3},{6,0},{7,1},{8,14},{9,15},{10,... | collective-permute-start | bytes 393224 | tf_op jit(solution)/shard_map/ppermute | solution.py:46
  115.5 3.3 %class_backward.1 = (f32[1408,512]{1,0:T(8,128)}, f32[128,512]{1,0:T(8,128)}) custom-call(s32[11]{0:T(128)S(1)} %copy-done.12, bf16[1408,512]{1,0:T(8,128)(2,1)S(1)} %bitcast.30, bf16[8,16,768]{2,1,0:T(8,128)(2,1)S(1)} %copy-done.5, bf16[8,16,1152]{2,1,0:T(8,128)(2,1)S(1)} %copy-done.3, bf16[896,128]{1,0:T(8,128)(2,1)S(1)} %get-tuple-element.55.refs_0_, ...), custom_call_target="tpu_custom_call" | custom-call | flops 184549376 | bytes 2883584 | tf_op jit(solution)/shard_map/class_backward/pallas_call | solution.py:581
  118.8 0.1 collective-permute-done.12.refs_5_
  118.9 5.2 %collective-permute-done.13.refs_6_ = bf16[512,128]{1,0:T(8,128)(2,1)S(1)} collective-permute-done((bf16[512,128]{1,0:T(8,128)(2,1)S(1)}, bf16[512,128]{1,0:T(8,128)(2,1)S(1)}, u32[]{:S(2)}, u32[]{:S(2)}) %collective-permute-start.13) | collective-permute-done | bytes 131104 | tf_op jit(solution)/shard_map/ppermute | solution.py:46
  124.1 1.0 finish.1
  (34 shorter events, 0.1 us)
Async XLA Ops:
  0.7 9.6 %copy-start.10 = (s32[11]{0:T(128)}, s32[11]{0:T(128)S(1)}, u32[]{:S(2)}) copy-start(s32[11]{0:T(128)S(1)} %stack.47.where_ref) | copy-start | bytes 136
  0.7 1.4 %copy-start = (bf16[16,196,192]{1,2,0:T(8,128)(2,1)S(1)}, bf16[16,196,192]{1,2,0:T(8,128)(2,1)}, u32[]{:S(2)}) copy-start(bf16[16,196,192]{1,2,0:T(8,128)(2,1)} %param.9) | copy-start | bytes 3612676
  4.0 16.6 %copy-start.7 = (bf16[147,16,128]{2,1,0:T(8,128)(2,1)}, bf16[147,16,128]{2,1,0:T(8,128)(2,1)S(1)}, u32[]{:S(2)}) copy-start(bf16[147,16,128]{2,1,0:T(8,128)(2,1)S(1)} %pack_patches.3.refs_7_.refs_15_) | copy-start | bytes 1806340
  4.0 16.6 %collective-permute-start.1 = (bf16[147,16,128]{2,1,0:T(8,128)(2,1)S(1)}, bf16[147,16,128]{2,1,0:T(8,128)(2,1)S(1)}, u32[]{:S(2)}, u32[]{:S(2)}) collective-permute-start(bf16[147,16,128]{2,1,0:T(8,128)(2,1)S(1)} %pack_patches.3.refs_7_.refs_15_), channel_id=1, source_target_pairs={{0,16},{8,24},{16,0},{24,8},{1,17},{9,25},{17,1},{25,9},{2,18},{10... | collective-permute-start | bytes 1806344 | tf_op jit(solution)/shard_map/ppermute | solution.py:46
  7.0 16.5 %collective-permute-start = (bf16[147,16,128]{2,1,0:T(8,128)(2,1)S(1)}, bf16[147,16,128]{2,1,0:T(8,128)(2,1)S(1)}, u32[]{:S(2)}, u32[]{:S(2)}) collective-permute-start(bf16[147,16,128]{2,1,0:T(8,128)(2,1)S(1)} %pack_patches.3.refs_7_.refs_15_), channel_id=1, source_target_pairs={{0,8},{8,0},{16,24},{24,16},{1,9},{9,1},{17,25},{25,17},{2,10},{10... | collective-permute-start | bytes 1806344 | tf_op jit(solution)/shard_map/ppermute | solution.py:46
  10.3 18.1 %copy-start.8 = (bf16[147,16,128]{2,1,0:T(8,128)(2,1)}, bf16[147,16,128]{2,1,0:T(8,128)(2,1)S(1)}, u32[]{:S(2)}) copy-start(bf16[147,16,128]{2,1,0:T(8,128)(2,1)S(1)} %pack_patches.2.refs_8_.refs_16_) | copy-start | bytes 1806340
  10.4 26.1 %collective-permute-start.2 = (bf16[147,16,128]{2,1,0:T(8,128)(2,1)S(1)}, bf16[147,16,128]{2,1,0:T(8,128)(2,1)S(1)}, u32[]{:S(2)}, u32[]{:S(2)}) collective-permute-start(bf16[147,16,128]{2,1,0:T(8,128)(2,1)S(1)} %pack_patches.2.refs_8_.refs_16_), channel_id=1, source_target_pairs={{0,8},{8,0},{16,24},{24,16},{1,9},{9,1},{17,25},{25,17},{2,10},{10... | collective-permute-start | bytes 1806344 | tf_op jit(solution)/shard_map/ppermute | solution.py:46
  20.6 21.2 %copy-start.14 = (bf16[147,16,128]{2,1,0:T(8,128)(2,1)}, bf16[147,16,128]{2,1,0:T(8,128)(2,1)S(1)}, u32[]{:S(2)}) copy-start(bf16[147,16,128]{2,1,0:T(8,128)(2,1)S(1)} %collective-permute-done.1.refs_11_.refs_19_) | copy-start | bytes 1806340
  23.5 18.3 %copy-start.15 = (bf16[147,16,128]{2,1,0:T(8,128)(2,1)}, bf16[147,16,128]{2,1,0:T(8,128)(2,1)S(1)}, u32[]{:S(2)}) copy-start(bf16[147,16,128]{2,1,0:T(8,128)(2,1)S(1)} %collective-permute-done.refs_9_.refs_17_) | copy-start | bytes 1806340
  23.5 13.2 %all-to-all-start = ((bf16[8,16,768]{2,1,0:T(8,128)(2,1)}), bf16[8,16,768]{2,1,0:T(8,128)(2,1)S(1)}, u32[]{:S(2)}, u32[]{:S(2)}) async-start(bf16[8,16,768]{2,1,0:T(8,128)(2,1)} %get-tuple-element.43), calls=%async_computation | async-start | bytes 393216 | tf_op jit(solution)/shard_map/all_to_all | solution.py:50
  28.4 18.5 %collective-permute-start.3 = (bf16[147,16,128]{2,1,0:T(8,128)(2,1)S(1)}, bf16[147,16,128]{2,1,0:T(8,128)(2,1)S(1)}, u32[]{:S(2)}, u32[]{:S(2)}) collective-permute-start(bf16[147,16,128]{2,1,0:T(8,128)(2,1)S(1)} %pack_patches.2.refs_8_.refs_16_), channel_id=1, source_target_pairs={{0,16},{8,24},{16,0},{24,8},{1,17},{9,25},{17,1},{25,9},{2,18},{10... | collective-permute-start | bytes 1806344 | tf_op jit(solution)/shard_map/ppermute | solution.py:46
  29.0 19.0 %collective-permute-start.4 = (bf16[147,16,128]{2,1,0:T(8,128)(2,1)S(1)}, bf16[147,16,128]{2,1,0:T(8,128)(2,1)}, u32[]{:S(2)}, u32[]{:S(2)}) collective-permute-start(bf16[147,16,128]{2,1,0:T(8,128)(2,1)S(1)} %collective-permute-done.1.refs_11_.refs_19_), channel_id=1, source_target_pairs={{0,8},{8,0},{16,24},{24,16},{1,9},{9,1},{17,25},{25,17},{2,10},{10... | collective-permute-start | bytes 1806344 | tf_op jit(solution)/shard_map/ppermute | solution.py:46
  36.4 5.4 %copy-start.16 = (bf16[147,16,128]{2,1,0:T(8,128)(2,1)}, bf16[147,16,128]{2,1,0:T(8,128)(2,1)S(1)}, u32[]{:S(2)}) copy-start(bf16[147,16,128]{2,1,0:T(8,128)(2,1)S(1)} %collective-permute-done.2.refs_10_.refs_18_) | copy-start | bytes 1806340
  36.4 21.0 %collective-permute-start.5 = (bf16[147,16,128]{2,1,0:T(8,128)(2,1)S(1)}, bf16[147,16,128]{2,1,0:T(8,128)(2,1)}, u32[]{:S(2)}, u32[]{:S(2)}) collective-permute-start(bf16[147,16,128]{2,1,0:T(8,128)(2,1)S(1)} %collective-permute-done.2.refs_10_.refs_18_), channel_id=1, source_target_pairs={{0,16},{8,24},{16,0},{24,8},{1,17},{9,25},{17,1},{25,9},{2,18},{10... | collective-permute-start | bytes 1806344 | tf_op jit(solution)/shard_map/ppermute | solution.py:46
  36.8 0.7 copy-start.4
  41.9 34.5 %all-to-all-start.1 = ((bf16[8,16,1152]{2,1,0:T(8,128)(2,1)}), bf16[8,16,1152]{2,1,0:T(8,128)(2,1)S(1)}, u32[]{:S(2)}, u32[]{:S(2)}) async-start(bf16[8,16,1152]{2,1,0:T(8,128)(2,1)} %class_logits.1), calls=%async_computation.1 | async-start | bytes 589824 | tf_op jit(solution)/shard_map/all_to_all | solution.py:50
  47.0 10.5 %copy-start.17 = (bf16[147,16,128]{2,1,0:T(8,128)(2,1)}, bf16[147,16,128]{2,1,0:T(8,128)(2,1)S(1)}, u32[]{:S(2)}) copy-start(bf16[147,16,128]{2,1,0:T(8,128)(2,1)S(1)} %collective-permute-done.3.refs_12_.refs_20_) | copy-start | bytes 1806340
  76.3 5.6 %copy-start.6 = (bf16[4,768,128]{2,1,0:T(8,128)(2,1)S(1)}, bf16[4,768,128]{2,1,0:T(8,128)(2,1)}, u32[]{:S(2)}) copy-start(bf16[4,768,128]{2,1,0:T(8,128)(2,1)} %get-tuple-element.52.keep_ref) | copy-start | bytes 2359300
  76.3 5.6 %copy-start.11 = (s32[11]{0:T(128)S(1)}, s32[11]{0:T(128)}, u32[]{:S(2)}) copy-start(s32[11]{0:T(128)} %copy-done.10) | copy-start | bytes 136
  76.3 5.6 %collective-permute-start.6 = (bf16[4,768,128]{2,1,0:T(8,128)(2,1)}, bf16[4,768,128]{2,1,0:T(8,128)(2,1)S(1)}, u32[]{:S(2)}, u32[]{:S(2)}) collective-permute-start(bf16[4,768,128]{2,1,0:T(8,128)(2,1)} %get-tuple-element.53), channel_id=1, source_target_pairs={{0,1},{1,0},{2,3},{3,2},{4,5},{5,4},{6,7},{7,6},{8,9},{9,8},{10,11... | collective-permute-start | bytes 2359304 | tf_op jit(solution)/shard_map/ppermute | solution.py:46
  76.4 0.7 copy-start.2
  80.3 1.6 %collective-permute-start.7 = (bf16[64,128]{1,0:T(8,128)(2,1)}, bf16[64,128]{1,0:T(8,128)(2,1)S(1)}, u32[]{:S(2)}, u32[]{:S(2)}) collective-permute-start(bf16[64,128]{1,0:T(8,128)(2,1)} %get-tuple-element.54.refs_0_), channel_id=1, source_target_pairs={{0,1},{1,0},{2,3},{3,2},{4,5},{5,4},{6,7},{7,6},{8,9},{9,8},{10,11... | collective-permute-start | bytes 49160 | tf_op jit(solution)/shard_map/ppermute | solution.py:46
  81.9 0.7 copy-start.13
  83.4 21.9 %collective-permute-start.10 = (bf16[896,128]{1,0:T(8,128)(2,1)S(1)}, bf16[896,128]{1,0:T(8,128)(2,1)S(1)}, u32[]{:S(2)}, u32[]{:S(2)}) collective-permute-start(bf16[896,128]{1,0:T(8,128)(2,1)S(1)} %get-tuple-element.58), channel_id=1, source_target_pairs={{0,6},{1,7},{2,4},{3,5},{4,2},{5,3},{6,0},{7,1},{8,14},{9,15},{10,... | collective-permute-start | bytes 688136 | tf_op jit(solution)/shard_map/ppermute | solution.py:46
  86.9 18.4 %collective-permute-start.8 = (bf16[896,128]{1,0:T(8,128)(2,1)S(1)}, bf16[896,128]{1,0:T(8,128)(2,1)S(1)}, u32[]{:S(2)}, u32[]{:S(2)}) collective-permute-start(bf16[896,128]{1,0:T(8,128)(2,1)S(1)} %get-tuple-element.56), channel_id=1, source_target_pairs={{0,2},{1,3},{2,0},{3,1},{4,6},{5,7},{6,4},{7,5},{8,10},{9,11},{10,... | collective-permute-start | bytes 688136 | tf_op jit(solution)/shard_map/ppermute | solution.py:46
  86.9 20.2 %collective-permute-start.9 = (bf16[896,128]{1,0:T(8,128)(2,1)S(1)}, bf16[896,128]{1,0:T(8,128)(2,1)S(1)}, u32[]{:S(2)}, u32[]{:S(2)}) collective-permute-start(bf16[896,128]{1,0:T(8,128)(2,1)S(1)} %get-tuple-element.57), channel_id=1, source_target_pairs={{0,4},{1,5},{2,6},{3,7},{4,0},{5,1},{6,2},{7,3},{8,12},{9,13},{10,... | collective-permute-start | bytes 688136 | tf_op jit(solution)/shard_map/ppermute | solution.py:46
  87.8 21.4 %copy-start.12 = (s32[11]{0:T(128)S(1)}, s32[11]{0:T(128)}, u32[]{:S(2)}) copy-start(s32[11]{0:T(128)} %copy-done.10) | copy-start | bytes 136
  87.8 27.6 %copy-start.1 = (bf16[1,1408,512]{2,1,0:T(8,128)(2,1)S(1)}, bf16[1,1408,512]{2,1,0:T(8,128)(2,1)}, u32[]{:S(2)}) copy-start(bf16[1,1408,512]{2,1,0:T(8,128)(2,1)} %param.15) | copy-start | bytes 4325380
  87.8 27.6 %copy-start.3 = (bf16[8,16,1152]{2,1,0:T(8,128)(2,1)S(1)}, bf16[8,16,1152]{2,1,0:T(8,128)(2,1)}, u32[]{:S(2)}) copy-start(bf16[8,16,1152]{2,1,0:T(8,128)(2,1)} %copy-done.2) | copy-start | bytes 884740
  87.8 27.6 %copy-start.5 = (bf16[8,16,768]{2,1,0:T(8,128)(2,1)S(1)}, bf16[8,16,768]{2,1,0:T(8,128)(2,1)}, u32[]{:S(2)}) copy-start(bf16[8,16,768]{2,1,0:T(8,128)(2,1)} %copy-done.4) | copy-start | bytes 589828
  107.2 2.1 %collective-permute-start.11 = (bf16[4,512,128]{2,1,0:T(8,128)(2,1)}, bf16[4,512,128]{2,1,0:T(8,128)(2,1)S(1)}, u32[]{:S(2)}, u32[]{:S(2)}) collective-permute-start(bf16[4,512,128]{2,1,0:T(8,128)(2,1)} %get-tuple-element.67), channel_id=1, source_target_pairs={{0,1},{1,0},{2,3},{3,2},{4,5},{5,4},{6,7},{7,6},{8,9},{9,8},{10,11... | collective-permute-start | bytes 1572872 | tf_op jit(solution)/shard_map/ppermute | solution.py:46
  109.3 1.0 copy-start.9
  111.0 7.9 %collective-permute-start.12 = (bf16[512,128]{1,0:T(8,128)(2,1)S(1)}, bf16[512,128]{1,0:T(8,128)(2,1)S(1)}, u32[]{:S(2)}, u32[]{:S(2)}) collective-permute-start(bf16[512,128]{1,0:T(8,128)(2,1)S(1)} %get-tuple-element.69), channel_id=1, source_target_pairs={{0,2},{1,3},{2,0},{3,1},{4,6},{5,7},{6,4},{7,5},{8,10},{9,11},{10,... | collective-permute-start | bytes 393224 | tf_op jit(solution)/shard_map/ppermute | solution.py:46
  111.1 13.0 %collective-permute-start.13 = (bf16[512,128]{1,0:T(8,128)(2,1)S(1)}, bf16[512,128]{1,0:T(8,128)(2,1)S(1)}, u32[]{:S(2)}, u32[]{:S(2)}) collective-permute-start(bf16[512,128]{1,0:T(8,128)(2,1)S(1)} %get-tuple-element.70), channel_id=1, source_target_pairs={{0,4},{1,5},{2,6},{3,7},{4,0},{5,1},{6,2},{7,3},{8,12},{9,13},{10,... | collective-permute-start | bytes 393224 | tf_op jit(solution)/shard_map/ppermute | solution.py:46
  114.0 10.1 %collective-permute-start.14 = (bf16[512,128]{1,0:T(8,128)(2,1)S(1)}, bf16[512,128]{1,0:T(8,128)(2,1)S(1)}, u32[]{:S(2)}, u32[]{:S(2)}) collective-permute-start(bf16[512,128]{1,0:T(8,128)(2,1)S(1)} %get-tuple-element.71), channel_id=1, source_target_pairs={{0,6},{1,7},{2,4},{3,5},{4,2},{5,3},{6,0},{7,1},{8,14},{9,15},{10,... | collective-permute-start | bytes 393224 | tf_op jit(solution)/shard_map/ppermute | solution.py:46

commit v9 on v8

--- a/solution.py
+++ b/solution.py
@@ -50,8 +50,10 @@
     return lax.all_to_all(value, "dp", 0, 0, axis_index_groups=groups, tiled=True)
 
 
-def pack_kernel(first, where_ref, patches_ref, out_ref, turned, own, shared):
-    images, span, pix = patches_ref.shape
+def pack_kernel(first, where_ref, *refs):
+    patches_refs, (out_ref, turned, own, shared) = refs[:-4], refs[-4:]
+    several, span, pix = patches_refs[0].shape
+    images = turned.shape[0]
     padded = turned.shape[1]
     count = out_ref.shape[0] // 3 * 2
     parity = where_ref[PARITY]
@@ -61,8 +63,9 @@
     column = lax.broadcasted_iota(jnp.int32, (padded, pix), 1)
     pick = ((row < count) & (column == row + first)).astype(F32).astype(BF16)
     for i in range(images):
-        turned[i, :, :LANES] = dot(pick, patches_ref[i, pl.ds(at_own, LANES), :], COLS_1).astype(BF16)
-        turned[i, :, LANES:] = dot(pick, patches_ref[i, pl.ds(at_shared, 64), :], COLS_1).astype(BF16)
+        patches_ref, j = patches_refs[i // several], i % several
+        turned[i, :, :LANES] = dot(pick, patches_ref[j, pl.ds(at_own, LANES), :], COLS_1).astype(BF16)
+        turned[i, :, LANES:] = dot(pick, patches_ref[j, pl.ds(at_shared, 64), :], COLS_1).astype(BF16)
     size = 16 * images
     row = lax.broadcasted_iota(jnp.int32, (size, size), 0)
     column = lax.broadcasted_iota(jnp.int32, (size, size), 1)
@@ -89,18 +92,24 @@
     images, span, pix = patches.shape
     half = pix // 2
     padded = -(-half // 16) * 16
+    several = images // 4
+    lanes = LANES if h == 0 and half <= LANES < pix else pix
+    group = lambda j: pl.BlockSpec((several, span, lanes), lambda i: (j, 0, 0))
+    dims = (half + half // 2, images, LANES)
     return call(
         functools.partial(pack_kernel, h * half),
-        shape((half + half // 2, images, LANES), BF16),
+        shape(dims, BF16),
         limit=20,
-        in_specs=[SMEM, VMEM],
+        grid=(1,),
+        in_specs=[SMEM, *[group(j) for j in range(4)]],
+        out_specs=pl.BlockSpec(dims, lambda i: (0, 0, 0)),
         scratch_shapes=[
             pltpu.VMEM((images, padded, span), BF16),
             pltpu.VMEM((padded, images, LANES), BF16),
             pltpu.VMEM((padded, images, 64), BF16),
         ],
         name="pack_patches",
-    )(where, patches)
+    )(where, *[patches] * 4)
 
 
 def after(value, other):
@@ -190,6 +199,30 @@
     return hidden, feature, aux_pre, sent
 
 
+def recon_kernel(n_feature, n_tiles, *refs):
+    feature_refs, decode_refs, recon_refs = refs[:n_feature], refs[n_feature : n_feature + n_tiles], refs[n_feature + n_tiles :]
+    feature = jnp.concatenate([ref[...] for ref in feature_refs], axis=1)
+    for decode_ref, recon_ref in zip(decode_refs, recon_refs):
+        recon_ref[...] = dot(feature, decode_ref[...])
+
+
+def reconstruct(feature, decode, n_tiles):
+    rows = feature[0].shape[0]
+    width = decode.shape[0]
+    block = pl.BlockSpec((rows // STEPS, TILE), lambda g: (g, 0))
+    return call(
+        functools.partial(recon_kernel, len(feature), n_tiles),
+        [shape((rows, TILE), F32)] * n_tiles,
+        limit=57,
+        flops=2 * rows * width * n_tiles * TILE,
+        moved=rows * (2 * width + 4 * n_tiles * TILE),
+        grid=(STEPS,),
+        in_specs=[*[block] * len(feature), *[pl.BlockSpec((width, TILE), lambda g, j=j: (0, j)) for j in range(n_tiles)]],
+        out_specs=[block] * n_tiles,
+        name="reconstruct",
+    )(*feature, *[decode] * n_tiles)
+
+
 def own_index(h):
     per_half = STEPS // 2
     return lambda g, where: (jnp.clip(g - h * per_half, 0, per_half - 1), 0, 0)
@@ -281,9 +314,10 @@
         total[...] = now if g == 0 else total[...] + now
 
 
-def residual_kernel(groups, scale, n_feature, n_tiles, n_patch, where_ref, *refs):
+def residual_kernel(groups, scale, n_feature, n_recon, n_tiles, n_patch, where_ref, *refs):
     feature_refs, refs = refs[:n_feature], refs[n_feature:]
-    decode_refs, refs = refs[:n_tiles], refs[n_tiles:]
+    recon_refs, refs = refs[:n_recon], refs[n_recon:]
+    decode_refs, refs = refs[: n_tiles - n_recon], refs[n_tiles - n_recon :]
     patch_refs, refs = refs[:n_patch], refs[n_patch:]
     grad_refs, refs = refs[:n_tiles], refs[n_tiles:]
     keep_ref, send_ref, target, feature, grads, total, sems = refs
@@ -298,7 +332,7 @@
         now = feature[here]
         for j, grad_ref in enumerate(grad_refs):
             cut = slice(j * TILE, (j + 1) * TILE)
-            recon = dot(now, decode_refs[j][...])
+            recon = recon_refs[j][...] if j < n_recon else dot(now, decode_refs[j - n_recon][...])
             grad = ((recon - target[:, :, cut].reshape(size, TILE).astype(F32)) * scale).astype(BF16)
             grad_ref[...] = grad
             grads[here, cut] = grad
@@ -309,7 +343,7 @@
     by_step(copies_of(feature_refs, feature, sems), body)
 
 
-def residual(where, feature, decode, patch_args, patch_specs, images, scale, groups):
+def residual(where, feature, recon, decode, patch_args, patch_specs, images, scale, groups):
     rows = feature[0].shape[0]
     width, n = decode.shape
     size = rows // STEPS
@@ -319,15 +353,20 @@
     block = pl.BlockSpec((size, TILE), lambda g, where: (g, 0))
     column = lambda j: pl.BlockSpec((width, TILE), lambda g, where: (0, j))
     *grad, keep, send = call(
-        functools.partial(residual_kernel, groups, scale, len(feature), n_tiles, len(patch_args)),
+        functools.partial(residual_kernel, groups, scale, len(feature), len(recon), n_tiles, len(patch_args)),
         [*[shape((rows, TILE), BF16)] * n_tiles, shape(parts, BF16), shape(parts, BF16)],
         limit=58,
-        flops=4 * rows * width * n,
+        flops=2 * rows * width * (2 * n - len(recon) * TILE),
         moved=rows * (2 * width + 6 * n),
         grid_spec=pltpu.PrefetchScalarGridSpec(
             num_scalar_prefetch=1,
             grid=(STEPS,),
-            in_specs=[*[HBM] * len(feature), *[column(j) for j in range(n_tiles)], *patch_specs],
+            in_specs=[
+                *[HBM] * len(feature),
+                *[block] * len(recon),
+                *[column(j) for j in range(len(recon), n_tiles)],
+                *patch_specs,
+            ],
             out_specs=[*[block] * n_tiles, dealt, dealt],
             scratch_shapes=[
                 pltpu.VMEM((size // images, images, n), BF16),
@@ -338,29 +377,31 @@
             ],
         ),
         name="residual",
-    )(where, *feature, *[decode] * n_tiles, *patch_args)
+    )(where, *feature, *recon, *[decode] * (n_tiles - len(recon)), *patch_args)
     return grad, keep, send
 
 
 def backward_kernel(groups, n_grad, n_decode, where_ref, *refs):
     grad_refs, refs = refs[:n_grad], refs[n_grad:]
     decode_refs, refs = refs[:n_decode], refs[n_decode:]
-    (hidden_ref, acts_ref, pooled_ref, second_ref, keep_ref, send_ref,
-     hidden, acts, feature_grads, hidden_grads, total_second, total_first, sems) = refs
+    (hidden_ref, acts_ref, aux_grad_ref, aux_ref, second_ref, keep_ref, send_ref,
+     hidden, acts, feature_grads, hidden_grads, pooled, total_second, total_first, sems) = refs
     rows, width = feature_grads.shape
     size = grad_refs[0].shape[0]
-    images = pooled_ref.shape[0]
+    images = aux_grad_ref.shape[0]
     pairs = [(total_second, hidden, feature_grads), (total_first, hidden_grads, acts)]
 
     def body(g):
         here = slice(g * size, (g + 1) * size)
         if g:
             contract(g - 1, rows, pairs)
+        else:
+            pooled[...] = dot(aux_grad_ref[...], aux_ref[...], COLS_1) / (rows // images)
         grad = jnp.concatenate([ref[...] for ref in grad_refs], axis=1)
         for j, decode_ref in enumerate(decode_refs):
             cut = slice(j * TILE, (j + 1) * TILE)
             back = dot(grad, decode_ref[...], COLS_1).reshape(size // images, images, TILE)
-            feature_grads[here, cut] = (back + pooled_ref[:, cut][None]).astype(BF16).reshape(size, TILE)
+            feature_grads[here, cut] = (back + pooled[:, cut][None]).astype(BF16).reshape(size, TILE)
         hidden_back = dot(feature_grads[here], second_ref[...], COLS_1)
         hidden_grads[here] = jnp.where(hidden[here].astype(F32) > 0, hidden_back, 0.0).astype(BF16)
         if g == STEPS - 1:
@@ -382,7 +423,7 @@
     by_step([one + other for one, other in copies], body)
 
 
-def backward(where, grad, hidden, acts, decode, pooled, second, groups):
+def backward(where, grad, hidden, acts, decode, aux_grad, aux, second, groups):
     rows, width = acts.shape
     inner, n = hidden.shape[1], len(grad) * TILE
     n_decode = width // TILE
@@ -394,7 +435,7 @@
     return call(
         functools.partial(backward_kernel, groups, len(grad), n_decode),
         [shape(parts, BF16), shape(parts, BF16)],
-        limit=58,
+        limit=44,
         flops=2 * rows * width * (n + 3 * inner),
         moved=2 * rows * (width + n + inner),
         grid_spec=pltpu.PrefetchScalarGridSpec(
@@ -405,7 +446,8 @@
                 *[row_block(j) for j in range(n_decode)],
                 HBM,
                 HBM,
-                whole(pooled),
+                whole(aux_grad),
+                whole(aux),
                 whole(second),
             ],
             out_specs=[dealt, dealt],
@@ -414,13 +456,14 @@
                 pltpu.VMEM((rows, width), BF16),
                 pltpu.VMEM((rows, width), BF16),
                 pltpu.VMEM((rows, inner), BF16),
+                pltpu.VMEM((aux_grad.shape[0], width), F32),
                 pltpu.VMEM((inner, width), F32),
                 pltpu.VMEM((inner, width), F32),
                 pltpu.SemaphoreType.DMA((2, STEPS, 1)),
             ],
         ),
         name="backward",
-    )(where, *grad, *[decode] * n_decode, hidden, acts, pooled, second)
+    )(where, *grad, *[decode] * n_decode, hidden, acts, aux_grad, aux, second)
 
 
 TOPS, DENOMS = 3, 19
@@ -447,19 +490,10 @@
     return (digits[:, 0:1] * LANES + digits[:, 1:2]).astype(jnp.int32)
 
 
-def logits_kernel(where_ref, got_ref, klass_hbm, sent_ref, klass_ref, logits_ref, sems):
+def logits_kernel(where_ref, got_ref, klass_ref, sent_ref, logits_ref):
     groups, images, _ = got_ref.shape
     classes, head = klass_ref.shape
-    size = classes // sems.shape[0]
-    copies = [
-        pltpu.make_async_copy(klass_hbm.at[pl.ds(j * size, size)], klass_ref.at[pl.ds(j * size, size)], sems.at[j])
-        for j in range(sems.shape[0])
-    ]
-    for copy in copies:
-        copy.start()
     got = got_ref[...].reshape(groups * images, -1)
-    for copy in copies:
-        copy.wait()
     logits_ref[...] = dot(got[:, :head], klass_ref[...], COLS_1)
     logits = logits_ref[...]
     ids = lax.broadcasted_iota(jnp.int32, logits.shape, 1) + where_ref[ME] * classes
@@ -489,27 +523,16 @@
     return call(
         logits_kernel,
         shape((groups, images, 2 * head + LANES), BF16),
-        limit=58,
+        limit=16,
         flops=2e10,
-        in_specs=[SMEM, VMEM, HBM],
-        scratch_shapes=[
-            pltpu.VMEM(klass.shape, BF16),
-            pltpu.VMEM((groups * images, classes), F32),
-            pltpu.SemaphoreType.DMA((4,)),
-        ],
+        in_specs=[SMEM, VMEM, VMEM],
+        scratch_shapes=[pltpu.VMEM((groups * images, classes), F32)],
         name="class_logits",
     )(where, got, klass)
 
 
-def aux_kernel(pix, norm, got_ref, aux_pre_ref, aux_hbm, pooled_ref, grad_ref, aux_ref, sems):
-    size = aux_ref.shape[0] // sems.shape[0]
-    copies = [
-        pltpu.make_async_copy(aux_hbm.at[pl.ds(j * size, size)], aux_ref.at[pl.ds(j * size, size)], sems.at[j])
-        for j in range(sems.shape[0])
-    ]
-    for copy in copies:
-        copy.start()
-    groups = got_ref.shape[0]
+def aux_kernel(norm, got_ref, aux_pre_ref, grad_ref, cut_ref):
+    groups, images, _ = got_ref.shape
     head = aux_pre_ref.shape[1]
     stats = [from_digits(got_ref[d, :, 2 * head :]) for d in range(groups)]
     top = functools.reduce(jnp.maximum, [s[:, 0:1] for s in stats])
@@ -520,27 +543,21 @@
     row = sum(got_ref[d, :, head : 2 * head].astype(F32) for d in range(groups))
     back = rest + row * ((own - 1.0) / norm).astype(BF16).astype(F32)
     aux_grad = jnp.where(aux_pre_ref[...] > 0, back, 0.0).astype(BF16)
-    for copy in copies:
-        copy.wait()
-    pooled_ref[...] = dot(aux_grad, aux_ref[...], COLS_1) / pix
-    images, part = aux_grad.shape[0], grad_ref.shape[1]
+    grad_ref[...] = aux_grad
+    part = cut_ref.shape[1]
     for q in range(head // part):
-        grad_ref[q * images : (q + 1) * images, :] = aux_grad[:, q * part : (q + 1) * part]
-
-
-def aux_backward(got, aux_pre, aux, pix, norm):
-    groups, images, _ = got.shape
-    width, head = aux.shape
-    part = width // groups
+        cut_ref[q * images : (q + 1) * images, :] = aux_grad[:, q * part : (q + 1) * part]
+
+
+def aux_backward(got, aux_pre, part, norm):
+    images, head = aux_pre.shape
     return call(
-        functools.partial(aux_kernel, pix, norm),
-        [shape((images, width), F32), shape((images * head // part, part), BF16)],
-        limit=58,
+        functools.partial(aux_kernel, norm),
+        [shape((images, head), BF16), shape((images * head // part, part), BF16)],
+        limit=16,
         flops=2e10,
-        in_specs=[VMEM, VMEM, HBM],
-        scratch_shapes=[pltpu.VMEM(aux.shape, BF16), pltpu.SemaphoreType.DMA((4,))],
         name="aux_backward",
-    )(got, aux_pre, aux)
+    )(got, aux_pre)
 
 
 def class_kernel(norm, n, where_ref, klass_ref, got_ref, stats_ref, *refs):
@@ -670,8 +687,7 @@
         where = jnp.stack([section & 1, me & 1, me, *tiles]).astype(jnp.int32)
         turned = patches.transpose(0, 2, 1)
         halves = [pack(where, turned, h) for h in range(2)]
-        x = [swap(half, "section", 1) for half in halves]
-        y = [swap(half, "section", 2) for half in halves]
+        x, y = [swap(halves[0], "section", 1)], [swap(halves[1], "section", 2)]
         first = after(first, halves[1])
     else:
         where = jnp.stack([section & 1, me & 1, me]).astype(jnp.int32)
@@ -680,19 +696,22 @@
     hidden, feature, aux_pre, sent = forward(acts, first, second, aux, labels, groups)
     if paired:
         sent = after(sent, (x[0], y[0]))
-        diagonal = [swap(after(y[0], aux_pre), "section", 1), swap(after(x[1], aux_pre), "section", 2)]
+        diagonal = [swap(after(x[0], aux_pre), "section", 2), swap(after(y[0], aux_pre), "section", 1)]
+        x.append(swap(after(halves[1], aux_pre), "section", 1))
+        y.insert(0, swap(after(halves[0], aux_pre), "section", 2))
         target = patch_operands([halves, x, y, diagonal], [0, 1, 2, 3], [0, 1, 2, 3])
     else:
         target = [target], [pl.BlockSpec((pix // STEPS, images, n_decode), lambda g, where: (g, 0, 0))]
     got = exchange(sent)
-    sent = class_logits(where, got, klass)
+    recon = reconstruct([after(feature[0], sent), *feature[1:]], decode, 1)
+    sent = class_logits(where, after(got, recon[0]), klass)
     partial = exchange(sent)
-    grad, keep, send = residual(after(where, sent), feature, decode, *target, images, scale, groups)
-    pooled_grad, aux_grad = aux_backward(partial, aux_pre, aux, pix, norm)
-    chip_decode = add_cores(where, keep, send, [aux_grad])
+    grad, keep, send = residual(after(where, sent), feature, recon, decode, *target, images, scale, groups)
+    aux_grad, aux_cut = aux_backward(partial, aux_pre, width // groups, norm)
+    chip_decode = add_cores(where, keep, send, [aux_cut])
     sum_decode = exchange_chips(chip_decode)
     keep, send = backward(
-        where, grad, hidden, acts.reshape(rows, width), decode, after(pooled_grad, chip_decode[0]), second, groups
+        where, grad, hidden, acts.reshape(rows, width), decode, after(aux_grad, chip_decode[0]), aux, second, groups
     )
     sum_last = exchange_chips(add_cores(where, keep, after(send, sum_decode)))
     grad_class, grad_aux = class_backward(where, klass, got, partial, sum_decode, n_decode, norm)

time: 126 us -> 122 us (0.968)
  starting transfers between devices: 26.7 us -> 30.6 us
  local copies, waits for them, and re-layouts: 4.69 us -> 1.55 us
  waiting for transfers between devices: 29.9 us -> 27.6 us
  Pallas kernels: 62.8 us -> 60.8 us
    ppermute x15, starting transfers between devices: 16.8 us -> 20.7 us  [swap(): return lax.ppermute(value, axis, [(i, i ^ bits) for i in range(count)])]
    unnamed x36 -> x28, local copies, waits for them, and re-layouts: 4.6 us -> 1.46 us
    pallas_call x1, Pallas kernels: 17.4 us -> 14.3 us  [backward(): call(functools.partial(backward_kernel, groups, len(grad), n_decode), [sh...]
    pallas_call x4 -> x5, Pallas kernels: 25.7 us -> 28.5 us  [the longest x1 18 us: residual(): call(functools.partial(residual_kernel, groups, scale, len(feature), len(...]
    ppermute x15, waiting for transfers between devices: 29.6 us -> 27.6 us  [swap(): return lax.ppermute(value, axis, [(i, i ^ bits) for i in range(count)])]
    pallas_call x1, Pallas kernels: 4.4 us -> 2.68 us  [class_logits(): call(logits_kernel, shape((groups, images, 2 * head + LANES), BF16), limi...]
  transfers between devices with their start and end apart: 17 -> 17, of which waited for: 10 -> 8; matrix products, arithmetic and copies ran while one was open for 0% -> 0% of each run, Pallas kernels for 47% -> 47%
where the time goes in v9:
time: 122 us; the launch traced here: 121 us
  Pallas kernels  60.8 us (50%)
  starting transfers between devices  30.6 us (25%)
  waiting for transfers between devices  27.6 us (23%)
  local copies, waits for them, and re-layouts  1.55 us (1%)
    ppermute x15, waiting for transfers between devices, swap(): return lax.ppermute(value, axis, [(i, i ^ bits) for i in range(count)])  27.6 us
    ppermute x15, starting transfers between devices, swap(): return lax.ppermute(value, axis, [(i, i ^ bits) for i in range(count)])  20.7 us
    pallas_call x1, Pallas kernels, residual(): call(functools.partial(residual_kernel, groups, scale, len(feature), len(...  18 us
    pallas_call x1, Pallas kernels, backward(): call(functools.partial(backward_kernel, groups, len(grad), n_decode), [sh...  14.3 us
    all_to_all x2, starting transfers between devices, exchange(): lax.all_to_all(value, 'dp', 0, 0, axis_index_groups=groups, tiled=True)  9.91 us
    pallas_call x1, Pallas kernels, forward(): call(functools.partial(forward_kernel, n_tiles, pix), [shape((pix * image...  9.66 us
    pallas_call x1, Pallas kernels, reconstruct(): call(functools.partial(recon_kernel, len(feature), n_tiles), [shape((rows...  6.52 us
    pallas_call x2, Pallas kernels, pack(): call(functools.partial(pack_kernel, h * half), shape(dims, BF16), limit=2...  3.62 us
  transfers between devices with their start and end apart: 17, of which 8 were waited for; matrix products, arithmetic and copies ran while one was open for 0% of the time, Pallas kernels for 47%

profile of v9, /device:TPU:0, one launch (start us, length us, event | category | flops | bytes accessed | tf_op | source)
XLA Modules:
  0.0 121.4 jit_solution(8178595187034690034)
XLA Ops:
  0.7 0.1 stack.47.where_ref
  0.7 0.0 copy-start
  0.8 1.4 %copy-done = bf16[16,196,192]{1,2,0:T(8,128)(2,1)S(1)} copy-done((bf16[16,196,192]{1,2,0:T(8,128)(2,1)S(1)}, bf16[16,196,192]{1,2,0:T(8,128)(2,1)}, u32[]{:S(2)}) %copy-start) | copy-done | bytes 1204248
  2.2 1.8 %pack_patches.3.refs_7_.refs_15_ = bf16[147,16,128]{2,1,0:T(8,128)(2,1)S(1)} custom-call(s32[11]{0:T(128)S(1)} %stack.47.where_ref, bf16[16,192,196]{2,1,0:T(8,128)(2,1)S(1)} %bitcast.27, bf16[16,192,196]{2,1,0:T(8,128)(2,1)S(1)} %bitcast.28, bf16[16,192,196]{2,1,0:T(8,128)(2,1)S(1)} %bitcast.29, bf16[16,192,196]{2,1,0:T(8,128)(2,1)S(1)} %bitcast.30), custom_call_target="tpu_custom_call" | custom-call | tf_op jit(solution)/shard_map/pack_patches/pallas_call | solution.py:99
  4.0 3.0 %collective-permute-start = (bf16[147,16,128]{2,1,0:T(8,128)(2,1)S(1)}, bf16[147,16,128]{2,1,0:T(8,128)(2,1)}, u32[]{:S(2)}, u32[]{:S(2)}) collective-permute-start(bf16[147,16,128]{2,1,0:T(8,128)(2,1)S(1)} %pack_patches.3.refs_7_.refs_15_), channel_id=1, source_target_pairs={{0,8},{8,0},{16,24},{24,16},{1,9},{9,1},{17,25},{25,17},{2,10},{10... | collective-permute-start | bytes 1806344 | tf_op jit(solution)/shard_map/ppermute | solution.py:46
  7.0 1.8 %pack_patches.2.refs_8_.refs_16_ = bf16[147,16,128]{2,1,0:T(8,128)(2,1)S(1)} custom-call(s32[11]{0:T(128)S(1)} %stack.47.where_ref, bf16[16,192,196]{2,1,0:T(8,128)(2,1)S(1)} %bitcast.31, bf16[16,192,196]{2,1,0:T(8,128)(2,1)S(1)} %bitcast.32, bf16[16,192,196]{2,1,0:T(8,128)(2,1)S(1)} %bitcast.33, bf16[16,192,196]{2,1,0:T(8,128)(2,1)S(1)} %bitcast.34), custom_call_target="tpu_custom_call" | custom-call | tf_op jit(solution)/shard_map/pack_patches/pallas_call | solution.py:99
  8.8 1.6 %collective-permute-start.1 = (bf16[147,16,128]{2,1,0:T(8,128)(2,1)S(1)}, bf16[147,16,128]{2,1,0:T(8,128)(2,1)}, u32[]{:S(2)}, u32[]{:S(2)}) collective-permute-start(bf16[147,16,128]{2,1,0:T(8,128)(2,1)S(1)} %pack_patches.2.refs_8_.refs_16_), channel_id=1, source_target_pairs={{0,16},{8,24},{16,0},{24,8},{1,17},{9,25},{17,1},{25,9},{2,18},{10... | collective-permute-start | bytes 1806344 | tf_op jit(solution)/shard_map/ppermute | solution.py:46
  10.4 9.7 %forward.1 = (bf16[3136,256]{1,0:T(8,128)(2,1)}, bf16[3136,256]{1,0:T(8,128)(2,1)}, bf16[3136,256]{1,0:T(8,128)(2,1)}, bf16[3136,256]{1,0:T(8,128)(2,1)}, bf16[3...) custom-call(bf16[196,16,1024]{2,1,0:T(8,128)(2,1)} %bitcast.48, ...), custom_call_target="tpu_custom_call" | custom-call | flops 3288334336 | bytes 14450688 | tf_op jit(solution)/shard_map/forward/pallas_call | solution.py:171
  20.1 0.6 collective-permute-done.refs_9_.refs_17_
  20.7 3.3 %collective-permute-done.1.refs_12_.refs_20_ = bf16[147,16,128]{2,1,0:T(8,128)(2,1)} collective-permute-done((bf16[147,16,128]{2,1,0:T(8,128)(2,1)S(1)}, bf16[147,16,128]{2,1,0:T(8,128)(2,1)}, u32[]{:S(2)}, u32[]{:S(2)}) %collective-permute-start.1) | collective-permute-done | bytes 602144 | tf_op jit(solution)/shard_map/ppermute | solution.py:46
  24.0 4.9 %all-to-all-start = ((bf16[8,16,768]{2,1,0:T(8,128)(2,1)}), bf16[8,16,768]{2,1,0:T(8,128)(2,1)S(1)}, u32[]{:S(2)}, u32[]{:S(2)}) async-start(bf16[8,16,768]{2,1,0:T(8,128)(2,1)} %get-tuple-element.47), calls=%async_computation | async-start | bytes 393216 | tf_op jit(solution)/shard_map/all_to_all | solution.py:50
  28.9 0.6 collective-permute-start.2
  29.5 1.5 %collective-permute-start.3 = (bf16[147,16,128]{2,1,0:T(8,128)(2,1)S(1)}, bf16[147,16,128]{2,1,0:T(8,128)(2,1)}, u32[]{:S(2)}, u32[]{:S(2)}) collective-permute-start(bf16[147,16,128]{2,1,0:T(8,128)(2,1)S(1)} %pack_patches.3.refs_7_.refs_15_), channel_id=1, source_target_pairs={{0,16},{8,24},{16,0},{24,8},{1,17},{9,25},{17,1},{25,9},{2,18},{10... | collective-permute-start | bytes 1806344 | tf_op jit(solution)/shard_map/ppermute | solution.py:46
  31.1 0.5 collective-permute-start.4
  31.6 1.5 %collective-permute-start.5 = (bf16[147,16,128]{2,1,0:T(8,128)(2,1)}, bf16[147,16,128]{2,1,0:T(8,128)(2,1)}, u32[]{:S(2)}, u32[]{:S(2)}) collective-permute-start(bf16[147,16,128]{2,1,0:T(8,128)(2,1)} %collective-permute-done.1.refs_12_.refs_20_), channel_id=1, source_target_pairs={{0,8},{8,0},{16,24},{24,16},{1,9},{9,1},{17,25},{25,17},{2,10},{10... | collective-permute-start | bytes 1806344 | tf_op jit(solution)/shard_map/ppermute | solution.py:46
  33.1 6.5 %reconstruct.1.refs_4_ = f32[3136,256]{1,0:T(8,128)} custom-call(bf16[3136,256]{1,0:T(8,128)(2,1)} %get-tuple-element.49.refs_0_, bf16[3136,256]{1,0:T(8,128)(2,1)} %get-tuple-element.50.refs_1_, bf16[3136,256]{1,0:T(8,128)(2,1)} %get-tuple-element.51.refs_2_, bf16[3136,256]{1,0:T(8,128)(2,1)} %get-tuple-element.52.refs_3_, bf16[1024,768]{1,0:T(8,128)(2,1)} %bitcast.35), custom_call_target="tpu_custom_call" | custom-call | flops 1644167168 | bytes 9633792 | tf_op jit(solution)/shard_map/reconstruct/pallas_call | solution.py:213
  39.6 0.0 all-to-all-done.got_ref
  39.6 2.7 %class_logits.1 = bf16[8,16,1152]{2,1,0:T(8,128)(2,1)} custom-call(s32[11]{0:T(128)S(1)} %stack.47.where_ref, bf16[8,16,768]{2,1,0:T(8,128)(2,1)S(1)} %all-to-all-done.got_ref, bf16[1408,512]{1,0:T(8,128)(2,1)S(1)} %bitcast.42), custom_call_target="tpu_custom_call" | custom-call | flops 20000000000 | tf_op jit(solution)/shard_map/class_logits/pallas_call | solution.py:523
  42.3 5.0 %all-to-all-start.1 = ((bf16[8,16,1152]{2,1,0:T(8,128)(2,1)}), bf16[8,16,1152]{2,1,0:T(8,128)(2,1)S(1)}, u32[]{:S(2)}, u32[]{:S(2)}) async-start(bf16[8,16,1152]{2,1,0:T(8,128)(2,1)} %class_logits.1), calls=%async_computation.1 | async-start | bytes 589824 | tf_op jit(solution)/shard_map/all_to_all | solution.py:50
  47.3 0.0 collective-permute-done.2.refs_10_.refs_18_
  47.3 10.9 %collective-permute-done.4.refs_13_.refs_21_ = bf16[147,16,128]{2,1,0:T(8,128)(2,1)} collective-permute-done((bf16[147,16,128]{2,1,0:T(8,128)(2,1)}, bf16[147,16,128]{2,1,0:T(8,128)(2,1)}, u32[]{:S(2)}, u32[]{:S(2)}) %collective-permute-start.4) | collective-permute-done | bytes 602144 | tf_op jit(solution)/shard_map/ppermute | solution.py:46
  58.2 0.0 collective-permute-done.5.refs_14_.refs_22_
  58.2 18.0 %residual.1 = (bf16[3136,256]{1,0:T(8,128)(2,1)}, bf16[3136,256]{1,0:T(8,128)(2,1)}, bf16[3136,256]{1,0:T(8,128)(2,1)}, bf16[4,768,128]{2,1,0:T(8,128)(2,1)}, bf16[4,768,128]{2,1,0:T(8,128)(2,1)}) custom-call(s32[11]{0:T(128)} %copy-done.8, bf16[3136,256]{1,0:T(8,128)(2,1)} %get-tuple-element.49.refs_0_, bf16[3136,256]{1,0:T(8,128)(2,1)} %get-tuple-element.50.refs_1_, ...), custom_call_target="tpu_custom_call" | custom-call | flops 8220835840 | bytes 20873216 | tf_op jit(solution)/shard_map/residual/pallas_call | solution.py:355
  76.2 0.0 copy-start.9
  76.3 0.1 collective-permute-start.6
  76.4 0.0 copy-start.3
  76.4 0.0 copy-start.7
  76.4 0.3 aux_backward.1
  76.7 0.5 collective-permute-start.7
  77.3 1.4 %collective-permute-done.7.refs_1_ = bf16[64,128]{1,0:T(8,128)(2,1)S(1)} collective-permute-done((bf16[64,128]{1,0:T(8,128)(2,1)S(1)}, bf16[64,128]{1,0:T(8,128)(2,1)S(1)}, u32[]{:S(2)}, u32[]{:S(2)}) %collective-permute-start.7) | collective-permute-done | bytes 16416 | tf_op jit(solution)/shard_map/ppermute | solution.py:46
  78.6 0.2 collective-permute-done.6.got_ref
  78.8 0.7 add_cores.2
  79.6 1.7 %collective-permute-start.8 = (bf16[896,128]{1,0:T(8,128)(2,1)S(1)}, bf16[896,128]{1,0:T(8,128)(2,1)S(1)}, u32[]{:S(2)}, u32[]{:S(2)}) collective-permute-start(bf16[896,128]{1,0:T(8,128)(2,1)S(1)} %get-tuple-element.64), channel_id=1, source_target_pairs={{0,2},{1,3},{2,0},{3,1},{4,6},{5,7},{6,4},{7,5},{8,10},{9,11},{10,... | collective-permute-start | bytes 688136 | tf_op jit(solution)/shard_map/ppermute | solution.py:46
  81.3 2.4 %collective-permute-start.9 = (bf16[896,128]{1,0:T(8,128)(2,1)S(1)}, bf16[896,128]{1,0:T(8,128)(2,1)S(1)}, u32[]{:S(2)}, u32[]{:S(2)}) collective-permute-start(bf16[896,128]{1,0:T(8,128)(2,1)S(1)} %get-tuple-element.65), channel_id=1, source_target_pairs={{0,4},{1,5},{2,6},{3,7},{4,0},{5,1},{6,2},{7,3},{8,12},{9,13},{10,... | collective-permute-start | bytes 688136 | tf_op jit(solution)/shard_map/ppermute | solution.py:46
  83.7 0.4 collective-permute-start.10
  84.0 14.3 %backward.1 = (bf16[4,512,128]{2,1,0:T(8,128)(2,1)S(1)}, bf16[4,512,128]{2,1,0:T(8,128)(2,1)S(1)}) custom-call(s32[11]{0:T(128)S(1)} %copy-done.9, bf16[3136,256]{1,0:T(8,128)(2,1)S(1)} %copy-done.11, bf16[3136,256]{1,0:T(8,128)(2,1)S(1)} %copy-done.12, bf16[3136,256]{1,0:T(8,128)(2,1)S(1)} %copy-done.13, bf16[1024,768]{1,0:T(8,128)(2,1)S(1)} %bitcast.38, ...), custom_call_target="tpu_custom_call" | custom-call | flops 9865003008 | bytes 12845056 | tf_op jit(solution)/shard_map/backward/pallas_call | solution.py:435
  98.4 0.0 collective-permute-done.8.refs_1_
  98.4 2.1 %collective-permute-done.9.refs_2_ = bf16[896,128]{1,0:T(8,128)(2,1)S(1)} collective-permute-done((bf16[896,128]{1,0:T(8,128)(2,1)S(1)}, bf16[896,128]{1,0:T(8,128)(2,1)S(1)}, u32[]{:S(2)}, u32[]{:S(2)}) %collective-permute-start.9) | collective-permute-done | bytes 229408 | tf_op jit(solution)/shard_map/ppermute | solution.py:46
  100.5 0.0 collective-permute-done.10.refs_3_
  100.5 1.9 %collective-permute-done.11.got_ref = bf16[4,512,128]{2,1,0:T(8,128)(2,1)S(1)} collective-permute-done((bf16[4,512,128]{2,1,0:T(8,128)(2,1)S(1)}, bf16[4,512,128]{2,1,0:T(8,128)(2,1)S(1)}, u32[]{:S(2)}, u32[]{:S(2)}) %collective-permute-start.11) | collective-permute-done | bytes 524320 | tf_op jit(solution)/shard_map/ppermute | solution.py:46
  102.4 0.7 add_cores.3
  103.1 4.5 %collective-permute-start.12 = (bf16[512,128]{1,0:T(8,128)(2,1)S(1)}, bf16[512,128]{1,0:T(8,128)(2,1)S(1)}, u32[]{:S(2)}, u32[]{:S(2)}) collective-permute-start(bf16[512,128]{1,0:T(8,128)(2,1)S(1)} %get-tuple-element.77), channel_id=1, source_target_pairs={{0,2},{1,3},{2,0},{3,1},{4,6},{5,7},{6,4},{7,5},{8,10},{9,11},{10,... | collective-permute-start | bytes 393224 | tf_op jit(solution)/shard_map/ppermute | solution.py:46
  107.6 1.0 collective-permute-start.13
  108.5 1.5 %collective-permute-start.14 = (bf16[512,128]{1,0:T(8,128)(2,1)S(1)}, bf16[512,128]{1,0:T(8,128)(2,1)S(1)}, u32[]{:S(2)}, u32[]{:S(2)}) collective-permute-start(bf16[512,128]{1,0:T(8,128)(2,1)S(1)} %get-tuple-element.79), channel_id=1, source_target_pairs={{0,6},{1,7},{2,4},{3,5},{4,2},{5,3},{6,0},{7,1},{8,14},{9,15},{10,... | collective-permute-start | bytes 393224 | tf_op jit(solution)/shard_map/ppermute | solution.py:46
  110.0 3.3 %class_backward.1 = (f32[1408,512]{1,0:T(8,128)}, f32[128,512]{1,0:T(8,128)}) custom-call(s32[11]{0:T(128)S(1)} %copy-done.9, bf16[1408,512]{1,0:T(8,128)(2,1)S(1)} %bitcast.43, bf16[8,16,768]{2,1,0:T(8,128)(2,1)S(1)} %all-to-all-done.got_ref, bf16[8,16,1152]{2,1,0:T(8,128)(2,1)S(1)} %all-to-all-done.1.got_ref.stats_ref, ...), custom_call_target="tpu_custom_call" | custom-call | flops 184549376 | bytes 2883584 | tf_op jit(solution)/shard_map/class_backward/pallas_call | solution.py:598
  113.3 7.1 %collective-permute-done.13.refs_6_ = bf16[512,128]{1,0:T(8,128)(2,1)S(1)} collective-permute-done((bf16[512,128]{1,0:T(8,128)(2,1)S(1)}, bf16[512,128]{1,0:T(8,128)(2,1)S(1)}, u32[]{:S(2)}, u32[]{:S(2)}) %collective-permute-start.13) | collective-permute-done | bytes 131104 | tf_op jit(solution)/shard_map/ppermute | solution.py:46
  120.5 0.0 collective-permute-done.14.refs_7_
  120.5 1.0 finish.1
  (27 shorter events, 0.1 us)
Async XLA Ops:
  0.7 38.8 %copy-start.8 = (s32[11]{0:T(128)}, s32[11]{0:T(128)S(1)}, u32[]{:S(2)}) copy-start(s32[11]{0:T(128)S(1)} %stack.47.where_ref) | copy-start | bytes 136
  0.7 1.4 %copy-start = (bf16[16,196,192]{1,2,0:T(8,128)(2,1)S(1)}, bf16[16,196,192]{1,2,0:T(8,128)(2,1)}, u32[]{:S(2)}) copy-start(bf16[16,196,192]{1,2,0:T(8,128)(2,1)} %param.9) | copy-start | bytes 3612676
  4.0 25.5 %copy-start.5 = (bf16[147,16,128]{2,1,0:T(8,128)(2,1)}, bf16[147,16,128]{2,1,0:T(8,128)(2,1)S(1)}, u32[]{:S(2)}) copy-start(bf16[147,16,128]{2,1,0:T(8,128)(2,1)S(1)} %pack_patches.3.refs_7_.refs_15_) | copy-start | bytes 1806340
  4.0 16.7 %collective-permute-start = (bf16[147,16,128]{2,1,0:T(8,128)(2,1)S(1)}, bf16[147,16,128]{2,1,0:T(8,128)(2,1)}, u32[]{:S(2)}, u32[]{:S(2)}) collective-permute-start(bf16[147,16,128]{2,1,0:T(8,128)(2,1)S(1)} %pack_patches.3.refs_7_.refs_15_), channel_id=1, source_target_pairs={{0,8},{8,0},{16,24},{24,16},{1,9},{9,1},{17,25},{25,17},{2,10},{10... | collective-permute-start | bytes 1806344 | tf_op jit(solution)/shard_map/ppermute | solution.py:46
  8.8 20.1 %copy-start.6 = (bf16[147,16,128]{2,1,0:T(8,128)(2,1)}, bf16[147,16,128]{2,1,0:T(8,128)(2,1)S(1)}, u32[]{:S(2)}) copy-start(bf16[147,16,128]{2,1,0:T(8,128)(2,1)S(1)} %pack_patches.2.refs_8_.refs_16_) | copy-start | bytes 1806340
  8.8 15.2 %collective-permute-start.1 = (bf16[147,16,128]{2,1,0:T(8,128)(2,1)S(1)}, bf16[147,16,128]{2,1,0:T(8,128)(2,1)}, u32[]{:S(2)}, u32[]{:S(2)}) collective-permute-start(bf16[147,16,128]{2,1,0:T(8,128)(2,1)S(1)} %pack_patches.2.refs_8_.refs_16_), channel_id=1, source_target_pairs={{0,16},{8,24},{16,0},{24,8},{1,17},{9,25},{17,1},{25,9},{2,18},{10... | collective-permute-start | bytes 1806344 | tf_op jit(solution)/shard_map/ppermute | solution.py:46
  24.0 15.5 %all-to-all-start = ((bf16[8,16,768]{2,1,0:T(8,128)(2,1)}), bf16[8,16,768]{2,1,0:T(8,128)(2,1)S(1)}, u32[]{:S(2)}, u32[]{:S(2)}) async-start(bf16[8,16,768]{2,1,0:T(8,128)(2,1)} %get-tuple-element.47), calls=%async_computation | async-start | bytes 393216 | tf_op jit(solution)/shard_map/all_to_all | solution.py:50
  28.9 18.4 %collective-permute-start.2 = (bf16[147,16,128]{2,1,0:T(8,128)(2,1)S(1)}, bf16[147,16,128]{2,1,0:T(8,128)(2,1)}, u32[]{:S(2)}, u32[]{:S(2)}) collective-permute-start(bf16[147,16,128]{2,1,0:T(8,128)(2,1)S(1)} %pack_patches.2.refs_8_.refs_16_), channel_id=1, source_target_pairs={{0,8},{8,0},{16,24},{24,16},{1,9},{9,1},{17,25},{25,17},{2,10},{10... | collective-permute-start | bytes 1806344 | tf_op jit(solution)/shard_map/ppermute | solution.py:46
  29.5 17.8 %collective-permute-start.3 = (bf16[147,16,128]{2,1,0:T(8,128)(2,1)S(1)}, bf16[147,16,128]{2,1,0:T(8,128)(2,1)}, u32[]{:S(2)}, u32[]{:S(2)}) collective-permute-start(bf16[147,16,128]{2,1,0:T(8,128)(2,1)S(1)} %pack_patches.3.refs_7_.refs_15_), channel_id=1, source_target_pairs={{0,16},{8,24},{16,0},{24,8},{1,17},{9,25},{17,1},{25,9},{2,18},{10... | collective-permute-start | bytes 1806344 | tf_op jit(solution)/shard_map/ppermute | solution.py:46
  31.1 27.1 %collective-permute-start.4 = (bf16[147,16,128]{2,1,0:T(8,128)(2,1)}, bf16[147,16,128]{2,1,0:T(8,128)(2,1)}, u32[]{:S(2)}, u32[]{:S(2)}) collective-permute-start(bf16[147,16,128]{2,1,0:T(8,128)(2,1)} %collective-permute-done.refs_9_.refs_17_), channel_id=1, source_target_pairs={{0,16},{8,24},{16,0},{24,8},{1,17},{9,25},{17,1},{25,9},{2,18},{10... | collective-permute-start | bytes 1806344 | tf_op jit(solution)/shard_map/ppermute | solution.py:46
  31.6 26.6 %collective-permute-start.5 = (bf16[147,16,128]{2,1,0:T(8,128)(2,1)}, bf16[147,16,128]{2,1,0:T(8,128)(2,1)}, u32[]{:S(2)}, u32[]{:S(2)}) collective-permute-start(bf16[147,16,128]{2,1,0:T(8,128)(2,1)} %collective-permute-done.1.refs_12_.refs_20_), channel_id=1, source_target_pairs={{0,8},{8,0},{16,24},{24,16},{1,9},{9,1},{17,25},{25,17},{2,10},{10... | collective-permute-start | bytes 1806344 | tf_op jit(solution)/shard_map/ppermute | solution.py:46
  33.1 6.5 %copy-start.2 = (bf16[1,1408,512]{2,1,0:T(8,128)(2,1)S(1)}, bf16[1,1408,512]{2,1,0:T(8,128)(2,1)}, u32[]{:S(2)}) copy-start(bf16[1,1408,512]{2,1,0:T(8,128)(2,1)} %param.15) | copy-start | bytes 4325380
  42.3 34.1 %all-to-all-start.1 = ((bf16[8,16,1152]{2,1,0:T(8,128)(2,1)}), bf16[8,16,1152]{2,1,0:T(8,128)(2,1)S(1)}, u32[]{:S(2)}, u32[]{:S(2)}) async-start(bf16[8,16,1152]{2,1,0:T(8,128)(2,1)} %class_logits.1), calls=%async_computation.1 | async-start | bytes 589824 | tf_op jit(solution)/shard_map/all_to_all | solution.py:50
  47.3 29.1 %copy-start.10 = (f32[16,512]{1,0:T(8,128)S(1)}, f32[16,512]{1,0:T(8,128)}, u32[]{:S(2)}) copy-start(f32[16,512]{1,0:T(8,128)} %get-tuple-element.55.aux_pre_ref) | copy-start | bytes 98308
  76.2 2.6 %copy-start.4 = (bf16[4,768,128]{2,1,0:T(8,128)(2,1)S(1)}, bf16[4,768,128]{2,1,0:T(8,128)(2,1)}, u32[]{:S(2)}) copy-start(bf16[4,768,128]{2,1,0:T(8,128)(2,1)} %get-tuple-element.60.keep_ref) | copy-start | bytes 2359300
  76.2 2.6 %copy-start.9 = (s32[11]{0:T(128)S(1)}, s32[11]{0:T(128)}, u32[]{:S(2)}) copy-start(s32[11]{0:T(128)} %copy-done.8) | copy-start | bytes 136
  76.3 2.6 %collective-permute-start.6 = (bf16[4,768,128]{2,1,0:T(8,128)(2,1)}, bf16[4,768,128]{2,1,0:T(8,128)(2,1)S(1)}, u32[]{:S(2)}, u32[]{:S(2)}) collective-permute-start(bf16[4,768,128]{2,1,0:T(8,128)(2,1)} %get-tuple-element.61), channel_id=1, source_target_pairs={{0,1},{1,0},{2,3},{3,2},{4,5},{5,4},{6,7},{7,6},{8,9},{9,8},{10,11... | collective-permute-start | bytes 2359304 | tf_op jit(solution)/shard_map/ppermute | solution.py:46
  76.4 7.7 %copy-start.3 = (bf16[1,1024,512]{2,1,0:T(8,128)(2,1)S(1)}, bf16[1,1024,512]{2,1,0:T(8,128)(2,1)}, u32[]{:S(2)}) copy-start(bf16[1,1024,512]{2,1,0:T(8,128)(2,1)} %param.14) | copy-start | bytes 3145732
  76.4 7.7 %copy-start.7 = (bf16[1,256,1024]{2,1,0:T(8,128)(2,1)S(1)}, bf16[1,256,1024]{2,1,0:T(8,128)(2,1)}, u32[]{:S(2)}) copy-start(bf16[1,256,1024]{2,1,0:T(8,128)(2,1)} %param.12) | copy-start | bytes 1572868
  76.4 7.6 %copy-start.11 = (bf16[3136,256]{1,0:T(8,128)(2,1)S(1)}, bf16[3136,256]{1,0:T(8,128)(2,1)}, u32[]{:S(2)}) copy-start(bf16[3136,256]{1,0:T(8,128)(2,1)} %get-tuple-element.67.refs_0_) | copy-start | bytes 4816900
  76.4 7.6 %copy-start.12 = (bf16[3136,256]{1,0:T(8,128)(2,1)S(1)}, bf16[3136,256]{1,0:T(8,128)(2,1)}, u32[]{:S(2)}) copy-start(bf16[3136,256]{1,0:T(8,128)(2,1)} %get-tuple-element.68.refs_1_) | copy-start | bytes 4816900
  76.4 7.6 %copy-start.13 = (bf16[3136,256]{1,0:T(8,128)(2,1)S(1)}, bf16[3136,256]{1,0:T(8,128)(2,1)}, u32[]{:S(2)}) copy-start(bf16[3136,256]{1,0:T(8,128)(2,1)} %get-tuple-element.69.refs_2_) | copy-start | bytes 4816900
  76.7 7.3 %copy-start.1 = (bf16[1,1024,768]{2,1,0:T(8,128)(2,1)S(1)}, bf16[1,1024,768]{2,1,0:T(8,128)(2,1)}, u32[]{:S(2)}) copy-start(bf16[1,1024,768]{2,1,0:T(8,128)(2,1)} %param.13) | copy-start | bytes 4718596
  76.7 1.9 %collective-permute-start.7 = (bf16[64,128]{1,0:T(8,128)(2,1)S(1)}, bf16[64,128]{1,0:T(8,128)(2,1)S(1)}, u32[]{:S(2)}, u32[]{:S(2)}) collective-permute-start(bf16[64,128]{1,0:T(8,128)(2,1)S(1)} %get-tuple-element.62.refs_0_), channel_id=1, source_target_pairs={{0,1},{1,0},{2,3},{3,2},{4,5},{5,4},{6,7},{7,6},{8,9},{9,8},{10,11... | collective-permute-start | bytes 49160 | tf_op jit(solution)/shard_map/ppermute | solution.py:46
  79.6 18.8 %collective-permute-start.8 = (bf16[896,128]{1,0:T(8,128)(2,1)S(1)}, bf16[896,128]{1,0:T(8,128)(2,1)S(1)}, u32[]{:S(2)}, u32[]{:S(2)}) collective-permute-start(bf16[896,128]{1,0:T(8,128)(2,1)S(1)} %get-tuple-element.64), channel_id=1, source_target_pairs={{0,2},{1,3},{2,0},{3,1},{4,6},{5,7},{6,4},{7,5},{8,10},{9,11},{10,... | collective-permute-start | bytes 688136 | tf_op jit(solution)/shard_map/ppermute | solution.py:46
  81.3 19.2 %collective-permute-start.9 = (bf16[896,128]{1,0:T(8,128)(2,1)S(1)}, bf16[896,128]{1,0:T(8,128)(2,1)S(1)}, u32[]{:S(2)}, u32[]{:S(2)}) collective-permute-start(bf16[896,128]{1,0:T(8,128)(2,1)S(1)} %get-tuple-element.65), channel_id=1, source_target_pairs={{0,4},{1,5},{2,6},{3,7},{4,0},{5,1},{6,2},{7,3},{8,12},{9,13},{10,... | collective-permute-start | bytes 688136 | tf_op jit(solution)/shard_map/ppermute | solution.py:46
  83.7 16.9 %collective-permute-start.10 = (bf16[896,128]{1,0:T(8,128)(2,1)S(1)}, bf16[896,128]{1,0:T(8,128)(2,1)S(1)}, u32[]{:S(2)}, u32[]{:S(2)}) collective-permute-start(bf16[896,128]{1,0:T(8,128)(2,1)S(1)} %get-tuple-element.66), channel_id=1, source_target_pairs={{0,6},{1,7},{2,4},{3,5},{4,2},{5,3},{6,0},{7,1},{8,14},{9,15},{10,... | collective-permute-start | bytes 688136 | tf_op jit(solution)/shard_map/ppermute | solution.py:46
  100.5 1.9 %collective-permute-start.11 = (bf16[4,512,128]{2,1,0:T(8,128)(2,1)S(1)}, bf16[4,512,128]{2,1,0:T(8,128)(2,1)S(1)}, u32[]{:S(2)}, u32[]{:S(2)}) collective-permute-start(bf16[4,512,128]{2,1,0:T(8,128)(2,1)S(1)} %get-tuple-element.75), channel_id=1, source_target_pairs={{0,1},{1,0},{2,3},{3,2},{4,5},{5,4},{6,7},{7,6},{8,9},{9,8},{10,11... | collective-permute-start | bytes 1572872 | tf_op jit(solution)/shard_map/ppermute | solution.py:46
  103.1 10.2 %collective-permute-start.12 = (bf16[512,128]{1,0:T(8,128)(2,1)S(1)}, bf16[512,128]{1,0:T(8,128)(2,1)S(1)}, u32[]{:S(2)}, u32[]{:S(2)}) collective-permute-start(bf16[512,128]{1,0:T(8,128)(2,1)S(1)} %get-tuple-element.77), channel_id=1, source_target_pairs={{0,2},{1,3},{2,0},{3,1},{4,6},{5,7},{6,4},{7,5},{8,10},{9,11},{10,... | collective-permute-start | bytes 393224 | tf_op jit(solution)/shard_map/ppermute | solution.py:46
  107.6 12.9 %collective-permute-start.13 = (bf16[512,128]{1,0:T(8,128)(2,1)S(1)}, bf16[512,128]{1,0:T(8,128)(2,1)S(1)}, u32[]{:S(2)}, u32[]{:S(2)}) collective-permute-start(bf16[512,128]{1,0:T(8,128)(2,1)S(1)} %get-tuple-element.78), channel_id=1, source_target_pairs={{0,4},{1,5},{2,6},{3,7},{4,0},{5,1},{6,2},{7,3},{8,12},{9,13},{10,... | collective-permute-start | bytes 393224 | tf_op jit(solution)/shard_map/ppermute | solution.py:46
  108.5 11.9 %collective-permute-start.14 = (bf16[512,128]{1,0:T(8,128)(2,1)S(1)}, bf16[512,128]{1,0:T(8,128)(2,1)S(1)}, u32[]{:S(2)}, u32[]{:S(2)}) collective-permute-start(bf16[512,128]{1,0:T(8,128)(2,1)S(1)} %get-tuple-element.79), channel_id=1, source_target_pairs={{0,6},{1,7},{2,4},{3,5},{4,2},{5,3},{6,0},{7,1},{8,14},{9,15},{10,... | collective-permute-start | bytes 393224 | tf_op jit(solution)/shard_map/ppermute | solution.py:46

commit v10 on v9

--- a/solution.py
+++ b/solution.py
@@ -177,8 +177,6 @@
             shape((groups, images, head + 2 * LANES), BF16),
         ],
         limit=58,
-        flops=4 * pix * images * width * inner,
-        moved=2 * pix * images * (2 * width + inner),
         grid=(STEPS,),
         in_specs=[
             *[column(j) for j in range(n_tiles)],
@@ -199,30 +197,6 @@
     return hidden, feature, aux_pre, sent
 
 
-def recon_kernel(n_feature, n_tiles, *refs):
-    feature_refs, decode_refs, recon_refs = refs[:n_feature], refs[n_feature : n_feature + n_tiles], refs[n_feature + n_tiles :]
-    feature = jnp.concatenate([ref[...] for ref in feature_refs], axis=1)
-    for decode_ref, recon_ref in zip(decode_refs, recon_refs):
-        recon_ref[...] = dot(feature, decode_ref[...])
-
-
-def reconstruct(feature, decode, n_tiles):
-    rows = feature[0].shape[0]
-    width = decode.shape[0]
-    block = pl.BlockSpec((rows // STEPS, TILE), lambda g: (g, 0))
-    return call(
-        functools.partial(recon_kernel, len(feature), n_tiles),
-        [shape((rows, TILE), F32)] * n_tiles,
-        limit=57,
-        flops=2 * rows * width * n_tiles * TILE,
-        moved=rows * (2 * width + 4 * n_tiles * TILE),
-        grid=(STEPS,),
-        in_specs=[*[block] * len(feature), *[pl.BlockSpec((width, TILE), lambda g, j=j: (0, j)) for j in range(n_tiles)]],
-        out_specs=[block] * n_tiles,
-        name="reconstruct",
-    )(*feature, *[decode] * n_tiles)
-
-
 def own_index(h):
     per_half = STEPS // 2
     return lambda g, where: (jnp.clip(g - h * per_half, 0, per_half - 1), 0, 0)
@@ -314,10 +288,9 @@
         total[...] = now if g == 0 else total[...] + now
 
 
-def residual_kernel(groups, scale, n_feature, n_recon, n_tiles, n_patch, where_ref, *refs):
+def residual_kernel(groups, scale, n_feature, n_tiles, n_patch, where_ref, *refs):
     feature_refs, refs = refs[:n_feature], refs[n_feature:]
-    recon_refs, refs = refs[:n_recon], refs[n_recon:]
-    decode_refs, refs = refs[: n_tiles - n_recon], refs[n_tiles - n_recon :]
+    decode_refs, refs = refs[:n_tiles], refs[n_tiles:]
     patch_refs, refs = refs[:n_patch], refs[n_patch:]
     grad_refs, refs = refs[:n_tiles], refs[n_tiles:]
     keep_ref, send_ref, target, feature, grads, total, sems = refs
@@ -332,7 +305,7 @@
         now = feature[here]
         for j, grad_ref in enumerate(grad_refs):
             cut = slice(j * TILE, (j + 1) * TILE)
-            recon = recon_refs[j][...] if j < n_recon else dot(now, decode_refs[j - n_recon][...])
+            recon = sum(dot(now[:, k : k + TILE], decode_refs[j][k : k + TILE]) for k in range(0, width, TILE))
             grad = ((recon - target[:, :, cut].reshape(size, TILE).astype(F32)) * scale).astype(BF16)
             grad_ref[...] = grad
             grads[here, cut] = grad
@@ -343,7 +316,7 @@
     by_step(copies_of(feature_refs, feature, sems), body)
 
 
-def residual(where, feature, recon, decode, patch_args, patch_specs, images, scale, groups):
+def residual(where, feature, decode, patch_args, patch_specs, images, scale, groups):
     rows = feature[0].shape[0]
     width, n = decode.shape
     size = rows // STEPS
@@ -353,18 +326,17 @@
     block = pl.BlockSpec((size, TILE), lambda g, where: (g, 0))
     column = lambda j: pl.BlockSpec((width, TILE), lambda g, where: (0, j))
     *grad, keep, send = call(
-        functools.partial(residual_kernel, groups, scale, len(feature), len(recon), n_tiles, len(patch_args)),
+        functools.partial(residual_kernel, groups, scale, len(feature), n_tiles, len(patch_args)),
         [*[shape((rows, TILE), BF16)] * n_tiles, shape(parts, BF16), shape(parts, BF16)],
         limit=58,
-        flops=2 * rows * width * (2 * n - len(recon) * TILE),
+        flops=4 * rows * width * n,
         moved=rows * (2 * width + 6 * n),
         grid_spec=pltpu.PrefetchScalarGridSpec(
             num_scalar_prefetch=1,
             grid=(STEPS,),
             in_specs=[
                 *[HBM] * len(feature),
-                *[block] * len(recon),
-                *[column(j) for j in range(len(recon), n_tiles)],
+                *[column(j) for j in range(n_tiles)],
                 *patch_specs,
             ],
             out_specs=[*[block] * n_tiles, dealt, dealt],
@@ -377,7 +349,7 @@
             ],
         ),
         name="residual",
-    )(where, *feature, *recon, *[decode] * (n_tiles - len(recon)), *patch_args)
+    )(where, *feature, *[decode] * n_tiles, *patch_args)
     return grad, keep, send
 
 
@@ -524,7 +496,6 @@
         logits_kernel,
         shape((groups, images, 2 * head + LANES), BF16),
         limit=16,
-        flops=2e10,
         in_specs=[SMEM, VMEM, VMEM],
         scratch_shapes=[pltpu.VMEM((groups * images, classes), F32)],
         name="class_logits",
@@ -560,8 +531,7 @@
     )(got, aux_pre)
 
 
-def class_kernel(norm, n, where_ref, klass_ref, got_ref, stats_ref, *refs):
-    grads_refs, (class_ref, aux_ref) = refs[:-2], refs[-2:]
+def class_kernel(norm, where_ref, klass_ref, got_ref, stats_ref, mine_ref, other_ref, class_ref, aux_ref):
     groups, images, _ = got_ref.shape
     head = class_ref.shape[1]
     classes, part = class_ref.shape[0], aux_ref.shape[0]
@@ -580,23 +550,20 @@
     class_ref[...] = dot(logit_grad, got[:, :head], ROWS_0)
     total = jnp.zeros(aux_ref.shape, F32)
     for d in range(groups):
-        k, core = d // 2, d % 2
-        at = n + core * (head // part) * images
-        grad = jnp.concatenate(
-            [grads_refs[k][at + q * images : at + (q + 1) * images, :] for q in range(head // part)], axis=1
-        )
-        pooled = got_ref[((where_ref[ME] >> 1) ^ k) * 2 + core, :, head : head + part]
+        k, ref = d // 2, other_ref if d % 2 else mine_ref
+        grad = jnp.concatenate([ref[k, q * images : (q + 1) * images] for q in range(head // part)], axis=1)
+        pooled = got_ref[where_ref[ME] ^ d, :, head : head + part]
         total += dot(pooled, grad, ROWS_0).astype(BF16).astype(F32)
     aux_ref[...] = total
 
 
-def class_backward(where, klass, got, partial, grads, n_decode, norm):
+def class_backward(where, klass, got, partial, mine, other, norm):
     groups, images, wide = partial.shape
     classes, head = klass.shape
     whole = lambda *dims: pl.BlockSpec(dims, lambda i: (0,) * len(dims))
-    part = grads[0].shape[1]
+    part = mine.shape[2]
     return call(
-        functools.partial(class_kernel, norm, n_decode),
+        functools.partial(class_kernel, norm),
         [shape((classes, head), F32), shape((part, head), F32)],
         limit=20,
         flops=2 * groups * images * classes * head,
@@ -607,40 +574,42 @@
             whole(*klass.shape),
             whole(*got.shape),
             pl.BlockSpec((groups, images, LANES), lambda i: (0, 0, wide // LANES - 1)),
-            *[whole(*g.shape) for g in grads],
+            whole(*mine.shape),
+            whole(*other.shape),
         ],
         out_specs=[whole(classes, head), whole(part, head)],
         name="class_backward",
-    )(where, klass, got, partial, *grads)
-
-
-def chip_kernel(n_extra, where_ref, keep_ref, got_ref, *refs):
-    extra, outs = refs[:n_extra], refs[n_extra:]
+    )(where, klass, got, partial, mine, other)
+
+
+def chip_kernel(chips, below, collect, where_ref, keep_ref, got_ref, *refs):
+    refs, outs = refs[: below + collect], refs[below + collect :]
     n = keep_ref.shape[1]
     chip = where_ref[ME] >> 1
-    for k, out_ref in enumerate(outs):
-        out_ref[:n] = (keep_ref[chip ^ k].astype(F32) + got_ref[chip ^ k].astype(F32)).astype(BF16)
-    if n_extra:
-        mine, other = extra[0][...].astype(F32), extra[1][...].astype(F32)
-        even = where_ref[CORE] == 0
-        pair = [jnp.where(even, mine, other).astype(BF16), jnp.where(even, other, mine).astype(BF16)]
-        size = mine.shape[0]
-        for out_ref in outs:
-            for c in range(2):
-                out_ref[n + c * size : n + (c + 1) * size] = pair[c]
-
-
-def add_cores(where, keep, send, extra=()):
+    for k in range(chips):
+        outs[k][:n] = (keep_ref[chip ^ k].astype(F32) + got_ref[chip ^ k].astype(F32)).astype(BF16)
+        for ref in refs[:below]:
+            outs[k][n:] = ref[...]
+    if collect:
+        size = outs[-1].shape[1]
+        for k, ref in enumerate(refs[below:]):
+            outs[-1][k] = ref[ref.shape[0] - size :]
+
+
+def add_cores(where, keep, send, below=(), collect=(), size=0):
     chips, n, part = keep.shape
-    extra = [e for own in extra for e in (own, swap(own, "dp", 1))]
-    rows = n + sum(e.shape[0] for e in extra)
-    return call(
-        functools.partial(chip_kernel, len(extra)),
-        [shape((rows, part), BF16)] * chips,
+    rows = n + sum(e.shape[0] for e in below)
+    outs = [shape((rows, part), BF16)] * chips
+    if collect:
+        outs.append(shape((len(collect), size, part), BF16))
+    outs = call(
+        functools.partial(chip_kernel, chips, len(below), len(collect)),
+        outs,
         limit=16,
-        in_specs=[SMEM, VMEM, VMEM, *[VMEM] * len(extra)],
+        in_specs=[SMEM, VMEM, VMEM, *[VMEM] * (len(below) + len(collect))],
         name="add_cores",
-    )(where, keep, swap(send, "dp", 1), *extra)
+    )(where, keep, swap(send, "dp", 1), *below, *collect)
+    return (outs[:chips], outs[chips]) if collect else outs
 
 
 def exchange_chips(parts):
@@ -695,26 +664,26 @@
 
     hidden, feature, aux_pre, sent = forward(acts, first, second, aux, labels, groups)
     if paired:
-        sent = after(sent, (x[0], y[0]))
+        sent = after(sent, x[0])
         diagonal = [swap(after(x[0], aux_pre), "section", 2), swap(after(y[0], aux_pre), "section", 1)]
-        x.append(swap(after(halves[1], aux_pre), "section", 1))
-        y.insert(0, swap(after(halves[0], aux_pre), "section", 2))
+        x.append(swap(halves[1], "section", 1))
+        y.insert(0, swap(halves[0], "section", 2))
         target = patch_operands([halves, x, y, diagonal], [0, 1, 2, 3], [0, 1, 2, 3])
     else:
         target = [target], [pl.BlockSpec((pix // STEPS, images, n_decode), lambda g, where: (g, 0, 0))]
     got = exchange(sent)
-    recon = reconstruct([after(feature[0], sent), *feature[1:]], decode, 1)
-    sent = class_logits(where, after(got, recon[0]), klass)
+    sent = class_logits(where, got, klass)
     partial = exchange(sent)
-    grad, keep, send = residual(after(where, sent), feature, recon, decode, *target, images, scale, groups)
+    grad, keep, send = residual(after(where, sent), feature, decode, *target, images, scale, groups)
     aux_grad, aux_cut = aux_backward(partial, aux_pre, width // groups, norm)
     chip_decode = add_cores(where, keep, send, [aux_cut])
     sum_decode = exchange_chips(chip_decode)
     keep, send = backward(
         where, grad, hidden, acts.reshape(rows, width), decode, after(aux_grad, chip_decode[0]), aux, second, groups
     )
-    sum_last = exchange_chips(add_cores(where, keep, after(send, sum_decode)))
-    grad_class, grad_aux = class_backward(where, klass, got, partial, sum_decode, n_decode, norm)
+    chip_last, mine = add_cores(where, keep, after(send, sum_decode), collect=sum_decode, size=aux_cut.shape[0])
+    sum_last = exchange_chips(chip_last)
+    grad_class, grad_aux = class_backward(where, klass, got, partial, mine, swap(mine, "dp", 1), norm)
     grad_first, grad_second, grad_decode = finish(sum_decode, sum_last, inner, groups, n_decode)
     return grad_first[None], grad_second[None], grad_decode[None], grad_aux[None], grad_class[None]
 

time: 122 us -> 113 us (0.926)
  blocking collectives: 0 us -> 13.2 us
  starting transfers between devices: 30.6 us -> 21.9 us
  waiting for transfers between devices: 27.6 us -> 19.6 us
  Pallas kernels: 60.8 us -> 55.4 us
    all_to_all x0 -> x1, blocking collectives: none -> 13.2 us  [exchange(): lax.all_to_all(value, 'dp', 0, 0, axis_index_groups=groups, tiled=True)]
    ppermute x15, waiting for transfers between devices: 27.6 us -> 19.6 us  [swap(): return lax.ppermute(value, axis, [(i, i ^ bits) for i in range(count)])]
    all_to_all x2 -> x1, starting transfers between devices: 9.91 us -> 3.6 us  [exchange(): lax.all_to_all(value, 'dp', 0, 0, axis_index_groups=groups, tiled=True)]
    pallas_call x5 -> x4, Pallas kernels: 29.3 us -> 23.7 us  [the longest x1 19 us: residual(): call(functools.partial(residual_kernel, groups, scale, len(feature), n_ti...]
    ppermute x15, starting transfers between devices: 20.7 us -> 18.3 us  [swap(): return lax.ppermute(value, axis, [(i, i ^ bits) for i in range(count)])]
  transfers between devices with their start and end apart: 17 -> 16, of which waited for: 8 -> 8; matrix products, arithmetic and copies ran while one was open for 0% -> 0% of each run, Pallas kernels for 47% -> 45%
where the time goes in v10:
time: 113 us
  Pallas kernels  55.4 us (49%)
  starting transfers between devices  21.9 us (19%)
  waiting for transfers between devices  19.6 us (17%)
  blocking collectives  13.2 us (12%)
  local copies, waits for them, and re-layouts  1.55 us (1%)
    ppermute x15, waiting for transfers between devices, swap(): return lax.ppermute(value, axis, [(i, i ^ bits) for i in range(count)])  19.6 us
    pallas_call x1, Pallas kernels, residual(): call(functools.partial(residual_kernel, groups, scale, len(feature), n_ti...  19 us
    ppermute x15, starting transfers between devices, swap(): return lax.ppermute(value, axis, [(i, i ^ bits) for i in range(count)])  18.3 us
    pallas_call x1, Pallas kernels, backward(): call(functools.partial(backward_kernel, groups, len(grad), n_decode), [sh...  14.3 us
    all_to_all x1, blocking collectives, exchange(): lax.all_to_all(value, 'dp', 0, 0, axis_index_groups=groups, tiled=True)  13.2 us
    pallas_call x1, Pallas kernels, forward(): call(functools.partial(forward_kernel, n_tiles, pix), [shape((pix * image...  9.74 us
    pallas_call x2, Pallas kernels, pack(): call(functools.partial(pack_kernel, h * half), shape(dims, BF16), limit=2...  3.62 us
    all_to_all x1, starting transfers between devices, exchange(): lax.all_to_all(value, 'dp', 0, 0, axis_index_groups=groups, tiled=True)  3.6 us
  transfers between devices with their start and end apart: 16, of which 8 were waited for; matrix products, arithmetic and copies ran while one was open for 0% of the time, Pallas kernels for 45%

profile of v10, /device:TPU:0, one launch (start us, length us, event | category | flops | bytes accessed | tf_op | source)
XLA Modules:
  0.0 112.6 jit_solution(9890164129726377172)
XLA Ops:
  0.7 0.1 stack.47.where_ref
  0.7 0.0 copy-start
  0.8 1.4 %copy-done = bf16[16,196,192]{1,2,0:T(8,128)(2,1)S(1)} copy-done((bf16[16,196,192]{1,2,0:T(8,128)(2,1)S(1)}, bf16[16,196,192]{1,2,0:T(8,128)(2,1)}, u32[]{:S(2)}) %copy-start) | copy-done | bytes 1204248
  2.2 1.8 %pack_patches.2.refs_8_.refs_16_ = bf16[147,16,128]{2,1,0:T(8,128)(2,1)S(1)} custom-call(s32[11]{0:T(128)S(1)} %stack.47.where_ref, bf16[16,192,196]{2,1,0:T(8,128)(2,1)S(1)} %bitcast.27, bf16[16,192,196]{2,1,0:T(8,128)(2,1)S(1)} %bitcast.28, bf16[16,192,196]{2,1,0:T(8,128)(2,1)S(1)} %bitcast.29, bf16[16,192,196]{2,1,0:T(8,128)(2,1)S(1)} %bitcast.30), custom_call_target="tpu_custom_call" | custom-call | tf_op jit(solution)/shard_map/pack_patches/pallas_call | solution.py:99
  4.0 3.0 %collective-permute-start.3 = (bf16[147,16,128]{2,1,0:T(8,128)(2,1)S(1)}, bf16[147,16,128]{2,1,0:T(8,128)(2,1)}, u32[]{:S(2)}, u32[]{:S(2)}) collective-permute-start(bf16[147,16,128]{2,1,0:T(8,128)(2,1)S(1)} %pack_patches.2.refs_8_.refs_16_), channel_id=1, source_target_pairs={{0,16},{8,24},{16,0},{24,8},{1,17},{9,25},{17,1},{25,9},{2,18},{10... | collective-permute-start | bytes 1806344 | tf_op jit(solution)/shard_map/ppermute | solution.py:46
  7.0 1.8 %pack_patches.3.refs_7_.refs_15_ = bf16[147,16,128]{2,1,0:T(8,128)(2,1)S(1)} custom-call(s32[11]{0:T(128)S(1)} %stack.47.where_ref, bf16[16,192,196]{2,1,0:T(8,128)(2,1)S(1)} %bitcast.31, bf16[16,192,196]{2,1,0:T(8,128)(2,1)S(1)} %bitcast.32, bf16[16,192,196]{2,1,0:T(8,128)(2,1)S(1)} %bitcast.33, bf16[16,192,196]{2,1,0:T(8,128)(2,1)S(1)} %bitcast.34), custom_call_target="tpu_custom_call" | custom-call | tf_op jit(solution)/shard_map/pack_patches/pallas_call | solution.py:99
  8.8 1.6 %collective-permute-start = (bf16[147,16,128]{2,1,0:T(8,128)(2,1)S(1)}, bf16[147,16,128]{2,1,0:T(8,128)(2,1)}, u32[]{:S(2)}, u32[]{:S(2)}) collective-permute-start(bf16[147,16,128]{2,1,0:T(8,128)(2,1)S(1)} %pack_patches.3.refs_7_.refs_15_), channel_id=1, source_target_pairs={{0,8},{8,0},{16,24},{24,16},{1,9},{9,1},{17,25},{25,17},{2,10},{10... | collective-permute-start | bytes 1806344 | tf_op jit(solution)/shard_map/ppermute | solution.py:46
  10.4 0.5 collective-permute-start.2
  10.9 0.1 collective-permute-start.1
  11.0 9.7 %forward.1 = (bf16[3136,256]{1,0:T(8,128)(2,1)}, bf16[3136,256]{1,0:T(8,128)(2,1)}, bf16[3136,256]{1,0:T(8,128)(2,1)}, bf16[3136,256]{1,0:T(8,128)(2,1)}, bf16[3...) custom-call(bf16[196,16,1024]{2,1,0:T(8,128)(2,1)} %bitcast.48, ...), custom_call_target="tpu_custom_call" | custom-call | tf_op jit(solution)/shard_map/forward/pallas_call | solution.py:171
  20.8 0.8 collective-permute-done.3.refs_12_.refs_20_
  21.5 4.0 %collective-permute-done.refs_9_.refs_17_ = bf16[147,16,128]{2,1,0:T(8,128)(2,1)} collective-permute-done((bf16[147,16,128]{2,1,0:T(8,128)(2,1)S(1)}, bf16[147,16,128]{2,1,0:T(8,128)(2,1)}, u32[]{:S(2)}, u32[]{:S(2)}) %collective-permute-start) | collective-permute-done | bytes 602144 | tf_op jit(solution)/shard_map/ppermute | solution.py:46
  25.5 0.0 collective-permute-start.4
  25.5 2.0 %collective-permute-start.5 = (bf16[147,16,128]{2,1,0:T(8,128)(2,1)}, bf16[147,16,128]{2,1,0:T(8,128)(2,1)}, u32[]{:S(2)}, u32[]{:S(2)}) collective-permute-start(bf16[147,16,128]{2,1,0:T(8,128)(2,1)} %collective-permute-done.3.refs_12_.refs_20_), channel_id=1, source_target_pairs={{0,8},{8,0},{16,24},{24,16},{1,9},{9,1},{17,25},{25,17},{2,10},{10... | collective-permute-start | bytes 1806344 | tf_op jit(solution)/shard_map/ppermute | solution.py:46
  27.5 13.2 %all_to_all.10.got_ref = bf16[8,16,768]{2,1,0:T(8,128)(2,1)S(1)} all-to-all(bf16[8,16,768]{2,1,0:T(8,128)(2,1)} %get-tuple-element.44), channel_id=1, replica_groups=mesh['section'=4,'dp'=8] {'dp'}, dimensions={0} | all-to-all | bytes 393216 | tf_op jit(solution)/shard_map/all_to_all | solution.py:50
  40.8 2.7 %class_logits.1 = bf16[8,16,1152]{2,1,0:T(8,128)(2,1)} custom-call(s32[11]{0:T(128)S(1)} %stack.47.where_ref, bf16[8,16,768]{2,1,0:T(8,128)(2,1)S(1)} %all_to_all.10.got_ref, bf16[1408,512]{1,0:T(8,128)(2,1)S(1)} %bitcast.35), custom_call_target="tpu_custom_call" | custom-call | tf_op jit(solution)/shard_map/class_logits/pallas_call | solution.py:495
  43.4 3.6 %all-to-all-start.1 = ((bf16[8,16,1152]{2,1,0:T(8,128)(2,1)}), bf16[8,16,1152]{2,1,0:T(8,128)(2,1)S(1)}, u32[]{:S(2)}, u32[]{:S(2)}) async-start(bf16[8,16,1152]{2,1,0:T(8,128)(2,1)} %class_logits.1), calls=%async_computation.1 | async-start | bytes 589824 | tf_op jit(solution)/shard_map/all_to_all | solution.py:50
  47.0 0.0 collective-permute-done.2.refs_11_.refs_19_
  47.1 0.0 collective-permute-done.1.refs_10_.refs_18_
  47.1 0.0 collective-permute-done.4.refs_13_.refs_21_
  47.1 2.8 %collective-permute-done.5.refs_14_.refs_22_ = bf16[147,16,128]{2,1,0:T(8,128)(2,1)} collective-permute-done((bf16[147,16,128]{2,1,0:T(8,128)(2,1)}, bf16[147,16,128]{2,1,0:T(8,128)(2,1)}, u32[]{:S(2)}, u32[]{:S(2)}) %collective-permute-start.5) | collective-permute-done | bytes 602144 | tf_op jit(solution)/shard_map/ppermute | solution.py:46
  49.9 19.0 %residual.1 = (bf16[3136,256]{1,0:T(8,128)(2,1)}, bf16[3136,256]{1,0:T(8,128)(2,1)}, bf16[3136,256]{1,0:T(8,128)(2,1)}, bf16[4,768,128]{2,1,0:T(8,128)(2,1)}, bf16[4,768,128]{2,1,0:T(8,128)(2,1)}) custom-call(s32[11]{0:T(128)} %copy-done.7, bf16[3136,256]{1,0:T(8,128)(2,1)} %get-tuple-element.46.refs_0_, bf16[3136,256]{1,0:T(8,128)(2,1)} %get-tuple-element.47.refs_1_, ...), custom_call_target="tpu_custom_call" | custom-call | flops 9865003008 | bytes 20873216 | tf_op jit(solution)/shard_map/residual/pallas_call | solution.py:328
  68.9 0.0 copy-start.8
  68.9 0.1 collective-permute-start.6
  69.0 0.0 all-to-all-done.1.got_ref.stats_ref
  69.0 0.0 copy-start.9
  69.0 0.3 aux_backward.1
  69.4 0.0 copy-start.6
  69.4 2.1 %collective-permute-done.6.got_ref = bf16[4,768,128]{2,1,0:T(8,128)(2,1)S(1)} collective-permute-done((bf16[4,768,128]{2,1,0:T(8,128)(2,1)}, bf16[4,768,128]{2,1,0:T(8,128)(2,1)S(1)}, u32[]{:S(2)}, u32[]{:S(2)}) %collective-permute-start.6) | collective-permute-done | bytes 786464 | tf_op jit(solution)/shard_map/ppermute | solution.py:46
  71.5 0.7 add_cores.2
  72.2 1.6 %collective-permute-start.7 = (bf16[832,128]{1,0:T(8,128)(2,1)S(1)}, bf16[832,128]{1,0:T(8,128)(2,1)S(1)}, u32[]{:S(2)}, u32[]{:S(2)}) collective-permute-start(bf16[832,128]{1,0:T(8,128)(2,1)S(1)} %get-tuple-element.57), channel_id=1, source_target_pairs={{0,2},{1,3},{2,0},{3,1},{4,6},{5,7},{6,4},{7,5},{8,10},{9,11},{10,... | collective-permute-start | bytes 638984 | tf_op jit(solution)/shard_map/ppermute | solution.py:46
  73.8 2.6 %collective-permute-start.8 = (bf16[832,128]{1,0:T(8,128)(2,1)S(1)}, bf16[832,128]{1,0:T(8,128)(2,1)S(1)}, u32[]{:S(2)}, u32[]{:S(2)}) collective-permute-start(bf16[832,128]{1,0:T(8,128)(2,1)S(1)} %get-tuple-element.58), channel_id=1, source_target_pairs={{0,4},{1,5},{2,6},{3,7},{4,0},{5,1},{6,2},{7,3},{8,12},{9,13},{10,... | collective-permute-start | bytes 638984 | tf_op jit(solution)/shard_map/ppermute | solution.py:46
  76.4 0.2 collective-permute-start.9
  76.7 14.3 %backward.1 = (bf16[4,512,128]{2,1,0:T(8,128)(2,1)S(1)}, bf16[4,512,128]{2,1,0:T(8,128)(2,1)S(1)}) custom-call(s32[11]{0:T(128)S(1)} %copy-done.8, bf16[3136,256]{1,0:T(8,128)(2,1)S(1)} %copy-done.11, bf16[3136,256]{1,0:T(8,128)(2,1)S(1)} %copy-done.12, bf16[3136,256]{1,0:T(8,128)(2,1)S(1)} %copy-done.13, bf16[1024,768]{1,0:T(8,128)(2,1)S(1)} %bitcast.44, ...), custom_call_target="tpu_custom_call" | custom-call | flops 9865003008 | bytes 12845056 | tf_op jit(solution)/shard_map/backward/pallas_call | solution.py:407
  91.0 1.0 collective-permute-done.8.refs_2_
  92.0 0.0 collective-permute-done.9.refs_3_
  92.0 0.0 collective-permute-start.10
  92.0 1.9 %collective-permute-done.10.got_ref = bf16[4,512,128]{2,1,0:T(8,128)(2,1)S(1)} collective-permute-done((bf16[4,512,128]{2,1,0:T(8,128)(2,1)S(1)}, bf16[4,512,128]{2,1,0:T(8,128)(2,1)S(1)}, u32[]{:S(2)}, u32[]{:S(2)}) %collective-permute-start.10) | collective-permute-done | bytes 524320 | tf_op jit(solution)/shard_map/ppermute | solution.py:46
  93.9 0.7 add_cores.3
  94.6 4.1 %collective-permute-start.11 = (bf16[512,128]{1,0:T(8,128)(2,1)S(1)}, bf16[512,128]{1,0:T(8,128)(2,1)S(1)}, u32[]{:S(2)}, u32[]{:S(2)}) collective-permute-start(bf16[512,128]{1,0:T(8,128)(2,1)S(1)} %get-tuple-element.70), channel_id=1, source_target_pairs={{0,2},{1,3},{2,0},{3,1},{4,6},{5,7},{6,4},{7,5},{8,10},{9,11},{10,... | collective-permute-start | bytes 393224 | tf_op jit(solution)/shard_map/ppermute | solution.py:46
  98.7 1.1 collective-permute-start.12
  99.8 1.4 %collective-permute-start.13 = (bf16[512,128]{1,0:T(8,128)(2,1)S(1)}, bf16[512,128]{1,0:T(8,128)(2,1)S(1)}, u32[]{:S(2)}, u32[]{:S(2)}) collective-permute-start(bf16[512,128]{1,0:T(8,128)(2,1)S(1)} %get-tuple-element.72), channel_id=1, source_target_pairs={{0,6},{1,7},{2,4},{3,5},{4,2},{5,3},{6,0},{7,1},{8,14},{9,15},{10,... | collective-permute-start | bytes 393224 | tf_op jit(solution)/shard_map/ppermute | solution.py:46
  101.2 0.0 collective-permute-start.14
  101.2 1.3 %collective-permute-done.14.other_ref = bf16[4,64,128]{2,1,0:T(8,128)(2,1)S(1)} collective-permute-done((bf16[4,64,128]{2,1,0:T(8,128)(2,1)S(1)}, bf16[4,64,128]{2,1,0:T(8,128)(2,1)S(1)}, u32[]{:S(2)}, u32[]{:S(2)}) %collective-permute-start.14) | collective-permute-done | bytes 65568 | tf_op jit(solution)/shard_map/ppermute | solution.py:46
  102.4 3.3 %class_backward.1 = (f32[1408,512]{1,0:T(8,128)}, f32[128,512]{1,0:T(8,128)}) custom-call(s32[11]{0:T(128)S(1)} %copy-done.8, bf16[1408,512]{1,0:T(8,128)(2,1)S(1)} %bitcast.36, bf16[8,16,768]{2,1,0:T(8,128)(2,1)S(1)} %all_to_all.10.got_ref, bf16[8,16,1152]{2,1,0:T(8,128)(2,1)S(1)} %all-to-all-done.1.got_ref.stats_ref, ...), custom_call_target="tpu_custom_call" | custom-call | flops 184549376 | bytes 2883584 | tf_op jit(solution)/shard_map/class_backward/pallas_call | solution.py:565
  105.7 0.0 collective-permute-done.11.refs_5_
  105.7 5.8 %collective-permute-done.12.refs_6_ = bf16[512,128]{1,0:T(8,128)(2,1)S(1)} collective-permute-done((bf16[512,128]{1,0:T(8,128)(2,1)S(1)}, bf16[512,128]{1,0:T(8,128)(2,1)S(1)}, u32[]{:S(2)}, u32[]{:S(2)}) %collective-permute-start.12) | collective-permute-done | bytes 131104 | tf_op jit(solution)/shard_map/ppermute | solution.py:46
  111.6 1.0 finish.1
  (25 shorter events, 0.1 us)
Async XLA Ops:
  0.7 40.0 %copy-start.7 = (s32[11]{0:T(128)}, s32[11]{0:T(128)S(1)}, u32[]{:S(2)}) copy-start(s32[11]{0:T(128)S(1)} %stack.47.where_ref) | copy-start | bytes 136
  0.7 1.4 %copy-start = (bf16[16,196,192]{1,2,0:T(8,128)(2,1)S(1)}, bf16[16,196,192]{1,2,0:T(8,128)(2,1)}, u32[]{:S(2)}) copy-start(bf16[16,196,192]{1,2,0:T(8,128)(2,1)} %param.9) | copy-start | bytes 3612676
  4.0 6.9 %copy-start.4 = (bf16[147,16,128]{2,1,0:T(8,128)(2,1)}, bf16[147,16,128]{2,1,0:T(8,128)(2,1)S(1)}, u32[]{:S(2)}) copy-start(bf16[147,16,128]{2,1,0:T(8,128)(2,1)S(1)} %pack_patches.2.refs_8_.refs_16_) | copy-start | bytes 1806340
  4.0 17.6 %collective-permute-start.3 = (bf16[147,16,128]{2,1,0:T(8,128)(2,1)S(1)}, bf16[147,16,128]{2,1,0:T(8,128)(2,1)}, u32[]{:S(2)}, u32[]{:S(2)}) collective-permute-start(bf16[147,16,128]{2,1,0:T(8,128)(2,1)S(1)} %pack_patches.2.refs_8_.refs_16_), channel_id=1, source_target_pairs={{0,16},{8,24},{16,0},{24,8},{1,17},{9,25},{17,1},{25,9},{2,18},{10... | collective-permute-start | bytes 1806344 | tf_op jit(solution)/shard_map/ppermute | solution.py:46
  8.8 11.9 %copy-start.5 = (bf16[147,16,128]{2,1,0:T(8,128)(2,1)}, bf16[147,16,128]{2,1,0:T(8,128)(2,1)S(1)}, u32[]{:S(2)}) copy-start(bf16[147,16,128]{2,1,0:T(8,128)(2,1)S(1)} %pack_patches.3.refs_7_.refs_15_) | copy-start | bytes 1806340
  8.8 16.7 %collective-permute-start = (bf16[147,16,128]{2,1,0:T(8,128)(2,1)S(1)}, bf16[147,16,128]{2,1,0:T(8,128)(2,1)}, u32[]{:S(2)}, u32[]{:S(2)}) collective-permute-start(bf16[147,16,128]{2,1,0:T(8,128)(2,1)S(1)} %pack_patches.3.refs_7_.refs_15_), channel_id=1, source_target_pairs={{0,8},{8,0},{16,24},{24,16},{1,9},{9,1},{17,25},{25,17},{2,10},{10... | collective-permute-start | bytes 1806344 | tf_op jit(solution)/shard_map/ppermute | solution.py:46
  10.4 36.6 %collective-permute-start.2 = (bf16[147,16,128]{2,1,0:T(8,128)(2,1)S(1)}, bf16[147,16,128]{2,1,0:T(8,128)(2,1)}, u32[]{:S(2)}, u32[]{:S(2)}) collective-permute-start(bf16[147,16,128]{2,1,0:T(8,128)(2,1)S(1)} %pack_patches.3.refs_7_.refs_15_), channel_id=1, source_target_pairs={{0,16},{8,24},{16,0},{24,8},{1,17},{9,25},{17,1},{25,9},{2,18},{10... | collective-permute-start | bytes 1806344 | tf_op jit(solution)/shard_map/ppermute | solution.py:46
  10.9 36.1 %collective-permute-start.1 = (bf16[147,16,128]{2,1,0:T(8,128)(2,1)S(1)}, bf16[147,16,128]{2,1,0:T(8,128)(2,1)}, u32[]{:S(2)}, u32[]{:S(2)}) collective-permute-start(bf16[147,16,128]{2,1,0:T(8,128)(2,1)S(1)} %pack_patches.2.refs_8_.refs_16_), channel_id=1, source_target_pairs={{0,8},{8,0},{16,24},{24,16},{1,9},{9,1},{17,25},{25,17},{2,10},{10... | collective-permute-start | bytes 1806344 | tf_op jit(solution)/shard_map/ppermute | solution.py:46
  11.0 29.8 %copy-start.1 = (bf16[1,1408,512]{2,1,0:T(8,128)(2,1)S(1)}, bf16[1,1408,512]{2,1,0:T(8,128)(2,1)}, u32[]{:S(2)}) copy-start(bf16[1,1408,512]{2,1,0:T(8,128)(2,1)} %param.15) | copy-start | bytes 4325380
  25.5 21.5 %collective-permute-start.4 = (bf16[147,16,128]{2,1,0:T(8,128)(2,1)}, bf16[147,16,128]{2,1,0:T(8,128)(2,1)}, u32[]{:S(2)}, u32[]{:S(2)}) collective-permute-start(bf16[147,16,128]{2,1,0:T(8,128)(2,1)} %collective-permute-done.refs_9_.refs_17_), channel_id=1, source_target_pairs={{0,16},{8,24},{16,0},{24,8},{1,17},{9,25},{17,1},{25,9},{2,18},{10... | collective-permute-start | bytes 1806344 | tf_op jit(solution)/shard_map/ppermute | solution.py:46
  25.5 24.3 %collective-permute-start.5 = (bf16[147,16,128]{2,1,0:T(8,128)(2,1)}, bf16[147,16,128]{2,1,0:T(8,128)(2,1)}, u32[]{:S(2)}, u32[]{:S(2)}) collective-permute-start(bf16[147,16,128]{2,1,0:T(8,128)(2,1)} %collective-permute-done.3.refs_12_.refs_20_), channel_id=1, source_target_pairs={{0,8},{8,0},{16,24},{24,16},{1,9},{9,1},{17,25},{25,17},{2,10},{10... | collective-permute-start | bytes 1806344 | tf_op jit(solution)/shard_map/ppermute | solution.py:46
  43.4 25.5 %all-to-all-start.1 = ((bf16[8,16,1152]{2,1,0:T(8,128)(2,1)}), bf16[8,16,1152]{2,1,0:T(8,128)(2,1)S(1)}, u32[]{:S(2)}, u32[]{:S(2)}) async-start(bf16[8,16,1152]{2,1,0:T(8,128)(2,1)} %class_logits.1), calls=%async_computation.1 | async-start | bytes 589824 | tf_op jit(solution)/shard_map/all_to_all | solution.py:50
  49.9 19.1 %copy-start.10 = (f32[16,512]{1,0:T(8,128)S(1)}, f32[16,512]{1,0:T(8,128)}, u32[]{:S(2)}) copy-start(f32[16,512]{1,0:T(8,128)} %get-tuple-element.50.aux_pre_ref) | copy-start | bytes 98308
  68.9 2.6 %copy-start.3 = (bf16[4,768,128]{2,1,0:T(8,128)(2,1)S(1)}, bf16[4,768,128]{2,1,0:T(8,128)(2,1)}, u32[]{:S(2)}) copy-start(bf16[4,768,128]{2,1,0:T(8,128)(2,1)} %get-tuple-element.53.keep_ref) | copy-start | bytes 2359300
  68.9 2.6 %copy-start.8 = (s32[11]{0:T(128)S(1)}, s32[11]{0:T(128)}, u32[]{:S(2)}) copy-start(s32[11]{0:T(128)} %copy-done.7) | copy-start | bytes 136
  68.9 2.6 %collective-permute-start.6 = (bf16[4,768,128]{2,1,0:T(8,128)(2,1)}, bf16[4,768,128]{2,1,0:T(8,128)(2,1)S(1)}, u32[]{:S(2)}, u32[]{:S(2)}) collective-permute-start(bf16[4,768,128]{2,1,0:T(8,128)(2,1)} %get-tuple-element.54), channel_id=1, source_target_pairs={{0,1},{1,0},{2,3},{3,2},{4,5},{5,4},{6,7},{7,6},{8,9},{9,8},{10,11... | collective-permute-start | bytes 2359304 | tf_op jit(solution)/shard_map/ppermute | solution.py:46
  69.0 7.7 %copy-start.9 = (bf16[1,1024,768]{2,1,0:T(8,128)(2,1)S(1)}, bf16[1,1024,768]{2,1,0:T(8,128)(2,1)}, u32[]{:S(2)}) copy-start(bf16[1,1024,768]{2,1,0:T(8,128)(2,1)} %param.13) | copy-start | bytes 4718596
  69.0 7.6 %copy-start.11 = (bf16[3136,256]{1,0:T(8,128)(2,1)S(1)}, bf16[3136,256]{1,0:T(8,128)(2,1)}, u32[]{:S(2)}) copy-start(bf16[3136,256]{1,0:T(8,128)(2,1)} %get-tuple-element.60.refs_0_) | copy-start | bytes 4816900
  69.0 7.6 %copy-start.12 = (bf16[3136,256]{1,0:T(8,128)(2,1)S(1)}, bf16[3136,256]{1,0:T(8,128)(2,1)}, u32[]{:S(2)}) copy-start(bf16[3136,256]{1,0:T(8,128)(2,1)} %get-tuple-element.61.refs_1_) | copy-start | bytes 4816900
  69.0 7.6 %copy-start.13 = (bf16[3136,256]{1,0:T(8,128)(2,1)S(1)}, bf16[3136,256]{1,0:T(8,128)(2,1)}, u32[]{:S(2)}) copy-start(bf16[3136,256]{1,0:T(8,128)(2,1)} %get-tuple-element.62.refs_2_) | copy-start | bytes 4816900
  69.4 7.3 %copy-start.2 = (bf16[1,1024,512]{2,1,0:T(8,128)(2,1)S(1)}, bf16[1,1024,512]{2,1,0:T(8,128)(2,1)}, u32[]{:S(2)}) copy-start(bf16[1,1024,512]{2,1,0:T(8,128)(2,1)} %param.14) | copy-start | bytes 3145732
  69.4 7.3 %copy-start.6 = (bf16[1,256,1024]{2,1,0:T(8,128)(2,1)S(1)}, bf16[1,256,1024]{2,1,0:T(8,128)(2,1)}, u32[]{:S(2)}) copy-start(bf16[1,256,1024]{2,1,0:T(8,128)(2,1)} %param.12) | copy-start | bytes 1572868
  72.2 18.8 %collective-permute-start.7 = (bf16[832,128]{1,0:T(8,128)(2,1)S(1)}, bf16[832,128]{1,0:T(8,128)(2,1)S(1)}, u32[]{:S(2)}, u32[]{:S(2)}) collective-permute-start(bf16[832,128]{1,0:T(8,128)(2,1)S(1)} %get-tuple-element.57), channel_id=1, source_target_pairs={{0,2},{1,3},{2,0},{3,1},{4,6},{5,7},{6,4},{7,5},{8,10},{9,11},{10,... | collective-permute-start | bytes 638984 | tf_op jit(solution)/shard_map/ppermute | solution.py:46
  73.8 18.2 %collective-permute-start.8 = (bf16[832,128]{1,0:T(8,128)(2,1)S(1)}, bf16[832,128]{1,0:T(8,128)(2,1)S(1)}, u32[]{:S(2)}, u32[]{:S(2)}) collective-permute-start(bf16[832,128]{1,0:T(8,128)(2,1)S(1)} %get-tuple-element.58), channel_id=1, source_target_pairs={{0,4},{1,5},{2,6},{3,7},{4,0},{5,1},{6,2},{7,3},{8,12},{9,13},{10,... | collective-permute-start | bytes 638984 | tf_op jit(solution)/shard_map/ppermute | solution.py:46
  76.4 15.6 %collective-permute-start.9 = (bf16[832,128]{1,0:T(8,128)(2,1)S(1)}, bf16[832,128]{1,0:T(8,128)(2,1)S(1)}, u32[]{:S(2)}, u32[]{:S(2)}) collective-permute-start(bf16[832,128]{1,0:T(8,128)(2,1)S(1)} %get-tuple-element.59), channel_id=1, source_target_pairs={{0,6},{1,7},{2,4},{3,5},{4,2},{5,3},{6,0},{7,1},{8,14},{9,15},{10,... | collective-permute-start | bytes 638984 | tf_op jit(solution)/shard_map/ppermute | solution.py:46
  92.0 1.9 %collective-permute-start.10 = (bf16[4,512,128]{2,1,0:T(8,128)(2,1)S(1)}, bf16[4,512,128]{2,1,0:T(8,128)(2,1)S(1)}, u32[]{:S(2)}, u32[]{:S(2)}) collective-permute-start(bf16[4,512,128]{2,1,0:T(8,128)(2,1)S(1)} %get-tuple-element.68), channel_id=1, source_target_pairs={{0,1},{1,0},{2,3},{3,2},{4,5},{5,4},{6,7},{7,6},{8,9},{9,8},{10,11... | collective-permute-start | bytes 1572872 | tf_op jit(solution)/shard_map/ppermute | solution.py:46
  94.6 11.2 %collective-permute-start.11 = (bf16[512,128]{1,0:T(8,128)(2,1)S(1)}, bf16[512,128]{1,0:T(8,128)(2,1)S(1)}, u32[]{:S(2)}, u32[]{:S(2)}) collective-permute-start(bf16[512,128]{1,0:T(8,128)(2,1)S(1)} %get-tuple-element.70), channel_id=1, source_target_pairs={{0,2},{1,3},{2,0},{3,1},{4,6},{5,7},{6,4},{7,5},{8,10},{9,11},{10,... | collective-permute-start | bytes 393224 | tf_op jit(solution)/shard_map/ppermute | solution.py:46
  98.7 12.9 %collective-permute-start.12 = (bf16[512,128]{1,0:T(8,128)(2,1)S(1)}, bf16[512,128]{1,0:T(8,128)(2,1)S(1)}, u32[]{:S(2)}, u32[]{:S(2)}) collective-permute-start(bf16[512,128]{1,0:T(8,128)(2,1)S(1)} %get-tuple-element.71), channel_id=1, source_target_pairs={{0,4},{1,5},{2,6},{3,7},{4,0},{5,1},{6,2},{7,3},{8,12},{9,13},{10,... | collective-permute-start | bytes 393224 | tf_op jit(solution)/shard_map/ppermute | solution.py:46
  99.8 11.8 %collective-permute-start.13 = (bf16[512,128]{1,0:T(8,128)(2,1)S(1)}, bf16[512,128]{1,0:T(8,128)(2,1)S(1)}, u32[]{:S(2)}, u32[]{:S(2)}) collective-permute-start(bf16[512,128]{1,0:T(8,128)(2,1)S(1)} %get-tuple-element.72), channel_id=1, source_target_pairs={{0,6},{1,7},{2,4},{3,5},{4,2},{5,3},{6,0},{7,1},{8,14},{9,15},{10,... | collective-permute-start | bytes 393224 | tf_op jit(solution)/shard_map/ppermute | solution.py:46
  101.2 1.3 %collective-permute-start.14 = (bf16[4,64,128]{2,1,0:T(8,128)(2,1)S(1)}, bf16[4,64,128]{2,1,0:T(8,128)(2,1)S(1)}, u32[]{:S(2)}, u32[]{:S(2)}) collective-permute-start(bf16[4,64,128]{2,1,0:T(8,128)(2,1)S(1)} %get-tuple-element.76.mine_ref), channel_id=1, source_target_pairs={{0,1},{1,0},{2,3},{3,2},{4,5},{5,4},{6,7},{7,6},{8,9},{9,8},{10,11... | collective-permute-start | bytes 196616 | tf_op jit(solution)/shard_map/ppermute | solution.py:46

commit v11 on v10

--- a/solution.py
+++ b/solution.py
@@ -328,7 +328,7 @@
     *grad, keep, send = call(
         functools.partial(residual_kernel, groups, scale, len(feature), n_tiles, len(patch_args)),
         [*[shape((rows, TILE), BF16)] * n_tiles, shape(parts, BF16), shape(parts, BF16)],
-        limit=58,
+        limit=44,
         flops=4 * rows * width * n,
         moved=rows * (2 * width + 6 * n),
         grid_spec=pltpu.PrefetchScalarGridSpec(
@@ -613,7 +613,8 @@
 
 
 def exchange_chips(parts):
-    return [parts[0]] + [swap(part, "dp", 2 * k) for k, part in enumerate(parts) if k]
+    got = {k: swap(parts[k], "dp", 2 * k) for k in reversed(range(1, len(parts)))}
+    return [parts[0]] + [got[k] for k in range(1, len(parts))]
 
 
 def finish_kernel(inner, chips, *refs):
@@ -665,13 +666,14 @@
     hidden, feature, aux_pre, sent = forward(acts, first, second, aux, labels, groups)
     if paired:
         sent = after(sent, x[0])
-        diagonal = [swap(after(x[0], aux_pre), "section", 2), swap(after(y[0], aux_pre), "section", 1)]
+    got = exchange(sent)
+    if paired:
+        diagonal = [swap(after(x[0], got), "section", 2), swap(after(y[0], got), "section", 1)]
         x.append(swap(halves[1], "section", 1))
         y.insert(0, swap(halves[0], "section", 2))
         target = patch_operands([halves, x, y, diagonal], [0, 1, 2, 3], [0, 1, 2, 3])
     else:
         target = [target], [pl.BlockSpec((pix // STEPS, images, n_decode), lambda g, where: (g, 0, 0))]
-    got = exchange(sent)
     sent = class_logits(where, got, klass)
     partial = exchange(sent)
     grad, keep, send = residual(after(where, sent), feature, decode, *target, images, scale, groups)

time: 113 us -> 121 us (1.071)
  blocking collectives: 13.2 us -> 0 us
  waiting for transfers between devices: 19.6 us -> 30.7 us
  starting transfers between devices: 21.9 us -> 30.4 us
  local copies, waits for them, and re-layouts: 1.55 us -> 5.17 us
  Pallas kernels: 55.4 us -> 53.9 us
    all_to_all x1 -> x0, blocking collectives: 13.2 us -> none  [exchange(): lax.all_to_all(value, 'dp', 0, 0, axis_index_groups=groups, tiled=True)]
    ppermute x15, waiting for transfers between devices: 19.6 us -> 25.3 us  [swap(): return lax.ppermute(value, axis, [(i, i ^ bits) for i in range(count)])]
    all_to_all x1 -> x2, waiting for transfers between devices: 0.01 us -> 5.32 us  [exchange(): lax.all_to_all(value, 'dp', 0, 0, axis_index_groups=groups, tiled=True)]
    all_to_all x1 -> x2, starting transfers between devices: 3.6 us -> 8.72 us  [exchange(): lax.all_to_all(value, 'dp', 0, 0, axis_index_groups=groups, tiled=True)]
    unnamed x28 -> x26, local copies, waits for them, and re-layouts: 1.46 us -> 5.08 us
    ppermute x15, starting transfers between devices: 18.3 us -> 21.6 us  [swap(): return lax.ppermute(value, axis, [(i, i ^ bits) for i in range(count)])]
    pallas_call x1, Pallas kernels: 19 us -> 17.5 us  [residual(): call(functools.partial(residual_kernel, groups, scale, len(feature), n_ti...]
  transfers between devices with their start and end apart: 16 -> 17, of which waited for: 8 -> 10; matrix products, arithmetic and copies ran while one was open for 0% -> 0% of each run, Pallas kernels for 45% -> 41%
where the time goes in v11:
time: 121 us
  Pallas kernels  53.9 us (45%)
  waiting for transfers between devices  30.7 us (25%)
  starting transfers between devices  30.4 us (25%)
  local copies, waits for them, and re-layouts  5.17 us (4%)
    ppermute x15, waiting for transfers between devices, swap(): return lax.ppermute(value, axis, [(i, i ^ bits) for i in range(count)])  25.3 us
    ppermute x15, starting transfers between devices, swap(): return lax.ppermute(value, axis, [(i, i ^ bits) for i in range(count)])  21.6 us
    pallas_call x1, Pallas kernels, residual(): call(functools.partial(residual_kernel, groups, scale, len(feature), n_ti...  17.5 us
    pallas_call x1, Pallas kernels, backward(): call(functools.partial(backward_kernel, groups, len(grad), n_decode), [sh...  14.3 us
    pallas_call x1, Pallas kernels, forward(): call(functools.partial(forward_kernel, n_tiles, pix), [shape((pix * image...  9.74 us
    all_to_all x2, starting transfers between devices, exchange(): lax.all_to_all(value, 'dp', 0, 0, axis_index_groups=groups, tiled=True)  8.72 us
    all_to_all x2, waiting for transfers between devices, exchange(): lax.all_to_all(value, 'dp', 0, 0, axis_index_groups=groups, tiled=True)  5.32 us
    unnamed x26, local copies, waits for them, and re-layouts  5.08 us
  transfers between devices with their start and end apart: 17, of which 10 were waited for; matrix products, arithmetic and copies ran while one was open for 0% of the time, Pallas kernels for 41%

profile of v11, /device:TPU:0, one launch (start us, length us, event | category | flops | bytes accessed | tf_op | source)
XLA Modules:
  0.0 120.9 jit_solution(18197735089235860236)
XLA Ops:
  0.7 0.1 stack.47.where_ref
  0.7 1.4 %copy-done = bf16[16,196,192]{1,2,0:T(8,128)(2,1)S(1)} copy-done((bf16[16,196,192]{1,2,0:T(8,128)(2,1)S(1)}, bf16[16,196,192]{1,2,0:T(8,128)(2,1)}, u32[]{:S(2)}) %copy-start) | copy-done | bytes 1204248
  2.2 1.8 %pack_patches.3.refs_7_.refs_15_ = bf16[147,16,128]{2,1,0:T(8,128)(2,1)S(1)} custom-call(s32[11]{0:T(128)S(1)} %stack.47.where_ref, bf16[16,192,196]{2,1,0:T(8,128)(2,1)S(1)} %bitcast.27, bf16[16,192,196]{2,1,0:T(8,128)(2,1)S(1)} %bitcast.28, bf16[16,192,196]{2,1,0:T(8,128)(2,1)S(1)} %bitcast.29, bf16[16,192,196]{2,1,0:T(8,128)(2,1)S(1)} %bitcast.30), custom_call_target="tpu_custom_call" | custom-call | tf_op jit(solution)/shard_map/pack_patches/pallas_call | solution.py:99
  4.0 3.0 %collective-permute-start = (bf16[147,16,128]{2,1,0:T(8,128)(2,1)S(1)}, bf16[147,16,128]{2,1,0:T(8,128)(2,1)}, u32[]{:S(2)}, u32[]{:S(2)}) collective-permute-start(bf16[147,16,128]{2,1,0:T(8,128)(2,1)S(1)} %pack_patches.3.refs_7_.refs_15_), channel_id=1, source_target_pairs={{0,8},{8,0},{16,24},{24,16},{1,9},{9,1},{17,25},{25,17},{2,10},{10... | collective-permute-start | bytes 1806344 | tf_op jit(solution)/shard_map/ppermute | solution.py:46
  7.0 1.8 %pack_patches.2.refs_8_.refs_16_ = bf16[147,16,128]{2,1,0:T(8,128)(2,1)S(1)} custom-call(s32[11]{0:T(128)S(1)} %stack.47.where_ref, bf16[16,192,196]{2,1,0:T(8,128)(2,1)S(1)} %bitcast.31, bf16[16,192,196]{2,1,0:T(8,128)(2,1)S(1)} %bitcast.32, bf16[16,192,196]{2,1,0:T(8,128)(2,1)S(1)} %bitcast.33, bf16[16,192,196]{2,1,0:T(8,128)(2,1)S(1)} %bitcast.34), custom_call_target="tpu_custom_call" | custom-call | tf_op jit(solution)/shard_map/pack_patches/pallas_call | solution.py:99
  8.8 1.6 %collective-permute-start.3 = (bf16[147,16,128]{2,1,0:T(8,128)(2,1)S(1)}, bf16[147,16,128]{2,1,0:T(8,128)(2,1)}, u32[]{:S(2)}, u32[]{:S(2)}) collective-permute-start(bf16[147,16,128]{2,1,0:T(8,128)(2,1)S(1)} %pack_patches.2.refs_8_.refs_16_), channel_id=1, source_target_pairs={{0,16},{8,24},{16,0},{24,8},{1,17},{9,25},{17,1},{25,9},{2,18},{10... | collective-permute-start | bytes 1806344 | tf_op jit(solution)/shard_map/ppermute | solution.py:46
  10.4 9.7 %forward.1 = (bf16[3136,256]{1,0:T(8,128)(2,1)}, bf16[3136,256]{1,0:T(8,128)(2,1)}, bf16[3136,256]{1,0:T(8,128)(2,1)}, bf16[3136,256]{1,0:T(8,128)(2,1)}, bf16[3...) custom-call(bf16[196,16,1024]{2,1,0:T(8,128)(2,1)} %bitcast.48, ...), custom_call_target="tpu_custom_call" | custom-call | tf_op jit(solution)/shard_map/forward/pallas_call | solution.py:171
  20.2 0.5 collective-permute-done.refs_9_.refs_17_
  20.7 5.1 %all-to-all-start = ((bf16[8,16,768]{2,1,0:T(8,128)(2,1)}), bf16[8,16,768]{2,1,0:T(8,128)(2,1)S(1)}, u32[]{:S(2)}, u32[]{:S(2)}) async-start(bf16[8,16,768]{2,1,0:T(8,128)(2,1)} %get-tuple-element.44), calls=%async_computation | async-start | bytes 393216 | tf_op jit(solution)/shard_map/all_to_all | solution.py:50
  25.8 1.5 %collective-permute-start.2 = (bf16[147,16,128]{2,1,0:T(8,128)(2,1)S(1)}, bf16[147,16,128]{2,1,0:T(8,128)(2,1)}, u32[]{:S(2)}, u32[]{:S(2)}) collective-permute-start(bf16[147,16,128]{2,1,0:T(8,128)(2,1)S(1)} %pack_patches.3.refs_7_.refs_15_), channel_id=1, source_target_pairs={{0,16},{8,24},{16,0},{24,8},{1,17},{9,25},{17,1},{25,9},{2,18},{10... | collective-permute-start | bytes 1806344 | tf_op jit(solution)/shard_map/ppermute | solution.py:46
  27.3 1.5 %collective-permute-start.1 = (bf16[147,16,128]{2,1,0:T(8,128)(2,1)S(1)}, bf16[147,16,128]{2,1,0:T(8,128)(2,1)}, u32[]{:S(2)}, u32[]{:S(2)}) collective-permute-start(bf16[147,16,128]{2,1,0:T(8,128)(2,1)S(1)} %pack_patches.2.refs_8_.refs_16_), channel_id=1, source_target_pairs={{0,8},{8,0},{16,24},{24,16},{1,9},{9,1},{17,25},{25,17},{2,10},{10... | collective-permute-start | bytes 1806344 | tf_op jit(solution)/shard_map/ppermute | solution.py:46
  28.8 0.0 collective-permute-done.3.refs_12_.refs_20_
  28.8 5.3 %all-to-all-done.got_ref = bf16[8,16,768]{2,1,0:T(8,128)(2,1)S(1)} async-done(((bf16[8,16,768]{2,1,0:T(8,128)(2,1)}), bf16[8,16,768]{2,1,0:T(8,128)(2,1)S(1)}, u32[]{:S(2)}, u32[]{:S(2)}) %all-to-all-start) | async-done | bytes 196640 | tf_op jit(solution)/shard_map/all_to_all | solution.py:50
  34.1 1.5 %collective-permute-start.4 = (bf16[147,16,128]{2,1,0:T(8,128)(2,1)}, bf16[147,16,128]{2,1,0:T(8,128)(2,1)}, u32[]{:S(2)}, u32[]{:S(2)}) collective-permute-start(bf16[147,16,128]{2,1,0:T(8,128)(2,1)} %collective-permute-done.refs_9_.refs_17_), channel_id=1, source_target_pairs={{0,16},{8,24},{16,0},{24,8},{1,17},{9,25},{17,1},{25,9},{2,18},{10... | collective-permute-start | bytes 1806344 | tf_op jit(solution)/shard_map/ppermute | solution.py:46
  35.7 1.5 %collective-permute-start.5 = (bf16[147,16,128]{2,1,0:T(8,128)(2,1)}, bf16[147,16,128]{2,1,0:T(8,128)(2,1)}, u32[]{:S(2)}, u32[]{:S(2)}) collective-permute-start(bf16[147,16,128]{2,1,0:T(8,128)(2,1)} %collective-permute-done.3.refs_12_.refs_20_), channel_id=1, source_target_pairs={{0,8},{8,0},{16,24},{24,16},{1,9},{9,1},{17,25},{25,17},{2,10},{10... | collective-permute-start | bytes 1806344 | tf_op jit(solution)/shard_map/ppermute | solution.py:46
  37.2 2.7 %class_logits.1 = bf16[8,16,1152]{2,1,0:T(8,128)(2,1)} custom-call(s32[11]{0:T(128)S(1)} %stack.47.where_ref, bf16[8,16,768]{2,1,0:T(8,128)(2,1)S(1)} %all-to-all-done.got_ref, bf16[1408,512]{1,0:T(8,128)(2,1)S(1)} %bitcast.35), custom_call_target="tpu_custom_call" | custom-call | tf_op jit(solution)/shard_map/class_logits/pallas_call | solution.py:495
  39.8 3.6 %all-to-all-start.1 = ((bf16[8,16,1152]{2,1,0:T(8,128)(2,1)}), bf16[8,16,1152]{2,1,0:T(8,128)(2,1)S(1)}, u32[]{:S(2)}, u32[]{:S(2)}) async-start(bf16[8,16,1152]{2,1,0:T(8,128)(2,1)} %class_logits.1), calls=%async_computation.1 | async-start | bytes 589824 | tf_op jit(solution)/shard_map/all_to_all | solution.py:50
  43.4 0.0 collective-permute-done.2.refs_11_.refs_19_
  43.5 0.4 collective-permute-done.1.refs_10_.refs_18_
  43.9 11.0 %collective-permute-done.4.refs_13_.refs_21_ = bf16[147,16,128]{2,1,0:T(8,128)(2,1)} collective-permute-done((bf16[147,16,128]{2,1,0:T(8,128)(2,1)}, bf16[147,16,128]{2,1,0:T(8,128)(2,1)}, u32[]{:S(2)}, u32[]{:S(2)}) %collective-permute-start.4) | collective-permute-done | bytes 602144 | tf_op jit(solution)/shard_map/ppermute | solution.py:46
  54.8 1.2 %collective-permute-done.5.refs_14_.refs_22_ = bf16[147,16,128]{2,1,0:T(8,128)(2,1)} collective-permute-done((bf16[147,16,128]{2,1,0:T(8,128)(2,1)}, bf16[147,16,128]{2,1,0:T(8,128)(2,1)}, u32[]{:S(2)}, u32[]{:S(2)}) %collective-permute-start.5) | collective-permute-done | bytes 602144 | tf_op jit(solution)/shard_map/ppermute | solution.py:46
  56.1 1.1 copy-done.4
  57.1 1.4 %copy-done.6 = bf16[1,1024,768]{2,1,0:T(8,128)(2,1)S(1)} copy-done((bf16[1,1024,768]{2,1,0:T(8,128)(2,1)S(1)}, bf16[1,1024,768]{2,1,0:T(8,128)(2,1)}, u32[]{:S(2)}) %copy-start.6) | copy-done | bytes 1572888
  58.5 17.5 %residual.1 = (bf16[3136,256]{1,0:T(8,128)(2,1)S(1)}, bf16[3136,256]{1,0:T(8,128)(2,1)}, bf16[3136,256]{1,0:T(8,128)(2,1)}, bf16[4,768,128]{2,1,0:T(8,128)(2,1)S(1)}, bf16[4,768,128]{2,1,0:T(8,128)(2,1)}) custom-call(s32[11]{0:T(128)S(1)} %stack.47.where_ref, bf16[3136,256]{1,0:T(8,128)(2,1)} %get-tuple-element.46.refs_0_, ...), custom_call_target="tpu_custom_call" | custom-call | flops 9865003008 | bytes 20873216 | tf_op jit(solution)/shard_map/residual/pallas_call | solution.py:328
  76.1 1.2 copy-done.9
  77.2 0.0 collective-permute-start.6
  77.2 0.0 all-to-all-done.1.got_ref.stats_ref
  77.2 0.0 copy-start.7
  77.3 0.3 aux_backward.1
  77.6 0.0 copy-start.5
  77.6 2.1 %collective-permute-done.6.got_ref = bf16[4,768,128]{2,1,0:T(8,128)(2,1)S(1)} collective-permute-done((bf16[4,768,128]{2,1,0:T(8,128)(2,1)}, bf16[4,768,128]{2,1,0:T(8,128)(2,1)S(1)}, u32[]{:S(2)}, u32[]{:S(2)}) %collective-permute-start.6) | collective-permute-done | bytes 786464 | tf_op jit(solution)/shard_map/ppermute | solution.py:46
  79.7 0.7 add_cores.2
  80.4 1.7 %collective-permute-start.7 = (bf16[832,128]{1,0:T(8,128)(2,1)S(1)}, bf16[832,128]{1,0:T(8,128)(2,1)S(1)}, u32[]{:S(2)}, u32[]{:S(2)}) collective-permute-start(bf16[832,128]{1,0:T(8,128)(2,1)S(1)} %get-tuple-element.57), channel_id=1, source_target_pairs={{0,2},{1,3},{2,0},{3,1},{4,6},{5,7},{6,4},{7,5},{8,10},{9,11},{10,... | collective-permute-start | bytes 638984 | tf_op jit(solution)/shard_map/ppermute | solution.py:46
  82.2 2.4 %collective-permute-start.8 = (bf16[832,128]{1,0:T(8,128)(2,1)S(1)}, bf16[832,128]{1,0:T(8,128)(2,1)S(1)}, u32[]{:S(2)}, u32[]{:S(2)}) collective-permute-start(bf16[832,128]{1,0:T(8,128)(2,1)S(1)} %get-tuple-element.58), channel_id=1, source_target_pairs={{0,4},{1,5},{2,6},{3,7},{4,0},{5,1},{6,2},{7,3},{8,12},{9,13},{10,... | collective-permute-start | bytes 638984 | tf_op jit(solution)/shard_map/ppermute | solution.py:46
  84.5 0.4 collective-permute-start.9
  84.9 14.3 %backward.1 = (bf16[4,512,128]{2,1,0:T(8,128)(2,1)S(1)}, bf16[4,512,128]{2,1,0:T(8,128)(2,1)S(1)}) custom-call(s32[11]{0:T(128)S(1)} %stack.47.where_ref, bf16[3136,256]{1,0:T(8,128)(2,1)S(1)} %copy-done.10, bf16[3136,256]{1,0:T(8,128)(2,1)S(1)} %copy-done.11, bf16[3136,256]{1,0:T(8,128)(2,1)S(1)} %copy-done.12, bf16[1024,768]{1,0:T(8,128)(2,1)S(1)} %bitcast.44, ...), custom_call_target="tpu_custom_call" | custom-call | flops 9865003008 | bytes 12845056 | tf_op jit(solution)/shard_map/backward/pallas_call | solution.py:407
  99.3 0.0 collective-permute-done.7.refs_1_
  99.3 1.1 collective-permute-done.8.refs_2_
  100.3 0.0 collective-permute-done.9.refs_3_
  100.3 1.9 %collective-permute-done.10.got_ref = bf16[4,512,128]{2,1,0:T(8,128)(2,1)S(1)} collective-permute-done((bf16[4,512,128]{2,1,0:T(8,128)(2,1)S(1)}, bf16[4,512,128]{2,1,0:T(8,128)(2,1)S(1)}, u32[]{:S(2)}, u32[]{:S(2)}) %collective-permute-start.10) | collective-permute-done | bytes 524320 | tf_op jit(solution)/shard_map/ppermute | solution.py:46
  102.3 0.7 add_cores.3
  102.9 4.1 %collective-permute-start.11 = (bf16[512,128]{1,0:T(8,128)(2,1)S(1)}, bf16[512,128]{1,0:T(8,128)(2,1)S(1)}, u32[]{:S(2)}, u32[]{:S(2)}) collective-permute-start(bf16[512,128]{1,0:T(8,128)(2,1)S(1)} %get-tuple-element.70), channel_id=1, source_target_pairs={{0,2},{1,3},{2,0},{3,1},{4,6},{5,7},{6,4},{7,5},{8,10},{9,11},{10,... | collective-permute-start | bytes 393224 | tf_op jit(solution)/shard_map/ppermute | solution.py:46
  107.0 1.0 collective-permute-start.12
  108.0 1.5 %collective-permute-start.13 = (bf16[512,128]{1,0:T(8,128)(2,1)S(1)}, bf16[512,128]{1,0:T(8,128)(2,1)S(1)}, u32[]{:S(2)}, u32[]{:S(2)}) collective-permute-start(bf16[512,128]{1,0:T(8,128)(2,1)S(1)} %get-tuple-element.72), channel_id=1, source_target_pairs={{0,6},{1,7},{2,4},{3,5},{4,2},{5,3},{6,0},{7,1},{8,14},{9,15},{10,... | collective-permute-start | bytes 393224 | tf_op jit(solution)/shard_map/ppermute | solution.py:46
  109.5 1.3 %collective-permute-done.14.other_ref = bf16[4,64,128]{2,1,0:T(8,128)(2,1)S(1)} collective-permute-done((bf16[4,64,128]{2,1,0:T(8,128)(2,1)S(1)}, bf16[4,64,128]{2,1,0:T(8,128)(2,1)S(1)}, u32[]{:S(2)}, u32[]{:S(2)}) %collective-permute-start.14) | collective-permute-done | bytes 65568 | tf_op jit(solution)/shard_map/ppermute | solution.py:46
  110.7 3.3 %class_backward.1 = (f32[1408,512]{1,0:T(8,128)}, f32[128,512]{1,0:T(8,128)}) custom-call(s32[11]{0:T(128)S(1)} %stack.47.where_ref, bf16[1408,512]{1,0:T(8,128)(2,1)S(1)} %bitcast.36, bf16[8,16,768]{2,1,0:T(8,128)(2,1)S(1)} %all-to-all-done.got_ref, bf16[8,16,1152]{2,1,0:T(8,128)(2,1)S(1)} %all-to-all-done.1.got_ref.stats_ref, ...), custom_call_target="tpu_custom_call" | custom-call | flops 184549376 | bytes 2883584 | tf_op jit(solution)/shard_map/class_backward/pallas_call | solution.py:565
  114.0 5.9 %collective-permute-done.12.refs_6_ = bf16[512,128]{1,0:T(8,128)(2,1)S(1)} collective-permute-done((bf16[512,128]{1,0:T(8,128)(2,1)S(1)}, bf16[512,128]{1,0:T(8,128)(2,1)S(1)}, u32[]{:S(2)}, u32[]{:S(2)}) %collective-permute-start.12) | collective-permute-done | bytes 131104 | tf_op jit(solution)/shard_map/ppermute | solution.py:46
  119.9 1.0 finish.1
  (24 shorter events, 0.0 us)
Async XLA Ops:
  0.7 1.4 %copy-start = (bf16[16,196,192]{1,2,0:T(8,128)(2,1)S(1)}, bf16[16,196,192]{1,2,0:T(8,128)(2,1)}, u32[]{:S(2)}) copy-start(bf16[16,196,192]{1,2,0:T(8,128)(2,1)} %param.9) | copy-start | bytes 3612676
  4.0 16.7 %collective-permute-start = (bf16[147,16,128]{2,1,0:T(8,128)(2,1)S(1)}, bf16[147,16,128]{2,1,0:T(8,128)(2,1)}, u32[]{:S(2)}, u32[]{:S(2)}) collective-permute-start(bf16[147,16,128]{2,1,0:T(8,128)(2,1)S(1)} %pack_patches.3.refs_7_.refs_15_), channel_id=1, source_target_pairs={{0,8},{8,0},{16,24},{24,16},{1,9},{9,1},{17,25},{25,17},{2,10},{10... | collective-permute-start | bytes 1806344 | tf_op jit(solution)/shard_map/ppermute | solution.py:46
  8.8 18.5 %copy-start.3 = (bf16[147,16,128]{2,1,0:T(8,128)(2,1)}, bf16[147,16,128]{2,1,0:T(8,128)(2,1)S(1)}, u32[]{:S(2)}) copy-start(bf16[147,16,128]{2,1,0:T(8,128)(2,1)S(1)} %pack_patches.2.refs_8_.refs_16_) | copy-start | bytes 1806340
  8.8 20.0 %collective-permute-start.3 = (bf16[147,16,128]{2,1,0:T(8,128)(2,1)S(1)}, bf16[147,16,128]{2,1,0:T(8,128)(2,1)}, u32[]{:S(2)}, u32[]{:S(2)}) collective-permute-start(bf16[147,16,128]{2,1,0:T(8,128)(2,1)S(1)} %pack_patches.2.refs_8_.refs_16_), channel_id=1, source_target_pairs={{0,16},{8,24},{16,0},{24,8},{1,17},{9,25},{17,1},{25,9},{2,18},{10... | collective-permute-start | bytes 1806344 | tf_op jit(solution)/shard_map/ppermute | solution.py:46
  10.4 26.8 %copy-start.1 = (bf16[1,1408,512]{2,1,0:T(8,128)(2,1)S(1)}, bf16[1,1408,512]{2,1,0:T(8,128)(2,1)}, u32[]{:S(2)}) copy-start(bf16[1,1408,512]{2,1,0:T(8,128)(2,1)} %param.15) | copy-start | bytes 4325380
  20.7 13.5 %all-to-all-start = ((bf16[8,16,768]{2,1,0:T(8,128)(2,1)}), bf16[8,16,768]{2,1,0:T(8,128)(2,1)S(1)}, u32[]{:S(2)}, u32[]{:S(2)}) async-start(bf16[8,16,768]{2,1,0:T(8,128)(2,1)} %get-tuple-element.44), calls=%async_computation | async-start | bytes 393216 | tf_op jit(solution)/shard_map/all_to_all | solution.py:50
  25.8 17.6 %collective-permute-start.2 = (bf16[147,16,128]{2,1,0:T(8,128)(2,1)S(1)}, bf16[147,16,128]{2,1,0:T(8,128)(2,1)}, u32[]{:S(2)}, u32[]{:S(2)}) collective-permute-start(bf16[147,16,128]{2,1,0:T(8,128)(2,1)S(1)} %pack_patches.3.refs_7_.refs_15_), channel_id=1, source_target_pairs={{0,16},{8,24},{16,0},{24,8},{1,17},{9,25},{17,1},{25,9},{2,18},{10... | collective-permute-start | bytes 1806344 | tf_op jit(solution)/shard_map/ppermute | solution.py:46
  27.3 16.5 %collective-permute-start.1 = (bf16[147,16,128]{2,1,0:T(8,128)(2,1)S(1)}, bf16[147,16,128]{2,1,0:T(8,128)(2,1)}, u32[]{:S(2)}, u32[]{:S(2)}) collective-permute-start(bf16[147,16,128]{2,1,0:T(8,128)(2,1)S(1)} %pack_patches.2.refs_8_.refs_16_), channel_id=1, source_target_pairs={{0,8},{8,0},{16,24},{24,16},{1,9},{9,1},{17,25},{25,17},{2,10},{10... | collective-permute-start | bytes 1806344 | tf_op jit(solution)/shard_map/ppermute | solution.py:46
  34.1 20.7 %collective-permute-start.4 = (bf16[147,16,128]{2,1,0:T(8,128)(2,1)}, bf16[147,16,128]{2,1,0:T(8,128)(2,1)}, u32[]{:S(2)}, u32[]{:S(2)}) collective-permute-start(bf16[147,16,128]{2,1,0:T(8,128)(2,1)} %collective-permute-done.refs_9_.refs_17_), channel_id=1, source_target_pairs={{0,16},{8,24},{16,0},{24,8},{1,17},{9,25},{17,1},{25,9},{2,18},{10... | collective-permute-start | bytes 1806344 | tf_op jit(solution)/shard_map/ppermute | solution.py:46
  35.7 20.4 %collective-permute-start.5 = (bf16[147,16,128]{2,1,0:T(8,128)(2,1)}, bf16[147,16,128]{2,1,0:T(8,128)(2,1)}, u32[]{:S(2)}, u32[]{:S(2)}) collective-permute-start(bf16[147,16,128]{2,1,0:T(8,128)(2,1)} %collective-permute-done.3.refs_12_.refs_20_), channel_id=1, source_target_pairs={{0,8},{8,0},{16,24},{24,16},{1,9},{9,1},{17,25},{25,17},{2,10},{10... | collective-permute-start | bytes 1806344 | tf_op jit(solution)/shard_map/ppermute | solution.py:46
  39.8 37.4 %all-to-all-start.1 = ((bf16[8,16,1152]{2,1,0:T(8,128)(2,1)}), bf16[8,16,1152]{2,1,0:T(8,128)(2,1)S(1)}, u32[]{:S(2)}, u32[]{:S(2)}) async-start(bf16[8,16,1152]{2,1,0:T(8,128)(2,1)} %class_logits.1), calls=%async_computation.1 | async-start | bytes 589824 | tf_op jit(solution)/shard_map/all_to_all | solution.py:50
  56.1 1.1 copy-start.4
  57.1 1.4 %copy-start.6 = (bf16[1,1024,768]{2,1,0:T(8,128)(2,1)S(1)}, bf16[1,1024,768]{2,1,0:T(8,128)(2,1)}, u32[]{:S(2)}) copy-start(bf16[1,1024,768]{2,1,0:T(8,128)(2,1)} %param.13) | copy-start | bytes 4718596
  58.5 18.7 %copy-start.8 = (f32[16,512]{1,0:T(8,128)S(1)}, f32[16,512]{1,0:T(8,128)}, u32[]{:S(2)}) copy-start(f32[16,512]{1,0:T(8,128)} %get-tuple-element.54.aux_pre_ref) | copy-start | bytes 98308
  76.1 1.2 copy-start.9
  77.2 2.5 %collective-permute-start.6 = (bf16[4,768,128]{2,1,0:T(8,128)(2,1)}, bf16[4,768,128]{2,1,0:T(8,128)(2,1)S(1)}, u32[]{:S(2)}, u32[]{:S(2)}) collective-permute-start(bf16[4,768,128]{2,1,0:T(8,128)(2,1)} %get-tuple-element.53), channel_id=1, source_target_pairs={{0,1},{1,0},{2,3},{3,2},{4,5},{5,4},{6,7},{7,6},{8,9},{9,8},{10,11... | collective-permute-start | bytes 2359304 | tf_op jit(solution)/shard_map/ppermute | solution.py:46
  77.2 7.7 %copy-start.7 = (bf16[1,1024,768]{2,1,0:T(8,128)(2,1)S(1)}, bf16[1,1024,768]{2,1,0:T(8,128)(2,1)}, u32[]{:S(2)}) copy-start(bf16[1,1024,768]{2,1,0:T(8,128)(2,1)} %param.13) | copy-start | bytes 4718596
  77.2 7.7 %copy-start.10 = (bf16[3136,256]{1,0:T(8,128)(2,1)S(1)}, bf16[3136,256]{1,0:T(8,128)(2,1)}, u32[]{:S(2)}) copy-start(bf16[3136,256]{1,0:T(8,128)(2,1)} %copy-done.9) | copy-start | bytes 4816900
  77.3 7.7 %copy-start.11 = (bf16[3136,256]{1,0:T(8,128)(2,1)S(1)}, bf16[3136,256]{1,0:T(8,128)(2,1)}, u32[]{:S(2)}) copy-start(bf16[3136,256]{1,0:T(8,128)(2,1)} %get-tuple-element.61.refs_1_) | copy-start | bytes 4816900
  77.3 7.6 %copy-start.12 = (bf16[3136,256]{1,0:T(8,128)(2,1)S(1)}, bf16[3136,256]{1,0:T(8,128)(2,1)}, u32[]{:S(2)}) copy-start(bf16[3136,256]{1,0:T(8,128)(2,1)} %get-tuple-element.62.refs_2_) | copy-start | bytes 4816900
  77.6 7.3 %copy-start.2 = (bf16[1,1024,512]{2,1,0:T(8,128)(2,1)S(1)}, bf16[1,1024,512]{2,1,0:T(8,128)(2,1)}, u32[]{:S(2)}) copy-start(bf16[1,1024,512]{2,1,0:T(8,128)(2,1)} %param.14) | copy-start | bytes 3145732
  77.6 7.3 %copy-start.5 = (bf16[1,256,1024]{2,1,0:T(8,128)(2,1)S(1)}, bf16[1,256,1024]{2,1,0:T(8,128)(2,1)}, u32[]{:S(2)}) copy-start(bf16[1,256,1024]{2,1,0:T(8,128)(2,1)} %param.12) | copy-start | bytes 1572868
  80.4 18.8 %collective-permute-start.7 = (bf16[832,128]{1,0:T(8,128)(2,1)S(1)}, bf16[832,128]{1,0:T(8,128)(2,1)S(1)}, u32[]{:S(2)}, u32[]{:S(2)}) collective-permute-start(bf16[832,128]{1,0:T(8,128)(2,1)S(1)} %get-tuple-element.57), channel_id=1, source_target_pairs={{0,2},{1,3},{2,0},{3,1},{4,6},{5,7},{6,4},{7,5},{8,10},{9,11},{10,... | collective-permute-start | bytes 638984 | tf_op jit(solution)/shard_map/ppermute | solution.py:46
  82.2 18.2 %collective-permute-start.8 = (bf16[832,128]{1,0:T(8,128)(2,1)S(1)}, bf16[832,128]{1,0:T(8,128)(2,1)S(1)}, u32[]{:S(2)}, u32[]{:S(2)}) collective-permute-start(bf16[832,128]{1,0:T(8,128)(2,1)S(1)} %get-tuple-element.58), channel_id=1, source_target_pairs={{0,4},{1,5},{2,6},{3,7},{4,0},{5,1},{6,2},{7,3},{8,12},{9,13},{10,... | collective-permute-start | bytes 638984 | tf_op jit(solution)/shard_map/ppermute | solution.py:46
  84.5 15.8 %collective-permute-start.9 = (bf16[832,128]{1,0:T(8,128)(2,1)S(1)}, bf16[832,128]{1,0:T(8,128)(2,1)S(1)}, u32[]{:S(2)}, u32[]{:S(2)}) collective-permute-start(bf16[832,128]{1,0:T(8,128)(2,1)S(1)} %get-tuple-element.59), channel_id=1, source_target_pairs={{0,6},{1,7},{2,4},{3,5},{4,2},{5,3},{6,0},{7,1},{8,14},{9,15},{10,... | collective-permute-start | bytes 638984 | tf_op jit(solution)/shard_map/ppermute | solution.py:46
  100.3 1.9 %collective-permute-start.10 = (bf16[4,512,128]{2,1,0:T(8,128)(2,1)S(1)}, bf16[4,512,128]{2,1,0:T(8,128)(2,1)S(1)}, u32[]{:S(2)}, u32[]{:S(2)}) collective-permute-start(bf16[4,512,128]{2,1,0:T(8,128)(2,1)S(1)} %get-tuple-element.68), channel_id=1, source_target_pairs={{0,1},{1,0},{2,3},{3,2},{4,5},{5,4},{6,7},{7,6},{8,9},{9,8},{10,11... | collective-permute-start | bytes 1572872 | tf_op jit(solution)/shard_map/ppermute | solution.py:46
  102.9 11.1 %collective-permute-start.11 = (bf16[512,128]{1,0:T(8,128)(2,1)S(1)}, bf16[512,128]{1,0:T(8,128)(2,1)S(1)}, u32[]{:S(2)}, u32[]{:S(2)}) collective-permute-start(bf16[512,128]{1,0:T(8,128)(2,1)S(1)} %get-tuple-element.70), channel_id=1, source_target_pairs={{0,2},{1,3},{2,0},{3,1},{4,6},{5,7},{6,4},{7,5},{8,10},{9,11},{10,... | collective-permute-start | bytes 393224 | tf_op jit(solution)/shard_map/ppermute | solution.py:46
  107.0 12.9 %collective-permute-start.12 = (bf16[512,128]{1,0:T(8,128)(2,1)S(1)}, bf16[512,128]{1,0:T(8,128)(2,1)S(1)}, u32[]{:S(2)}, u32[]{:S(2)}) collective-permute-start(bf16[512,128]{1,0:T(8,128)(2,1)S(1)} %get-tuple-element.71), channel_id=1, source_target_pairs={{0,4},{1,5},{2,6},{3,7},{4,0},{5,1},{6,2},{7,3},{8,12},{9,13},{10,... | collective-permute-start | bytes 393224 | tf_op jit(solution)/shard_map/ppermute | solution.py:46
  108.0 11.9 %collective-permute-start.13 = (bf16[512,128]{1,0:T(8,128)(2,1)S(1)}, bf16[512,128]{1,0:T(8,128)(2,1)S(1)}, u32[]{:S(2)}, u32[]{:S(2)}) collective-permute-start(bf16[512,128]{1,0:T(8,128)(2,1)S(1)} %get-tuple-element.72), channel_id=1, source_target_pairs={{0,6},{1,7},{2,4},{3,5},{4,2},{5,3},{6,0},{7,1},{8,14},{9,15},{10,... | collective-permute-start | bytes 393224 | tf_op jit(solution)/shard_map/ppermute | solution.py:46
  109.5 1.3 %collective-permute-start.14 = (bf16[4,64,128]{2,1,0:T(8,128)(2,1)S(1)}, bf16[4,64,128]{2,1,0:T(8,128)(2,1)S(1)}, u32[]{:S(2)}, u32[]{:S(2)}) collective-permute-start(bf16[4,64,128]{2,1,0:T(8,128)(2,1)S(1)} %get-tuple-element.76.mine_ref), channel_id=1, source_target_pairs={{0,1},{1,0},{2,3},{3,2},{4,5},{5,4},{6,7},{7,6},{8,9},{9,8},{10,11... | collective-permute-start | bytes 196616 | tf_op jit(solution)/shard_map/ppermute | solution.py:46

commit v12 on v11

--- a/solution.py
+++ b/solution.py
@@ -281,11 +281,11 @@
 
 
 def contract(g, rows, pairs):
-    unit = rows // STEPS // TILE * TILE
-    span = slice(g * unit, rows if g == STEPS - 1 else (g + 1) * unit)
+    middle = rows // STEPS * 2 // TILE * TILE
+    span = slice(0, middle) if g == 2 else slice(middle, rows)
     for total, left, right in pairs:
         now = dot(left[span], right[span], ROWS_0)
-        total[...] = now if g == 0 else total[...] + now
+        total[...] = now if g == 2 else total[...] + now
 
 
 def residual_kernel(groups, scale, n_feature, n_tiles, n_patch, where_ref, *refs):
@@ -300,8 +300,8 @@
     def body(g):
         here = slice(g * size, (g + 1) * size)
         lay_target(g, where_ref, patch_refs, target)
-        if g:
-            contract(g - 1, rows, [(total, grads, feature)])
+        if g == 2:
+            contract(g, rows, [(total, grads, feature)])
         now = feature[here]
         for j, grad_ref in enumerate(grad_refs):
             cut = slice(j * TILE, (j + 1) * TILE)
@@ -328,7 +328,7 @@
     *grad, keep, send = call(
         functools.partial(residual_kernel, groups, scale, len(feature), n_tiles, len(patch_args)),
         [*[shape((rows, TILE), BF16)] * n_tiles, shape(parts, BF16), shape(parts, BF16)],
-        limit=44,
+        limit=58,
         flops=4 * rows * width * n,
         moved=rows * (2 * width + 6 * n),
         grid_spec=pltpu.PrefetchScalarGridSpec(
@@ -365,9 +365,9 @@
 
     def body(g):
         here = slice(g * size, (g + 1) * size)
-        if g:
-            contract(g - 1, rows, pairs)
-        else:
+        if g == 2:
+            contract(g, rows, pairs)
+        if g == 0:
             pooled[...] = dot(aux_grad_ref[...], aux_ref[...], COLS_1) / (rows // images)
         grad = jnp.concatenate([ref[...] for ref in grad_refs], axis=1)
         for j, decode_ref in enumerate(decode_refs):
@@ -668,9 +668,10 @@
         sent = after(sent, x[0])
     got = exchange(sent)
     if paired:
-        diagonal = [swap(after(x[0], got), "section", 2), swap(after(y[0], got), "section", 1)]
         x.append(swap(halves[1], "section", 1))
         y.insert(0, swap(halves[0], "section", 2))
+        ready = (got, x[1], y[0])
+        diagonal = [swap(after(x[0], ready), "section", 2), swap(after(y[1], ready), "section", 1)]
         target = patch_operands([halves, x, y, diagonal], [0, 1, 2, 3], [0, 1, 2, 3])
     else:
         target = [target], [pl.BlockSpec((pix // STEPS, images, n_decode), lambda g, where: (g, 0, 0))]

time: 121 us -> 114 us (0.942)
  local copies, waits for them, and re-layouts: 5.17 us -> 1.56 us
  waiting for transfers between devices: 30.7 us -> 27.2 us
  starting transfers between devices: 30.4 us -> 28.6 us
    all_to_all x2, waiting for transfers between devices: 5.32 us -> 0.15 us  [exchange(): lax.all_to_all(value, 'dp', 0, 0, axis_index_groups=groups, tiled=True)]
    unnamed x26 -> x32, local copies, waits for them, and re-layouts: 5.08 us -> 1.47 us
    ppermute x15, starting transfers between devices: 21.6 us -> 19.3 us  [swap(): return lax.ppermute(value, axis, [(i, i ^ bits) for i in range(count)])]
    ppermute x15, waiting for transfers between devices: 25.3 us -> 27 us  [swap(): return lax.ppermute(value, axis, [(i, i ^ bits) for i in range(count)])]
    pallas_call x1, Pallas kernels: 17.5 us -> 18.8 us  [residual(): call(functools.partial(residual_kernel, groups, scale, len(feature), n_ti...]
  transfers between devices with their start and end apart: 17 -> 17, of which waited for: 10 -> 10; matrix products, arithmetic and copies ran while one was open for 0% -> 0% of each run, Pallas kernels for 41% -> 45%
where the time goes in v12:
time: 114 us; the launch traced here: 113 us
  Pallas kernels  55.1 us (48%)
  starting transfers between devices  28.6 us (25%)
  waiting for transfers between devices  27.2 us (24%)
  local copies, waits for them, and re-layouts  1.56 us (1%)
    ppermute x15, waiting for transfers between devices, swap(): return lax.ppermute(value, axis, [(i, i ^ bits) for i in range(count)])  27 us
    ppermute x15, starting transfers between devices, swap(): return lax.ppermute(value, axis, [(i, i ^ bits) for i in range(count)])  19.3 us
    pallas_call x1, Pallas kernels, residual(): call(functools.partial(residual_kernel, groups, scale, len(feature), n_ti...  18.8 us
    pallas_call x1, Pallas kernels, backward(): call(functools.partial(backward_kernel, groups, len(grad), n_decode), [sh...  14.2 us
    pallas_call x1, Pallas kernels, forward(): call(functools.partial(forward_kernel, n_tiles, pix), [shape((pix * image...  9.73 us
    all_to_all x2, starting transfers between devices, exchange(): lax.all_to_all(value, 'dp', 0, 0, axis_index_groups=groups, tiled=True)  9.22 us
    pallas_call x2, Pallas kernels, pack(): call(functools.partial(pack_kernel, h * half), shape(dims, BF16), limit=2...  3.64 us
    pallas_call x1, Pallas kernels, class_backward(): call(functools.partial(class_kernel, norm), [shape((classes, head), F32),...  3.31 us
  transfers between devices with their start and end apart: 17, of which 10 were waited for; matrix products, arithmetic and copies ran while one was open for 0% of the time, Pallas kernels for 45%

profile of v12, /device:TPU:0, one launch (start us, length us, event | category | flops | bytes accessed | tf_op | source)
XLA Modules:
  0.0 113.3 jit_solution(12689649697819844669)
XLA Ops:
  0.7 0.1 stack.47.where_ref
  0.7 0.0 copy-start
  0.8 1.4 %copy-done = bf16[16,196,192]{1,2,0:T(8,128)(2,1)S(1)} copy-done((bf16[16,196,192]{1,2,0:T(8,128)(2,1)S(1)}, bf16[16,196,192]{1,2,0:T(8,128)(2,1)}, u32[]{:S(2)}) %copy-start) | copy-done | bytes 1204248
  2.2 1.8 %pack_patches.3.refs_7_.refs_15_ = bf16[147,16,128]{2,1,0:T(8,128)(2,1)S(1)} custom-call(s32[11]{0:T(128)S(1)} %stack.47.where_ref, bf16[16,192,196]{2,1,0:T(8,128)(2,1)S(1)} %bitcast.27, bf16[16,192,196]{2,1,0:T(8,128)(2,1)S(1)} %bitcast.28, bf16[16,192,196]{2,1,0:T(8,128)(2,1)S(1)} %bitcast.29, bf16[16,192,196]{2,1,0:T(8,128)(2,1)S(1)} %bitcast.30), custom_call_target="tpu_custom_call" | custom-call | tf_op jit(solution)/shard_map/pack_patches/pallas_call | solution.py:99
  4.0 3.0 %collective-permute-start = (bf16[147,16,128]{2,1,0:T(8,128)(2,1)S(1)}, bf16[147,16,128]{2,1,0:T(8,128)(2,1)S(1)}, u32[]{:S(2)}, u32[]{:S(2)}) collective-permute-start(bf16[147,16,128]{2,1,0:T(8,128)(2,1)S(1)} %pack_patches.3.refs_7_.refs_15_), channel_id=1, source_target_pairs={{0,8},{8,0},{16,24},{24,16},{1,9},{9,1},{17,25},{25,17},{2,10},{10... | collective-permute-start | bytes 1806344 | tf_op jit(solution)/shard_map/ppermute | solution.py:46
  7.0 1.5 %collective-permute-start.2 = (bf16[147,16,128]{2,1,0:T(8,128)(2,1)S(1)}, bf16[147,16,128]{2,1,0:T(8,128)(2,1)}, u32[]{:S(2)}, u32[]{:S(2)}) collective-permute-start(bf16[147,16,128]{2,1,0:T(8,128)(2,1)S(1)} %pack_patches.3.refs_7_.refs_15_), channel_id=1, source_target_pairs={{0,16},{8,24},{16,0},{24,8},{1,17},{9,25},{17,1},{25,9},{2,18},{10... | collective-permute-start | bytes 1806344 | tf_op jit(solution)/shard_map/ppermute | solution.py:46
  8.5 1.8 %pack_patches.2.refs_8_.refs_16_ = bf16[147,16,128]{2,1,0:T(8,128)(2,1)S(1)} custom-call(s32[11]{0:T(128)S(1)} %stack.47.where_ref, bf16[16,192,196]{2,1,0:T(8,128)(2,1)S(1)} %bitcast.31, bf16[16,192,196]{2,1,0:T(8,128)(2,1)S(1)} %bitcast.32, bf16[16,192,196]{2,1,0:T(8,128)(2,1)S(1)} %bitcast.33, bf16[16,192,196]{2,1,0:T(8,128)(2,1)S(1)} %bitcast.34), custom_call_target="tpu_custom_call" | custom-call | tf_op jit(solution)/shard_map/pack_patches/pallas_call | solution.py:99
  10.4 0.6 collective-permute-start.3
  10.9 0.1 collective-permute-start.1
  11.1 9.7 %forward.1 = (bf16[3136,256]{1,0:T(8,128)(2,1)}, bf16[3136,256]{1,0:T(8,128)(2,1)}, bf16[3136,256]{1,0:T(8,128)(2,1)}, bf16[3136,256]{1,0:T(8,128)(2,1)}, bf16[3...) custom-call(bf16[196,16,1024]{2,1,0:T(8,128)(2,1)} %bitcast.48, ...), custom_call_target="tpu_custom_call" | custom-call | tf_op jit(solution)/shard_map/forward/pallas_call | solution.py:171
  20.8 0.6 collective-permute-done.refs_9_.refs_17_
  21.4 5.4 %all-to-all-start = ((bf16[8,16,768]{2,1,0:T(8,128)(2,1)}), bf16[8,16,768]{2,1,0:T(8,128)(2,1)S(1)}, u32[]{:S(2)}, u32[]{:S(2)}) async-start(bf16[8,16,768]{2,1,0:T(8,128)(2,1)} %get-tuple-element.44), calls=%async_computation | async-start | bytes 393216 | tf_op jit(solution)/shard_map/all_to_all | solution.py:50
  26.9 8.2 %collective-permute-done.3.refs_12_.refs_20_ = bf16[147,16,128]{2,1,0:T(8,128)(2,1)} collective-permute-done((bf16[147,16,128]{2,1,0:T(8,128)(2,1)S(1)}, bf16[147,16,128]{2,1,0:T(8,128)(2,1)}, u32[]{:S(2)}, u32[]{:S(2)}) %collective-permute-start.3) | collective-permute-done | bytes 602144 | tf_op jit(solution)/shard_map/ppermute | solution.py:46
  35.1 0.0 collective-permute-done.1.refs_10_.refs_18_
  35.1 0.1 all-to-all-done.got_ref
  35.2 1.5 %collective-permute-start.4 = (bf16[147,16,128]{2,1,0:T(8,128)(2,1)S(1)}, bf16[147,16,128]{2,1,0:T(8,128)(2,1)S(1)}, u32[]{:S(2)}, u32[]{:S(2)}) collective-permute-start(bf16[147,16,128]{2,1,0:T(8,128)(2,1)S(1)} %collective-permute-done.refs_9_.refs_17_), channel_id=1, source_target_pairs={{0,16},{8,24},{16,0},{24,8},{1,17},{9,25},{17,1},{25,9},{2,18},{10... | collective-permute-start | bytes 1806344 | tf_op jit(solution)/shard_map/ppermute | solution.py:46
  36.7 1.5 %collective-permute-start.5 = (bf16[147,16,128]{2,1,0:T(8,128)(2,1)}, bf16[147,16,128]{2,1,0:T(8,128)(2,1)}, u32[]{:S(2)}, u32[]{:S(2)}) collective-permute-start(bf16[147,16,128]{2,1,0:T(8,128)(2,1)} %collective-permute-done.3.refs_12_.refs_20_), channel_id=1, source_target_pairs={{0,8},{8,0},{16,24},{24,16},{1,9},{9,1},{17,25},{25,17},{2,10},{10... | collective-permute-start | bytes 1806344 | tf_op jit(solution)/shard_map/ppermute | solution.py:46
  38.2 2.7 %class_logits.1 = bf16[8,16,1152]{2,1,0:T(8,128)(2,1)} custom-call(s32[11]{0:T(128)S(1)} %stack.47.where_ref, bf16[8,16,768]{2,1,0:T(8,128)(2,1)S(1)} %all-to-all-done.got_ref, bf16[1408,512]{1,0:T(8,128)(2,1)S(1)} %bitcast.35), custom_call_target="tpu_custom_call" | custom-call | tf_op jit(solution)/shard_map/class_logits/pallas_call | solution.py:495
  40.9 3.8 %all-to-all-start.1 = ((bf16[8,16,1152]{2,1,0:T(8,128)(2,1)}), bf16[8,16,1152]{2,1,0:T(8,128)(2,1)S(1)}, u32[]{:S(2)}, u32[]{:S(2)}) async-start(bf16[8,16,1152]{2,1,0:T(8,128)(2,1)} %class_logits.1), calls=%async_computation.1 | async-start | bytes 589824 | tf_op jit(solution)/shard_map/all_to_all | solution.py:50
  44.7 4.6 %collective-permute-done.4.refs_13_.refs_21_ = bf16[147,16,128]{2,1,0:T(8,128)(2,1)S(1)} collective-permute-done((bf16[147,16,128]{2,1,0:T(8,128)(2,1)S(1)}, bf16[147,16,128]{2,1,0:T(8,128)(2,1)S(1)}, u32[]{:S(2)}, u32[]{:S(2)}) %collective-permute-start.4) | collective-permute-done | bytes 602144 | tf_op jit(solution)/shard_map/ppermute | solution.py:46
  49.3 1.6 %collective-permute-done.5.refs_14_.refs_22_ = bf16[147,16,128]{2,1,0:T(8,128)(2,1)} collective-permute-done((bf16[147,16,128]{2,1,0:T(8,128)(2,1)}, bf16[147,16,128]{2,1,0:T(8,128)(2,1)}, u32[]{:S(2)}, u32[]{:S(2)}) %collective-permute-start.5) | collective-permute-done | bytes 602144 | tf_op jit(solution)/shard_map/ppermute | solution.py:46
  50.9 18.8 %residual.1 = (bf16[3136,256]{1,0:T(8,128)(2,1)}, bf16[3136,256]{1,0:T(8,128)(2,1)}, bf16[3136,256]{1,0:T(8,128)(2,1)}, bf16[4,768,128]{2,1,0:T(8,128)(2,1)}, bf16[4,768,128]{2,1,0:T(8,128)(2,1)}) custom-call(s32[11]{0:T(128)} %copy-done.7, bf16[3136,256]{1,0:T(8,128)(2,1)} %get-tuple-element.46.refs_0_, bf16[3136,256]{1,0:T(8,128)(2,1)} %get-tuple-element.47.refs_1_, ...), custom_call_target="tpu_custom_call" | custom-call | flops 9865003008 | bytes 20873216 | tf_op jit(solution)/shard_map/residual/pallas_call | solution.py:328
  69.7 0.1 collective-permute-start.6
  69.8 0.0 copy-start.8
  69.9 0.0 copy-start.9
  69.9 0.3 aux_backward.1
  70.2 0.0 copy-start.6
  70.2 2.1 %collective-permute-done.6.got_ref = bf16[4,768,128]{2,1,0:T(8,128)(2,1)S(1)} collective-permute-done((bf16[4,768,128]{2,1,0:T(8,128)(2,1)}, bf16[4,768,128]{2,1,0:T(8,128)(2,1)S(1)}, u32[]{:S(2)}, u32[]{:S(2)}) %collective-permute-start.6) | collective-permute-done | bytes 786464 | tf_op jit(solution)/shard_map/ppermute | solution.py:46
  72.3 0.7 add_cores.2
  73.0 1.5 %collective-permute-start.7 = (bf16[832,128]{1,0:T(8,128)(2,1)S(1)}, bf16[832,128]{1,0:T(8,128)(2,1)S(1)}, u32[]{:S(2)}, u32[]{:S(2)}) collective-permute-start(bf16[832,128]{1,0:T(8,128)(2,1)S(1)} %get-tuple-element.57), channel_id=1, source_target_pairs={{0,2},{1,3},{2,0},{3,1},{4,6},{5,7},{6,4},{7,5},{8,10},{9,11},{10,... | collective-permute-start | bytes 638984 | tf_op jit(solution)/shard_map/ppermute | solution.py:46
  74.6 2.6 %collective-permute-start.8 = (bf16[832,128]{1,0:T(8,128)(2,1)S(1)}, bf16[832,128]{1,0:T(8,128)(2,1)S(1)}, u32[]{:S(2)}, u32[]{:S(2)}) collective-permute-start(bf16[832,128]{1,0:T(8,128)(2,1)S(1)} %get-tuple-element.58), channel_id=1, source_target_pairs={{0,4},{1,5},{2,6},{3,7},{4,0},{5,1},{6,2},{7,3},{8,12},{9,13},{10,... | collective-permute-start | bytes 638984 | tf_op jit(solution)/shard_map/ppermute | solution.py:46
  77.1 0.3 collective-permute-start.9
  77.5 14.2 %backward.1 = (bf16[4,512,128]{2,1,0:T(8,128)(2,1)S(1)}, bf16[4,512,128]{2,1,0:T(8,128)(2,1)S(1)}) custom-call(s32[11]{0:T(128)S(1)} %copy-done.8, bf16[3136,256]{1,0:T(8,128)(2,1)S(1)} %copy-done.11, bf16[3136,256]{1,0:T(8,128)(2,1)S(1)} %copy-done.12, bf16[3136,256]{1,0:T(8,128)(2,1)S(1)} %copy-done.13, bf16[1024,768]{1,0:T(8,128)(2,1)S(1)} %bitcast.44, ...), custom_call_target="tpu_custom_call" | custom-call | flops 9865003008 | bytes 12845056 | tf_op jit(solution)/shard_map/backward/pallas_call | solution.py:407
  91.8 0.0 collective-permute-done.7.refs_1_
  91.8 0.9 collective-permute-done.8.refs_2_
  92.7 0.0 collective-permute-done.9.refs_3_
  92.7 0.0 collective-permute-start.10
  92.7 1.9 %collective-permute-done.10.got_ref = bf16[4,512,128]{2,1,0:T(8,128)(2,1)S(1)} collective-permute-done((bf16[4,512,128]{2,1,0:T(8,128)(2,1)S(1)}, bf16[4,512,128]{2,1,0:T(8,128)(2,1)S(1)}, u32[]{:S(2)}, u32[]{:S(2)}) %collective-permute-start.10) | collective-permute-done | bytes 524320 | tf_op jit(solution)/shard_map/ppermute | solution.py:46
  94.6 0.7 add_cores.3
  95.3 4.1 %collective-permute-start.11 = (bf16[512,128]{1,0:T(8,128)(2,1)S(1)}, bf16[512,128]{1,0:T(8,128)(2,1)S(1)}, u32[]{:S(2)}, u32[]{:S(2)}) collective-permute-start(bf16[512,128]{1,0:T(8,128)(2,1)S(1)} %get-tuple-element.70), channel_id=1, source_target_pairs={{0,2},{1,3},{2,0},{3,1},{4,6},{5,7},{6,4},{7,5},{8,10},{9,11},{10,... | collective-permute-start | bytes 393224 | tf_op jit(solution)/shard_map/ppermute | solution.py:46
  99.4 1.1 collective-permute-start.12
  100.5 1.4 %collective-permute-start.13 = (bf16[512,128]{1,0:T(8,128)(2,1)S(1)}, bf16[512,128]{1,0:T(8,128)(2,1)S(1)}, u32[]{:S(2)}, u32[]{:S(2)}) collective-permute-start(bf16[512,128]{1,0:T(8,128)(2,1)S(1)} %get-tuple-element.72), channel_id=1, source_target_pairs={{0,6},{1,7},{2,4},{3,5},{4,2},{5,3},{6,0},{7,1},{8,14},{9,15},{10,... | collective-permute-start | bytes 393224 | tf_op jit(solution)/shard_map/ppermute | solution.py:46
  101.9 0.0 collective-permute-start.14
  101.9 1.3 %collective-permute-done.14.other_ref = bf16[4,64,128]{2,1,0:T(8,128)(2,1)S(1)} collective-permute-done((bf16[4,64,128]{2,1,0:T(8,128)(2,1)S(1)}, bf16[4,64,128]{2,1,0:T(8,128)(2,1)S(1)}, u32[]{:S(2)}, u32[]{:S(2)}) %collective-permute-start.14) | collective-permute-done | bytes 65568 | tf_op jit(solution)/shard_map/ppermute | solution.py:46
  103.2 3.3 %class_backward.1 = (f32[1408,512]{1,0:T(8,128)}, f32[128,512]{1,0:T(8,128)}) custom-call(s32[11]{0:T(128)S(1)} %copy-done.8, bf16[1408,512]{1,0:T(8,128)(2,1)S(1)} %bitcast.36, bf16[8,16,768]{2,1,0:T(8,128)(2,1)S(1)} %all-to-all-done.got_ref, bf16[8,16,1152]{2,1,0:T(8,128)(2,1)S(1)} %all-to-all-done.1.got_ref.stats_ref, ...), custom_call_target="tpu_custom_call" | custom-call | flops 184549376 | bytes 2883584 | tf_op jit(solution)/shard_map/class_backward/pallas_call | solution.py:565
  106.5 5.9 %collective-permute-done.12.refs_6_ = bf16[512,128]{1,0:T(8,128)(2,1)S(1)} collective-permute-done((bf16[512,128]{1,0:T(8,128)(2,1)S(1)}, bf16[512,128]{1,0:T(8,128)(2,1)S(1)}, u32[]{:S(2)}, u32[]{:S(2)}) %collective-permute-start.12) | collective-permute-done | bytes 131104 | tf_op jit(solution)/shard_map/ppermute | solution.py:46
  112.3 0.0 collective-permute-done.13.refs_7_
  112.3 1.0 finish.1
  (30 shorter events, 0.1 us)
Async XLA Ops:
  0.7 37.5 %copy-start.7 = (s32[11]{0:T(128)}, s32[11]{0:T(128)S(1)}, u32[]{:S(2)}) copy-start(s32[11]{0:T(128)S(1)} %stack.47.where_ref) | copy-start | bytes 136
  0.7 1.4 %copy-start = (bf16[16,196,192]{1,2,0:T(8,128)(2,1)S(1)}, bf16[16,196,192]{1,2,0:T(8,128)(2,1)}, u32[]{:S(2)}) copy-start(bf16[16,196,192]{1,2,0:T(8,128)(2,1)} %param.9) | copy-start | bytes 3612676
  4.0 6.4 %copy-start.4 = (bf16[147,16,128]{2,1,0:T(8,128)(2,1)}, bf16[147,16,128]{2,1,0:T(8,128)(2,1)S(1)}, u32[]{:S(2)}) copy-start(bf16[147,16,128]{2,1,0:T(8,128)(2,1)S(1)} %pack_patches.3.refs_7_.refs_15_) | copy-start | bytes 1806340
  4.0 17.4 %collective-permute-start = (bf16[147,16,128]{2,1,0:T(8,128)(2,1)S(1)}, bf16[147,16,128]{2,1,0:T(8,128)(2,1)S(1)}, u32[]{:S(2)}, u32[]{:S(2)}) collective-permute-start(bf16[147,16,128]{2,1,0:T(8,128)(2,1)S(1)} %pack_patches.3.refs_7_.refs_15_), channel_id=1, source_target_pairs={{0,8},{8,0},{16,24},{24,16},{1,9},{9,1},{17,25},{25,17},{2,10},{10... | collective-permute-start | bytes 1806344 | tf_op jit(solution)/shard_map/ppermute | solution.py:46
  7.0 19.9 %collective-permute-start.2 = (bf16[147,16,128]{2,1,0:T(8,128)(2,1)S(1)}, bf16[147,16,128]{2,1,0:T(8,128)(2,1)}, u32[]{:S(2)}, u32[]{:S(2)}) collective-permute-start(bf16[147,16,128]{2,1,0:T(8,128)(2,1)S(1)} %pack_patches.3.refs_7_.refs_15_), channel_id=1, source_target_pairs={{0,16},{8,24},{16,0},{24,8},{1,17},{9,25},{17,1},{25,9},{2,18},{10... | collective-permute-start | bytes 1806344 | tf_op jit(solution)/shard_map/ppermute | solution.py:46
  10.4 10.4 %copy-start.5 = (bf16[147,16,128]{2,1,0:T(8,128)(2,1)}, bf16[147,16,128]{2,1,0:T(8,128)(2,1)S(1)}, u32[]{:S(2)}) copy-start(bf16[147,16,128]{2,1,0:T(8,128)(2,1)S(1)} %pack_patches.2.refs_8_.refs_16_) | copy-start | bytes 1806340
  10.4 24.7 %collective-permute-start.3 = (bf16[147,16,128]{2,1,0:T(8,128)(2,1)S(1)}, bf16[147,16,128]{2,1,0:T(8,128)(2,1)}, u32[]{:S(2)}, u32[]{:S(2)}) collective-permute-start(bf16[147,16,128]{2,1,0:T(8,128)(2,1)S(1)} %pack_patches.2.refs_8_.refs_16_), channel_id=1, source_target_pairs={{0,16},{8,24},{16,0},{24,8},{1,17},{9,25},{17,1},{25,9},{2,18},{10... | collective-permute-start | bytes 1806344 | tf_op jit(solution)/shard_map/ppermute | solution.py:46
  10.9 24.1 %collective-permute-start.1 = (bf16[147,16,128]{2,1,0:T(8,128)(2,1)S(1)}, bf16[147,16,128]{2,1,0:T(8,128)(2,1)}, u32[]{:S(2)}, u32[]{:S(2)}) collective-permute-start(bf16[147,16,128]{2,1,0:T(8,128)(2,1)S(1)} %pack_patches.2.refs_8_.refs_16_), channel_id=1, source_target_pairs={{0,8},{8,0},{16,24},{24,16},{1,9},{9,1},{17,25},{25,17},{2,10},{10... | collective-permute-start | bytes 1806344 | tf_op jit(solution)/shard_map/ppermute | solution.py:46
  11.1 27.2 %copy-start.1 = (bf16[1,1408,512]{2,1,0:T(8,128)(2,1)S(1)}, bf16[1,1408,512]{2,1,0:T(8,128)(2,1)}, u32[]{:S(2)}) copy-start(bf16[1,1408,512]{2,1,0:T(8,128)(2,1)} %param.15) | copy-start | bytes 4325380
  21.4 29.5 %copy-start.14 = (bf16[147,16,128]{2,1,0:T(8,128)(2,1)}, bf16[147,16,128]{2,1,0:T(8,128)(2,1)S(1)}, u32[]{:S(2)}) copy-start(bf16[147,16,128]{2,1,0:T(8,128)(2,1)S(1)} %collective-permute-done.refs_9_.refs_17_) | copy-start | bytes 1806340
  21.4 13.8 %all-to-all-start = ((bf16[8,16,768]{2,1,0:T(8,128)(2,1)}), bf16[8,16,768]{2,1,0:T(8,128)(2,1)S(1)}, u32[]{:S(2)}, u32[]{:S(2)}) async-start(bf16[8,16,768]{2,1,0:T(8,128)(2,1)} %get-tuple-element.44), calls=%async_computation | async-start | bytes 393216 | tf_op jit(solution)/shard_map/all_to_all | solution.py:50
  35.2 14.1 %collective-permute-start.4 = (bf16[147,16,128]{2,1,0:T(8,128)(2,1)S(1)}, bf16[147,16,128]{2,1,0:T(8,128)(2,1)S(1)}, u32[]{:S(2)}, u32[]{:S(2)}) collective-permute-start(bf16[147,16,128]{2,1,0:T(8,128)(2,1)S(1)} %collective-permute-done.refs_9_.refs_17_), channel_id=1, source_target_pairs={{0,16},{8,24},{16,0},{24,8},{1,17},{9,25},{17,1},{25,9},{2,18},{10... | collective-permute-start | bytes 1806344 | tf_op jit(solution)/shard_map/ppermute | solution.py:46
  36.7 14.2 %collective-permute-start.5 = (bf16[147,16,128]{2,1,0:T(8,128)(2,1)}, bf16[147,16,128]{2,1,0:T(8,128)(2,1)}, u32[]{:S(2)}, u32[]{:S(2)}) collective-permute-start(bf16[147,16,128]{2,1,0:T(8,128)(2,1)} %collective-permute-done.3.refs_12_.refs_20_), channel_id=1, source_target_pairs={{0,8},{8,0},{16,24},{24,16},{1,9},{9,1},{17,25},{25,17},{2,10},{10... | collective-permute-start | bytes 1806344 | tf_op jit(solution)/shard_map/ppermute | solution.py:46
  40.9 28.9 %all-to-all-start.1 = ((bf16[8,16,1152]{2,1,0:T(8,128)(2,1)}), bf16[8,16,1152]{2,1,0:T(8,128)(2,1)S(1)}, u32[]{:S(2)}, u32[]{:S(2)}) async-start(bf16[8,16,1152]{2,1,0:T(8,128)(2,1)} %class_logits.1), calls=%async_computation.1 | async-start | bytes 589824 | tf_op jit(solution)/shard_map/all_to_all | solution.py:50
  49.3 1.6 %copy-start.15 = (bf16[147,16,128]{2,1,0:T(8,128)(2,1)}, bf16[147,16,128]{2,1,0:T(8,128)(2,1)S(1)}, u32[]{:S(2)}) copy-start(bf16[147,16,128]{2,1,0:T(8,128)(2,1)S(1)} %collective-permute-done.4.refs_13_.refs_21_) | copy-start | bytes 1806340
  50.9 18.9 %copy-start.10 = (f32[16,512]{1,0:T(8,128)S(1)}, f32[16,512]{1,0:T(8,128)}, u32[]{:S(2)}) copy-start(f32[16,512]{1,0:T(8,128)} %get-tuple-element.54.aux_pre_ref) | copy-start | bytes 98308
  69.7 2.6 %collective-permute-start.6 = (bf16[4,768,128]{2,1,0:T(8,128)(2,1)}, bf16[4,768,128]{2,1,0:T(8,128)(2,1)S(1)}, u32[]{:S(2)}, u32[]{:S(2)}) collective-permute-start(bf16[4,768,128]{2,1,0:T(8,128)(2,1)} %get-tuple-element.53), channel_id=1, source_target_pairs={{0,1},{1,0},{2,3},{3,2},{4,5},{5,4},{6,7},{7,6},{8,9},{9,8},{10,11... | collective-permute-start | bytes 2359304 | tf_op jit(solution)/shard_map/ppermute | solution.py:46
  69.8 2.5 %copy-start.3 = (bf16[4,768,128]{2,1,0:T(8,128)(2,1)S(1)}, bf16[4,768,128]{2,1,0:T(8,128)(2,1)}, u32[]{:S(2)}) copy-start(bf16[4,768,128]{2,1,0:T(8,128)(2,1)} %get-tuple-element.52.keep_ref) | copy-start | bytes 2359300
  69.8 2.5 %copy-start.8 = (s32[11]{0:T(128)S(1)}, s32[11]{0:T(128)}, u32[]{:S(2)}) copy-start(s32[11]{0:T(128)} %copy-done.7) | copy-start | bytes 136
  69.9 7.6 %copy-start.9 = (bf16[1,1024,768]{2,1,0:T(8,128)(2,1)S(1)}, bf16[1,1024,768]{2,1,0:T(8,128)(2,1)}, u32[]{:S(2)}) copy-start(bf16[1,1024,768]{2,1,0:T(8,128)(2,1)} %param.13) | copy-start | bytes 4718596
  69.9 7.6 %copy-start.11 = (bf16[3136,256]{1,0:T(8,128)(2,1)S(1)}, bf16[3136,256]{1,0:T(8,128)(2,1)}, u32[]{:S(2)}) copy-start(bf16[3136,256]{1,0:T(8,128)(2,1)} %get-tuple-element.60.refs_0_) | copy-start | bytes 4816900
  69.9 7.6 %copy-start.12 = (bf16[3136,256]{1,0:T(8,128)(2,1)S(1)}, bf16[3136,256]{1,0:T(8,128)(2,1)}, u32[]{:S(2)}) copy-start(bf16[3136,256]{1,0:T(8,128)(2,1)} %get-tuple-element.61.refs_1_) | copy-start | bytes 4816900
  69.9 7.6 %copy-start.13 = (bf16[3136,256]{1,0:T(8,128)(2,1)S(1)}, bf16[3136,256]{1,0:T(8,128)(2,1)}, u32[]{:S(2)}) copy-start(bf16[3136,256]{1,0:T(8,128)(2,1)} %get-tuple-element.62.refs_2_) | copy-start | bytes 4816900
  70.2 7.3 %copy-start.2 = (bf16[1,1024,512]{2,1,0:T(8,128)(2,1)S(1)}, bf16[1,1024,512]{2,1,0:T(8,128)(2,1)}, u32[]{:S(2)}) copy-start(bf16[1,1024,512]{2,1,0:T(8,128)(2,1)} %param.14) | copy-start | bytes 3145732
  70.2 7.3 %copy-start.6 = (bf16[1,256,1024]{2,1,0:T(8,128)(2,1)S(1)}, bf16[1,256,1024]{2,1,0:T(8,128)(2,1)}, u32[]{:S(2)}) copy-start(bf16[1,256,1024]{2,1,0:T(8,128)(2,1)} %param.12) | copy-start | bytes 1572868
  73.0 18.7 %collective-permute-start.7 = (bf16[832,128]{1,0:T(8,128)(2,1)S(1)}, bf16[832,128]{1,0:T(8,128)(2,1)S(1)}, u32[]{:S(2)}, u32[]{:S(2)}) collective-permute-start(bf16[832,128]{1,0:T(8,128)(2,1)S(1)} %get-tuple-element.57), channel_id=1, source_target_pairs={{0,2},{1,3},{2,0},{3,1},{4,6},{5,7},{6,4},{7,5},{8,10},{9,11},{10,... | collective-permute-start | bytes 638984 | tf_op jit(solution)/shard_map/ppermute | solution.py:46
  74.6 18.2 %collective-permute-start.8 = (bf16[832,128]{1,0:T(8,128)(2,1)S(1)}, bf16[832,128]{1,0:T(8,128)(2,1)S(1)}, u32[]{:S(2)}, u32[]{:S(2)}) collective-permute-start(bf16[832,128]{1,0:T(8,128)(2,1)S(1)} %get-tuple-element.58), channel_id=1, source_target_pairs={{0,4},{1,5},{2,6},{3,7},{4,0},{5,1},{6,2},{7,3},{8,12},{9,13},{10,... | collective-permute-start | bytes 638984 | tf_op jit(solution)/shard_map/ppermute | solution.py:46
  77.1 15.6 %collective-permute-start.9 = (bf16[832,128]{1,0:T(8,128)(2,1)S(1)}, bf16[832,128]{1,0:T(8,128)(2,1)S(1)}, u32[]{:S(2)}, u32[]{:S(2)}) collective-permute-start(bf16[832,128]{1,0:T(8,128)(2,1)S(1)} %get-tuple-element.59), channel_id=1, source_target_pairs={{0,6},{1,7},{2,4},{3,5},{4,2},{5,3},{6,0},{7,1},{8,14},{9,15},{10,... | collective-permute-start | bytes 638984 | tf_op jit(solution)/shard_map/ppermute | solution.py:46
  92.7 1.9 %collective-permute-start.10 = (bf16[4,512,128]{2,1,0:T(8,128)(2,1)S(1)}, bf16[4,512,128]{2,1,0:T(8,128)(2,1)S(1)}, u32[]{:S(2)}, u32[]{:S(2)}) collective-permute-start(bf16[4,512,128]{2,1,0:T(8,128)(2,1)S(1)} %get-tuple-element.68), channel_id=1, source_target_pairs={{0,1},{1,0},{2,3},{3,2},{4,5},{5,4},{6,7},{7,6},{8,9},{9,8},{10,11... | collective-permute-start | bytes 1572872 | tf_op jit(solution)/shard_map/ppermute | solution.py:46
  95.3 11.2 %collective-permute-start.11 = (bf16[512,128]{1,0:T(8,128)(2,1)S(1)}, bf16[512,128]{1,0:T(8,128)(2,1)S(1)}, u32[]{:S(2)}, u32[]{:S(2)}) collective-permute-start(bf16[512,128]{1,0:T(8,128)(2,1)S(1)} %get-tuple-element.70), channel_id=1, source_target_pairs={{0,2},{1,3},{2,0},{3,1},{4,6},{5,7},{6,4},{7,5},{8,10},{9,11},{10,... | collective-permute-start | bytes 393224 | tf_op jit(solution)/shard_map/ppermute | solution.py:46
  99.4 12.9 %collective-permute-start.12 = (bf16[512,128]{1,0:T(8,128)(2,1)S(1)}, bf16[512,128]{1,0:T(8,128)(2,1)S(1)}, u32[]{:S(2)}, u32[]{:S(2)}) collective-permute-start(bf16[512,128]{1,0:T(8,128)(2,1)S(1)} %get-tuple-element.71), channel_id=1, source_target_pairs={{0,4},{1,5},{2,6},{3,7},{4,0},{5,1},{6,2},{7,3},{8,12},{9,13},{10,... | collective-permute-start | bytes 393224 | tf_op jit(solution)/shard_map/ppermute | solution.py:46
  100.5 11.8 %collective-permute-start.13 = (bf16[512,128]{1,0:T(8,128)(2,1)S(1)}, bf16[512,128]{1,0:T(8,128)(2,1)S(1)}, u32[]{:S(2)}, u32[]{:S(2)}) collective-permute-start(bf16[512,128]{1,0:T(8,128)(2,1)S(1)} %get-tuple-element.72), channel_id=1, source_target_pairs={{0,6},{1,7},{2,4},{3,5},{4,2},{5,3},{6,0},{7,1},{8,14},{9,15},{10,... | collective-permute-start | bytes 393224 | tf_op jit(solution)/shard_map/ppermute | solution.py:46
  101.9 1.3 %collective-permute-start.14 = (bf16[4,64,128]{2,1,0:T(8,128)(2,1)S(1)}, bf16[4,64,128]{2,1,0:T(8,128)(2,1)S(1)}, u32[]{:S(2)}, u32[]{:S(2)}) collective-permute-start(bf16[4,64,128]{2,1,0:T(8,128)(2,1)S(1)} %get-tuple-element.76.mine_ref), channel_id=1, source_target_pairs={{0,1},{1,0},{2,3},{3,2},{4,5},{5,4},{6,7},{7,6},{8,9},{9,8},{10,11... | collective-permute-start | bytes 196616 | tf_op jit(solution)/shard_map/ppermute | solution.py:46

commit v13 on v12

--- a/solution.py
+++ b/solution.py
@@ -176,7 +176,7 @@
             shape((images, head), F32),
             shape((groups, images, head + 2 * LANES), BF16),
         ],
-        limit=58,
+        limit=53,
         grid=(STEPS,),
         in_specs=[
             *[column(j) for j in range(n_tiles)],
@@ -328,7 +328,7 @@
     *grad, keep, send = call(
         functools.partial(residual_kernel, groups, scale, len(feature), n_tiles, len(patch_args)),
         [*[shape((rows, TILE), BF16)] * n_tiles, shape(parts, BF16), shape(parts, BF16)],
-        limit=58,
+        limit=42,
         flops=4 * rows * width * n,
         moved=rows * (2 * width + 6 * n),
         grid_spec=pltpu.PrefetchScalarGridSpec(
@@ -670,8 +670,7 @@
     if paired:
         x.append(swap(halves[1], "section", 1))
         y.insert(0, swap(halves[0], "section", 2))
-        ready = (got, x[1], y[0])
-        diagonal = [swap(after(x[0], ready), "section", 2), swap(after(y[1], ready), "section", 1)]
+        diagonal = [swap(after(x[0], aux_pre), "section", 2), swap(after(y[1], aux_pre), "section", 1)]
         target = patch_operands([halves, x, y, diagonal], [0, 1, 2, 3], [0, 1, 2, 3])
     else:
         target = [target], [pl.BlockSpec((pix // STEPS, images, n_decode), lambda g, where: (g, 0, 0))]

time: 114 us -> 116 us (1.018)
  blocking collectives: 0 us -> 13 us
  waiting for transfers between devices: 27.2 us -> 20.2 us
  starting transfers between devices: 28.6 us -> 21.8 us
  local copies, waits for them, and re-layouts: 1.56 us -> 6.35 us
  Pallas kernels: 55.1 us -> 53.4 us
    all_to_all x0 -> x1, blocking collectives: none -> 13 us  [exchange(): lax.all_to_all(value, 'dp', 0, 0, axis_index_groups=groups, tiled=True)]
    ppermute x15, waiting for transfers between devices: 27 us -> 20.2 us  [swap(): return lax.ppermute(value, axis, [(i, i ^ bits) for i in range(count)])]
    all_to_all x2 -> x1, starting transfers between devices: 9.22 us -> 3.6 us  [exchange(): lax.all_to_all(value, 'dp', 0, 0, axis_index_groups=groups, tiled=True)]
    unnamed x32 -> x30, local copies, waits for them, and re-layouts: 1.47 us -> 6.26 us
    pallas_call x1, Pallas kernels: 18.8 us -> 17.4 us  [residual(): call(functools.partial(residual_kernel, groups, scale, len(feature), n_ti...]
  transfers between devices with their start and end apart: 17 -> 16, of which waited for: 10 -> 8; matrix products, arithmetic and copies ran while one was open for 0% -> 0% of each run, Pallas kernels for 45% -> 43%
where the time goes in v13:
time: 116 us
  Pallas kernels  53.4 us (46%)
  starting transfers between devices  21.8 us (19%)
  waiting for transfers between devices  20.2 us (17%)
  blocking collectives  13 us (11%)
  local copies, waits for them, and re-layouts  6.35 us (5%)
    ppermute x15, waiting for transfers between devices, swap(): return lax.ppermute(value, axis, [(i, i ^ bits) for i in range(count)])  20.2 us
    ppermute x15, starting transfers between devices, swap(): return lax.ppermute(value, axis, [(i, i ^ bits) for i in range(count)])  18.2 us
    pallas_call x1, Pallas kernels, residual(): call(functools.partial(residual_kernel, groups, scale, len(feature), n_ti...  17.4 us
    pallas_call x1, Pallas kernels, backward(): call(functools.partial(backward_kernel, groups, len(grad), n_decode), [sh...  14.2 us
    all_to_all x1, blocking collectives, exchange(): lax.all_to_all(value, 'dp', 0, 0, axis_index_groups=groups, tiled=True)  13 us
    pallas_call x1, Pallas kernels, forward(): call(functools.partial(forward_kernel, n_tiles, pix), [shape((pix * image...  9.54 us
    unnamed x30, local copies, waits for them, and re-layouts  6.26 us
    pallas_call x2, Pallas kernels, pack(): call(functools.partial(pack_kernel, h * half), shape(dims, BF16), limit=2...  3.63 us
  transfers between devices with their start and end apart: 16, of which 8 were waited for; matrix products, arithmetic and copies ran while one was open for 0% of the time, Pallas kernels for 43%

profile of v13, /device:TPU:0, one launch (start us, length us, event | category | flops | bytes accessed | tf_op | source)
XLA Modules:
  0.0 115.7 jit_solution(165640300318383343)
XLA Ops:
  0.7 0.1 stack.47.where_ref
  0.7 1.4 %copy-done = bf16[16,196,192]{1,2,0:T(8,128)(2,1)S(1)} copy-done((bf16[16,196,192]{1,2,0:T(8,128)(2,1)S(1)}, bf16[16,196,192]{1,2,0:T(8,128)(2,1)}, u32[]{:S(2)}) %copy-start) | copy-done | bytes 1204248
  2.2 1.8 %pack_patches.2.refs_8_.refs_16_ = bf16[147,16,128]{2,1,0:T(8,128)(2,1)S(1)} custom-call(s32[11]{0:T(128)S(1)} %stack.47.where_ref, bf16[16,192,196]{2,1,0:T(8,128)(2,1)S(1)} %bitcast.27, bf16[16,192,196]{2,1,0:T(8,128)(2,1)S(1)} %bitcast.28, bf16[16,192,196]{2,1,0:T(8,128)(2,1)S(1)} %bitcast.29, bf16[16,192,196]{2,1,0:T(8,128)(2,1)S(1)} %bitcast.30), custom_call_target="tpu_custom_call" | custom-call | tf_op jit(solution)/shard_map/pack_patches/pallas_call | solution.py:99
  4.0 0.0 copy-start.5
  4.0 0.0 copy-start.7
  4.0 3.0 %collective-permute-start.3 = (bf16[147,16,128]{2,1,0:T(8,128)(2,1)S(1)}, bf16[147,16,128]{2,1,0:T(8,128)(2,1)}, u32[]{:S(2)}, u32[]{:S(2)}) collective-permute-start(bf16[147,16,128]{2,1,0:T(8,128)(2,1)S(1)} %pack_patches.2.refs_8_.refs_16_), channel_id=1, source_target_pairs={{0,16},{8,24},{16,0},{24,8},{1,17},{9,25},{17,1},{25,9},{2,18},{10... | collective-permute-start | bytes 1806344 | tf_op jit(solution)/shard_map/ppermute | solution.py:46
  7.0 1.8 %pack_patches.3.refs_7_.refs_15_ = bf16[147,16,128]{2,1,0:T(8,128)(2,1)S(1)} custom-call(s32[11]{0:T(128)S(1)} %stack.47.where_ref, bf16[16,192,196]{2,1,0:T(8,128)(2,1)S(1)} %bitcast.31, bf16[16,192,196]{2,1,0:T(8,128)(2,1)S(1)} %bitcast.32, bf16[16,192,196]{2,1,0:T(8,128)(2,1)S(1)} %bitcast.33, bf16[16,192,196]{2,1,0:T(8,128)(2,1)S(1)} %bitcast.34), custom_call_target="tpu_custom_call" | custom-call | tf_op jit(solution)/shard_map/pack_patches/pallas_call | solution.py:99
  8.9 1.6 %collective-permute-start = (bf16[147,16,128]{2,1,0:T(8,128)(2,1)S(1)}, bf16[147,16,128]{2,1,0:T(8,128)(2,1)}, u32[]{:S(2)}, u32[]{:S(2)}) collective-permute-start(bf16[147,16,128]{2,1,0:T(8,128)(2,1)S(1)} %pack_patches.3.refs_7_.refs_15_), channel_id=1, source_target_pairs={{0,8},{8,0},{16,24},{24,16},{1,9},{9,1},{17,25},{25,17},{2,10},{10... | collective-permute-start | bytes 1806344 | tf_op jit(solution)/shard_map/ppermute | solution.py:46
  10.4 0.5 collective-permute-start.2
  10.9 0.1 collective-permute-start.1
  11.0 9.5 %forward.1 = (bf16[3136,256]{1,0:T(8,128)(2,1)}, bf16[3136,256]{1,0:T(8,128)(2,1)}, bf16[3136,256]{1,0:T(8,128)(2,1)}, bf16[3136,256]{1,0:T(8,128)(2,1)}, bf16[3...) custom-call(bf16[196,16,1024]{2,1,0:T(8,128)(2,1)} %bitcast.49, ...), custom_call_target="tpu_custom_call" | custom-call | tf_op jit(solution)/shard_map/forward/pallas_call | solution.py:171
  20.6 1.0 collective-permute-done.3.refs_12_.refs_20_
  21.6 4.0 %collective-permute-done.refs_9_.refs_17_ = bf16[147,16,128]{2,1,0:T(8,128)(2,1)} collective-permute-done((bf16[147,16,128]{2,1,0:T(8,128)(2,1)S(1)}, bf16[147,16,128]{2,1,0:T(8,128)(2,1)}, u32[]{:S(2)}, u32[]{:S(2)}) %collective-permute-start) | collective-permute-done | bytes 602144 | tf_op jit(solution)/shard_map/ppermute | solution.py:46
  25.6 2.0 %collective-permute-start.5 = (bf16[147,16,128]{2,1,0:T(8,128)(2,1)}, bf16[147,16,128]{2,1,0:T(8,128)(2,1)}, u32[]{:S(2)}, u32[]{:S(2)}) collective-permute-start(bf16[147,16,128]{2,1,0:T(8,128)(2,1)} %collective-permute-done.3.refs_12_.refs_20_), channel_id=1, source_target_pairs={{0,8},{8,0},{16,24},{24,16},{1,9},{9,1},{17,25},{25,17},{2,10},{10... | collective-permute-start | bytes 1806344 | tf_op jit(solution)/shard_map/ppermute | solution.py:46
  27.6 13.0 %all_to_all.10.got_ref = bf16[8,16,768]{2,1,0:T(8,128)(2,1)S(1)} all-to-all(bf16[8,16,768]{2,1,0:T(8,128)(2,1)S(1)} %get-tuple-element.44), channel_id=1, replica_groups=mesh['section'=4,'dp'=8] {'dp'}, dimensions={0} | all-to-all | bytes 393216 | tf_op jit(solution)/shard_map/all_to_all | solution.py:50
  40.6 2.7 %class_logits.1 = bf16[8,16,1152]{2,1,0:T(8,128)(2,1)} custom-call(s32[11]{0:T(128)S(1)} %stack.47.where_ref, bf16[8,16,768]{2,1,0:T(8,128)(2,1)S(1)} %all_to_all.10.got_ref, bf16[1408,512]{1,0:T(8,128)(2,1)S(1)} %bitcast.35), custom_call_target="tpu_custom_call" | custom-call | tf_op jit(solution)/shard_map/class_logits/pallas_call | solution.py:495
  43.2 3.6 %all-to-all-start.1 = ((bf16[8,16,1152]{2,1,0:T(8,128)(2,1)}), bf16[8,16,1152]{2,1,0:T(8,128)(2,1)S(1)}, u32[]{:S(2)}, u32[]{:S(2)}) async-start(bf16[8,16,1152]{2,1,0:T(8,128)(2,1)} %class_logits.1), calls=%async_computation.1 | async-start | bytes 589824 | tf_op jit(solution)/shard_map/all_to_all | solution.py:50
  46.9 0.0 collective-permute-done.4.refs_13_.refs_21_
  46.9 3.0 %collective-permute-done.5.refs_14_.refs_22_ = bf16[147,16,128]{2,1,0:T(8,128)(2,1)} collective-permute-done((bf16[147,16,128]{2,1,0:T(8,128)(2,1)}, bf16[147,16,128]{2,1,0:T(8,128)(2,1)}, u32[]{:S(2)}, u32[]{:S(2)}) %collective-permute-start.5) | collective-permute-done | bytes 602144 | tf_op jit(solution)/shard_map/ppermute | solution.py:46
  49.9 1.1 copy-done.4
  51.0 1.4 %copy-done.8 = bf16[1,1024,768]{2,1,0:T(8,128)(2,1)S(1)} copy-done((bf16[1,1024,768]{2,1,0:T(8,128)(2,1)S(1)}, bf16[1,1024,768]{2,1,0:T(8,128)(2,1)}, u32[]{:S(2)}) %copy-start.8) | copy-done | bytes 1572888
  52.4 17.4 %residual.1 = (bf16[3136,256]{1,0:T(8,128)(2,1)S(1)}, bf16[3136,256]{1,0:T(8,128)(2,1)S(1)}, bf16[3136,256]{1,0:T(8,128)(2,1)}, bf16[4,768,128]{2,1,0:T(8,128)(2,1)S(1)}, bf16[4,768,128]{2,1,0:T(8,128)(2,1)}) custom-call(s32[11]{0:T(128)S(1)} %stack.47.where_ref, bf16[3136,256]{1,0:T(8,128)(2,1)} %get-tuple-element.46.refs_0_, ...), custom_call_target="tpu_custom_call" | custom-call | flops 9865003008 | bytes 20873216 | tf_op jit(solution)/shard_map/residual/pallas_call | solution.py:328
  69.8 1.2 %copy-done.10 = bf16[3136,256]{1,0:T(8,128)(2,1)} copy-done((bf16[3136,256]{1,0:T(8,128)(2,1)}, bf16[3136,256]{1,0:T(8,128)(2,1)S(1)}, u32[]{:S(2)}) %copy-start.10) | copy-done | bytes 1605656
  70.9 1.2 %copy-done.12 = bf16[3136,256]{1,0:T(8,128)(2,1)} copy-done((bf16[3136,256]{1,0:T(8,128)(2,1)}, bf16[3136,256]{1,0:T(8,128)(2,1)S(1)}, u32[]{:S(2)}) %copy-start.12) | copy-done | bytes 1605656
  72.1 0.0 collective-permute-start.6
  72.1 0.0 all-to-all-done.1.got_ref.stats_ref
  72.1 0.3 aux_backward.1
  72.5 0.0 copy-start.6
  72.5 2.1 %collective-permute-done.6.got_ref = bf16[4,768,128]{2,1,0:T(8,128)(2,1)S(1)} collective-permute-done((bf16[4,768,128]{2,1,0:T(8,128)(2,1)}, bf16[4,768,128]{2,1,0:T(8,128)(2,1)S(1)}, u32[]{:S(2)}, u32[]{:S(2)}) %collective-permute-start.6) | collective-permute-done | bytes 786464 | tf_op jit(solution)/shard_map/ppermute | solution.py:46
  74.6 0.7 add_cores.2
  75.3 1.6 %collective-permute-start.7 = (bf16[832,128]{1,0:T(8,128)(2,1)S(1)}, bf16[832,128]{1,0:T(8,128)(2,1)S(1)}, u32[]{:S(2)}, u32[]{:S(2)}) collective-permute-start(bf16[832,128]{1,0:T(8,128)(2,1)S(1)} %get-tuple-element.57), channel_id=1, source_target_pairs={{0,2},{1,3},{2,0},{3,1},{4,6},{5,7},{6,4},{7,5},{8,10},{9,11},{10,... | collective-permute-start | bytes 638984 | tf_op jit(solution)/shard_map/ppermute | solution.py:46
  76.9 2.6 %collective-permute-start.8 = (bf16[832,128]{1,0:T(8,128)(2,1)S(1)}, bf16[832,128]{1,0:T(8,128)(2,1)S(1)}, u32[]{:S(2)}, u32[]{:S(2)}) collective-permute-start(bf16[832,128]{1,0:T(8,128)(2,1)S(1)} %get-tuple-element.58), channel_id=1, source_target_pairs={{0,4},{1,5},{2,6},{3,7},{4,0},{5,1},{6,2},{7,3},{8,12},{9,13},{10,... | collective-permute-start | bytes 638984 | tf_op jit(solution)/shard_map/ppermute | solution.py:46
  79.5 0.2 collective-permute-start.9
  79.8 14.2 %backward.1 = (bf16[4,512,128]{2,1,0:T(8,128)(2,1)S(1)}, bf16[4,512,128]{2,1,0:T(8,128)(2,1)S(1)}) custom-call(s32[11]{0:T(128)S(1)} %stack.47.where_ref, bf16[3136,256]{1,0:T(8,128)(2,1)S(1)} %copy-done.11, bf16[3136,256]{1,0:T(8,128)(2,1)S(1)} %copy-done.13, bf16[3136,256]{1,0:T(8,128)(2,1)S(1)} %copy-done.14, bf16[1024,768]{1,0:T(8,128)(2,1)S(1)} %bitcast.45, ...), custom_call_target="tpu_custom_call" | custom-call | flops 9865003008 | bytes 12845056 | tf_op jit(solution)/shard_map/backward/pallas_call | solution.py:407
  94.0 0.0 collective-permute-done.7.refs_1_
  94.0 1.1 collective-permute-done.8.refs_2_
  95.1 0.0 collective-permute-done.9.refs_3_
  95.1 0.0 collective-permute-start.10
  95.1 1.9 %collective-permute-done.10.got_ref = bf16[4,512,128]{2,1,0:T(8,128)(2,1)S(1)} collective-permute-done((bf16[4,512,128]{2,1,0:T(8,128)(2,1)S(1)}, bf16[4,512,128]{2,1,0:T(8,128)(2,1)S(1)}, u32[]{:S(2)}, u32[]{:S(2)}) %collective-permute-start.10) | collective-permute-done | bytes 524320 | tf_op jit(solution)/shard_map/ppermute | solution.py:46
  97.0 0.7 add_cores.3
  97.7 4.1 %collective-permute-start.11 = (bf16[512,128]{1,0:T(8,128)(2,1)S(1)}, bf16[512,128]{1,0:T(8,128)(2,1)S(1)}, u32[]{:S(2)}, u32[]{:S(2)}) collective-permute-start(bf16[512,128]{1,0:T(8,128)(2,1)S(1)} %get-tuple-element.70), channel_id=1, source_target_pairs={{0,2},{1,3},{2,0},{3,1},{4,6},{5,7},{6,4},{7,5},{8,10},{9,11},{10,... | collective-permute-start | bytes 393224 | tf_op jit(solution)/shard_map/ppermute | solution.py:46
  101.8 1.1 collective-permute-start.12
  102.9 1.4 %collective-permute-start.13 = (bf16[512,128]{1,0:T(8,128)(2,1)S(1)}, bf16[512,128]{1,0:T(8,128)(2,1)S(1)}, u32[]{:S(2)}, u32[]{:S(2)}) collective-permute-start(bf16[512,128]{1,0:T(8,128)(2,1)S(1)} %get-tuple-element.72), channel_id=1, source_target_pairs={{0,6},{1,7},{2,4},{3,5},{4,2},{5,3},{6,0},{7,1},{8,14},{9,15},{10,... | collective-permute-start | bytes 393224 | tf_op jit(solution)/shard_map/ppermute | solution.py:46
  104.3 1.3 %collective-permute-done.14.other_ref = bf16[4,64,128]{2,1,0:T(8,128)(2,1)S(1)} collective-permute-done((bf16[4,64,128]{2,1,0:T(8,128)(2,1)S(1)}, bf16[4,64,128]{2,1,0:T(8,128)(2,1)S(1)}, u32[]{:S(2)}, u32[]{:S(2)}) %collective-permute-start.14) | collective-permute-done | bytes 65568 | tf_op jit(solution)/shard_map/ppermute | solution.py:46
  105.5 3.3 %class_backward.1 = (f32[1408,512]{1,0:T(8,128)}, f32[128,512]{1,0:T(8,128)}) custom-call(s32[11]{0:T(128)S(1)} %stack.47.where_ref, bf16[1408,512]{1,0:T(8,128)(2,1)S(1)} %bitcast.36, bf16[8,16,768]{2,1,0:T(8,128)(2,1)S(1)} %all_to_all.10.got_ref, bf16[8,16,1152]{2,1,0:T(8,128)(2,1)S(1)} %all-to-all-done.1.got_ref.stats_ref, ...), custom_call_target="tpu_custom_call" | custom-call | flops 184549376 | bytes 2883584 | tf_op jit(solution)/shard_map/class_backward/pallas_call | solution.py:565
  108.9 0.0 collective-permute-done.11.refs_5_
  108.9 5.8 %collective-permute-done.12.refs_6_ = bf16[512,128]{1,0:T(8,128)(2,1)S(1)} collective-permute-done((bf16[512,128]{1,0:T(8,128)(2,1)S(1)}, bf16[512,128]{1,0:T(8,128)(2,1)S(1)}, u32[]{:S(2)}, u32[]{:S(2)}) %collective-permute-start.12) | collective-permute-done | bytes 131104 | tf_op jit(solution)/shard_map/ppermute | solution.py:46
  114.7 1.0 finish.1
  (27 shorter events, 0.1 us)
Async XLA Ops:
  0.7 1.4 %copy-start = (bf16[16,196,192]{1,2,0:T(8,128)(2,1)S(1)}, bf16[16,196,192]{1,2,0:T(8,128)(2,1)}, u32[]{:S(2)}) copy-start(bf16[16,196,192]{1,2,0:T(8,128)(2,1)} %param.9) | copy-start | bytes 3612676
  4.0 7.0 %copy-start.5 = (bf16[1,1024,256]{2,1,0:T(8,128)(2,1)S(1)}, bf16[1,1024,256]{2,1,0:T(8,128)(2,1)}, u32[]{:S(2)}) copy-start(bf16[1,1024,256]{2,1,0:T(8,128)(2,1)} %param.11) | copy-start | bytes 1572868
  4.0 7.0 %copy-start.7 = (s32[16]{0:T(128)S(1)}, s32[16]{0:T(128)}, u32[]{:S(2)}) copy-start(s32[16]{0:T(128)} %refs_7_.1) | copy-start | bytes 196
  4.0 17.6 %collective-permute-start.3 = (bf16[147,16,128]{2,1,0:T(8,128)(2,1)S(1)}, bf16[147,16,128]{2,1,0:T(8,128)(2,1)}, u32[]{:S(2)}, u32[]{:S(2)}) collective-permute-start(bf16[147,16,128]{2,1,0:T(8,128)(2,1)S(1)} %pack_patches.2.refs_8_.refs_16_), channel_id=1, source_target_pairs={{0,16},{8,24},{16,0},{24,8},{1,17},{9,25},{17,1},{25,9},{2,18},{10... | collective-permute-start | bytes 1806344 | tf_op jit(solution)/shard_map/ppermute | solution.py:46
  8.9 11.7 %copy-start.3 = (bf16[147,16,128]{2,1,0:T(8,128)(2,1)}, bf16[147,16,128]{2,1,0:T(8,128)(2,1)S(1)}, u32[]{:S(2)}) copy-start(bf16[147,16,128]{2,1,0:T(8,128)(2,1)S(1)} %pack_patches.3.refs_7_.refs_15_) | copy-start | bytes 1806340
  8.9 16.7 %collective-permute-start = (bf16[147,16,128]{2,1,0:T(8,128)(2,1)S(1)}, bf16[147,16,128]{2,1,0:T(8,128)(2,1)}, u32[]{:S(2)}, u32[]{:S(2)}) collective-permute-start(bf16[147,16,128]{2,1,0:T(8,128)(2,1)S(1)} %pack_patches.3.refs_7_.refs_15_), channel_id=1, source_target_pairs={{0,8},{8,0},{16,24},{24,16},{1,9},{9,1},{17,25},{25,17},{2,10},{10... | collective-permute-start | bytes 1806344 | tf_op jit(solution)/shard_map/ppermute | solution.py:46
  10.4 36.4 %collective-permute-start.2 = (bf16[147,16,128]{2,1,0:T(8,128)(2,1)S(1)}, bf16[147,16,128]{2,1,0:T(8,128)(2,1)}, u32[]{:S(2)}, u32[]{:S(2)}) collective-permute-start(bf16[147,16,128]{2,1,0:T(8,128)(2,1)S(1)} %pack_patches.3.refs_7_.refs_15_), channel_id=1, source_target_pairs={{0,16},{8,24},{16,0},{24,8},{1,17},{9,25},{17,1},{25,9},{2,18},{10... | collective-permute-start | bytes 1806344 | tf_op jit(solution)/shard_map/ppermute | solution.py:46
  10.9 35.9 %collective-permute-start.1 = (bf16[147,16,128]{2,1,0:T(8,128)(2,1)S(1)}, bf16[147,16,128]{2,1,0:T(8,128)(2,1)}, u32[]{:S(2)}, u32[]{:S(2)}) collective-permute-start(bf16[147,16,128]{2,1,0:T(8,128)(2,1)S(1)} %pack_patches.2.refs_8_.refs_16_), channel_id=1, source_target_pairs={{0,8},{8,0},{16,24},{24,16},{1,9},{9,1},{17,25},{25,17},{2,10},{10... | collective-permute-start | bytes 1806344 | tf_op jit(solution)/shard_map/ppermute | solution.py:46
  11.0 29.5 %copy-start.1 = (bf16[1,1408,512]{2,1,0:T(8,128)(2,1)S(1)}, bf16[1,1408,512]{2,1,0:T(8,128)(2,1)}, u32[]{:S(2)}) copy-start(bf16[1,1408,512]{2,1,0:T(8,128)(2,1)} %param.15) | copy-start | bytes 4325380
  25.6 21.3 %collective-permute-start.4 = (bf16[147,16,128]{2,1,0:T(8,128)(2,1)}, bf16[147,16,128]{2,1,0:T(8,128)(2,1)}, u32[]{:S(2)}, u32[]{:S(2)}) collective-permute-start(bf16[147,16,128]{2,1,0:T(8,128)(2,1)} %collective-permute-done.refs_9_.refs_17_), channel_id=1, source_target_pairs={{0,16},{8,24},{16,0},{24,8},{1,17},{9,25},{17,1},{25,9},{2,18},{10... | collective-permute-start | bytes 1806344 | tf_op jit(solution)/shard_map/ppermute | solution.py:46
  25.6 24.3 %collective-permute-start.5 = (bf16[147,16,128]{2,1,0:T(8,128)(2,1)}, bf16[147,16,128]{2,1,0:T(8,128)(2,1)}, u32[]{:S(2)}, u32[]{:S(2)}) collective-permute-start(bf16[147,16,128]{2,1,0:T(8,128)(2,1)} %collective-permute-done.3.refs_12_.refs_20_), channel_id=1, source_target_pairs={{0,8},{8,0},{16,24},{24,16},{1,9},{9,1},{17,25},{25,17},{2,10},{10... | collective-permute-start | bytes 1806344 | tf_op jit(solution)/shard_map/ppermute | solution.py:46
  43.2 28.8 %all-to-all-start.1 = ((bf16[8,16,1152]{2,1,0:T(8,128)(2,1)}), bf16[8,16,1152]{2,1,0:T(8,128)(2,1)S(1)}, u32[]{:S(2)}, u32[]{:S(2)}) async-start(bf16[8,16,1152]{2,1,0:T(8,128)(2,1)} %class_logits.1), calls=%async_computation.1 | async-start | bytes 589824 | tf_op jit(solution)/shard_map/all_to_all | solution.py:50
  49.9 1.1 copy-start.4
  51.0 1.4 %copy-start.8 = (bf16[1,1024,768]{2,1,0:T(8,128)(2,1)S(1)}, bf16[1,1024,768]{2,1,0:T(8,128)(2,1)}, u32[]{:S(2)}) copy-start(bf16[1,1024,768]{2,1,0:T(8,128)(2,1)} %param.13) | copy-start | bytes 4718596
  69.7 1.2 %copy-start.10 = (bf16[3136,256]{1,0:T(8,128)(2,1)}, bf16[3136,256]{1,0:T(8,128)(2,1)S(1)}, u32[]{:S(2)}) copy-start(bf16[3136,256]{1,0:T(8,128)(2,1)S(1)} %get-tuple-element.60.refs_0_) | copy-start | bytes 4816900
  70.9 1.2 %copy-start.12 = (bf16[3136,256]{1,0:T(8,128)(2,1)}, bf16[3136,256]{1,0:T(8,128)(2,1)S(1)}, u32[]{:S(2)}) copy-start(bf16[3136,256]{1,0:T(8,128)(2,1)S(1)} %get-tuple-element.61.refs_1_) | copy-start | bytes 4816900
  72.1 2.5 %collective-permute-start.6 = (bf16[4,768,128]{2,1,0:T(8,128)(2,1)}, bf16[4,768,128]{2,1,0:T(8,128)(2,1)S(1)}, u32[]{:S(2)}, u32[]{:S(2)}) collective-permute-start(bf16[4,768,128]{2,1,0:T(8,128)(2,1)} %get-tuple-element.54), channel_id=1, source_target_pairs={{0,1},{1,0},{2,3},{3,2},{4,5},{5,4},{6,7},{7,6},{8,9},{9,8},{10,11... | collective-permute-start | bytes 2359304 | tf_op jit(solution)/shard_map/ppermute | solution.py:46
  72.1 7.7 %copy-start.9 = (bf16[1,1024,768]{2,1,0:T(8,128)(2,1)S(1)}, bf16[1,1024,768]{2,1,0:T(8,128)(2,1)}, u32[]{:S(2)}) copy-start(bf16[1,1024,768]{2,1,0:T(8,128)(2,1)} %param.13) | copy-start | bytes 4718596
  72.1 7.7 %copy-start.11 = (bf16[3136,256]{1,0:T(8,128)(2,1)S(1)}, bf16[3136,256]{1,0:T(8,128)(2,1)}, u32[]{:S(2)}) copy-start(bf16[3136,256]{1,0:T(8,128)(2,1)} %copy-done.10) | copy-start | bytes 4816900
  72.1 7.7 %copy-start.13 = (bf16[3136,256]{1,0:T(8,128)(2,1)S(1)}, bf16[3136,256]{1,0:T(8,128)(2,1)}, u32[]{:S(2)}) copy-start(bf16[3136,256]{1,0:T(8,128)(2,1)} %copy-done.12) | copy-start | bytes 4816900
  72.1 7.7 %copy-start.14 = (bf16[3136,256]{1,0:T(8,128)(2,1)S(1)}, bf16[3136,256]{1,0:T(8,128)(2,1)}, u32[]{:S(2)}) copy-start(bf16[3136,256]{1,0:T(8,128)(2,1)} %get-tuple-element.62.refs_2_) | copy-start | bytes 4816900
  72.5 7.3 %copy-start.2 = (bf16[1,1024,512]{2,1,0:T(8,128)(2,1)S(1)}, bf16[1,1024,512]{2,1,0:T(8,128)(2,1)}, u32[]{:S(2)}) copy-start(bf16[1,1024,512]{2,1,0:T(8,128)(2,1)} %param.14) | copy-start | bytes 3145732
  72.5 7.3 %copy-start.6 = (bf16[1,256,1024]{2,1,0:T(8,128)(2,1)S(1)}, bf16[1,256,1024]{2,1,0:T(8,128)(2,1)}, u32[]{:S(2)}) copy-start(bf16[1,256,1024]{2,1,0:T(8,128)(2,1)} %param.12) | copy-start | bytes 1572868
  75.3 18.7 %collective-permute-start.7 = (bf16[832,128]{1,0:T(8,128)(2,1)S(1)}, bf16[832,128]{1,0:T(8,128)(2,1)S(1)}, u32[]{:S(2)}, u32[]{:S(2)}) collective-permute-start(bf16[832,128]{1,0:T(8,128)(2,1)S(1)} %get-tuple-element.57), channel_id=1, source_target_pairs={{0,2},{1,3},{2,0},{3,1},{4,6},{5,7},{6,4},{7,5},{8,10},{9,11},{10,... | collective-permute-start | bytes 638984 | tf_op jit(solution)/shard_map/ppermute | solution.py:46
  76.9 18.2 %collective-permute-start.8 = (bf16[832,128]{1,0:T(8,128)(2,1)S(1)}, bf16[832,128]{1,0:T(8,128)(2,1)S(1)}, u32[]{:S(2)}, u32[]{:S(2)}) collective-permute-start(bf16[832,128]{1,0:T(8,128)(2,1)S(1)} %get-tuple-element.58), channel_id=1, source_target_pairs={{0,4},{1,5},{2,6},{3,7},{4,0},{5,1},{6,2},{7,3},{8,12},{9,13},{10,... | collective-permute-start | bytes 638984 | tf_op jit(solution)/shard_map/ppermute | solution.py:46
  79.5 15.6 %collective-permute-start.9 = (bf16[832,128]{1,0:T(8,128)(2,1)S(1)}, bf16[832,128]{1,0:T(8,128)(2,1)S(1)}, u32[]{:S(2)}, u32[]{:S(2)}) collective-permute-start(bf16[832,128]{1,0:T(8,128)(2,1)S(1)} %get-tuple-element.59), channel_id=1, source_target_pairs={{0,6},{1,7},{2,4},{3,5},{4,2},{5,3},{6,0},{7,1},{8,14},{9,15},{10,... | collective-permute-start | bytes 638984 | tf_op jit(solution)/shard_map/ppermute | solution.py:46
  95.1 1.9 %collective-permute-start.10 = (bf16[4,512,128]{2,1,0:T(8,128)(2,1)S(1)}, bf16[4,512,128]{2,1,0:T(8,128)(2,1)S(1)}, u32[]{:S(2)}, u32[]{:S(2)}) collective-permute-start(bf16[4,512,128]{2,1,0:T(8,128)(2,1)S(1)} %get-tuple-element.68), channel_id=1, source_target_pairs={{0,1},{1,0},{2,3},{3,2},{4,5},{5,4},{6,7},{7,6},{8,9},{9,8},{10,11... | collective-permute-start | bytes 1572872 | tf_op jit(solution)/shard_map/ppermute | solution.py:46
  97.7 11.2 %collective-permute-start.11 = (bf16[512,128]{1,0:T(8,128)(2,1)S(1)}, bf16[512,128]{1,0:T(8,128)(2,1)S(1)}, u32[]{:S(2)}, u32[]{:S(2)}) collective-permute-start(bf16[512,128]{1,0:T(8,128)(2,1)S(1)} %get-tuple-element.70), channel_id=1, source_target_pairs={{0,2},{1,3},{2,0},{3,1},{4,6},{5,7},{6,4},{7,5},{8,10},{9,11},{10,... | collective-permute-start | bytes 393224 | tf_op jit(solution)/shard_map/ppermute | solution.py:46
  101.8 12.9 %collective-permute-start.12 = (bf16[512,128]{1,0:T(8,128)(2,1)S(1)}, bf16[512,128]{1,0:T(8,128)(2,1)S(1)}, u32[]{:S(2)}, u32[]{:S(2)}) collective-permute-start(bf16[512,128]{1,0:T(8,128)(2,1)S(1)} %get-tuple-element.71), channel_id=1, source_target_pairs={{0,4},{1,5},{2,6},{3,7},{4,0},{5,1},{6,2},{7,3},{8,12},{9,13},{10,... | collective-permute-start | bytes 393224 | tf_op jit(solution)/shard_map/ppermute | solution.py:46
  102.9 11.8 %collective-permute-start.13 = (bf16[512,128]{1,0:T(8,128)(2,1)S(1)}, bf16[512,128]{1,0:T(8,128)(2,1)S(1)}, u32[]{:S(2)}, u32[]{:S(2)}) collective-permute-start(bf16[512,128]{1,0:T(8,128)(2,1)S(1)} %get-tuple-element.72), channel_id=1, source_target_pairs={{0,6},{1,7},{2,4},{3,5},{4,2},{5,3},{6,0},{7,1},{8,14},{9,15},{10,... | collective-permute-start | bytes 393224 | tf_op jit(solution)/shard_map/ppermute | solution.py:46
  104.3 1.3 %collective-permute-start.14 = (bf16[4,64,128]{2,1,0:T(8,128)(2,1)S(1)}, bf16[4,64,128]{2,1,0:T(8,128)(2,1)S(1)}, u32[]{:S(2)}, u32[]{:S(2)}) collective-permute-start(bf16[4,64,128]{2,1,0:T(8,128)(2,1)S(1)} %get-tuple-element.76.mine_ref), channel_id=1, source_target_pairs={{0,1},{1,0},{2,3},{3,2},{4,5},{5,4},{6,7},{7,6},{8,9},{9,8},{10,11... | collective-permute-start | bytes 196616 | tf_op jit(solution)/shard_map/ppermute | solution.py:46

commit v14 on v10

--- a/solution.py
+++ b/solution.py
@@ -197,6 +197,28 @@
     return hidden, feature, aux_pre, sent
 
 
+def recon_kernel(n_feature, n_tiles, *refs):
+    feature_refs, decode_refs, recon_refs = refs[:n_feature], refs[n_feature : n_feature + n_tiles], refs[n_feature + n_tiles :]
+    feature = jnp.concatenate([ref[...] for ref in feature_refs], axis=1)
+    for decode_ref, recon_ref in zip(decode_refs, recon_refs):
+        recon_ref[...] = dot(feature, decode_ref[...])
+
+
+def reconstruct(feature, decode, n_tiles):
+    rows = feature[0].shape[0]
+    width = decode.shape[0]
+    block = pl.BlockSpec((rows // STEPS, TILE), lambda g: (g, 0))
+    return call(
+        functools.partial(recon_kernel, len(feature), n_tiles),
+        [shape((rows, TILE), F32)] * n_tiles,
+        limit=57,
+        grid=(STEPS,),
+        in_specs=[*[block] * len(feature), *[pl.BlockSpec((width, TILE), lambda g, j=j: (0, j)) for j in range(n_tiles)]],
+        out_specs=[block] * n_tiles,
+        name="reconstruct",
+    )(*feature, *[decode] * n_tiles)
+
+
 def own_index(h):
     per_half = STEPS // 2
     return lambda g, where: (jnp.clip(g - h * per_half, 0, per_half - 1), 0, 0)
@@ -290,7 +312,7 @@
 
 def residual_kernel(groups, scale, n_feature, n_tiles, n_patch, where_ref, *refs):
     feature_refs, refs = refs[:n_feature], refs[n_feature:]
-    decode_refs, refs = refs[:n_tiles], refs[n_tiles:]
+    recon_refs, refs = refs[:n_tiles], refs[n_tiles:]
     patch_refs, refs = refs[:n_patch], refs[n_patch:]
     grad_refs, refs = refs[:n_tiles], refs[n_tiles:]
     keep_ref, send_ref, target, feature, grads, total, sems = refs
@@ -302,11 +324,9 @@
         lay_target(g, where_ref, patch_refs, target)
         if g:
             contract(g - 1, rows, [(total, grads, feature)])
-        now = feature[here]
         for j, grad_ref in enumerate(grad_refs):
             cut = slice(j * TILE, (j + 1) * TILE)
-            recon = sum(dot(now[:, k : k + TILE], decode_refs[j][k : k + TILE]) for k in range(0, width, TILE))
-            grad = ((recon - target[:, :, cut].reshape(size, TILE).astype(F32)) * scale).astype(BF16)
+            grad = ((recon_refs[j][...] - target[:, :, cut].reshape(size, TILE).astype(F32)) * scale).astype(BF16)
             grad_ref[...] = grad
             grads[here, cut] = grad
         if g == STEPS - 1:
@@ -316,27 +336,26 @@
     by_step(copies_of(feature_refs, feature, sems), body)
 
 
-def residual(where, feature, decode, patch_args, patch_specs, images, scale, groups):
+def residual(where, feature, recon, patch_args, patch_specs, images, scale, groups):
     rows = feature[0].shape[0]
-    width, n = decode.shape
+    n_tiles = len(recon)
+    width, n = len(feature) * TILE, n_tiles * TILE
     size = rows // STEPS
-    n_tiles = n // TILE
     parts = (groups // 2, n, width // groups)
     dealt = pl.BlockSpec(parts, lambda g, where: (0, 0, 0))
     block = pl.BlockSpec((size, TILE), lambda g, where: (g, 0))
-    column = lambda j: pl.BlockSpec((width, TILE), lambda g, where: (0, j))
     *grad, keep, send = call(
         functools.partial(residual_kernel, groups, scale, len(feature), n_tiles, len(patch_args)),
         [*[shape((rows, TILE), BF16)] * n_tiles, shape(parts, BF16), shape(parts, BF16)],
         limit=58,
-        flops=4 * rows * width * n,
+        flops=2 * rows * width * n,
         moved=rows * (2 * width + 6 * n),
         grid_spec=pltpu.PrefetchScalarGridSpec(
             num_scalar_prefetch=1,
             grid=(STEPS,),
             in_specs=[
                 *[HBM] * len(feature),
-                *[column(j) for j in range(n_tiles)],
+                *[block] * n_tiles,
                 *patch_specs,
             ],
             out_specs=[*[block] * n_tiles, dealt, dealt],
@@ -349,7 +368,7 @@
             ],
         ),
         name="residual",
-    )(where, *feature, *[decode] * n_tiles, *patch_args)
+    )(where, *feature, *recon, *patch_args)
     return grad, keep, send
 
 
@@ -672,9 +691,10 @@
     else:
         target = [target], [pl.BlockSpec((pix // STEPS, images, n_decode), lambda g, where: (g, 0, 0))]
     got = exchange(sent)
-    sent = class_logits(where, got, klass)
+    recon = reconstruct([after(feature[0], sent), *feature[1:]], decode, n_decode // TILE)
+    sent = class_logits(where, after(got, recon[0]), klass)
     partial = exchange(sent)
-    grad, keep, send = residual(after(where, sent), feature, decode, *target, images, scale, groups)
+    grad, keep, send = residual(after(where, sent), feature, recon, *target, images, scale, groups)
     aux_grad, aux_cut = aux_backward(partial, aux_pre, width // groups, norm)
     chip_decode = add_cores(where, keep, send, [aux_cut])
     sum_decode = exchange_chips(chip_decode)

time: 113 us -> 112 us (level)
  blocking collectives: 13.2 us -> 0 us
  Pallas kernels: 55.4 us -> 62.7 us
  starting transfers between devices: 21.9 us -> 28.8 us
  waiting for transfers between devices: 19.6 us -> 17 us
    all_to_all x1 -> x0, blocking collectives: 13.2 us -> none  [exchange(): lax.all_to_all(value, 'dp', 0, 0, axis_index_groups=groups, tiled=True)]
    pallas_call x0 -> x1, Pallas kernels: none -> 9.77 us  [reconstruct(): call(functools.partial(recon_kernel, len(feature), n_tiles), [shape((rows...]
    all_to_all x1 -> x2, starting transfers between devices: 3.6 us -> 9.98 us  [exchange(): lax.all_to_all(value, 'dp', 0, 0, axis_index_groups=groups, tiled=True)]
    pallas_call x1, Pallas kernels: 19 us -> 16 us  [residual(): call(functools.partial(residual_kernel, groups, scale, len(feature), n_ti...]
    ppermute x15, waiting for transfers between devices: 19.6 us -> 17 us  [swap(): return lax.ppermute(value, axis, [(i, i ^ bits) for i in range(count)])]
  transfers between devices with their start and end apart: 16 -> 17, of which waited for: 8 -> 7; matrix products, arithmetic and copies ran while one was open for 0% -> 0% of each run, Pallas kernels for 45% -> 52%
where the time goes in v14:
time: 112 us; the launch traced here: 111 us
  Pallas kernels  62.7 us (56%)
  starting transfers between devices  28.8 us (26%)
  waiting for transfers between devices  17 us (15%)
  local copies, waits for them, and re-layouts  1.55 us (1%)
    ppermute x15, starting transfers between devices, swap(): return lax.ppermute(value, axis, [(i, i ^ bits) for i in range(count)])  18.8 us
    ppermute x15, waiting for transfers between devices, swap(): return lax.ppermute(value, axis, [(i, i ^ bits) for i in range(count)])  17 us
    pallas_call x1, Pallas kernels, residual(): call(functools.partial(residual_kernel, groups, scale, len(feature), n_ti...  16 us
    pallas_call x1, Pallas kernels, backward(): call(functools.partial(backward_kernel, groups, len(grad), n_decode), [sh...  14.3 us
    all_to_all x2, starting transfers between devices, exchange(): lax.all_to_all(value, 'dp', 0, 0, axis_index_groups=groups, tiled=True)  9.98 us
    pallas_call x1, Pallas kernels, reconstruct(): call(functools.partial(recon_kernel, len(feature), n_tiles), [shape((rows...  9.77 us
    pallas_call x1, Pallas kernels, forward(): call(functools.partial(forward_kernel, n_tiles, pix), [shape((pix * image...  9.66 us
    pallas_call x2, Pallas kernels, pack(): call(functools.partial(pack_kernel, h * half), shape(dims, BF16), limit=2...  3.62 us
  transfers between devices with their start and end apart: 17, of which 7 were waited for; matrix products, arithmetic and copies ran while one was open for 0% of the time, Pallas kernels for 52%

profile of v14, /device:TPU:0, one launch (start us, length us, event | category | flops | bytes accessed | tf_op | source)
XLA Modules:
  0.0 111.0 jit_solution(10329074288780099961)
XLA Ops:
  0.7 0.1 stack.47.where_ref
  0.7 0.0 copy-start
  0.8 1.4 %copy-done = bf16[16,196,192]{1,2,0:T(8,128)(2,1)S(1)} copy-done((bf16[16,196,192]{1,2,0:T(8,128)(2,1)S(1)}, bf16[16,196,192]{1,2,0:T(8,128)(2,1)}, u32[]{:S(2)}) %copy-start) | copy-done | bytes 1204248
  2.2 1.8 %pack_patches.2.refs_8_.refs_16_ = bf16[147,16,128]{2,1,0:T(8,128)(2,1)S(1)} custom-call(s32[11]{0:T(128)S(1)} %stack.47.where_ref, bf16[16,192,196]{2,1,0:T(8,128)(2,1)S(1)} %bitcast.27, bf16[16,192,196]{2,1,0:T(8,128)(2,1)S(1)} %bitcast.28, bf16[16,192,196]{2,1,0:T(8,128)(2,1)S(1)} %bitcast.29, bf16[16,192,196]{2,1,0:T(8,128)(2,1)S(1)} %bitcast.30), custom_call_target="tpu_custom_call" | custom-call | tf_op jit(solution)/shard_map/pack_patches/pallas_call | solution.py:99
  4.0 3.0 %collective-permute-start.3 = (bf16[147,16,128]{2,1,0:T(8,128)(2,1)S(1)}, bf16[147,16,128]{2,1,0:T(8,128)(2,1)}, u32[]{:S(2)}, u32[]{:S(2)}) collective-permute-start(bf16[147,16,128]{2,1,0:T(8,128)(2,1)S(1)} %pack_patches.2.refs_8_.refs_16_), channel_id=1, source_target_pairs={{0,16},{8,24},{16,0},{24,8},{1,17},{9,25},{17,1},{25,9},{2,18},{10... | collective-permute-start | bytes 1806344 | tf_op jit(solution)/shard_map/ppermute | solution.py:46
  7.0 1.8 %pack_patches.3.refs_7_.refs_15_ = bf16[147,16,128]{2,1,0:T(8,128)(2,1)S(1)} custom-call(s32[11]{0:T(128)S(1)} %stack.47.where_ref, bf16[16,192,196]{2,1,0:T(8,128)(2,1)S(1)} %bitcast.31, bf16[16,192,196]{2,1,0:T(8,128)(2,1)S(1)} %bitcast.32, bf16[16,192,196]{2,1,0:T(8,128)(2,1)S(1)} %bitcast.33, bf16[16,192,196]{2,1,0:T(8,128)(2,1)S(1)} %bitcast.34), custom_call_target="tpu_custom_call" | custom-call | tf_op jit(solution)/shard_map/pack_patches/pallas_call | solution.py:99
  8.8 1.6 %collective-permute-start = (bf16[147,16,128]{2,1,0:T(8,128)(2,1)S(1)}, bf16[147,16,128]{2,1,0:T(8,128)(2,1)}, u32[]{:S(2)}, u32[]{:S(2)}) collective-permute-start(bf16[147,16,128]{2,1,0:T(8,128)(2,1)S(1)} %pack_patches.3.refs_7_.refs_15_), channel_id=1, source_target_pairs={{0,8},{8,0},{16,24},{24,16},{1,9},{9,1},{17,25},{25,17},{2,10},{10... | collective-permute-start | bytes 1806344 | tf_op jit(solution)/shard_map/ppermute | solution.py:46
  10.4 0.5 collective-permute-start.2
  10.9 0.1 collective-permute-start.1
  11.0 9.7 %forward.1 = (bf16[3136,256]{1,0:T(8,128)(2,1)}, bf16[3136,256]{1,0:T(8,128)(2,1)}, bf16[3136,256]{1,0:T(8,128)(2,1)}, bf16[3136,256]{1,0:T(8,128)(2,1)}, bf16[3...) custom-call(bf16[196,16,1024]{2,1,0:T(8,128)(2,1)} %bitcast.48, ...), custom_call_target="tpu_custom_call" | custom-call | tf_op jit(solution)/shard_map/forward/pallas_call | solution.py:171
  20.7 0.9 collective-permute-done.3.refs_12_.refs_20_
  21.5 4.0 %collective-permute-done.refs_9_.refs_17_ = bf16[147,16,128]{2,1,0:T(8,128)(2,1)} collective-permute-done((bf16[147,16,128]{2,1,0:T(8,128)(2,1)S(1)}, bf16[147,16,128]{2,1,0:T(8,128)(2,1)}, u32[]{:S(2)}, u32[]{:S(2)}) %collective-permute-start) | collective-permute-done | bytes 602144 | tf_op jit(solution)/shard_map/ppermute | solution.py:46
  25.5 0.0 collective-permute-start.4
  25.5 2.0 %collective-permute-start.5 = (bf16[147,16,128]{2,1,0:T(8,128)(2,1)}, bf16[147,16,128]{2,1,0:T(8,128)(2,1)}, u32[]{:S(2)}, u32[]{:S(2)}) collective-permute-start(bf16[147,16,128]{2,1,0:T(8,128)(2,1)} %collective-permute-done.3.refs_12_.refs_20_), channel_id=1, source_target_pairs={{0,8},{8,0},{16,24},{24,16},{1,9},{9,1},{17,25},{25,17},{2,10},{10... | collective-permute-start | bytes 1806344 | tf_op jit(solution)/shard_map/ppermute | solution.py:46
  27.5 4.9 %all-to-all-start = ((bf16[8,16,768]{2,1,0:T(8,128)(2,1)}), bf16[8,16,768]{2,1,0:T(8,128)(2,1)S(1)}, u32[]{:S(2)}, u32[]{:S(2)}) async-start(bf16[8,16,768]{2,1,0:T(8,128)(2,1)} %get-tuple-element.49), calls=%async_computation | async-start | bytes 393216 | tf_op jit(solution)/shard_map/all_to_all | solution.py:50
  32.4 9.8 %reconstruct.1 = (f32[3136,256]{1,0:T(8,128)}, f32[3136,256]{1,0:T(8,128)}, f32[3136,256]{1,0:T(8,128)}) custom-call(bf16[3136,256]{1,0:T(8,128)(2,1)} %get-tuple-element.51.refs_0_, bf16[3136,256]{1,0:T(8,128)(2,1)} %get-tuple-element.52.refs_1_, bf16[3136,256]{1,0:T(8,128)(2,1)} %get-tuple-element.53.refs_2_, bf16[3136,256]{1,0:T(8,128)(2,1)} %get-tuple-element.54.refs_3_, ...), custom_call_target="tpu_custom_call" | custom-call | tf_op jit(solution)/shard_map/reconstruct/pallas_call | solution.py:211
  42.2 0.0 all-to-all-done.got_ref
  42.2 2.7 %class_logits.1 = bf16[8,16,1152]{2,1,0:T(8,128)(2,1)} custom-call(s32[11]{0:T(128)S(1)} %stack.47.where_ref, bf16[8,16,768]{2,1,0:T(8,128)(2,1)S(1)} %all-to-all-done.got_ref, bf16[1408,512]{1,0:T(8,128)(2,1)S(1)} %bitcast.42), custom_call_target="tpu_custom_call" | custom-call | tf_op jit(solution)/shard_map/class_logits/pallas_call | solution.py:514
  44.9 5.1 %all-to-all-start.1 = ((bf16[8,16,1152]{2,1,0:T(8,128)(2,1)}), bf16[8,16,1152]{2,1,0:T(8,128)(2,1)S(1)}, u32[]{:S(2)}, u32[]{:S(2)}) async-start(bf16[8,16,1152]{2,1,0:T(8,128)(2,1)} %class_logits.1), calls=%async_computation.1 | async-start | bytes 589824 | tf_op jit(solution)/shard_map/all_to_all | solution.py:50
  50.0 0.0 collective-permute-done.2.refs_11_.refs_19_
  50.0 0.0 collective-permute-done.1.refs_10_.refs_18_
  50.0 0.0 collective-permute-done.4.refs_13_.refs_21_
  50.0 0.0 collective-permute-done.5.refs_14_.refs_22_
  50.0 0.0 copy-start.13
  50.0 16.0 %residual.1 = (bf16[3136,256]{1,0:T(8,128)(2,1)}, bf16[3136,256]{1,0:T(8,128)(2,1)}, bf16[3136,256]{1,0:T(8,128)(2,1)}, bf16[4,768,128]{2,1,0:T(8,128)(2,1)}, bf16[4,768,128]{2,1,0:T(8,128)(2,1)}) custom-call(s32[11]{0:T(128)} %copy-done.8, bf16[3136,256]{1,0:T(8,128)(2,1)} %get-tuple-element.51.refs_0_, bf16[3136,256]{1,0:T(8,128)(2,1)} %get-tuple-element.52.refs_1_, ...), custom_call_target="tpu_custom_call" | custom-call | flops 4932501504 | bytes 20873216 | tf_op jit(solution)/shard_map/residual/pallas_call | solution.py:347
  66.1 0.0 copy-start.9
  66.1 0.6 collective-permute-start.6
  66.6 0.0 all-to-all-done.1.got_ref.stats_ref
  66.7 0.3 aux_backward.1
  67.0 1.9 %collective-permute-done.6.got_ref = bf16[4,768,128]{2,1,0:T(8,128)(2,1)} collective-permute-done((bf16[4,768,128]{2,1,0:T(8,128)(2,1)}, bf16[4,768,128]{2,1,0:T(8,128)(2,1)}, u32[]{:S(2)}, u32[]{:S(2)}) %collective-permute-start.6) | collective-permute-done | bytes 786464 | tf_op jit(solution)/shard_map/ppermute | solution.py:46
  68.9 1.4 %add_cores.2 = (bf16[832,128]{1,0:T(8,128)(2,1)S(1)}, bf16[832,128]{1,0:T(8,128)(2,1)S(1)}, bf16[832,128]{1,0:T(8,128)(2,1)S(1)}, bf16[832,128]{1,0:T(8,128)(2,1)S(1)}) custom-call(s32[11]{0:T(128)S(1)} %copy-done.9, bf16[4,768,128]{2,1,0:T(8,128)(2,1)S(1)} %copy-done.6, bf16[4,768,128]{2,1,0:T(8,128)(2,1)} %collective-permute-done.6.got_ref, ...), custom_call_target="tpu_custom_call" | custom-call | tf_op jit(solution)/shard_map/add_cores/pallas_call | solution.py:624
  70.3 1.9 %collective-permute-start.7 = (bf16[832,128]{1,0:T(8,128)(2,1)S(1)}, bf16[832,128]{1,0:T(8,128)(2,1)S(1)}, u32[]{:S(2)}, u32[]{:S(2)}) collective-permute-start(bf16[832,128]{1,0:T(8,128)(2,1)S(1)} %get-tuple-element.67), channel_id=1, source_target_pairs={{0,2},{1,3},{2,0},{3,1},{4,6},{5,7},{6,4},{7,5},{8,10},{9,11},{10,... | collective-permute-start | bytes 638984 | tf_op jit(solution)/shard_map/ppermute | solution.py:46
  72.2 2.4 %collective-permute-start.8 = (bf16[832,128]{1,0:T(8,128)(2,1)S(1)}, bf16[832,128]{1,0:T(8,128)(2,1)S(1)}, u32[]{:S(2)}, u32[]{:S(2)}) collective-permute-start(bf16[832,128]{1,0:T(8,128)(2,1)S(1)} %get-tuple-element.68), channel_id=1, source_target_pairs={{0,4},{1,5},{2,6},{3,7},{4,0},{5,1},{6,2},{7,3},{8,12},{9,13},{10,... | collective-permute-start | bytes 638984 | tf_op jit(solution)/shard_map/ppermute | solution.py:46
  74.6 0.2 collective-permute-start.9
  74.8 14.3 %backward.1 = (bf16[4,512,128]{2,1,0:T(8,128)(2,1)S(1)}, bf16[4,512,128]{2,1,0:T(8,128)(2,1)S(1)}) custom-call(s32[11]{0:T(128)S(1)} %copy-done.9, bf16[3136,256]{1,0:T(8,128)(2,1)S(1)} %copy-done.10, bf16[3136,256]{1,0:T(8,128)(2,1)S(1)} %copy-done.11, bf16[3136,256]{1,0:T(8,128)(2,1)S(1)} %copy-done.12, bf16[1024,768]{1,0:T(8,128)(2,1)S(1)} %bitcast.38, ...), custom_call_target="tpu_custom_call" | custom-call | flops 9865003008 | bytes 12845056 | tf_op jit(solution)/shard_map/backward/pallas_call | solution.py:426
  89.1 0.0 collective-permute-done.7.refs_1_
  89.2 1.2 %collective-permute-done.8.refs_2_ = bf16[832,128]{1,0:T(8,128)(2,1)S(1)} collective-permute-done((bf16[832,128]{1,0:T(8,128)(2,1)S(1)}, bf16[832,128]{1,0:T(8,128)(2,1)S(1)}, u32[]{:S(2)}, u32[]{:S(2)}) %collective-permute-start.8) | collective-permute-done | bytes 213024 | tf_op jit(solution)/shard_map/ppermute | solution.py:46
  90.4 0.0 collective-permute-done.9.refs_3_
  90.4 1.9 %collective-permute-done.10.got_ref = bf16[4,512,128]{2,1,0:T(8,128)(2,1)S(1)} collective-permute-done((bf16[4,512,128]{2,1,0:T(8,128)(2,1)S(1)}, bf16[4,512,128]{2,1,0:T(8,128)(2,1)S(1)}, u32[]{:S(2)}, u32[]{:S(2)}) %collective-permute-start.10) | collective-permute-done | bytes 524320 | tf_op jit(solution)/shard_map/ppermute | solution.py:46
  92.3 0.7 add_cores.3
  92.9 4.2 %collective-permute-start.11 = (bf16[512,128]{1,0:T(8,128)(2,1)S(1)}, bf16[512,128]{1,0:T(8,128)(2,1)S(1)}, u32[]{:S(2)}, u32[]{:S(2)}) collective-permute-start(bf16[512,128]{1,0:T(8,128)(2,1)S(1)} %get-tuple-element.80), channel_id=1, source_target_pairs={{0,2},{1,3},{2,0},{3,1},{4,6},{5,7},{6,4},{7,5},{8,10},{9,11},{10,... | collective-permute-start | bytes 393224 | tf_op jit(solution)/shard_map/ppermute | solution.py:46
  97.1 1.0 collective-permute-start.12
  98.1 1.5 %collective-permute-start.13 = (bf16[512,128]{1,0:T(8,128)(2,1)S(1)}, bf16[512,128]{1,0:T(8,128)(2,1)S(1)}, u32[]{:S(2)}, u32[]{:S(2)}) collective-permute-start(bf16[512,128]{1,0:T(8,128)(2,1)S(1)} %get-tuple-element.82), channel_id=1, source_target_pairs={{0,6},{1,7},{2,4},{3,5},{4,2},{5,3},{6,0},{7,1},{8,14},{9,15},{10,... | collective-permute-start | bytes 393224 | tf_op jit(solution)/shard_map/ppermute | solution.py:46
  99.6 0.0 collective-permute-start.14
  99.6 1.3 %collective-permute-done.14.other_ref = bf16[4,64,128]{2,1,0:T(8,128)(2,1)S(1)} collective-permute-done((bf16[4,64,128]{2,1,0:T(8,128)(2,1)S(1)}, bf16[4,64,128]{2,1,0:T(8,128)(2,1)S(1)}, u32[]{:S(2)}, u32[]{:S(2)}) %collective-permute-start.14) | collective-permute-done | bytes 65568 | tf_op jit(solution)/shard_map/ppermute | solution.py:46
  100.8 3.3 %class_backward.1 = (f32[1408,512]{1,0:T(8,128)}, f32[128,512]{1,0:T(8,128)}) custom-call(s32[11]{0:T(128)S(1)} %copy-done.9, bf16[1408,512]{1,0:T(8,128)(2,1)S(1)} %bitcast.43, bf16[8,16,768]{2,1,0:T(8,128)(2,1)S(1)} %all-to-all-done.got_ref, bf16[8,16,1152]{2,1,0:T(8,128)(2,1)S(1)} %all-to-all-done.1.got_ref.stats_ref, ...), custom_call_target="tpu_custom_call" | custom-call | flops 184549376 | bytes 2883584 | tf_op jit(solution)/shard_map/class_backward/pallas_call | solution.py:584
  104.1 5.9 %collective-permute-done.12.refs_6_ = bf16[512,128]{1,0:T(8,128)(2,1)S(1)} collective-permute-done((bf16[512,128]{1,0:T(8,128)(2,1)S(1)}, bf16[512,128]{1,0:T(8,128)(2,1)S(1)}, u32[]{:S(2)}, u32[]{:S(2)}) %collective-permute-start.12) | collective-permute-done | bytes 131104 | tf_op jit(solution)/shard_map/ppermute | solution.py:46
  110.0 1.0 finish.1
  (27 shorter events, 0.1 us)
Async XLA Ops:
  0.7 41.5 %copy-start.8 = (s32[11]{0:T(128)}, s32[11]{0:T(128)S(1)}, u32[]{:S(2)}) copy-start(s32[11]{0:T(128)S(1)} %stack.47.where_ref) | copy-start | bytes 136
  0.7 1.4 %copy-start = (bf16[16,196,192]{1,2,0:T(8,128)(2,1)S(1)}, bf16[16,196,192]{1,2,0:T(8,128)(2,1)}, u32[]{:S(2)}) copy-start(bf16[16,196,192]{1,2,0:T(8,128)(2,1)} %param.9) | copy-start | bytes 3612676
  4.0 6.9 %copy-start.3 = (bf16[147,16,128]{2,1,0:T(8,128)(2,1)}, bf16[147,16,128]{2,1,0:T(8,128)(2,1)S(1)}, u32[]{:S(2)}) copy-start(bf16[147,16,128]{2,1,0:T(8,128)(2,1)S(1)} %pack_patches.2.refs_8_.refs_16_) | copy-start | bytes 1806340
  4.0 17.6 %collective-permute-start.3 = (bf16[147,16,128]{2,1,0:T(8,128)(2,1)S(1)}, bf16[147,16,128]{2,1,0:T(8,128)(2,1)}, u32[]{:S(2)}, u32[]{:S(2)}) collective-permute-start(bf16[147,16,128]{2,1,0:T(8,128)(2,1)S(1)} %pack_patches.2.refs_8_.refs_16_), channel_id=1, source_target_pairs={{0,16},{8,24},{16,0},{24,8},{1,17},{9,25},{17,1},{25,9},{2,18},{10... | collective-permute-start | bytes 1806344 | tf_op jit(solution)/shard_map/ppermute | solution.py:46
  8.8 11.8 %copy-start.4 = (bf16[147,16,128]{2,1,0:T(8,128)(2,1)}, bf16[147,16,128]{2,1,0:T(8,128)(2,1)S(1)}, u32[]{:S(2)}) copy-start(bf16[147,16,128]{2,1,0:T(8,128)(2,1)S(1)} %pack_patches.3.refs_7_.refs_15_) | copy-start | bytes 1806340
  8.8 16.7 %collective-permute-start = (bf16[147,16,128]{2,1,0:T(8,128)(2,1)S(1)}, bf16[147,16,128]{2,1,0:T(8,128)(2,1)}, u32[]{:S(2)}, u32[]{:S(2)}) collective-permute-start(bf16[147,16,128]{2,1,0:T(8,128)(2,1)S(1)} %pack_patches.3.refs_7_.refs_15_), channel_id=1, source_target_pairs={{0,8},{8,0},{16,24},{24,16},{1,9},{9,1},{17,25},{25,17},{2,10},{10... | collective-permute-start | bytes 1806344 | tf_op jit(solution)/shard_map/ppermute | solution.py:46
  10.4 39.6 %collective-permute-start.2 = (bf16[147,16,128]{2,1,0:T(8,128)(2,1)S(1)}, bf16[147,16,128]{2,1,0:T(8,128)(2,1)}, u32[]{:S(2)}, u32[]{:S(2)}) collective-permute-start(bf16[147,16,128]{2,1,0:T(8,128)(2,1)S(1)} %pack_patches.3.refs_7_.refs_15_), channel_id=1, source_target_pairs={{0,16},{8,24},{16,0},{24,8},{1,17},{9,25},{17,1},{25,9},{2,18},{10... | collective-permute-start | bytes 1806344 | tf_op jit(solution)/shard_map/ppermute | solution.py:46
  10.9 39.1 %collective-permute-start.1 = (bf16[147,16,128]{2,1,0:T(8,128)(2,1)S(1)}, bf16[147,16,128]{2,1,0:T(8,128)(2,1)}, u32[]{:S(2)}, u32[]{:S(2)}) collective-permute-start(bf16[147,16,128]{2,1,0:T(8,128)(2,1)S(1)} %pack_patches.2.refs_8_.refs_16_), channel_id=1, source_target_pairs={{0,8},{8,0},{16,24},{24,16},{1,9},{9,1},{17,25},{25,17},{2,10},{10... | collective-permute-start | bytes 1806344 | tf_op jit(solution)/shard_map/ppermute | solution.py:46
  25.5 24.5 %collective-permute-start.4 = (bf16[147,16,128]{2,1,0:T(8,128)(2,1)}, bf16[147,16,128]{2,1,0:T(8,128)(2,1)}, u32[]{:S(2)}, u32[]{:S(2)}) collective-permute-start(bf16[147,16,128]{2,1,0:T(8,128)(2,1)} %collective-permute-done.refs_9_.refs_17_), channel_id=1, source_target_pairs={{0,16},{8,24},{16,0},{24,8},{1,17},{9,25},{17,1},{25,9},{2,18},{10... | collective-permute-start | bytes 1806344 | tf_op jit(solution)/shard_map/ppermute | solution.py:46
  25.5 24.5 %collective-permute-start.5 = (bf16[147,16,128]{2,1,0:T(8,128)(2,1)}, bf16[147,16,128]{2,1,0:T(8,128)(2,1)}, u32[]{:S(2)}, u32[]{:S(2)}) collective-permute-start(bf16[147,16,128]{2,1,0:T(8,128)(2,1)} %collective-permute-done.3.refs_12_.refs_20_), channel_id=1, source_target_pairs={{0,8},{8,0},{16,24},{24,16},{1,9},{9,1},{17,25},{25,17},{2,10},{10... | collective-permute-start | bytes 1806344 | tf_op jit(solution)/shard_map/ppermute | solution.py:46
  27.5 14.7 %all-to-all-start = ((bf16[8,16,768]{2,1,0:T(8,128)(2,1)}), bf16[8,16,768]{2,1,0:T(8,128)(2,1)S(1)}, u32[]{:S(2)}, u32[]{:S(2)}) async-start(bf16[8,16,768]{2,1,0:T(8,128)(2,1)} %get-tuple-element.49), calls=%async_computation | async-start | bytes 393216 | tf_op jit(solution)/shard_map/all_to_all | solution.py:50
  32.4 9.8 %copy-start.2 = (bf16[1,1408,512]{2,1,0:T(8,128)(2,1)S(1)}, bf16[1,1408,512]{2,1,0:T(8,128)(2,1)}, u32[]{:S(2)}) copy-start(bf16[1,1408,512]{2,1,0:T(8,128)(2,1)} %param.15) | copy-start | bytes 4325380
  44.9 21.8 %all-to-all-start.1 = ((bf16[8,16,1152]{2,1,0:T(8,128)(2,1)}), bf16[8,16,1152]{2,1,0:T(8,128)(2,1)S(1)}, u32[]{:S(2)}, u32[]{:S(2)}) async-start(bf16[8,16,1152]{2,1,0:T(8,128)(2,1)} %class_logits.1), calls=%async_computation.1 | async-start | bytes 589824 | tf_op jit(solution)/shard_map/all_to_all | solution.py:50
  50.0 16.6 %copy-start.13 = (f32[16,512]{1,0:T(8,128)S(1)}, f32[16,512]{1,0:T(8,128)}, u32[]{:S(2)}) copy-start(f32[16,512]{1,0:T(8,128)} %get-tuple-element.60.aux_pre_ref) | copy-start | bytes 98308
  66.1 2.8 %copy-start.6 = (bf16[4,768,128]{2,1,0:T(8,128)(2,1)S(1)}, bf16[4,768,128]{2,1,0:T(8,128)(2,1)}, u32[]{:S(2)}) copy-start(bf16[4,768,128]{2,1,0:T(8,128)(2,1)} %get-tuple-element.63.keep_ref) | copy-start | bytes 2359300
  66.1 2.8 %copy-start.9 = (s32[11]{0:T(128)S(1)}, s32[11]{0:T(128)}, u32[]{:S(2)}) copy-start(s32[11]{0:T(128)} %copy-done.8) | copy-start | bytes 136
  66.1 2.8 %collective-permute-start.6 = (bf16[4,768,128]{2,1,0:T(8,128)(2,1)}, bf16[4,768,128]{2,1,0:T(8,128)(2,1)}, u32[]{:S(2)}, u32[]{:S(2)}) collective-permute-start(bf16[4,768,128]{2,1,0:T(8,128)(2,1)} %get-tuple-element.64), channel_id=1, source_target_pairs={{0,1},{1,0},{2,3},{3,2},{4,5},{5,4},{6,7},{7,6},{8,9},{9,8},{10,11... | collective-permute-start | bytes 2359304 | tf_op jit(solution)/shard_map/ppermute | solution.py:46
  66.6 8.1 %copy-start.5 = (bf16[1,1024,512]{2,1,0:T(8,128)(2,1)S(1)}, bf16[1,1024,512]{2,1,0:T(8,128)(2,1)}, u32[]{:S(2)}) copy-start(bf16[1,1024,512]{2,1,0:T(8,128)(2,1)} %param.14) | copy-start | bytes 3145732
  66.6 8.1 %copy-start.7 = (bf16[1,256,1024]{2,1,0:T(8,128)(2,1)S(1)}, bf16[1,256,1024]{2,1,0:T(8,128)(2,1)}, u32[]{:S(2)}) copy-start(bf16[1,256,1024]{2,1,0:T(8,128)(2,1)} %param.12) | copy-start | bytes 1572868
  66.7 8.1 %copy-start.10 = (bf16[3136,256]{1,0:T(8,128)(2,1)S(1)}, bf16[3136,256]{1,0:T(8,128)(2,1)}, u32[]{:S(2)}) copy-start(bf16[3136,256]{1,0:T(8,128)(2,1)} %get-tuple-element.70.refs_0_) | copy-start | bytes 4816900
  66.7 8.1 %copy-start.11 = (bf16[3136,256]{1,0:T(8,128)(2,1)S(1)}, bf16[3136,256]{1,0:T(8,128)(2,1)}, u32[]{:S(2)}) copy-start(bf16[3136,256]{1,0:T(8,128)(2,1)} %get-tuple-element.71.refs_1_) | copy-start | bytes 4816900
  66.7 8.1 %copy-start.12 = (bf16[3136,256]{1,0:T(8,128)(2,1)S(1)}, bf16[3136,256]{1,0:T(8,128)(2,1)}, u32[]{:S(2)}) copy-start(bf16[3136,256]{1,0:T(8,128)(2,1)} %get-tuple-element.72.refs_2_) | copy-start | bytes 4816900
  67.0 7.8 %copy-start.1 = (bf16[1,1024,768]{2,1,0:T(8,128)(2,1)S(1)}, bf16[1,1024,768]{2,1,0:T(8,128)(2,1)}, u32[]{:S(2)}) copy-start(bf16[1,1024,768]{2,1,0:T(8,128)(2,1)} %param.13) | copy-start | bytes 4718596
  70.3 18.8 %collective-permute-start.7 = (bf16[832,128]{1,0:T(8,128)(2,1)S(1)}, bf16[832,128]{1,0:T(8,128)(2,1)S(1)}, u32[]{:S(2)}, u32[]{:S(2)}) collective-permute-start(bf16[832,128]{1,0:T(8,128)(2,1)S(1)} %get-tuple-element.67), channel_id=1, source_target_pairs={{0,2},{1,3},{2,0},{3,1},{4,6},{5,7},{6,4},{7,5},{8,10},{9,11},{10,... | collective-permute-start | bytes 638984 | tf_op jit(solution)/shard_map/ppermute | solution.py:46
  72.2 18.2 %collective-permute-start.8 = (bf16[832,128]{1,0:T(8,128)(2,1)S(1)}, bf16[832,128]{1,0:T(8,128)(2,1)S(1)}, u32[]{:S(2)}, u32[]{:S(2)}) collective-permute-start(bf16[832,128]{1,0:T(8,128)(2,1)S(1)} %get-tuple-element.68), channel_id=1, source_target_pairs={{0,4},{1,5},{2,6},{3,7},{4,0},{5,1},{6,2},{7,3},{8,12},{9,13},{10,... | collective-permute-start | bytes 638984 | tf_op jit(solution)/shard_map/ppermute | solution.py:46
  74.6 15.8 %collective-permute-start.9 = (bf16[832,128]{1,0:T(8,128)(2,1)S(1)}, bf16[832,128]{1,0:T(8,128)(2,1)S(1)}, u32[]{:S(2)}, u32[]{:S(2)}) collective-permute-start(bf16[832,128]{1,0:T(8,128)(2,1)S(1)} %get-tuple-element.69), channel_id=1, source_target_pairs={{0,6},{1,7},{2,4},{3,5},{4,2},{5,3},{6,0},{7,1},{8,14},{9,15},{10,... | collective-permute-start | bytes 638984 | tf_op jit(solution)/shard_map/ppermute | solution.py:46
  90.4 1.9 %collective-permute-start.10 = (bf16[4,512,128]{2,1,0:T(8,128)(2,1)S(1)}, bf16[4,512,128]{2,1,0:T(8,128)(2,1)S(1)}, u32[]{:S(2)}, u32[]{:S(2)}) collective-permute-start(bf16[4,512,128]{2,1,0:T(8,128)(2,1)S(1)} %get-tuple-element.78), channel_id=1, source_target_pairs={{0,1},{1,0},{2,3},{3,2},{4,5},{5,4},{6,7},{7,6},{8,9},{9,8},{10,11... | collective-permute-start | bytes 1572872 | tf_op jit(solution)/shard_map/ppermute | solution.py:46
  92.9 11.2 %collective-permute-start.11 = (bf16[512,128]{1,0:T(8,128)(2,1)S(1)}, bf16[512,128]{1,0:T(8,128)(2,1)S(1)}, u32[]{:S(2)}, u32[]{:S(2)}) collective-permute-start(bf16[512,128]{1,0:T(8,128)(2,1)S(1)} %get-tuple-element.80), channel_id=1, source_target_pairs={{0,2},{1,3},{2,0},{3,1},{4,6},{5,7},{6,4},{7,5},{8,10},{9,11},{10,... | collective-permute-start | bytes 393224 | tf_op jit(solution)/shard_map/ppermute | solution.py:46
  97.1 12.9 %collective-permute-start.12 = (bf16[512,128]{1,0:T(8,128)(2,1)S(1)}, bf16[512,128]{1,0:T(8,128)(2,1)S(1)}, u32[]{:S(2)}, u32[]{:S(2)}) collective-permute-start(bf16[512,128]{1,0:T(8,128)(2,1)S(1)} %get-tuple-element.81), channel_id=1, source_target_pairs={{0,4},{1,5},{2,6},{3,7},{4,0},{5,1},{6,2},{7,3},{8,12},{9,13},{10,... | collective-permute-start | bytes 393224 | tf_op jit(solution)/shard_map/ppermute | solution.py:46
  98.1 11.9 %collective-permute-start.13 = (bf16[512,128]{1,0:T(8,128)(2,1)S(1)}, bf16[512,128]{1,0:T(8,128)(2,1)S(1)}, u32[]{:S(2)}, u32[]{:S(2)}) collective-permute-start(bf16[512,128]{1,0:T(8,128)(2,1)S(1)} %get-tuple-element.82), channel_id=1, source_target_pairs={{0,6},{1,7},{2,4},{3,5},{4,2},{5,3},{6,0},{7,1},{8,14},{9,15},{10,... | collective-permute-start | bytes 393224 | tf_op jit(solution)/shard_map/ppermute | solution.py:46
  99.6 1.3 %collective-permute-start.14 = (bf16[4,64,128]{2,1,0:T(8,128)(2,1)S(1)}, bf16[4,64,128]{2,1,0:T(8,128)(2,1)S(1)}, u32[]{:S(2)}, u32[]{:S(2)}) collective-permute-start(bf16[4,64,128]{2,1,0:T(8,128)(2,1)S(1)} %get-tuple-element.86.mine_ref), channel_id=1, source_target_pairs={{0,1},{1,0},{2,3},{3,2},{4,5},{5,4},{6,7},{7,6},{8,9},{9,8},{10,11... | collective-permute-start | bytes 196616 | tf_op jit(solution)/shard_map/ppermute | solution.py:46

commit v15 on v14

--- a/solution.py
+++ b/solution.py
@@ -322,15 +322,13 @@
     def body(g):
         here = slice(g * size, (g + 1) * size)
         lay_target(g, where_ref, patch_refs, target)
-        if g:
-            contract(g - 1, rows, [(total, grads, feature)])
         for j, grad_ref in enumerate(grad_refs):
             cut = slice(j * TILE, (j + 1) * TILE)
             grad = ((recon_refs[j][...] - target[:, :, cut].reshape(size, TILE).astype(F32)) * scale).astype(BF16)
             grad_ref[...] = grad
             grads[here, cut] = grad
+        contract(g, rows, [(total, grads, feature)])
         if g == STEPS - 1:
-            contract(g, rows, [(total, grads, feature)])
             deal(where_ref, [total], width // groups, keep_ref, send_ref)
 
     by_step(copies_of(feature_refs, feature, sems), body)

time: 112 us -> 111 us (level)
  no operation moved by 1% of the time
where the time goes in v15:
time: 111 us; the launch traced here: 110 us
  Pallas kernels  61.8 us (56%)
  starting transfers between devices  28.8 us (26%)
  waiting for transfers between devices  17 us (15%)
  local copies, waits for them, and re-layouts  1.55 us (1%)
    ppermute x15, starting transfers between devices, swap(): return lax.ppermute(value, axis, [(i, i ^ bits) for i in range(count)])  18.8 us
    ppermute x15, waiting for transfers between devices, swap(): return lax.ppermute(value, axis, [(i, i ^ bits) for i in range(count)])  17 us
    pallas_call x1, Pallas kernels, residual(): call(functools.partial(residual_kernel, groups, scale, len(feature), n_ti...  15 us
    pallas_call x1, Pallas kernels, backward(): call(functools.partial(backward_kernel, groups, len(grad), n_decode), [sh...  14.3 us
    all_to_all x2, starting transfers between devices, exchange(): lax.all_to_all(value, 'dp', 0, 0, axis_index_groups=groups, tiled=True)  9.98 us
    pallas_call x1, Pallas kernels, reconstruct(): call(functools.partial(recon_kernel, len(feature), n_tiles), [shape((rows...  9.77 us
    pallas_call x1, Pallas kernels, forward(): call(functools.partial(forward_kernel, n_tiles, pix), [shape((pix * image...  9.66 us
    pallas_call x2, Pallas kernels, pack(): call(functools.partial(pack_kernel, h * half), shape(dims, BF16), limit=2...  3.62 us
  transfers between devices with their start and end apart: 17, of which 7 were waited for; matrix products, arithmetic and copies ran while one was open for 0% of the time, Pallas kernels for 52%

profile of v15, /device:TPU:0, one launch (start us, length us, event | category | flops | bytes accessed | tf_op | source)
XLA Modules:
  0.0 110.0 jit_solution(8768713443942501588)
XLA Ops:
  0.7 0.1 stack.47.where_ref
  0.7 0.0 copy-start
  0.8 1.4 %copy-done = bf16[16,196,192]{1,2,0:T(8,128)(2,1)S(1)} copy-done((bf16[16,196,192]{1,2,0:T(8,128)(2,1)S(1)}, bf16[16,196,192]{1,2,0:T(8,128)(2,1)}, u32[]{:S(2)}) %copy-start) | copy-done | bytes 1204248
  2.2 1.8 %pack_patches.2.refs_8_.refs_16_ = bf16[147,16,128]{2,1,0:T(8,128)(2,1)S(1)} custom-call(s32[11]{0:T(128)S(1)} %stack.47.where_ref, bf16[16,192,196]{2,1,0:T(8,128)(2,1)S(1)} %bitcast.27, bf16[16,192,196]{2,1,0:T(8,128)(2,1)S(1)} %bitcast.28, bf16[16,192,196]{2,1,0:T(8,128)(2,1)S(1)} %bitcast.29, bf16[16,192,196]{2,1,0:T(8,128)(2,1)S(1)} %bitcast.30), custom_call_target="tpu_custom_call" | custom-call | tf_op jit(solution)/shard_map/pack_patches/pallas_call | solution.py:99
  4.0 3.0 %collective-permute-start.3 = (bf16[147,16,128]{2,1,0:T(8,128)(2,1)S(1)}, bf16[147,16,128]{2,1,0:T(8,128)(2,1)}, u32[]{:S(2)}, u32[]{:S(2)}) collective-permute-start(bf16[147,16,128]{2,1,0:T(8,128)(2,1)S(1)} %pack_patches.2.refs_8_.refs_16_), channel_id=1, source_target_pairs={{0,16},{8,24},{16,0},{24,8},{1,17},{9,25},{17,1},{25,9},{2,18},{10... | collective-permute-start | bytes 1806344 | tf_op jit(solution)/shard_map/ppermute | solution.py:46
  7.0 1.8 %pack_patches.3.refs_7_.refs_15_ = bf16[147,16,128]{2,1,0:T(8,128)(2,1)S(1)} custom-call(s32[11]{0:T(128)S(1)} %stack.47.where_ref, bf16[16,192,196]{2,1,0:T(8,128)(2,1)S(1)} %bitcast.31, bf16[16,192,196]{2,1,0:T(8,128)(2,1)S(1)} %bitcast.32, bf16[16,192,196]{2,1,0:T(8,128)(2,1)S(1)} %bitcast.33, bf16[16,192,196]{2,1,0:T(8,128)(2,1)S(1)} %bitcast.34), custom_call_target="tpu_custom_call" | custom-call | tf_op jit(solution)/shard_map/pack_patches/pallas_call | solution.py:99
  8.8 1.6 %collective-permute-start = (bf16[147,16,128]{2,1,0:T(8,128)(2,1)S(1)}, bf16[147,16,128]{2,1,0:T(8,128)(2,1)}, u32[]{:S(2)}, u32[]{:S(2)}) collective-permute-start(bf16[147,16,128]{2,1,0:T(8,128)(2,1)S(1)} %pack_patches.3.refs_7_.refs_15_), channel_id=1, source_target_pairs={{0,8},{8,0},{16,24},{24,16},{1,9},{9,1},{17,25},{25,17},{2,10},{10... | collective-permute-start | bytes 1806344 | tf_op jit(solution)/shard_map/ppermute | solution.py:46
  10.4 0.5 collective-permute-start.2
  10.9 0.1 collective-permute-start.1
  11.0 9.7 %forward.1 = (bf16[3136,256]{1,0:T(8,128)(2,1)}, bf16[3136,256]{1,0:T(8,128)(2,1)}, bf16[3136,256]{1,0:T(8,128)(2,1)}, bf16[3136,256]{1,0:T(8,128)(2,1)}, bf16[3...) custom-call(bf16[196,16,1024]{2,1,0:T(8,128)(2,1)} %bitcast.48, ...), custom_call_target="tpu_custom_call" | custom-call | tf_op jit(solution)/shard_map/forward/pallas_call | solution.py:171
  20.7 0.9 collective-permute-done.3.refs_12_.refs_20_
  21.5 4.0 %collective-permute-done.refs_9_.refs_17_ = bf16[147,16,128]{2,1,0:T(8,128)(2,1)} collective-permute-done((bf16[147,16,128]{2,1,0:T(8,128)(2,1)S(1)}, bf16[147,16,128]{2,1,0:T(8,128)(2,1)}, u32[]{:S(2)}, u32[]{:S(2)}) %collective-permute-start) | collective-permute-done | bytes 602144 | tf_op jit(solution)/shard_map/ppermute | solution.py:46
  25.5 0.0 collective-permute-start.4
  25.5 2.0 %collective-permute-start.5 = (bf16[147,16,128]{2,1,0:T(8,128)(2,1)}, bf16[147,16,128]{2,1,0:T(8,128)(2,1)}, u32[]{:S(2)}, u32[]{:S(2)}) collective-permute-start(bf16[147,16,128]{2,1,0:T(8,128)(2,1)} %collective-permute-done.3.refs_12_.refs_20_), channel_id=1, source_target_pairs={{0,8},{8,0},{16,24},{24,16},{1,9},{9,1},{17,25},{25,17},{2,10},{10... | collective-permute-start | bytes 1806344 | tf_op jit(solution)/shard_map/ppermute | solution.py:46
  27.5 4.9 %all-to-all-start = ((bf16[8,16,768]{2,1,0:T(8,128)(2,1)}), bf16[8,16,768]{2,1,0:T(8,128)(2,1)S(1)}, u32[]{:S(2)}, u32[]{:S(2)}) async-start(bf16[8,16,768]{2,1,0:T(8,128)(2,1)} %get-tuple-element.49), calls=%async_computation | async-start | bytes 393216 | tf_op jit(solution)/shard_map/all_to_all | solution.py:50
  32.4 9.8 %reconstruct.1 = (f32[3136,256]{1,0:T(8,128)}, f32[3136,256]{1,0:T(8,128)}, f32[3136,256]{1,0:T(8,128)}) custom-call(bf16[3136,256]{1,0:T(8,128)(2,1)} %get-tuple-element.51.refs_0_, bf16[3136,256]{1,0:T(8,128)(2,1)} %get-tuple-element.52.refs_1_, bf16[3136,256]{1,0:T(8,128)(2,1)} %get-tuple-element.53.refs_2_, bf16[3136,256]{1,0:T(8,128)(2,1)} %get-tuple-element.54.refs_3_, ...), custom_call_target="tpu_custom_call" | custom-call | tf_op jit(solution)/shard_map/reconstruct/pallas_call | solution.py:211
  42.2 0.0 all-to-all-done.got_ref
  42.2 2.7 %class_logits.1 = bf16[8,16,1152]{2,1,0:T(8,128)(2,1)} custom-call(s32[11]{0:T(128)S(1)} %stack.47.where_ref, bf16[8,16,768]{2,1,0:T(8,128)(2,1)S(1)} %all-to-all-done.got_ref, bf16[1408,512]{1,0:T(8,128)(2,1)S(1)} %bitcast.42), custom_call_target="tpu_custom_call" | custom-call | tf_op jit(solution)/shard_map/class_logits/pallas_call | solution.py:512
  44.9 5.1 %all-to-all-start.1 = ((bf16[8,16,1152]{2,1,0:T(8,128)(2,1)}), bf16[8,16,1152]{2,1,0:T(8,128)(2,1)S(1)}, u32[]{:S(2)}, u32[]{:S(2)}) async-start(bf16[8,16,1152]{2,1,0:T(8,128)(2,1)} %class_logits.1), calls=%async_computation.1 | async-start | bytes 589824 | tf_op jit(solution)/shard_map/all_to_all | solution.py:50
  50.0 0.0 collective-permute-done.2.refs_11_.refs_19_
  50.0 0.0 collective-permute-done.1.refs_10_.refs_18_
  50.0 0.0 collective-permute-done.4.refs_13_.refs_21_
  50.0 0.0 collective-permute-done.5.refs_14_.refs_22_
  50.0 0.0 copy-start.13
  50.0 15.0 %residual.1 = (bf16[3136,256]{1,0:T(8,128)(2,1)}, bf16[3136,256]{1,0:T(8,128)(2,1)}, bf16[3136,256]{1,0:T(8,128)(2,1)}, bf16[4,768,128]{2,1,0:T(8,128)(2,1)}, bf16[4,768,128]{2,1,0:T(8,128)(2,1)}) custom-call(s32[11]{0:T(128)} %copy-done.8, bf16[3136,256]{1,0:T(8,128)(2,1)} %get-tuple-element.51.refs_0_, bf16[3136,256]{1,0:T(8,128)(2,1)} %get-tuple-element.52.refs_1_, ...), custom_call_target="tpu_custom_call" | custom-call | flops 4932501504 | bytes 20873216 | tf_op jit(solution)/shard_map/residual/pallas_call | solution.py:345
  65.1 0.0 copy-start.9
  65.1 0.6 collective-permute-start.6
  65.7 0.0 all-to-all-done.1.got_ref.stats_ref
  65.7 0.3 aux_backward.1
  66.0 1.9 %collective-permute-done.6.got_ref = bf16[4,768,128]{2,1,0:T(8,128)(2,1)} collective-permute-done((bf16[4,768,128]{2,1,0:T(8,128)(2,1)}, bf16[4,768,128]{2,1,0:T(8,128)(2,1)}, u32[]{:S(2)}, u32[]{:S(2)}) %collective-permute-start.6) | collective-permute-done | bytes 786464 | tf_op jit(solution)/shard_map/ppermute | solution.py:46
  67.9 1.4 %add_cores.2 = (bf16[832,128]{1,0:T(8,128)(2,1)S(1)}, bf16[832,128]{1,0:T(8,128)(2,1)S(1)}, bf16[832,128]{1,0:T(8,128)(2,1)S(1)}, bf16[832,128]{1,0:T(8,128)(2,1)S(1)}) custom-call(s32[11]{0:T(128)S(1)} %copy-done.9, bf16[4,768,128]{2,1,0:T(8,128)(2,1)S(1)} %copy-done.6, bf16[4,768,128]{2,1,0:T(8,128)(2,1)} %collective-permute-done.6.got_ref, ...), custom_call_target="tpu_custom_call" | custom-call | tf_op jit(solution)/shard_map/add_cores/pallas_call | solution.py:622
  69.3 1.9 %collective-permute-start.7 = (bf16[832,128]{1,0:T(8,128)(2,1)S(1)}, bf16[832,128]{1,0:T(8,128)(2,1)S(1)}, u32[]{:S(2)}, u32[]{:S(2)}) collective-permute-start(bf16[832,128]{1,0:T(8,128)(2,1)S(1)} %get-tuple-element.67), channel_id=1, source_target_pairs={{0,2},{1,3},{2,0},{3,1},{4,6},{5,7},{6,4},{7,5},{8,10},{9,11},{10,... | collective-permute-start | bytes 638984 | tf_op jit(solution)/shard_map/ppermute | solution.py:46
  71.2 2.4 %collective-permute-start.8 = (bf16[832,128]{1,0:T(8,128)(2,1)S(1)}, bf16[832,128]{1,0:T(8,128)(2,1)S(1)}, u32[]{:S(2)}, u32[]{:S(2)}) collective-permute-start(bf16[832,128]{1,0:T(8,128)(2,1)S(1)} %get-tuple-element.68), channel_id=1, source_target_pairs={{0,4},{1,5},{2,6},{3,7},{4,0},{5,1},{6,2},{7,3},{8,12},{9,13},{10,... | collective-permute-start | bytes 638984 | tf_op jit(solution)/shard_map/ppermute | solution.py:46
  73.6 0.2 collective-permute-start.9
  73.8 14.3 %backward.1 = (bf16[4,512,128]{2,1,0:T(8,128)(2,1)S(1)}, bf16[4,512,128]{2,1,0:T(8,128)(2,1)S(1)}) custom-call(s32[11]{0:T(128)S(1)} %copy-done.9, bf16[3136,256]{1,0:T(8,128)(2,1)S(1)} %copy-done.10, bf16[3136,256]{1,0:T(8,128)(2,1)S(1)} %copy-done.11, bf16[3136,256]{1,0:T(8,128)(2,1)S(1)} %copy-done.12, bf16[1024,768]{1,0:T(8,128)(2,1)S(1)} %bitcast.38, ...), custom_call_target="tpu_custom_call" | custom-call | flops 9865003008 | bytes 12845056 | tf_op jit(solution)/shard_map/backward/pallas_call | solution.py:424
  88.2 1.2 %collective-permute-done.8.refs_2_ = bf16[832,128]{1,0:T(8,128)(2,1)S(1)} collective-permute-done((bf16[832,128]{1,0:T(8,128)(2,1)S(1)}, bf16[832,128]{1,0:T(8,128)(2,1)S(1)}, u32[]{:S(2)}, u32[]{:S(2)}) %collective-permute-start.8) | collective-permute-done | bytes 213024 | tf_op jit(solution)/shard_map/ppermute | solution.py:46
  89.4 1.9 %collective-permute-done.10.got_ref = bf16[4,512,128]{2,1,0:T(8,128)(2,1)S(1)} collective-permute-done((bf16[4,512,128]{2,1,0:T(8,128)(2,1)S(1)}, bf16[4,512,128]{2,1,0:T(8,128)(2,1)S(1)}, u32[]{:S(2)}, u32[]{:S(2)}) %collective-permute-start.10) | collective-permute-done | bytes 524320 | tf_op jit(solution)/shard_map/ppermute | solution.py:46
  91.3 0.7 add_cores.3
  92.0 4.2 %collective-permute-start.11 = (bf16[512,128]{1,0:T(8,128)(2,1)S(1)}, bf16[512,128]{1,0:T(8,128)(2,1)S(1)}, u32[]{:S(2)}, u32[]{:S(2)}) collective-permute-start(bf16[512,128]{1,0:T(8,128)(2,1)S(1)} %get-tuple-element.80), channel_id=1, source_target_pairs={{0,2},{1,3},{2,0},{3,1},{4,6},{5,7},{6,4},{7,5},{8,10},{9,11},{10,... | collective-permute-start | bytes 393224 | tf_op jit(solution)/shard_map/ppermute | solution.py:46
  96.2 1.0 collective-permute-start.12
  97.1 1.5 %collective-permute-start.13 = (bf16[512,128]{1,0:T(8,128)(2,1)S(1)}, bf16[512,128]{1,0:T(8,128)(2,1)S(1)}, u32[]{:S(2)}, u32[]{:S(2)}) collective-permute-start(bf16[512,128]{1,0:T(8,128)(2,1)S(1)} %get-tuple-element.82), channel_id=1, source_target_pairs={{0,6},{1,7},{2,4},{3,5},{4,2},{5,3},{6,0},{7,1},{8,14},{9,15},{10,... | collective-permute-start | bytes 393224 | tf_op jit(solution)/shard_map/ppermute | solution.py:46
  98.6 0.0 collective-permute-start.14
  98.6 1.3 %collective-permute-done.14.other_ref = bf16[4,64,128]{2,1,0:T(8,128)(2,1)S(1)} collective-permute-done((bf16[4,64,128]{2,1,0:T(8,128)(2,1)S(1)}, bf16[4,64,128]{2,1,0:T(8,128)(2,1)S(1)}, u32[]{:S(2)}, u32[]{:S(2)}) %collective-permute-start.14) | collective-permute-done | bytes 65568 | tf_op jit(solution)/shard_map/ppermute | solution.py:46
  99.8 3.3 %class_backward.1 = (f32[1408,512]{1,0:T(8,128)}, f32[128,512]{1,0:T(8,128)}) custom-call(s32[11]{0:T(128)S(1)} %copy-done.9, bf16[1408,512]{1,0:T(8,128)(2,1)S(1)} %bitcast.43, bf16[8,16,768]{2,1,0:T(8,128)(2,1)S(1)} %all-to-all-done.got_ref, bf16[8,16,1152]{2,1,0:T(8,128)(2,1)S(1)} %all-to-all-done.1.got_ref.stats_ref, ...), custom_call_target="tpu_custom_call" | custom-call | flops 184549376 | bytes 2883584 | tf_op jit(solution)/shard_map/class_backward/pallas_call | solution.py:582
  103.2 0.0 collective-permute-done.11.refs_5_
  103.2 5.9 %collective-permute-done.12.refs_6_ = bf16[512,128]{1,0:T(8,128)(2,1)S(1)} collective-permute-done((bf16[512,128]{1,0:T(8,128)(2,1)S(1)}, bf16[512,128]{1,0:T(8,128)(2,1)S(1)}, u32[]{:S(2)}, u32[]{:S(2)}) %collective-permute-start.12) | collective-permute-done | bytes 131104 | tf_op jit(solution)/shard_map/ppermute | solution.py:46
  109.1 0.0 collective-permute-done.13.refs_7_
  109.1 1.0 finish.1
  (27 shorter events, 0.1 us)
Async XLA Ops:
  0.7 41.5 %copy-start.8 = (s32[11]{0:T(128)}, s32[11]{0:T(128)S(1)}, u32[]{:S(2)}) copy-start(s32[11]{0:T(128)S(1)} %stack.47.where_ref) | copy-start | bytes 136
  0.7 1.4 %copy-start = (bf16[16,196,192]{1,2,0:T(8,128)(2,1)S(1)}, bf16[16,196,192]{1,2,0:T(8,128)(2,1)}, u32[]{:S(2)}) copy-start(bf16[16,196,192]{1,2,0:T(8,128)(2,1)} %param.9) | copy-start | bytes 3612676
  4.0 6.9 %copy-start.3 = (bf16[147,16,128]{2,1,0:T(8,128)(2,1)}, bf16[147,16,128]{2,1,0:T(8,128)(2,1)S(1)}, u32[]{:S(2)}) copy-start(bf16[147,16,128]{2,1,0:T(8,128)(2,1)S(1)} %pack_patches.2.refs_8_.refs_16_) | copy-start | bytes 1806340
  4.0 17.6 %collective-permute-start.3 = (bf16[147,16,128]{2,1,0:T(8,128)(2,1)S(1)}, bf16[147,16,128]{2,1,0:T(8,128)(2,1)}, u32[]{:S(2)}, u32[]{:S(2)}) collective-permute-start(bf16[147,16,128]{2,1,0:T(8,128)(2,1)S(1)} %pack_patches.2.refs_8_.refs_16_), channel_id=1, source_target_pairs={{0,16},{8,24},{16,0},{24,8},{1,17},{9,25},{17,1},{25,9},{2,18},{10... | collective-permute-start | bytes 1806344 | tf_op jit(solution)/shard_map/ppermute | solution.py:46
  8.8 11.8 %copy-start.4 = (bf16[147,16,128]{2,1,0:T(8,128)(2,1)}, bf16[147,16,128]{2,1,0:T(8,128)(2,1)S(1)}, u32[]{:S(2)}) copy-start(bf16[147,16,128]{2,1,0:T(8,128)(2,1)S(1)} %pack_patches.3.refs_7_.refs_15_) | copy-start | bytes 1806340
  8.8 16.7 %collective-permute-start = (bf16[147,16,128]{2,1,0:T(8,128)(2,1)S(1)}, bf16[147,16,128]{2,1,0:T(8,128)(2,1)}, u32[]{:S(2)}, u32[]{:S(2)}) collective-permute-start(bf16[147,16,128]{2,1,0:T(8,128)(2,1)S(1)} %pack_patches.3.refs_7_.refs_15_), channel_id=1, source_target_pairs={{0,8},{8,0},{16,24},{24,16},{1,9},{9,1},{17,25},{25,17},{2,10},{10... | collective-permute-start | bytes 1806344 | tf_op jit(solution)/shard_map/ppermute | solution.py:46
  10.4 39.6 %collective-permute-start.2 = (bf16[147,16,128]{2,1,0:T(8,128)(2,1)S(1)}, bf16[147,16,128]{2,1,0:T(8,128)(2,1)}, u32[]{:S(2)}, u32[]{:S(2)}) collective-permute-start(bf16[147,16,128]{2,1,0:T(8,128)(2,1)S(1)} %pack_patches.3.refs_7_.refs_15_), channel_id=1, source_target_pairs={{0,16},{8,24},{16,0},{24,8},{1,17},{9,25},{17,1},{25,9},{2,18},{10... | collective-permute-start | bytes 1806344 | tf_op jit(solution)/shard_map/ppermute | solution.py:46
  10.9 39.1 %collective-permute-start.1 = (bf16[147,16,128]{2,1,0:T(8,128)(2,1)S(1)}, bf16[147,16,128]{2,1,0:T(8,128)(2,1)}, u32[]{:S(2)}, u32[]{:S(2)}) collective-permute-start(bf16[147,16,128]{2,1,0:T(8,128)(2,1)S(1)} %pack_patches.2.refs_8_.refs_16_), channel_id=1, source_target_pairs={{0,8},{8,0},{16,24},{24,16},{1,9},{9,1},{17,25},{25,17},{2,10},{10... | collective-permute-start | bytes 1806344 | tf_op jit(solution)/shard_map/ppermute | solution.py:46
  25.5 24.5 %collective-permute-start.4 = (bf16[147,16,128]{2,1,0:T(8,128)(2,1)}, bf16[147,16,128]{2,1,0:T(8,128)(2,1)}, u32[]{:S(2)}, u32[]{:S(2)}) collective-permute-start(bf16[147,16,128]{2,1,0:T(8,128)(2,1)} %collective-permute-done.refs_9_.refs_17_), channel_id=1, source_target_pairs={{0,16},{8,24},{16,0},{24,8},{1,17},{9,25},{17,1},{25,9},{2,18},{10... | collective-permute-start | bytes 1806344 | tf_op jit(solution)/shard_map/ppermute | solution.py:46
  25.5 24.5 %collective-permute-start.5 = (bf16[147,16,128]{2,1,0:T(8,128)(2,1)}, bf16[147,16,128]{2,1,0:T(8,128)(2,1)}, u32[]{:S(2)}, u32[]{:S(2)}) collective-permute-start(bf16[147,16,128]{2,1,0:T(8,128)(2,1)} %collective-permute-done.3.refs_12_.refs_20_), channel_id=1, source_target_pairs={{0,8},{8,0},{16,24},{24,16},{1,9},{9,1},{17,25},{25,17},{2,10},{10... | collective-permute-start | bytes 1806344 | tf_op jit(solution)/shard_map/ppermute | solution.py:46
  27.5 14.7 %all-to-all-start = ((bf16[8,16,768]{2,1,0:T(8,128)(2,1)}), bf16[8,16,768]{2,1,0:T(8,128)(2,1)S(1)}, u32[]{:S(2)}, u32[]{:S(2)}) async-start(bf16[8,16,768]{2,1,0:T(8,128)(2,1)} %get-tuple-element.49), calls=%async_computation | async-start | bytes 393216 | tf_op jit(solution)/shard_map/all_to_all | solution.py:50
  32.4 9.8 %copy-start.2 = (bf16[1,1408,512]{2,1,0:T(8,128)(2,1)S(1)}, bf16[1,1408,512]{2,1,0:T(8,128)(2,1)}, u32[]{:S(2)}) copy-start(bf16[1,1408,512]{2,1,0:T(8,128)(2,1)} %param.15) | copy-start | bytes 4325380
  44.9 20.8 %all-to-all-start.1 = ((bf16[8,16,1152]{2,1,0:T(8,128)(2,1)}), bf16[8,16,1152]{2,1,0:T(8,128)(2,1)S(1)}, u32[]{:S(2)}, u32[]{:S(2)}) async-start(bf16[8,16,1152]{2,1,0:T(8,128)(2,1)} %class_logits.1), calls=%async_computation.1 | async-start | bytes 589824 | tf_op jit(solution)/shard_map/all_to_all | solution.py:50
  50.0 15.6 %copy-start.13 = (f32[16,512]{1,0:T(8,128)S(1)}, f32[16,512]{1,0:T(8,128)}, u32[]{:S(2)}) copy-start(f32[16,512]{1,0:T(8,128)} %get-tuple-element.60.aux_pre_ref) | copy-start | bytes 98308
  65.1 2.8 %copy-start.6 = (bf16[4,768,128]{2,1,0:T(8,128)(2,1)S(1)}, bf16[4,768,128]{2,1,0:T(8,128)(2,1)}, u32[]{:S(2)}) copy-start(bf16[4,768,128]{2,1,0:T(8,128)(2,1)} %get-tuple-element.63.keep_ref) | copy-start | bytes 2359300
  65.1 2.8 %copy-start.9 = (s32[11]{0:T(128)S(1)}, s32[11]{0:T(128)}, u32[]{:S(2)}) copy-start(s32[11]{0:T(128)} %copy-done.8) | copy-start | bytes 136
  65.1 2.8 %collective-permute-start.6 = (bf16[4,768,128]{2,1,0:T(8,128)(2,1)}, bf16[4,768,128]{2,1,0:T(8,128)(2,1)}, u32[]{:S(2)}, u32[]{:S(2)}) collective-permute-start(bf16[4,768,128]{2,1,0:T(8,128)(2,1)} %get-tuple-element.64), channel_id=1, source_target_pairs={{0,1},{1,0},{2,3},{3,2},{4,5},{5,4},{6,7},{7,6},{8,9},{9,8},{10,11... | collective-permute-start | bytes 2359304 | tf_op jit(solution)/shard_map/ppermute | solution.py:46
  65.7 8.1 %copy-start.5 = (bf16[1,1024,512]{2,1,0:T(8,128)(2,1)S(1)}, bf16[1,1024,512]{2,1,0:T(8,128)(2,1)}, u32[]{:S(2)}) copy-start(bf16[1,1024,512]{2,1,0:T(8,128)(2,1)} %param.14) | copy-start | bytes 3145732
  65.7 8.1 %copy-start.7 = (bf16[1,256,1024]{2,1,0:T(8,128)(2,1)S(1)}, bf16[1,256,1024]{2,1,0:T(8,128)(2,1)}, u32[]{:S(2)}) copy-start(bf16[1,256,1024]{2,1,0:T(8,128)(2,1)} %param.12) | copy-start | bytes 1572868
  65.7 8.1 %copy-start.10 = (bf16[3136,256]{1,0:T(8,128)(2,1)S(1)}, bf16[3136,256]{1,0:T(8,128)(2,1)}, u32[]{:S(2)}) copy-start(bf16[3136,256]{1,0:T(8,128)(2,1)} %get-tuple-element.70.refs_0_) | copy-start | bytes 4816900
  65.7 8.1 %copy-start.11 = (bf16[3136,256]{1,0:T(8,128)(2,1)S(1)}, bf16[3136,256]{1,0:T(8,128)(2,1)}, u32[]{:S(2)}) copy-start(bf16[3136,256]{1,0:T(8,128)(2,1)} %get-tuple-element.71.refs_1_) | copy-start | bytes 4816900
  65.7 8.1 %copy-start.12 = (bf16[3136,256]{1,0:T(8,128)(2,1)S(1)}, bf16[3136,256]{1,0:T(8,128)(2,1)}, u32[]{:S(2)}) copy-start(bf16[3136,256]{1,0:T(8,128)(2,1)} %get-tuple-element.72.refs_2_) | copy-start | bytes 4816900
  66.0 7.8 %copy-start.1 = (bf16[1,1024,768]{2,1,0:T(8,128)(2,1)S(1)}, bf16[1,1024,768]{2,1,0:T(8,128)(2,1)}, u32[]{:S(2)}) copy-start(bf16[1,1024,768]{2,1,0:T(8,128)(2,1)} %param.13) | copy-start | bytes 4718596
  69.3 18.8 %collective-permute-start.7 = (bf16[832,128]{1,0:T(8,128)(2,1)S(1)}, bf16[832,128]{1,0:T(8,128)(2,1)S(1)}, u32[]{:S(2)}, u32[]{:S(2)}) collective-permute-start(bf16[832,128]{1,0:T(8,128)(2,1)S(1)} %get-tuple-element.67), channel_id=1, source_target_pairs={{0,2},{1,3},{2,0},{3,1},{4,6},{5,7},{6,4},{7,5},{8,10},{9,11},{10,... | collective-permute-start | bytes 638984 | tf_op jit(solution)/shard_map/ppermute | solution.py:46
  71.2 18.2 %collective-permute-start.8 = (bf16[832,128]{1,0:T(8,128)(2,1)S(1)}, bf16[832,128]{1,0:T(8,128)(2,1)S(1)}, u32[]{:S(2)}, u32[]{:S(2)}) collective-permute-start(bf16[832,128]{1,0:T(8,128)(2,1)S(1)} %get-tuple-element.68), channel_id=1, source_target_pairs={{0,4},{1,5},{2,6},{3,7},{4,0},{5,1},{6,2},{7,3},{8,12},{9,13},{10,... | collective-permute-start | bytes 638984 | tf_op jit(solution)/shard_map/ppermute | solution.py:46
  73.6 15.8 %collective-permute-start.9 = (bf16[832,128]{1,0:T(8,128)(2,1)S(1)}, bf16[832,128]{1,0:T(8,128)(2,1)S(1)}, u32[]{:S(2)}, u32[]{:S(2)}) collective-permute-start(bf16[832,128]{1,0:T(8,128)(2,1)S(1)} %get-tuple-element.69), channel_id=1, source_target_pairs={{0,6},{1,7},{2,4},{3,5},{4,2},{5,3},{6,0},{7,1},{8,14},{9,15},{10,... | collective-permute-start | bytes 638984 | tf_op jit(solution)/shard_map/ppermute | solution.py:46
  89.4 1.9 %collective-permute-start.10 = (bf16[4,512,128]{2,1,0:T(8,128)(2,1)S(1)}, bf16[4,512,128]{2,1,0:T(8,128)(2,1)S(1)}, u32[]{:S(2)}, u32[]{:S(2)}) collective-permute-start(bf16[4,512,128]{2,1,0:T(8,128)(2,1)S(1)} %get-tuple-element.78), channel_id=1, source_target_pairs={{0,1},{1,0},{2,3},{3,2},{4,5},{5,4},{6,7},{7,6},{8,9},{9,8},{10,11... | collective-permute-start | bytes 1572872 | tf_op jit(solution)/shard_map/ppermute | solution.py:46
  92.0 11.2 %collective-permute-start.11 = (bf16[512,128]{1,0:T(8,128)(2,1)S(1)}, bf16[512,128]{1,0:T(8,128)(2,1)S(1)}, u32[]{:S(2)}, u32[]{:S(2)}) collective-permute-start(bf16[512,128]{1,0:T(8,128)(2,1)S(1)} %get-tuple-element.80), channel_id=1, source_target_pairs={{0,2},{1,3},{2,0},{3,1},{4,6},{5,7},{6,4},{7,5},{8,10},{9,11},{10,... | collective-permute-start | bytes 393224 | tf_op jit(solution)/shard_map/ppermute | solution.py:46
  96.2 12.9 %collective-permute-start.12 = (bf16[512,128]{1,0:T(8,128)(2,1)S(1)}, bf16[512,128]{1,0:T(8,128)(2,1)S(1)}, u32[]{:S(2)}, u32[]{:S(2)}) collective-permute-start(bf16[512,128]{1,0:T(8,128)(2,1)S(1)} %get-tuple-element.81), channel_id=1, source_target_pairs={{0,4},{1,5},{2,6},{3,7},{4,0},{5,1},{6,2},{7,3},{8,12},{9,13},{10,... | collective-permute-start | bytes 393224 | tf_op jit(solution)/shard_map/ppermute | solution.py:46
  97.1 11.9 %collective-permute-start.13 = (bf16[512,128]{1,0:T(8,128)(2,1)S(1)}, bf16[512,128]{1,0:T(8,128)(2,1)S(1)}, u32[]{:S(2)}, u32[]{:S(2)}) collective-permute-start(bf16[512,128]{1,0:T(8,128)(2,1)S(1)} %get-tuple-element.82), channel_id=1, source_target_pairs={{0,6},{1,7},{2,4},{3,5},{4,2},{5,3},{6,0},{7,1},{8,14},{9,15},{10,... | collective-permute-start | bytes 393224 | tf_op jit(solution)/shard_map/ppermute | solution.py:46
  98.6 1.3 %collective-permute-start.14 = (bf16[4,64,128]{2,1,0:T(8,128)(2,1)S(1)}, bf16[4,64,128]{2,1,0:T(8,128)(2,1)S(1)}, u32[]{:S(2)}, u32[]{:S(2)}) collective-permute-start(bf16[4,64,128]{2,1,0:T(8,128)(2,1)S(1)} %get-tuple-element.86.mine_ref), channel_id=1, source_target_pairs={{0,1},{1,0},{2,3},{3,2},{4,5},{5,4},{6,7},{7,6},{8,9},{9,8},{10,11... | collective-permute-start | bytes 196616 | tf_op jit(solution)/shard_map/ppermute | solution.py:46

commit v16 on v15

--- a/solution.py
+++ b/solution.py
@@ -51,21 +51,16 @@
 
 
 def pack_kernel(first, where_ref, *refs):
-    patches_refs, (out_ref, turned, own, shared) = refs[:-4], refs[-4:]
+    patches_refs, (out_ref, turned, mixed) = refs[:-3], refs[-3:]
     several, span, pix = patches_refs[0].shape
-    images = turned.shape[0]
-    padded = turned.shape[1]
+    images, padded, _ = turned.shape
     count = out_ref.shape[0] // 3 * 2
-    parity = where_ref[PARITY]
-    at_own = pl.multiple_of(64 * parity, 64)
-    at_shared = pl.multiple_of(128 * (1 - parity), 64)
+    quarter = count // 2
     row = lax.broadcasted_iota(jnp.int32, (padded, pix), 0)
     column = lax.broadcasted_iota(jnp.int32, (padded, pix), 1)
     pick = ((row < count) & (column == row + first)).astype(F32).astype(BF16)
     for i in range(images):
-        patches_ref, j = patches_refs[i // several], i % several
-        turned[i, :, :LANES] = dot(pick, patches_ref[j, pl.ds(at_own, LANES), :], COLS_1).astype(BF16)
-        turned[i, :, LANES:] = dot(pick, patches_ref[j, pl.ds(at_shared, 64), :], COLS_1).astype(BF16)
+        turned[i] = dot(pick, patches_refs[i // several][i % several], COLS_1).astype(BF16)
     size = 16 * images
     row = lax.broadcasted_iota(jnp.int32, (size, size), 0)
     column = lax.broadcasted_iota(jnp.int32, (size, size), 1)
@@ -73,19 +68,17 @@
     order = order.astype(F32).astype(BF16)
     for b in range(padded // 16):
         rows = turned[:, 16 * b : 16 * b + 16, :].reshape(size, span)
-        out = dot(order, rows).astype(BF16)
-        own[16 * b : 16 * b + 16] = out[:, :LANES].reshape(16, images, LANES)
-        shared[16 * b : 16 * b + 16] = out[:, LANES:].reshape(16, images, 64)
-    out_ref[:count] = own[:count]
-    lower, upper = shared[: count // 2], shared[count // 2 : count]
-
-    @pl.when(parity == 0)
+        mixed[16 * b : 16 * b + 16] = dot(order, rows).astype(BF16).reshape(16, images, span)
+
+    @pl.when(where_ref[PARITY] == 0)
     def _():
-        out_ref[count:] = jnp.concatenate([lower, upper], axis=2)
-
-    @pl.when(parity == 1)
+        out_ref[:count] = mixed[:count, :, :LANES]
+        out_ref[count:] = jnp.concatenate([mixed[:quarter, :, LANES:], mixed[quarter:count, :, LANES:]], axis=2)
+
+    @pl.when(where_ref[PARITY] == 1)
     def _():
-        out_ref[count:] = jnp.concatenate([upper, lower], axis=2)
+        out_ref[:count] = mixed[:count, :, 64:]
+        out_ref[count:] = jnp.concatenate([mixed[quarter:count, :, :64], mixed[:quarter, :, :64]], axis=2)
 
 
 def pack(where, patches, h):
@@ -105,8 +98,7 @@
         out_specs=pl.BlockSpec(dims, lambda i: (0, 0, 0)),
         scratch_shapes=[
             pltpu.VMEM((images, padded, span), BF16),
-            pltpu.VMEM((padded, images, LANES), BF16),
-            pltpu.VMEM((padded, images, 64), BF16),
+            pltpu.VMEM((padded, images, span), BF16),
         ],
         name="pack_patches",
     )(where, *[patches] * 4)

time: 111 us -> 111 us (level)
  no operation moved by 1% of the time
where the time goes in v16:
time: 111 us; the launch traced here: 110 us
  Pallas kernels  61.5 us (55%)
  starting transfers between devices  29.7 us (27%)
  waiting for transfers between devices  16.6 us (15%)
  local copies, waits for them, and re-layouts  1.55 us (1%)
    ppermute x15, starting transfers between devices, swap(): return lax.ppermute(value, axis, [(i, i ^ bits) for i in range(count)])  19.7 us
    ppermute x15, waiting for transfers between devices, swap(): return lax.ppermute(value, axis, [(i, i ^ bits) for i in range(count)])  16.6 us
    pallas_call x1, Pallas kernels, residual(): call(functools.partial(residual_kernel, groups, scale, len(feature), n_ti...  15 us
    pallas_call x1, Pallas kernels, backward(): call(functools.partial(backward_kernel, groups, len(grad), n_decode), [sh...  14.3 us
    all_to_all x2, starting transfers between devices, exchange(): lax.all_to_all(value, 'dp', 0, 0, axis_index_groups=groups, tiled=True)  9.96 us
    pallas_call x1, Pallas kernels, reconstruct(): call(functools.partial(recon_kernel, len(feature), n_tiles), [shape((rows...  9.77 us
    pallas_call x1, Pallas kernels, forward(): call(functools.partial(forward_kernel, n_tiles, pix), [shape((pix * image...  9.66 us
    pallas_call x2, Pallas kernels, pack(): call(functools.partial(pack_kernel, h * half), shape(dims, BF16), limit=2...  3.37 us
  transfers between devices with their start and end apart: 17, of which 7 were waited for; matrix products, arithmetic and copies ran while one was open for 0% of the time, Pallas kernels for 52%

profile of v16, /device:TPU:0, one launch (start us, length us, event | category | flops | bytes accessed | tf_op | source)
XLA Modules:
  0.0 110.2 jit_solution(6080173662584597873)
XLA Ops:
  0.7 0.1 stack.47.where_ref
  0.7 0.0 copy-start
  0.8 1.4 %copy-done = bf16[16,196,192]{1,2,0:T(8,128)(2,1)S(1)} copy-done((bf16[16,196,192]{1,2,0:T(8,128)(2,1)S(1)}, bf16[16,196,192]{1,2,0:T(8,128)(2,1)}, u32[]{:S(2)}) %copy-start) | copy-done | bytes 1204248
  2.2 1.7 %pack_patches.2.refs_8_.refs_16_ = bf16[147,16,128]{2,1,0:T(8,128)(2,1)S(1)} custom-call(s32[11]{0:T(128)S(1)} %stack.47.where_ref, bf16[16,192,196]{2,1,0:T(8,128)(2,1)S(1)} %bitcast.27, bf16[16,192,196]{2,1,0:T(8,128)(2,1)S(1)} %bitcast.28, bf16[16,192,196]{2,1,0:T(8,128)(2,1)S(1)} %bitcast.29, bf16[16,192,196]{2,1,0:T(8,128)(2,1)S(1)} %bitcast.30), custom_call_target="tpu_custom_call" | custom-call | tf_op jit(solution)/shard_map/pack_patches/pallas_call | solution.py:92
  3.9 3.0 %collective-permute-start.3 = (bf16[147,16,128]{2,1,0:T(8,128)(2,1)S(1)}, bf16[147,16,128]{2,1,0:T(8,128)(2,1)}, u32[]{:S(2)}, u32[]{:S(2)}) collective-permute-start(bf16[147,16,128]{2,1,0:T(8,128)(2,1)S(1)} %pack_patches.2.refs_8_.refs_16_), channel_id=1, source_target_pairs={{0,16},{8,24},{16,0},{24,8},{1,17},{9,25},{17,1},{25,9},{2,18},{10... | collective-permute-start | bytes 1806344 | tf_op jit(solution)/shard_map/ppermute | solution.py:46
  6.9 1.7 %pack_patches.3.refs_7_.refs_15_ = bf16[147,16,128]{2,1,0:T(8,128)(2,1)S(1)} custom-call(s32[11]{0:T(128)S(1)} %stack.47.where_ref, bf16[16,192,196]{2,1,0:T(8,128)(2,1)S(1)} %bitcast.31, bf16[16,192,196]{2,1,0:T(8,128)(2,1)S(1)} %bitcast.32, bf16[16,192,196]{2,1,0:T(8,128)(2,1)S(1)} %bitcast.33, bf16[16,192,196]{2,1,0:T(8,128)(2,1)S(1)} %bitcast.34), custom_call_target="tpu_custom_call" | custom-call | tf_op jit(solution)/shard_map/pack_patches/pallas_call | solution.py:92
  8.6 2.0 %collective-permute-start = (bf16[147,16,128]{2,1,0:T(8,128)(2,1)S(1)}, bf16[147,16,128]{2,1,0:T(8,128)(2,1)}, u32[]{:S(2)}, u32[]{:S(2)}) collective-permute-start(bf16[147,16,128]{2,1,0:T(8,128)(2,1)S(1)} %pack_patches.3.refs_7_.refs_15_), channel_id=1, source_target_pairs={{0,8},{8,0},{16,24},{24,16},{1,9},{9,1},{17,25},{25,17},{2,10},{10... | collective-permute-start | bytes 1806344 | tf_op jit(solution)/shard_map/ppermute | solution.py:46
  10.6 0.5 collective-permute-start.2
  11.1 0.1 collective-permute-start.1
  11.2 9.7 %forward.1 = (bf16[3136,256]{1,0:T(8,128)(2,1)}, bf16[3136,256]{1,0:T(8,128)(2,1)}, bf16[3136,256]{1,0:T(8,128)(2,1)}, bf16[3136,256]{1,0:T(8,128)(2,1)}, bf16[3...) custom-call(bf16[196,16,1024]{2,1,0:T(8,128)(2,1)} %bitcast.48, ...), custom_call_target="tpu_custom_call" | custom-call | tf_op jit(solution)/shard_map/forward/pallas_call | solution.py:163
  20.8 0.6 collective-permute-done.3.refs_12_.refs_20_
  21.4 3.8 %collective-permute-done.refs_9_.refs_17_ = bf16[147,16,128]{2,1,0:T(8,128)(2,1)} collective-permute-done((bf16[147,16,128]{2,1,0:T(8,128)(2,1)S(1)}, bf16[147,16,128]{2,1,0:T(8,128)(2,1)}, u32[]{:S(2)}, u32[]{:S(2)}) %collective-permute-start) | collective-permute-done | bytes 602144 | tf_op jit(solution)/shard_map/ppermute | solution.py:46
  25.3 0.4 collective-permute-start.4
  25.7 2.1 %collective-permute-start.5 = (bf16[147,16,128]{2,1,0:T(8,128)(2,1)}, bf16[147,16,128]{2,1,0:T(8,128)(2,1)}, u32[]{:S(2)}, u32[]{:S(2)}) collective-permute-start(bf16[147,16,128]{2,1,0:T(8,128)(2,1)} %collective-permute-done.3.refs_12_.refs_20_), channel_id=1, source_target_pairs={{0,8},{8,0},{16,24},{24,16},{1,9},{9,1},{17,25},{25,17},{2,10},{10... | collective-permute-start | bytes 1806344 | tf_op jit(solution)/shard_map/ppermute | solution.py:46
  27.7 4.9 %all-to-all-start = ((bf16[8,16,768]{2,1,0:T(8,128)(2,1)}), bf16[8,16,768]{2,1,0:T(8,128)(2,1)S(1)}, u32[]{:S(2)}, u32[]{:S(2)}) async-start(bf16[8,16,768]{2,1,0:T(8,128)(2,1)} %get-tuple-element.49), calls=%async_computation | async-start | bytes 393216 | tf_op jit(solution)/shard_map/all_to_all | solution.py:50
  32.6 9.8 %reconstruct.1 = (f32[3136,256]{1,0:T(8,128)}, f32[3136,256]{1,0:T(8,128)}, f32[3136,256]{1,0:T(8,128)}) custom-call(bf16[3136,256]{1,0:T(8,128)(2,1)} %get-tuple-element.51.refs_0_, bf16[3136,256]{1,0:T(8,128)(2,1)} %get-tuple-element.52.refs_1_, bf16[3136,256]{1,0:T(8,128)(2,1)} %get-tuple-element.53.refs_2_, bf16[3136,256]{1,0:T(8,128)(2,1)} %get-tuple-element.54.refs_3_, ...), custom_call_target="tpu_custom_call" | custom-call | tf_op jit(solution)/shard_map/reconstruct/pallas_call | solution.py:203
  42.4 0.0 all-to-all-done.got_ref
  42.4 2.7 %class_logits.1 = bf16[8,16,1152]{2,1,0:T(8,128)(2,1)} custom-call(s32[11]{0:T(128)S(1)} %stack.47.where_ref, bf16[8,16,768]{2,1,0:T(8,128)(2,1)S(1)} %all-to-all-done.got_ref, bf16[1408,512]{1,0:T(8,128)(2,1)S(1)} %bitcast.42), custom_call_target="tpu_custom_call" | custom-call | tf_op jit(solution)/shard_map/class_logits/pallas_call | solution.py:504
  45.1 5.1 %all-to-all-start.1 = ((bf16[8,16,1152]{2,1,0:T(8,128)(2,1)}), bf16[8,16,1152]{2,1,0:T(8,128)(2,1)S(1)}, u32[]{:S(2)}, u32[]{:S(2)}) async-start(bf16[8,16,1152]{2,1,0:T(8,128)(2,1)} %class_logits.1), calls=%async_computation.1 | async-start | bytes 589824 | tf_op jit(solution)/shard_map/all_to_all | solution.py:50
  50.2 0.0 collective-permute-done.2.refs_11_.refs_19_
  50.2 0.0 collective-permute-done.1.refs_10_.refs_18_
  50.2 0.0 collective-permute-done.4.refs_13_.refs_21_
  50.2 0.0 collective-permute-done.5.refs_14_.refs_22_
  50.2 0.0 copy-start.13
  50.2 15.0 %residual.1 = (bf16[3136,256]{1,0:T(8,128)(2,1)}, bf16[3136,256]{1,0:T(8,128)(2,1)}, bf16[3136,256]{1,0:T(8,128)(2,1)}, bf16[4,768,128]{2,1,0:T(8,128)(2,1)}, bf16[4,768,128]{2,1,0:T(8,128)(2,1)}) custom-call(s32[11]{0:T(128)} %copy-done.8, bf16[3136,256]{1,0:T(8,128)(2,1)} %get-tuple-element.51.refs_0_, bf16[3136,256]{1,0:T(8,128)(2,1)} %get-tuple-element.52.refs_1_, ...), custom_call_target="tpu_custom_call" | custom-call | flops 4932501504 | bytes 20873216 | tf_op jit(solution)/shard_map/residual/pallas_call | solution.py:337
  65.3 0.0 copy-start.9
  65.3 0.6 collective-permute-start.6
  65.8 0.0 all-to-all-done.1.got_ref.stats_ref
  65.9 0.3 aux_backward.1
  66.2 1.9 %collective-permute-done.6.got_ref = bf16[4,768,128]{2,1,0:T(8,128)(2,1)} collective-permute-done((bf16[4,768,128]{2,1,0:T(8,128)(2,1)}, bf16[4,768,128]{2,1,0:T(8,128)(2,1)}, u32[]{:S(2)}, u32[]{:S(2)}) %collective-permute-start.6) | collective-permute-done | bytes 786464 | tf_op jit(solution)/shard_map/ppermute | solution.py:46
  68.1 1.4 %add_cores.2 = (bf16[832,128]{1,0:T(8,128)(2,1)S(1)}, bf16[832,128]{1,0:T(8,128)(2,1)S(1)}, bf16[832,128]{1,0:T(8,128)(2,1)S(1)}, bf16[832,128]{1,0:T(8,128)(2,1)S(1)}) custom-call(s32[11]{0:T(128)S(1)} %copy-done.9, bf16[4,768,128]{2,1,0:T(8,128)(2,1)S(1)} %copy-done.6, bf16[4,768,128]{2,1,0:T(8,128)(2,1)} %collective-permute-done.6.got_ref, ...), custom_call_target="tpu_custom_call" | custom-call | tf_op jit(solution)/shard_map/add_cores/pallas_call | solution.py:614
  69.5 1.9 %collective-permute-start.7 = (bf16[832,128]{1,0:T(8,128)(2,1)S(1)}, bf16[832,128]{1,0:T(8,128)(2,1)S(1)}, u32[]{:S(2)}, u32[]{:S(2)}) collective-permute-start(bf16[832,128]{1,0:T(8,128)(2,1)S(1)} %get-tuple-element.67), channel_id=1, source_target_pairs={{0,2},{1,3},{2,0},{3,1},{4,6},{5,7},{6,4},{7,5},{8,10},{9,11},{10,... | collective-permute-start | bytes 638984 | tf_op jit(solution)/shard_map/ppermute | solution.py:46
  71.4 2.4 %collective-permute-start.8 = (bf16[832,128]{1,0:T(8,128)(2,1)S(1)}, bf16[832,128]{1,0:T(8,128)(2,1)S(1)}, u32[]{:S(2)}, u32[]{:S(2)}) collective-permute-start(bf16[832,128]{1,0:T(8,128)(2,1)S(1)} %get-tuple-element.68), channel_id=1, source_target_pairs={{0,4},{1,5},{2,6},{3,7},{4,0},{5,1},{6,2},{7,3},{8,12},{9,13},{10,... | collective-permute-start | bytes 638984 | tf_op jit(solution)/shard_map/ppermute | solution.py:46
  73.7 0.2 collective-permute-start.9
  74.0 14.3 %backward.1 = (bf16[4,512,128]{2,1,0:T(8,128)(2,1)S(1)}, bf16[4,512,128]{2,1,0:T(8,128)(2,1)S(1)}) custom-call(s32[11]{0:T(128)S(1)} %copy-done.9, bf16[3136,256]{1,0:T(8,128)(2,1)S(1)} %copy-done.10, bf16[3136,256]{1,0:T(8,128)(2,1)S(1)} %copy-done.11, bf16[3136,256]{1,0:T(8,128)(2,1)S(1)} %copy-done.12, bf16[1024,768]{1,0:T(8,128)(2,1)S(1)} %bitcast.38, ...), custom_call_target="tpu_custom_call" | custom-call | flops 9865003008 | bytes 12845056 | tf_op jit(solution)/shard_map/backward/pallas_call | solution.py:416
  88.3 0.0 collective-permute-done.7.refs_1_
  88.3 1.2 %collective-permute-done.8.refs_2_ = bf16[832,128]{1,0:T(8,128)(2,1)S(1)} collective-permute-done((bf16[832,128]{1,0:T(8,128)(2,1)S(1)}, bf16[832,128]{1,0:T(8,128)(2,1)S(1)}, u32[]{:S(2)}, u32[]{:S(2)}) %collective-permute-start.8) | collective-permute-done | bytes 213024 | tf_op jit(solution)/shard_map/ppermute | solution.py:46
  89.5 0.0 collective-permute-done.9.refs_3_
  89.5 1.9 %collective-permute-done.10.got_ref = bf16[4,512,128]{2,1,0:T(8,128)(2,1)S(1)} collective-permute-done((bf16[4,512,128]{2,1,0:T(8,128)(2,1)S(1)}, bf16[4,512,128]{2,1,0:T(8,128)(2,1)S(1)}, u32[]{:S(2)}, u32[]{:S(2)}) %collective-permute-start.10) | collective-permute-done | bytes 524320 | tf_op jit(solution)/shard_map/ppermute | solution.py:46
  91.5 0.7 add_cores.3
  92.1 4.2 %collective-permute-start.11 = (bf16[512,128]{1,0:T(8,128)(2,1)S(1)}, bf16[512,128]{1,0:T(8,128)(2,1)S(1)}, u32[]{:S(2)}, u32[]{:S(2)}) collective-permute-start(bf16[512,128]{1,0:T(8,128)(2,1)S(1)} %get-tuple-element.80), channel_id=1, source_target_pairs={{0,2},{1,3},{2,0},{3,1},{4,6},{5,7},{6,4},{7,5},{8,10},{9,11},{10,... | collective-permute-start | bytes 393224 | tf_op jit(solution)/shard_map/ppermute | solution.py:46
  96.3 1.0 collective-permute-start.12
  97.3 1.5 %collective-permute-start.13 = (bf16[512,128]{1,0:T(8,128)(2,1)S(1)}, bf16[512,128]{1,0:T(8,128)(2,1)S(1)}, u32[]{:S(2)}, u32[]{:S(2)}) collective-permute-start(bf16[512,128]{1,0:T(8,128)(2,1)S(1)} %get-tuple-element.82), channel_id=1, source_target_pairs={{0,6},{1,7},{2,4},{3,5},{4,2},{5,3},{6,0},{7,1},{8,14},{9,15},{10,... | collective-permute-start | bytes 393224 | tf_op jit(solution)/shard_map/ppermute | solution.py:46
  98.8 0.0 collective-permute-start.14
  98.8 1.3 %collective-permute-done.14.other_ref = bf16[4,64,128]{2,1,0:T(8,128)(2,1)S(1)} collective-permute-done((bf16[4,64,128]{2,1,0:T(8,128)(2,1)S(1)}, bf16[4,64,128]{2,1,0:T(8,128)(2,1)S(1)}, u32[]{:S(2)}, u32[]{:S(2)}) %collective-permute-start.14) | collective-permute-done | bytes 65568 | tf_op jit(solution)/shard_map/ppermute | solution.py:46
  100.0 3.3 %class_backward.1 = (f32[1408,512]{1,0:T(8,128)}, f32[128,512]{1,0:T(8,128)}) custom-call(s32[11]{0:T(128)S(1)} %copy-done.9, bf16[1408,512]{1,0:T(8,128)(2,1)S(1)} %bitcast.43, bf16[8,16,768]{2,1,0:T(8,128)(2,1)S(1)} %all-to-all-done.got_ref, bf16[8,16,1152]{2,1,0:T(8,128)(2,1)S(1)} %all-to-all-done.1.got_ref.stats_ref, ...), custom_call_target="tpu_custom_call" | custom-call | flops 184549376 | bytes 2883584 | tf_op jit(solution)/shard_map/class_backward/pallas_call | solution.py:574
  103.3 5.9 %collective-permute-done.12.refs_6_ = bf16[512,128]{1,0:T(8,128)(2,1)S(1)} collective-permute-done((bf16[512,128]{1,0:T(8,128)(2,1)S(1)}, bf16[512,128]{1,0:T(8,128)(2,1)S(1)}, u32[]{:S(2)}, u32[]{:S(2)}) %collective-permute-start.12) | collective-permute-done | bytes 131104 | tf_op jit(solution)/shard_map/ppermute | solution.py:46
  109.2 1.0 finish.1
  (27 shorter events, 0.1 us)
Async XLA Ops:
  0.7 41.6 %copy-start.8 = (s32[11]{0:T(128)}, s32[11]{0:T(128)S(1)}, u32[]{:S(2)}) copy-start(s32[11]{0:T(128)S(1)} %stack.47.where_ref) | copy-start | bytes 136
  0.7 1.4 %copy-start = (bf16[16,196,192]{1,2,0:T(8,128)(2,1)S(1)}, bf16[16,196,192]{1,2,0:T(8,128)(2,1)}, u32[]{:S(2)}) copy-start(bf16[16,196,192]{1,2,0:T(8,128)(2,1)} %param.9) | copy-start | bytes 3612676
  3.8 7.2 %copy-start.3 = (bf16[147,16,128]{2,1,0:T(8,128)(2,1)}, bf16[147,16,128]{2,1,0:T(8,128)(2,1)S(1)}, u32[]{:S(2)}) copy-start(bf16[147,16,128]{2,1,0:T(8,128)(2,1)S(1)} %pack_patches.2.refs_8_.refs_16_) | copy-start | bytes 1806340
  3.9 17.6 %collective-permute-start.3 = (bf16[147,16,128]{2,1,0:T(8,128)(2,1)S(1)}, bf16[147,16,128]{2,1,0:T(8,128)(2,1)}, u32[]{:S(2)}, u32[]{:S(2)}) collective-permute-start(bf16[147,16,128]{2,1,0:T(8,128)(2,1)S(1)} %pack_patches.2.refs_8_.refs_16_), channel_id=1, source_target_pairs={{0,16},{8,24},{16,0},{24,8},{1,17},{9,25},{17,1},{25,9},{2,18},{10... | collective-permute-start | bytes 1806344 | tf_op jit(solution)/shard_map/ppermute | solution.py:46
  8.6 12.3 %copy-start.4 = (bf16[147,16,128]{2,1,0:T(8,128)(2,1)}, bf16[147,16,128]{2,1,0:T(8,128)(2,1)S(1)}, u32[]{:S(2)}) copy-start(bf16[147,16,128]{2,1,0:T(8,128)(2,1)S(1)} %pack_patches.3.refs_7_.refs_15_) | copy-start | bytes 1806340
  8.6 16.7 %collective-permute-start = (bf16[147,16,128]{2,1,0:T(8,128)(2,1)S(1)}, bf16[147,16,128]{2,1,0:T(8,128)(2,1)}, u32[]{:S(2)}, u32[]{:S(2)}) collective-permute-start(bf16[147,16,128]{2,1,0:T(8,128)(2,1)S(1)} %pack_patches.3.refs_7_.refs_15_), channel_id=1, source_target_pairs={{0,8},{8,0},{16,24},{24,16},{1,9},{9,1},{17,25},{25,17},{2,10},{10... | collective-permute-start | bytes 1806344 | tf_op jit(solution)/shard_map/ppermute | solution.py:46
  10.6 39.6 %collective-permute-start.2 = (bf16[147,16,128]{2,1,0:T(8,128)(2,1)S(1)}, bf16[147,16,128]{2,1,0:T(8,128)(2,1)}, u32[]{:S(2)}, u32[]{:S(2)}) collective-permute-start(bf16[147,16,128]{2,1,0:T(8,128)(2,1)S(1)} %pack_patches.3.refs_7_.refs_15_), channel_id=1, source_target_pairs={{0,16},{8,24},{16,0},{24,8},{1,17},{9,25},{17,1},{25,9},{2,18},{10... | collective-permute-start | bytes 1806344 | tf_op jit(solution)/shard_map/ppermute | solution.py:46
  11.1 39.1 %collective-permute-start.1 = (bf16[147,16,128]{2,1,0:T(8,128)(2,1)S(1)}, bf16[147,16,128]{2,1,0:T(8,128)(2,1)}, u32[]{:S(2)}, u32[]{:S(2)}) collective-permute-start(bf16[147,16,128]{2,1,0:T(8,128)(2,1)S(1)} %pack_patches.2.refs_8_.refs_16_), channel_id=1, source_target_pairs={{0,8},{8,0},{16,24},{24,16},{1,9},{9,1},{17,25},{25,17},{2,10},{10... | collective-permute-start | bytes 1806344 | tf_op jit(solution)/shard_map/ppermute | solution.py:46
  25.3 24.9 %collective-permute-start.4 = (bf16[147,16,128]{2,1,0:T(8,128)(2,1)}, bf16[147,16,128]{2,1,0:T(8,128)(2,1)}, u32[]{:S(2)}, u32[]{:S(2)}) collective-permute-start(bf16[147,16,128]{2,1,0:T(8,128)(2,1)} %collective-permute-done.refs_9_.refs_17_), channel_id=1, source_target_pairs={{0,16},{8,24},{16,0},{24,8},{1,17},{9,25},{17,1},{25,9},{2,18},{10... | collective-permute-start | bytes 1806344 | tf_op jit(solution)/shard_map/ppermute | solution.py:46
  25.7 24.5 %collective-permute-start.5 = (bf16[147,16,128]{2,1,0:T(8,128)(2,1)}, bf16[147,16,128]{2,1,0:T(8,128)(2,1)}, u32[]{:S(2)}, u32[]{:S(2)}) collective-permute-start(bf16[147,16,128]{2,1,0:T(8,128)(2,1)} %collective-permute-done.3.refs_12_.refs_20_), channel_id=1, source_target_pairs={{0,8},{8,0},{16,24},{24,16},{1,9},{9,1},{17,25},{25,17},{2,10},{10... | collective-permute-start | bytes 1806344 | tf_op jit(solution)/shard_map/ppermute | solution.py:46
  27.7 14.7 %all-to-all-start = ((bf16[8,16,768]{2,1,0:T(8,128)(2,1)}), bf16[8,16,768]{2,1,0:T(8,128)(2,1)S(1)}, u32[]{:S(2)}, u32[]{:S(2)}) async-start(bf16[8,16,768]{2,1,0:T(8,128)(2,1)} %get-tuple-element.49), calls=%async_computation | async-start | bytes 393216 | tf_op jit(solution)/shard_map/all_to_all | solution.py:50
  32.6 9.8 %copy-start.2 = (bf16[1,1408,512]{2,1,0:T(8,128)(2,1)S(1)}, bf16[1,1408,512]{2,1,0:T(8,128)(2,1)}, u32[]{:S(2)}) copy-start(bf16[1,1408,512]{2,1,0:T(8,128)(2,1)} %param.15) | copy-start | bytes 4325380
  45.1 20.8 %all-to-all-start.1 = ((bf16[8,16,1152]{2,1,0:T(8,128)(2,1)}), bf16[8,16,1152]{2,1,0:T(8,128)(2,1)S(1)}, u32[]{:S(2)}, u32[]{:S(2)}) async-start(bf16[8,16,1152]{2,1,0:T(8,128)(2,1)} %class_logits.1), calls=%async_computation.1 | async-start | bytes 589824 | tf_op jit(solution)/shard_map/all_to_all | solution.py:50
  50.2 15.6 %copy-start.13 = (f32[16,512]{1,0:T(8,128)S(1)}, f32[16,512]{1,0:T(8,128)}, u32[]{:S(2)}) copy-start(f32[16,512]{1,0:T(8,128)} %get-tuple-element.60.aux_pre_ref) | copy-start | bytes 98308
  65.2 2.8 %copy-start.6 = (bf16[4,768,128]{2,1,0:T(8,128)(2,1)S(1)}, bf16[4,768,128]{2,1,0:T(8,128)(2,1)}, u32[]{:S(2)}) copy-start(bf16[4,768,128]{2,1,0:T(8,128)(2,1)} %get-tuple-element.63.keep_ref) | copy-start | bytes 2359300
  65.3 2.8 %copy-start.9 = (s32[11]{0:T(128)S(1)}, s32[11]{0:T(128)}, u32[]{:S(2)}) copy-start(s32[11]{0:T(128)} %copy-done.8) | copy-start | bytes 136
  65.3 2.8 %collective-permute-start.6 = (bf16[4,768,128]{2,1,0:T(8,128)(2,1)}, bf16[4,768,128]{2,1,0:T(8,128)(2,1)}, u32[]{:S(2)}, u32[]{:S(2)}) collective-permute-start(bf16[4,768,128]{2,1,0:T(8,128)(2,1)} %get-tuple-element.64), channel_id=1, source_target_pairs={{0,1},{1,0},{2,3},{3,2},{4,5},{5,4},{6,7},{7,6},{8,9},{9,8},{10,11... | collective-permute-start | bytes 2359304 | tf_op jit(solution)/shard_map/ppermute | solution.py:46
  65.8 8.1 %copy-start.5 = (bf16[1,1024,512]{2,1,0:T(8,128)(2,1)S(1)}, bf16[1,1024,512]{2,1,0:T(8,128)(2,1)}, u32[]{:S(2)}) copy-start(bf16[1,1024,512]{2,1,0:T(8,128)(2,1)} %param.14) | copy-start | bytes 3145732
  65.8 8.1 %copy-start.7 = (bf16[1,256,1024]{2,1,0:T(8,128)(2,1)S(1)}, bf16[1,256,1024]{2,1,0:T(8,128)(2,1)}, u32[]{:S(2)}) copy-start(bf16[1,256,1024]{2,1,0:T(8,128)(2,1)} %param.12) | copy-start | bytes 1572868
  65.8 8.1 %copy-start.10 = (bf16[3136,256]{1,0:T(8,128)(2,1)S(1)}, bf16[3136,256]{1,0:T(8,128)(2,1)}, u32[]{:S(2)}) copy-start(bf16[3136,256]{1,0:T(8,128)(2,1)} %get-tuple-element.70.refs_0_) | copy-start | bytes 4816900
  65.9 8.1 %copy-start.11 = (bf16[3136,256]{1,0:T(8,128)(2,1)S(1)}, bf16[3136,256]{1,0:T(8,128)(2,1)}, u32[]{:S(2)}) copy-start(bf16[3136,256]{1,0:T(8,128)(2,1)} %get-tuple-element.71.refs_1_) | copy-start | bytes 4816900
  65.9 8.1 %copy-start.12 = (bf16[3136,256]{1,0:T(8,128)(2,1)S(1)}, bf16[3136,256]{1,0:T(8,128)(2,1)}, u32[]{:S(2)}) copy-start(bf16[3136,256]{1,0:T(8,128)(2,1)} %get-tuple-element.72.refs_2_) | copy-start | bytes 4816900
  66.2 7.8 %copy-start.1 = (bf16[1,1024,768]{2,1,0:T(8,128)(2,1)S(1)}, bf16[1,1024,768]{2,1,0:T(8,128)(2,1)}, u32[]{:S(2)}) copy-start(bf16[1,1024,768]{2,1,0:T(8,128)(2,1)} %param.13) | copy-start | bytes 4718596
  69.5 18.8 %collective-permute-start.7 = (bf16[832,128]{1,0:T(8,128)(2,1)S(1)}, bf16[832,128]{1,0:T(8,128)(2,1)S(1)}, u32[]{:S(2)}, u32[]{:S(2)}) collective-permute-start(bf16[832,128]{1,0:T(8,128)(2,1)S(1)} %get-tuple-element.67), channel_id=1, source_target_pairs={{0,2},{1,3},{2,0},{3,1},{4,6},{5,7},{6,4},{7,5},{8,10},{9,11},{10,... | collective-permute-start | bytes 638984 | tf_op jit(solution)/shard_map/ppermute | solution.py:46
  71.4 18.2 %collective-permute-start.8 = (bf16[832,128]{1,0:T(8,128)(2,1)S(1)}, bf16[832,128]{1,0:T(8,128)(2,1)S(1)}, u32[]{:S(2)}, u32[]{:S(2)}) collective-permute-start(bf16[832,128]{1,0:T(8,128)(2,1)S(1)} %get-tuple-element.68), channel_id=1, source_target_pairs={{0,4},{1,5},{2,6},{3,7},{4,0},{5,1},{6,2},{7,3},{8,12},{9,13},{10,... | collective-permute-start | bytes 638984 | tf_op jit(solution)/shard_map/ppermute | solution.py:46
  73.7 15.8 %collective-permute-start.9 = (bf16[832,128]{1,0:T(8,128)(2,1)S(1)}, bf16[832,128]{1,0:T(8,128)(2,1)S(1)}, u32[]{:S(2)}, u32[]{:S(2)}) collective-permute-start(bf16[832,128]{1,0:T(8,128)(2,1)S(1)} %get-tuple-element.69), channel_id=1, source_target_pairs={{0,6},{1,7},{2,4},{3,5},{4,2},{5,3},{6,0},{7,1},{8,14},{9,15},{10,... | collective-permute-start | bytes 638984 | tf_op jit(solution)/shard_map/ppermute | solution.py:46
  89.5 1.9 %collective-permute-start.10 = (bf16[4,512,128]{2,1,0:T(8,128)(2,1)S(1)}, bf16[4,512,128]{2,1,0:T(8,128)(2,1)S(1)}, u32[]{:S(2)}, u32[]{:S(2)}) collective-permute-start(bf16[4,512,128]{2,1,0:T(8,128)(2,1)S(1)} %get-tuple-element.78), channel_id=1, source_target_pairs={{0,1},{1,0},{2,3},{3,2},{4,5},{5,4},{6,7},{7,6},{8,9},{9,8},{10,11... | collective-permute-start | bytes 1572872 | tf_op jit(solution)/shard_map/ppermute | solution.py:46
  92.1 11.2 %collective-permute-start.11 = (bf16[512,128]{1,0:T(8,128)(2,1)S(1)}, bf16[512,128]{1,0:T(8,128)(2,1)S(1)}, u32[]{:S(2)}, u32[]{:S(2)}) collective-permute-start(bf16[512,128]{1,0:T(8,128)(2,1)S(1)} %get-tuple-element.80), channel_id=1, source_target_pairs={{0,2},{1,3},{2,0},{3,1},{4,6},{5,7},{6,4},{7,5},{8,10},{9,11},{10,... | collective-permute-start | bytes 393224 | tf_op jit(solution)/shard_map/ppermute | solution.py:46
  96.3 12.9 %collective-permute-start.12 = (bf16[512,128]{1,0:T(8,128)(2,1)S(1)}, bf16[512,128]{1,0:T(8,128)(2,1)S(1)}, u32[]{:S(2)}, u32[]{:S(2)}) collective-permute-start(bf16[512,128]{1,0:T(8,128)(2,1)S(1)} %get-tuple-element.81), channel_id=1, source_target_pairs={{0,4},{1,5},{2,6},{3,7},{4,0},{5,1},{6,2},{7,3},{8,12},{9,13},{10,... | collective-permute-start | bytes 393224 | tf_op jit(solution)/shard_map/ppermute | solution.py:46
  97.3 11.9 %collective-permute-start.13 = (bf16[512,128]{1,0:T(8,128)(2,1)S(1)}, bf16[512,128]{1,0:T(8,128)(2,1)S(1)}, u32[]{:S(2)}, u32[]{:S(2)}) collective-permute-start(bf16[512,128]{1,0:T(8,128)(2,1)S(1)} %get-tuple-element.82), channel_id=1, source_target_pairs={{0,6},{1,7},{2,4},{3,5},{4,2},{5,3},{6,0},{7,1},{8,14},{9,15},{10,... | collective-permute-start | bytes 393224 | tf_op jit(solution)/shard_map/ppermute | solution.py:46
  98.8 1.3 %collective-permute-start.14 = (bf16[4,64,128]{2,1,0:T(8,128)(2,1)S(1)}, bf16[4,64,128]{2,1,0:T(8,128)(2,1)S(1)}, u32[]{:S(2)}, u32[]{:S(2)}) collective-permute-start(bf16[4,64,128]{2,1,0:T(8,128)(2,1)S(1)} %get-tuple-element.86.mine_ref), channel_id=1, source_target_pairs={{0,1},{1,0},{2,3},{3,2},{4,5},{5,4},{6,7},{7,6},{8,9},{9,8},{10,11... | collective-permute-start | bytes 196616 | tf_op jit(solution)/shard_map/ppermute | solution.py:46

commit v17 on v16

--- a/solution.py
+++ b/solution.py
@@ -374,9 +374,7 @@
 
     def body(g):
         here = slice(g * size, (g + 1) * size)
-        if g:
-            contract(g - 1, rows, pairs)
-        else:
+        if g == 0:
             pooled[...] = dot(aux_grad_ref[...], aux_ref[...], COLS_1) / (rows // images)
         grad = jnp.concatenate([ref[...] for ref in grad_refs], axis=1)
         for j, decode_ref in enumerate(decode_refs):
@@ -385,8 +383,8 @@
             feature_grads[here, cut] = (back + pooled[:, cut][None]).astype(BF16).reshape(size, TILE)
         hidden_back = dot(feature_grads[here], second_ref[...], COLS_1)
         hidden_grads[here] = jnp.where(hidden[here].astype(F32) > 0, hidden_back, 0.0).astype(BF16)
+        contract(g, rows, pairs)
         if g == STEPS - 1:
-            contract(g, rows, pairs)
             part = width // groups
             tall = total_second.shape[0] // groups
             second = jnp.concatenate(

time: 111 us -> 111 us (level)
  transfers between devices with their start and end apart: 17 -> 17, of which waited for: 7 -> 7; matrix products, arithmetic and copies ran while one was open for 0% -> 0% of each run, Pallas kernels for 52% -> 51%
where the time goes in v17:
time: 111 us; the launch traced here: 110 us
  Pallas kernels  61.2 us (55%)
  starting transfers between devices  29.7 us (27%)
  waiting for transfers between devices  16.9 us (15%)
  local copies, waits for them, and re-layouts  1.55 us (1%)
    ppermute x15, starting transfers between devices, swap(): return lax.ppermute(value, axis, [(i, i ^ bits) for i in range(count)])  19.7 us
    ppermute x15, waiting for transfers between devices, swap(): return lax.ppermute(value, axis, [(i, i ^ bits) for i in range(count)])  16.9 us
    pallas_call x1, Pallas kernels, residual(): call(functools.partial(residual_kernel, groups, scale, len(feature), n_ti...  15 us
    pallas_call x1, Pallas kernels, backward(): call(functools.partial(backward_kernel, groups, len(grad), n_decode), [sh...  14 us
    all_to_all x2, starting transfers between devices, exchange(): lax.all_to_all(value, 'dp', 0, 0, axis_index_groups=groups, tiled=True)  9.96 us
    pallas_call x1, Pallas kernels, reconstruct(): call(functools.partial(recon_kernel, len(feature), n_tiles), [shape((rows...  9.77 us
    pallas_call x1, Pallas kernels, forward(): call(functools.partial(forward_kernel, n_tiles, pix), [shape((pix * image...  9.66 us
    pallas_call x2, Pallas kernels, pack(): call(functools.partial(pack_kernel, h * half), shape(dims, BF16), limit=2...  3.37 us
  transfers between devices with their start and end apart: 17, of which 7 were waited for; matrix products, arithmetic and copies ran while one was open for 0% of the time, Pallas kernels for 51%

profile of v17, /device:TPU:0, one launch (start us, length us, event | category | flops | bytes accessed | tf_op | source)
XLA Modules:
  0.0 110.2 jit_solution(2865046898936283429)
XLA Ops:
  0.7 0.1 stack.47.where_ref
  0.7 0.0 copy-start
  0.8 1.4 %copy-done = bf16[16,196,192]{1,2,0:T(8,128)(2,1)S(1)} copy-done((bf16[16,196,192]{1,2,0:T(8,128)(2,1)S(1)}, bf16[16,196,192]{1,2,0:T(8,128)(2,1)}, u32[]{:S(2)}) %copy-start) | copy-done | bytes 1204248
  2.2 1.7 %pack_patches.2.refs_8_.refs_16_ = bf16[147,16,128]{2,1,0:T(8,128)(2,1)S(1)} custom-call(s32[11]{0:T(128)S(1)} %stack.47.where_ref, bf16[16,192,196]{2,1,0:T(8,128)(2,1)S(1)} %bitcast.27, bf16[16,192,196]{2,1,0:T(8,128)(2,1)S(1)} %bitcast.28, bf16[16,192,196]{2,1,0:T(8,128)(2,1)S(1)} %bitcast.29, bf16[16,192,196]{2,1,0:T(8,128)(2,1)S(1)} %bitcast.30), custom_call_target="tpu_custom_call" | custom-call | tf_op jit(solution)/shard_map/pack_patches/pallas_call | solution.py:92
  3.9 3.0 %collective-permute-start.3 = (bf16[147,16,128]{2,1,0:T(8,128)(2,1)S(1)}, bf16[147,16,128]{2,1,0:T(8,128)(2,1)}, u32[]{:S(2)}, u32[]{:S(2)}) collective-permute-start(bf16[147,16,128]{2,1,0:T(8,128)(2,1)S(1)} %pack_patches.2.refs_8_.refs_16_), channel_id=1, source_target_pairs={{0,16},{8,24},{16,0},{24,8},{1,17},{9,25},{17,1},{25,9},{2,18},{10... | collective-permute-start | bytes 1806344 | tf_op jit(solution)/shard_map/ppermute | solution.py:46
  6.9 1.7 %pack_patches.3.refs_7_.refs_15_ = bf16[147,16,128]{2,1,0:T(8,128)(2,1)S(1)} custom-call(s32[11]{0:T(128)S(1)} %stack.47.where_ref, bf16[16,192,196]{2,1,0:T(8,128)(2,1)S(1)} %bitcast.31, bf16[16,192,196]{2,1,0:T(8,128)(2,1)S(1)} %bitcast.32, bf16[16,192,196]{2,1,0:T(8,128)(2,1)S(1)} %bitcast.33, bf16[16,192,196]{2,1,0:T(8,128)(2,1)S(1)} %bitcast.34), custom_call_target="tpu_custom_call" | custom-call | tf_op jit(solution)/shard_map/pack_patches/pallas_call | solution.py:92
  8.6 2.0 %collective-permute-start = (bf16[147,16,128]{2,1,0:T(8,128)(2,1)S(1)}, bf16[147,16,128]{2,1,0:T(8,128)(2,1)}, u32[]{:S(2)}, u32[]{:S(2)}) collective-permute-start(bf16[147,16,128]{2,1,0:T(8,128)(2,1)S(1)} %pack_patches.3.refs_7_.refs_15_), channel_id=1, source_target_pairs={{0,8},{8,0},{16,24},{24,16},{1,9},{9,1},{17,25},{25,17},{2,10},{10... | collective-permute-start | bytes 1806344 | tf_op jit(solution)/shard_map/ppermute | solution.py:46
  10.6 0.5 collective-permute-start.2
  11.1 0.1 collective-permute-start.1
  11.2 9.7 %forward.1 = (bf16[3136,256]{1,0:T(8,128)(2,1)}, bf16[3136,256]{1,0:T(8,128)(2,1)}, bf16[3136,256]{1,0:T(8,128)(2,1)}, bf16[3136,256]{1,0:T(8,128)(2,1)}, bf16[3...) custom-call(bf16[196,16,1024]{2,1,0:T(8,128)(2,1)} %bitcast.48, ...), custom_call_target="tpu_custom_call" | custom-call | tf_op jit(solution)/shard_map/forward/pallas_call | solution.py:163
  20.8 0.6 collective-permute-done.3.refs_12_.refs_20_
  21.4 3.8 %collective-permute-done.refs_9_.refs_17_ = bf16[147,16,128]{2,1,0:T(8,128)(2,1)} collective-permute-done((bf16[147,16,128]{2,1,0:T(8,128)(2,1)S(1)}, bf16[147,16,128]{2,1,0:T(8,128)(2,1)}, u32[]{:S(2)}, u32[]{:S(2)}) %collective-permute-start) | collective-permute-done | bytes 602144 | tf_op jit(solution)/shard_map/ppermute | solution.py:46
  25.3 0.4 collective-permute-start.4
  25.7 2.1 %collective-permute-start.5 = (bf16[147,16,128]{2,1,0:T(8,128)(2,1)}, bf16[147,16,128]{2,1,0:T(8,128)(2,1)}, u32[]{:S(2)}, u32[]{:S(2)}) collective-permute-start(bf16[147,16,128]{2,1,0:T(8,128)(2,1)} %collective-permute-done.3.refs_12_.refs_20_), channel_id=1, source_target_pairs={{0,8},{8,0},{16,24},{24,16},{1,9},{9,1},{17,25},{25,17},{2,10},{10... | collective-permute-start | bytes 1806344 | tf_op jit(solution)/shard_map/ppermute | solution.py:46
  27.7 4.9 %all-to-all-start = ((bf16[8,16,768]{2,1,0:T(8,128)(2,1)}), bf16[8,16,768]{2,1,0:T(8,128)(2,1)S(1)}, u32[]{:S(2)}, u32[]{:S(2)}) async-start(bf16[8,16,768]{2,1,0:T(8,128)(2,1)} %get-tuple-element.49), calls=%async_computation | async-start | bytes 393216 | tf_op jit(solution)/shard_map/all_to_all | solution.py:50
  32.6 9.8 %reconstruct.1 = (f32[3136,256]{1,0:T(8,128)}, f32[3136,256]{1,0:T(8,128)}, f32[3136,256]{1,0:T(8,128)}) custom-call(bf16[3136,256]{1,0:T(8,128)(2,1)} %get-tuple-element.51.refs_0_, bf16[3136,256]{1,0:T(8,128)(2,1)} %get-tuple-element.52.refs_1_, bf16[3136,256]{1,0:T(8,128)(2,1)} %get-tuple-element.53.refs_2_, bf16[3136,256]{1,0:T(8,128)(2,1)} %get-tuple-element.54.refs_3_, ...), custom_call_target="tpu_custom_call" | custom-call | tf_op jit(solution)/shard_map/reconstruct/pallas_call | solution.py:203
  42.4 0.0 all-to-all-done.got_ref
  42.4 2.7 %class_logits.1 = bf16[8,16,1152]{2,1,0:T(8,128)(2,1)} custom-call(s32[11]{0:T(128)S(1)} %stack.47.where_ref, bf16[8,16,768]{2,1,0:T(8,128)(2,1)S(1)} %all-to-all-done.got_ref, bf16[1408,512]{1,0:T(8,128)(2,1)S(1)} %bitcast.42), custom_call_target="tpu_custom_call" | custom-call | tf_op jit(solution)/shard_map/class_logits/pallas_call | solution.py:502
  45.1 5.1 %all-to-all-start.1 = ((bf16[8,16,1152]{2,1,0:T(8,128)(2,1)}), bf16[8,16,1152]{2,1,0:T(8,128)(2,1)S(1)}, u32[]{:S(2)}, u32[]{:S(2)}) async-start(bf16[8,16,1152]{2,1,0:T(8,128)(2,1)} %class_logits.1), calls=%async_computation.1 | async-start | bytes 589824 | tf_op jit(solution)/shard_map/all_to_all | solution.py:50
  50.2 0.0 collective-permute-done.2.refs_11_.refs_19_
  50.2 0.0 collective-permute-done.1.refs_10_.refs_18_
  50.2 0.0 collective-permute-done.4.refs_13_.refs_21_
  50.2 0.0 collective-permute-done.5.refs_14_.refs_22_
  50.2 0.0 copy-start.13
  50.2 15.0 %residual.1 = (bf16[3136,256]{1,0:T(8,128)(2,1)}, bf16[3136,256]{1,0:T(8,128)(2,1)}, bf16[3136,256]{1,0:T(8,128)(2,1)}, bf16[4,768,128]{2,1,0:T(8,128)(2,1)}, bf16[4,768,128]{2,1,0:T(8,128)(2,1)}) custom-call(s32[11]{0:T(128)} %copy-done.8, bf16[3136,256]{1,0:T(8,128)(2,1)} %get-tuple-element.51.refs_0_, bf16[3136,256]{1,0:T(8,128)(2,1)} %get-tuple-element.52.refs_1_, ...), custom_call_target="tpu_custom_call" | custom-call | flops 4932501504 | bytes 20873216 | tf_op jit(solution)/shard_map/residual/pallas_call | solution.py:337
  65.3 0.0 copy-start.9
  65.3 0.6 collective-permute-start.6
  65.8 0.0 all-to-all-done.1.got_ref.stats_ref
  65.9 0.3 aux_backward.1
  66.2 1.9 %collective-permute-done.6.got_ref = bf16[4,768,128]{2,1,0:T(8,128)(2,1)} collective-permute-done((bf16[4,768,128]{2,1,0:T(8,128)(2,1)}, bf16[4,768,128]{2,1,0:T(8,128)(2,1)}, u32[]{:S(2)}, u32[]{:S(2)}) %collective-permute-start.6) | collective-permute-done | bytes 786464 | tf_op jit(solution)/shard_map/ppermute | solution.py:46
  68.1 1.4 %add_cores.2 = (bf16[832,128]{1,0:T(8,128)(2,1)S(1)}, bf16[832,128]{1,0:T(8,128)(2,1)S(1)}, bf16[832,128]{1,0:T(8,128)(2,1)S(1)}, bf16[832,128]{1,0:T(8,128)(2,1)S(1)}) custom-call(s32[11]{0:T(128)S(1)} %copy-done.9, bf16[4,768,128]{2,1,0:T(8,128)(2,1)S(1)} %copy-done.6, bf16[4,768,128]{2,1,0:T(8,128)(2,1)} %collective-permute-done.6.got_ref, ...), custom_call_target="tpu_custom_call" | custom-call | tf_op jit(solution)/shard_map/add_cores/pallas_call | solution.py:612
  69.5 1.9 %collective-permute-start.7 = (bf16[832,128]{1,0:T(8,128)(2,1)S(1)}, bf16[832,128]{1,0:T(8,128)(2,1)S(1)}, u32[]{:S(2)}, u32[]{:S(2)}) collective-permute-start(bf16[832,128]{1,0:T(8,128)(2,1)S(1)} %get-tuple-element.67), channel_id=1, source_target_pairs={{0,2},{1,3},{2,0},{3,1},{4,6},{5,7},{6,4},{7,5},{8,10},{9,11},{10,... | collective-permute-start | bytes 638984 | tf_op jit(solution)/shard_map/ppermute | solution.py:46
  71.4 2.4 %collective-permute-start.8 = (bf16[832,128]{1,0:T(8,128)(2,1)S(1)}, bf16[832,128]{1,0:T(8,128)(2,1)S(1)}, u32[]{:S(2)}, u32[]{:S(2)}) collective-permute-start(bf16[832,128]{1,0:T(8,128)(2,1)S(1)} %get-tuple-element.68), channel_id=1, source_target_pairs={{0,4},{1,5},{2,6},{3,7},{4,0},{5,1},{6,2},{7,3},{8,12},{9,13},{10,... | collective-permute-start | bytes 638984 | tf_op jit(solution)/shard_map/ppermute | solution.py:46
  73.7 0.2 collective-permute-start.9
  74.0 14.0 %backward.1 = (bf16[4,512,128]{2,1,0:T(8,128)(2,1)S(1)}, bf16[4,512,128]{2,1,0:T(8,128)(2,1)S(1)}) custom-call(s32[11]{0:T(128)S(1)} %copy-done.9, bf16[3136,256]{1,0:T(8,128)(2,1)S(1)} %copy-done.10, bf16[3136,256]{1,0:T(8,128)(2,1)S(1)} %copy-done.11, bf16[3136,256]{1,0:T(8,128)(2,1)S(1)} %copy-done.12, bf16[1024,768]{1,0:T(8,128)(2,1)S(1)} %bitcast.38, ...), custom_call_target="tpu_custom_call" | custom-call | flops 9865003008 | bytes 12845056 | tf_op jit(solution)/shard_map/backward/pallas_call | solution.py:414
  88.0 0.0 collective-permute-done.7.refs_1_
  88.0 1.5 %collective-permute-done.8.refs_2_ = bf16[832,128]{1,0:T(8,128)(2,1)S(1)} collective-permute-done((bf16[832,128]{1,0:T(8,128)(2,1)S(1)}, bf16[832,128]{1,0:T(8,128)(2,1)S(1)}, u32[]{:S(2)}, u32[]{:S(2)}) %collective-permute-start.8) | collective-permute-done | bytes 213024 | tf_op jit(solution)/shard_map/ppermute | solution.py:46
  89.5 0.0 collective-permute-done.9.refs_3_
  89.5 1.9 %collective-permute-done.10.got_ref = bf16[4,512,128]{2,1,0:T(8,128)(2,1)S(1)} collective-permute-done((bf16[4,512,128]{2,1,0:T(8,128)(2,1)S(1)}, bf16[4,512,128]{2,1,0:T(8,128)(2,1)S(1)}, u32[]{:S(2)}, u32[]{:S(2)}) %collective-permute-start.10) | collective-permute-done | bytes 524320 | tf_op jit(solution)/shard_map/ppermute | solution.py:46
  91.5 0.7 add_cores.3
  92.1 4.2 %collective-permute-start.11 = (bf16[512,128]{1,0:T(8,128)(2,1)S(1)}, bf16[512,128]{1,0:T(8,128)(2,1)S(1)}, u32[]{:S(2)}, u32[]{:S(2)}) collective-permute-start(bf16[512,128]{1,0:T(8,128)(2,1)S(1)} %get-tuple-element.80), channel_id=1, source_target_pairs={{0,2},{1,3},{2,0},{3,1},{4,6},{5,7},{6,4},{7,5},{8,10},{9,11},{10,... | collective-permute-start | bytes 393224 | tf_op jit(solution)/shard_map/ppermute | solution.py:46
  96.3 1.0 collective-permute-start.12
  97.3 1.5 %collective-permute-start.13 = (bf16[512,128]{1,0:T(8,128)(2,1)S(1)}, bf16[512,128]{1,0:T(8,128)(2,1)S(1)}, u32[]{:S(2)}, u32[]{:S(2)}) collective-permute-start(bf16[512,128]{1,0:T(8,128)(2,1)S(1)} %get-tuple-element.82), channel_id=1, source_target_pairs={{0,6},{1,7},{2,4},{3,5},{4,2},{5,3},{6,0},{7,1},{8,14},{9,15},{10,... | collective-permute-start | bytes 393224 | tf_op jit(solution)/shard_map/ppermute | solution.py:46
  98.8 0.0 collective-permute-start.14
  98.8 1.3 %collective-permute-done.14.other_ref = bf16[4,64,128]{2,1,0:T(8,128)(2,1)S(1)} collective-permute-done((bf16[4,64,128]{2,1,0:T(8,128)(2,1)S(1)}, bf16[4,64,128]{2,1,0:T(8,128)(2,1)S(1)}, u32[]{:S(2)}, u32[]{:S(2)}) %collective-permute-start.14) | collective-permute-done | bytes 65568 | tf_op jit(solution)/shard_map/ppermute | solution.py:46
  100.0 3.3 %class_backward.1 = (f32[1408,512]{1,0:T(8,128)}, f32[128,512]{1,0:T(8,128)}) custom-call(s32[11]{0:T(128)S(1)} %copy-done.9, bf16[1408,512]{1,0:T(8,128)(2,1)S(1)} %bitcast.43, bf16[8,16,768]{2,1,0:T(8,128)(2,1)S(1)} %all-to-all-done.got_ref, bf16[8,16,1152]{2,1,0:T(8,128)(2,1)S(1)} %all-to-all-done.1.got_ref.stats_ref, ...), custom_call_target="tpu_custom_call" | custom-call | flops 184549376 | bytes 2883584 | tf_op jit(solution)/shard_map/class_backward/pallas_call | solution.py:572
  103.3 5.9 %collective-permute-done.12.refs_6_ = bf16[512,128]{1,0:T(8,128)(2,1)S(1)} collective-permute-done((bf16[512,128]{1,0:T(8,128)(2,1)S(1)}, bf16[512,128]{1,0:T(8,128)(2,1)S(1)}, u32[]{:S(2)}, u32[]{:S(2)}) %collective-permute-start.12) | collective-permute-done | bytes 131104 | tf_op jit(solution)/shard_map/ppermute | solution.py:46
  109.2 1.0 finish.1
  (27 shorter events, 0.1 us)
Async XLA Ops:
  0.7 41.6 %copy-start.8 = (s32[11]{0:T(128)}, s32[11]{0:T(128)S(1)}, u32[]{:S(2)}) copy-start(s32[11]{0:T(128)S(1)} %stack.47.where_ref) | copy-start | bytes 136
  0.7 1.4 %copy-start = (bf16[16,196,192]{1,2,0:T(8,128)(2,1)S(1)}, bf16[16,196,192]{1,2,0:T(8,128)(2,1)}, u32[]{:S(2)}) copy-start(bf16[16,196,192]{1,2,0:T(8,128)(2,1)} %param.9) | copy-start | bytes 3612676
  3.8 7.2 %copy-start.3 = (bf16[147,16,128]{2,1,0:T(8,128)(2,1)}, bf16[147,16,128]{2,1,0:T(8,128)(2,1)S(1)}, u32[]{:S(2)}) copy-start(bf16[147,16,128]{2,1,0:T(8,128)(2,1)S(1)} %pack_patches.2.refs_8_.refs_16_) | copy-start | bytes 1806340
  3.9 17.6 %collective-permute-start.3 = (bf16[147,16,128]{2,1,0:T(8,128)(2,1)S(1)}, bf16[147,16,128]{2,1,0:T(8,128)(2,1)}, u32[]{:S(2)}, u32[]{:S(2)}) collective-permute-start(bf16[147,16,128]{2,1,0:T(8,128)(2,1)S(1)} %pack_patches.2.refs_8_.refs_16_), channel_id=1, source_target_pairs={{0,16},{8,24},{16,0},{24,8},{1,17},{9,25},{17,1},{25,9},{2,18},{10... | collective-permute-start | bytes 1806344 | tf_op jit(solution)/shard_map/ppermute | solution.py:46
  8.6 12.3 %copy-start.4 = (bf16[147,16,128]{2,1,0:T(8,128)(2,1)}, bf16[147,16,128]{2,1,0:T(8,128)(2,1)S(1)}, u32[]{:S(2)}) copy-start(bf16[147,16,128]{2,1,0:T(8,128)(2,1)S(1)} %pack_patches.3.refs_7_.refs_15_) | copy-start | bytes 1806340
  8.6 16.7 %collective-permute-start = (bf16[147,16,128]{2,1,0:T(8,128)(2,1)S(1)}, bf16[147,16,128]{2,1,0:T(8,128)(2,1)}, u32[]{:S(2)}, u32[]{:S(2)}) collective-permute-start(bf16[147,16,128]{2,1,0:T(8,128)(2,1)S(1)} %pack_patches.3.refs_7_.refs_15_), channel_id=1, source_target_pairs={{0,8},{8,0},{16,24},{24,16},{1,9},{9,1},{17,25},{25,17},{2,10},{10... | collective-permute-start | bytes 1806344 | tf_op jit(solution)/shard_map/ppermute | solution.py:46
  10.6 39.6 %collective-permute-start.2 = (bf16[147,16,128]{2,1,0:T(8,128)(2,1)S(1)}, bf16[147,16,128]{2,1,0:T(8,128)(2,1)}, u32[]{:S(2)}, u32[]{:S(2)}) collective-permute-start(bf16[147,16,128]{2,1,0:T(8,128)(2,1)S(1)} %pack_patches.3.refs_7_.refs_15_), channel_id=1, source_target_pairs={{0,16},{8,24},{16,0},{24,8},{1,17},{9,25},{17,1},{25,9},{2,18},{10... | collective-permute-start | bytes 1806344 | tf_op jit(solution)/shard_map/ppermute | solution.py:46
  11.1 39.1 %collective-permute-start.1 = (bf16[147,16,128]{2,1,0:T(8,128)(2,1)S(1)}, bf16[147,16,128]{2,1,0:T(8,128)(2,1)}, u32[]{:S(2)}, u32[]{:S(2)}) collective-permute-start(bf16[147,16,128]{2,1,0:T(8,128)(2,1)S(1)} %pack_patches.2.refs_8_.refs_16_), channel_id=1, source_target_pairs={{0,8},{8,0},{16,24},{24,16},{1,9},{9,1},{17,25},{25,17},{2,10},{10... | collective-permute-start | bytes 1806344 | tf_op jit(solution)/shard_map/ppermute | solution.py:46
  25.3 24.9 %collective-permute-start.4 = (bf16[147,16,128]{2,1,0:T(8,128)(2,1)}, bf16[147,16,128]{2,1,0:T(8,128)(2,1)}, u32[]{:S(2)}, u32[]{:S(2)}) collective-permute-start(bf16[147,16,128]{2,1,0:T(8,128)(2,1)} %collective-permute-done.refs_9_.refs_17_), channel_id=1, source_target_pairs={{0,16},{8,24},{16,0},{24,8},{1,17},{9,25},{17,1},{25,9},{2,18},{10... | collective-permute-start | bytes 1806344 | tf_op jit(solution)/shard_map/ppermute | solution.py:46
  25.7 24.5 %collective-permute-start.5 = (bf16[147,16,128]{2,1,0:T(8,128)(2,1)}, bf16[147,16,128]{2,1,0:T(8,128)(2,1)}, u32[]{:S(2)}, u32[]{:S(2)}) collective-permute-start(bf16[147,16,128]{2,1,0:T(8,128)(2,1)} %collective-permute-done.3.refs_12_.refs_20_), channel_id=1, source_target_pairs={{0,8},{8,0},{16,24},{24,16},{1,9},{9,1},{17,25},{25,17},{2,10},{10... | collective-permute-start | bytes 1806344 | tf_op jit(solution)/shard_map/ppermute | solution.py:46
  27.7 14.7 %all-to-all-start = ((bf16[8,16,768]{2,1,0:T(8,128)(2,1)}), bf16[8,16,768]{2,1,0:T(8,128)(2,1)S(1)}, u32[]{:S(2)}, u32[]{:S(2)}) async-start(bf16[8,16,768]{2,1,0:T(8,128)(2,1)} %get-tuple-element.49), calls=%async_computation | async-start | bytes 393216 | tf_op jit(solution)/shard_map/all_to_all | solution.py:50
  32.6 9.8 %copy-start.2 = (bf16[1,1408,512]{2,1,0:T(8,128)(2,1)S(1)}, bf16[1,1408,512]{2,1,0:T(8,128)(2,1)}, u32[]{:S(2)}) copy-start(bf16[1,1408,512]{2,1,0:T(8,128)(2,1)} %param.15) | copy-start | bytes 4325380
  45.1 20.8 %all-to-all-start.1 = ((bf16[8,16,1152]{2,1,0:T(8,128)(2,1)}), bf16[8,16,1152]{2,1,0:T(8,128)(2,1)S(1)}, u32[]{:S(2)}, u32[]{:S(2)}) async-start(bf16[8,16,1152]{2,1,0:T(8,128)(2,1)} %class_logits.1), calls=%async_computation.1 | async-start | bytes 589824 | tf_op jit(solution)/shard_map/all_to_all | solution.py:50
  50.2 15.6 %copy-start.13 = (f32[16,512]{1,0:T(8,128)S(1)}, f32[16,512]{1,0:T(8,128)}, u32[]{:S(2)}) copy-start(f32[16,512]{1,0:T(8,128)} %get-tuple-element.60.aux_pre_ref) | copy-start | bytes 98308
  65.2 2.8 %copy-start.6 = (bf16[4,768,128]{2,1,0:T(8,128)(2,1)S(1)}, bf16[4,768,128]{2,1,0:T(8,128)(2,1)}, u32[]{:S(2)}) copy-start(bf16[4,768,128]{2,1,0:T(8,128)(2,1)} %get-tuple-element.63.keep_ref) | copy-start | bytes 2359300
  65.3 2.8 %copy-start.9 = (s32[11]{0:T(128)S(1)}, s32[11]{0:T(128)}, u32[]{:S(2)}) copy-start(s32[11]{0:T(128)} %copy-done.8) | copy-start | bytes 136
  65.3 2.8 %collective-permute-start.6 = (bf16[4,768,128]{2,1,0:T(8,128)(2,1)}, bf16[4,768,128]{2,1,0:T(8,128)(2,1)}, u32[]{:S(2)}, u32[]{:S(2)}) collective-permute-start(bf16[4,768,128]{2,1,0:T(8,128)(2,1)} %get-tuple-element.64), channel_id=1, source_target_pairs={{0,1},{1,0},{2,3},{3,2},{4,5},{5,4},{6,7},{7,6},{8,9},{9,8},{10,11... | collective-permute-start | bytes 2359304 | tf_op jit(solution)/shard_map/ppermute | solution.py:46
  65.8 8.1 %copy-start.5 = (bf16[1,1024,512]{2,1,0:T(8,128)(2,1)S(1)}, bf16[1,1024,512]{2,1,0:T(8,128)(2,1)}, u32[]{:S(2)}) copy-start(bf16[1,1024,512]{2,1,0:T(8,128)(2,1)} %param.14) | copy-start | bytes 3145732
  65.8 8.1 %copy-start.7 = (bf16[1,256,1024]{2,1,0:T(8,128)(2,1)S(1)}, bf16[1,256,1024]{2,1,0:T(8,128)(2,1)}, u32[]{:S(2)}) copy-start(bf16[1,256,1024]{2,1,0:T(8,128)(2,1)} %param.12) | copy-start | bytes 1572868
  65.8 8.1 %copy-start.10 = (bf16[3136,256]{1,0:T(8,128)(2,1)S(1)}, bf16[3136,256]{1,0:T(8,128)(2,1)}, u32[]{:S(2)}) copy-start(bf16[3136,256]{1,0:T(8,128)(2,1)} %get-tuple-element.70.refs_0_) | copy-start | bytes 4816900
  65.9 8.1 %copy-start.11 = (bf16[3136,256]{1,0:T(8,128)(2,1)S(1)}, bf16[3136,256]{1,0:T(8,128)(2,1)}, u32[]{:S(2)}) copy-start(bf16[3136,256]{1,0:T(8,128)(2,1)} %get-tuple-element.71.refs_1_) | copy-start | bytes 4816900
  65.9 8.1 %copy-start.12 = (bf16[3136,256]{1,0:T(8,128)(2,1)S(1)}, bf16[3136,256]{1,0:T(8,128)(2,1)}, u32[]{:S(2)}) copy-start(bf16[3136,256]{1,0:T(8,128)(2,1)} %get-tuple-element.72.refs_2_) | copy-start | bytes 4816900
  66.2 7.8 %copy-start.1 = (bf16[1,1024,768]{2,1,0:T(8,128)(2,1)S(1)}, bf16[1,1024,768]{2,1,0:T(8,128)(2,1)}, u32[]{:S(2)}) copy-start(bf16[1,1024,768]{2,1,0:T(8,128)(2,1)} %param.13) | copy-start | bytes 4718596
  69.5 18.5 %collective-permute-start.7 = (bf16[832,128]{1,0:T(8,128)(2,1)S(1)}, bf16[832,128]{1,0:T(8,128)(2,1)S(1)}, u32[]{:S(2)}, u32[]{:S(2)}) collective-permute-start(bf16[832,128]{1,0:T(8,128)(2,1)S(1)} %get-tuple-element.67), channel_id=1, source_target_pairs={{0,2},{1,3},{2,0},{3,1},{4,6},{5,7},{6,4},{7,5},{8,10},{9,11},{10,... | collective-permute-start | bytes 638984 | tf_op jit(solution)/shard_map/ppermute | solution.py:46
  71.4 18.2 %collective-permute-start.8 = (bf16[832,128]{1,0:T(8,128)(2,1)S(1)}, bf16[832,128]{1,0:T(8,128)(2,1)S(1)}, u32[]{:S(2)}, u32[]{:S(2)}) collective-permute-start(bf16[832,128]{1,0:T(8,128)(2,1)S(1)} %get-tuple-element.68), channel_id=1, source_target_pairs={{0,4},{1,5},{2,6},{3,7},{4,0},{5,1},{6,2},{7,3},{8,12},{9,13},{10,... | collective-permute-start | bytes 638984 | tf_op jit(solution)/shard_map/ppermute | solution.py:46
  73.7 15.8 %collective-permute-start.9 = (bf16[832,128]{1,0:T(8,128)(2,1)S(1)}, bf16[832,128]{1,0:T(8,128)(2,1)S(1)}, u32[]{:S(2)}, u32[]{:S(2)}) collective-permute-start(bf16[832,128]{1,0:T(8,128)(2,1)S(1)} %get-tuple-element.69), channel_id=1, source_target_pairs={{0,6},{1,7},{2,4},{3,5},{4,2},{5,3},{6,0},{7,1},{8,14},{9,15},{10,... | collective-permute-start | bytes 638984 | tf_op jit(solution)/shard_map/ppermute | solution.py:46
  89.5 1.9 %collective-permute-start.10 = (bf16[4,512,128]{2,1,0:T(8,128)(2,1)S(1)}, bf16[4,512,128]{2,1,0:T(8,128)(2,1)S(1)}, u32[]{:S(2)}, u32[]{:S(2)}) collective-permute-start(bf16[4,512,128]{2,1,0:T(8,128)(2,1)S(1)} %get-tuple-element.78), channel_id=1, source_target_pairs={{0,1},{1,0},{2,3},{3,2},{4,5},{5,4},{6,7},{7,6},{8,9},{9,8},{10,11... | collective-permute-start | bytes 1572872 | tf_op jit(solution)/shard_map/ppermute | solution.py:46
  92.1 11.2 %collective-permute-start.11 = (bf16[512,128]{1,0:T(8,128)(2,1)S(1)}, bf16[512,128]{1,0:T(8,128)(2,1)S(1)}, u32[]{:S(2)}, u32[]{:S(2)}) collective-permute-start(bf16[512,128]{1,0:T(8,128)(2,1)S(1)} %get-tuple-element.80), channel_id=1, source_target_pairs={{0,2},{1,3},{2,0},{3,1},{4,6},{5,7},{6,4},{7,5},{8,10},{9,11},{10,... | collective-permute-start | bytes 393224 | tf_op jit(solution)/shard_map/ppermute | solution.py:46
  96.3 12.9 %collective-permute-start.12 = (bf16[512,128]{1,0:T(8,128)(2,1)S(1)}, bf16[512,128]{1,0:T(8,128)(2,1)S(1)}, u32[]{:S(2)}, u32[]{:S(2)}) collective-permute-start(bf16[512,128]{1,0:T(8,128)(2,1)S(1)} %get-tuple-element.81), channel_id=1, source_target_pairs={{0,4},{1,5},{2,6},{3,7},{4,0},{5,1},{6,2},{7,3},{8,12},{9,13},{10,... | collective-permute-start | bytes 393224 | tf_op jit(solution)/shard_map/ppermute | solution.py:46
  97.3 11.9 %collective-permute-start.13 = (bf16[512,128]{1,0:T(8,128)(2,1)S(1)}, bf16[512,128]{1,0:T(8,128)(2,1)S(1)}, u32[]{:S(2)}, u32[]{:S(2)}) collective-permute-start(bf16[512,128]{1,0:T(8,128)(2,1)S(1)} %get-tuple-element.82), channel_id=1, source_target_pairs={{0,6},{1,7},{2,4},{3,5},{4,2},{5,3},{6,0},{7,1},{8,14},{9,15},{10,... | collective-permute-start | bytes 393224 | tf_op jit(solution)/shard_map/ppermute | solution.py:46
  98.8 1.3 %collective-permute-start.14 = (bf16[4,64,128]{2,1,0:T(8,128)(2,1)S(1)}, bf16[4,64,128]{2,1,0:T(8,128)(2,1)S(1)}, u32[]{:S(2)}, u32[]{:S(2)}) collective-permute-start(bf16[4,64,128]{2,1,0:T(8,128)(2,1)S(1)} %get-tuple-element.86.mine_ref), channel_id=1, source_target_pairs={{0,1},{1,0},{2,3},{3,2},{4,5},{5,4},{6,7},{7,6},{8,9},{9,8},{10,11... | collective-permute-start | bytes 196616 | tf_op jit(solution)/shard_map/ppermute | solution.py:46
